TPU v7x, 32 devices: a whole 2x2x4 slice. The times are simulated.
32 devices in a mesh: groups: 2 (over y), wide: 4 (over z), narrow: 4 (over x, core).
Axes of the slice: x: 2, y: 2, z: 4, core: 2. Of those that a mesh axis runs over, the one named last changes fastest.
Arguments:
- embeddings: bfloat16 [32768, 1024], P(('groups', 'wide'), 'narrow'), parts along dimension 0, may hold values from -6 to 6
- pair_list: int32 [32, 2], P(('groups', 'wide')), parts along dimension 0, may hold values from 0 to 31, as said below
Outputs:
- weights: float32 [32768], P(('groups', 'wide')), parts along dimension 0
- neighbour_mean: bfloat16 [32768, 1024], P(('groups', 'wide'), 'narrow'), parts along dimension 0
There are 2 independent parts, one for each index of `groups`. A program takes and returns all parts, laid end to end along the dimension named above; each array names one. Nothing has to cross between parts.
Inputs may be any that keep to these rules, and one draw needn't show every extreme that they name: `pair_list`: the pairs on the shard of wide index w all have a row block owned by w, that is a // 8 == w. Among those pairs, at most 2 have a column block owned by any one index of wide, and for every w some index of wide owns exactly 2 of them.
All inputs are finite; a program needn't handle non-finite values.
Results may differ from a plain program's by a relative error of at most 0.002.
Values may be sent and summed in bfloat16 or wider, within the bound.
No kernel may reach another device: no remote copies, remote signals or barrier semaphores. Data moves between devices by JAX's collectives and lax.ppermute only.
A program may use at most 64 MiB of HBM per device.

v0:
```python
import jax
import jax.numpy as jnp
from jax import lax
from jax.sharding import PartitionSpec as P

F = 1024
BR = 512
BLK_DEV = 8


def on_device(embeddings, pair_list):
    wide_count = lax.axis_size("wide")
    wide_self = lax.axis_index("wide")
    pair_count = pair_list.shape[0]
    capacity = max(2, 2 * pair_count // wide_count)
    feat_slice = embeddings.shape[1]
    blocks = embeddings.reshape(BLK_DEV, BR, feat_slice)
    every_pair = lax.all_gather(pair_list, "wide", axis=0, tiled=True).reshape(
        wide_count, pair_count, 2
    )
    every_col = every_pair[:, :, 1]
    is_mine = (every_col // BLK_DEV == wide_self).astype(jnp.int32)
    ranks = jnp.cumsum(is_mine, axis=1) - 1
    slot_ids = jnp.arange(capacity, dtype=jnp.int32)
    picked = (is_mine[:, None, :] == 1) & (ranks[:, None, :] == slot_ids[None, :, None])
    send_local = jnp.sum(jnp.where(picked, every_col[:, None, :] % BLK_DEV, 0), axis=-1)
    send_valid = jnp.any(picked, axis=-1)
    outgoing = jnp.where(
        send_valid[:, :, None, None], blocks[send_local], jnp.zeros((), jnp.bfloat16)
    )
    incoming = lax.all_to_all(outgoing, "wide", split_axis=0, concat_axis=0, tiled=True)
    incoming = incoming.reshape(wide_count * capacity, BR, feat_slice)
    row_local = pair_list[:, 0] % BLK_DEV
    col_owner = pair_list[:, 1] // BLK_DEV
    positions = jnp.arange(pair_count, dtype=jnp.int32)
    earlier = (col_owner[None, :] == col_owner[:, None]) & (positions[None, :] < positions[:, None])
    own_rank = jnp.sum(earlier.astype(jnp.int32), axis=1)
    slot_index = col_owner * capacity + own_rank
    col_slices = incoming[slot_index]
    row_slices = blocks[row_local]
    row_full, col_full = (
        lax.all_to_all(row_slices, "narrow", split_axis=0, concat_axis=2, tiled=True),
        lax.all_to_all(col_slices, "narrow", split_axis=0, concat_axis=2, tiled=True),
    )
    gram = jnp.einsum("pik,pjk->pij", row_full, col_full, preferred_element_type=jnp.float32)
    row_square = jnp.sum(jnp.square(row_full.astype(jnp.float32)), axis=-1)
    col_square = jnp.sum(jnp.square(col_full.astype(jnp.float32)), axis=-1)
    kernel = jnp.exp(-(row_square[:, :, None] + col_square[:, None, :] - 2.0 * gram) / F)
    row_part = jnp.sum(kernel, axis=2)
    col_part = jnp.sum(kernel, axis=1)
    part_sums = jnp.einsum(
        "pij,pjk->pik", kernel.astype(jnp.bfloat16), col_full, preferred_element_type=jnp.float32
    ).astype(jnp.bfloat16)
    sums_back = lax.all_to_all(part_sums, "narrow", split_axis=2, concat_axis=0, tiled=True)
    sums = (
        jnp.zeros((BLK_DEV, BR, feat_slice), jnp.float32)
        .at[row_local]
        .add(sums_back.astype(jnp.float32))
    )
    row_every, col_every = (
        lax.all_gather(row_part, "narrow", axis=0, tiled=True),
        lax.all_gather(col_part, "narrow", axis=0, tiled=True),
    )
    slot_mass = jnp.zeros((wide_count * capacity, BR), jnp.float32).at[slot_index].set(col_every)
    mass_back = lax.all_to_all(
        slot_mass.reshape(wide_count, capacity, BR).astype(jnp.bfloat16),
        "wide",
        split_axis=0,
        concat_axis=0,
        tiled=True,
    ).astype(jnp.float32)
    mass_back = jnp.where(send_valid[:, :, None], mass_back, 0.0)
    col_mass = (
        jnp.zeros((BLK_DEV, BR), jnp.float32)
        .at[send_local.reshape(-1)]
        .add(mass_back.reshape(-1, BR))
    )
    row_mass = jnp.zeros((BLK_DEV, BR), jnp.float32).at[row_local].add(row_every)
    weights = 1.0 / (1.0 + (row_mass + col_mass) / BR)
    mean_rows = (blocks.astype(jnp.float32) + sums) / (1.0 + row_mass)[:, :, None]
    return (
        weights.reshape(BLK_DEV * BR),
        mean_rows.astype(jnp.bfloat16).reshape(BLK_DEV * BR, feat_slice),
    )


def solution(mesh):
    in_specs = (P(("groups", "wide"), "narrow"), P(("groups", "wide"), None))
    out_specs = (P(("groups", "wide")), P(("groups", "wide"), "narrow"))
    return jax.shard_map(
        on_device, mesh=mesh, in_specs=in_specs, out_specs=out_specs, check_vma=False
    )
```

profile of v0, /device:TPU:0, one launch (start us, length us, event | category | flops | bytes accessed | tf_op | source)
XLA Modules:
  0.0 172.6 jit_solution(921181018899522880)
XLA Ops:
  0.6 12.8 %all-gather.2 = s32[4,4,2]{1,2,0:T(2,128)S(1)} all-gather(s32[1,4,2]{1,2,0:T(2,128)} %bitcast.97), channel_id=1, replica_groups=mesh['groups'=2,'wide'=4,'narrow'=4] {'wide'}, dimensions={0}, use_global_device_ids=true | all-gather | bytes 160 | tf_op jit(solution)/shard_map/all_gather | solution.py:18
  14.3 2.3 %gather_fusion.1 = bf16[8,512,256]{2,1,0:T(8,128)(2,1)S(1)} fusion(bf16[8,512,256]{2,1,0:T(8,128)(2,1)} %bitcast.84, s32[1024]{0:T(1024)S(1)} %pad_clamp_fusion.1), kind=kCustom, calls=%fused_computation.1 | custom fusion | bytes 4194336 | tf_op jit(solution)/shard_map/gather | solution.py:29
  16.6 1.5 broadcast_select_fusion
  18.1 4.6 %all-to-all-start.1 = ((bf16[4,2,512,256]{3,2,1,0:T(8,128)(2,1)}), bf16[4,2,512,256]{3,2,1,0:T(8,128)(2,1)}, u32[]{:S(2)}, u32[]{:S(2)}) async-start(bf16[4,2,512,256]{3,2,1,0:T(8,128)(2,1)} %broadcast_select_fusion), calls=%async_computation.1 | async-start | bytes 4194304 | tf_op jit(solution)/shard_map/all_to_all | solution.py:31
  22.8 1.6 gather_fusion
  24.4 44.9 %all-to-all-done.1 = bf16[4,2,512,256]{3,2,1,0:T(8,128)(2,1)} async-done(((bf16[4,2,512,256]{3,2,1,0:T(8,128)(2,1)}), bf16[4,2,512,256]{3,2,1,0:T(8,128)(2,1)}, u32[]{:S(2)}, u32[]{:S(2)}) %all-to-all-start.1) | async-done | bytes 2097184 | tf_op jit(solution)/shard_map/all_to_all | solution.py:31
  69.2 3.5 %all-to-all-start = ((bf16[4,512,256]{2,1,0:T(8,128)(2,1)}), bf16[4,512,256]{2,1,0:T(8,128)(2,1)S(1)}, u32[]{:S(2)}, u32[]{:S(2)}) async-start(bf16[4,512,256]{2,1,0:T(8,128)(2,1)} %gather_fusion), calls=%async_computation | async-start | bytes 2097152 | tf_op jit(solution)/shard_map/all_to_all | solution.py:42
  73.0 3.2 %gather_fusion.2 = bf16[4,512,256]{2,1,0:T(8,128)(2,1)} fusion(bf16[8,512,256]{2,1,0:T(8,128)(2,1)} %bitcast.8, s32[1024]{0:T(1024)S(1)} %pad_clamp_fusion), kind=kCustom, calls=%fused_computation.2 | custom fusion | bytes 2097168 | tf_op jit(solution)/shard_map/gather | solution.py:39
  76.1 11.0 %all-to-all-done = bf16[4,512,256]{2,1,0:T(8,128)(2,1)S(1)} async-done(((bf16[4,512,256]{2,1,0:T(8,128)(2,1)}), bf16[4,512,256]{2,1,0:T(8,128)(2,1)S(1)}, u32[]{:S(2)}, u32[]{:S(2)}) %all-to-all-start) | async-done | bytes 1048608 | tf_op jit(solution)/shard_map/all_to_all | solution.py:42
  87.2 1.0 copy-done.1
  88.2 3.5 %all-to-all-start.2 = ((bf16[4,512,256]{2,1,0:T(8,128)(2,1)}), bf16[4,512,256]{2,1,0:T(8,128)(2,1)S(1)}, u32[]{:S(2)}, u32[]{:S(2)}) async-start(bf16[4,512,256]{2,1,0:T(8,128)(2,1)} %gather_fusion.2), calls=%async_computation.2 | async-start | bytes 2097152 | tf_op jit(solution)/shard_map/all_to_all | solution.py:43
  91.9 1.5 multiply_reduce_fusion.1
  93.4 12.7 %all-to-all-done.2 = bf16[4,512,256]{2,1,0:T(8,128)(2,1)S(1)} async-done(((bf16[4,512,256]{2,1,0:T(8,128)(2,1)}), bf16[4,512,256]{2,1,0:T(8,128)(2,1)S(1)}, u32[]{:S(2)}, u32[]{:S(2)}) %all-to-all-start.2) | async-done | bytes 1048608 | tf_op jit(solution)/shard_map/all_to_all | solution.py:43
  106.1 1.3 copy.19
  107.7 2.9 %fusion.27 = (f32[512]{0:T(512)S(1)}, f32[512]{0:T(512)S(1)}, bf16[512,512]{1,0:T(8,128)(2,1)}) fusion(bf16[4,512,256]{2,1,0:T(8,128)(2,1)S(1)} %all-to-all-done.2, bf16[4,512,256]{2,1,0:T(8,128)(2,1)} %copy-done.1, f32[512]{0:T(512)S(1)} %multiply_reduce_fusion, f32[512]{0:T(512)S(1)} %multiply_reduce_fusion.1), kind=kOutput, calls=%fused_computation.76 | convolution fusion | flops 538967040 | bytes 2629632 | tf_op jit(solution)/shard_map/pik,pjk->pij/dot_general | solution.py:45
  110.6 5.1 %all-gather.4 = f32[4,1,512]{2,1,0:T(1,128)S(1)} all-gather(f32[1,1,512]{2,1,0:T(1,128)S(1)} %bitcast.99), channel_id=3, replica_groups=mesh['groups'=2,'wide'=4,'narrow'=4] {'narrow'}, dimensions={0}, use_global_device_ids=true | all-gather | bytes 10240 | tf_op jit(solution)/shard_map/all_gather | solution.py:62
  115.8 0.6 scatter_custom_fusion.1
  117.0 3.2 %all-to-all-start.3 = ((bf16[4,2,512]{2,1,0:T(2,128)(2,1)}), bf16[4,2,512]{2,1,0:T(2,128)(2,1)S(1)}, u32[]{:S(2)}, u32[]{:S(2)}) async-start(bf16[4,2,512]{2,1,0:T(2,128)(2,1)} %convert_element_type.68), calls=%async_computation.3 | async-start | bytes 16384 | tf_op jit(solution)/shard_map/all_to_all | solution.py:65
  120.3 2.1 %fusion.5 = bf16[1,512,1024]{2,1,0:T(8,128)(2,1)S(1)} fusion(bf16[512,1024]{0,1:T(8,128)(2,1)} %bitcast.93, bf16[512,512]{1,0:T(8,128)(2,1)} %get-tuple-element.8), kind=kOutput, calls=%fused_computation.18 | convolution fusion | flops 537395200 | bytes 2621440 | tf_op jit(solution)/shard_map/pij,pjk->pik/dot_general | solution.py:51
  122.4 3.9 %copy.20 = bf16[1,512,1024]{1,0,2:T(2,128)(2,1)} copy(bf16[1,512,1024]{2,1,0:T(8,128)(2,1)S(1)} %fusion.5) | data formatting | bytes 2097152 | tf_op jit(solution)/shard_map/convert_element_type | solution.py:53
  126.9 8.1 %reduce.8 = bf16[1024,512]{1,0:T(8,128)(2,1)S(1)} reduce(bf16[1024,1,512]{2,1,0:T(2,128)(2,1)} %bitcast.89, bf16[]{:T(256)} %broadcast.300), dimensions={1}, to_apply=%bitcast.76.reduce_sub_computation | reduce | bytes 2097154
  135.0 2.0 %reshape.331 = bf16[4,2,65536]{2,1,0:T(2,128)(2,1)} reshape(bf16[1024,512]{1,0:T(8,128)(2,1)S(1)} %reduce.8) | data formatting | bytes 2097152
  137.0 3.5 %all-to-all-start.4 = ((bf16[4,2,65536]{2,1,0:T(2,128)(2,1)}), bf16[4,2,65536]{2,1,0:T(2,128)(2,1)S(1)}, u32[]{:S(2)}, u32[]{:S(2)}) async-start(bf16[4,2,65536]{2,1,0:T(2,128)(2,1)} %reshape.331), calls=%async_computation.4 | async-start | bytes 2097152 | tf_op jit(solution)/shard_map/all_to_all | solution.py:54
  140.5 2.3 %convert_element_type.70 = f32[8,512,256]{2,1,0:T(8,128)} convert(bf16[8,512,256]{2,1,0:T(8,128)(2,1)S(1)} %bitcast.86) | non-fusion elementwise | flops 1048576 | bytes 6291456 | tf_op jit(solution)/shard_map/convert_element_type | solution.py:80
  142.8 13.1 %all-gather.3 = f32[4,1,512]{2,1,0:T(1,128)S(1)} all-gather(f32[1,1,512]{2,1,0:T(1,128)S(1)} %bitcast.98), channel_id=2, replica_groups=mesh['groups'=2,'wide'=4,'narrow'=4] {'narrow'}, dimensions={0}, use_global_device_ids=true | all-gather | bytes 10240 | tf_op jit(solution)/shard_map/all_gather | solution.py:61
  155.9 0.6 scatter_custom_fusion
  156.6 0.7 scatter_fusion
  157.3 0.6 copy.24
  157.9 2.3 %reshape.332 = bf16[1024,1,512]{2,1,0:T(2,128)(2,1)} reshape(bf16[4,2,65536]{2,1,0:T(2,128)(2,1)S(1)} %all-to-all-done.4) | data formatting | bytes 2097152
  160.2 4.7 %copy.21 = f32[1,512,4,256]{3,1,2,0:T(8,128)S(1)} copy(bf16[1,512,4,256]{1,0,3,2:T(2,128)(2,1)} %bitcast.91) | data formatting | bytes 3145728 | tf_op jit(solution)/shard_map/convert_element_type | solution.py:58
  164.9 4.2 %scatter_fusion.1 = f32[8,512,256]{2,1,0:T(8,128)} fusion(f32[8,512,256]{2,1,0:T(8,128)} %convert_element_type.70, s32[4]{0:T(128)S(1)} %get-tuple-element.7, f32[4,512,256]{2,1,0:T(8,128)S(1)} %bitcast.88), kind=kCustom, calls=%fused_computation.6 | custom fusion | flops 524288 | bytes 6291472 | tf_op jit(solution)/shard_map/scatter-add | solution.py:58
  169.1 3.5 %divide_convert_fusion = bf16[8,512,256]{2,1,0:T(8,128)(2,1)} fusion(f32[8,512,256]{2,1,0:T(8,128)} %scatter_fusion.1, f32[8,512]{1,0:T(8,128)S(1)} %broadcast_add_fusion), kind=kLoop, calls=%fused_computation.7 | loop fusion | flops 2097152 | bytes 6307840 | tf_op jit(solution)/shard_map/convert_element_type | solution.py:83
  (35 shorter events, 2.8 us)
Async XLA Ops:
  18.1 4.6 %copy-start.2 = (s32[4,2]{0,1:T(2,128)S(1)}, s32[4,2]{0,1:T(2,128)}, u32[]{:S(2)}) copy-start(s32[4,2]{0,1:T(2,128)} %param.3) | copy-start | bytes 100
  18.1 4.6 %copy-start = (bf16[4096,256]{1,0:T(8,128)(2,1)S(1)}, bf16[4096,256]{1,0:T(8,128)(2,1)}, u32[]{:S(2)}) copy-start(bf16[4096,256]{1,0:T(8,128)(2,1)} %param.2) | copy-start | bytes 6291460
  18.1 51.1 %all-to-all-start.1 = ((bf16[4,2,512,256]{3,2,1,0:T(8,128)(2,1)}), bf16[4,2,512,256]{3,2,1,0:T(8,128)(2,1)}, u32[]{:S(2)}, u32[]{:S(2)}) async-start(bf16[4,2,512,256]{3,2,1,0:T(8,128)(2,1)} %broadcast_select_fusion), calls=%async_computation.1 | async-start | bytes 4194304 | tf_op jit(solution)/shard_map/all_to_all | solution.py:31
  69.2 18.0 %all-to-all-start = ((bf16[4,512,256]{2,1,0:T(8,128)(2,1)}), bf16[4,512,256]{2,1,0:T(8,128)(2,1)S(1)}, u32[]{:S(2)}, u32[]{:S(2)}) async-start(bf16[4,512,256]{2,1,0:T(8,128)(2,1)} %gather_fusion), calls=%async_computation | async-start | bytes 2097152 | tf_op jit(solution)/shard_map/all_to_all | solution.py:42
  87.2 1.0 copy-start.1
  88.2 18.0 %all-to-all-start.2 = ((bf16[4,512,256]{2,1,0:T(8,128)(2,1)}), bf16[4,512,256]{2,1,0:T(8,128)(2,1)S(1)}, u32[]{:S(2)}, u32[]{:S(2)}) async-start(bf16[4,512,256]{2,1,0:T(8,128)(2,1)} %gather_fusion.2), calls=%async_computation.2 | async-start | bytes 2097152 | tf_op jit(solution)/shard_map/all_to_all | solution.py:43
  117.0 19.9 %all-to-all-start.3 = ((bf16[4,2,512]{2,1,0:T(2,128)(2,1)}), bf16[4,2,512]{2,1,0:T(2,128)(2,1)S(1)}, u32[]{:S(2)}, u32[]{:S(2)}) async-start(bf16[4,2,512]{2,1,0:T(2,128)(2,1)} %convert_element_type.68), calls=%async_computation.3 | async-start | bytes 16384 | tf_op jit(solution)/shard_map/all_to_all | solution.py:65
  137.0 20.9 %all-to-all-start.4 = ((bf16[4,2,65536]{2,1,0:T(2,128)(2,1)}), bf16[4,2,65536]{2,1,0:T(2,128)(2,1)S(1)}, u32[]{:S(2)}, u32[]{:S(2)}) async-start(bf16[4,2,65536]{2,1,0:T(2,128)(2,1)} %reshape.331), calls=%async_computation.4 | async-start | bytes 2097152 | tf_op jit(solution)/shard_map/all_to_all | solution.py:54
where the time goes:
time: 173 us
  waiting for transfers between devices  68.6 us (40%)
  blocking collectives  31.1 us (18%)
  local copies, waits for them, and re-layouts  25.1 us (15%)
  other arithmetic  23.6 us (14%)
  starting transfers between devices  18.4 us (11%)
  matrix products  5.05 us (3%)
    all_to_all x1, waiting for transfers between devices, on_device(): lax.all_to_all(outgoing, 'wide', split_axis=0, concat_axis=0, tiled=True)  44.9 us
    all_gather x1, blocking collectives, on_device(): lax.all_gather(row_part, 'narrow', axis=0, tiled=True)  13.1 us
    all_gather x1, blocking collectives, on_device(): lax.all_gather(pair_list, 'wide', axis=0, tiled=True)  12.8 us
    all_to_all x1, waiting for transfers between devices, on_device(): lax.all_to_all(col_slices, 'narrow', split_axis=0, concat_axis=2, tiled=T...  12.7 us
    all_to_all x1, waiting for transfers between devices, on_device(): lax.all_to_all(row_slices, 'narrow', split_axis=0, concat_axis=2, tiled=T...  11 us
    unnamed x2, other arithmetic  8.09 us
    unnamed x10, local copies, waits for them, and re-layouts  6.47 us
    all_gather x1, blocking collectives, on_device(): lax.all_gather(col_part, 'narrow', axis=0, tiled=True)  5.15 us
  transfers between devices with their start and end apart: 5, of which 3 were waited for; matrix products, arithmetic and copies ran while one was open for 16% of the time, Pallas kernels for 0%

commit v1 on v0

v1 whole, which is shorter than its diff:
```python
import functools

import jax
import jax.numpy as jnp
from jax import lax
from jax.experimental import pallas as pl
from jax.experimental.pallas import tpu as pltpu
from jax.sharding import PartitionSpec as P

F = 1024
BR = 512
BLK_DEV = 8
CHUNKS = ((0, 256), (256, 128), (384, 128))
VMEM_LIMIT = 48 * 1024 * 1024


def vmem():
    return pl.BlockSpec(memory_space=pltpu.VMEM)


def smem():
    return pl.BlockSpec(memory_space=pltpu.SMEM)


def anywhere():
    return pl.BlockSpec(memory_space=pl.ANY)


def params():
    return pltpu.CompilerParams(vmem_limit_bytes=VMEM_LIMIT)


def pack_kernel(wide_count, pair_count, capacity, me_ref, pairs_ref, blocks_ref, *rest):
    outs, sems = rest[:-1], rest[-1]
    me = me_ref[0]
    copies = []
    for shift in range(1, wide_count):
        target = lax.rem(me + shift, wide_count)
        picks = [jnp.int32(0)] * capacity
        count = jnp.int32(0)
        for pair in range(pair_count):
            col = pairs_ref[target, 2 * pair + 1]
            mine = col // BLK_DEV == me
            local = lax.rem(col, BLK_DEV)
            for slot in range(capacity):
                picks[slot] = jnp.where(mine & (count == slot), local, picks[slot])
            count = count + mine.astype(jnp.int32)
        for chunk, (start, size) in enumerate(CHUNKS):
            out = outs[(shift - 1) * len(CHUNKS) + chunk]
            for slot in range(capacity):
                copies.append(
                    pltpu.make_async_copy(
                        blocks_ref.at[picks[slot], pl.ds(start, size)],
                        out.at[slot],
                        sems.at[len(copies)],
                    )
                )
                copies[-1].start()
    for copy in copies:
        copy.wait()


def pack(me, pairs, blocks, wide_count, pair_count, capacity):
    feat = blocks.shape[-1]
    shapes = [
        jax.ShapeDtypeStruct((capacity, size, feat), blocks.dtype)
        for _ in range(1, wide_count)
        for _, size in CHUNKS
    ]
    return pl.pallas_call(
        functools.partial(pack_kernel, wide_count, pair_count, capacity),
        out_shape=shapes,
        in_specs=[smem(), smem(), anywhere()],
        out_specs=[anywhere()] * len(shapes),
        scratch_shapes=[pltpu.SemaphoreType.DMA((len(shapes) * capacity,))],
        compiler_params=params(),
        name="pack",
    )(me, pairs, blocks)


def select_kernel(wide_count, pair_count, start, size, me_ref, pairs_ref, blocks_ref, *rest):
    received, out_ref, sems = rest[:-2], rest[-2], rest[-1]
    me = me_ref[0]
    owners = [pairs_ref[me, 2 * pair + 1] // BLK_DEV for pair in range(pair_count)]
    for pair in range(pair_count):
        local = lax.rem(pairs_ref[me, 2 * pair + 1], BLK_DEV)
        shift = lax.rem(me - owners[pair] + wide_count, wide_count)
        rank = jnp.int32(0)
        for before in range(pair):
            rank = rank + (owners[before] == owners[pair]).astype(jnp.int32)
        out = out_ref.at[pair]

        @pl.when(shift == 0)
        def _():
            pltpu.make_async_copy(
                blocks_ref.at[local, pl.ds(start, size)], out, sems.at[pair]
            ).start()

        for other in range(1, wide_count):

            @pl.when(shift == other)
            def _():
                pltpu.make_async_copy(received[other - 1].at[rank], out, sems.at[pair]).start()

    for pair in range(pair_count):
        pltpu.make_async_copy(
            blocks_ref.at[0, pl.ds(start, size)], out_ref.at[pair], sems.at[pair]
        ).wait()


def select(me, pairs, blocks, received, wide_count, pair_count, start, size):
    feat = blocks.shape[-1]
    return pl.pallas_call(
        functools.partial(select_kernel, wide_count, pair_count, start, size),
        out_shape=jax.ShapeDtypeStruct((pair_count, size, feat), blocks.dtype),
        in_specs=[smem(), smem()] + [anywhere()] * (1 + len(received)),
        out_specs=anywhere(),
        scratch_shapes=[pltpu.SemaphoreType.DMA((pair_count,))],
        compiler_params=params(),
        name="select",
    )(me, pairs, blocks, *received)


def tree(parts):
    while len(parts) > 1:
        half = len(parts) // 2
        parts = [parts[i] + parts[i + half] for i in range(half)]
    return parts[0]


def across(left, right):
    return lax.dot_general(
        left, right, (((1,), (1,)), ((), ())), preferred_element_type=jnp.float32
    )


def col_square(block):
    square = jnp.square(block.astype(jnp.float32))
    high = square.astype(jnp.bfloat16)
    low = (square - high.astype(jnp.float32)).astype(jnp.bfloat16)
    ones = jnp.ones((8, block.shape[1]), jnp.bfloat16)
    return (across(ones, high) + across(ones, low))[:1]


def kernel_kernel(narrow_count, first, *refs):
    rows = refs[:narrow_count]
    cols = refs[narrow_count : 2 * narrow_count]
    rest = refs[2 * narrow_count :]
    if first:
        kernel_ref, col_ref, mass_ref, square_ref = rest
    else:
        square_ref, before_ref, kernel_ref, col_ref, mass_ref = rest
    for pair in range(rows[0].shape[0]):
        if first:
            square = tree(
                [
                    jnp.sum(jnp.square(row[pair].astype(jnp.float32)), axis=1, keepdims=True)
                    for row in rows
                ]
            )
            square_ref[pair] = square
        else:
            square = square_ref[pair]
        gram = tree([across(row[pair], col[pair]) for row, col in zip(rows, cols)])
        other = tree([col_square(col[pair]) for col in cols])
        kernel = jnp.exp((square + other - 2.0 * gram) * (-1.0 / F))
        kernel_ref[pair] = kernel.astype(jnp.bfloat16)
        col_ref[pair : pair + 1] = jnp.sum(kernel, axis=0, keepdims=True)
        mass = jnp.sum(kernel, axis=1, keepdims=True)
        mass_ref[pair] = mass if first else before_ref[pair] + mass


def kernels(rows, cols, square, before, size):
    pair_count = rows[0].shape[0]
    first = square is None
    column = jax.ShapeDtypeStruct((pair_count, BR, 1), jnp.float32)
    shapes = [
        jax.ShapeDtypeStruct((pair_count, BR, size), jnp.bfloat16),
        jax.ShapeDtypeStruct((pair_count, size), jnp.float32),
        column,
    ] + ([column] if first else [])
    args = [*rows, *cols] + ([] if first else [square, before])
    return pl.pallas_call(
        functools.partial(kernel_kernel, len(rows), first),
        out_shape=shapes,
        in_specs=[vmem()] * len(args),
        out_specs=[vmem()] * len(shapes),
        compiler_params=params(),
        name="kernels",
    )(*args)


def mean_kernel(pair_count, local_ref, *refs):
    chunks = len(CHUNKS)
    kernel_refs, col_refs = refs[:chunks], refs[chunks : 2 * chunks]
    block_ref, mass_ref, out_ref, total, weight = refs[2 * chunks :]
    here = pl.program_id(0)
    total[...] = jnp.zeros_like(total)
    weight[...] = jnp.zeros_like(weight)
    for pair in range(pair_count):

        @pl.when(local_ref[pair] == here)
        def _():
            part = jnp.zeros(total.shape, jnp.float32)
            for kernel_ref, col_ref in zip(kernel_refs, col_refs):
                part = part + jnp.dot(
                    kernel_ref[pair], col_ref[pair], preferred_element_type=jnp.float32
                )
            total[...] += part.astype(jnp.bfloat16).astype(jnp.float32)
            weight[...] += mass_ref[pair]

    mean = (block_ref[0].astype(jnp.float32) + total[...]) / (1.0 + weight[...])
    out_ref[0] = mean.astype(jnp.bfloat16)


def means(row_local, kernel_parts, col_parts, blocks, mass):
    pair_count = mass.shape[0]
    feat = blocks.shape[-1]
    whole = [
        pl.BlockSpec(part.shape, lambda k, local: (0, 0, 0)) for part in [*kernel_parts, *col_parts]
    ]
    block = pl.BlockSpec((1, BR, feat), lambda k, local: (k, 0, 0))
    return pl.pallas_call(
        functools.partial(mean_kernel, pair_count),
        out_shape=jax.ShapeDtypeStruct(blocks.shape, jnp.bfloat16),
        grid_spec=pltpu.PrefetchScalarGridSpec(
            num_scalar_prefetch=1,
            grid=(BLK_DEV,),
            in_specs=[*whole, block, pl.BlockSpec(mass.shape, lambda k, local: (0, 0, 0))],
            out_specs=block,
            scratch_shapes=[
                pltpu.VMEM((BR, feat), jnp.float32),
                pltpu.VMEM((BR, 1), jnp.float32),
            ],
        ),
        compiler_params=params(),
        name="means",
    )(row_local, *kernel_parts, *col_parts, blocks, mass)


def gather_narrow(part):
    count = lax.axis_size("narrow")
    parts = [part]
    step = count // 2
    while step:
        perm = [(i, i ^ step) for i in range(count)]
        parts = parts + [lax.ppermute(x, "narrow", perm) for x in parts]
        step //= 2
    return parts


def on_device(embeddings, pair_list):
    wide_count = lax.axis_size("wide")
    me = lax.axis_index("wide").astype(jnp.int32).reshape(1)
    pair_count = pair_list.shape[0]
    capacity = max(2, 2 * pair_count // wide_count)
    feat = embeddings.shape[1]
    blocks = embeddings.reshape(BLK_DEV, BR, feat)
    row_local = pair_list[:, 0] % BLK_DEV
    rows = gather_narrow(blocks[row_local])
    every_pair = lax.all_gather(pair_list.reshape(1, 2 * pair_count), "wide", axis=0, tiled=True)
    outgoing = pack(me, every_pair, blocks, wide_count, pair_count, capacity)
    kernel_parts, col_parts, col_sums = [], [], []
    square = mass = None
    for chunk, (start, size) in enumerate(CHUNKS):
        received = [
            lax.ppermute(
                outgoing[(shift - 1) * len(CHUNKS) + chunk],
                "wide",
                [(i, (i + shift) % wide_count) for i in range(wide_count)],
            )
            for shift in range(1, wide_count)
        ]
        col_part = select(me, every_pair, blocks, received, wide_count, pair_count, start, size)
        cols = gather_narrow(col_part)
        if chunk == 0:
            kernel, col_sum, mass, square = kernels(rows, cols, None, None, size)
        else:
            kernel, col_sum, mass = kernels(rows, cols, square, mass, size)
        kernel_parts.append(kernel)
        col_parts.append(col_part)
        col_sums.append(col_sum)
    mean = means(row_local, kernel_parts, col_parts, blocks, mass)
    col_sum = jnp.concatenate(col_sums, axis=1)
    every_sum = lax.all_gather(col_sum, "wide", axis=0, tiled=True)
    mine = every_pair.reshape(-1, 2)[:, 1][None, :] == (
        me[0] * BLK_DEV + jnp.arange(BLK_DEV, dtype=jnp.int32)[:, None]
    )
    col_mass = jnp.sum(jnp.where(mine[:, :, None], every_sum[None], 0.0), axis=1)
    here = row_local[None, :] == jnp.arange(BLK_DEV, dtype=jnp.int32)[:, None]
    row_mass = jnp.sum(jnp.where(here[:, :, None], mass.reshape(pair_count, BR)[None], 0.0), axis=1)
    weights = 1.0 / (1.0 + (row_mass + col_mass) / BR)
    return weights.reshape(BLK_DEV * BR), mean.reshape(BLK_DEV * BR, feat)


def solution(mesh):
    in_specs = (P(("groups", "wide"), "narrow"), P(("groups", "wide"), None))
    out_specs = (P(("groups", "wide")), P(("groups", "wide"), "narrow"))
    return jax.shard_map(
        on_device, mesh=mesh, in_specs=in_specs, out_specs=out_specs, check_vma=False
    )
```

time: 173 us -> 131 us (0.76)
  waiting for transfers between devices: 68.6 us -> 35.8 us
  Pallas kernels: 0 us -> 32.3 us
  other arithmetic: 23.6 us -> 2.9 us
  local copies, waits for them, and re-layouts: 25.1 us -> 8.32 us
  blocking collectives: 31.1 us -> 24.2 us
  starting transfers between devices: 18.4 us -> 25.2 us
  matrix products: 5.05 us -> 0 us
    all_to_all x5 -> x0, waiting for transfers between devices: 68.6 us -> none  [the longest x1 44.9 us: on_device(): lax.all_to_all(outgoing, 'wide', split_axis=0, concat_axis=0, tiled=True)]
    ppermute x0 -> x21, waiting for transfers between devices: none -> 35.8 us  [the longest x9 28.6 us: on_device(): lax.ppermute(outgoing[(shift - 1) * len(CHUNKS) + chunk], 'wide', [(i, (i...]
    pallas_call x0 -> x8, Pallas kernels: none -> 32.3 us  [the longest x3 15 us: kernels(): pl.pallas_call(functools.partial(kernel_kernel, len(rows), first), out_sh...]
    ppermute x0 -> x21, starting transfers between devices: none -> 25.2 us  [the longest x9 17.5 us: on_device(): lax.ppermute(outgoing[(shift - 1) * len(CHUNKS) + chunk], 'wide', [(i, (i...]
    all_to_all x5 -> x0, starting transfers between devices: 18.4 us -> none  [the longest x1 4.57 us: on_device(): lax.all_to_all(outgoing, 'wide', split_axis=0, concat_axis=0, tiled=True)]
    convert_element_type x3 -> x0, local copies, waits for them, and re-layouts: 9.16 us -> none  [the longest x1 4.67 us: on_device(): sums_back.astype(jnp.float32)]
    unnamed x2, other arithmetic: 8.09 us -> 0.02 us
    all_gather x3 -> x2, blocking collectives: 31.1 us -> 24.2 us  [the longest x1 13.1 us: on_device(): every_sum = lax.all_gather(col_sum, 'wide', axis=0, tiled=True)]
  transfers between devices with their start and end apart: 5 -> 21, of which waited for: 3 -> 6; matrix products, arithmetic and copies ran while one was open for 16% -> 2% of each run, Pallas kernels for 0% -> 15%
where the time goes in v1:
time: 131 us; the launch traced here: 130 us
  waiting for transfers between devices  35.8 us (27%)
  Pallas kernels  32.3 us (25%)
  starting transfers between devices  25.2 us (19%)
  blocking collectives  24.2 us (18%)
  local copies, waits for them, and re-layouts  8.32 us (6%)
  other arithmetic  2.9 us (2%)
    ppermute x9, waiting for transfers between devices, on_device(): lax.ppermute(outgoing[(shift - 1) * len(CHUNKS) + chunk], 'wide', [(i, (i...  28.6 us
    ppermute x9, starting transfers between devices, on_device(): lax.ppermute(outgoing[(shift - 1) * len(CHUNKS) + chunk], 'wide', [(i, (i...  17.5 us
    pallas_call x3, Pallas kernels, kernels(): pl.pallas_call(functools.partial(kernel_kernel, len(rows), first), out_sh...  15 us
    all_gather x1, blocking collectives, on_device(): every_sum = lax.all_gather(col_sum, 'wide', axis=0, tiled=True)  13.1 us
    all_gather x1, blocking collectives, on_device(): lax.all_gather(pair_list.reshape(1, 2 * pair_count), 'wide', axis=0, tile...  11.1 us
    pallas_call x1, Pallas kernels, means(): pl.pallas_call(functools.partial(mean_kernel, pair_count), out_shape=jax....  7.74 us
    ppermute x12, starting transfers between devices, gather_narrow(): parts = parts + [lax.ppermute(x, 'narrow', perm) for x in parts]  7.73 us
    ppermute x12, waiting for transfers between devices, gather_narrow(): parts = parts + [lax.ppermute(x, 'narrow', perm) for x in parts]  7.24 us
  transfers between devices with their start and end apart: 21, of which 6 were waited for; matrix products, arithmetic and copies ran while one was open for 2% of the time, Pallas kernels for 15%

profile of v1, /device:TPU:0, one launch (start us, length us, event | category | flops | bytes accessed | tf_op | source)
XLA Modules:
  0.0 129.5 jit_solution(17383913597774052984)
XLA Ops:
  0.7 0.8 fusion.2
  1.5 2.2 %gather_fusion = bf16[4,512,256]{2,1,0:T(8,128)(2,1)S(1)} fusion(bf16[8,512,256]{2,1,0:T(8,128)(2,1)} %bitcast.13, s32[1024]{0:T(1024)S(1)} %pad_clamp_fusion), kind=kCustom, calls=%fused_computation | custom fusion | bytes 2097168 | tf_op jit(solution)/shard_map/gather | solution.py:260
  3.7 3.0 %collective-permute-start = (bf16[4,512,256]{2,1,0:T(8,128)(2,1)S(1)}, bf16[4,512,256]{2,1,0:T(8,128)(2,1)}, u32[]{:S(2)}, u32[]{:S(2)}) collective-permute-start(bf16[4,512,256]{2,1,0:T(8,128)(2,1)S(1)} %gather_fusion), channel_id=1, source_target_pairs={{0,2},{1,3},{2,0},{3,1},{4,6},{5,7},{6,4},{7,5},{8,10},{9,11},{10,... | collective-permute-start | bytes 3145736 | tf_op jit(solution)/shard_map/ppermute | solution.py:247
  6.9 11.1 %all-gather = s32[4,1,8]{2,1,0:T(1,128)S(1)} all-gather(s32[1,1,8]{2,1,0:T(1,128)S(1)} %reshape.117), channel_id=1, replica_groups=mesh['groups'=2,'wide'=4,'narrow'=4] {'wide'}, dimensions={0}, use_global_device_ids=true | all-gather | bytes 160 | tf_op jit(solution)/shard_map/all_gather | solution.py:261
  18.0 3.3 %pack.1 = (bf16[2,256,256]{2,1,0:T(8,128)(2,1)S(1)}, bf16[2,128,256]{2,1,0:T(8,128)(2,1)S(1)}, bf16[2,128,256]{2,1,0:T(8,128)(2,1)S(1)}, bf16[2,256,256]{2,1,0:T...) custom-call(s32[1]{0:T(128)} %bitcast.3.me_ref, ...), custom_call_target="tpu_custom_call" | custom-call | tf_op jit(solution)/shard_map/pack/pallas_call | solution.py:70
  21.4 1.0 collective-permute-start.11
  22.4 1.1 collective-permute-start.9
  23.5 15.6 %collective-permute-done.10.rest_1_ = bf16[2,256,256]{2,1,0:T(8,128)(2,1)S(1)} collective-permute-done((bf16[2,256,256]{2,1,0:T(8,128)(2,1)S(1)}, bf16[2,256,256]{2,1,0:T(8,128)(2,1)S(1)}, u32[]{:S(2)}, u32[]{:S(2)}) %collective-permute-start.10) | collective-permute-done | bytes 262176 | tf_op jit(solution)/shard_map/ppermute | solution.py:267
  39.1 1.4 %select.16.refs_4_.refs_3_ = bf16[4,256,256]{2,1,0:T(8,128)(2,1)} custom-call(s32[1]{0:T(128)} %bitcast.3.me_ref, s32[4,8]{1,0:T(4,128)S(1)} %bitcast.20, bf16[8,512,256]{2,1,0:T(8,128)(2,1)S(1)} %bitcast.16, bf16[2,256,256]{2,1,0:T(8,128)(2,1)S(1)} %collective-permute-done.9.rest_0_, bf16[2,256,256]{2,1,0:T(8,128)(2,1)S(1)} %collective-permute-done.10.rest_1_, ...), custom_call_target="tpu_custom_call" | custom-call | tf_op jit(solution)/shard_map/select/pallas_call | solution.py:113
  41.1 4.9 %collective-permute-start.15 = (bf16[2,128,256]{2,1,0:T(8,128)(2,1)S(1)}, bf16[2,128,256]{2,1,0:T(8,128)(2,1)S(1)}, u32[]{:S(2)}, u32[]{:S(2)}) collective-permute-start(bf16[2,128,256]{2,1,0:T(8,128)(2,1)S(1)} %get-tuple-element.28), channel_id=1, source_target_pairs={{0,4},{4,8},{8,12},{12,0},{1,5},{5,9},{9,13},{13,1},{2,6},{6,10},{... | collective-permute-start | bytes 393224 | tf_op jit(solution)/shard_map/ppermute | solution.py:267
  46.2 3.6 %collective-permute-done.15.rest_0_ = bf16[2,128,256]{2,1,0:T(8,128)(2,1)S(1)} collective-permute-done((bf16[2,128,256]{2,1,0:T(8,128)(2,1)S(1)}, bf16[2,128,256]{2,1,0:T(8,128)(2,1)S(1)}, u32[]{:S(2)}, u32[]{:S(2)}) %collective-permute-start.15) | collective-permute-done | bytes 131104 | tf_op jit(solution)/shard_map/ppermute | solution.py:267
  49.8 1.9 %collective-permute-start.17 = (bf16[2,128,256]{2,1,0:T(8,128)(2,1)S(1)}, bf16[2,128,256]{2,1,0:T(8,128)(2,1)S(1)}, u32[]{:S(2)}, u32[]{:S(2)}) collective-permute-start(bf16[2,128,256]{2,1,0:T(8,128)(2,1)S(1)} %get-tuple-element.30), channel_id=1, source_target_pairs={{0,12},{4,0},{8,4},{12,8},{1,13},{5,1},{9,5},{13,9},{2,14},{6,2},{... | collective-permute-start | bytes 393224 | tf_op jit(solution)/shard_map/ppermute | solution.py:267
  51.8 3.8 %collective-permute-done.16.rest_1_ = bf16[2,128,256]{2,1,0:T(8,128)(2,1)S(1)} collective-permute-done((bf16[2,128,256]{2,1,0:T(8,128)(2,1)S(1)}, bf16[2,128,256]{2,1,0:T(8,128)(2,1)S(1)}, u32[]{:S(2)}, u32[]{:S(2)}) %collective-permute-start.16) | collective-permute-done | bytes 131104 | tf_op jit(solution)/shard_map/ppermute | solution.py:267
  55.6 2.9 %collective-permute-start.3 = (bf16[2,128,256]{2,1,0:T(8,128)(2,1)S(1)}, bf16[2,128,256]{2,1,0:T(8,128)(2,1)S(1)}, u32[]{:S(2)}, u32[]{:S(2)}) collective-permute-start(bf16[2,128,256]{2,1,0:T(8,128)(2,1)S(1)} %get-tuple-element.21), channel_id=1, source_target_pairs={{0,4},{4,8},{8,12},{12,0},{1,5},{5,9},{9,13},{13,1},{2,6},{6,10},{... | collective-permute-start | bytes 393224 | tf_op jit(solution)/shard_map/ppermute | solution.py:267
  58.6 3.4 %collective-permute-start.4 = (bf16[2,128,256]{2,1,0:T(8,128)(2,1)S(1)}, bf16[2,128,256]{2,1,0:T(8,128)(2,1)S(1)}, u32[]{:S(2)}, u32[]{:S(2)}) collective-permute-start(bf16[2,128,256]{2,1,0:T(8,128)(2,1)S(1)} %get-tuple-element.22), channel_id=1, source_target_pairs={{0,8},{4,12},{8,0},{12,4},{1,9},{5,13},{9,1},{13,5},{2,10},{6,14},... | collective-permute-start | bytes 393224 | tf_op jit(solution)/shard_map/ppermute | solution.py:267
  61.9 3.9 %collective-permute-done.3.rest_0_ = bf16[2,128,256]{2,1,0:T(8,128)(2,1)S(1)} collective-permute-done((bf16[2,128,256]{2,1,0:T(8,128)(2,1)S(1)}, bf16[2,128,256]{2,1,0:T(8,128)(2,1)S(1)}, u32[]{:S(2)}, u32[]{:S(2)}) %collective-permute-start.3) | collective-permute-done | bytes 131104 | tf_op jit(solution)/shard_map/ppermute | solution.py:267
  65.8 1.9 %collective-permute-start.5 = (bf16[2,128,256]{2,1,0:T(8,128)(2,1)}, bf16[2,128,256]{2,1,0:T(8,128)(2,1)}, u32[]{:S(2)}, u32[]{:S(2)}) collective-permute-start(bf16[2,128,256]{2,1,0:T(8,128)(2,1)} %get-tuple-element.23), channel_id=1, source_target_pairs={{0,12},{4,0},{8,4},{12,8},{1,13},{5,1},{9,5},{13,9},{2,14},{6,2},{... | collective-permute-start | bytes 393224 | tf_op jit(solution)/shard_map/ppermute | solution.py:267
  67.8 1.1 select.17.refs_4_
  68.8 1.7 %collective-permute-done.4.rest_1_ = bf16[2,128,256]{2,1,0:T(8,128)(2,1)S(1)} collective-permute-done((bf16[2,128,256]{2,1,0:T(8,128)(2,1)S(1)}, bf16[2,128,256]{2,1,0:T(8,128)(2,1)S(1)}, u32[]{:S(2)}, u32[]{:S(2)}) %collective-permute-start.4) | collective-permute-done | bytes 131104 | tf_op jit(solution)/shard_map/ppermute | solution.py:267
  71.2 1.5 %collective-permute-start.18 = (bf16[4,128,256]{2,1,0:T(8,128)(2,1)S(1)}, bf16[4,128,256]{2,1,0:T(8,128)(2,1)}, u32[]{:S(2)}, u32[]{:S(2)}) collective-permute-start(bf16[4,128,256]{2,1,0:T(8,128)(2,1)S(1)} %select.17.refs_4_), channel_id=1, source_target_pairs={{0,2},{1,3},{2,0},{3,1},{4,6},{5,7},{6,4},{7,5},{8,10},{9,11},{10,... | collective-permute-start | bytes 786440 | tf_op jit(solution)/shard_map/ppermute | solution.py:247
  75.2 0.9 copy-done.9
  76.1 3.7 %select.15.refs_4_.refs_5_ = bf16[4,128,256]{2,1,0:T(8,128)(2,1)} custom-call(s32[1]{0:T(128)} %bitcast.3.me_ref, s32[4,8]{1,0:T(4,128)S(1)} %bitcast.22, bf16[8,512,256]{2,1,0:T(8,128)(2,1)S(1)} %bitcast.18, bf16[2,128,256]{2,1,0:T(8,128)(2,1)S(1)} %collective-permute-done.3.rest_0_, bf16[2,128,256]{2,1,0:T(8,128)(2,1)S(1)} %copy-done.9, ...), custom_call_target="tpu_custom_call" | custom-call | tf_op jit(solution)/shard_map/select/pallas_call | solution.py:113
  79.8 1.1 collective-permute-start.6
  81.1 7.2 %collective-permute-done.6.refs_5_ = bf16[4,128,256]{2,1,0:T(8,128)(2,1)S(1)} collective-permute-done((bf16[4,128,256]{2,1,0:T(8,128)(2,1)}, bf16[4,128,256]{2,1,0:T(8,128)(2,1)S(1)}, u32[]{:S(2)}, u32[]{:S(2)}) %collective-permute-start.6) | collective-permute-done | bytes 262176 | tf_op jit(solution)/shard_map/ppermute | solution.py:247
  89.5 5.9 %kernels.3 = (bf16[4,512,256]{2,1,0:T(8,128)(2,1)S(1)}, f32[4,256]{1,0:T(4,128)S(1)}, f32[4,512,1]{2,1,0:T(8,128)S(1)}, f32[4,512,1]{2,1,0:T(8,128)S(1)}) custom-call(bf16[4,512,256]{2,1,0:T(8,128)(2,1)} %copy-done.1, bf16[4,512,256]{2,1,0:T(8,128)(2,1)} %collective-permute-done.refs_1_, bf16[4,512,256]{2,1,0:T(8,128)(2,1)} %collective-permute-done.1.refs_2_, ...), custom_call_target="tpu_custom_call" | custom-call | tf_op jit(solution)/shard_map/kernels/pallas_call | solution.py:183
  95.4 1.0 copy-done.3
  96.3 1.0 copy-done.5
  97.3 4.6 %kernels.4 = (bf16[4,512,128]{2,1,0:T(8,128)(2,1)S(1)}, f32[4,128]{1,0:T(4,128)S(1)}, f32[4,512,1]{2,1,0:T(8,128)S(1)}) custom-call(bf16[4,512,256]{2,1,0:T(8,128)(2,1)S(1)} %copy-done.2, bf16[4,512,256]{2,1,0:T(8,128)(2,1)} %collective-permute-done.refs_1_, bf16[4,512,256]{2,1,0:T(8,128)(2,1)} %collective-permute-done.1.refs_2_, ...), custom_call_target="tpu_custom_call" | custom-call | tf_op jit(solution)/shard_map/kernels/pallas_call | solution.py:183
  101.9 1.0 copy-done.4
  102.9 4.5 %kernels.5 = (bf16[4,512,128]{2,1,0:T(8,128)(2,1)S(1)}, f32[4,128]{1,0:T(4,128)S(1)}, f32[4,512,1]{2,1,0:T(8,128)S(1)}) custom-call(bf16[4,512,256]{2,1,0:T(8,128)(2,1)S(1)} %copy-done.2, bf16[4,512,256]{2,1,0:T(8,128)(2,1)} %collective-permute-done.refs_1_, bf16[4,512,256]{2,1,0:T(8,128)(2,1)} %collective-permute-done.1.refs_2_, ...), custom_call_target="tpu_custom_call" | custom-call | tf_op jit(solution)/shard_map/kernels/pallas_call | solution.py:183
  107.5 13.1 %all-gather.1 = f32[4,4,512]{2,1,0:T(4,128)S(1)} all-gather(f32[1,4,512]{2,1,0:T(4,128)S(1)} %maximum_bitcast_fusion), channel_id=1, replica_groups=mesh['groups'=2,'wide'=4,'narrow'=4] {'wide'}, dimensions={0}, use_global_device_ids=true | all-gather | bytes 40960 | tf_op jit(solution)/shard_map/all_gather | solution.py:285
  121.8 7.7 %means.1 = bf16[8,512,256]{2,1,0:T(8,128)(2,1)} custom-call(s32[4]{0:T(128)S(1)} %and_select_fusion.1.local_ref, bf16[4,512,256]{2,1,0:T(8,128)(2,1)S(1)} %get-tuple-element.37.refs_0_, bf16[4,512,128]{2,1,0:T(8,128)(2,1)S(1)} %get-tuple-element.38.refs_1_, bf16[4,512,128]{2,1,0:T(8,128)(2,1)S(1)} %get-tuple-element.39.refs_2_, ...), custom_call_target="tpu_custom_call" | custom-call | tf_op jit(solution)/shard_map/means/pallas_call | solution.py:223
  (62 shorter events, 6.8 us)
Async XLA Ops:
  0.6 6.1 %copy-start.10 = (s32[4,2]{0,1:T(2,128)S(1)}, s32[4,2]{0,1:T(2,128)}, u32[]{:S(2)}) copy-start(s32[4,2]{0,1:T(2,128)} %param.3) | copy-start | bytes 100
  0.6 17.4 %copy-start = (bf16[4096,256]{1,0:T(8,128)(2,1)S(1)}, bf16[4096,256]{1,0:T(8,128)(2,1)}, u32[]{:S(2)}) copy-start(bf16[4096,256]{1,0:T(8,128)(2,1)} %param.2) | copy-start | bytes 6291460
  3.7 37.4 %copy-start.1 = (bf16[4,512,256]{2,1,0:T(8,128)(2,1)}, bf16[4,512,256]{2,1,0:T(8,128)(2,1)S(1)}, u32[]{:S(2)}) copy-start(bf16[4,512,256]{2,1,0:T(8,128)(2,1)S(1)} %gather_fusion) | copy-start | bytes 3145732
  3.7 58.2 %collective-permute-start = (bf16[4,512,256]{2,1,0:T(8,128)(2,1)S(1)}, bf16[4,512,256]{2,1,0:T(8,128)(2,1)}, u32[]{:S(2)}, u32[]{:S(2)}) collective-permute-start(bf16[4,512,256]{2,1,0:T(8,128)(2,1)S(1)} %gather_fusion), channel_id=1, source_target_pairs={{0,2},{1,3},{2,0},{3,1},{4,6},{5,7},{6,4},{7,5},{8,10},{9,11},{10,... | collective-permute-start | bytes 3145736 | tf_op jit(solution)/shard_map/ppermute | solution.py:247
  21.4 17.7 %collective-permute-start.10 = (bf16[2,256,256]{2,1,0:T(8,128)(2,1)S(1)}, bf16[2,256,256]{2,1,0:T(8,128)(2,1)S(1)}, u32[]{:S(2)}, u32[]{:S(2)}) collective-permute-start(bf16[2,256,256]{2,1,0:T(8,128)(2,1)S(1)} %get-tuple-element.25), channel_id=1, source_target_pairs={{0,8},{4,12},{8,0},{12,4},{1,9},{5,13},{9,1},{13,5},{2,10},{6,14},... | collective-permute-start | bytes 786440 | tf_op jit(solution)/shard_map/ppermute | solution.py:267
  21.4 17.6 %collective-permute-start.11 = (bf16[2,256,256]{2,1,0:T(8,128)(2,1)S(1)}, bf16[2,256,256]{2,1,0:T(8,128)(2,1)S(1)}, u32[]{:S(2)}, u32[]{:S(2)}) collective-permute-start(bf16[2,256,256]{2,1,0:T(8,128)(2,1)S(1)} %get-tuple-element.26), channel_id=1, source_target_pairs={{0,12},{4,0},{8,4},{12,8},{1,13},{5,1},{9,5},{13,9},{2,14},{6,2},{... | collective-permute-start | bytes 786440 | tf_op jit(solution)/shard_map/ppermute | solution.py:267
  22.4 16.6 %collective-permute-start.9 = (bf16[2,256,256]{2,1,0:T(8,128)(2,1)S(1)}, bf16[2,256,256]{2,1,0:T(8,128)(2,1)S(1)}, u32[]{:S(2)}, u32[]{:S(2)}) collective-permute-start(bf16[2,256,256]{2,1,0:T(8,128)(2,1)S(1)} %get-tuple-element.24), channel_id=1, source_target_pairs={{0,4},{4,8},{8,12},{12,0},{1,5},{5,9},{9,13},{13,1},{2,6},{6,10},{... | collective-permute-start | bytes 786440 | tf_op jit(solution)/shard_map/ppermute | solution.py:267
  40.5 33.5 %collective-permute-start.12 = (bf16[4,256,256]{2,1,0:T(8,128)(2,1)}, bf16[4,256,256]{2,1,0:T(8,128)(2,1)}, u32[]{:S(2)}, u32[]{:S(2)}) collective-permute-start(bf16[4,256,256]{2,1,0:T(8,128)(2,1)} %select.16.refs_4_.refs_3_), channel_id=1, source_target_pairs={{0,2},{1,3},{2,0},{3,1},{4,6},{5,7},{6,4},{7,5},{8,10},{9,11},{10,... | collective-permute-start | bytes 1572872 | tf_op jit(solution)/shard_map/ppermute | solution.py:247
  41.1 47.8 %collective-permute-start.1 = (bf16[4,512,256]{2,1,0:T(8,128)(2,1)S(1)}, bf16[4,512,256]{2,1,0:T(8,128)(2,1)}, u32[]{:S(2)}, u32[]{:S(2)}) collective-permute-start(bf16[4,512,256]{2,1,0:T(8,128)(2,1)S(1)} %gather_fusion), channel_id=1, source_target_pairs={{0,1},{1,0},{2,3},{3,2},{4,5},{5,4},{6,7},{7,6},{8,9},{9,8},{10,11... | collective-permute-start | bytes 3145736 | tf_op jit(solution)/shard_map/ppermute | solution.py:247
  41.1 8.7 %collective-permute-start.15 = (bf16[2,128,256]{2,1,0:T(8,128)(2,1)S(1)}, bf16[2,128,256]{2,1,0:T(8,128)(2,1)S(1)}, u32[]{:S(2)}, u32[]{:S(2)}) collective-permute-start(bf16[2,128,256]{2,1,0:T(8,128)(2,1)S(1)} %get-tuple-element.28), channel_id=1, source_target_pairs={{0,4},{4,8},{8,12},{12,0},{1,5},{5,9},{9,13},{13,1},{2,6},{6,10},{... | collective-permute-start | bytes 393224 | tf_op jit(solution)/shard_map/ppermute | solution.py:267
  46.0 9.6 %collective-permute-start.16 = (bf16[2,128,256]{2,1,0:T(8,128)(2,1)S(1)}, bf16[2,128,256]{2,1,0:T(8,128)(2,1)S(1)}, u32[]{:S(2)}, u32[]{:S(2)}) collective-permute-start(bf16[2,128,256]{2,1,0:T(8,128)(2,1)S(1)} %get-tuple-element.29), channel_id=1, source_target_pairs={{0,8},{4,12},{8,0},{12,4},{1,9},{5,13},{9,1},{13,5},{2,10},{6,14},... | collective-permute-start | bytes 393224 | tf_op jit(solution)/shard_map/ppermute | solution.py:267
  49.8 8.7 %collective-permute-start.17 = (bf16[2,128,256]{2,1,0:T(8,128)(2,1)S(1)}, bf16[2,128,256]{2,1,0:T(8,128)(2,1)S(1)}, u32[]{:S(2)}, u32[]{:S(2)}) collective-permute-start(bf16[2,128,256]{2,1,0:T(8,128)(2,1)S(1)} %get-tuple-element.30), channel_id=1, source_target_pairs={{0,12},{4,0},{8,4},{12,8},{1,13},{5,1},{9,5},{13,9},{2,14},{6,2},{... | collective-permute-start | bytes 393224 | tf_op jit(solution)/shard_map/ppermute | solution.py:267
  55.6 10.2 %collective-permute-start.3 = (bf16[2,128,256]{2,1,0:T(8,128)(2,1)S(1)}, bf16[2,128,256]{2,1,0:T(8,128)(2,1)S(1)}, u32[]{:S(2)}, u32[]{:S(2)}) collective-permute-start(bf16[2,128,256]{2,1,0:T(8,128)(2,1)S(1)} %get-tuple-element.21), channel_id=1, source_target_pairs={{0,4},{4,8},{8,12},{12,0},{1,5},{5,9},{9,13},{13,1},{2,6},{6,10},{... | collective-permute-start | bytes 393224 | tf_op jit(solution)/shard_map/ppermute | solution.py:267
  58.6 12.0 %collective-permute-start.4 = (bf16[2,128,256]{2,1,0:T(8,128)(2,1)S(1)}, bf16[2,128,256]{2,1,0:T(8,128)(2,1)S(1)}, u32[]{:S(2)}, u32[]{:S(2)}) collective-permute-start(bf16[2,128,256]{2,1,0:T(8,128)(2,1)S(1)} %get-tuple-element.22), channel_id=1, source_target_pairs={{0,8},{4,12},{8,0},{12,4},{1,9},{5,13},{9,1},{13,5},{2,10},{6,14},... | collective-permute-start | bytes 393224 | tf_op jit(solution)/shard_map/ppermute | solution.py:267
  61.9 27.5 %collective-permute-start.2 = (bf16[4,512,256]{2,1,0:T(8,128)(2,1)}, bf16[4,512,256]{2,1,0:T(8,128)(2,1)}, u32[]{:S(2)}, u32[]{:S(2)}) collective-permute-start(bf16[4,512,256]{2,1,0:T(8,128)(2,1)} %collective-permute-done.refs_1_), channel_id=1, source_target_pairs={{0,1},{1,0},{2,3},{3,2},{4,5},{5,4},{6,7},{7,6},{8,9},{9,8},{10,11... | collective-permute-start | bytes 3145736 | tf_op jit(solution)/shard_map/ppermute | solution.py:247
  65.8 8.1 %collective-permute-start.5 = (bf16[2,128,256]{2,1,0:T(8,128)(2,1)}, bf16[2,128,256]{2,1,0:T(8,128)(2,1)}, u32[]{:S(2)}, u32[]{:S(2)}) collective-permute-start(bf16[2,128,256]{2,1,0:T(8,128)(2,1)} %get-tuple-element.23), channel_id=1, source_target_pairs={{0,12},{4,0},{8,4},{12,8},{1,13},{5,1},{9,5},{13,9},{2,14},{6,2},{... | collective-permute-start | bytes 393224 | tf_op jit(solution)/shard_map/ppermute | solution.py:267
  70.5 0.6 copy-start.8
  71.2 8.6 %collective-permute-start.18 = (bf16[4,128,256]{2,1,0:T(8,128)(2,1)S(1)}, bf16[4,128,256]{2,1,0:T(8,128)(2,1)}, u32[]{:S(2)}, u32[]{:S(2)}) collective-permute-start(bf16[4,128,256]{2,1,0:T(8,128)(2,1)S(1)} %select.17.refs_4_), channel_id=1, source_target_pairs={{0,2},{1,3},{2,0},{3,1},{4,6},{5,7},{6,4},{7,5},{8,10},{9,11},{10,... | collective-permute-start | bytes 786440 | tf_op jit(solution)/shard_map/ppermute | solution.py:247
  73.9 14.4 %collective-permute-start.13 = (bf16[4,256,256]{2,1,0:T(8,128)(2,1)}, bf16[4,256,256]{2,1,0:T(8,128)(2,1)}, u32[]{:S(2)}, u32[]{:S(2)}) collective-permute-start(bf16[4,256,256]{2,1,0:T(8,128)(2,1)} %select.16.refs_4_.refs_3_), channel_id=1, source_target_pairs={{0,1},{1,0},{2,3},{3,2},{4,5},{5,4},{6,7},{7,6},{8,9},{9,8},{10,11... | collective-permute-start | bytes 1572872 | tf_op jit(solution)/shard_map/ppermute | solution.py:247
  74.0 15.0 %collective-permute-start.14 = (bf16[4,256,256]{2,1,0:T(8,128)(2,1)}, bf16[4,256,256]{2,1,0:T(8,128)(2,1)}, u32[]{:S(2)}, u32[]{:S(2)}) collective-permute-start(bf16[4,256,256]{2,1,0:T(8,128)(2,1)} %collective-permute-done.12.refs_5_), channel_id=1, source_target_pairs={{0,1},{1,0},{2,3},{3,2},{4,5},{5,4},{6,7},{7,6},{8,9},{9,8},{10,11... | collective-permute-start | bytes 1572872 | tf_op jit(solution)/shard_map/ppermute | solution.py:247
  75.1 0.9 copy-start.9
  79.8 8.6 %collective-permute-start.6 = (bf16[4,128,256]{2,1,0:T(8,128)(2,1)}, bf16[4,128,256]{2,1,0:T(8,128)(2,1)S(1)}, u32[]{:S(2)}, u32[]{:S(2)}) collective-permute-start(bf16[4,128,256]{2,1,0:T(8,128)(2,1)} %select.15.refs_4_.refs_5_), channel_id=1, source_target_pairs={{0,2},{1,3},{2,0},{3,1},{4,6},{5,7},{6,4},{7,5},{8,10},{9,11},{10,... | collective-permute-start | bytes 786440 | tf_op jit(solution)/shard_map/ppermute | solution.py:247
  88.4 7.0 %copy-start.6 = (bf16[4,128,256]{2,1,0:T(8,128)(2,1)}, bf16[4,128,256]{2,1,0:T(8,128)(2,1)S(1)}, u32[]{:S(2)}) copy-start(bf16[4,128,256]{2,1,0:T(8,128)(2,1)S(1)} %collective-permute-done.6.refs_5_) | copy-start | bytes 786436
  88.4 9.0 %collective-permute-start.19 = (bf16[4,128,256]{2,1,0:T(8,128)(2,1)S(1)}, bf16[4,128,256]{2,1,0:T(8,128)(2,1)S(1)}, u32[]{:S(2)}, u32[]{:S(2)}) collective-permute-start(bf16[4,128,256]{2,1,0:T(8,128)(2,1)S(1)} %select.17.refs_4_), channel_id=1, source_target_pairs={{0,1},{1,0},{2,3},{3,2},{4,5},{5,4},{6,7},{7,6},{8,9},{9,8},{10,11... | collective-permute-start | bytes 786440 | tf_op jit(solution)/shard_map/ppermute | solution.py:247
  88.4 14.5 %collective-permute-start.7 = (bf16[4,128,256]{2,1,0:T(8,128)(2,1)}, bf16[4,128,256]{2,1,0:T(8,128)(2,1)S(1)}, u32[]{:S(2)}, u32[]{:S(2)}) collective-permute-start(bf16[4,128,256]{2,1,0:T(8,128)(2,1)} %select.15.refs_4_.refs_5_), channel_id=1, source_target_pairs={{0,1},{1,0},{2,3},{3,2},{4,5},{5,4},{6,7},{7,6},{8,9},{9,8},{10,11... | collective-permute-start | bytes 786440 | tf_op jit(solution)/shard_map/ppermute | solution.py:247
  88.9 8.4 %collective-permute-start.20 = (bf16[4,128,256]{2,1,0:T(8,128)(2,1)}, bf16[4,128,256]{2,1,0:T(8,128)(2,1)S(1)}, u32[]{:S(2)}, u32[]{:S(2)}) collective-permute-start(bf16[4,128,256]{2,1,0:T(8,128)(2,1)} %collective-permute-done.18.refs_5_), channel_id=1, source_target_pairs={{0,1},{1,0},{2,3},{3,2},{4,5},{5,4},{6,7},{7,6},{8,9},{9,8},{10,11... | collective-permute-start | bytes 786440 | tf_op jit(solution)/shard_map/ppermute | solution.py:247
  88.9 14.0 %collective-permute-start.8 = (bf16[4,128,256]{2,1,0:T(8,128)(2,1)S(1)}, bf16[4,128,256]{2,1,0:T(8,128)(2,1)S(1)}, u32[]{:S(2)}, u32[]{:S(2)}) collective-permute-start(bf16[4,128,256]{2,1,0:T(8,128)(2,1)S(1)} %collective-permute-done.6.refs_5_), channel_id=1, source_target_pairs={{0,1},{1,0},{2,3},{3,2},{4,5},{5,4},{6,7},{7,6},{8,9},{9,8},{10,11... | collective-permute-start | bytes 786440 | tf_op jit(solution)/shard_map/ppermute | solution.py:247
  89.5 7.9 %copy-start.2 = (bf16[4,512,256]{2,1,0:T(8,128)(2,1)S(1)}, bf16[4,512,256]{2,1,0:T(8,128)(2,1)}, u32[]{:S(2)}) copy-start(bf16[4,512,256]{2,1,0:T(8,128)(2,1)} %copy-done.1) | copy-start | bytes 3145732
  95.4 1.0 copy-start.3
  96.3 1.0 copy-start.5
  97.3 5.6 %copy-start.7 = (bf16[4,128,256]{2,1,0:T(8,128)(2,1)S(1)}, bf16[4,128,256]{2,1,0:T(8,128)(2,1)}, u32[]{:S(2)}) copy-start(bf16[4,128,256]{2,1,0:T(8,128)(2,1)} %copy-done.6) | copy-start | bytes 786436
  101.9 1.0 copy-start.4

commit v2 on v1

v2 whole, which is shorter than its diff:
```python
import functools

import jax
import jax.numpy as jnp
from jax import lax
from jax.experimental import pallas as pl
from jax.experimental.pallas import tpu as pltpu
from jax.sharding import PartitionSpec as P

F = 1024
BR = 512
BLK_DEV = 8
LANES = 128
CHUNKS = ((0, 384), (384, 128))
VMEM_LIMIT = 48 * 1024 * 1024


def smem():
    return pl.BlockSpec(memory_space=pltpu.SMEM)


def anywhere():
    return pl.BlockSpec(memory_space=pl.ANY)


def params():
    return pltpu.CompilerParams(vmem_limit_bytes=VMEM_LIMIT)


def pack_kernel(wide_count, pair_count, capacity, me_ref, pairs_ref, blocks_ref, *rest):
    outs, rows_ref, sems = rest[: len(CHUNKS)], rest[-2], rest[-1]
    me = me_ref[0]
    copies = []

    def send(source, target):
        copies.append(pltpu.make_async_copy(source, target, sems.at[len(copies)]))
        copies[-1].start()

    for target in range(wide_count):
        picks = [jnp.int32(0)] * capacity
        count = jnp.int32(0)
        for pair in range(pair_count):
            col = pairs_ref[target, 2 * pair + 1]
            mine = (col >> 3) == me
            for slot in range(capacity):
                picks[slot] = jnp.where(mine & (count == slot), col & 7, picks[slot])
            count = count + mine.astype(jnp.int32)
        for slot in range(capacity):
            for out, (start, size) in zip(outs, CHUNKS):
                send(blocks_ref.at[picks[slot], pl.ds(start, size)], out.at[target, slot])
    for pair in range(pair_count):
        send(blocks_ref.at[pairs_ref[me, 2 * pair] & 7], rows_ref.at[pair])
    for copy in copies:
        copy.wait()


def pack(me, pairs, blocks, wide_count, pair_count, capacity):
    feat = blocks.shape[-1]
    shapes = [
        jax.ShapeDtypeStruct((wide_count, capacity, size, feat), blocks.dtype)
        for _, size in CHUNKS
    ] + [jax.ShapeDtypeStruct((pair_count, BR, feat), blocks.dtype)]
    copies = wide_count * capacity * len(CHUNKS) + pair_count
    return pl.pallas_call(
        functools.partial(pack_kernel, wide_count, pair_count, capacity),
        out_shape=shapes,
        in_specs=[smem(), smem(), anywhere()],
        out_specs=[anywhere()] * len(shapes),
        scratch_shapes=[pltpu.SemaphoreType.DMA((copies,))],
        compiler_params=params(),
        name="pack",
    )(me, pairs, blocks)


def select_kernel(pair_count, me_ref, pairs_ref, received_ref, out_ref, sems):
    me = me_ref[0]
    owners = [pairs_ref[me, 2 * pair + 1] >> 3 for pair in range(pair_count)]
    copies = []
    for pair in range(pair_count):
        rank = jnp.int32(0)
        for before in range(pair):
            rank = rank + (owners[before] == owners[pair]).astype(jnp.int32)
        copies.append(
            pltpu.make_async_copy(
                received_ref.at[owners[pair], rank], out_ref.at[pair], sems.at[pair]
            )
        )
        copies[-1].start()
    for copy in copies:
        copy.wait()


def select(me, pairs, received, pair_count):
    _, _, size, feat = received.shape
    return pl.pallas_call(
        functools.partial(select_kernel, pair_count),
        out_shape=jax.ShapeDtypeStruct((pair_count, size, feat), received.dtype),
        in_specs=[smem(), smem(), anywhere()],
        out_specs=anywhere(),
        scratch_shapes=[pltpu.SemaphoreType.DMA((pair_count,))],
        compiler_params=params(),
        name="select",
    )(me, pairs, received)


def tree(parts):
    while len(parts) > 1:
        half = len(parts) // 2
        parts = [parts[i] + parts[i + half] for i in range(half)]
    return parts[0]


def across(left, right):
    return lax.dot_general(
        left, right, (((1,), (1,)), ((), ())), preferred_element_type=jnp.float32
    )


def col_square(block):
    square = jnp.square(block.astype(jnp.float32))
    high = square.astype(jnp.bfloat16)
    low = (square - high.astype(jnp.float32)).astype(jnp.bfloat16)
    ones = jnp.ones((8, block.shape[1]), jnp.bfloat16)
    return (across(ones, high) + across(ones, low))[:1]


def chunk_kernel(narrow_count, first, last, *refs):
    rows, cols = refs[:narrow_count], refs[narrow_count : 2 * narrow_count]
    rest = list(refs[2 * narrow_count :])
    if first:
        square = tree(
            [
                jnp.sum(jnp.square(row[0].astype(jnp.float32)), axis=1, keepdims=True)
                for row in rows
            ]
        )
        square = jnp.broadcast_to(square, (BR, LANES))
    else:
        square_ref, mass_in, total_in, sums_in = rest[:4]
        rest = rest[4:]
        square = square_ref[0]
    gram = tree([across(row[0], col[0]) for row, col in zip(rows, cols)])
    other = tree([col_square(col[0]) for col in cols])
    size = gram.shape[1]
    pieces, mass = [], None
    for at in range(0, size, LANES):
        here = slice(at, at + LANES)
        piece = jnp.exp((square + other[:, here] - 2.0 * gram[:, here]) * (-1.0 / F))
        mass = piece if mass is None else mass + piece
        pieces.append(piece)
    kernel = jnp.concatenate(pieces, axis=1) if len(pieces) > 1 else pieces[0]
    sums = jnp.sum(kernel, axis=0, keepdims=True)
    total = jnp.dot(kernel.astype(jnp.bfloat16), cols[0][0], preferred_element_type=jnp.float32)
    if not first:
        mass = mass_in[0] + mass
        total = total_in[0] + total
        sums = jnp.concatenate([sums_in[0], sums], axis=1)
    if last:
        part_ref, mass_ref, row_ref, sums_ref = rest
        part_ref[0] = total.astype(jnp.bfloat16)
        mass_ref[0] = jnp.broadcast_to(jnp.sum(mass, axis=1, keepdims=True), (BR, LANES))
        row_ref[0] = jnp.sum(mass.T, axis=0, keepdims=True)
        for wide in range(sums_ref.shape[0]):
            sums_ref[wide, 0] = sums
    else:
        square_ref, mass_ref, total_ref, sums_ref = rest
        if first:
            square_ref[0] = square
        mass_ref[0] = mass
        total_ref[0] = total
        sums_ref[0] = sums


def by_pair(shape):
    return pl.BlockSpec((1, *shape[1:]), lambda p: (p,) + (0,) * (len(shape) - 1))


def chunk_step(rows, cols, carry, done, last, wide_count):
    pair_count, size, feat = cols[0].shape
    first = carry is None
    lanes = jax.ShapeDtypeStruct((pair_count, BR, LANES), jnp.float32)
    if last:
        shapes = [
            jax.ShapeDtypeStruct((pair_count, BR, feat), jnp.bfloat16),
            lanes,
            jax.ShapeDtypeStruct((pair_count, 1, BR), jnp.float32),
            jax.ShapeDtypeStruct((wide_count, pair_count, 1, BR), jnp.float32),
        ]
        out_specs = [by_pair(s.shape) for s in shapes[:3]] + [
            pl.BlockSpec((wide_count, 1, 1, BR), lambda p: (0, p, 0, 0))
        ]
    else:
        shapes = [
            lanes,
            lanes,
            jax.ShapeDtypeStruct((pair_count, BR, feat), jnp.float32),
            jax.ShapeDtypeStruct((pair_count, 1, done + size), jnp.float32),
        ]
        out_specs = [by_pair(s.shape) for s in shapes]
    args = [*rows, *cols, *([] if first else carry)]
    return pl.pallas_call(
        functools.partial(chunk_kernel, len(rows), first, last),
        grid=(pair_count,),
        out_shape=shapes,
        in_specs=[by_pair(a.shape) for a in args],
        out_specs=out_specs,
        compiler_params=params(),
        cost_estimate=pl.CostEstimate(
            flops=2 * pair_count * BR * size * (F + feat),
            transcendentals=pair_count * BR * size,
            bytes_accessed=8 * 1024 * 1024,
        ),
        name="chunk",
    )(*args)


def mean_kernel(pair_count, local_ref, part_ref, mass_ref, block_ref, _, out_ref, total, weight):
    here = local_ref[pl.program_id(0)]
    total[...] = block_ref[0].astype(jnp.float32)
    weight[...] = jnp.ones_like(weight)
    for pair in range(pair_count):

        @pl.when(local_ref[pair] == here)
        def _():
            total[...] += part_ref[pair].astype(jnp.float32)
            weight[...] += mass_ref[pair]

    scale = 1.0 / weight[...]
    for at in range(0, total.shape[1], LANES):
        lanes = slice(at, at + LANES)
        out_ref[0, :, lanes] = (total[:, lanes] * scale).astype(jnp.bfloat16)


def means(row_local, part, mass, blocks):
    pair_count = mass.shape[0]
    feat = blocks.shape[-1]
    block = pl.BlockSpec((1, BR, feat), lambda p, local: (local[p], 0, 0))
    return pl.pallas_call(
        functools.partial(mean_kernel, pair_count),
        out_shape=jax.ShapeDtypeStruct(blocks.shape, jnp.bfloat16),
        grid_spec=pltpu.PrefetchScalarGridSpec(
            num_scalar_prefetch=1,
            grid=(pair_count,),
            in_specs=[
                pl.BlockSpec(part.shape, lambda p, local: (0, 0, 0)),
                pl.BlockSpec(mass.shape, lambda p, local: (0, 0, 0)),
                block,
                anywhere(),
            ],
            out_specs=block,
            scratch_shapes=[
                pltpu.VMEM((BR, feat), jnp.float32),
                pltpu.VMEM((BR, LANES), jnp.float32),
            ],
        ),
        input_output_aliases={4: 0},
        compiler_params=params(),
        cost_estimate=pl.CostEstimate(
            flops=pair_count * BR * feat * 4, transcendentals=0, bytes_accessed=4 * 1024 * 1024
        ),
        name="means",
    )(row_local, part, mass, blocks, blocks + jnp.zeros((), blocks.dtype))


def gather_narrow(part):
    count = lax.axis_size("narrow")
    parts = [part]
    step = count // 2
    while step:
        perm = [(i, i ^ step) for i in range(count)]
        parts = parts + [lax.ppermute(x, "narrow", perm) for x in parts]
        step //= 2
    return parts


def to_all(parts):
    return lax.all_to_all(parts, "wide", split_axis=0, concat_axis=0, tiled=True)


def on_device(embeddings, pair_list):
    wide_count = lax.axis_size("wide")
    me = lax.axis_index("wide").astype(jnp.int32).reshape(1)
    pair_count = pair_list.shape[0]
    capacity = max(2, 2 * pair_count // wide_count)
    feat = embeddings.shape[1]
    blocks = embeddings.reshape(BLK_DEV, BR, feat)
    row_local = pair_list[:, 0] % BLK_DEV
    every_pair = to_all(
        jnp.broadcast_to(pair_list.reshape(1, 2 * pair_count), (wide_count, 2 * pair_count))
    )
    *outgoing, row_slices = pack(me, every_pair, blocks, wide_count, pair_count, capacity)
    rows = gather_narrow(row_slices)
    carry, done = None, 0
    for chunk, (start, size) in enumerate(CHUNKS):
        received = to_all(outgoing[chunk])
        cols = gather_narrow(select(me, every_pair, received, pair_count))
        carry = chunk_step(rows, cols, carry, done, chunk == len(CHUNKS) - 1, wide_count)
        done += size
    part, mass, row_sums, col_sums = carry
    every_sum = to_all(col_sums).reshape(wide_count * pair_count, BR)
    mean = means(row_local, part, mass, blocks)
    block_ids = jnp.arange(BLK_DEV, dtype=jnp.int32)[:, None]
    mine = every_pair.reshape(-1, 2)[:, 1][None, :] == me[0] * BLK_DEV + block_ids
    col_mass = jnp.sum(jnp.where(mine[:, :, None], every_sum[None], 0.0), axis=1)
    here = row_local[None, :] == block_ids
    row_mass = jnp.sum(jnp.where(here[:, :, None], row_sums.reshape(1, pair_count, BR), 0.0), axis=1)
    weights = 1.0 / (1.0 + (row_mass + col_mass) / BR)
    return weights.reshape(BLK_DEV * BR), mean.reshape(BLK_DEV * BR, feat)


def solution(mesh):
    in_specs = (P(("groups", "wide"), "narrow"), P(("groups", "wide"), None))
    out_specs = (P(("groups", "wide")), P(("groups", "wide"), "narrow"))
    return jax.shard_map(
        on_device, mesh=mesh, in_specs=in_specs, out_specs=out_specs, check_vma=False
    )
```

time: 131 us -> 142 us (1.084)
  blocking collectives: 24.2 us -> 0 us
  waiting for transfers between devices: 35.8 us -> 58.8 us
  Pallas kernels: 32.3 us -> 47.2 us
  local copies, waits for them, and re-layouts: 8.32 us -> 10.9 us
  starting transfers between devices: 25.2 us -> 23 us
  other arithmetic: 2.9 us -> 1.11 us
    all_to_all x0 -> x4, waiting for transfers between devices: none -> 41.5 us  [to_all(): lax.all_to_all(parts, 'wide', split_axis=0, concat_axis=0, tiled=True)]
    ppermute x9 -> x0, waiting for transfers between devices: 28.6 us -> none  [on_device(): lax.ppermute(outgoing[(shift - 1) * len(CHUNKS) + chunk], 'wide', [(i, (i...]
    all_gather x2 -> x0, blocking collectives: 24.2 us -> none  [the longest x1 13.1 us: on_device(): every_sum = lax.all_gather(col_sum, 'wide', axis=0, tiled=True)]
    pallas_call x6 -> x4, Pallas kernels: 21.2 us -> 42.3 us  [the longest x2 26.5 us: select(): pl.pallas_call(functools.partial(select_kernel, pair_count), out_shape=ja...]
    ppermute x9 -> x0, starting transfers between devices: 17.5 us -> none  [on_device(): lax.ppermute(outgoing[(shift - 1) * len(CHUNKS) + chunk], 'wide', [(i, (i...]
    all_to_all x0 -> x4, starting transfers between devices: none -> 17.4 us  [to_all(): lax.all_to_all(parts, 'wide', split_axis=0, concat_axis=0, tiled=True)]
    ppermute x12 -> x9, waiting for transfers between devices: 7.24 us -> 17.3 us  [gather_narrow(): parts = parts + [lax.ppermute(x, 'narrow', perm) for x in parts]]
    pallas_call x1, Pallas kernels: 7.74 us -> 2.56 us  [means(): pl.pallas_call(functools.partial(mean_kernel, pair_count), out_shape=jax....]
  transfers between devices with their start and end apart: 21 -> 13, of which waited for: 6 -> 5; matrix products, arithmetic and copies ran while one was open for 2% -> 2% of each run, Pallas kernels for 15% -> 27%
where the time goes in v2:
time: 142 us
  waiting for transfers between devices  58.8 us (41%)
  Pallas kernels  47.2 us (33%)
  starting transfers between devices  23 us (16%)
  local copies, waits for them, and re-layouts  10.9 us (8%)
    all_to_all x4, waiting for transfers between devices, to_all(): lax.all_to_all(parts, 'wide', split_axis=0, concat_axis=0, tiled=True)  41.5 us
    pallas_call x2, Pallas kernels, select(): pl.pallas_call(functools.partial(select_kernel, pair_count), out_shape=ja...  26.5 us
    all_to_all x4, starting transfers between devices, to_all(): lax.all_to_all(parts, 'wide', split_axis=0, concat_axis=0, tiled=True)  17.4 us
    ppermute x9, waiting for transfers between devices, gather_narrow(): parts = parts + [lax.ppermute(x, 'narrow', perm) for x in parts]  17.3 us
    pallas_call x2, Pallas kernels, chunk_step(): pl.pallas_call(functools.partial(chunk_kernel, len(rows), first, last), g...  15.8 us
    unnamed x22, local copies, waits for them, and re-layouts  9.48 us
    ppermute x9, starting transfers between devices, gather_narrow(): parts = parts + [lax.ppermute(x, 'narrow', perm) for x in parts]  5.61 us
  transfers between devices with their start and end apart: 13, of which 5 were waited for; matrix products, arithmetic and copies ran while one was open for 2% of the time, Pallas kernels for 27%

profile of v2, /device:TPU:0, one launch (start us, length us, event | category | flops | bytes accessed | tf_op | source)
XLA Modules:
  0.0 141.9 jit_solution(2939147268820257323)
XLA Ops:
  0.6 0.8 copy.8
  1.5 0.6 broadcast_in_dim.57
  2.1 6.3 %all-to-all-start = ((s32[4,1,8]{2,1,0:T(1,128)}), s32[4,1,8]{2,1,0:T(1,128)S(1)}, u32[]{:S(2)}, u32[]{:S(2)}) async-start(s32[4,1,8]{2,1,0:T(1,128)} %broadcast_in_dim.57), calls=%async_computation | async-start | bytes 4096 | tf_op jit(solution)/shard_map/all_to_all | solution.py:277
  8.4 5.5 %all-to-all-done = s32[4,1,8]{2,1,0:T(1,128)S(1)} async-done(((s32[4,1,8]{2,1,0:T(1,128)}), s32[4,1,8]{2,1,0:T(1,128)S(1)}, u32[]{:S(2)}, u32[]{:S(2)}) %all-to-all-start) | async-done | bytes 160 | tf_op jit(solution)/shard_map/all_to_all | solution.py:277
  13.9 1.6 %copy-done = bf16[4096,256]{1,0:T(8,128)(2,1)S(1)} copy-done((bf16[4096,256]{1,0:T(8,128)(2,1)S(1)}, bf16[4096,256]{1,0:T(8,128)(2,1)}, u32[]{:S(2)}) %copy-start) | copy-done | bytes 2097176
  15.4 2.4 %pack.1 = (bf16[4,2,384,256]{3,2,1,0:T(8,128)(2,1)}, bf16[4,2,128,256]{3,2,1,0:T(8,128)(2,1)}, bf16[4,512,256]{2,1,0:T(8,128)(2,1)}) custom-call(s32[1]{0:T(128)} %bitcast.1.me_ref, s32[4,8]{1,0:T(4,128)S(1)} %bitcast.15, bf16[8,512,256]{2,1,0:T(8,128)(2,1)S(1)} %bitcast.12), custom_call_target="tpu_custom_call" | custom-call | tf_op jit(solution)/shard_map/pack/pallas_call | solution.py:64
  17.9 4.4 %all-to-all-start.2 = ((bf16[4,2,384,256]{3,2,1,0:T(8,128)(2,1)}), bf16[4,2,384,256]{3,2,1,0:T(8,128)(2,1)}, u32[]{:S(2)}, u32[]{:S(2)}) async-start(bf16[4,2,384,256]{3,2,1,0:T(8,128)(2,1)} %get-tuple-element.15), calls=%async_computation.2 | async-start | bytes 3145728 | tf_op jit(solution)/shard_map/all_to_all | solution.py:277
  22.3 1.6 %collective-permute-start = (bf16[4,512,256]{2,1,0:T(8,128)(2,1)}, bf16[4,512,256]{2,1,0:T(8,128)(2,1)}, u32[]{:S(2)}, u32[]{:S(2)}) collective-permute-start(bf16[4,512,256]{2,1,0:T(8,128)(2,1)} %get-tuple-element.13.refs_0_), channel_id=1, source_target_pairs={{0,2},{1,3},{2,0},{3,1},{4,6},{5,7},{6,4},{7,5},{8,10},{9,11},{10,... | collective-permute-start | bytes 3145736 | tf_op jit(solution)/shard_map/ppermute | solution.py:271
  23.8 34.3 %all-to-all-done.2.received_ref = bf16[4,2,384,256]{3,2,1,0:T(8,128)(2,1)} async-done(((bf16[4,2,384,256]{3,2,1,0:T(8,128)(2,1)}), bf16[4,2,384,256]{3,2,1,0:T(8,128)(2,1)}, u32[]{:S(2)}, u32[]{:S(2)}) %all-to-all-start.2) | async-done | bytes 1572896 | tf_op jit(solution)/shard_map/all_to_all | solution.py:277
  58.1 25.5 %select.13.refs_4_ = bf16[4,384,256]{2,1,0:T(8,128)(2,1)} custom-call(s32[1]{0:T(128)} %bitcast.1.me_ref, s32[4,8]{1,0:T(4,128)S(1)} %bitcast.16, bf16[4,2,384,256]{3,2,1,0:T(8,128)(2,1)} %all-to-all-done.2.received_ref), custom_call_target="tpu_custom_call" | custom-call | tf_op jit(solution)/shard_map/select/pallas_call | solution.py:95
  83.6 1.6 %collective-permute-start.6 = (bf16[4,384,256]{2,1,0:T(8,128)(2,1)}, bf16[4,384,256]{2,1,0:T(8,128)(2,1)}, u32[]{:S(2)}, u32[]{:S(2)}) collective-permute-start(bf16[4,384,256]{2,1,0:T(8,128)(2,1)} %select.13.refs_4_), channel_id=1, source_target_pairs={{0,2},{1,3},{2,0},{3,1},{4,6},{5,7},{6,4},{7,5},{8,10},{9,11},{10,... | collective-permute-start | bytes 2359304 | tf_op jit(solution)/shard_map/ppermute | solution.py:271
  85.2 3.5 %all-to-all-start.1 = ((bf16[4,2,128,256]{3,2,1,0:T(8,128)(2,1)}), bf16[4,2,128,256]{3,2,1,0:T(8,128)(2,1)S(1)}, u32[]{:S(2)}, u32[]{:S(2)}) async-start(bf16[4,2,128,256]{3,2,1,0:T(8,128)(2,1)} %get-tuple-element.14), calls=%async_computation.1 | async-start | bytes 1048576 | tf_op jit(solution)/shard_map/all_to_all | solution.py:277
  88.8 0.5 collective-permute-start.2
  89.3 13.2 %collective-permute-done.6.refs_5_ = bf16[4,384,256]{2,1,0:T(8,128)(2,1)} collective-permute-done((bf16[4,384,256]{2,1,0:T(8,128)(2,1)}, bf16[4,384,256]{2,1,0:T(8,128)(2,1)}, u32[]{:S(2)}, u32[]{:S(2)}) %collective-permute-start.6) | collective-permute-done | bytes 786464 | tf_op jit(solution)/shard_map/ppermute | solution.py:271
  102.5 1.0 select.12.refs_4_
  103.5 1.6 %collective-permute-start.3 = (bf16[4,128,256]{2,1,0:T(8,128)(2,1)S(1)}, bf16[4,128,256]{2,1,0:T(8,128)(2,1)S(1)}, u32[]{:S(2)}, u32[]{:S(2)}) collective-permute-start(bf16[4,128,256]{2,1,0:T(8,128)(2,1)S(1)} %select.12.refs_4_), channel_id=1, source_target_pairs={{0,2},{1,3},{2,0},{3,1},{4,6},{5,7},{6,4},{7,5},{8,10},{9,11},{10,... | collective-permute-start | bytes 786440 | tf_op jit(solution)/shard_map/ppermute | solution.py:271
  105.1 1.3 copy.14._
  106.5 0.5 broadcast.85
  107.0 0.7 reduce.6
  107.9 0.3 collective-permute-start.4
  108.2 4.1 %collective-permute-done.3.refs_5_ = bf16[4,128,256]{2,1,0:T(8,128)(2,1)S(1)} collective-permute-done((bf16[4,128,256]{2,1,0:T(8,128)(2,1)S(1)}, bf16[4,128,256]{2,1,0:T(8,128)(2,1)S(1)}, u32[]{:S(2)}, u32[]{:S(2)}) %collective-permute-start.3) | collective-permute-done | bytes 262176 | tf_op jit(solution)/shard_map/ppermute | solution.py:271
  112.4 9.6 %chunk.2 = (f32[4,512,128]{2,1,0:T(8,128)S(1)}, f32[4,512,128]{2,1,0:T(8,128)S(1)}, f32[4,512,256]{2,1,0:T(8,128)}, f32[4,1,384]{2,1,0:T(1,128)S(1)}) custom-call(bf16[4,512,256]{2,1,0:T(8,128)(2,1)} %get-tuple-element.13.refs_0_, bf16[4,512,256]{2,1,0:T(8,128)(2,1)} %collective-permute-done.refs_1_, bf16[4,512,256]{2,1,0:T(8,128)(2,1)} %collective-permute-done.1.refs_2_, ...), custom_call_target="tpu_custom_call" | custom-call | flops 2013265920 | bytes 8388608 | tf_op jit(solution)/shard_map/chunk/pallas_call | solution.py:201
  122.0 1.0 copy-done.4
  123.0 1.0 copy-done.5
  124.1 0.9 copy-done.7
  125.0 6.1 %chunk.3 = (bf16[4,512,256]{2,1,0:T(8,128)(2,1)S(1)}, f32[4,512,128]{2,1,0:T(8,128)S(1)}, f32[4,1,512]{2,1,0:T(1,128)S(1)}, f32[4,4,1,512]{3,2,1,0:T(1,128)}) custom-call(bf16[4,512,256]{2,1,0:T(8,128)(2,1)} %get-tuple-element.13.refs_0_, bf16[4,512,256]{2,1,0:T(8,128)(2,1)} %collective-permute-done.refs_1_, ...), custom_call_target="tpu_custom_call" | custom-call | flops 671088640 | bytes 8388608 | tf_op jit(solution)/shard_map/chunk/pallas_call | solution.py:201
  131.2 1.0 copy-done.2
  132.1 3.3 %all-to-all-start.3 = ((f32[4,4,1,512]{3,2,1,0:T(1,128)}), f32[4,4,1,512]{3,2,1,0:T(1,128)S(1)}, u32[]{:S(2)}, u32[]{:S(2)}) async-start(f32[4,4,1,512]{3,2,1,0:T(1,128)} %get-tuple-element.21), calls=%async_computation.3 | async-start | bytes 65536 | tf_op jit(solution)/shard_map/all_to_all | solution.py:277
  135.5 1.2 copy-done.3
  136.7 2.6 %means.1 = bf16[8,512,256]{2,1,0:T(8,128)(2,1)} custom-call(s32[4]{0:T(128)S(1)} %and_select_fusion.local_ref, bf16[4,512,256]{2,1,0:T(8,128)(2,1)S(1)} %get-tuple-element.22.part_ref, f32[4,512,128]{2,1,0:T(8,128)S(1)} %copy-done.3, bf16[8,512,256]{2,1,0:T(8,128)(2,1)S(1)} %bitcast.14, bf16[8,512,256]{2,1,0:T(8,128)(2,1)} %copy.14._), custom_call_target="tpu_custom_call", output_to_operand_aliasing={{}: (4, {})} | custom-call | flops 2097152 | bytes 4194304 | tf_op jit(solution)/shard_map/means/pallas_call | solution.py:238
  139.3 1.7 %all-to-all-done.3 = f32[4,4,1,512]{3,2,1,0:T(1,128)S(1)} async-done(((f32[4,4,1,512]{3,2,1,0:T(1,128)}), f32[4,4,1,512]{3,2,1,0:T(1,128)S(1)}, u32[]{:S(2)}, u32[]{:S(2)}) %all-to-all-start.3) | async-done | bytes 32800 | tf_op jit(solution)/shard_map/all_to_all | solution.py:277
  141.3 0.6 copy.11
  (37 shorter events, 1.0 us)
Async XLA Ops:
  2.1 11.8 %all-to-all-start = ((s32[4,1,8]{2,1,0:T(1,128)}), s32[4,1,8]{2,1,0:T(1,128)S(1)}, u32[]{:S(2)}, u32[]{:S(2)}) async-start(s32[4,1,8]{2,1,0:T(1,128)} %broadcast_in_dim.57), calls=%async_computation | async-start | bytes 4096 | tf_op jit(solution)/shard_map/all_to_all | solution.py:277
  13.9 1.6 %copy-start = (bf16[4096,256]{1,0:T(8,128)(2,1)S(1)}, bf16[4096,256]{1,0:T(8,128)(2,1)}, u32[]{:S(2)}) copy-start(bf16[4096,256]{1,0:T(8,128)(2,1)} %param.2) | copy-start | bytes 6291460
  17.9 40.2 %all-to-all-start.2 = ((bf16[4,2,384,256]{3,2,1,0:T(8,128)(2,1)}), bf16[4,2,384,256]{3,2,1,0:T(8,128)(2,1)}, u32[]{:S(2)}, u32[]{:S(2)}) async-start(bf16[4,2,384,256]{3,2,1,0:T(8,128)(2,1)} %get-tuple-element.15), calls=%async_computation.2 | async-start | bytes 3145728 | tf_op jit(solution)/shard_map/all_to_all | solution.py:277
  22.2 80.3 %copy-start.8 = (s32[4,2]{0,1:T(2,128)S(1)}, s32[4,2]{0,1:T(2,128)}, u32[]{:S(2)}) copy-start(s32[4,2]{0,1:T(2,128)} %param.3) | copy-start | bytes 100
  22.2 82.9 %copy-start.1 = (bf16[4096,256]{1,0:T(8,128)(2,1)S(1)}, bf16[4096,256]{1,0:T(8,128)(2,1)}, u32[]{:S(2)}) copy-start(bf16[4096,256]{1,0:T(8,128)(2,1)} %param.2) | copy-start | bytes 6291460
  22.3 66.5 %collective-permute-start = (bf16[4,512,256]{2,1,0:T(8,128)(2,1)}, bf16[4,512,256]{2,1,0:T(8,128)(2,1)}, u32[]{:S(2)}, u32[]{:S(2)}) collective-permute-start(bf16[4,512,256]{2,1,0:T(8,128)(2,1)} %get-tuple-element.13.refs_0_), channel_id=1, source_target_pairs={{0,2},{1,3},{2,0},{3,1},{4,6},{5,7},{6,4},{7,5},{8,10},{9,11},{10,... | collective-permute-start | bytes 3145736 | tf_op jit(solution)/shard_map/ppermute | solution.py:271
  83.6 18.9 %collective-permute-start.6 = (bf16[4,384,256]{2,1,0:T(8,128)(2,1)}, bf16[4,384,256]{2,1,0:T(8,128)(2,1)}, u32[]{:S(2)}, u32[]{:S(2)}) collective-permute-start(bf16[4,384,256]{2,1,0:T(8,128)(2,1)} %select.13.refs_4_), channel_id=1, source_target_pairs={{0,2},{1,3},{2,0},{3,1},{4,6},{5,7},{6,4},{7,5},{8,10},{9,11},{10,... | collective-permute-start | bytes 2359304 | tf_op jit(solution)/shard_map/ppermute | solution.py:271
  85.2 17.3 %all-to-all-start.1 = ((bf16[4,2,128,256]{3,2,1,0:T(8,128)(2,1)}), bf16[4,2,128,256]{3,2,1,0:T(8,128)(2,1)S(1)}, u32[]{:S(2)}, u32[]{:S(2)}) async-start(bf16[4,2,128,256]{3,2,1,0:T(8,128)(2,1)} %get-tuple-element.14), calls=%async_computation.1 | async-start | bytes 1048576 | tf_op jit(solution)/shard_map/all_to_all | solution.py:277
  88.7 19.2 %collective-permute-start.1 = (bf16[4,512,256]{2,1,0:T(8,128)(2,1)}, bf16[4,512,256]{2,1,0:T(8,128)(2,1)}, u32[]{:S(2)}, u32[]{:S(2)}) collective-permute-start(bf16[4,512,256]{2,1,0:T(8,128)(2,1)} %get-tuple-element.13.refs_0_), channel_id=1, source_target_pairs={{0,1},{1,0},{2,3},{3,2},{4,5},{5,4},{6,7},{7,6},{8,9},{9,8},{10,11... | collective-permute-start | bytes 3145736 | tf_op jit(solution)/shard_map/ppermute | solution.py:271
  88.8 23.6 %collective-permute-start.2 = (bf16[4,512,256]{2,1,0:T(8,128)(2,1)}, bf16[4,512,256]{2,1,0:T(8,128)(2,1)}, u32[]{:S(2)}, u32[]{:S(2)}) collective-permute-start(bf16[4,512,256]{2,1,0:T(8,128)(2,1)} %collective-permute-done.refs_1_), channel_id=1, source_target_pairs={{0,1},{1,0},{2,3},{3,2},{4,5},{5,4},{6,7},{7,6},{8,9},{9,8},{10,11... | collective-permute-start | bytes 3145736 | tf_op jit(solution)/shard_map/ppermute | solution.py:271
  89.3 23.1 %collective-permute-start.7 = (bf16[4,384,256]{2,1,0:T(8,128)(2,1)}, bf16[4,384,256]{2,1,0:T(8,128)(2,1)}, u32[]{:S(2)}, u32[]{:S(2)}) collective-permute-start(bf16[4,384,256]{2,1,0:T(8,128)(2,1)} %select.13.refs_4_), channel_id=1, source_target_pairs={{0,1},{1,0},{2,3},{3,2},{4,5},{5,4},{6,7},{7,6},{8,9},{9,8},{10,11... | collective-permute-start | bytes 2359304 | tf_op jit(solution)/shard_map/ppermute | solution.py:271
  102.5 9.9 %collective-permute-start.8 = (bf16[4,384,256]{2,1,0:T(8,128)(2,1)}, bf16[4,384,256]{2,1,0:T(8,128)(2,1)}, u32[]{:S(2)}, u32[]{:S(2)}) collective-permute-start(bf16[4,384,256]{2,1,0:T(8,128)(2,1)} %collective-permute-done.6.refs_5_), channel_id=1, source_target_pairs={{0,1},{1,0},{2,3},{3,2},{4,5},{5,4},{6,7},{7,6},{8,9},{9,8},{10,11... | collective-permute-start | bytes 2359304 | tf_op jit(solution)/shard_map/ppermute | solution.py:271
  103.5 8.8 %collective-permute-start.3 = (bf16[4,128,256]{2,1,0:T(8,128)(2,1)S(1)}, bf16[4,128,256]{2,1,0:T(8,128)(2,1)S(1)}, u32[]{:S(2)}, u32[]{:S(2)}) collective-permute-start(bf16[4,128,256]{2,1,0:T(8,128)(2,1)S(1)} %select.12.refs_4_), channel_id=1, source_target_pairs={{0,2},{1,3},{2,0},{3,1},{4,6},{5,7},{6,4},{7,5},{8,10},{9,11},{10,... | collective-permute-start | bytes 786440 | tf_op jit(solution)/shard_map/ppermute | solution.py:271
  107.9 16.1 %collective-permute-start.4 = (bf16[4,128,256]{2,1,0:T(8,128)(2,1)S(1)}, bf16[4,128,256]{2,1,0:T(8,128)(2,1)S(1)}, u32[]{:S(2)}, u32[]{:S(2)}) collective-permute-start(bf16[4,128,256]{2,1,0:T(8,128)(2,1)S(1)} %select.12.refs_4_), channel_id=1, source_target_pairs={{0,1},{1,0},{2,3},{3,2},{4,5},{5,4},{6,7},{7,6},{8,9},{9,8},{10,11... | collective-permute-start | bytes 786440 | tf_op jit(solution)/shard_map/ppermute | solution.py:271
  112.3 9.7 %copy-start.6 = (bf16[4,128,256]{2,1,0:T(8,128)(2,1)}, bf16[4,128,256]{2,1,0:T(8,128)(2,1)S(1)}, u32[]{:S(2)}) copy-start(bf16[4,128,256]{2,1,0:T(8,128)(2,1)S(1)} %collective-permute-done.3.refs_5_) | copy-start | bytes 786436
  112.3 11.8 %collective-permute-start.5 = (bf16[4,128,256]{2,1,0:T(8,128)(2,1)S(1)}, bf16[4,128,256]{2,1,0:T(8,128)(2,1)S(1)}, u32[]{:S(2)}, u32[]{:S(2)}) collective-permute-start(bf16[4,128,256]{2,1,0:T(8,128)(2,1)S(1)} %collective-permute-done.3.refs_5_), channel_id=1, source_target_pairs={{0,1},{1,0},{2,3},{3,2},{4,5},{5,4},{6,7},{7,6},{8,9},{9,8},{10,11... | collective-permute-start | bytes 786440 | tf_op jit(solution)/shard_map/ppermute | solution.py:271
  122.0 1.0 copy-start.4
  123.0 1.0 copy-start.5
  124.1 1.0 copy-start.7
  131.1 1.0 copy-start.2
  132.1 8.9 %all-to-all-start.3 = ((f32[4,4,1,512]{3,2,1,0:T(1,128)}), f32[4,4,1,512]{3,2,1,0:T(1,128)S(1)}, u32[]{:S(2)}, u32[]{:S(2)}) async-start(f32[4,4,1,512]{3,2,1,0:T(1,128)} %get-tuple-element.21), calls=%async_computation.3 | async-start | bytes 65536 | tf_op jit(solution)/shard_map/all_to_all | solution.py:277
  135.5 1.2 copy-start.3

commit v3 on v2

v3 whole, which is shorter than its diff:
```python
import functools

import jax
import jax.numpy as jnp
from jax import lax
from jax.experimental import pallas as pl
from jax.experimental.pallas import tpu as pltpu
from jax.sharding import PartitionSpec as P

F = 1024
BR = 512
BLK_DEV = 8
LANES = 128
CHUNKS = ((0, 384), (384, 128))


def smem():
    return pl.BlockSpec(memory_space=pltpu.SMEM)


def vmem():
    return pl.BlockSpec(memory_space=pltpu.VMEM)


def anywhere():
    return pl.BlockSpec(memory_space=pl.ANY)


def in_vmem(x):
    return pltpu.with_memory_space_constraint(x, pltpu.VMEM)


def in_hbm(x):
    return pltpu.with_memory_space_constraint(x, pltpu.HBM)


def params(mebibytes):
    return pltpu.CompilerParams(vmem_limit_bytes=mebibytes * 1024 * 1024)


def pack_kernel(wide_count, pair_count, capacity, me_ref, *refs):
    lists, blocks_ref, outs = refs[:wide_count], refs[wide_count], refs[wide_count + 1 : -2]
    rows_ref, sems = refs[-2:]
    me = me_ref[0]
    copies = []

    def send(source, target):
        copies.append(pltpu.make_async_copy(source, target, sems.at[len(copies)]))
        copies[-1].start()

    for chunk, (start, size) in enumerate(CHUNKS):
        for shift in range(1, wide_count):
            asked = lists[wide_count - shift]
            picks = [jnp.int32(0)] * capacity
            count = jnp.int32(0)
            for pair in range(pair_count):
                col = asked[pair, 1]
                mine = (col >> 3) == me
                for slot in range(capacity):
                    picks[slot] = jnp.where(mine & (count == slot), col & 7, picks[slot])
                count = count + mine.astype(jnp.int32)
            out = outs[chunk * (wide_count - 1) + shift - 1]
            for slot in range(capacity):
                send(blocks_ref.at[picks[slot], pl.ds(start, size)], out.at[slot])
    for pair in range(pair_count):
        send(blocks_ref.at[lists[0][pair, 0] & 7], rows_ref.at[pair])
    for copy in copies:
        copy.wait()


def pack(me, lists, blocks, capacity):
    wide_count, pair_count = len(lists), lists[0].shape[0]
    feat = blocks.shape[-1]
    shapes = [
        pltpu.VMEM((capacity, size, feat), blocks.dtype)
        for _, size in CHUNKS
        for _ in range(1, wide_count)
    ] + [pltpu.HBM((pair_count, BR, feat), blocks.dtype)]
    copies = (len(shapes) - 1) * capacity + pair_count
    outs = pl.pallas_call(
        functools.partial(pack_kernel, wide_count, pair_count, capacity),
        out_shape=shapes,
        in_specs=[smem()] * (1 + wide_count) + [anywhere()],
        out_specs=[anywhere()] * len(shapes),
        scratch_shapes=[pltpu.SemaphoreType.DMA((copies,))],
        compiler_params=params(4),
        name="pack",
    )(me, *lists, in_hbm(blocks))
    each = wide_count - 1
    return [outs[c * each : (c + 1) * each] for c in range(len(CHUNKS))], outs[-1]


def select_kernel(wide_count, pair_count, start, size, me_ref, list_ref, blocks_ref, *refs):
    received, out_ref, sems = refs[:-2], refs[-2], refs[-1]
    me = me_ref[0]
    owners = [list_ref[pair, 1] >> 3 for pair in range(pair_count)]
    for pair in range(pair_count):
        shift = me - owners[pair]
        shift = jnp.where(shift < 0, shift + wide_count, shift)
        rank = jnp.int32(0)
        for before in range(pair):
            rank = rank + (owners[before] == owners[pair]).astype(jnp.int32)

        @pl.when(shift == 0)
        def _():
            source = blocks_ref.at[list_ref[pair, 1] & 7, pl.ds(start, size)]
            pltpu.make_async_copy(source, out_ref.at[pair], sems.at[pair]).start()

        for other in range(1, wide_count):

            @pl.when(shift == other)
            def _():
                source = received[other - 1].at[rank]
                pltpu.make_async_copy(source, out_ref.at[pair], sems.at[pair]).start()

    for pair in range(pair_count):
        source = blocks_ref.at[0, pl.ds(start, size)]
        pltpu.make_async_copy(source, out_ref.at[pair], sems.at[pair]).wait()


def select(me, pairs, blocks, received, start, size):
    pair_count, feat = pairs.shape[0], blocks.shape[-1]
    return pl.pallas_call(
        functools.partial(select_kernel, len(received) + 1, pair_count, start, size),
        out_shape=pltpu.HBM((pair_count, size, feat), blocks.dtype),
        in_specs=[smem(), smem(), anywhere()] + [anywhere()] * len(received),
        out_specs=anywhere(),
        scratch_shapes=[pltpu.SemaphoreType.DMA((pair_count,))],
        compiler_params=params(4),
        name="select",
    )(me, pairs, in_hbm(blocks), *[in_vmem(x) for x in received])


def tree(parts):
    while len(parts) > 1:
        half = len(parts) // 2
        parts = [parts[i] + parts[i + half] for i in range(half)]
    return parts[0]


def across(left, right):
    return lax.dot_general(
        left, right, (((1,), (1,)), ((), ())), preferred_element_type=jnp.float32
    )


def lane_sum(block):
    square = jnp.square(block.astype(jnp.float32))
    return sum(square[:, at : at + LANES] for at in range(0, square.shape[1], LANES))


def chunk_kernel(narrow_count, first, last, *refs):
    rows, cols = refs[:narrow_count], refs[narrow_count : 2 * narrow_count]
    rest = list(refs[2 * narrow_count :])
    if not first:
        square_in, mass_in, total_in, sums_in = rest[:4]
        rest = rest[4:]
    if last:
        part_ref, mass_ref, row_ref, sums_ref = rest
    else:
        square_ref, mass_ref, total_ref, sums_ref = rest
    for pair in range(rows[0].shape[0]):
        if first:
            square = jnp.sum(tree([lane_sum(row[pair]) for row in rows]), axis=1, keepdims=True)
            square = jnp.broadcast_to(square, (BR, LANES))
        else:
            square = square_in[pair]
        gram = tree([across(row[pair], col[pair]) for row, col in zip(rows, cols)])
        other = jnp.sum(tree([lane_sum(col[pair]) for col in cols]).T, axis=0, keepdims=True)
        size = gram.shape[1]
        pieces, mass = [], None
        for at in range(0, size, LANES):
            here = slice(at, at + LANES)
            piece = jnp.exp((square + other[:, here] - 2.0 * gram[:, here]) * (-1.0 / F))
            mass = piece if mass is None else mass + piece
            pieces.append(piece)
        kernel = jnp.concatenate(pieces, axis=1) if len(pieces) > 1 else pieces[0]
        sums = jnp.sum(kernel, axis=0, keepdims=True)
        total = jnp.dot(
            kernel.astype(jnp.bfloat16), cols[0][pair], preferred_element_type=jnp.float32
        )
        if not first:
            mass = mass_in[pair] + mass
            total = total_in[pair] + total
            sums = jnp.concatenate([sums_in[pair : pair + 1], sums], axis=1)
        sums_ref[pair : pair + 1] = sums
        if last:
            part_ref[pair] = total.astype(jnp.bfloat16)
            mass_ref[pair] = jnp.broadcast_to(jnp.sum(mass, axis=1, keepdims=True), (BR, LANES))
            row_ref[pair : pair + 1] = jnp.sum(mass.T, axis=0, keepdims=True)
        else:
            if first:
                square_ref[pair] = square
            mass_ref[pair] = mass
            total_ref[pair] = total


def chunk_step(rows, cols, carry, done, last):
    pair_count, size, feat = cols[0].shape
    first = carry is None
    lanes = pltpu.VMEM((pair_count, BR, LANES), jnp.float32)
    sums = pltpu.VMEM((pair_count, done + size), jnp.float32)
    if last:
        shapes = [
            pltpu.VMEM((pair_count, BR, feat), jnp.bfloat16),
            lanes,
            pltpu.VMEM((pair_count, BR), jnp.float32),
            sums,
        ]
    else:
        shapes = [lanes, lanes, pltpu.VMEM((pair_count, BR, feat), jnp.float32), sums]
    args = [*rows, *cols, *([] if first else carry)]
    return pl.pallas_call(
        functools.partial(chunk_kernel, len(rows), first, last),
        out_shape=shapes,
        in_specs=[vmem()] * len(args),
        out_specs=[vmem()] * len(shapes),
        compiler_params=params(16),
        cost_estimate=pl.CostEstimate(
            flops=2 * pair_count * BR * size * (F + feat),
            transcendentals=pair_count * BR * size,
            bytes_accessed=8 * 1024 * 1024,
        ),
        name="chunk",
    )(*[in_vmem(x) for x in args])


def mean_kernel(pair_count, local_ref, part_ref, mass_ref, block_ref, _, out_ref, total, weight):
    here = local_ref[pl.program_id(0)]
    total[...] = block_ref[0].astype(jnp.float32)
    weight[...] = jnp.ones_like(weight)
    for pair in range(pair_count):

        @pl.when(local_ref[pair] == here)
        def _():
            total[...] += part_ref[pair].astype(jnp.float32)
            weight[...] += mass_ref[pair]

    scale = 1.0 / weight[...]
    for at in range(0, total.shape[1], LANES):
        lanes = slice(at, at + LANES)
        out_ref[0, :, lanes] = (total[:, lanes] * scale).astype(jnp.bfloat16)


def means(row_local, part, mass, blocks):
    pair_count = mass.shape[0]
    feat = blocks.shape[-1]
    block = pl.BlockSpec((1, BR, feat), lambda p, local: (local[p], 0, 0))
    return pl.pallas_call(
        functools.partial(mean_kernel, pair_count),
        out_shape=jax.ShapeDtypeStruct(blocks.shape, jnp.bfloat16),
        grid_spec=pltpu.PrefetchScalarGridSpec(
            num_scalar_prefetch=1,
            grid=(pair_count,),
            in_specs=[
                pl.BlockSpec(part.shape, lambda p, local: (0, 0, 0)),
                pl.BlockSpec(mass.shape, lambda p, local: (0, 0, 0)),
                block,
                anywhere(),
            ],
            out_specs=block,
            scratch_shapes=[
                pltpu.VMEM((BR, feat), jnp.float32),
                pltpu.VMEM((BR, LANES), jnp.float32),
            ],
        ),
        input_output_aliases={4: 0},
        compiler_params=params(16),
        cost_estimate=pl.CostEstimate(
            flops=pair_count * BR * feat * 4, transcendentals=0, bytes_accessed=4 * 1024 * 1024
        ),
        name="means",
    )(row_local, part, mass, in_hbm(blocks), in_hbm(blocks))


def gather_narrow(part, before=None):
    count = lax.axis_size("narrow")
    parts = [part]
    step = count // 2
    while step:
        perm = [(i, i ^ step) for i in range(count)]
        if step == 1 and before is not None:
            came, before = lax.optimization_barrier((parts[1:], before))
            parts = [part, *came]
        parts = parts + [lax.ppermute(x, "narrow", perm) for x in parts]
        step //= 2
    return parts, before


def from_others(part):
    count = lax.axis_size("wide")
    return [part] + [
        lax.ppermute(part, "wide", [(i, (i + shift) % count) for i in range(count)])
        for shift in range(1, count)
    ]


def on_device(embeddings, pair_list):
    wide_count = lax.axis_size("wide")
    me = lax.axis_index("wide").astype(jnp.int32).reshape(1)
    pair_count = pair_list.shape[0]
    capacity = max(2, 2 * pair_count // wide_count)
    feat = embeddings.shape[1]
    blocks = embeddings.reshape(BLK_DEV, BR, feat)
    row_local = pair_list[:, 0] % BLK_DEV
    lists = from_others(pair_list)
    outgoing, row_slices = pack(me, lists, blocks, capacity)
    rows, _ = gather_narrow(row_slices)
    carry, done = None, 0
    for chunk, (start, size) in enumerate(CHUNKS):
        received = [
            lax.ppermute(
                outgoing[chunk][shift - 1],
                "wide",
                [(i, (i + shift) % wide_count) for i in range(wide_count)],
            )
            for shift in range(1, wide_count)
        ]
        if chunk == 0:
            rows, received = lax.optimization_barrier((rows, received))
        col_part = select(me, pair_list, blocks, received, start, size)
        cols, carry = gather_narrow(col_part, carry)
        carry = chunk_step(rows, cols, carry, done, chunk == len(CHUNKS) - 1)
        done += size
    part, mass, row_sums, col_sums = carry
    every_sum = jnp.concatenate(from_others(col_sums), axis=0)
    mean = means(row_local, part, mass, blocks)
    block_ids = jnp.arange(BLK_DEV, dtype=jnp.int32)[:, None]
    every_col = jnp.concatenate([x[:, 1] for x in lists])
    mine = every_col[None, :] == me[0] * BLK_DEV + block_ids
    col_mass = jnp.sum(jnp.where(mine[:, :, None], every_sum[None], 0.0), axis=1)
    here = row_local[None, :] == block_ids
    row_mass = jnp.sum(jnp.where(here[:, :, None], row_sums[None], 0.0), axis=1)
    weights = 1.0 / (1.0 + (row_mass + col_mass) / BR)
    return weights.reshape(BLK_DEV * BR), mean.reshape(BLK_DEV * BR, feat)


def solution(mesh):
    in_specs = (P(("groups", "wide"), "narrow"), P(("groups", "wide"), None))
    out_specs = (P(("groups", "wide")), P(("groups", "wide"), "narrow"))
    return jax.shard_map(
        on_device, mesh=mesh, in_specs=in_specs, out_specs=out_specs, check_vma=False
    )
```

time: 142 us -> 177 us (1.25); the launches traced: 142 us -> 180 us
  starting transfers between devices: 23 us -> 44.7 us
  waiting for transfers between devices: 58.8 us -> 78.9 us
  local copies, waits for them, and re-layouts: 10.9 us -> 5 us
  Pallas kernels: 47.2 us -> 49.3 us
    all_to_all x4 -> x0, waiting for transfers between devices: 41.5 us -> none  [to_all(): lax.all_to_all(parts, 'wide', split_axis=0, concat_axis=0, tiled=True)]
    ppermute x0 -> x12, starting transfers between devices: none -> 40 us  [the longest x6 25.3 us: on_device(): lax.ppermute(outgoing[chunk][shift - 1], 'wide', [(i, (i + shift) % wide_...]
    ppermute x0 -> x12, waiting for transfers between devices: none -> 37.5 us  [the longest x6 35.2 us: on_device(): lax.ppermute(outgoing[chunk][shift - 1], 'wide', [(i, (i + shift) % wide_...]
    pallas_call x1, Pallas kernels: 2.42 us -> 33.7 us  [pack(): pl.pallas_call(functools.partial(pack_kernel, wide_count, pair_count, cap...]
    pallas_call x4, Pallas kernels: 42.3 us -> 11.3 us  [the longest x2 8.44 us: chunk_step(): pl.pallas_call(functools.partial(chunk_kernel, len(rows), first, last), o...]
    ppermute x9, waiting for transfers between devices: 17.3 us -> 41.4 us  [gather_narrow(): parts = parts + [lax.ppermute(x, 'narrow', perm) for x in parts]]
    all_to_all x4 -> x0, starting transfers between devices: 17.4 us -> none  [to_all(): lax.all_to_all(parts, 'wide', split_axis=0, concat_axis=0, tiled=True)]
    unnamed x22 -> x11, local copies, waits for them, and re-layouts: 9.48 us -> 4.45 us
  transfers between devices with their start and end apart: 13 -> 21, of which waited for: 5 -> 10; matrix products, arithmetic and copies ran while one was open for 2% -> 3% of each run, Pallas kernels for 27% -> 6%
where the time goes in v3:
time: 177 us; the launch traced here: 180 us
  waiting for transfers between devices  78.9 us (45%)
  Pallas kernels  49.3 us (28%)
  starting transfers between devices  44.7 us (25%)
  local copies, waits for them, and re-layouts  5 us (3%)
    ppermute x9, waiting for transfers between devices, gather_narrow(): parts = parts + [lax.ppermute(x, 'narrow', perm) for x in parts]  41.4 us
    ppermute x6, waiting for transfers between devices, on_device(): lax.ppermute(outgoing[chunk][shift - 1], 'wide', [(i, (i + shift) % wide_...  35.2 us
    pallas_call x1, Pallas kernels, pack(): pl.pallas_call(functools.partial(pack_kernel, wide_count, pair_count, cap...  33.7 us
    ppermute x6, starting transfers between devices, on_device(): lax.ppermute(outgoing[chunk][shift - 1], 'wide', [(i, (i + shift) % wide_...  25.3 us
    ppermute x6, starting transfers between devices, from_others(): lax.ppermute(part, 'wide', [(i, (i + shift) % count) for i in range(count)])  14.7 us
    pallas_call x2, Pallas kernels, chunk_step(): pl.pallas_call(functools.partial(chunk_kernel, len(rows), first, last), o...  8.44 us
    ppermute x9, starting transfers between devices, gather_narrow(): parts = parts + [lax.ppermute(x, 'narrow', perm) for x in parts]  4.75 us
    unnamed x11, local copies, waits for them, and re-layouts  4.45 us
  transfers between devices with their start and end apart: 21, of which 10 were waited for; matrix products, arithmetic and copies ran while one was open for 3% of the time, Pallas kernels for 6%

profile of v3, /device:TPU:0, one launch (start us, length us, event | category | flops | bytes accessed | tf_op | source)
XLA Modules:
  0.0 179.8 jit_solution(6290678984965418171)
XLA Ops:
  0.6 0.8 copy.20.refs_0_.list_ref
  1.4 3.0 %collective-permute-start = (s32[4,2]{1,0:T(4,128)S(1)}, s32[4,2]{1,0:T(4,128)S(1)}, u32[]{:S(2)}, u32[]{:S(2)}) collective-permute-start(s32[4,2]{1,0:T(4,128)S(1)} %copy.20.refs_0_.list_ref), channel_id=1, source_target_pairs={{0,4},{4,8},{8,12},{12,0},{1,5},{5,9},{9,13},{13,1},{2,6},{6,10},{... | collective-permute-start | bytes 104 | tf_op jit(solution)/shard_map/ppermute | solution.py:293
  4.4 2.6 %collective-permute-start.1 = (s32[4,2]{1,0:T(4,128)S(1)}, s32[4,2]{1,0:T(4,128)S(1)}, u32[]{:S(2)}, u32[]{:S(2)}) collective-permute-start(s32[4,2]{1,0:T(4,128)S(1)} %copy.20.refs_0_.list_ref), channel_id=1, source_target_pairs={{0,8},{4,12},{8,0},{12,4},{1,9},{5,13},{9,1},{13,5},{2,10},{6,14},... | collective-permute-start | bytes 104 | tf_op jit(solution)/shard_map/ppermute | solution.py:293
  7.0 1.3 collective-permute-start.2
  8.4 0.6 collective-permute-done.1.refs_2_
  8.9 1.7 collective-permute-done.2.refs_3_
  10.6 33.7 %pack.1 = (bf16[2,384,256]{2,1,0:T(8,128)(2,1)S(1)}, bf16[2,384,256]{2,1,0:T(8,128)(2,1)S(1)}, bf16[2,384,256]{2,1,0:T(8,128)(2,1)S(1)}, bf16[2,128,256]{2,1,0:T...) custom-call(s32[1]{0:T(128)} %bitcast.1.me_ref, ...), custom_call_target="tpu_custom_call" | custom-call | tf_op jit(solution)/shard_map/pack/pallas_call | solution.py:80
  44.3 1.6 collective-permute-start.3
  45.9 22.2 %collective-permute-done.3.refs_1_ = bf16[4,512,256]{2,1,0:T(8,128)(2,1)S(1)} collective-permute-done((bf16[4,512,256]{2,1,0:T(8,128)(2,1)}, bf16[4,512,256]{2,1,0:T(8,128)(2,1)S(1)}, u32[]{:S(2)}, u32[]{:S(2)}) %collective-permute-start.3) | collective-permute-done | bytes 1048608 | tf_op jit(solution)/shard_map/ppermute | solution.py:285
  68.1 3.4 %collective-permute-start.7 = (bf16[2,384,256]{2,1,0:T(8,128)(2,1)S(1)}, bf16[2,384,256]{2,1,0:T(8,128)(2,1)S(1)}, u32[]{:S(2)}, u32[]{:S(2)}) collective-permute-start(bf16[2,384,256]{2,1,0:T(8,128)(2,1)S(1)} %get-tuple-element.31), channel_id=1, source_target_pairs={{0,8},{4,12},{8,0},{12,4},{1,9},{5,13},{9,1},{13,5},{2,10},{6,14},... | collective-permute-start | bytes 1179656 | tf_op jit(solution)/shard_map/ppermute | solution.py:312
  71.5 0.4 collective-permute-start.8
  71.9 10.0 %collective-permute-done.6.refs_0_ = bf16[2,384,256]{2,1,0:T(8,128)(2,1)S(1)} collective-permute-done((bf16[2,384,256]{2,1,0:T(8,128)(2,1)S(1)}, bf16[2,384,256]{2,1,0:T(8,128)(2,1)S(1)}, u32[]{:S(2)}, u32[]{:S(2)}) %collective-permute-start.6) | collective-permute-done | bytes 393248 | tf_op jit(solution)/shard_map/ppermute | solution.py:312
  81.9 16.3 %collective-permute-done.7.refs_1_ = bf16[2,384,256]{2,1,0:T(8,128)(2,1)S(1)} collective-permute-done((bf16[2,384,256]{2,1,0:T(8,128)(2,1)S(1)}, bf16[2,384,256]{2,1,0:T(8,128)(2,1)S(1)}, u32[]{:S(2)}, u32[]{:S(2)}) %collective-permute-start.7) | collective-permute-done | bytes 393248 | tf_op jit(solution)/shard_map/ppermute | solution.py:312
  98.3 1.6 select.13.refs_4_
  99.9 1.6 collective-permute-start.13
  101.4 0.7 and_select_fusion.local_ref
  102.1 16.9 %collective-permute-done.13.refs_5_ = bf16[4,384,256]{2,1,0:T(8,128)(2,1)} collective-permute-done((bf16[4,384,256]{2,1,0:T(8,128)(2,1)}, bf16[4,384,256]{2,1,0:T(8,128)(2,1)}, u32[]{:S(2)}, u32[]{:S(2)}) %collective-permute-start.13) | collective-permute-done | bytes 786464 | tf_op jit(solution)/shard_map/ppermute | solution.py:285
  119.1 3.1 %copy.24._ = bf16[8,512,256]{2,1,0:T(8,128)(2,1)} copy(bf16[8,512,256]{2,1,0:T(8,128)(2,1)} %bitcast.12) | data formatting | bytes 4194304
  122.2 14.1 %collective-permute-start.10 = (bf16[2,128,256]{2,1,0:T(8,128)(2,1)S(1)}, bf16[2,128,256]{2,1,0:T(8,128)(2,1)S(1)}, u32[]{:S(2)}, u32[]{:S(2)}) collective-permute-start(bf16[2,128,256]{2,1,0:T(8,128)(2,1)S(1)} %get-tuple-element.38), channel_id=1, source_target_pairs={{0,8},{4,12},{8,0},{12,4},{1,9},{5,13},{9,1},{13,5},{2,10},{6,14},... | collective-permute-start | bytes 393224 | tf_op jit(solution)/shard_map/ppermute | solution.py:312
  136.3 6.8 %collective-permute-start.11 = (bf16[2,128,256]{2,1,0:T(8,128)(2,1)S(1)}, bf16[2,128,256]{2,1,0:T(8,128)(2,1)S(1)}, u32[]{:S(2)}, u32[]{:S(2)}) collective-permute-start(bf16[2,128,256]{2,1,0:T(8,128)(2,1)S(1)} %get-tuple-element.39), channel_id=1, source_target_pairs={{0,12},{4,0},{8,4},{12,8},{1,13},{5,1},{9,5},{13,9},{2,14},{6,2},{... | collective-permute-start | bytes 393224 | tf_op jit(solution)/shard_map/ppermute | solution.py:312
  143.2 0.5 collective-permute-start.9
  144.0 3.5 %collective-permute-done.11.refs_2_ = bf16[2,128,256]{2,1,0:T(8,128)(2,1)S(1)} collective-permute-done((bf16[2,128,256]{2,1,0:T(8,128)(2,1)S(1)}, bf16[2,128,256]{2,1,0:T(8,128)(2,1)S(1)}, u32[]{:S(2)}, u32[]{:S(2)}) %collective-permute-start.11) | collective-permute-done | bytes 131104 | tf_op jit(solution)/shard_map/ppermute | solution.py:312
  147.5 5.3 %collective-permute-done.9.refs_0_ = bf16[2,128,256]{2,1,0:T(8,128)(2,1)S(1)} collective-permute-done((bf16[2,128,256]{2,1,0:T(8,128)(2,1)S(1)}, bf16[2,128,256]{2,1,0:T(8,128)(2,1)S(1)}, u32[]{:S(2)}, u32[]{:S(2)}) %collective-permute-start.9) | collective-permute-done | bytes 131104 | tf_op jit(solution)/shard_map/ppermute | solution.py:312
  152.9 1.3 select.12.refs_4_
  154.2 1.6 collective-permute-start.12
  156.1 5.7 %chunk.2 = (f32[4,512,128]{2,1,0:T(8,128)S(1)}, f32[4,512,128]{2,1,0:T(8,128)S(1)}, f32[4,512,256]{2,1,0:T(8,128)S(1)}, f32[4,384]{1,0:T(4,128)S(1)}) custom-call(bf16[4,512,256]{2,1,0:T(8,128)(2,1)S(1)} %copy-done, bf16[4,512,256]{2,1,0:T(8,128)(2,1)S(1)} %collective-permute-done.3.refs_1_, bf16[4,512,256]{2,1,0:T(8,128)(2,1)S(1)} %collective-permute-done.4.refs_2_, ...), custom_call_target="tpu_custom_call" | custom-call | flops 2013265920 | bytes 8388608 | tf_op jit(solution)/shard_map/chunk/pallas_call | solution.py:213
  161.7 0.9 collective-permute-done.12.refs_5_
  162.8 1.4 collective-permute-done.17.refs_7_
  164.2 2.8 %chunk.3 = (bf16[4,512,256]{2,1,0:T(8,128)(2,1)S(1)}, f32[4,512,128]{2,1,0:T(8,128)S(1)}, f32[4,512]{1,0:T(4,128)S(1)}, f32[4,512]{1,0:T(4,128)S(1)}) custom-call(bf16[4,512,256]{2,1,0:T(8,128)(2,1)S(1)} %copy-done, bf16[4,512,256]{2,1,0:T(8,128)(2,1)S(1)} %collective-permute-done.3.refs_1_, bf16[4,512,256]{2,1,0:T(8,128)(2,1)S(1)} %collective-permute-done.4.refs_2_, ...), custom_call_target="tpu_custom_call" | custom-call | flops 671088640 | bytes 8388608 | tf_op jit(solution)/shard_map/chunk/pallas_call | solution.py:213
  167.0 7.7 %collective-permute-start.19 = (f32[4,512]{1,0:T(4,128)S(1)}, f32[4,512]{1,0:T(4,128)S(1)}, u32[]{:S(2)}, u32[]{:S(2)}) collective-permute-start(f32[4,512]{1,0:T(4,128)S(1)} %get-tuple-element.53), channel_id=1, source_target_pairs={{0,8},{4,12},{8,0},{12,4},{1,9},{5,13},{9,1},{13,5},{2,10},{6,14},... | collective-permute-start | bytes 24584 | tf_op jit(solution)/shard_map/ppermute | solution.py:293
  174.8 4.3 %means.1 = bf16[8,512,256]{2,1,0:T(8,128)(2,1)} custom-call(s32[4]{0:T(128)S(1)} %and_select_fusion.local_ref, bf16[4,512,256]{2,1,0:T(8,128)(2,1)S(1)} %get-tuple-element.54.part_ref, f32[4,512,128]{2,1,0:T(8,128)S(1)} %get-tuple-element.55.mass_ref, bf16[8,512,256]{2,1,0:T(8,128)(2,1)} %bitcast.14, ...), custom_call_target="tpu_custom_call", output_to_operand_aliasing={{}: (4, {})} | custom-call | flops 2097152 | bytes 4194304 | tf_op jit(solution)/shard_map/means/pallas_call | solution.py:249
  179.2 0.6 copy.23
  (40 shorter events, 1.2 us)
Async XLA Ops:
  1.4 7.0 %collective-permute-start = (s32[4,2]{1,0:T(4,128)S(1)}, s32[4,2]{1,0:T(4,128)S(1)}, u32[]{:S(2)}, u32[]{:S(2)}) collective-permute-start(s32[4,2]{1,0:T(4,128)S(1)} %copy.20.refs_0_.list_ref), channel_id=1, source_target_pairs={{0,4},{4,8},{8,12},{12,0},{1,5},{5,9},{9,13},{13,1},{2,6},{6,10},{... | collective-permute-start | bytes 104 | tf_op jit(solution)/shard_map/ppermute | solution.py:293
  4.4 4.5 %collective-permute-start.1 = (s32[4,2]{1,0:T(4,128)S(1)}, s32[4,2]{1,0:T(4,128)S(1)}, u32[]{:S(2)}, u32[]{:S(2)}) collective-permute-start(s32[4,2]{1,0:T(4,128)S(1)} %copy.20.refs_0_.list_ref), channel_id=1, source_target_pairs={{0,8},{4,12},{8,0},{12,4},{1,9},{5,13},{9,1},{13,5},{2,10},{6,14},... | collective-permute-start | bytes 104 | tf_op jit(solution)/shard_map/ppermute | solution.py:293
  7.0 3.6 %collective-permute-start.2 = (s32[4,2]{1,0:T(4,128)S(1)}, s32[4,2]{1,0:T(4,128)S(1)}, u32[]{:S(2)}, u32[]{:S(2)}) collective-permute-start(s32[4,2]{1,0:T(4,128)S(1)} %copy.20.refs_0_.list_ref), channel_id=1, source_target_pairs={{0,12},{4,0},{8,4},{12,8},{1,13},{5,1},{9,5},{13,9},{2,14},{6,2},{... | collective-permute-start | bytes 104 | tf_op jit(solution)/shard_map/ppermute | solution.py:293
  44.3 23.8 %collective-permute-start.3 = (bf16[4,512,256]{2,1,0:T(8,128)(2,1)}, bf16[4,512,256]{2,1,0:T(8,128)(2,1)S(1)}, u32[]{:S(2)}, u32[]{:S(2)}) collective-permute-start(bf16[4,512,256]{2,1,0:T(8,128)(2,1)} %get-tuple-element.33.refs_0_), channel_id=1, source_target_pairs={{0,2},{1,3},{2,0},{3,1},{4,6},{5,7},{6,4},{7,5},{8,10},{9,11},{10,... | collective-permute-start | bytes 3145736 | tf_op jit(solution)/shard_map/ppermute | solution.py:285
  45.9 52.4 %collective-permute-start.4 = (bf16[4,512,256]{2,1,0:T(8,128)(2,1)}, bf16[4,512,256]{2,1,0:T(8,128)(2,1)S(1)}, u32[]{:S(2)}, u32[]{:S(2)}) collective-permute-start(bf16[4,512,256]{2,1,0:T(8,128)(2,1)} %get-tuple-element.33.refs_0_), channel_id=1, source_target_pairs={{0,1},{1,0},{2,3},{3,2},{4,5},{5,4},{6,7},{7,6},{8,9},{9,8},{10,11... | collective-permute-start | bytes 3145736 | tf_op jit(solution)/shard_map/ppermute | solution.py:285
  68.1 30.2 %collective-permute-start.5 = (bf16[4,512,256]{2,1,0:T(8,128)(2,1)S(1)}, bf16[4,512,256]{2,1,0:T(8,128)(2,1)S(1)}, u32[]{:S(2)}, u32[]{:S(2)}) collective-permute-start(bf16[4,512,256]{2,1,0:T(8,128)(2,1)S(1)} %collective-permute-done.3.refs_1_), channel_id=1, source_target_pairs={{0,1},{1,0},{2,3},{3,2},{4,5},{5,4},{6,7},{7,6},{8,9},{9,8},{10,11... | collective-permute-start | bytes 3145736 | tf_op jit(solution)/shard_map/ppermute | solution.py:285
  68.1 13.9 %collective-permute-start.6 = (bf16[2,384,256]{2,1,0:T(8,128)(2,1)S(1)}, bf16[2,384,256]{2,1,0:T(8,128)(2,1)S(1)}, u32[]{:S(2)}, u32[]{:S(2)}) collective-permute-start(bf16[2,384,256]{2,1,0:T(8,128)(2,1)S(1)} %get-tuple-element.30), channel_id=1, source_target_pairs={{0,4},{4,8},{8,12},{12,0},{1,5},{5,9},{9,13},{13,1},{2,6},{6,10},{... | collective-permute-start | bytes 1179656 | tf_op jit(solution)/shard_map/ppermute | solution.py:312
  68.1 30.2 %collective-permute-start.7 = (bf16[2,384,256]{2,1,0:T(8,128)(2,1)S(1)}, bf16[2,384,256]{2,1,0:T(8,128)(2,1)S(1)}, u32[]{:S(2)}, u32[]{:S(2)}) collective-permute-start(bf16[2,384,256]{2,1,0:T(8,128)(2,1)S(1)} %get-tuple-element.31), channel_id=1, source_target_pairs={{0,8},{4,12},{8,0},{12,4},{1,9},{5,13},{9,1},{13,5},{2,10},{6,14},... | collective-permute-start | bytes 1179656 | tf_op jit(solution)/shard_map/ppermute | solution.py:312
  71.5 26.8 %collective-permute-start.8 = (bf16[2,384,256]{2,1,0:T(8,128)(2,1)S(1)}, bf16[2,384,256]{2,1,0:T(8,128)(2,1)S(1)}, u32[]{:S(2)}, u32[]{:S(2)}) collective-permute-start(bf16[2,384,256]{2,1,0:T(8,128)(2,1)S(1)} %get-tuple-element.32), channel_id=1, source_target_pairs={{0,12},{4,0},{8,4},{12,8},{1,13},{5,1},{9,5},{13,9},{2,14},{6,2},{... | collective-permute-start | bytes 1179656 | tf_op jit(solution)/shard_map/ppermute | solution.py:312
  99.9 19.2 %collective-permute-start.13 = (bf16[4,384,256]{2,1,0:T(8,128)(2,1)}, bf16[4,384,256]{2,1,0:T(8,128)(2,1)}, u32[]{:S(2)}, u32[]{:S(2)}) collective-permute-start(bf16[4,384,256]{2,1,0:T(8,128)(2,1)} %select.13.refs_4_), channel_id=1, source_target_pairs={{0,2},{1,3},{2,0},{3,1},{4,6},{5,7},{6,4},{7,5},{8,10},{9,11},{10,... | collective-permute-start | bytes 2359304 | tf_op jit(solution)/shard_map/ppermute | solution.py:285
  102.1 53.9 %collective-permute-start.14 = (bf16[4,384,256]{2,1,0:T(8,128)(2,1)}, bf16[4,384,256]{2,1,0:T(8,128)(2,1)S(1)}, u32[]{:S(2)}, u32[]{:S(2)}) collective-permute-start(bf16[4,384,256]{2,1,0:T(8,128)(2,1)} %select.13.refs_4_), channel_id=1, source_target_pairs={{0,1},{1,0},{2,3},{3,2},{4,5},{5,4},{6,7},{7,6},{8,9},{9,8},{10,11... | collective-permute-start | bytes 2359304 | tf_op jit(solution)/shard_map/ppermute | solution.py:285
  119.0 37.0 %collective-permute-start.15 = (bf16[4,384,256]{2,1,0:T(8,128)(2,1)}, bf16[4,384,256]{2,1,0:T(8,128)(2,1)S(1)}, u32[]{:S(2)}, u32[]{:S(2)}) collective-permute-start(bf16[4,384,256]{2,1,0:T(8,128)(2,1)} %collective-permute-done.13.refs_5_), channel_id=1, source_target_pairs={{0,1},{1,0},{2,3},{3,2},{4,5},{5,4},{6,7},{7,6},{8,9},{9,8},{10,11... | collective-permute-start | bytes 2359304 | tf_op jit(solution)/shard_map/ppermute | solution.py:285
  119.1 3.1 %copy-start.3 = (s32[4,2]{0,1:T(2,128)S(1)}, s32[4,2]{0,1:T(2,128)}, u32[]{:S(2)}) copy-start(s32[4,2]{0,1:T(2,128)} %param.3) | copy-start | bytes 100
  122.1 33.9 %copy-start = (bf16[4,512,256]{2,1,0:T(8,128)(2,1)S(1)}, bf16[4,512,256]{2,1,0:T(8,128)(2,1)}, u32[]{:S(2)}) copy-start(bf16[4,512,256]{2,1,0:T(8,128)(2,1)} %get-tuple-element.33.refs_0_) | copy-start | bytes 3145732
  122.1 34.0 %copy-start.2 = (bf16[4,384,256]{2,1,0:T(8,128)(2,1)S(1)}, bf16[4,384,256]{2,1,0:T(8,128)(2,1)}, u32[]{:S(2)}) copy-start(bf16[4,384,256]{2,1,0:T(8,128)(2,1)} %select.13.refs_4_) | copy-start | bytes 2359300
  122.2 21.8 %collective-permute-start.10 = (bf16[2,128,256]{2,1,0:T(8,128)(2,1)S(1)}, bf16[2,128,256]{2,1,0:T(8,128)(2,1)S(1)}, u32[]{:S(2)}, u32[]{:S(2)}) collective-permute-start(bf16[2,128,256]{2,1,0:T(8,128)(2,1)S(1)} %get-tuple-element.38), channel_id=1, source_target_pairs={{0,8},{4,12},{8,0},{12,4},{1,9},{5,13},{9,1},{13,5},{2,10},{6,14},... | collective-permute-start | bytes 393224 | tf_op jit(solution)/shard_map/ppermute | solution.py:312
  136.3 11.2 %collective-permute-start.11 = (bf16[2,128,256]{2,1,0:T(8,128)(2,1)S(1)}, bf16[2,128,256]{2,1,0:T(8,128)(2,1)S(1)}, u32[]{:S(2)}, u32[]{:S(2)}) collective-permute-start(bf16[2,128,256]{2,1,0:T(8,128)(2,1)S(1)} %get-tuple-element.39), channel_id=1, source_target_pairs={{0,12},{4,0},{8,4},{12,8},{1,13},{5,1},{9,5},{13,9},{2,14},{6,2},{... | collective-permute-start | bytes 393224 | tf_op jit(solution)/shard_map/ppermute | solution.py:312
  143.2 9.7 %collective-permute-start.9 = (bf16[2,128,256]{2,1,0:T(8,128)(2,1)S(1)}, bf16[2,128,256]{2,1,0:T(8,128)(2,1)S(1)}, u32[]{:S(2)}, u32[]{:S(2)}) collective-permute-start(bf16[2,128,256]{2,1,0:T(8,128)(2,1)S(1)} %get-tuple-element.37), channel_id=1, source_target_pairs={{0,4},{4,8},{8,12},{12,0},{1,5},{5,9},{9,13},{13,1},{2,6},{6,10},{... | collective-permute-start | bytes 393224 | tf_op jit(solution)/shard_map/ppermute | solution.py:312
  154.2 8.4 %collective-permute-start.12 = (bf16[4,128,256]{2,1,0:T(8,128)(2,1)}, bf16[4,128,256]{2,1,0:T(8,128)(2,1)S(1)}, u32[]{:S(2)}, u32[]{:S(2)}) collective-permute-start(bf16[4,128,256]{2,1,0:T(8,128)(2,1)} %select.12.refs_4_), channel_id=1, source_target_pairs={{0,2},{1,3},{2,0},{3,1},{4,6},{5,7},{6,4},{7,5},{8,10},{9,11},{10,... | collective-permute-start | bytes 786440 | tf_op jit(solution)/shard_map/ppermute | solution.py:285
  156.0 8.2 %copy-start.1 = (bf16[4,128,256]{2,1,0:T(8,128)(2,1)S(1)}, bf16[4,128,256]{2,1,0:T(8,128)(2,1)}, u32[]{:S(2)}) copy-start(bf16[4,128,256]{2,1,0:T(8,128)(2,1)} %select.12.refs_4_) | copy-start | bytes 786436
  156.0 6.8 %collective-permute-start.16 = (bf16[4,128,256]{2,1,0:T(8,128)(2,1)}, bf16[4,128,256]{2,1,0:T(8,128)(2,1)S(1)}, u32[]{:S(2)}, u32[]{:S(2)}) collective-permute-start(bf16[4,128,256]{2,1,0:T(8,128)(2,1)} %select.12.refs_4_), channel_id=1, source_target_pairs={{0,1},{1,0},{2,3},{3,2},{4,5},{5,4},{6,7},{7,6},{8,9},{9,8},{10,11... | collective-permute-start | bytes 786440 | tf_op jit(solution)/shard_map/ppermute | solution.py:285
  162.6 1.5 collective-permute-start.17
  167.0 12.1 %collective-permute-start.18 = (f32[4,512]{1,0:T(4,128)S(1)}, f32[4,512]{1,0:T(4,128)S(1)}, u32[]{:S(2)}, u32[]{:S(2)}) collective-permute-start(f32[4,512]{1,0:T(4,128)S(1)} %get-tuple-element.53), channel_id=1, source_target_pairs={{0,4},{4,8},{8,12},{12,0},{1,5},{5,9},{9,13},{13,1},{2,6},{6,10},{... | collective-permute-start | bytes 24584 | tf_op jit(solution)/shard_map/ppermute | solution.py:293
  167.0 12.0 %collective-permute-start.19 = (f32[4,512]{1,0:T(4,128)S(1)}, f32[4,512]{1,0:T(4,128)S(1)}, u32[]{:S(2)}, u32[]{:S(2)}) collective-permute-start(f32[4,512]{1,0:T(4,128)S(1)} %get-tuple-element.53), channel_id=1, source_target_pairs={{0,8},{4,12},{8,0},{12,4},{1,9},{5,13},{9,1},{13,5},{2,10},{6,14},... | collective-permute-start | bytes 24584 | tf_op jit(solution)/shard_map/ppermute | solution.py:293
  174.7 4.3 %collective-permute-start.20 = (f32[4,512]{1,0:T(4,128)S(1)}, f32[4,512]{1,0:T(4,128)S(1)}, u32[]{:S(2)}, u32[]{:S(2)}) collective-permute-start(f32[4,512]{1,0:T(4,128)S(1)} %get-tuple-element.53), channel_id=1, source_target_pairs={{0,12},{4,0},{8,4},{12,8},{1,13},{5,1},{9,5},{13,9},{2,14},{6,2},{... | collective-permute-start | bytes 24584 | tf_op jit(solution)/shard_map/ppermute | solution.py:293

commit v4 on v3

--- a/solution.py
+++ b/solution.py
@@ -11,7 +11,7 @@
 BR = 512
 BLK_DEV = 8
 LANES = 128
-CHUNKS = ((0, 384), (384, 128))
+CHUNKS = ((0, 256), (256, 128), (384, 128))
 
 
 def smem():
@@ -75,7 +75,7 @@
         pltpu.VMEM((capacity, size, feat), blocks.dtype)
         for _, size in CHUNKS
         for _ in range(1, wide_count)
-    ] + [pltpu.HBM((pair_count, BR, feat), blocks.dtype)]
+    ] + [pltpu.VMEM((pair_count, BR, feat), blocks.dtype)]
     copies = (len(shapes) - 1) * capacity + pair_count
     outs = pl.pallas_call(
         functools.partial(pack_kernel, wide_count, pair_count, capacity),
@@ -122,7 +122,7 @@
     pair_count, feat = pairs.shape[0], blocks.shape[-1]
     return pl.pallas_call(
         functools.partial(select_kernel, len(received) + 1, pair_count, start, size),
-        out_shape=pltpu.HBM((pair_count, size, feat), blocks.dtype),
+        out_shape=pltpu.VMEM((pair_count, size, feat), blocks.dtype),
         in_specs=[smem(), smem(), anywhere()] + [anywhere()] * len(received),
         out_specs=anywhere(),
         scratch_shapes=[pltpu.SemaphoreType.DMA((pair_count,))],
@@ -149,24 +149,28 @@
     return sum(square[:, at : at + LANES] for at in range(0, square.shape[1], LANES))
 
 
-def chunk_kernel(narrow_count, first, last, *refs):
-    rows, cols = refs[:narrow_count], refs[narrow_count : 2 * narrow_count]
-    rest = list(refs[2 * narrow_count :])
+def chunk_kernel(first, last, *refs):
+    all_rows, all_cols, rest = refs[:2], refs[2:4], refs[4:]
+    half_count, pair_count = refs[0].shape[:2]
     if not first:
         square_in, mass_in, total_in, sums_in = rest[:4]
         rest = rest[4:]
     if last:
         part_ref, mass_ref, row_ref, sums_ref = rest
+    elif first:
+        square_ref, mass_ref, total_ref, sums_ref = rest
     else:
-        square_ref, mass_ref, total_ref, sums_ref = rest
-    for pair in range(rows[0].shape[0]):
+        mass_ref, total_ref, sums_ref = rest
+    for pair in range(pair_count):
+        rows = [ref.at[i, pair] for ref in all_rows for i in range(half_count)]
+        cols = [ref.at[i, pair] for ref in all_cols for i in range(half_count)]
         if first:
-            square = jnp.sum(tree([lane_sum(row[pair]) for row in rows]), axis=1, keepdims=True)
+            square = jnp.sum(tree([lane_sum(row[...]) for row in rows]), axis=1, keepdims=True)
             square = jnp.broadcast_to(square, (BR, LANES))
         else:
             square = square_in[pair]
-        gram = tree([across(row[pair], col[pair]) for row, col in zip(rows, cols)])
-        other = jnp.sum(tree([lane_sum(col[pair]) for col in cols]).T, axis=0, keepdims=True)
+        gram = tree([across(row[...], col[...]) for row, col in zip(rows, cols)])
+        other = jnp.sum(tree([lane_sum(col[...]) for col in cols]).T, axis=0, keepdims=True)
         size = gram.shape[1]
         pieces, mass = [], None
         for at in range(0, size, LANES):
@@ -177,7 +181,7 @@
         kernel = jnp.concatenate(pieces, axis=1) if len(pieces) > 1 else pieces[0]
         sums = jnp.sum(kernel, axis=0, keepdims=True)
         total = jnp.dot(
-            kernel.astype(jnp.bfloat16), cols[0][pair], preferred_element_type=jnp.float32
+            kernel.astype(jnp.bfloat16), cols[0][...], preferred_element_type=jnp.float32
         )
         if not first:
             mass = mass_in[pair] + mass
@@ -196,7 +200,7 @@
 
 
 def chunk_step(rows, cols, carry, done, last):
-    pair_count, size, feat = cols[0].shape
+    _, pair_count, size, feat = cols[0].shape
     first = carry is None
     lanes = pltpu.VMEM((pair_count, BR, LANES), jnp.float32)
     sums = pltpu.VMEM((pair_count, done + size), jnp.float32)
@@ -208,10 +212,10 @@
             sums,
         ]
     else:
-        shapes = [lanes, lanes, pltpu.VMEM((pair_count, BR, feat), jnp.float32), sums]
+        shapes = [lanes] * (1 + first) + [pltpu.VMEM((pair_count, BR, feat), jnp.float32), sums]
     args = [*rows, *cols, *([] if first else carry)]
-    return pl.pallas_call(
-        functools.partial(chunk_kernel, len(rows), first, last),
+    outs = pl.pallas_call(
+        functools.partial(chunk_kernel, first, last),
         out_shape=shapes,
         in_specs=[vmem()] * len(args),
         out_specs=[vmem()] * len(shapes),
@@ -223,6 +227,7 @@
         ),
         name="chunk",
     )(*[in_vmem(x) for x in args])
+    return outs if first or last else [carry[0], *outs]
 
 
 def mean_kernel(pair_count, local_ref, part_ref, mass_ref, block_ref, _, out_ref, total, weight):
@@ -273,18 +278,26 @@
     )(row_local, part, mass, in_hbm(blocks), in_hbm(blocks))
 
 
-def gather_narrow(part, before=None):
+def hop(parts, step):
     count = lax.axis_size("narrow")
-    parts = [part]
-    step = count // 2
-    while step:
-        perm = [(i, i ^ step) for i in range(count)]
-        if step == 1 and before is not None:
-            came, before = lax.optimization_barrier((parts[1:], before))
-            parts = [part, *came]
-        parts = parts + [lax.ppermute(x, "narrow", perm) for x in parts]
+    return parts, lax.ppermute(parts, "narrow", [(i, i ^ step) for i in range(count)])
+
+
+def first_hops(part):
+    parts = part[None]
+    step = lax.axis_size("narrow") // 2
+    while step > 1:
+        parts = jnp.concatenate(hop(parts, step), axis=0)
         step //= 2
-    return parts, before
+    return parts
+
+
+def to_wide(pieces):
+    count = lax.axis_size("wide")
+    return [
+        lax.ppermute(piece, "wide", [(i, (i + shift) % count) for i in range(count)])
+        for shift, piece in enumerate(pieces, 1)
+    ]
 
 
 def from_others(part):
@@ -305,23 +318,32 @@
     row_local = pair_list[:, 0] % BLK_DEV
     lists = from_others(pair_list)
     outgoing, row_slices = pack(me, lists, blocks, capacity)
-    rows, _ = gather_narrow(row_slices)
-    carry, done = None, 0
-    for chunk, (start, size) in enumerate(CHUNKS):
-        received = [
-            lax.ppermute(
-                outgoing[chunk][shift - 1],
-                "wide",
-                [(i, (i + shift) % wide_count) for i in range(wide_count)],
-            )
-            for shift in range(1, wide_count)
-        ]
-        if chunk == 0:
-            rows, received = lax.optimization_barrier((rows, received))
-        col_part = select(me, pair_list, blocks, received, start, size)
-        cols, carry = gather_narrow(col_part, carry)
-        carry = chunk_step(rows, cols, carry, done, chunk == len(CHUNKS) - 1)
-        done += size
+    chunks = len(CHUNKS)
+    fixed = lax.optimization_barrier
+    rows_half, received = fixed((first_hops(row_slices), to_wide(outgoing[0])))
+    rows = carry = half = None
+    done = 0
+    for phase in range(1, chunks + 2):
+        last_half = half
+        if phase <= chunks:
+            start, size = CHUNKS[phase - 1]
+            picked = select(me, pair_list, blocks, received, start, size)
+            half = first_hops(picked)
+        else:
+            half = None
+        if phase < chunks:
+            received = to_wide(outgoing[phase])
+        if phase == 1:
+            rows = hop(rows_half, 1)
+            half, received, rows = fixed((half, received, rows))
+            continue
+        whole = hop(last_half, 1)
+        carry = chunk_step(rows, whole, carry, done, phase == chunks + 1)
+        done += CHUNKS[phase - 2][1]
+        if phase < chunks:
+            half, received, carry = fixed((half, received, carry))
+        elif phase == chunks:
+            half, carry = fixed((half, carry))
     part, mass, row_sums, col_sums = carry
     every_sum = jnp.concatenate(from_others(col_sums), axis=0)
     mean = means(row_local, part, mass, blocks)

time: 177 us -> 107 us (0.60); the launches traced: 180 us -> 106 us
  waiting for transfers between devices: 78.9 us -> 42.2 us
  Pallas kernels: 49.3 us -> 21.7 us
  starting transfers between devices: 44.7 us -> 29 us
  local copies, waits for them, and re-layouts: 5 us -> 9.94 us
    ppermute x15 -> x17, waiting for transfers between devices: 76.6 us -> 39.9 us  [the longest x8 37.9 us: hop(): lax.ppermute(parts, 'narrow', [(i, i ^ step) for i in range(count)])]
    pallas_call x1, Pallas kernels: 33.7 us -> 2.67 us  [pack(): pl.pallas_call(functools.partial(pack_kernel, wide_count, pair_count, cap...]
    ppermute x15 -> x17, starting transfers between devices: 30 us -> 17.7 us  [the longest x9 11.2 us: to_wide(): lax.ppermute(piece, 'wide', [(i, (i + shift) % count) for i in range(coun...]
    unnamed x11 -> x19, local copies, waits for them, and re-layouts: 4.45 us -> 9.39 us
    ppermute x6, starting transfers between devices: 14.7 us -> 11.3 us  [from_others(): lax.ppermute(part, 'wide', [(i, (i + shift) % count) for i in range(count)])]
    concatenate x0 -> x4, other arithmetic: none -> 2.15 us  [first_hops(): parts = jnp.concatenate(hop(parts, step), axis=0)]
    pallas_call x2 -> x3, Pallas kernels: 2.88 us -> 4.97 us  [select(): pl.pallas_call(functools.partial(select_kernel, len(received) + 1, pair_c...]
    pallas_call x2 -> x3, Pallas kernels: 8.44 us -> 9.78 us  [chunk_step(): pl.pallas_call(functools.partial(chunk_kernel, first, last), out_shape=sh...]
  transfers between devices with their start and end apart: 21 -> 23, of which waited for: 10 -> 8; matrix products, arithmetic and copies ran while one was open for 3% -> 4% of each run, Pallas kernels for 6% -> 12%
where the time goes in v4:
time: 107 us; the launch traced here: 106 us
  waiting for transfers between devices  42.2 us (39%)
  starting transfers between devices  29 us (27%)
  Pallas kernels  21.7 us (20%)
  local copies, waits for them, and re-layouts  9.94 us (9%)
  other arithmetic  2.61 us (2%)
    ppermute x8, waiting for transfers between devices, hop(): lax.ppermute(parts, 'narrow', [(i, i ^ step) for i in range(count)])  37.9 us
    ppermute x6, starting transfers between devices, from_others(): lax.ppermute(part, 'wide', [(i, (i + shift) % count) for i in range(count)])  11.3 us
    ppermute x9, starting transfers between devices, to_wide(): lax.ppermute(piece, 'wide', [(i, (i + shift) % count) for i in range(coun...  11.2 us
    pallas_call x3, Pallas kernels, chunk_step(): pl.pallas_call(functools.partial(chunk_kernel, first, last), out_shape=sh...  9.78 us
    unnamed x19, local copies, waits for them, and re-layouts  9.39 us
    ppermute x8, starting transfers between devices, hop(): lax.ppermute(parts, 'narrow', [(i, i ^ step) for i in range(count)])  6.44 us
    pallas_call x3, Pallas kernels, select(): pl.pallas_call(functools.partial(select_kernel, len(received) + 1, pair_c...  4.97 us
    pallas_call x1, Pallas kernels, means(): pl.pallas_call(functools.partial(mean_kernel, pair_count), out_shape=jax....  4.31 us
  transfers between devices with their start and end apart: 23, of which 8 were waited for; matrix products, arithmetic and copies ran while one was open for 4% of the time, Pallas kernels for 12%

profile of v4, /device:TPU:0, one launch (start us, length us, event | category | flops | bytes accessed | tf_op | source)
XLA Modules:
  0.0 106.3 jit_solution(3842783142177922139)
XLA Ops:
  1.4 3.0 %collective-permute-start = (s32[4,2]{1,0:T(4,128)S(1)}, s32[4,2]{1,0:T(4,128)S(1)}, u32[]{:S(2)}, u32[]{:S(2)}) collective-permute-start(s32[4,2]{1,0:T(4,128)S(1)} %copy.23.refs_0_.list_ref), channel_id=1, source_target_pairs={{0,4},{4,8},{8,12},{12,0},{1,5},{5,9},{9,13},{13,1},{2,6},{6,10},{... | collective-permute-start | bytes 104 | tf_op jit(solution)/shard_map/ppermute | solution.py:306
  4.4 2.6 %collective-permute-start.1 = (s32[4,2]{1,0:T(4,128)S(1)}, s32[4,2]{1,0:T(4,128)S(1)}, u32[]{:S(2)}, u32[]{:S(2)}) collective-permute-start(s32[4,2]{1,0:T(4,128)S(1)} %copy.23.refs_0_.list_ref), channel_id=1, source_target_pairs={{0,8},{4,12},{8,0},{12,4},{1,9},{5,13},{9,1},{13,5},{2,10},{6,14},... | collective-permute-start | bytes 104 | tf_op jit(solution)/shard_map/ppermute | solution.py:306
  7.0 1.3 %collective-permute-start.2 = (s32[4,2]{1,0:T(4,128)S(1)}, s32[4,2]{1,0:T(4,128)S(1)}, u32[]{:S(2)}, u32[]{:S(2)}) collective-permute-start(s32[4,2]{1,0:T(4,128)S(1)} %copy.23.refs_0_.list_ref), channel_id=1, source_target_pairs={{0,12},{4,0},{8,4},{12,8},{1,13},{5,1},{9,5},{13,9},{2,14},{6,2},{... | collective-permute-start | bytes 104 | tf_op jit(solution)/shard_map/ppermute | solution.py:306
  8.9 1.7 %collective-permute-done.2.refs_3_ = s32[4,2]{1,0:T(4,128)S(1)} collective-permute-done((s32[4,2]{1,0:T(4,128)S(1)}, s32[4,2]{1,0:T(4,128)S(1)}, u32[]{:S(2)}, u32[]{:S(2)}) %collective-permute-start.2) | collective-permute-done | bytes 64 | tf_op jit(solution)/shard_map/ppermute | solution.py:306
  10.6 2.7 %pack.1 = (bf16[2,256,256]{2,1,0:T(8,128)(2,1)S(1)}, bf16[2,256,256]{2,1,0:T(8,128)(2,1)S(1)}, bf16[2,256,256]{2,1,0:T(8,128)(2,1)S(1)}, bf16[2,128,256]{2,1,0:T...) custom-call(s32[1]{0:T(128)} %bitcast.1.me_ref, ...), custom_call_target="tpu_custom_call" | custom-call | tf_op jit(solution)/shard_map/pack/pallas_call | solution.py:80
  13.3 1.6 %collective-permute-start.3 = (bf16[1,4,512,256]{3,2,1,0:T(8,128)(2,1)S(1)}, bf16[1,4,512,256]{3,2,1,0:T(8,128)(2,1)S(1)}, u32[]{:S(2)}, u32[]{:S(2)}) collective-permute-start(bf16[1,4,512,256]{3,2,1,0:T(8,128)(2,1)S(1)} %bitcast.16), channel_id=1, source_target_pairs={{0,2},{1,3},{2,0},{3,1},{4,6},{5,7},{6,4},{7,5},{8,10},{9,11},{10,... | collective-permute-start | bytes 3145736 | tf_op jit(solution)/shard_map/ppermute | solution.py:283
  15.0 3.5 %collective-permute-start.5 = (bf16[2,256,256]{2,1,0:T(8,128)(2,1)S(1)}, bf16[2,256,256]{2,1,0:T(8,128)(2,1)S(1)}, u32[]{:S(2)}, u32[]{:S(2)}) collective-permute-start(bf16[2,256,256]{2,1,0:T(8,128)(2,1)S(1)} %get-tuple-element.48), channel_id=1, source_target_pairs={{0,8},{4,12},{8,0},{12,4},{1,9},{5,13},{9,1},{13,5},{2,10},{6,14},... | collective-permute-start | bytes 786440 | tf_op jit(solution)/shard_map/ppermute | solution.py:298
  18.7 18.1 %collective-permute-done.3 = bf16[1,4,512,256]{3,2,1,0:T(8,128)(2,1)S(1)} collective-permute-done((bf16[1,4,512,256]{3,2,1,0:T(8,128)(2,1)S(1)}, bf16[1,4,512,256]{3,2,1,0:T(8,128)(2,1)S(1)}, u32[]{:S(2)}, u32[]{:S(2)}) %collective-permute-start.3) | collective-permute-done | bytes 1048608 | tf_op jit(solution)/shard_map/ppermute | solution.py:283
  37.1 1.8 %select.13 = bf16[4,256,256]{2,1,0:T(8,128)(2,1)S(1)} custom-call(s32[1]{0:T(128)} %bitcast.1.me_ref, s32[4,2]{1,0:T(4,128)S(1)} %copy.23.refs_0_.list_ref, bf16[8,512,256]{2,1,0:T(8,128)(2,1)} %bitcast.23, bf16[2,256,256]{2,1,0:T(8,128)(2,1)S(1)} %collective-permute-done.4.refs_0_, bf16[2,256,256]{2,1,0:T(8,128)(2,1)S(1)} %collective-permute-done.5.refs_1_, ...), custom_call_target="tpu_custom_call" | custom-call | tf_op jit(solution)/shard_map/select/pallas_call | solution.py:123
  38.9 1.6 %collective-permute-start.7 = (bf16[1,4,256,256]{3,2,1,0:T(8,128)(2,1)S(1)}, bf16[1,4,256,256]{3,2,1,0:T(8,128)(2,1)S(1)}, u32[]{:S(2)}, u32[]{:S(2)}) collective-permute-start(bf16[1,4,256,256]{3,2,1,0:T(8,128)(2,1)S(1)} %bitcast.14), channel_id=1, source_target_pairs={{0,2},{1,3},{2,0},{3,1},{4,6},{5,7},{6,4},{7,5},{8,10},{9,11},{10,... | collective-permute-start | bytes 1572872 | tf_op jit(solution)/shard_map/ppermute | solution.py:283
  40.5 2.9 %collective-permute-start.10 = (bf16[2,128,256]{2,1,0:T(8,128)(2,1)S(1)}, bf16[2,128,256]{2,1,0:T(8,128)(2,1)S(1)}, u32[]{:S(2)}, u32[]{:S(2)}) collective-permute-start(bf16[2,128,256]{2,1,0:T(8,128)(2,1)S(1)} %get-tuple-element.55), channel_id=1, source_target_pairs={{0,12},{4,0},{8,4},{12,8},{1,13},{5,1},{9,5},{13,9},{2,14},{6,2},{... | collective-permute-start | bytes 393224 | tf_op jit(solution)/shard_map/ppermute | solution.py:298
  44.0 9.3 %collective-permute-done.7 = bf16[1,4,256,256]{3,2,1,0:T(8,128)(2,1)S(1)} collective-permute-done((bf16[1,4,256,256]{3,2,1,0:T(8,128)(2,1)S(1)}, bf16[1,4,256,256]{3,2,1,0:T(8,128)(2,1)S(1)}, u32[]{:S(2)}, u32[]{:S(2)}) %collective-permute-start.7) | collective-permute-done | bytes 524320 | tf_op jit(solution)/shard_map/ppermute | solution.py:283
  53.4 2.0 %collective-permute-done.9.refs_1_ = bf16[2,128,256]{2,1,0:T(8,128)(2,1)S(1)} collective-permute-done((bf16[2,128,256]{2,1,0:T(8,128)(2,1)S(1)}, bf16[2,128,256]{2,1,0:T(8,128)(2,1)S(1)}, u32[]{:S(2)}, u32[]{:S(2)}) %collective-permute-start.9) | collective-permute-done | bytes 131104 | tf_op jit(solution)/shard_map/ppermute | solution.py:298
  55.5 1.6 %select.14 = bf16[4,128,256]{2,1,0:T(8,128)(2,1)S(1)} custom-call(s32[1]{0:T(128)} %bitcast.1.me_ref, s32[4,2]{1,0:T(4,128)S(1)} %copy.23.refs_0_.list_ref, bf16[8,512,256]{2,1,0:T(8,128)(2,1)} %bitcast.24, bf16[2,128,256]{2,1,0:T(8,128)(2,1)S(1)} %collective-permute-done.8.refs_0_, bf16[2,128,256]{2,1,0:T(8,128)(2,1)S(1)} %collective-permute-done.9.refs_1_, ...), custom_call_target="tpu_custom_call" | custom-call | tf_op jit(solution)/shard_map/select/pallas_call | solution.py:123
  57.1 1.6 %collective-permute-start.12 = (bf16[1,4,128,256]{3,2,1,0:T(8,128)(2,1)S(1)}, bf16[1,4,128,256]{3,2,1,0:T(8,128)(2,1)S(1)}, u32[]{:S(2)}, u32[]{:S(2)}) collective-permute-start(bf16[1,4,128,256]{3,2,1,0:T(8,128)(2,1)S(1)} %bitcast.18), channel_id=1, source_target_pairs={{0,2},{1,3},{2,0},{3,1},{4,6},{5,7},{6,4},{7,5},{8,10},{9,11},{10,... | collective-permute-start | bytes 786440 | tf_op jit(solution)/shard_map/ppermute | solution.py:283
  58.7 3.2 %collective-permute-start.14 = (bf16[2,128,256]{2,1,0:T(8,128)(2,1)S(1)}, bf16[2,128,256]{2,1,0:T(8,128)(2,1)S(1)}, u32[]{:S(2)}, u32[]{:S(2)}) collective-permute-start(bf16[2,128,256]{2,1,0:T(8,128)(2,1)S(1)} %get-tuple-element.63), channel_id=1, source_target_pairs={{0,8},{4,12},{8,0},{12,4},{1,9},{5,13},{9,1},{13,5},{2,10},{6,14},... | collective-permute-start | bytes 393224 | tf_op jit(solution)/shard_map/ppermute | solution.py:298
  62.6 3.3 %collective-permute-done.12 = bf16[1,4,128,256]{3,2,1,0:T(8,128)(2,1)S(1)} collective-permute-done((bf16[1,4,128,256]{3,2,1,0:T(8,128)(2,1)S(1)}, bf16[1,4,128,256]{3,2,1,0:T(8,128)(2,1)S(1)}, u32[]{:S(2)}, u32[]{:S(2)}) %collective-permute-start.12) | collective-permute-done | bytes 262176 | tf_op jit(solution)/shard_map/ppermute | solution.py:283
  66.7 3.1 %chunk.3 = (f32[4,512,128]{2,1,0:T(8,128)S(1)}, f32[4,512,128]{2,1,0:T(8,128)S(1)}, f32[4,512,256]{2,1,0:T(8,128)S(1)}, f32[4,256]{1,0:T(4,128)S(1)}) custom-call(bf16[2,4,512,256]{3,2,1,0:T(8,128)(2,1)S(1)} %pad_maximum_fusion.refs_0_, bf16[2,4,512,256]{3,2,1,0:T(8,128)(2,1)S(1)} %collective-permute-done.11.refs_1_, ...), custom_call_target="tpu_custom_call" | custom-call | flops 1342177280 | bytes 8388608 | tf_op jit(solution)/shard_map/chunk/pallas_call | solution.py:217
  69.8 1.3 %copy-done.2 = f32[4,512,256]{2,1,0:T(8,128)} copy-done((f32[4,512,256]{2,1,0:T(8,128)}, f32[4,512,256]{2,1,0:T(8,128)S(1)}, u32[]{:S(2)}) %copy-start.2) | copy-done | bytes 2097176
  72.2 1.6 %select.15 = bf16[4,128,256]{2,1,0:T(8,128)(2,1)S(1)} custom-call(s32[1]{0:T(128)} %bitcast.1.me_ref, s32[4,2]{1,0:T(4,128)S(1)} %copy.23.refs_0_.list_ref, bf16[8,512,256]{2,1,0:T(8,128)(2,1)} %bitcast.25, bf16[2,128,256]{2,1,0:T(8,128)(2,1)S(1)} %collective-permute-done.13.refs_0_, bf16[2,128,256]{2,1,0:T(8,128)(2,1)S(1)} %collective-permute-done.14.refs_1_, ...), custom_call_target="tpu_custom_call" | custom-call | tf_op jit(solution)/shard_map/select/pallas_call | solution.py:123
  73.8 1.6 %collective-permute-start.17 = (bf16[1,4,128,256]{3,2,1,0:T(8,128)(2,1)S(1)}, bf16[1,4,128,256]{3,2,1,0:T(8,128)(2,1)}, u32[]{:S(2)}, u32[]{:S(2)}) collective-permute-start(bf16[1,4,128,256]{3,2,1,0:T(8,128)(2,1)S(1)} %bitcast.20), channel_id=1, source_target_pairs={{0,2},{1,3},{2,0},{3,1},{4,6},{5,7},{6,4},{7,5},{8,10},{9,11},{10,... | collective-permute-start | bytes 786440 | tf_op jit(solution)/shard_map/ppermute | solution.py:283
  75.4 1.3 %copy.27._ = bf16[8,512,256]{2,1,0:T(8,128)(2,1)} copy(bf16[8,512,256]{2,1,0:T(8,128)(2,1)S(1)} %bitcast.27) | data formatting | bytes 4194304
  76.9 5.7 %collective-permute-done.17 = bf16[1,4,128,256]{3,2,1,0:T(8,128)(2,1)} collective-permute-done((bf16[1,4,128,256]{3,2,1,0:T(8,128)(2,1)S(1)}, bf16[1,4,128,256]{3,2,1,0:T(8,128)(2,1)}, u32[]{:S(2)}, u32[]{:S(2)}) %collective-permute-start.17) | collective-permute-done | bytes 262176 | tf_op jit(solution)/shard_map/ppermute | solution.py:283
  83.7 1.6 %copy-done.1 = bf16[2,4,512,256]{3,2,1,0:T(8,128)(2,1)S(1)} copy-done((bf16[2,4,512,256]{3,2,1,0:T(8,128)(2,1)S(1)}, bf16[2,4,512,256]{3,2,1,0:T(8,128)(2,1)}, u32[]{:S(2)}) %copy-start.1) | copy-done | bytes 2097176
  85.3 1.6 %copy-done.3 = f32[4,512,256]{2,1,0:T(8,128)S(1)} copy-done((f32[4,512,256]{2,1,0:T(8,128)S(1)}, f32[4,512,256]{2,1,0:T(8,128)}, u32[]{:S(2)}) %copy-start.3) | copy-done | bytes 2097176
  86.9 1.2 %copy-done.5 = f32[4,512,128]{2,1,0:T(8,128)S(1)} copy-done((f32[4,512,128]{2,1,0:T(8,128)S(1)}, f32[4,512,128]{2,1,0:T(8,128)}, u32[]{:S(2)}) %copy-start.5) | copy-done | bytes 1048600
  88.1 3.9 %chunk.4 = (f32[4,512,128]{2,1,0:T(8,128)S(1)}, f32[4,512,256]{2,1,0:T(8,128)S(1)}, f32[4,384]{1,0:T(4,128)S(1)}) custom-call(bf16[2,4,512,256]{3,2,1,0:T(8,128)(2,1)S(1)} %pad_maximum_fusion.refs_0_, bf16[2,4,512,256]{3,2,1,0:T(8,128)(2,1)S(1)} %copy-done.1, bf16[2,4,128,256]{3,2,1,0:T(8,128)(2,1)} %pad_maximum_fusion.2.refs_2_, ...), custom_call_target="tpu_custom_call" | custom-call | flops 671088640 | bytes 8388608 | tf_op jit(solution)/shard_map/chunk/pallas_call | solution.py:217
  92.6 1.4 %collective-permute-done.19.refs_3_ = bf16[2,4,128,256]{3,2,1,0:T(8,128)(2,1)S(1)} collective-permute-done((bf16[2,4,128,256]{3,2,1,0:T(8,128)(2,1)S(1)}, bf16[2,4,128,256]{3,2,1,0:T(8,128)(2,1)S(1)}, u32[]{:S(2)}, u32[]{:S(2)}) %collective-permute-start.19) | collective-permute-done | bytes 524320 | tf_op jit(solution)/shard_map/ppermute | solution.py:283
  94.0 2.8 %chunk.5 = (bf16[4,512,256]{2,1,0:T(8,128)(2,1)S(1)}, f32[4,512,128]{2,1,0:T(8,128)S(1)}, f32[4,512]{1,0:T(4,128)S(1)}, f32[4,512]{1,0:T(4,128)S(1)}) custom-call(bf16[2,4,512,256]{3,2,1,0:T(8,128)(2,1)S(1)} %pad_maximum_fusion.refs_0_, bf16[2,4,512,256]{3,2,1,0:T(8,128)(2,1)S(1)} %copy-done.1, bf16[2,4,128,256]{3,2,1,0:T(8,128)(2,1)S(1)} %pad_maximum_fusion.3.refs_2_, ...), custom_call_target="tpu_custom_call" | custom-call | flops 671088640 | bytes 8388608 | tf_op jit(solution)/shard_map/chunk/pallas_call | solution.py:217
  96.8 1.9 %collective-permute-start.20 = (f32[4,512]{1,0:T(4,128)S(1)}, f32[4,512]{1,0:T(4,128)S(1)}, u32[]{:S(2)}, u32[]{:S(2)}) collective-permute-start(f32[4,512]{1,0:T(4,128)S(1)} %get-tuple-element.87), channel_id=1, source_target_pairs={{0,4},{4,8},{8,12},{12,0},{1,5},{5,9},{9,13},{13,1},{2,6},{6,10},{... | collective-permute-start | bytes 24584 | tf_op jit(solution)/shard_map/ppermute | solution.py:306
  98.7 1.5 %collective-permute-start.21 = (f32[4,512]{1,0:T(4,128)S(1)}, f32[4,512]{1,0:T(4,128)S(1)}, u32[]{:S(2)}, u32[]{:S(2)}) collective-permute-start(f32[4,512]{1,0:T(4,128)S(1)} %get-tuple-element.87), channel_id=1, source_target_pairs={{0,8},{4,12},{8,0},{12,4},{1,9},{5,13},{9,1},{13,5},{2,10},{6,14},... | collective-permute-start | bytes 24584 | tf_op jit(solution)/shard_map/ppermute | solution.py:306
  101.2 4.3 %means.1 = bf16[8,512,256]{2,1,0:T(8,128)(2,1)} custom-call(s32[4]{0:T(128)S(1)} %and_select_fusion.local_ref, bf16[4,512,256]{2,1,0:T(8,128)(2,1)S(1)} %get-tuple-element.88.part_ref, f32[4,512,128]{2,1,0:T(8,128)S(1)} %get-tuple-element.89.mass_ref, bf16[8,512,256]{2,1,0:T(8,128)(2,1)} %bitcast.26, ...), custom_call_target="tpu_custom_call", output_to_operand_aliasing={{}: (4, {})} | custom-call | flops 2097152 | bytes 4194304 | tf_op jit(solution)/shard_map/means/pallas_call | solution.py:254
  (58 shorter events, 8.9 us)
Async XLA Ops:
  1.4 7.0 %collective-permute-start = (s32[4,2]{1,0:T(4,128)S(1)}, s32[4,2]{1,0:T(4,128)S(1)}, u32[]{:S(2)}, u32[]{:S(2)}) collective-permute-start(s32[4,2]{1,0:T(4,128)S(1)} %copy.23.refs_0_.list_ref), channel_id=1, source_target_pairs={{0,4},{4,8},{8,12},{12,0},{1,5},{5,9},{9,13},{13,1},{2,6},{6,10},{... | collective-permute-start | bytes 104 | tf_op jit(solution)/shard_map/ppermute | solution.py:306
  4.4 4.5 %collective-permute-start.1 = (s32[4,2]{1,0:T(4,128)S(1)}, s32[4,2]{1,0:T(4,128)S(1)}, u32[]{:S(2)}, u32[]{:S(2)}) collective-permute-start(s32[4,2]{1,0:T(4,128)S(1)} %copy.23.refs_0_.list_ref), channel_id=1, source_target_pairs={{0,8},{4,12},{8,0},{12,4},{1,9},{5,13},{9,1},{13,5},{2,10},{6,14},... | collective-permute-start | bytes 104 | tf_op jit(solution)/shard_map/ppermute | solution.py:306
  7.0 3.6 %collective-permute-start.2 = (s32[4,2]{1,0:T(4,128)S(1)}, s32[4,2]{1,0:T(4,128)S(1)}, u32[]{:S(2)}, u32[]{:S(2)}) collective-permute-start(s32[4,2]{1,0:T(4,128)S(1)} %copy.23.refs_0_.list_ref), channel_id=1, source_target_pairs={{0,12},{4,0},{8,4},{12,8},{1,13},{5,1},{9,5},{13,9},{2,14},{6,2},{... | collective-permute-start | bytes 104 | tf_op jit(solution)/shard_map/ppermute | solution.py:306
  13.3 23.6 %collective-permute-start.3 = (bf16[1,4,512,256]{3,2,1,0:T(8,128)(2,1)S(1)}, bf16[1,4,512,256]{3,2,1,0:T(8,128)(2,1)S(1)}, u32[]{:S(2)}, u32[]{:S(2)}) collective-permute-start(bf16[1,4,512,256]{3,2,1,0:T(8,128)(2,1)S(1)} %bitcast.16), channel_id=1, source_target_pairs={{0,2},{1,3},{2,0},{3,1},{4,6},{5,7},{6,4},{7,5},{8,10},{9,11},{10,... | collective-permute-start | bytes 3145736 | tf_op jit(solution)/shard_map/ppermute | solution.py:283
  14.8 22.2 %collective-permute-start.4 = (bf16[2,256,256]{2,1,0:T(8,128)(2,1)S(1)}, bf16[2,256,256]{2,1,0:T(8,128)(2,1)S(1)}, u32[]{:S(2)}, u32[]{:S(2)}) collective-permute-start(bf16[2,256,256]{2,1,0:T(8,128)(2,1)S(1)} %get-tuple-element.47), channel_id=1, source_target_pairs={{0,4},{4,8},{8,12},{12,0},{1,5},{5,9},{9,13},{13,1},{2,6},{6,10},{... | collective-permute-start | bytes 786440 | tf_op jit(solution)/shard_map/ppermute | solution.py:298
  15.0 22.0 %collective-permute-start.5 = (bf16[2,256,256]{2,1,0:T(8,128)(2,1)S(1)}, bf16[2,256,256]{2,1,0:T(8,128)(2,1)S(1)}, u32[]{:S(2)}, u32[]{:S(2)}) collective-permute-start(bf16[2,256,256]{2,1,0:T(8,128)(2,1)S(1)} %get-tuple-element.48), channel_id=1, source_target_pairs={{0,8},{4,12},{8,0},{12,4},{1,9},{5,13},{9,1},{13,5},{2,10},{6,14},... | collective-permute-start | bytes 786440 | tf_op jit(solution)/shard_map/ppermute | solution.py:298
  18.5 18.5 %collective-permute-start.6 = (bf16[2,256,256]{2,1,0:T(8,128)(2,1)S(1)}, bf16[2,256,256]{2,1,0:T(8,128)(2,1)S(1)}, u32[]{:S(2)}, u32[]{:S(2)}) collective-permute-start(bf16[2,256,256]{2,1,0:T(8,128)(2,1)S(1)} %get-tuple-element.49), channel_id=1, source_target_pairs={{0,12},{4,0},{8,4},{12,8},{1,13},{5,1},{9,5},{13,9},{2,14},{6,2},{... | collective-permute-start | bytes 786440 | tf_op jit(solution)/shard_map/ppermute | solution.py:298
  37.1 18.4 %collective-permute-start.11 = (bf16[2,4,512,256]{3,2,1,0:T(8,128)(2,1)S(1)}, bf16[2,4,512,256]{3,2,1,0:T(8,128)(2,1)S(1)}, u32[]{:S(2)}, u32[]{:S(2)}) collective-permute-start(bf16[2,4,512,256]{3,2,1,0:T(8,128)(2,1)S(1)} %pad_maximum_fusion.refs_0_), channel_id=1, source_target_pairs={{0,1},{1,0},{2,3},{3,2},{4,5},{5,4},{6,7},{7,6},{8,9},{9,8},{10,11... | collective-permute-start | bytes 6291464 | tf_op jit(solution)/shard_map/ppermute | solution.py:283
  38.9 14.4 %collective-permute-start.7 = (bf16[1,4,256,256]{3,2,1,0:T(8,128)(2,1)S(1)}, bf16[1,4,256,256]{3,2,1,0:T(8,128)(2,1)S(1)}, u32[]{:S(2)}, u32[]{:S(2)}) collective-permute-start(bf16[1,4,256,256]{3,2,1,0:T(8,128)(2,1)S(1)} %bitcast.14), channel_id=1, source_target_pairs={{0,2},{1,3},{2,0},{3,1},{4,6},{5,7},{6,4},{7,5},{8,10},{9,11},{10,... | collective-permute-start | bytes 1572872 | tf_op jit(solution)/shard_map/ppermute | solution.py:283
  40.5 12.9 %collective-permute-start.10 = (bf16[2,128,256]{2,1,0:T(8,128)(2,1)S(1)}, bf16[2,128,256]{2,1,0:T(8,128)(2,1)S(1)}, u32[]{:S(2)}, u32[]{:S(2)}) collective-permute-start(bf16[2,128,256]{2,1,0:T(8,128)(2,1)S(1)} %get-tuple-element.55), channel_id=1, source_target_pairs={{0,12},{4,0},{8,4},{12,8},{1,13},{5,1},{9,5},{13,9},{2,14},{6,2},{... | collective-permute-start | bytes 393224 | tf_op jit(solution)/shard_map/ppermute | solution.py:298
  43.4 10.0 %collective-permute-start.8 = (bf16[2,128,256]{2,1,0:T(8,128)(2,1)S(1)}, bf16[2,128,256]{2,1,0:T(8,128)(2,1)S(1)}, u32[]{:S(2)}, u32[]{:S(2)}) collective-permute-start(bf16[2,128,256]{2,1,0:T(8,128)(2,1)S(1)} %get-tuple-element.53), channel_id=1, source_target_pairs={{0,4},{4,8},{8,12},{12,0},{1,5},{5,9},{9,13},{13,1},{2,6},{6,10},{... | collective-permute-start | bytes 393224 | tf_op jit(solution)/shard_map/ppermute | solution.py:298
  43.4 15.2 %copy-start.7 = (s32[4,2]{0,1:T(2,128)S(1)}, s32[4,2]{0,1:T(2,128)}, u32[]{:S(2)}) copy-start(s32[4,2]{0,1:T(2,128)} %param.3) | copy-start | bytes 100
  43.4 12.1 %collective-permute-start.9 = (bf16[2,128,256]{2,1,0:T(8,128)(2,1)S(1)}, bf16[2,128,256]{2,1,0:T(8,128)(2,1)S(1)}, u32[]{:S(2)}, u32[]{:S(2)}) collective-permute-start(bf16[2,128,256]{2,1,0:T(8,128)(2,1)S(1)} %get-tuple-element.54), channel_id=1, source_target_pairs={{0,8},{4,12},{8,0},{12,4},{1,9},{5,13},{9,1},{13,5},{2,10},{6,14},... | collective-permute-start | bytes 393224 | tf_op jit(solution)/shard_map/ppermute | solution.py:298
  55.5 14.3 %copy-start = (bf16[2,4,512,256]{3,2,1,0:T(8,128)(2,1)}, bf16[2,4,512,256]{3,2,1,0:T(8,128)(2,1)S(1)}, u32[]{:S(2)}) copy-start(bf16[2,4,512,256]{3,2,1,0:T(8,128)(2,1)S(1)} %collective-permute-done.11.refs_1_) | copy-start | bytes 6291460
  55.5 11.2 %collective-permute-start.16 = (bf16[2,4,256,256]{3,2,1,0:T(8,128)(2,1)S(1)}, bf16[2,4,256,256]{3,2,1,0:T(8,128)(2,1)S(1)}, u32[]{:S(2)}, u32[]{:S(2)}) collective-permute-start(bf16[2,4,256,256]{3,2,1,0:T(8,128)(2,1)S(1)} %pad_maximum_fusion.1.refs_2_), channel_id=1, source_target_pairs={{0,1},{1,0},{2,3},{3,2},{4,5},{5,4},{6,7},{7,6},{8,9},{9,8},{10,11... | collective-permute-start | bytes 3145736 | tf_op jit(solution)/shard_map/ppermute | solution.py:283
  57.1 8.8 %collective-permute-start.12 = (bf16[1,4,128,256]{3,2,1,0:T(8,128)(2,1)S(1)}, bf16[1,4,128,256]{3,2,1,0:T(8,128)(2,1)S(1)}, u32[]{:S(2)}, u32[]{:S(2)}) collective-permute-start(bf16[1,4,128,256]{3,2,1,0:T(8,128)(2,1)S(1)} %bitcast.18), channel_id=1, source_target_pairs={{0,2},{1,3},{2,0},{3,1},{4,6},{5,7},{6,4},{7,5},{8,10},{9,11},{10,... | collective-permute-start | bytes 786440 | tf_op jit(solution)/shard_map/ppermute | solution.py:283
  58.7 13.4 %collective-permute-start.13 = (bf16[2,128,256]{2,1,0:T(8,128)(2,1)S(1)}, bf16[2,128,256]{2,1,0:T(8,128)(2,1)S(1)}, u32[]{:S(2)}, u32[]{:S(2)}) collective-permute-start(bf16[2,128,256]{2,1,0:T(8,128)(2,1)S(1)} %get-tuple-element.62), channel_id=1, source_target_pairs={{0,4},{4,8},{8,12},{12,0},{1,5},{5,9},{9,13},{13,1},{2,6},{6,10},{... | collective-permute-start | bytes 393224 | tf_op jit(solution)/shard_map/ppermute | solution.py:298
  58.7 13.4 %collective-permute-start.14 = (bf16[2,128,256]{2,1,0:T(8,128)(2,1)S(1)}, bf16[2,128,256]{2,1,0:T(8,128)(2,1)S(1)}, u32[]{:S(2)}, u32[]{:S(2)}) collective-permute-start(bf16[2,128,256]{2,1,0:T(8,128)(2,1)S(1)} %get-tuple-element.63), channel_id=1, source_target_pairs={{0,8},{4,12},{8,0},{12,4},{1,9},{5,13},{9,1},{13,5},{2,10},{6,14},... | collective-permute-start | bytes 393224 | tf_op jit(solution)/shard_map/ppermute | solution.py:298
  62.0 10.1 %collective-permute-start.15 = (bf16[2,128,256]{2,1,0:T(8,128)(2,1)S(1)}, bf16[2,128,256]{2,1,0:T(8,128)(2,1)S(1)}, u32[]{:S(2)}, u32[]{:S(2)}) collective-permute-start(bf16[2,128,256]{2,1,0:T(8,128)(2,1)S(1)} %get-tuple-element.64), channel_id=1, source_target_pairs={{0,12},{4,0},{8,4},{12,8},{1,13},{5,1},{9,5},{13,9},{2,14},{6,2},{... | collective-permute-start | bytes 393224 | tf_op jit(solution)/shard_map/ppermute | solution.py:298
  69.8 1.3 %copy-start.2 = (f32[4,512,256]{2,1,0:T(8,128)}, f32[4,512,256]{2,1,0:T(8,128)S(1)}, u32[]{:S(2)}) copy-start(f32[4,512,256]{2,1,0:T(8,128)S(1)} %get-tuple-element.76.refs_6_) | copy-start | bytes 6291460
  71.1 1.0 copy-start.4
  72.1 3.3 %copy-start.6 = (bf16[4096,256]{1,0:T(8,128)(2,1)S(1)}, bf16[4096,256]{1,0:T(8,128)(2,1)}, u32[]{:S(2)}) copy-start(bf16[4096,256]{1,0:T(8,128)(2,1)} %param.2) | copy-start | bytes 6291460
  72.1 11.6 %collective-permute-start.18 = (bf16[2,4,128,256]{3,2,1,0:T(8,128)(2,1)}, bf16[2,4,128,256]{3,2,1,0:T(8,128)(2,1)}, u32[]{:S(2)}, u32[]{:S(2)}) collective-permute-start(bf16[2,4,128,256]{3,2,1,0:T(8,128)(2,1)} %pad_maximum_fusion.2.refs_2_), channel_id=1, source_target_pairs={{0,1},{1,0},{2,3},{3,2},{4,5},{5,4},{6,7},{7,6},{8,9},{9,8},{10,11... | collective-permute-start | bytes 1572872 | tf_op jit(solution)/shard_map/ppermute | solution.py:283
  73.8 8.9 %collective-permute-start.17 = (bf16[1,4,128,256]{3,2,1,0:T(8,128)(2,1)S(1)}, bf16[1,4,128,256]{3,2,1,0:T(8,128)(2,1)}, u32[]{:S(2)}, u32[]{:S(2)}) collective-permute-start(bf16[1,4,128,256]{3,2,1,0:T(8,128)(2,1)S(1)} %bitcast.20), channel_id=1, source_target_pairs={{0,2},{1,3},{2,0},{3,1},{4,6},{5,7},{6,4},{7,5},{8,10},{9,11},{10,... | collective-permute-start | bytes 786440 | tf_op jit(solution)/shard_map/ppermute | solution.py:283
  83.7 1.6 %copy-start.1 = (bf16[2,4,512,256]{3,2,1,0:T(8,128)(2,1)S(1)}, bf16[2,4,512,256]{3,2,1,0:T(8,128)(2,1)}, u32[]{:S(2)}) copy-start(bf16[2,4,512,256]{3,2,1,0:T(8,128)(2,1)} %copy-done) | copy-start | bytes 6291460
  85.3 1.6 %copy-start.3 = (f32[4,512,256]{2,1,0:T(8,128)S(1)}, f32[4,512,256]{2,1,0:T(8,128)}, u32[]{:S(2)}) copy-start(f32[4,512,256]{2,1,0:T(8,128)} %copy-done.2) | copy-start | bytes 6291460
  86.9 1.2 %copy-start.5 = (f32[4,512,128]{2,1,0:T(8,128)S(1)}, f32[4,512,128]{2,1,0:T(8,128)}, u32[]{:S(2)}) copy-start(f32[4,512,128]{2,1,0:T(8,128)} %copy-done.4) | copy-start | bytes 3145732
  92.0 2.0 %collective-permute-start.19 = (bf16[2,4,128,256]{3,2,1,0:T(8,128)(2,1)S(1)}, bf16[2,4,128,256]{3,2,1,0:T(8,128)(2,1)S(1)}, u32[]{:S(2)}, u32[]{:S(2)}) collective-permute-start(bf16[2,4,128,256]{3,2,1,0:T(8,128)(2,1)S(1)} %pad_maximum_fusion.3.refs_2_), channel_id=1, source_target_pairs={{0,1},{1,0},{2,3},{3,2},{4,5},{5,4},{6,7},{7,6},{8,9},{9,8},{10,11... | collective-permute-start | bytes 1572872 | tf_op jit(solution)/shard_map/ppermute | solution.py:283
  96.8 8.7 %collective-permute-start.20 = (f32[4,512]{1,0:T(4,128)S(1)}, f32[4,512]{1,0:T(4,128)S(1)}, u32[]{:S(2)}, u32[]{:S(2)}) collective-permute-start(f32[4,512]{1,0:T(4,128)S(1)} %get-tuple-element.87), channel_id=1, source_target_pairs={{0,4},{4,8},{8,12},{12,0},{1,5},{5,9},{9,13},{13,1},{2,6},{6,10},{... | collective-permute-start | bytes 24584 | tf_op jit(solution)/shard_map/ppermute | solution.py:306
  98.7 6.8 %collective-permute-start.21 = (f32[4,512]{1,0:T(4,128)S(1)}, f32[4,512]{1,0:T(4,128)S(1)}, u32[]{:S(2)}, u32[]{:S(2)}) collective-permute-start(f32[4,512]{1,0:T(4,128)S(1)} %get-tuple-element.87), channel_id=1, source_target_pairs={{0,8},{4,12},{8,0},{12,4},{1,9},{5,13},{9,1},{13,5},{2,10},{6,14},... | collective-permute-start | bytes 24584 | tf_op jit(solution)/shard_map/ppermute | solution.py:306
  100.2 5.3 %collective-permute-start.22 = (f32[4,512]{1,0:T(4,128)S(1)}, f32[4,512]{1,0:T(4,128)S(1)}, u32[]{:S(2)}, u32[]{:S(2)}) collective-permute-start(f32[4,512]{1,0:T(4,128)S(1)} %get-tuple-element.87), channel_id=1, source_target_pairs={{0,12},{4,0},{8,4},{12,8},{1,13},{5,1},{9,5},{13,9},{2,14},{6,2},{... | collective-permute-start | bytes 24584 | tf_op jit(solution)/shard_map/ppermute | solution.py:306

commit v5 on v4

--- a/solution.py
+++ b/solution.py
@@ -11,7 +11,8 @@
 BR = 512
 BLK_DEV = 8
 LANES = 128
-CHUNKS = ((0, 256), (256, 128), (384, 128))
+CHUNKS = ((0, 320), (320, 192))
+WINDOWS = ((0, 256), (256, 512))
 
 
 def smem():
@@ -149,9 +150,21 @@
     return sum(square[:, at : at + LANES] for at in range(0, square.shape[1], LANES))
 
 
-def chunk_kernel(first, last, *refs):
-    all_rows, all_cols, rest = refs[:2], refs[2:4], refs[4:]
-    half_count, pair_count = refs[0].shape[:2]
+def segments(window):
+    low, high = window
+    held = []
+    for chunk, (start, size) in enumerate(CHUNKS):
+        first, end = max(low, start), min(high, start + size)
+        if first < end:
+            held.append((chunk, first - start, end - first))
+    return held
+
+
+def window_kernel(narrow_count, window, first, last, *refs):
+    held = segments(window)
+    all_rows, rest = refs[:narrow_count], refs[narrow_count:]
+    all_cols = [rest[i * narrow_count : (i + 1) * narrow_count] for i in range(len(held))]
+    rest = rest[len(held) * narrow_count :]
     if not first:
         square_in, mass_in, total_in, sums_in = rest[:4]
         rest = rest[4:]
@@ -161,28 +174,30 @@
         square_ref, mass_ref, total_ref, sums_ref = rest
     else:
         mass_ref, total_ref, sums_ref = rest
-    for pair in range(pair_count):
-        rows = [ref.at[i, pair] for ref in all_rows for i in range(half_count)]
-        cols = [ref.at[i, pair] for ref in all_cols for i in range(half_count)]
+    for pair in range(all_rows[0].shape[0]):
+        rows = [ref[pair] for ref in all_rows]
+        cols = []
+        for narrow in range(narrow_count):
+            pieces = [
+                refs[narrow][pair, at : at + size] for refs, (_, at, size) in zip(all_cols, held)
+            ]
+            cols.append(jnp.concatenate(pieces, axis=0) if len(pieces) > 1 else pieces[0])
         if first:
-            square = jnp.sum(tree([lane_sum(row[...]) for row in rows]), axis=1, keepdims=True)
+            square = jnp.sum(tree([lane_sum(row) for row in rows]), axis=1, keepdims=True)
             square = jnp.broadcast_to(square, (BR, LANES))
         else:
             square = square_in[pair]
-        gram = tree([across(row[...], col[...]) for row, col in zip(rows, cols)])
-        other = jnp.sum(tree([lane_sum(col[...]) for col in cols]).T, axis=0, keepdims=True)
-        size = gram.shape[1]
+        gram = tree([across(row, col) for row, col in zip(rows, cols)])
+        other = jnp.sum(tree([lane_sum(col) for col in cols]).T, axis=0, keepdims=True)
         pieces, mass = [], None
-        for at in range(0, size, LANES):
+        for at in range(0, gram.shape[1], LANES):
             here = slice(at, at + LANES)
             piece = jnp.exp((square + other[:, here] - 2.0 * gram[:, here]) * (-1.0 / F))
             mass = piece if mass is None else mass + piece
             pieces.append(piece)
         kernel = jnp.concatenate(pieces, axis=1) if len(pieces) > 1 else pieces[0]
         sums = jnp.sum(kernel, axis=0, keepdims=True)
-        total = jnp.dot(
-            kernel.astype(jnp.bfloat16), cols[0][...], preferred_element_type=jnp.float32
-        )
+        total = jnp.dot(kernel.astype(jnp.bfloat16), cols[0], preferred_element_type=jnp.float32)
         if not first:
             mass = mass_in[pair] + mass
             total = total_in[pair] + total
@@ -199,11 +214,13 @@
             total_ref[pair] = total
 
 
-def chunk_step(rows, cols, carry, done, last):
-    _, pair_count, size, feat = cols[0].shape
-    first = carry is None
+def window_step(rows, cols, index, carry):
+    pair_count, _, feat = rows[0].shape
+    window = WINDOWS[index]
+    size = window[1] - window[0]
+    first, last = index == 0, index == len(WINDOWS) - 1
     lanes = pltpu.VMEM((pair_count, BR, LANES), jnp.float32)
-    sums = pltpu.VMEM((pair_count, done + size), jnp.float32)
+    sums = pltpu.VMEM((pair_count, window[1]), jnp.float32)
     if last:
         shapes = [
             pltpu.VMEM((pair_count, BR, feat), jnp.bfloat16),
@@ -213,9 +230,12 @@
         ]
     else:
         shapes = [lanes] * (1 + first) + [pltpu.VMEM((pair_count, BR, feat), jnp.float32), sums]
-    args = [*rows, *cols, *([] if first else carry)]
+    args = list(rows)
+    for chunk, _, _ in segments(window):
+        args += cols[chunk]
+    args += [] if first else carry
     outs = pl.pallas_call(
-        functools.partial(chunk_kernel, first, last),
+        functools.partial(window_kernel, len(rows), window, first, last),
         out_shape=shapes,
         in_specs=[vmem()] * len(args),
         out_specs=[vmem()] * len(shapes),
@@ -225,69 +245,89 @@
             transcendentals=pair_count * BR * size,
             bytes_accessed=8 * 1024 * 1024,
         ),
-        name="chunk",
+        name="window",
     )(*[in_vmem(x) for x in args])
     return outs if first or last else [carry[0], *outs]
 
 
-def mean_kernel(pair_count, local_ref, part_ref, mass_ref, block_ref, _, out_ref, total, weight):
-    here = local_ref[pl.program_id(0)]
-    total[...] = block_ref[0].astype(jnp.float32)
-    weight[...] = jnp.ones_like(weight)
-    for pair in range(pair_count):
-
-        @pl.when(local_ref[pair] == here)
+def keep_kernel(block_ref, out_ref):
+    out_ref[...] = block_ref[...]
+
+
+def keep(blocks):
+    block = pl.BlockSpec((1, *blocks.shape[1:]), lambda k: (k, 0, 0))
+    return pl.pallas_call(
+        keep_kernel,
+        out_shape=pltpu.HBM(blocks.shape, blocks.dtype),
+        grid=(blocks.shape[0],),
+        in_specs=[block],
+        out_specs=block,
+        compiler_params=params(4),
+        name="keep",
+    )(in_hbm(blocks))
+
+
+def mean_kernel(local_ref, rows_ref, part_ref, mass_ref, _, out_ref, made, sems):
+    pair_count, _, feat = rows_ref.shape
+    local = [local_ref[pair, 0] & 7 for pair in range(pair_count)]
+
+    def copy(pair):
+        return pltpu.make_async_copy(made.at[pair], out_ref.at[local[pair]], sems.at[pair])
+
+    firsts = []
+    for pair in range(pair_count):
+        same = [local[other] == local[pair] for other in range(pair)]
+        firsts.append(jnp.logical_not(functools.reduce(jnp.logical_or, same, jnp.bool_(False))))
+    for pair in range(pair_count):
+
+        @pl.when(firsts[pair])
         def _():
-            total[...] += part_ref[pair].astype(jnp.float32)
-            weight[...] += mass_ref[pair]
-
-    scale = 1.0 / weight[...]
-    for at in range(0, total.shape[1], LANES):
-        lanes = slice(at, at + LANES)
-        out_ref[0, :, lanes] = (total[:, lanes] * scale).astype(jnp.bfloat16)
-
-
-def means(row_local, part, mass, blocks):
-    pair_count = mass.shape[0]
-    feat = blocks.shape[-1]
-    block = pl.BlockSpec((1, BR, feat), lambda p, local: (local[p], 0, 0))
+            mass = 1.0 + mass_ref[pair]
+            total = rows_ref[pair].astype(jnp.float32) + part_ref[pair].astype(jnp.float32)
+            for other in range(pair + 1, pair_count):
+                both = (local[other] == local[pair]).astype(jnp.float32)
+                mass = mass + both * mass_ref[other]
+                total = total + both * part_ref[other].astype(jnp.float32)
+            scale = 1.0 / mass
+            for at in range(0, feat, LANES):
+                lanes = slice(at, at + LANES)
+                made[pair, :, lanes] = (total[:, lanes] * scale).astype(jnp.bfloat16)
+            copy(pair).start()
+
+    for pair in range(pair_count):
+
+        @pl.when(firsts[pair])
+        def _():
+            copy(pair).wait()
+
+
+def means(pairs, rows, part, mass, blocks):
+    pair_count, _, feat = part.shape
     return pl.pallas_call(
-        functools.partial(mean_kernel, pair_count),
-        out_shape=jax.ShapeDtypeStruct(blocks.shape, jnp.bfloat16),
-        grid_spec=pltpu.PrefetchScalarGridSpec(
-            num_scalar_prefetch=1,
-            grid=(pair_count,),
-            in_specs=[
-                pl.BlockSpec(part.shape, lambda p, local: (0, 0, 0)),
-                pl.BlockSpec(mass.shape, lambda p, local: (0, 0, 0)),
-                block,
-                anywhere(),
-            ],
-            out_specs=block,
-            scratch_shapes=[
-                pltpu.VMEM((BR, feat), jnp.float32),
-                pltpu.VMEM((BR, LANES), jnp.float32),
-            ],
-        ),
+        mean_kernel,
+        out_shape=pltpu.HBM(blocks.shape, jnp.bfloat16),
+        in_specs=[smem(), vmem(), vmem(), vmem(), anywhere()],
+        out_specs=anywhere(),
+        scratch_shapes=[
+            pltpu.VMEM((pair_count, BR, feat), jnp.bfloat16),
+            pltpu.SemaphoreType.DMA((pair_count,)),
+        ],
         input_output_aliases={4: 0},
         compiler_params=params(16),
-        cost_estimate=pl.CostEstimate(
-            flops=pair_count * BR * feat * 4, transcendentals=0, bytes_accessed=4 * 1024 * 1024
-        ),
         name="means",
-    )(row_local, part, mass, in_hbm(blocks), in_hbm(blocks))
+    )(pairs, *[in_vmem(x) for x in (rows, part, mass)], in_hbm(keep(blocks)))
 
 
 def hop(parts, step):
     count = lax.axis_size("narrow")
-    return parts, lax.ppermute(parts, "narrow", [(i, i ^ step) for i in range(count)])
+    return [lax.ppermute(part, "narrow", [(i, i ^ step) for i in range(count)]) for part in parts]
 
 
 def first_hops(part):
-    parts = part[None]
+    parts = [part]
     step = lax.axis_size("narrow") // 2
     while step > 1:
-        parts = jnp.concatenate(hop(parts, step), axis=0)
+        parts = parts + hop(parts, step)
         step //= 2
     return parts
 
@@ -315,43 +355,34 @@
     capacity = max(2, 2 * pair_count // wide_count)
     feat = embeddings.shape[1]
     blocks = embeddings.reshape(BLK_DEV, BR, feat)
-    row_local = pair_list[:, 0] % BLK_DEV
     lists = from_others(pair_list)
     outgoing, row_slices = pack(me, lists, blocks, capacity)
-    chunks = len(CHUNKS)
     fixed = lax.optimization_barrier
-    rows_half, received = fixed((first_hops(row_slices), to_wide(outgoing[0])))
-    rows = carry = half = None
-    done = 0
-    for phase in range(1, chunks + 2):
-        last_half = half
-        if phase <= chunks:
-            start, size = CHUNKS[phase - 1]
-            picked = select(me, pair_list, blocks, received, start, size)
-            half = first_hops(picked)
-        else:
-            half = None
-        if phase < chunks:
-            received = to_wide(outgoing[phase])
-        if phase == 1:
-            rows = hop(rows_half, 1)
-            half, received, rows = fixed((half, received, rows))
-            continue
-        whole = hop(last_half, 1)
-        carry = chunk_step(rows, whole, carry, done, phase == chunks + 1)
-        done += CHUNKS[phase - 2][1]
-        if phase < chunks:
-            half, received, carry = fixed((half, received, carry))
-        elif phase == chunks:
-            half, carry = fixed((half, carry))
+
+    def pick(received, chunk):
+        return select(me, pair_list, blocks, received, *CHUNKS[chunk])
+
+    rows = first_hops(row_slices)
+    rows_last = hop(rows[:1], 1)
+    rows, rows_last, received = fixed((rows, rows_last, to_wide(outgoing[0])))
+    cols_a = first_hops(pick(received, 0))
+    rows = rows + rows_last + hop(rows[1:], 1)
+    cols_a, rows, received = fixed((cols_a, rows, to_wide(outgoing[1])))
+    cols_b = first_hops(pick(received, 1))
+    last_b = hop(cols_b[:1], 1)
+    cols_a = cols_a + hop(cols_a, 1)
+    carry = window_step(rows, [cols_a], 0, None)
+    cols_b, last_b, carry = fixed((cols_b, last_b, carry))
+    cols_b = cols_b + last_b + hop(cols_b[1:], 1)
+    carry = window_step(rows, [cols_a, cols_b], 1, carry)
     part, mass, row_sums, col_sums = carry
     every_sum = jnp.concatenate(from_others(col_sums), axis=0)
-    mean = means(row_local, part, mass, blocks)
+    mean = means(pair_list, row_slices, part, mass, blocks)
     block_ids = jnp.arange(BLK_DEV, dtype=jnp.int32)[:, None]
     every_col = jnp.concatenate([x[:, 1] for x in lists])
     mine = every_col[None, :] == me[0] * BLK_DEV + block_ids
     col_mass = jnp.sum(jnp.where(mine[:, :, None], every_sum[None], 0.0), axis=1)
-    here = row_local[None, :] == block_ids
+    here = pair_list[:, 0][None, :] % BLK_DEV == block_ids
     row_mass = jnp.sum(jnp.where(here[:, :, None], row_sums[None], 0.0), axis=1)
     weights = 1.0 / (1.0 + (row_mass + col_mass) / BR)
     return weights.reshape(BLK_DEV * BR), mean.reshape(BLK_DEV * BR, feat)

time: 107 us -> 103 us (0.963)
  waiting for transfers between devices: 42.2 us -> 37.4 us
  starting transfers between devices: 29 us -> 31.3 us
  other arithmetic: 2.61 us -> 0.46 us
  Pallas kernels: 21.7 us -> 23.3 us
  local copies, waits for them, and re-layouts: 9.94 us -> 8.72 us
    ppermute x8 -> x9, waiting for transfers between devices: 37.9 us -> 1.03 us  [hop(): lax.ppermute(part, 'narrow', [(i, i ^ step) for i in range(count)])]
    ppermute x9 -> x6, waiting for transfers between devices: 2.06 us -> 32.6 us  [to_wide(): lax.ppermute(piece, 'wide', [(i, (i + shift) % count) for i in range(coun...]
    pallas_call x4, Pallas kernels: 14.1 us -> 16.5 us  [the longest x2 8.66 us: window_step(): pl.pallas_call(functools.partial(window_kernel, len(rows), window, first,...]
    ppermute x6, starting transfers between devices: 11.3 us -> 13.6 us  [from_others(): lax.ppermute(part, 'wide', [(i, (i + shift) % count) for i in range(count)])]
    concatenate x4 -> x0, other arithmetic: 2.15 us -> none  [first_hops(): parts = jnp.concatenate(hop(parts, step), axis=0)]
    ppermute x9 -> x6, starting transfers between devices: 11.2 us -> 12.9 us  [to_wide(): lax.ppermute(piece, 'wide', [(i, (i + shift) % count) for i in range(coun...]
    ppermute x8 -> x9, starting transfers between devices: 6.44 us -> 4.79 us  [hop(): lax.ppermute(part, 'narrow', [(i, i ^ step) for i in range(count)])]
    ppermute x6, waiting for transfers between devices: 2.24 us -> 3.75 us  [from_others(): lax.ppermute(part, 'wide', [(i, (i + shift) % count) for i in range(count)])]
  transfers between devices with their start and end apart: 23 -> 21, of which waited for: 8 -> 8; matrix products, arithmetic and copies ran while one was open for 4% -> 1% of each run, Pallas kernels for 12% -> 16%
where the time goes in v5:
time: 103 us; the launch traced here: 102 us
  waiting for transfers between devices  37.4 us (36%)
  starting transfers between devices  31.3 us (30%)
  Pallas kernels  23.3 us (23%)
  local copies, waits for them, and re-layouts  8.72 us (8%)
    ppermute x6, waiting for transfers between devices, to_wide(): lax.ppermute(piece, 'wide', [(i, (i + shift) % count) for i in range(coun...  32.6 us
    ppermute x6, starting transfers between devices, from_others(): lax.ppermute(part, 'wide', [(i, (i + shift) % count) for i in range(count)])  13.6 us
    ppermute x6, starting transfers between devices, to_wide(): lax.ppermute(piece, 'wide', [(i, (i + shift) % count) for i in range(coun...  12.9 us
    pallas_call x2, Pallas kernels, window_step(): pl.pallas_call(functools.partial(window_kernel, len(rows), window, first,...  8.66 us
    unnamed x24, local copies, waits for them, and re-layouts  8.17 us
    pallas_call x1, Pallas kernels, keep(): pl.pallas_call(keep_kernel, out_shape=pltpu.HBM(blocks.shape, blocks.dtyp...  5.78 us
    ppermute x9, starting transfers between devices, hop(): lax.ppermute(part, 'narrow', [(i, i ^ step) for i in range(count)])  4.79 us
    pallas_call x2, Pallas kernels, select(): pl.pallas_call(functools.partial(select_kernel, len(received) + 1, pair_c...  3.84 us
  transfers between devices with their start and end apart: 21, of which 8 were waited for; matrix products, arithmetic and copies ran while one was open for 1% of the time, Pallas kernels for 16%

profile of v5, /device:TPU:0, one launch (start us, length us, event | category | flops | bytes accessed | tf_op | source)
XLA Modules:
  0.0 102.0 jit_solution(11806848030305251598)
XLA Ops:
  0.6 0.8 copy.23.refs_0_.list_ref.local_ref
  1.4 3.0 %collective-permute-start = (s32[4,2]{1,0:T(4,128)S(1)}, s32[4,2]{1,0:T(4,128)S(1)}, u32[]{:S(2)}, u32[]{:S(2)}) collective-permute-start(s32[4,2]{1,0:T(4,128)S(1)} %copy.23.refs_0_.list_ref.local_ref), channel_id=1, source_target_pairs={{0,4},{4,8},{8,12},{12,0},{1,5},{5,9},{9,13},{13,1},{2,6},{6,10},{... | collective-permute-start | bytes 104 | tf_op jit(solution)/shard_map/ppermute | solution.py:346
  4.4 2.6 %collective-permute-start.1 = (s32[4,2]{1,0:T(4,128)S(1)}, s32[4,2]{1,0:T(4,128)S(1)}, u32[]{:S(2)}, u32[]{:S(2)}) collective-permute-start(s32[4,2]{1,0:T(4,128)S(1)} %copy.23.refs_0_.list_ref.local_ref), channel_id=1, source_target_pairs={{0,8},{4,12},{8,0},{12,4},{1,9},{5,13},{9,1},{13,5},{2,10},{6,14},... | collective-permute-start | bytes 104 | tf_op jit(solution)/shard_map/ppermute | solution.py:346
  7.0 1.3 %collective-permute-start.2 = (s32[4,2]{1,0:T(4,128)S(1)}, s32[4,2]{1,0:T(4,128)S(1)}, u32[]{:S(2)}, u32[]{:S(2)}) collective-permute-start(s32[4,2]{1,0:T(4,128)S(1)} %copy.23.refs_0_.list_ref.local_ref), channel_id=1, source_target_pairs={{0,12},{4,0},{8,4},{12,8},{1,13},{5,1},{9,5},{13,9},{2,14},{6,2},{... | collective-permute-start | bytes 104 | tf_op jit(solution)/shard_map/ppermute | solution.py:346
  8.9 1.7 %collective-permute-done.2.refs_3_ = s32[4,2]{1,0:T(4,128)S(1)} collective-permute-done((s32[4,2]{1,0:T(4,128)S(1)}, s32[4,2]{1,0:T(4,128)S(1)}, u32[]{:S(2)}, u32[]{:S(2)}) %collective-permute-start.2) | collective-permute-done | bytes 64 | tf_op jit(solution)/shard_map/ppermute | solution.py:346
  10.6 3.0 %pack.1 = (bf16[2,320,256]{2,1,0:T(8,128)(2,1)S(1)}, bf16[2,320,256]{2,1,0:T(8,128)(2,1)S(1)}, bf16[2,320,256]{2,1,0:T(8,128)(2,1)S(1)}, bf16[2,192,256]{2,1,0:T...) custom-call(s32[1]{0:T(128)} %bitcast.1.me_ref, ...), custom_call_target="tpu_custom_call" | custom-call | tf_op jit(solution)/shard_map/pack/pallas_call | solution.py:81
  13.6 1.6 %collective-permute-start.3 = (bf16[4,512,256]{2,1,0:T(8,128)(2,1)S(1)}, bf16[4,512,256]{2,1,0:T(8,128)(2,1)S(1)}, u32[]{:S(2)}, u32[]{:S(2)}) collective-permute-start(bf16[4,512,256]{2,1,0:T(8,128)(2,1)S(1)} %get-tuple-element.52.refs_0_.rows_ref), channel_id=1, source_target_pairs={{0,2},{1,3},{2,0},{3,1},{4,6},{5,7},{6,4},{7,5},{8,10},{9,11},{10,... | collective-permute-start | bytes 3145736 | tf_op jit(solution)/shard_map/ppermute | solution.py:323
  15.4 3.1 %collective-permute-start.6 = (bf16[2,320,256]{2,1,0:T(8,128)(2,1)S(1)}, bf16[2,320,256]{2,1,0:T(8,128)(2,1)S(1)}, u32[]{:S(2)}, u32[]{:S(2)}) collective-permute-start(bf16[2,320,256]{2,1,0:T(8,128)(2,1)S(1)} %get-tuple-element.41), channel_id=1, source_target_pairs={{0,8},{4,12},{8,0},{12,4},{1,9},{5,13},{9,1},{13,5},{2,10},{6,14},... | collective-permute-start | bytes 983048 | tf_op jit(solution)/shard_map/ppermute | solution.py:338
  19.0 8.6 %collective-permute-done.5.refs_0_ = bf16[2,320,256]{2,1,0:T(8,128)(2,1)S(1)} collective-permute-done((bf16[2,320,256]{2,1,0:T(8,128)(2,1)S(1)}, bf16[2,320,256]{2,1,0:T(8,128)(2,1)S(1)}, u32[]{:S(2)}, u32[]{:S(2)}) %collective-permute-start.5) | collective-permute-done | bytes 327712 | tf_op jit(solution)/shard_map/ppermute | solution.py:338
  27.6 13.4 %collective-permute-done.6.refs_1_ = bf16[2,320,256]{2,1,0:T(8,128)(2,1)S(1)} collective-permute-done((bf16[2,320,256]{2,1,0:T(8,128)(2,1)S(1)}, bf16[2,320,256]{2,1,0:T(8,128)(2,1)S(1)}, u32[]{:S(2)}, u32[]{:S(2)}) %collective-permute-start.6) | collective-permute-done | bytes 327712 | tf_op jit(solution)/shard_map/ppermute | solution.py:338
  41.1 1.0 copy-done
  42.1 2.0 %select.10.refs_4_ = bf16[4,320,256]{2,1,0:T(8,128)(2,1)S(1)} custom-call(s32[1]{0:T(128)} %bitcast.1.me_ref, s32[4,2]{1,0:T(4,128)S(1)} %copy.23.refs_0_.list_ref.local_ref, bf16[8,512,256]{2,1,0:T(8,128)(2,1)} %bitcast.11, bf16[2,320,256]{2,1,0:T(8,128)(2,1)S(1)} %collective-permute-done.5.refs_0_, ...), custom_call_target="tpu_custom_call" | custom-call | tf_op jit(solution)/shard_map/select/pallas_call | solution.py:124
  44.7 6.7 %collective-permute-start.10 = (bf16[2,192,256]{2,1,0:T(8,128)(2,1)S(1)}, bf16[2,192,256]{2,1,0:T(8,128)(2,1)S(1)}, u32[]{:S(2)}, u32[]{:S(2)}) collective-permute-start(bf16[2,192,256]{2,1,0:T(8,128)(2,1)S(1)} %get-tuple-element.49), channel_id=1, source_target_pairs={{0,4},{4,8},{8,12},{12,0},{1,5},{5,9},{9,13},{13,1},{2,6},{6,10},{... | collective-permute-start | bytes 589832 | tf_op jit(solution)/shard_map/ppermute | solution.py:338
  51.7 2.0 %collective-permute-start.12 = (bf16[2,192,256]{2,1,0:T(8,128)(2,1)S(1)}, bf16[2,192,256]{2,1,0:T(8,128)(2,1)S(1)}, u32[]{:S(2)}, u32[]{:S(2)}) collective-permute-start(bf16[2,192,256]{2,1,0:T(8,128)(2,1)S(1)} %get-tuple-element.51), channel_id=1, source_target_pairs={{0,12},{4,0},{8,4},{12,8},{1,13},{5,1},{9,5},{13,9},{2,14},{6,2},{... | collective-permute-start | bytes 589832 | tf_op jit(solution)/shard_map/ppermute | solution.py:338
  53.8 3.2 %collective-permute-done.10.refs_0_ = bf16[2,192,256]{2,1,0:T(8,128)(2,1)S(1)} collective-permute-done((bf16[2,192,256]{2,1,0:T(8,128)(2,1)S(1)}, bf16[2,192,256]{2,1,0:T(8,128)(2,1)S(1)}, u32[]{:S(2)}, u32[]{:S(2)}) %collective-permute-start.10) | collective-permute-done | bytes 196640 | tf_op jit(solution)/shard_map/ppermute | solution.py:338
  57.0 0.7 copy-done.4
  57.7 7.4 %collective-permute-done.11.refs_1_ = bf16[2,192,256]{2,1,0:T(8,128)(2,1)S(1)} collective-permute-done((bf16[2,192,256]{2,1,0:T(8,128)(2,1)S(1)}, bf16[2,192,256]{2,1,0:T(8,128)(2,1)S(1)}, u32[]{:S(2)}, u32[]{:S(2)}) %collective-permute-start.11) | collective-permute-done | bytes 196640 | tf_op jit(solution)/shard_map/ppermute | solution.py:338
  65.7 0.7 copy-done.8
  66.4 1.0 copy-done.2
  68.0 0.9 copy-done.5
  68.9 0.9 copy-done.7
  69.8 0.9 copy-done.9
  70.8 1.8 %select.11.refs_8_ = bf16[4,192,256]{2,1,0:T(8,128)(2,1)S(1)} custom-call(s32[1]{0:T(128)} %bitcast.1.me_ref, s32[4,2]{1,0:T(4,128)S(1)} %copy.23.refs_0_.list_ref.local_ref, bf16[8,512,256]{2,1,0:T(8,128)(2,1)} %bitcast.12, bf16[2,192,256]{2,1,0:T(8,128)(2,1)S(1)} %copy-done.5, bf16[2,192,256]{2,1,0:T(8,128)(2,1)S(1)} %copy-done.7, ...), custom_call_target="tpu_custom_call" | custom-call | tf_op jit(solution)/shard_map/select/pallas_call | solution.py:124
  72.6 1.6 %collective-permute-start.15 = (bf16[4,192,256]{2,1,0:T(8,128)(2,1)S(1)}, bf16[4,192,256]{2,1,0:T(8,128)(2,1)S(1)}, u32[]{:S(2)}, u32[]{:S(2)}) collective-permute-start(bf16[4,192,256]{2,1,0:T(8,128)(2,1)S(1)} %select.11.refs_8_), channel_id=1, source_target_pairs={{0,2},{1,3},{2,0},{3,1},{4,6},{5,7},{6,4},{7,5},{8,10},{9,11},{10,... | collective-permute-start | bytes 1179656 | tf_op jit(solution)/shard_map/ppermute | solution.py:323
  74.2 5.8 %keep.1._ = bf16[8,512,256]{2,1,0:T(8,128)(2,1)} custom-call(bf16[8,512,256]{2,1,0:T(8,128)(2,1)} %bitcast.13), custom_call_target="tpu_custom_call" | custom-call | tf_op jit(solution)/shard_map/keep/pallas_call | solution.py:259
  80.3 4.4 %window.2 = (f32[4,512,128]{2,1,0:T(8,128)S(1)}, f32[4,512,128]{2,1,0:T(8,128)S(1)}, f32[4,512,256]{2,1,0:T(8,128)S(1)}, f32[4,256]{1,0:T(4,128)S(1)}) custom-call(bf16[4,512,256]{2,1,0:T(8,128)(2,1)S(1)} %get-tuple-element.52.refs_0_.rows_ref, bf16[4,512,256]{2,1,0:T(8,128)(2,1)S(1)} %collective-permute-done.3.refs_1_, bf16[4,512,256]{2,1,0:T(8,128)(2,1)S(1)} %copy-done.1, ...), custom_call_target="tpu_custom_call" | custom-call | flops 1342177280 | bytes 8388608 | tf_op jit(solution)/shard_map/window/pallas_call | solution.py:237
  85.6 1.0 collective-permute-done.17.refs_11_
  86.6 4.3 %window.3 = (bf16[4,512,256]{2,1,0:T(8,128)(2,1)S(1)}, f32[4,512,128]{2,1,0:T(8,128)S(1)}, f32[4,512]{1,0:T(4,128)S(1)}, f32[4,512]{1,0:T(4,128)S(1)}) custom-call(bf16[4,512,256]{2,1,0:T(8,128)(2,1)S(1)} %get-tuple-element.52.refs_0_.rows_ref, bf16[4,512,256]{2,1,0:T(8,128)(2,1)S(1)} %collective-permute-done.3.refs_1_, bf16[4,512,256]{2,1,0:T(8,128)(2,1)S(1)} %copy-done.1, ...), custom_call_target="tpu_custom_call" | custom-call | flops 1342177280 | bytes 8388608 | tf_op jit(solution)/shard_map/window/pallas_call | solution.py:237
  90.9 3.4 %collective-permute-start.18 = (f32[4,512]{1,0:T(4,128)S(1)}, f32[4,512]{1,0:T(4,128)S(1)}, u32[]{:S(2)}, u32[]{:S(2)}) collective-permute-start(f32[4,512]{1,0:T(4,128)S(1)} %get-tuple-element.73), channel_id=1, source_target_pairs={{0,4},{4,8},{8,12},{12,0},{1,5},{5,9},{9,13},{13,1},{2,6},{6,10},{... | collective-permute-start | bytes 24584 | tf_op jit(solution)/shard_map/ppermute | solution.py:346
  94.4 3.2 %collective-permute-start.19 = (f32[4,512]{1,0:T(4,128)S(1)}, f32[4,512]{1,0:T(4,128)S(1)}, u32[]{:S(2)}, u32[]{:S(2)}) collective-permute-start(f32[4,512]{1,0:T(4,128)S(1)} %get-tuple-element.73), channel_id=1, source_target_pairs={{0,8},{4,12},{8,0},{12,4},{1,9},{5,13},{9,1},{13,5},{2,10},{6,14},... | collective-permute-start | bytes 24584 | tf_op jit(solution)/shard_map/ppermute | solution.py:346
  97.7 2.0 %means.1 = bf16[8,512,256]{2,1,0:T(8,128)(2,1)} custom-call(s32[4,2]{1,0:T(4,128)S(1)} %copy.23.refs_0_.list_ref.local_ref, bf16[4,512,256]{2,1,0:T(8,128)(2,1)S(1)} %get-tuple-element.52.refs_0_.rows_ref, bf16[4,512,256]{2,1,0:T(8,128)(2,1)S(1)} %get-tuple-element.74.part_ref, ...), custom_call_target="tpu_custom_call", output_to_operand_aliasing={{}: (4, {})} | custom-call | tf_op jit(solution)/shard_map/means/pallas_call | solution.py:306
  99.7 1.5 %collective-permute-done.20 = f32[4,512]{1,0:T(4,128)S(1)} collective-permute-done((f32[4,512]{1,0:T(4,128)S(1)}, f32[4,512]{1,0:T(4,128)S(1)}, u32[]{:S(2)}, u32[]{:S(2)}) %collective-permute-start.20) | collective-permute-done | bytes 8224 | tf_op jit(solution)/shard_map/ppermute | solution.py:346
  (54 shorter events, 5.6 us)
Async XLA Ops:
  1.4 7.0 %collective-permute-start = (s32[4,2]{1,0:T(4,128)S(1)}, s32[4,2]{1,0:T(4,128)S(1)}, u32[]{:S(2)}, u32[]{:S(2)}) collective-permute-start(s32[4,2]{1,0:T(4,128)S(1)} %copy.23.refs_0_.list_ref.local_ref), channel_id=1, source_target_pairs={{0,4},{4,8},{8,12},{12,0},{1,5},{5,9},{9,13},{13,1},{2,6},{6,10},{... | collective-permute-start | bytes 104 | tf_op jit(solution)/shard_map/ppermute | solution.py:346
  4.4 4.5 %collective-permute-start.1 = (s32[4,2]{1,0:T(4,128)S(1)}, s32[4,2]{1,0:T(4,128)S(1)}, u32[]{:S(2)}, u32[]{:S(2)}) collective-permute-start(s32[4,2]{1,0:T(4,128)S(1)} %copy.23.refs_0_.list_ref.local_ref), channel_id=1, source_target_pairs={{0,8},{4,12},{8,0},{12,4},{1,9},{5,13},{9,1},{13,5},{2,10},{6,14},... | collective-permute-start | bytes 104 | tf_op jit(solution)/shard_map/ppermute | solution.py:346
  7.0 3.6 %collective-permute-start.2 = (s32[4,2]{1,0:T(4,128)S(1)}, s32[4,2]{1,0:T(4,128)S(1)}, u32[]{:S(2)}, u32[]{:S(2)}) collective-permute-start(s32[4,2]{1,0:T(4,128)S(1)} %copy.23.refs_0_.list_ref.local_ref), channel_id=1, source_target_pairs={{0,12},{4,0},{8,4},{12,8},{1,13},{5,1},{9,5},{13,9},{2,14},{6,2},{... | collective-permute-start | bytes 104 | tf_op jit(solution)/shard_map/ppermute | solution.py:346
  13.6 40.2 %copy-start.10 = (s32[4,2]{0,1:T(2,128)S(1)}, s32[4,2]{0,1:T(2,128)}, u32[]{:S(2)}) copy-start(s32[4,2]{0,1:T(2,128)} %param.3) | copy-start | bytes 100
  13.6 27.5 %collective-permute-start.3 = (bf16[4,512,256]{2,1,0:T(8,128)(2,1)S(1)}, bf16[4,512,256]{2,1,0:T(8,128)(2,1)S(1)}, u32[]{:S(2)}, u32[]{:S(2)}) collective-permute-start(bf16[4,512,256]{2,1,0:T(8,128)(2,1)S(1)} %get-tuple-element.52.refs_0_.rows_ref), channel_id=1, source_target_pairs={{0,2},{1,3},{2,0},{3,1},{4,6},{5,7},{6,4},{7,5},{8,10},{9,11},{10,... | collective-permute-start | bytes 3145736 | tf_op jit(solution)/shard_map/ppermute | solution.py:323
  15.2 25.9 %collective-permute-start.4 = (bf16[4,512,256]{2,1,0:T(8,128)(2,1)S(1)}, bf16[4,512,256]{2,1,0:T(8,128)(2,1)S(1)}, u32[]{:S(2)}, u32[]{:S(2)}) collective-permute-start(bf16[4,512,256]{2,1,0:T(8,128)(2,1)S(1)} %get-tuple-element.52.refs_0_.rows_ref), channel_id=1, source_target_pairs={{0,1},{1,0},{2,3},{3,2},{4,5},{5,4},{6,7},{7,6},{8,9},{9,8},{10,11... | collective-permute-start | bytes 3145736 | tf_op jit(solution)/shard_map/ppermute | solution.py:323
  15.2 12.5 %collective-permute-start.5 = (bf16[2,320,256]{2,1,0:T(8,128)(2,1)S(1)}, bf16[2,320,256]{2,1,0:T(8,128)(2,1)S(1)}, u32[]{:S(2)}, u32[]{:S(2)}) collective-permute-start(bf16[2,320,256]{2,1,0:T(8,128)(2,1)S(1)} %get-tuple-element.40), channel_id=1, source_target_pairs={{0,4},{4,8},{8,12},{12,0},{1,5},{5,9},{9,13},{13,1},{2,6},{6,10},{... | collective-permute-start | bytes 983048 | tf_op jit(solution)/shard_map/ppermute | solution.py:338
  15.4 25.7 %collective-permute-start.6 = (bf16[2,320,256]{2,1,0:T(8,128)(2,1)S(1)}, bf16[2,320,256]{2,1,0:T(8,128)(2,1)S(1)}, u32[]{:S(2)}, u32[]{:S(2)}) collective-permute-start(bf16[2,320,256]{2,1,0:T(8,128)(2,1)S(1)} %get-tuple-element.41), channel_id=1, source_target_pairs={{0,8},{4,12},{8,0},{12,4},{1,9},{5,13},{9,1},{13,5},{2,10},{6,14},... | collective-permute-start | bytes 983048 | tf_op jit(solution)/shard_map/ppermute | solution.py:338
  18.5 22.6 %collective-permute-start.7 = (bf16[2,320,256]{2,1,0:T(8,128)(2,1)S(1)}, bf16[2,320,256]{2,1,0:T(8,128)(2,1)S(1)}, u32[]{:S(2)}, u32[]{:S(2)}) collective-permute-start(bf16[2,320,256]{2,1,0:T(8,128)(2,1)S(1)} %get-tuple-element.42), channel_id=1, source_target_pairs={{0,12},{4,0},{8,4},{12,8},{1,13},{5,1},{9,5},{13,9},{2,14},{6,2},{... | collective-permute-start | bytes 983048 | tf_op jit(solution)/shard_map/ppermute | solution.py:338
  41.1 1.0 copy-start
  42.1 24.3 %collective-permute-start.9 = (bf16[4,512,256]{2,1,0:T(8,128)(2,1)S(1)}, bf16[4,512,256]{2,1,0:T(8,128)(2,1)S(1)}, u32[]{:S(2)}, u32[]{:S(2)}) collective-permute-start(bf16[4,512,256]{2,1,0:T(8,128)(2,1)S(1)} %collective-permute-done.3.refs_1_), channel_id=1, source_target_pairs={{0,1},{1,0},{2,3},{3,2},{4,5},{5,4},{6,7},{7,6},{8,9},{9,8},{10,11... | collective-permute-start | bytes 3145736 | tf_op jit(solution)/shard_map/ppermute | solution.py:323
  44.1 22.3 %collective-permute-start.8 = (bf16[4,320,256]{2,1,0:T(8,128)(2,1)S(1)}, bf16[4,320,256]{2,1,0:T(8,128)(2,1)S(1)}, u32[]{:S(2)}, u32[]{:S(2)}) collective-permute-start(bf16[4,320,256]{2,1,0:T(8,128)(2,1)S(1)} %select.10.refs_4_), channel_id=1, source_target_pairs={{0,2},{1,3},{2,0},{3,1},{4,6},{5,7},{6,4},{7,5},{8,10},{9,11},{10,... | collective-permute-start | bytes 1966088 | tf_op jit(solution)/shard_map/ppermute | solution.py:323
  44.7 12.3 %collective-permute-start.10 = (bf16[2,192,256]{2,1,0:T(8,128)(2,1)S(1)}, bf16[2,192,256]{2,1,0:T(8,128)(2,1)S(1)}, u32[]{:S(2)}, u32[]{:S(2)}) collective-permute-start(bf16[2,192,256]{2,1,0:T(8,128)(2,1)S(1)} %get-tuple-element.49), channel_id=1, source_target_pairs={{0,4},{4,8},{8,12},{12,0},{1,5},{5,9},{9,13},{13,1},{2,6},{6,10},{... | collective-permute-start | bytes 589832 | tf_op jit(solution)/shard_map/ppermute | solution.py:338
  51.4 13.6 %collective-permute-start.11 = (bf16[2,192,256]{2,1,0:T(8,128)(2,1)S(1)}, bf16[2,192,256]{2,1,0:T(8,128)(2,1)S(1)}, u32[]{:S(2)}, u32[]{:S(2)}) collective-permute-start(bf16[2,192,256]{2,1,0:T(8,128)(2,1)S(1)} %get-tuple-element.50), channel_id=1, source_target_pairs={{0,8},{4,12},{8,0},{12,4},{1,9},{5,13},{9,1},{13,5},{2,10},{6,14},... | collective-permute-start | bytes 589832 | tf_op jit(solution)/shard_map/ppermute | solution.py:338
  51.7 14.0 %collective-permute-start.12 = (bf16[2,192,256]{2,1,0:T(8,128)(2,1)S(1)}, bf16[2,192,256]{2,1,0:T(8,128)(2,1)S(1)}, u32[]{:S(2)}, u32[]{:S(2)}) collective-permute-start(bf16[2,192,256]{2,1,0:T(8,128)(2,1)S(1)} %get-tuple-element.51), channel_id=1, source_target_pairs={{0,12},{4,0},{8,4},{12,8},{1,13},{5,1},{9,5},{13,9},{2,14},{6,2},{... | collective-permute-start | bytes 589832 | tf_op jit(solution)/shard_map/ppermute | solution.py:338
  57.0 0.7 copy-start.4
  65.0 0.7 copy-start.6
  65.7 0.7 copy-start.8
  66.4 1.0 copy-start.2
  67.4 12.9 %collective-permute-start.13 = (bf16[4,320,256]{2,1,0:T(8,128)(2,1)S(1)}, bf16[4,320,256]{2,1,0:T(8,128)(2,1)}, u32[]{:S(2)}, u32[]{:S(2)}) collective-permute-start(bf16[4,320,256]{2,1,0:T(8,128)(2,1)S(1)} %select.10.refs_4_), channel_id=1, source_target_pairs={{0,1},{1,0},{2,3},{3,2},{4,5},{5,4},{6,7},{7,6},{8,9},{9,8},{10,11... | collective-permute-start | bytes 1966088 | tf_op jit(solution)/shard_map/ppermute | solution.py:323
  67.4 12.9 %collective-permute-start.14 = (bf16[4,320,256]{2,1,0:T(8,128)(2,1)S(1)}, bf16[4,320,256]{2,1,0:T(8,128)(2,1)}, u32[]{:S(2)}, u32[]{:S(2)}) collective-permute-start(bf16[4,320,256]{2,1,0:T(8,128)(2,1)S(1)} %collective-permute-done.8.refs_5_), channel_id=1, source_target_pairs={{0,1},{1,0},{2,3},{3,2},{4,5},{5,4},{6,7},{7,6},{8,9},{9,8},{10,11... | collective-permute-start | bytes 1966088 | tf_op jit(solution)/shard_map/ppermute | solution.py:323
  68.0 0.9 copy-start.5
  68.9 0.9 copy-start.7
  69.8 0.9 copy-start.9
  72.6 12.1 %collective-permute-start.15 = (bf16[4,192,256]{2,1,0:T(8,128)(2,1)S(1)}, bf16[4,192,256]{2,1,0:T(8,128)(2,1)S(1)}, u32[]{:S(2)}, u32[]{:S(2)}) collective-permute-start(bf16[4,192,256]{2,1,0:T(8,128)(2,1)S(1)} %select.11.refs_8_), channel_id=1, source_target_pairs={{0,2},{1,3},{2,0},{3,1},{4,6},{5,7},{6,4},{7,5},{8,10},{9,11},{10,... | collective-permute-start | bytes 1179656 | tf_op jit(solution)/shard_map/ppermute | solution.py:323
  74.1 10.6 %collective-permute-start.16 = (bf16[4,192,256]{2,1,0:T(8,128)(2,1)S(1)}, bf16[4,192,256]{2,1,0:T(8,128)(2,1)S(1)}, u32[]{:S(2)}, u32[]{:S(2)}) collective-permute-start(bf16[4,192,256]{2,1,0:T(8,128)(2,1)S(1)} %select.11.refs_8_), channel_id=1, source_target_pairs={{0,1},{1,0},{2,3},{3,2},{4,5},{5,4},{6,7},{7,6},{8,9},{9,8},{10,11... | collective-permute-start | bytes 1179656 | tf_op jit(solution)/shard_map/ppermute | solution.py:323
  74.1 6.2 %copy-start.1 = (bf16[4,512,256]{2,1,0:T(8,128)(2,1)S(1)}, bf16[4,512,256]{2,1,0:T(8,128)(2,1)}, u32[]{:S(2)}) copy-start(bf16[4,512,256]{2,1,0:T(8,128)(2,1)} %copy-done) | copy-start | bytes 3145732
  74.1 6.2 %copy-start.3 = (bf16[4,512,256]{2,1,0:T(8,128)(2,1)S(1)}, bf16[4,512,256]{2,1,0:T(8,128)(2,1)}, u32[]{:S(2)}) copy-start(bf16[4,512,256]{2,1,0:T(8,128)(2,1)} %copy-done.2) | copy-start | bytes 3145732
  84.7 1.9 %collective-permute-start.17 = (bf16[4,192,256]{2,1,0:T(8,128)(2,1)S(1)}, bf16[4,192,256]{2,1,0:T(8,128)(2,1)S(1)}, u32[]{:S(2)}, u32[]{:S(2)}) collective-permute-start(bf16[4,192,256]{2,1,0:T(8,128)(2,1)S(1)} %collective-permute-done.15.refs_9_), channel_id=1, source_target_pairs={{0,1},{1,0},{2,3},{3,2},{4,5},{5,4},{6,7},{7,6},{8,9},{9,8},{10,11... | collective-permute-start | bytes 1179656 | tf_op jit(solution)/shard_map/ppermute | solution.py:323
  90.9 8.8 %collective-permute-start.18 = (f32[4,512]{1,0:T(4,128)S(1)}, f32[4,512]{1,0:T(4,128)S(1)}, u32[]{:S(2)}, u32[]{:S(2)}) collective-permute-start(f32[4,512]{1,0:T(4,128)S(1)} %get-tuple-element.73), channel_id=1, source_target_pairs={{0,4},{4,8},{8,12},{12,0},{1,5},{5,9},{9,13},{13,1},{2,6},{6,10},{... | collective-permute-start | bytes 24584 | tf_op jit(solution)/shard_map/ppermute | solution.py:346
  94.4 5.4 %collective-permute-start.19 = (f32[4,512]{1,0:T(4,128)S(1)}, f32[4,512]{1,0:T(4,128)S(1)}, u32[]{:S(2)}, u32[]{:S(2)}) collective-permute-start(f32[4,512]{1,0:T(4,128)S(1)} %get-tuple-element.73), channel_id=1, source_target_pairs={{0,8},{4,12},{8,0},{12,4},{1,9},{5,13},{9,1},{13,5},{2,10},{6,14},... | collective-permute-start | bytes 24584 | tf_op jit(solution)/shard_map/ppermute | solution.py:346
  97.6 3.7 %collective-permute-start.20 = (f32[4,512]{1,0:T(4,128)S(1)}, f32[4,512]{1,0:T(4,128)S(1)}, u32[]{:S(2)}, u32[]{:S(2)}) collective-permute-start(f32[4,512]{1,0:T(4,128)S(1)} %get-tuple-element.73), channel_id=1, source_target_pairs={{0,12},{4,0},{8,4},{12,8},{1,13},{5,1},{9,5},{13,9},{2,14},{6,2},{... | collective-permute-start | bytes 24584 | tf_op jit(solution)/shard_map/ppermute | solution.py:346

commit v6 on v5

--- a/solution.py
+++ b/solution.py
@@ -55,7 +55,7 @@
             picks = [jnp.int32(0)] * capacity
             count = jnp.int32(0)
             for pair in range(pair_count):
-                col = asked[pair, 1]
+                col = asked[1, pair]
                 mine = (col >> 3) == me
                 for slot in range(capacity):
                     picks[slot] = jnp.where(mine & (count == slot), col & 7, picks[slot])
@@ -64,13 +64,13 @@
             for slot in range(capacity):
                 send(blocks_ref.at[picks[slot], pl.ds(start, size)], out.at[slot])
     for pair in range(pair_count):
-        send(blocks_ref.at[lists[0][pair, 0] & 7], rows_ref.at[pair])
+        send(blocks_ref.at[lists[0][0, pair] & 7], rows_ref.at[pair])
     for copy in copies:
         copy.wait()
 
 
 def pack(me, lists, blocks, capacity):
-    wide_count, pair_count = len(lists), lists[0].shape[0]
+    wide_count, pair_count = len(lists), lists[0].shape[1]
     feat = blocks.shape[-1]
     shapes = [
         pltpu.VMEM((capacity, size, feat), blocks.dtype)
@@ -94,7 +94,7 @@
 def select_kernel(wide_count, pair_count, start, size, me_ref, list_ref, blocks_ref, *refs):
     received, out_ref, sems = refs[:-2], refs[-2], refs[-1]
     me = me_ref[0]
-    owners = [list_ref[pair, 1] >> 3 for pair in range(pair_count)]
+    owners = [list_ref[1, pair] >> 3 for pair in range(pair_count)]
     for pair in range(pair_count):
         shift = me - owners[pair]
         shift = jnp.where(shift < 0, shift + wide_count, shift)
@@ -104,7 +104,7 @@
 
         @pl.when(shift == 0)
         def _():
-            source = blocks_ref.at[list_ref[pair, 1] & 7, pl.ds(start, size)]
+            source = blocks_ref.at[list_ref[1, pair] & 7, pl.ds(start, size)]
             pltpu.make_async_copy(source, out_ref.at[pair], sems.at[pair]).start()
 
         for other in range(1, wide_count):
@@ -120,7 +120,7 @@
 
 
 def select(me, pairs, blocks, received, start, size):
-    pair_count, feat = pairs.shape[0], blocks.shape[-1]
+    pair_count, feat = pairs.shape[1], blocks.shape[-1]
     return pl.pallas_call(
         functools.partial(select_kernel, len(received) + 1, pair_count, start, size),
         out_shape=pltpu.VMEM((pair_count, size, feat), blocks.dtype),
@@ -160,9 +160,11 @@
     return held
 
 
-def window_kernel(narrow_count, window, first, last, *refs):
+def window_kernel(window, first, last, *refs):
     held = segments(window)
-    all_rows, rest = refs[:narrow_count], refs[narrow_count:]
+    all_rows, rest = refs[:2], refs[2:]
+    half_count, pair_count = refs[0].shape[:2]
+    narrow_count = 2 * half_count
     all_cols = [rest[i * narrow_count : (i + 1) * narrow_count] for i in range(len(held))]
     rest = rest[len(held) * narrow_count :]
     if not first:
@@ -174,8 +176,8 @@
         square_ref, mass_ref, total_ref, sums_ref = rest
     else:
         mass_ref, total_ref, sums_ref = rest
-    for pair in range(all_rows[0].shape[0]):
-        rows = [ref[pair] for ref in all_rows]
+    for pair in range(pair_count):
+        rows = [ref[i, pair] for ref in all_rows for i in range(half_count)]
         cols = []
         for narrow in range(narrow_count):
             pieces = [
@@ -215,7 +217,7 @@
 
 
 def window_step(rows, cols, index, carry):
-    pair_count, _, feat = rows[0].shape
+    _, pair_count, _, feat = rows[0].shape
     window = WINDOWS[index]
     size = window[1] - window[0]
     first, last = index == 0, index == len(WINDOWS) - 1
@@ -235,7 +237,7 @@
         args += cols[chunk]
     args += [] if first else carry
     outs = pl.pallas_call(
-        functools.partial(window_kernel, len(rows), window, first, last),
+        functools.partial(window_kernel, window, first, last),
         out_shape=shapes,
         in_specs=[vmem()] * len(args),
         out_specs=[vmem()] * len(shapes),
@@ -269,7 +271,7 @@
 
 def mean_kernel(local_ref, rows_ref, part_ref, mass_ref, _, out_ref, made, sems):
     pair_count, _, feat = rows_ref.shape
-    local = [local_ref[pair, 0] & 7 for pair in range(pair_count)]
+    local = [local_ref[0, pair] & 7 for pair in range(pair_count)]
 
     def copy(pair):
         return pltpu.make_async_copy(made.at[pair], out_ref.at[local[pair]], sems.at[pair])
@@ -301,11 +303,11 @@
             copy(pair).wait()
 
 
-def means(pairs, rows, part, mass, blocks):
+def means(pairs, rows, part, mass, kept):
     pair_count, _, feat = part.shape
     return pl.pallas_call(
         mean_kernel,
-        out_shape=pltpu.HBM(blocks.shape, jnp.bfloat16),
+        out_shape=pltpu.HBM(kept.shape, jnp.bfloat16),
         in_specs=[smem(), vmem(), vmem(), vmem(), anywhere()],
         out_specs=anywhere(),
         scratch_shapes=[
@@ -315,7 +317,37 @@
         input_output_aliases={4: 0},
         compiler_params=params(16),
         name="means",
-    )(pairs, *[in_vmem(x) for x in (rows, part, mass)], in_hbm(keep(blocks)))
+    )(pairs, *[in_vmem(x) for x in (rows, part, mass)], in_hbm(kept))
+
+
+def weight_kernel(wide_count, me_ref, *refs):
+    lists, rows_ref, sums, out_ref = refs[:wide_count], refs[wide_count], refs[wide_count + 1 : -1], refs[-1]
+    pair_count = rows_ref.shape[0]
+    first = me_ref[0] * BLK_DEV
+    for block in range(BLK_DEV):
+        mass = jnp.zeros((1, BR), jnp.float32)
+        for pair in range(pair_count):
+            here = (lists[0][0, pair] == first + block).astype(jnp.float32)
+            mass = mass + here * rows_ref[pair : pair + 1]
+            for asked, sums_ref in zip(lists, sums):
+                here = (asked[1, pair] == first + block).astype(jnp.float32)
+                mass = mass + here * sums_ref[pair : pair + 1]
+        weight = 1.0 / (1.0 + mass / BR)
+        for part in range(BR // LANES):
+            row = block * (BR // LANES) + part
+            out_ref[row : row + 1] = weight[:, part * LANES : (part + 1) * LANES]
+
+
+def block_weights(me, lists, row_sums, col_sums):
+    out = pl.pallas_call(
+        functools.partial(weight_kernel, len(lists)),
+        out_shape=jax.ShapeDtypeStruct((BLK_DEV * BR // LANES, LANES), jnp.float32),
+        in_specs=[smem()] * (1 + len(lists)) + [vmem()] * (1 + len(col_sums)),
+        out_specs=vmem(),
+        compiler_params=params(4),
+        name="weights",
+    )(me, *lists, row_sums, *col_sums)
+    return out.reshape(BLK_DEV * BR)
 
 
 def hop(parts, step):
@@ -351,22 +383,22 @@
 def on_device(embeddings, pair_list):
     wide_count = lax.axis_size("wide")
     me = lax.axis_index("wide").astype(jnp.int32).reshape(1)
-    pair_count = pair_list.shape[0]
+    pairs = pair_list.T
+    pair_count = pairs.shape[1]
     capacity = max(2, 2 * pair_count // wide_count)
     feat = embeddings.shape[1]
     blocks = embeddings.reshape(BLK_DEV, BR, feat)
-    lists = from_others(pair_list)
+    lists = from_others(pairs)
     outgoing, row_slices = pack(me, lists, blocks, capacity)
     fixed = lax.optimization_barrier
 
     def pick(received, chunk):
-        return select(me, pair_list, blocks, received, *CHUNKS[chunk])
-
-    rows = first_hops(row_slices)
-    rows_last = hop(rows[:1], 1)
-    rows, rows_last, received = fixed((rows, rows_last, to_wide(outgoing[0])))
+        return select(me, pairs, blocks, received, *CHUNKS[chunk])
+
+    rows = jnp.stack(first_hops(row_slices))
+    rows, received, kept = fixed((rows, to_wide(outgoing[0]), keep(blocks)))
     cols_a = first_hops(pick(received, 0))
-    rows = rows + rows_last + hop(rows[1:], 1)
+    rows = [rows, *hop([rows], 1)]
     cols_a, rows, received = fixed((cols_a, rows, to_wide(outgoing[1])))
     cols_b = first_hops(pick(received, 1))
     last_b = hop(cols_b[:1], 1)
@@ -374,18 +406,11 @@
     carry = window_step(rows, [cols_a], 0, None)
     cols_b, last_b, carry = fixed((cols_b, last_b, carry))
     cols_b = cols_b + last_b + hop(cols_b[1:], 1)
-    carry = window_step(rows, [cols_a, cols_b], 1, carry)
-    part, mass, row_sums, col_sums = carry
-    every_sum = jnp.concatenate(from_others(col_sums), axis=0)
-    mean = means(pair_list, row_slices, part, mass, blocks)
-    block_ids = jnp.arange(BLK_DEV, dtype=jnp.int32)[:, None]
-    every_col = jnp.concatenate([x[:, 1] for x in lists])
-    mine = every_col[None, :] == me[0] * BLK_DEV + block_ids
-    col_mass = jnp.sum(jnp.where(mine[:, :, None], every_sum[None], 0.0), axis=1)
-    here = pair_list[:, 0][None, :] % BLK_DEV == block_ids
-    row_mass = jnp.sum(jnp.where(here[:, :, None], row_sums[None], 0.0), axis=1)
-    weights = 1.0 / (1.0 + (row_mass + col_mass) / BR)
-    return weights.reshape(BLK_DEV * BR), mean.reshape(BLK_DEV * BR, feat)
+    part, mass, row_sums, col_sums = window_step(rows, [cols_a, cols_b], 1, carry)
+    every_sum = from_others(col_sums)
+    mean = means(pairs, row_slices, part, mass, kept)
+    weights = block_weights(me, lists, row_sums, every_sum)
+    return weights, mean.reshape(BLK_DEV * BR, feat)
 
 
 def solution(mesh):

time: 103 us -> 94.9 us (0.921)
  local copies, waits for them, and re-layouts: 8.72 us -> 0.68 us
  waiting for transfers between devices: 37.4 us -> 41 us
  Pallas kernels: 23.3 us -> 20.6 us
    ppermute x9 -> x8, waiting for transfers between devices: 1.03 us -> 20.8 us  [hop(): lax.ppermute(part, 'narrow', [(i, i ^ step) for i in range(count)])]
    ppermute x6, waiting for transfers between devices: 32.6 us -> 12.9 us  [to_wide(): lax.ppermute(piece, 'wide', [(i, (i + shift) % count) for i in range(coun...]
    unnamed x24 -> x4, local copies, waits for them, and re-layouts: 8.17 us -> 0.68 us
    ppermute x6, waiting for transfers between devices: 3.75 us -> 7.28 us  [from_others(): lax.ppermute(part, 'wide', [(i, (i + shift) % count) for i in range(count)])]
    pallas_call x2, Pallas kernels: 3.84 us -> 2.67 us  [select(): pl.pallas_call(functools.partial(select_kernel, len(received) + 1, pair_c...]
    pallas_call x3 -> x4, Pallas kernels: 10.7 us -> 9.68 us  [the longest x2 6.12 us: window_step(): pl.pallas_call(functools.partial(window_kernel, window, first, last), out...]
    ppermute x9 -> x8, starting transfers between devices: 4.79 us -> 4.36 us  [hop(): lax.ppermute(part, 'narrow', [(i, i ^ step) for i in range(count)])]
  transfers between devices with their start and end apart: 21 -> 20, of which waited for: 8 -> 11; matrix products, arithmetic and copies ran while one was open for 1% -> 0% of each run, Pallas kernels for 16% -> 14%
where the time goes in v6:
time: 94.9 us; the launch traced here: 94.6 us
  waiting for transfers between devices  41 us (43%)
  starting transfers between devices  31.4 us (33%)
  Pallas kernels  20.6 us (22%)
    ppermute x8, waiting for transfers between devices, hop(): lax.ppermute(part, 'narrow', [(i, i ^ step) for i in range(count)])  20.8 us
    ppermute x6, starting transfers between devices, to_wide(): lax.ppermute(piece, 'wide', [(i, (i + shift) % count) for i in range(coun...  13.5 us
    ppermute x6, starting transfers between devices, from_others(): lax.ppermute(part, 'wide', [(i, (i + shift) % count) for i in range(count)])  13.5 us
    ppermute x6, waiting for transfers between devices, to_wide(): lax.ppermute(piece, 'wide', [(i, (i + shift) % count) for i in range(coun...  12.9 us
    ppermute x6, waiting for transfers between devices, from_others(): lax.ppermute(part, 'wide', [(i, (i + shift) % count) for i in range(count)])  7.28 us
    pallas_call x2, Pallas kernels, window_step(): pl.pallas_call(functools.partial(window_kernel, window, first, last), out...  6.12 us
    pallas_call x1, Pallas kernels, keep(): pl.pallas_call(keep_kernel, out_shape=pltpu.HBM(blocks.shape, blocks.dtyp...  5.63 us
    ppermute x8, starting transfers between devices, hop(): lax.ppermute(part, 'narrow', [(i, i ^ step) for i in range(count)])  4.36 us
  transfers between devices with their start and end apart: 20, of which 11 were waited for; matrix products, arithmetic and copies ran while one was open for 0% of the time, Pallas kernels for 14%

profile of v6, /device:TPU:0, one launch (start us, length us, event | category | flops | bytes accessed | tf_op | source)
XLA Modules:
  0.0 94.6 jit_solution(3541448377732267682)
XLA Ops:
  0.6 5.1 %collective-permute-start.2 = (s32[2,4]{1,0:T(2,128)}, s32[2,4]{1,0:T(2,128)S(1)}, u32[]{:S(2)}, u32[]{:S(2)}) collective-permute-start(s32[2,4]{1,0:T(2,128)} %bitcast.8), channel_id=1, source_target_pairs={{0,12},{4,0},{8,4},{12,8},{1,13},{5,1},{9,5},{13,9},{2,14},{6,2},{... | collective-permute-start | bytes 104 | tf_op jit(solution)/shard_map/ppermute | solution.py:378
  5.7 1.0 %collective-permute-start = (s32[2,4]{1,0:T(2,128)}, s32[2,4]{1,0:T(2,128)S(1)}, u32[]{:S(2)}, u32[]{:S(2)}) collective-permute-start(s32[2,4]{1,0:T(2,128)} %bitcast.10), channel_id=1, source_target_pairs={{0,4},{4,8},{8,12},{12,0},{1,5},{5,9},{9,13},{13,1},{2,6},{6,10},{... | collective-permute-start | bytes 104 | tf_op jit(solution)/shard_map/ppermute | solution.py:378
  6.7 0.5 collective-permute-done.2.refs_3_
  7.2 3.2 %collective-permute-done.1.refs_2_ = s32[2,4]{1,0:T(2,128)S(1)} collective-permute-done((s32[2,4]{1,0:T(2,128)}, s32[2,4]{1,0:T(2,128)S(1)}, u32[]{:S(2)}, u32[]{:S(2)}) %collective-permute-start.1) | collective-permute-done | bytes 64 | tf_op jit(solution)/shard_map/ppermute | solution.py:378
  10.4 0.9 collective-permute-done.refs_1_
  11.3 0.7 copy-done
  12.0 2.6 %pack.1 = (bf16[2,320,256]{2,1,0:T(8,128)(2,1)S(1)}, bf16[2,320,256]{2,1,0:T(8,128)(2,1)S(1)}, bf16[2,320,256]{2,1,0:T(8,128)(2,1)S(1)}, bf16[2,192,256]{2,1,0:T...) custom-call(s32[1]{0:T(128)} %bitcast.me_ref, ...), custom_call_target="tpu_custom_call" | custom-call | tf_op jit(solution)/shard_map/pack/pallas_call | solution.py:81
  14.6 1.6 %collective-permute-start.3 = (bf16[4,512,256]{2,1,0:T(8,128)(2,1)S(1)}, bf16[4,512,256]{2,1,0:T(8,128)(2,1)S(1)}, u32[]{:S(2)}, u32[]{:S(2)}) collective-permute-start(bf16[4,512,256]{2,1,0:T(8,128)(2,1)S(1)} %get-tuple-element.36.rows_ref), channel_id=1, source_target_pairs={{0,2},{1,3},{2,0},{3,1},{4,6},{5,7},{6,4},{7,5},{8,10},{9,11},{10,... | collective-permute-start | bytes 3145736 | tf_op jit(solution)/shard_map/ppermute | solution.py:355
  16.2 1.2 %collective-permute-start.5 = (bf16[2,320,256]{2,1,0:T(8,128)(2,1)S(1)}, bf16[2,320,256]{2,1,0:T(8,128)(2,1)S(1)}, u32[]{:S(2)}, u32[]{:S(2)}) collective-permute-start(bf16[2,320,256]{2,1,0:T(8,128)(2,1)S(1)} %get-tuple-element.38), channel_id=1, source_target_pairs={{0,8},{4,12},{8,0},{12,4},{1,9},{5,13},{9,1},{13,5},{2,10},{6,14},... | collective-permute-start | bytes 983048 | tf_op jit(solution)/shard_map/ppermute | solution.py:370
  17.4 2.9 %collective-permute-start.6 = (bf16[2,320,256]{2,1,0:T(8,128)(2,1)S(1)}, bf16[2,320,256]{2,1,0:T(8,128)(2,1)S(1)}, u32[]{:S(2)}, u32[]{:S(2)}) collective-permute-start(bf16[2,320,256]{2,1,0:T(8,128)(2,1)S(1)} %get-tuple-element.39), channel_id=1, source_target_pairs={{0,12},{4,0},{8,4},{12,8},{1,13},{5,1},{9,5},{13,9},{2,14},{6,2},{... | collective-permute-start | bytes 983048 | tf_op jit(solution)/shard_map/ppermute | solution.py:370
  20.3 5.6 %keep.1._ = bf16[8,512,256]{2,1,0:T(8,128)(2,1)} custom-call(bf16[8,512,256]{2,1,0:T(8,128)(2,1)} %bitcast.17), custom_call_target="tpu_custom_call" | custom-call | tf_op jit(solution)/shard_map/keep/pallas_call | solution.py:261
  25.9 12.2 %collective-permute-done.3 = bf16[4,512,256]{2,1,0:T(8,128)(2,1)S(1)} collective-permute-done((bf16[4,512,256]{2,1,0:T(8,128)(2,1)S(1)}, bf16[4,512,256]{2,1,0:T(8,128)(2,1)S(1)}, u32[]{:S(2)}, u32[]{:S(2)}) %collective-permute-start.3) | collective-permute-done | bytes 1048608 | tf_op jit(solution)/shard_map/ppermute | solution.py:355
  38.4 1.6 %collective-permute-done.5.refs_1_ = bf16[2,320,256]{2,1,0:T(8,128)(2,1)S(1)} collective-permute-done((bf16[2,320,256]{2,1,0:T(8,128)(2,1)S(1)}, bf16[2,320,256]{2,1,0:T(8,128)(2,1)S(1)}, u32[]{:S(2)}, u32[]{:S(2)}) %collective-permute-start.5) | collective-permute-done | bytes 327712 | tf_op jit(solution)/shard_map/ppermute | solution.py:370
  40.0 1.5 %select.2.refs_2_ = bf16[4,320,256]{2,1,0:T(8,128)(2,1)S(1)} custom-call(s32[1]{0:T(128)} %bitcast.me_ref, s32[2,4]{1,0:T(2,128)S(1)} %bitcast.12, bf16[8,512,256]{2,1,0:T(8,128)(2,1)} %bitcast.18, bf16[2,320,256]{2,1,0:T(8,128)(2,1)S(1)} %collective-permute-done.4.refs_0_, bf16[2,320,256]{2,1,0:T(8,128)(2,1)S(1)} %collective-permute-done.5.refs_1_, ...), custom_call_target="tpu_custom_call" | custom-call | tf_op jit(solution)/shard_map/select/pallas_call | solution.py:124
  41.5 0.6 collective-permute-start.7
  42.1 7.1 %collective-permute-start.9 = (bf16[2,192,256]{2,1,0:T(8,128)(2,1)S(1)}, bf16[2,192,256]{2,1,0:T(8,128)(2,1)S(1)}, u32[]{:S(2)}, u32[]{:S(2)}) collective-permute-start(bf16[2,192,256]{2,1,0:T(8,128)(2,1)S(1)} %get-tuple-element.44), channel_id=1, source_target_pairs={{0,4},{4,8},{8,12},{12,0},{1,5},{5,9},{9,13},{13,1},{2,6},{6,10},{... | collective-permute-start | bytes 589832 | tf_op jit(solution)/shard_map/ppermute | solution.py:370
  49.5 2.0 %collective-permute-start.11 = (bf16[2,192,256]{2,1,0:T(8,128)(2,1)S(1)}, bf16[2,192,256]{2,1,0:T(8,128)(2,1)S(1)}, u32[]{:S(2)}, u32[]{:S(2)}) collective-permute-start(bf16[2,192,256]{2,1,0:T(8,128)(2,1)S(1)} %get-tuple-element.46), channel_id=1, source_target_pairs={{0,12},{4,0},{8,4},{12,8},{1,13},{5,1},{9,5},{13,9},{2,14},{6,2},{... | collective-permute-start | bytes 589832 | tf_op jit(solution)/shard_map/ppermute | solution.py:370
  51.5 3.2 %collective-permute-done.9.refs_0_ = bf16[2,192,256]{2,1,0:T(8,128)(2,1)S(1)} collective-permute-done((bf16[2,192,256]{2,1,0:T(8,128)(2,1)S(1)}, bf16[2,192,256]{2,1,0:T(8,128)(2,1)S(1)}, u32[]{:S(2)}, u32[]{:S(2)}) %collective-permute-start.9) | collective-permute-done | bytes 196640 | tf_op jit(solution)/shard_map/ppermute | solution.py:370
  54.7 8.0 %collective-permute-done.10.refs_1_ = bf16[2,192,256]{2,1,0:T(8,128)(2,1)S(1)} collective-permute-done((bf16[2,192,256]{2,1,0:T(8,128)(2,1)S(1)}, bf16[2,192,256]{2,1,0:T(8,128)(2,1)S(1)}, u32[]{:S(2)}, u32[]{:S(2)}) %collective-permute-start.10) | collective-permute-done | bytes 196640 | tf_op jit(solution)/shard_map/ppermute | solution.py:370
  62.9 0.5 collective-permute-start.13
  63.4 1.2 %select.3.refs_6_ = bf16[4,192,256]{2,1,0:T(8,128)(2,1)S(1)} custom-call(s32[1]{0:T(128)} %bitcast.me_ref, s32[2,4]{1,0:T(2,128)S(1)} %bitcast.13, bf16[8,512,256]{2,1,0:T(8,128)(2,1)} %bitcast.19, bf16[2,192,256]{2,1,0:T(8,128)(2,1)S(1)} %collective-permute-done.9.refs_0_, bf16[2,192,256]{2,1,0:T(8,128)(2,1)S(1)} %collective-permute-done.10.refs_1_, ...), custom_call_target="tpu_custom_call" | custom-call | tf_op jit(solution)/shard_map/select/pallas_call | solution.py:124
  64.7 1.5 %collective-permute-start.14 = (bf16[4,192,256]{2,1,0:T(8,128)(2,1)S(1)}, bf16[4,192,256]{2,1,0:T(8,128)(2,1)S(1)}, u32[]{:S(2)}, u32[]{:S(2)}) collective-permute-start(bf16[4,192,256]{2,1,0:T(8,128)(2,1)S(1)} %select.3.refs_6_), channel_id=1, source_target_pairs={{0,2},{1,3},{2,0},{3,1},{4,6},{5,7},{6,4},{7,5},{8,10},{9,11},{10,... | collective-permute-start | bytes 1179656 | tf_op jit(solution)/shard_map/ppermute | solution.py:355
  66.2 3.1 %window.2 = (f32[4,512,128]{2,1,0:T(8,128)S(1)}, f32[4,512,128]{2,1,0:T(8,128)S(1)}, f32[4,512,256]{2,1,0:T(8,128)S(1)}, f32[4,256]{1,0:T(4,128)S(1)}) custom-call(bf16[2,4,512,256]{3,2,1,0:T(8,128)(2,1)S(1)} %pad_maximum_fusion.refs_0_, bf16[2,4,512,256]{3,2,1,0:T(8,128)(2,1)S(1)} %collective-permute-done.8.refs_1_, ...), custom_call_target="tpu_custom_call" | custom-call | flops 1342177280 | bytes 8388608 | tf_op jit(solution)/shard_map/window/pallas_call | solution.py:239
  69.3 6.9 %collective-permute-done.14.refs_7_ = bf16[4,192,256]{2,1,0:T(8,128)(2,1)S(1)} collective-permute-done((bf16[4,192,256]{2,1,0:T(8,128)(2,1)S(1)}, bf16[4,192,256]{2,1,0:T(8,128)(2,1)S(1)}, u32[]{:S(2)}, u32[]{:S(2)}) %collective-permute-start.14) | collective-permute-done | bytes 393248 | tf_op jit(solution)/shard_map/ppermute | solution.py:355
  76.2 1.7 %collective-permute-done.16.refs_9_ = bf16[4,192,256]{2,1,0:T(8,128)(2,1)S(1)} collective-permute-done((bf16[4,192,256]{2,1,0:T(8,128)(2,1)S(1)}, bf16[4,192,256]{2,1,0:T(8,128)(2,1)S(1)}, u32[]{:S(2)}, u32[]{:S(2)}) %collective-permute-start.16) | collective-permute-done | bytes 393248 | tf_op jit(solution)/shard_map/ppermute | solution.py:355
  77.9 3.0 %window.3 = (bf16[4,512,256]{2,1,0:T(8,128)(2,1)S(1)}, f32[4,512,128]{2,1,0:T(8,128)S(1)}, f32[4,512]{1,0:T(4,128)S(1)}, f32[4,512]{1,0:T(4,128)S(1)}) custom-call(bf16[2,4,512,256]{3,2,1,0:T(8,128)(2,1)S(1)} %pad_maximum_fusion.refs_0_, bf16[2,4,512,256]{3,2,1,0:T(8,128)(2,1)S(1)} %collective-permute-done.8.refs_1_, ...), custom_call_target="tpu_custom_call" | custom-call | flops 1342177280 | bytes 8388608 | tf_op jit(solution)/shard_map/window/pallas_call | solution.py:239
  80.9 6.7 %collective-permute-start.19 = (f32[4,512]{1,0:T(4,128)S(1)}, f32[4,512]{1,0:T(4,128)S(1)}, u32[]{:S(2)}, u32[]{:S(2)}) collective-permute-start(f32[4,512]{1,0:T(4,128)S(1)} %get-tuple-element.66.refs_5_), channel_id=1, source_target_pairs={{0,12},{4,0},{8,4},{12,8},{1,13},{5,1},{9,5},{13,9},{2,14},{6,2},{... | collective-permute-start | bytes 24584 | tf_op jit(solution)/shard_map/ppermute | solution.py:378
  87.7 0.6 collective-permute-start.17
  88.3 2.2 %means.1 = bf16[8,512,256]{2,1,0:T(8,128)(2,1)} custom-call(s32[2,4]{1,0:T(2,128)S(1)} %bitcast.14, bf16[4,512,256]{2,1,0:T(8,128)(2,1)S(1)} %get-tuple-element.36.rows_ref, bf16[4,512,256]{2,1,0:T(8,128)(2,1)S(1)} %get-tuple-element.67.part_ref, f32[4,512,128]{2,1,0:T(8,128)S(1)} %get-tuple-element.68.mass_ref, ...), custom_call_target="tpu_custom_call", output_to_operand_aliasing={{}: (4, {})} | custom-call | tf_op jit(solution)/shard_map/means/pallas_call | solution.py:308
  90.5 1.7 %collective-permute-done.18.refs_7_ = f32[4,512]{1,0:T(4,128)S(1)} collective-permute-done((f32[4,512]{1,0:T(4,128)S(1)}, f32[4,512]{1,0:T(4,128)S(1)}, u32[]{:S(2)}, u32[]{:S(2)}) %collective-permute-start.18) | collective-permute-done | bytes 8224 | tf_op jit(solution)/shard_map/ppermute | solution.py:378
  92.2 1.0 %collective-permute-done.17.refs_6_ = f32[4,512]{1,0:T(4,128)S(1)} collective-permute-done((f32[4,512]{1,0:T(4,128)S(1)}, f32[4,512]{1,0:T(4,128)S(1)}, u32[]{:S(2)}, u32[]{:S(2)}) %collective-permute-start.17) | collective-permute-done | bytes 8224 | tf_op jit(solution)/shard_map/ppermute | solution.py:378
  93.2 1.4 %weights.1 = f32[32,128]{1,0:T(8,128)} custom-call(s32[1]{0:T(128)} %bitcast.me_ref, s32[2,4]{1,0:T(2,128)S(1)} %bitcast.15, s32[2,4]{1,0:T(2,128)S(1)} %collective-permute-done.refs_1_, s32[2,4]{1,0:T(2,128)S(1)} %collective-permute-done.1.refs_2_, s32[2,4]{1,0:T(2,128)S(1)} %collective-permute-done.2.refs_3_, f32[4,512]{1,0:T(4,128)S(1)} %get-tuple-element.65.refs_4_, ...), custom_call_target="tpu_custom_call" | custom-call | tf_op jit(solution)/shard_map/weights/pallas_call | solution.py:342
  (21 shorter events, 0.9 us)
Async XLA Ops:
  0.6 6.6 %collective-permute-start.2 = (s32[2,4]{1,0:T(2,128)}, s32[2,4]{1,0:T(2,128)S(1)}, u32[]{:S(2)}, u32[]{:S(2)}) collective-permute-start(s32[2,4]{1,0:T(2,128)} %bitcast.8), channel_id=1, source_target_pairs={{0,12},{4,0},{8,4},{12,8},{1,13},{5,1},{9,5},{13,9},{2,14},{6,2},{... | collective-permute-start | bytes 104 | tf_op jit(solution)/shard_map/ppermute | solution.py:378
  5.7 4.7 %collective-permute-start.1 = (s32[2,4]{1,0:T(2,128)}, s32[2,4]{1,0:T(2,128)S(1)}, u32[]{:S(2)}, u32[]{:S(2)}) collective-permute-start(s32[2,4]{1,0:T(2,128)} %bitcast.9), channel_id=1, source_target_pairs={{0,8},{4,12},{8,0},{12,4},{1,9},{5,13},{9,1},{13,5},{2,10},{6,14},... | collective-permute-start | bytes 104 | tf_op jit(solution)/shard_map/ppermute | solution.py:378
  5.7 5.6 %collective-permute-start = (s32[2,4]{1,0:T(2,128)}, s32[2,4]{1,0:T(2,128)S(1)}, u32[]{:S(2)}, u32[]{:S(2)}) collective-permute-start(s32[2,4]{1,0:T(2,128)} %bitcast.10), channel_id=1, source_target_pairs={{0,4},{4,8},{8,12},{12,0},{1,5},{5,9},{9,13},{13,1},{2,6},{6,10},{... | collective-permute-start | bytes 104 | tf_op jit(solution)/shard_map/ppermute | solution.py:378
  11.3 0.7 copy-start
  14.6 23.5 %collective-permute-start.3 = (bf16[4,512,256]{2,1,0:T(8,128)(2,1)S(1)}, bf16[4,512,256]{2,1,0:T(8,128)(2,1)S(1)}, u32[]{:S(2)}, u32[]{:S(2)}) collective-permute-start(bf16[4,512,256]{2,1,0:T(8,128)(2,1)S(1)} %get-tuple-element.36.rows_ref), channel_id=1, source_target_pairs={{0,2},{1,3},{2,0},{3,1},{4,6},{5,7},{6,4},{7,5},{8,10},{9,11},{10,... | collective-permute-start | bytes 3145736 | tf_op jit(solution)/shard_map/ppermute | solution.py:355
  16.2 22.2 %collective-permute-start.4 = (bf16[2,320,256]{2,1,0:T(8,128)(2,1)S(1)}, bf16[2,320,256]{2,1,0:T(8,128)(2,1)S(1)}, u32[]{:S(2)}, u32[]{:S(2)}) collective-permute-start(bf16[2,320,256]{2,1,0:T(8,128)(2,1)S(1)} %get-tuple-element.37), channel_id=1, source_target_pairs={{0,4},{4,8},{8,12},{12,0},{1,5},{5,9},{9,13},{13,1},{2,6},{6,10},{... | collective-permute-start | bytes 983048 | tf_op jit(solution)/shard_map/ppermute | solution.py:370
  16.2 23.8 %collective-permute-start.5 = (bf16[2,320,256]{2,1,0:T(8,128)(2,1)S(1)}, bf16[2,320,256]{2,1,0:T(8,128)(2,1)S(1)}, u32[]{:S(2)}, u32[]{:S(2)}) collective-permute-start(bf16[2,320,256]{2,1,0:T(8,128)(2,1)S(1)} %get-tuple-element.38), channel_id=1, source_target_pairs={{0,8},{4,12},{8,0},{12,4},{1,9},{5,13},{9,1},{13,5},{2,10},{6,14},... | collective-permute-start | bytes 983048 | tf_op jit(solution)/shard_map/ppermute | solution.py:370
  17.4 22.6 %collective-permute-start.6 = (bf16[2,320,256]{2,1,0:T(8,128)(2,1)S(1)}, bf16[2,320,256]{2,1,0:T(8,128)(2,1)S(1)}, u32[]{:S(2)}, u32[]{:S(2)}) collective-permute-start(bf16[2,320,256]{2,1,0:T(8,128)(2,1)S(1)} %get-tuple-element.39), channel_id=1, source_target_pairs={{0,12},{4,0},{8,4},{12,8},{1,13},{5,1},{9,5},{13,9},{2,14},{6,2},{... | collective-permute-start | bytes 983048 | tf_op jit(solution)/shard_map/ppermute | solution.py:370
  38.2 1.8 %copy-start.1 = (s32[4,2]{0,1:T(2,128)S(1)}, s32[4,2]{0,1:T(2,128)}, u32[]{:S(2)}) copy-start(s32[4,2]{0,1:T(2,128)} %param.3) | copy-start | bytes 100
  40.0 22.8 %collective-permute-start.8 = (bf16[2,4,512,256]{3,2,1,0:T(8,128)(2,1)S(1)}, bf16[2,4,512,256]{3,2,1,0:T(8,128)(2,1)S(1)}, u32[]{:S(2)}, u32[]{:S(2)}) collective-permute-start(bf16[2,4,512,256]{3,2,1,0:T(8,128)(2,1)S(1)} %pad_maximum_fusion.refs_0_), channel_id=1, source_target_pairs={{0,1},{1,0},{2,3},{3,2},{4,5},{5,4},{6,7},{7,6},{8,9},{9,8},{10,11... | collective-permute-start | bytes 6291464 | tf_op jit(solution)/shard_map/ppermute | solution.py:355
  41.5 21.3 %collective-permute-start.7 = (bf16[4,320,256]{2,1,0:T(8,128)(2,1)S(1)}, bf16[4,320,256]{2,1,0:T(8,128)(2,1)S(1)}, u32[]{:S(2)}, u32[]{:S(2)}) collective-permute-start(bf16[4,320,256]{2,1,0:T(8,128)(2,1)S(1)} %select.2.refs_2_), channel_id=1, source_target_pairs={{0,2},{1,3},{2,0},{3,1},{4,6},{5,7},{6,4},{7,5},{8,10},{9,11},{10,... | collective-permute-start | bytes 1966088 | tf_op jit(solution)/shard_map/ppermute | solution.py:355
  42.1 12.6 %collective-permute-start.9 = (bf16[2,192,256]{2,1,0:T(8,128)(2,1)S(1)}, bf16[2,192,256]{2,1,0:T(8,128)(2,1)S(1)}, u32[]{:S(2)}, u32[]{:S(2)}) collective-permute-start(bf16[2,192,256]{2,1,0:T(8,128)(2,1)S(1)} %get-tuple-element.44), channel_id=1, source_target_pairs={{0,4},{4,8},{8,12},{12,0},{1,5},{5,9},{9,13},{13,1},{2,6},{6,10},{... | collective-permute-start | bytes 589832 | tf_op jit(solution)/shard_map/ppermute | solution.py:370
  49.2 13.6 %collective-permute-start.10 = (bf16[2,192,256]{2,1,0:T(8,128)(2,1)S(1)}, bf16[2,192,256]{2,1,0:T(8,128)(2,1)S(1)}, u32[]{:S(2)}, u32[]{:S(2)}) collective-permute-start(bf16[2,192,256]{2,1,0:T(8,128)(2,1)S(1)} %get-tuple-element.45), channel_id=1, source_target_pairs={{0,8},{4,12},{8,0},{12,4},{1,9},{5,13},{9,1},{13,5},{2,10},{6,14},... | collective-permute-start | bytes 589832 | tf_op jit(solution)/shard_map/ppermute | solution.py:370
  49.5 13.3 %collective-permute-start.11 = (bf16[2,192,256]{2,1,0:T(8,128)(2,1)S(1)}, bf16[2,192,256]{2,1,0:T(8,128)(2,1)S(1)}, u32[]{:S(2)}, u32[]{:S(2)}) collective-permute-start(bf16[2,192,256]{2,1,0:T(8,128)(2,1)S(1)} %get-tuple-element.46), channel_id=1, source_target_pairs={{0,12},{4,0},{8,4},{12,8},{1,13},{5,1},{9,5},{13,9},{2,14},{6,2},{... | collective-permute-start | bytes 589832 | tf_op jit(solution)/shard_map/ppermute | solution.py:370
  62.8 3.4 %collective-permute-start.12 = (bf16[4,320,256]{2,1,0:T(8,128)(2,1)S(1)}, bf16[4,320,256]{2,1,0:T(8,128)(2,1)S(1)}, u32[]{:S(2)}, u32[]{:S(2)}) collective-permute-start(bf16[4,320,256]{2,1,0:T(8,128)(2,1)S(1)} %select.2.refs_2_), channel_id=1, source_target_pairs={{0,1},{1,0},{2,3},{3,2},{4,5},{5,4},{6,7},{7,6},{8,9},{9,8},{10,11... | collective-permute-start | bytes 1966088 | tf_op jit(solution)/shard_map/ppermute | solution.py:355
  62.9 3.3 %collective-permute-start.13 = (bf16[4,320,256]{2,1,0:T(8,128)(2,1)S(1)}, bf16[4,320,256]{2,1,0:T(8,128)(2,1)S(1)}, u32[]{:S(2)}, u32[]{:S(2)}) collective-permute-start(bf16[4,320,256]{2,1,0:T(8,128)(2,1)S(1)} %collective-permute-done.7.refs_3_), channel_id=1, source_target_pairs={{0,1},{1,0},{2,3},{3,2},{4,5},{5,4},{6,7},{7,6},{8,9},{9,8},{10,11... | collective-permute-start | bytes 1966088 | tf_op jit(solution)/shard_map/ppermute | solution.py:355
  64.5 4.7 %collective-permute-start.15 = (bf16[4,192,256]{2,1,0:T(8,128)(2,1)S(1)}, bf16[4,192,256]{2,1,0:T(8,128)(2,1)S(1)}, u32[]{:S(2)}, u32[]{:S(2)}) collective-permute-start(bf16[4,192,256]{2,1,0:T(8,128)(2,1)S(1)} %select.3.refs_6_), channel_id=1, source_target_pairs={{0,1},{1,0},{2,3},{3,2},{4,5},{5,4},{6,7},{7,6},{8,9},{9,8},{10,11... | collective-permute-start | bytes 1179656 | tf_op jit(solution)/shard_map/ppermute | solution.py:355
  64.7 11.5 %collective-permute-start.14 = (bf16[4,192,256]{2,1,0:T(8,128)(2,1)S(1)}, bf16[4,192,256]{2,1,0:T(8,128)(2,1)S(1)}, u32[]{:S(2)}, u32[]{:S(2)}) collective-permute-start(bf16[4,192,256]{2,1,0:T(8,128)(2,1)S(1)} %select.3.refs_6_), channel_id=1, source_target_pairs={{0,2},{1,3},{2,0},{3,1},{4,6},{5,7},{6,4},{7,5},{8,10},{9,11},{10,... | collective-permute-start | bytes 1179656 | tf_op jit(solution)/shard_map/ppermute | solution.py:355
  76.1 1.7 %collective-permute-start.16 = (bf16[4,192,256]{2,1,0:T(8,128)(2,1)S(1)}, bf16[4,192,256]{2,1,0:T(8,128)(2,1)S(1)}, u32[]{:S(2)}, u32[]{:S(2)}) collective-permute-start(bf16[4,192,256]{2,1,0:T(8,128)(2,1)S(1)} %collective-permute-done.14.refs_7_), channel_id=1, source_target_pairs={{0,1},{1,0},{2,3},{3,2},{4,5},{5,4},{6,7},{7,6},{8,9},{9,8},{10,11... | collective-permute-start | bytes 1179656 | tf_op jit(solution)/shard_map/ppermute | solution.py:355
  80.9 9.5 %collective-permute-start.19 = (f32[4,512]{1,0:T(4,128)S(1)}, f32[4,512]{1,0:T(4,128)S(1)}, u32[]{:S(2)}, u32[]{:S(2)}) collective-permute-start(f32[4,512]{1,0:T(4,128)S(1)} %get-tuple-element.66.refs_5_), channel_id=1, source_target_pairs={{0,12},{4,0},{8,4},{12,8},{1,13},{5,1},{9,5},{13,9},{2,14},{6,2},{... | collective-permute-start | bytes 24584 | tf_op jit(solution)/shard_map/ppermute | solution.py:378
  87.6 4.5 %collective-permute-start.18 = (f32[4,512]{1,0:T(4,128)S(1)}, f32[4,512]{1,0:T(4,128)S(1)}, u32[]{:S(2)}, u32[]{:S(2)}) collective-permute-start(f32[4,512]{1,0:T(4,128)S(1)} %get-tuple-element.66.refs_5_), channel_id=1, source_target_pairs={{0,8},{4,12},{8,0},{12,4},{1,9},{5,13},{9,1},{13,5},{2,10},{6,14},... | collective-permute-start | bytes 24584 | tf_op jit(solution)/shard_map/ppermute | solution.py:378
  87.7 5.4 %collective-permute-start.17 = (f32[4,512]{1,0:T(4,128)S(1)}, f32[4,512]{1,0:T(4,128)S(1)}, u32[]{:S(2)}, u32[]{:S(2)}) collective-permute-start(f32[4,512]{1,0:T(4,128)S(1)} %get-tuple-element.66.refs_5_), channel_id=1, source_target_pairs={{0,4},{4,8},{8,12},{12,0},{1,5},{5,9},{9,13},{13,1},{2,6},{6,10},{... | collective-permute-start | bytes 24584 | tf_op jit(solution)/shard_map/ppermute | solution.py:378

commit v7 on v6

v7 whole, which is shorter than its diff:
```python
import functools

import jax
import jax.numpy as jnp
from jax import lax
from jax.experimental import pallas as pl
from jax.experimental.pallas import tpu as pltpu
from jax.sharding import PartitionSpec as P

F = 1024
BR = 512
BLK_DEV = 8
LANES = 128
CHUNKS = ((0, 320), (320, 192))
WINDOWS = ((0, 256), (256, 512))


def smem():
    return pl.BlockSpec(memory_space=pltpu.SMEM)


def vmem():
    return pl.BlockSpec(memory_space=pltpu.VMEM)


def anywhere():
    return pl.BlockSpec(memory_space=pl.ANY)


def in_vmem(x):
    return pltpu.with_memory_space_constraint(x, pltpu.VMEM)


def in_hbm(x):
    return pltpu.with_memory_space_constraint(x, pltpu.HBM)


def params(mebibytes):
    return pltpu.CompilerParams(vmem_limit_bytes=mebibytes * 1024 * 1024)


def pack_kernel(wide_count, pair_count, capacity, me_ref, *refs):
    lists, blocks_ref = refs[: wide_count - 1], refs[wide_count - 1]
    outs, sems = refs[wide_count:-1], refs[-1]
    me = me_ref[0]
    copies = []

    def send(source, target):
        copies.append(pltpu.make_async_copy(source, target, sems.at[len(copies)]))
        copies[-1].start()

    for chunk, (start, size) in enumerate(CHUNKS):
        for shift in range(1, wide_count):
            asked = lists[wide_count - shift - 1]
            picks = [jnp.int32(0)] * capacity
            count = jnp.int32(0)
            for pair in range(pair_count):
                col = asked[1, pair]
                mine = (col >> 3) == me
                for slot in range(capacity):
                    picks[slot] = jnp.where(mine & (count == slot), col & 7, picks[slot])
                count = count + mine.astype(jnp.int32)
            out = outs[chunk * (wide_count - 1) + shift - 1]
            for slot in range(capacity):
                send(blocks_ref.at[picks[slot], pl.ds(start, size)], out.at[slot])
    for copy in copies:
        copy.wait()


def pack(me, lists, blocks, capacity):
    wide_count, pair_count = len(lists) + 1, lists[0].shape[1]
    feat = blocks.shape[-1]
    shapes = [
        pltpu.VMEM((capacity, size, feat), blocks.dtype)
        for _, size in CHUNKS
        for _ in range(1, wide_count)
    ]
    outs = pl.pallas_call(
        functools.partial(pack_kernel, wide_count, pair_count, capacity),
        out_shape=shapes,
        in_specs=[smem()] * wide_count + [anywhere()],
        out_specs=[anywhere()] * len(shapes),
        scratch_shapes=[pltpu.SemaphoreType.DMA((len(shapes) * capacity,))],
        compiler_params=params(4),
        name="pack",
    )(me, *lists, in_hbm(blocks))
    each = wide_count - 1
    return [outs[c * each : (c + 1) * each] for c in range(len(CHUNKS))]


def take_kernel(pairs_ref, blocks_ref, out_ref, sems):
    copies = []
    for pair in range(out_ref.shape[0]):
        source = blocks_ref.at[pairs_ref[0, pair] & 7]
        copies.append(pltpu.make_async_copy(source, out_ref.at[pair], sems.at[pair]))
        copies[-1].start()
    for copy in copies:
        copy.wait()


def take(pairs, blocks):
    pair_count = pairs.shape[1]
    return pl.pallas_call(
        take_kernel,
        out_shape=pltpu.VMEM((pair_count, *blocks.shape[1:]), blocks.dtype),
        in_specs=[smem(), anywhere()],
        out_specs=anywhere(),
        scratch_shapes=[pltpu.SemaphoreType.DMA((pair_count,))],
        compiler_params=params(4),
        name="take",
    )(pairs, in_hbm(blocks))


def select_kernel(wide_count, pair_count, start, size, me_ref, list_ref, blocks_ref, *refs):
    received, out_ref, sems = refs[:-2], refs[-2], refs[-1]
    me = me_ref[0]
    owners = [list_ref[1, pair] >> 3 for pair in range(pair_count)]
    for pair in range(pair_count):
        shift = me - owners[pair]
        shift = jnp.where(shift < 0, shift + wide_count, shift)
        rank = jnp.int32(0)
        for before in range(pair):
            rank = rank + (owners[before] == owners[pair]).astype(jnp.int32)

        @pl.when(shift == 0)
        def _():
            source = blocks_ref.at[list_ref[1, pair] & 7, pl.ds(start, size)]
            pltpu.make_async_copy(source, out_ref.at[pair], sems.at[pair]).start()

        for other in range(1, wide_count):

            @pl.when(shift == other)
            def _():
                source = received[other - 1].at[rank]
                pltpu.make_async_copy(source, out_ref.at[pair], sems.at[pair]).start()

    for pair in range(pair_count):
        source = blocks_ref.at[0, pl.ds(start, size)]
        pltpu.make_async_copy(source, out_ref.at[pair], sems.at[pair]).wait()


def select(me, pairs, blocks, received, start, size):
    pair_count, feat = pairs.shape[1], blocks.shape[-1]
    return pl.pallas_call(
        functools.partial(select_kernel, len(received) + 1, pair_count, start, size),
        out_shape=pltpu.VMEM((pair_count, size, feat), blocks.dtype),
        in_specs=[smem(), smem(), anywhere()] + [anywhere()] * len(received),
        out_specs=anywhere(),
        scratch_shapes=[pltpu.SemaphoreType.DMA((pair_count,))],
        compiler_params=params(4),
        name="select",
    )(me, pairs, in_hbm(blocks), *[in_vmem(x) for x in received])


def tree(parts):
    while len(parts) > 1:
        half = len(parts) // 2
        parts = [parts[i] + parts[i + half] for i in range(half)]
    return parts[0]


def across(left, right):
    return lax.dot_general(
        left, right, (((1,), (1,)), ((), ())), preferred_element_type=jnp.float32
    )


def lane_sum(block):
    square = jnp.square(block.astype(jnp.float32))
    return sum(square[:, at : at + LANES] for at in range(0, square.shape[1], LANES))


def segments(window):
    low, high = window
    held = []
    for chunk, (start, size) in enumerate(CHUNKS):
        first, end = max(low, start), min(high, start + size)
        if first < end:
            held.append((chunk, first - start, end - first))
    return held


def scores(rows, cols, square):
    gram = tree([across(row, col) for row, col in zip(rows, cols)])
    other = jnp.sum(tree([lane_sum(col) for col in cols]).T, axis=0, keepdims=True)
    pieces, mass = [], None
    for at in range(0, gram.shape[1], LANES):
        here = slice(at, at + LANES)
        piece = jnp.exp((square + other[:, here] - 2.0 * gram[:, here]) * (-1.0 / F))
        mass = piece if mass is None else mass + piece
        pieces.append(piece)
    kernel = jnp.concatenate(pieces, axis=1) if len(pieces) > 1 else pieces[0]
    return kernel.astype(jnp.bfloat16), jnp.sum(kernel, axis=0, keepdims=True), mass


def window_parts(window, refs, pair):
    held = segments(window)
    half_count = refs[0].shape[0]
    narrow_count = 2 * half_count
    rows = [ref[i, pair] for ref in refs[:2] for i in range(half_count)]
    chunks = [refs[2 + i * narrow_count :][:narrow_count] for i in range(len(held))]
    cols = [own_columns(window, [chunk[i] for chunk in chunks], pair) for i in range(narrow_count)]
    return rows, cols


def own_columns(window, chunks, pair):
    held = segments(window)
    pieces = [ref[pair, at : at + size] for ref, (_, at, size) in zip(chunks, held)]
    return jnp.concatenate(pieces, axis=0) if len(pieces) > 1 else pieces[0]


def first_kernel(window, *refs):
    square_ref, mass_ref, total_ref, sums_ref = refs[-4:]
    for pair in range(square_ref.shape[0]):
        rows, cols = window_parts(window, refs, pair)
        square = jnp.sum(tree([lane_sum(row) for row in rows]), axis=1, keepdims=True)
        square = jnp.broadcast_to(square, (BR, LANES))
        kernel, sums, mass = scores(rows, cols, square)
        square_ref[pair] = square
        mass_ref[pair] = mass
        sums_ref[pair : pair + 1] = sums
        total_ref[pair] = jnp.dot(kernel, cols[0], preferred_element_type=jnp.float32)


def last_kernel(window, wide_count, me_ref, pairs_ref, *refs):
    square_in, mass_in, sums_in = refs[-6 - wide_count : -3 - wide_count]
    kernel_ref, mass_ref, row_ref = refs[-3 - wide_count : -wide_count]
    shares = refs[-wide_count:]
    for ref in (row_ref, *shares):
        ref[...] = jnp.zeros_like(ref)
    for pair in range(square_in.shape[0]):
        rows, cols = window_parts(window, refs, pair)
        kernel, sums, mass = scores(rows, cols, square_in[pair])
        kernel_ref[pair] = kernel
        sums = jnp.concatenate([sums_in[pair : pair + 1], sums], axis=1)
        mass = mass_in[pair] + mass
        mass_ref[pair] = mass
        row_ref[pl.ds(pairs_ref[0, pair] & 7, 1)] += jnp.sum(mass.T, axis=0, keepdims=True)
        col = pairs_ref[1, pair]
        shift = (col >> 3) - me_ref[0]
        shift = jnp.where(shift < 0, shift + wide_count, shift)
        for other, ref in enumerate(shares):
            ref[pl.ds(col & 7, 1)] += jnp.where(shift == other, sums, 0.0)


def estimate(pair_count, size):
    return pl.CostEstimate(
        flops=2 * pair_count * BR * size * F,
        transcendentals=pair_count * BR * size,
        bytes_accessed=8 * 1024 * 1024,
    )


def first_window(rows, cols):
    _, pair_count, _, feat = rows[0].shape
    window = WINDOWS[0]
    lanes = pltpu.VMEM((pair_count, BR, LANES), jnp.float32)
    total = pltpu.VMEM((pair_count, BR, feat), jnp.float32)
    args = list(rows)
    for chunk, _, _ in segments(window):
        args += cols[chunk]
    return pl.pallas_call(
        functools.partial(first_kernel, window),
        out_shape=[lanes, lanes, total, pltpu.VMEM((pair_count, window[1]), jnp.float32)],
        in_specs=[vmem()] * len(args),
        out_specs=[vmem()] * 4,
        compiler_params=params(16),
        cost_estimate=estimate(pair_count, window[1]),
        name="first_window",
    )(*[in_vmem(x) for x in args])


def last_window(me, pairs, rows, cols, square, mass, sums, wide_count):
    pair_count = rows[0].shape[1]
    window = WINDOWS[1]
    size = window[1] - window[0]
    by_block = pltpu.VMEM((BLK_DEV, BR), jnp.float32)
    shapes = [
        pltpu.VMEM((pair_count, BR, size), jnp.bfloat16),
        pltpu.VMEM((pair_count, BR, LANES), jnp.float32),
    ] + [by_block] * (1 + wide_count)
    args = list(rows)
    for chunk, _, _ in segments(window):
        args += cols[chunk]
    args += [square, mass, sums]
    kernel, mass, row_sums, *shares = pl.pallas_call(
        functools.partial(last_kernel, window, wide_count),
        out_shape=shapes,
        in_specs=[smem(), smem()] + [vmem()] * len(args),
        out_specs=[vmem()] * len(shapes),
        compiler_params=params(16),
        cost_estimate=estimate(pair_count, size),
        name="last_window",
    )(me, pairs, *[in_vmem(x) for x in args])
    return kernel, mass, row_sums, shares


def keep_kernel(block_ref, out_ref):
    out_ref[...] = block_ref[...]


def keep(blocks):
    block = pl.BlockSpec((1, *blocks.shape[1:]), lambda k: (k, 0, 0))
    return pl.pallas_call(
        keep_kernel,
        out_shape=pltpu.HBM(blocks.shape, blocks.dtype),
        grid=(blocks.shape[0],),
        in_specs=[block],
        out_specs=block,
        compiler_params=params(4),
        name="keep",
    )(in_hbm(blocks))


def mean_kernel(window, local_ref, rows_ref, kernel_ref, mass_ref, total_ref, *refs):
    *chunks, _, out_ref, part, weight, total, mass, made, sems = refs
    pair_count, _, feat = rows_ref.shape
    local = [local_ref[0, pair] & 7 for pair in range(pair_count)]

    def copy(pair):
        return pltpu.make_async_copy(made.at[pair], out_ref.at[local[pair]], sems.at[pair])

    firsts = []
    for pair in range(pair_count):
        sums = total_ref[pair] + jnp.dot(
            kernel_ref[pair], own_columns(window, chunks, pair), preferred_element_type=jnp.float32
        )
        part[pair] = sums.astype(jnp.bfloat16)
        weight[pair] = jnp.broadcast_to(
            jnp.sum(mass_ref[pair], axis=1, keepdims=True), (BR, LANES)
        )
        same = [local[other] == local[pair] for other in range(pair)]
        firsts.append(jnp.logical_not(functools.reduce(jnp.logical_or, same, jnp.bool_(False))))
    for pair in range(pair_count):

        @pl.when(firsts[pair])
        def _():
            total[...] = rows_ref[pair].astype(jnp.float32) + part[pair].astype(jnp.float32)
            mass[...] = 1.0 + weight[pair]
            for other in range(pair + 1, pair_count):

                @pl.when(local[other] == local[pair])
                def _():
                    total[...] += part[other].astype(jnp.float32)
                    mass[...] += weight[other]

            scale = 1.0 / mass[...]
            for at in range(0, feat, LANES):
                lanes = slice(at, at + LANES)
                made[pair, :, lanes] = (total[:, lanes] * scale).astype(jnp.bfloat16)
            copy(pair).start()

    for pair in range(pair_count):

        @pl.when(firsts[pair])
        def _():
            copy(pair).wait()


def means(pairs, rows, kernel, mass, total, cols, kept):
    pair_count, _, feat = rows.shape
    window = WINDOWS[1]
    own = [cols[chunk][0] for chunk, _, _ in segments(window)]
    args = [in_vmem(x) for x in (rows, kernel, mass, total, *own)]
    return pl.pallas_call(
        functools.partial(mean_kernel, window),
        out_shape=pltpu.HBM(kept.shape, jnp.bfloat16),
        in_specs=[smem()] + [vmem()] * len(args) + [anywhere()],
        out_specs=anywhere(),
        scratch_shapes=[
            pltpu.VMEM((pair_count, BR, feat), jnp.bfloat16),
            pltpu.VMEM((pair_count, BR, LANES), jnp.float32),
            pltpu.VMEM((BR, feat), jnp.float32),
            pltpu.VMEM((BR, LANES), jnp.float32),
            pltpu.VMEM((pair_count, BR, feat), jnp.bfloat16),
            pltpu.SemaphoreType.DMA((pair_count,)),
        ],
        input_output_aliases={1 + len(args): 0},
        compiler_params=params(16),
        cost_estimate=estimate(pair_count, 128),
        name="means",
    )(pairs, *args, in_hbm(kept))


def weight_kernel(*refs):
    out_ref = refs[-1]
    mass = refs[0][...]
    for ref in refs[1:-1]:
        mass = mass + ref[...]
    weight = 1.0 / (1.0 + mass / BR)
    parts = BR // LANES
    for block in range(BLK_DEV):
        for part in range(parts):
            lanes = slice(part * LANES, (part + 1) * LANES)
            out_ref[block * parts + part : block * parts + part + 1] = weight[block : block + 1, lanes]


def block_weights(sums):
    out = pl.pallas_call(
        weight_kernel,
        out_shape=jax.ShapeDtypeStruct((BLK_DEV * BR // LANES, LANES), jnp.float32),
        in_specs=[vmem()] * len(sums),
        out_specs=vmem(),
        compiler_params=params(4),
        name="weights",
    )(*[in_vmem(x) for x in sums])
    return out.reshape(BLK_DEV * BR)


def hop(parts, step):
    count = lax.axis_size("narrow")
    return [lax.ppermute(part, "narrow", [(i, i ^ step) for i in range(count)]) for part in parts]


def first_hops(part):
    parts = [part]
    step = lax.axis_size("narrow") // 2
    while step > 1:
        parts = parts + hop(parts, step)
        step //= 2
    return parts


def to_wide(pieces):
    count = lax.axis_size("wide")
    return [
        lax.ppermute(piece, "wide", [(i, (i + shift) % count) for i in range(count)])
        for shift, piece in enumerate(pieces, 1)
    ]


def on_device(embeddings, pair_list):
    wide_count = lax.axis_size("wide")
    me = lax.axis_index("wide").astype(jnp.int32).reshape(1)
    pairs = pair_list.T
    pair_count = pairs.shape[1]
    capacity = max(2, 2 * pair_count // wide_count)
    feat = embeddings.shape[1]
    blocks = embeddings.reshape(BLK_DEV, BR, feat)
    lists = to_wide([pairs] * (wide_count - 1))
    fixed = lax.optimization_barrier
    lists, row_slices = fixed((lists, take(pairs, blocks)))
    outgoing = pack(me, lists, blocks, capacity)

    def pick(received, chunk):
        return select(me, pairs, blocks, received, *CHUNKS[chunk])

    rows = jnp.stack(first_hops(row_slices))
    rows, received, kept = fixed((rows, to_wide(outgoing[0]), keep(blocks)))
    cols_a = first_hops(pick(received, 0))
    rows = [rows, *hop([rows], 1)]
    cols_a, rows, received = fixed((cols_a, rows, to_wide(outgoing[1])))
    cols_b = first_hops(pick(received, 1))
    last_b = hop(cols_b[:1], 1)
    cols_a = cols_a + hop(cols_a, 1)
    carry = first_window(rows, [cols_a])
    cols_b, last_b, carry = fixed((cols_b, last_b, carry))
    cols_b = cols_b + last_b + hop(cols_b[1:], 1)
    square, mass, total, sums = carry
    kernel, mass, row_sums, shares = last_window(
        me, pairs, rows, [cols_a, cols_b], square, mass, sums, wide_count
    )
    came = to_wide(shares[1:])
    mean = means(pairs, row_slices, kernel, mass, total, [cols_a, cols_b], kept)
    weights = block_weights([row_sums, shares[0], *came])
    return weights, mean.reshape(BLK_DEV * BR, feat)


def solution(mesh):
    in_specs = (P(("groups", "wide"), "narrow"), P(("groups", "wide"), None))
    out_specs = (P(("groups", "wide")), P(("groups", "wide"), "narrow"))
    return jax.shard_map(
        on_device, mesh=mesh, in_specs=in_specs, out_specs=out_specs, check_vma=False
    )
```

time: 94.9 us -> 92.2 us (0.972)
  waiting for transfers between devices: 41 us -> 37.5 us
    ppermute x6 -> x12, starting transfers between devices: 13.5 us -> 27.1 us  [to_wide(): lax.ppermute(piece, 'wide', [(i, (i + shift) % count) for i in range(coun...]
    ppermute x6 -> x0, starting transfers between devices: 13.5 us -> none  [from_others(): lax.ppermute(part, 'wide', [(i, (i + shift) % count) for i in range(count)])]
    ppermute x6 -> x0, waiting for transfers between devices: 7.28 us -> none  [from_others(): lax.ppermute(part, 'wide', [(i, (i + shift) % count) for i in range(count)])]
    ppermute x6 -> x12, waiting for transfers between devices: 12.9 us -> 18.8 us  [to_wide(): lax.ppermute(piece, 'wide', [(i, (i + shift) % count) for i in range(coun...]
    ppermute x8, waiting for transfers between devices: 20.8 us -> 18.7 us  [hop(): lax.ppermute(part, 'narrow', [(i, i ^ step) for i in range(count)])]
    pallas_call x4 -> x5, Pallas kernels: 9.68 us -> 10.1 us  [the longest x1 3.1 us: first_window(): pl.pallas_call(functools.partial(first_kernel, window), out_shape=[lanes,...]
  transfers between devices with their start and end apart: 20 -> 20, of which waited for: 11 -> 9; matrix products, arithmetic and copies ran while one was open for 0% -> 0% of each run, Pallas kernels for 14% -> 20%
where the time goes in v7:
time: 92.2 us; the launch traced here: 91.8 us
  waiting for transfers between devices  37.5 us (41%)
  starting transfers between devices  31.4 us (34%)
  Pallas kernels  21.2 us (23%)
    ppermute x12, starting transfers between devices, to_wide(): lax.ppermute(piece, 'wide', [(i, (i + shift) % count) for i in range(coun...  27.1 us
    ppermute x12, waiting for transfers between devices, to_wide(): lax.ppermute(piece, 'wide', [(i, (i + shift) % count) for i in range(coun...  18.8 us
    ppermute x8, waiting for transfers between devices, hop(): lax.ppermute(part, 'narrow', [(i, i ^ step) for i in range(count)])  18.7 us
    pallas_call x1, Pallas kernels, keep(): pl.pallas_call(keep_kernel, out_shape=pltpu.HBM(blocks.shape, blocks.dtyp...  5.63 us
    ppermute x8, starting transfers between devices, hop(): lax.ppermute(part, 'narrow', [(i, i ^ step) for i in range(count)])  4.3 us
    pallas_call x2, Pallas kernels, select(): pl.pallas_call(functools.partial(select_kernel, len(received) + 1, pair_c...  3.37 us
    pallas_call x1, Pallas kernels, first_window(): pl.pallas_call(functools.partial(first_kernel, window), out_shape=[lanes,...  3.1 us
    pallas_call x1, Pallas kernels, last_window(): pl.pallas_call(functools.partial(last_kernel, window, wide_count), out_sh...  2.49 us
  transfers between devices with their start and end apart: 20, of which 9 were waited for; matrix products, arithmetic and copies ran while one was open for 0% of the time, Pallas kernels for 20%

profile of v7, /device:TPU:0, one launch (start us, length us, event | category | flops | bytes accessed | tf_op | source)
XLA Modules:
  0.0 91.8 jit_solution(1137135378744010621)
XLA Ops:
  0.6 5.1 %collective-permute-start.2 = (s32[2,4]{1,0:T(2,128)}, s32[2,4]{1,0:T(2,128)S(1)}, u32[]{:S(2)}, u32[]{:S(2)}) collective-permute-start(s32[2,4]{1,0:T(2,128)} %bitcast.8), channel_id=1, source_target_pairs={{0,12},{4,0},{8,4},{12,8},{1,13},{5,1},{9,5},{13,9},{2,14},{6,2},{... | collective-permute-start | bytes 104 | tf_op jit(solution)/shard_map/ppermute | solution.py:427
  5.7 1.0 %collective-permute-start = (s32[2,4]{1,0:T(2,128)}, s32[2,4]{1,0:T(2,128)S(1)}, u32[]{:S(2)}, u32[]{:S(2)}) collective-permute-start(s32[2,4]{1,0:T(2,128)} %bitcast.10), channel_id=1, source_target_pairs={{0,4},{4,8},{8,12},{12,0},{1,5},{5,9},{9,13},{13,1},{2,6},{6,10},{... | collective-permute-start | bytes 104 | tf_op jit(solution)/shard_map/ppermute | solution.py:427
  6.7 0.7 copy-done
  7.5 1.8 %take.1.rows_ref = bf16[4,512,256]{2,1,0:T(8,128)(2,1)S(1)} custom-call(s32[2,4]{1,0:T(2,128)S(1)} %bitcast.11, bf16[8,512,256]{2,1,0:T(8,128)(2,1)} %bitcast.16), custom_call_target="tpu_custom_call" | custom-call | tf_op jit(solution)/shard_map/take/pallas_call | solution.py:103
  9.2 1.2 %collective-permute-done.1.refs_1_ = s32[2,4]{1,0:T(2,128)S(1)} collective-permute-done((s32[2,4]{1,0:T(2,128)}, s32[2,4]{1,0:T(2,128)S(1)}, u32[]{:S(2)}, u32[]{:S(2)}) %collective-permute-start.1) | collective-permute-done | bytes 64 | tf_op jit(solution)/shard_map/ppermute | solution.py:427
  10.4 0.9 collective-permute-done.refs_0_
  11.3 1.5 %collective-permute-start.3 = (bf16[4,512,256]{2,1,0:T(8,128)(2,1)S(1)}, bf16[4,512,256]{2,1,0:T(8,128)(2,1)S(1)}, u32[]{:S(2)}, u32[]{:S(2)}) collective-permute-start(bf16[4,512,256]{2,1,0:T(8,128)(2,1)S(1)} %take.1.rows_ref), channel_id=1, source_target_pairs={{0,2},{1,3},{2,0},{3,1},{4,6},{5,7},{6,4},{7,5},{8,10},{9,11},{10,... | collective-permute-start | bytes 3145736 | tf_op jit(solution)/shard_map/ppermute | solution.py:412
  12.8 2.2 %pack.1 = (bf16[2,320,256]{2,1,0:T(8,128)(2,1)S(1)}, bf16[2,320,256]{2,1,0:T(8,128)(2,1)S(1)}, bf16[2,320,256]{2,1,0:T(8,128)(2,1)S(1)}, bf16[2,192,256]{2,1,0:T...) custom-call(s32[1]{0:T(128)} %bitcast.me_ref, ...), custom_call_target="tpu_custom_call" | custom-call | tf_op jit(solution)/shard_map/pack/pallas_call | solution.py:78
  15.0 0.7 collective-permute-start.4
  15.7 0.8 collective-permute-start.5
  16.4 2.6 %collective-permute-start.6 = (bf16[2,320,256]{2,1,0:T(8,128)(2,1)S(1)}, bf16[2,320,256]{2,1,0:T(8,128)(2,1)S(1)}, u32[]{:S(2)}, u32[]{:S(2)}) collective-permute-start(bf16[2,320,256]{2,1,0:T(8,128)(2,1)S(1)} %get-tuple-element.48), channel_id=1, source_target_pairs={{0,12},{4,0},{8,4},{12,8},{1,13},{5,1},{9,5},{13,9},{2,14},{6,2},{... | collective-permute-start | bytes 983048 | tf_op jit(solution)/shard_map/ppermute | solution.py:427
  19.1 5.6 %keep.1.refs_2_ = bf16[8,512,256]{2,1,0:T(8,128)(2,1)} custom-call(bf16[8,512,256]{2,1,0:T(8,128)(2,1)} %bitcast.18), custom_call_target="tpu_custom_call" | custom-call | tf_op jit(solution)/shard_map/keep/pallas_call | solution.py:304
  24.7 10.1 %collective-permute-done.3 = bf16[4,512,256]{2,1,0:T(8,128)(2,1)S(1)} collective-permute-done((bf16[4,512,256]{2,1,0:T(8,128)(2,1)S(1)}, bf16[4,512,256]{2,1,0:T(8,128)(2,1)S(1)}, u32[]{:S(2)}, u32[]{:S(2)}) %collective-permute-start.3) | collective-permute-done | bytes 1048608 | tf_op jit(solution)/shard_map/ppermute | solution.py:412
  35.0 3.8 %collective-permute-done.5.refs_1_ = bf16[2,320,256]{2,1,0:T(8,128)(2,1)S(1)} collective-permute-done((bf16[2,320,256]{2,1,0:T(8,128)(2,1)S(1)}, bf16[2,320,256]{2,1,0:T(8,128)(2,1)S(1)}, u32[]{:S(2)}, u32[]{:S(2)}) %collective-permute-start.5) | collective-permute-done | bytes 327712 | tf_op jit(solution)/shard_map/ppermute | solution.py:427
  38.8 1.7 %select.2.refs_2_.refs_0_ = bf16[4,320,256]{2,1,0:T(8,128)(2,1)S(1)} custom-call(s32[1]{0:T(128)} %bitcast.me_ref, s32[2,4]{1,0:T(2,128)S(1)} %bitcast.12, bf16[8,512,256]{2,1,0:T(8,128)(2,1)} %bitcast.19, bf16[2,320,256]{2,1,0:T(8,128)(2,1)S(1)} %collective-permute-done.4.refs_0_, bf16[2,320,256]{2,1,0:T(8,128)(2,1)S(1)} %collective-permute-done.5.refs_1_, ...), custom_call_target="tpu_custom_call" | custom-call | tf_op jit(solution)/shard_map/select/pallas_call | solution.py:144
  40.5 0.6 collective-permute-start.7
  41.1 7.3 %collective-permute-start.9 = (bf16[2,192,256]{2,1,0:T(8,128)(2,1)S(1)}, bf16[2,192,256]{2,1,0:T(8,128)(2,1)S(1)}, u32[]{:S(2)}, u32[]{:S(2)}) collective-permute-start(bf16[2,192,256]{2,1,0:T(8,128)(2,1)S(1)} %get-tuple-element.53), channel_id=1, source_target_pairs={{0,4},{4,8},{8,12},{12,0},{1,5},{5,9},{9,13},{13,1},{2,6},{6,10},{... | collective-permute-start | bytes 589832 | tf_op jit(solution)/shard_map/ppermute | solution.py:427
  48.8 1.9 %collective-permute-start.11 = (bf16[2,192,256]{2,1,0:T(8,128)(2,1)S(1)}, bf16[2,192,256]{2,1,0:T(8,128)(2,1)S(1)}, u32[]{:S(2)}, u32[]{:S(2)}) collective-permute-start(bf16[2,192,256]{2,1,0:T(8,128)(2,1)S(1)} %get-tuple-element.55), channel_id=1, source_target_pairs={{0,12},{4,0},{8,4},{12,8},{1,13},{5,1},{9,5},{13,9},{2,14},{6,2},{... | collective-permute-start | bytes 589832 | tf_op jit(solution)/shard_map/ppermute | solution.py:427
  50.7 3.4 %collective-permute-done.9.refs_0_ = bf16[2,192,256]{2,1,0:T(8,128)(2,1)S(1)} collective-permute-done((bf16[2,192,256]{2,1,0:T(8,128)(2,1)S(1)}, bf16[2,192,256]{2,1,0:T(8,128)(2,1)S(1)}, u32[]{:S(2)}, u32[]{:S(2)}) %collective-permute-start.9) | collective-permute-done | bytes 196640 | tf_op jit(solution)/shard_map/ppermute | solution.py:427
  54.1 8.0 %collective-permute-done.10.refs_1_ = bf16[2,192,256]{2,1,0:T(8,128)(2,1)S(1)} collective-permute-done((bf16[2,192,256]{2,1,0:T(8,128)(2,1)S(1)}, bf16[2,192,256]{2,1,0:T(8,128)(2,1)S(1)}, u32[]{:S(2)}, u32[]{:S(2)}) %collective-permute-start.10) | collective-permute-done | bytes 196640 | tf_op jit(solution)/shard_map/ppermute | solution.py:427
  62.2 0.5 collective-permute-start.12
  62.7 1.6 %select.3.refs_6_.refs_1_ = bf16[4,192,256]{2,1,0:T(8,128)(2,1)S(1)} custom-call(s32[1]{0:T(128)} %bitcast.me_ref, s32[2,4]{1,0:T(2,128)S(1)} %bitcast.13, bf16[8,512,256]{2,1,0:T(8,128)(2,1)} %bitcast.20, bf16[2,192,256]{2,1,0:T(8,128)(2,1)S(1)} %collective-permute-done.9.refs_0_, bf16[2,192,256]{2,1,0:T(8,128)(2,1)S(1)} %collective-permute-done.10.refs_1_, ...), custom_call_target="tpu_custom_call" | custom-call | tf_op jit(solution)/shard_map/select/pallas_call | solution.py:144
  64.5 1.5 %collective-permute-start.14 = (bf16[4,192,256]{2,1,0:T(8,128)(2,1)S(1)}, bf16[4,192,256]{2,1,0:T(8,128)(2,1)S(1)}, u32[]{:S(2)}, u32[]{:S(2)}) collective-permute-start(bf16[4,192,256]{2,1,0:T(8,128)(2,1)S(1)} %select.3.refs_6_.refs_1_), channel_id=1, source_target_pairs={{0,2},{1,3},{2,0},{3,1},{4,6},{5,7},{6,4},{7,5},{8,10},{9,11},{10,... | collective-permute-start | bytes 1179656 | tf_op jit(solution)/shard_map/ppermute | solution.py:412
  66.0 3.1 %first_window.1 = (f32[4,512,128]{2,1,0:T(8,128)S(1)}, f32[4,512,128]{2,1,0:T(8,128)S(1)}, f32[4,512,256]{2,1,0:T(8,128)S(1)}, f32[4,256]{1,0:T(4,128)S(1)}) custom-call(bf16[2,4,512,256]{3,2,1,0:T(8,128)(2,1)S(1)} %pad_maximum_fusion.refs_0_, bf16[2,4,512,256]{3,2,1,0:T(8,128)(2,1)S(1)} %collective-permute-done.8.refs_1_, ...), custom_call_target="tpu_custom_call" | custom-call | flops 1073741824 | bytes 8388608 | tf_op jit(solution)/shard_map/first_window/pallas_call | solution.py:262
  69.1 6.9 %collective-permute-done.14.refs_7_ = bf16[4,192,256]{2,1,0:T(8,128)(2,1)S(1)} collective-permute-done((bf16[4,192,256]{2,1,0:T(8,128)(2,1)S(1)}, bf16[4,192,256]{2,1,0:T(8,128)(2,1)S(1)}, u32[]{:S(2)}, u32[]{:S(2)}) %collective-permute-start.14) | collective-permute-done | bytes 393248 | tf_op jit(solution)/shard_map/ppermute | solution.py:412
  76.0 1.7 %collective-permute-done.16.refs_9_ = bf16[4,192,256]{2,1,0:T(8,128)(2,1)S(1)} collective-permute-done((bf16[4,192,256]{2,1,0:T(8,128)(2,1)S(1)}, bf16[4,192,256]{2,1,0:T(8,128)(2,1)S(1)}, u32[]{:S(2)}, u32[]{:S(2)}) %collective-permute-start.16) | collective-permute-done | bytes 393248 | tf_op jit(solution)/shard_map/ppermute | solution.py:412
  77.7 2.5 %last_window.1 = (bf16[4,512,256]{2,1,0:T(8,128)(2,1)S(1)}, f32[4,512,128]{2,1,0:T(8,128)S(1)}, f32[8,512]{1,0:T(8,128)S(1)}, f32[8,512]{1,0:T(8,128)S(1)}, f32[...) custom-call(s32[1]{0:T(128)} %bitcast.me_ref, s32[2,4]{1,0:T(2,128)S(1)} %bitcast.14, ...), custom_call_target="tpu_custom_call" | custom-call | flops 1073741824 | bytes 8388608 | tf_op jit(solution)/shard_map/last_window/pallas_call | solution.py:286
  80.2 4.2 %collective-permute-start.17 = (f32[8,512]{1,0:T(8,128)S(1)}, f32[8,512]{1,0:T(8,128)S(1)}, u32[]{:S(2)}, u32[]{:S(2)}) collective-permute-start(f32[8,512]{1,0:T(8,128)S(1)} %get-tuple-element.75), channel_id=1, source_target_pairs={{0,4},{4,8},{8,12},{12,0},{1,5},{5,9},{9,13},{13,1},{2,6},{6,10},{... | collective-permute-start | bytes 49160 | tf_op jit(solution)/shard_map/ppermute | solution.py:427
  84.4 3.1 %collective-permute-start.18 = (f32[8,512]{1,0:T(8,128)S(1)}, f32[8,512]{1,0:T(8,128)S(1)}, u32[]{:S(2)}, u32[]{:S(2)}) collective-permute-start(f32[8,512]{1,0:T(8,128)S(1)} %get-tuple-element.76), channel_id=1, source_target_pairs={{0,8},{4,12},{8,0},{12,4},{1,9},{5,13},{9,1},{13,5},{2,10},{6,14},... | collective-permute-start | bytes 49160 | tf_op jit(solution)/shard_map/ppermute | solution.py:427
  87.5 2.1 %means.1 = bf16[8,512,256]{2,1,0:T(8,128)(2,1)} custom-call(s32[2,4]{1,0:T(2,128)S(1)} %bitcast.15, bf16[4,512,256]{2,1,0:T(8,128)(2,1)S(1)} %take.1.rows_ref, bf16[4,512,256]{2,1,0:T(8,128)(2,1)S(1)} %get-tuple-element.78.kernel_ref, f32[4,512,128]{2,1,0:T(8,128)S(1)} %get-tuple-element.79.mass_ref, ...), custom_call_target="tpu_custom_call", output_to_operand_aliasing={{}: (7, {})} | custom-call | flops 536870912 | bytes 8388608 | tf_op jit(solution)/shard_map/means/pallas_call | solution.py:365
  89.6 1.6 %collective-permute-done.19.refs_4_ = f32[8,512]{1,0:T(8,128)S(1)} collective-permute-done((f32[8,512]{1,0:T(8,128)S(1)}, f32[8,512]{1,0:T(8,128)S(1)}, u32[]{:S(2)}, u32[]{:S(2)}) %collective-permute-start.19) | collective-permute-done | bytes 16416 | tf_op jit(solution)/shard_map/ppermute | solution.py:427
  91.2 0.6 weights.1
  (22 shorter events, 0.9 us)
Async XLA Ops:
  0.6 8.6 %collective-permute-start.2 = (s32[2,4]{1,0:T(2,128)}, s32[2,4]{1,0:T(2,128)S(1)}, u32[]{:S(2)}, u32[]{:S(2)}) collective-permute-start(s32[2,4]{1,0:T(2,128)} %bitcast.8), channel_id=1, source_target_pairs={{0,12},{4,0},{8,4},{12,8},{1,13},{5,1},{9,5},{13,9},{2,14},{6,2},{... | collective-permute-start | bytes 104 | tf_op jit(solution)/shard_map/ppermute | solution.py:427
  5.7 4.7 %collective-permute-start.1 = (s32[2,4]{1,0:T(2,128)}, s32[2,4]{1,0:T(2,128)S(1)}, u32[]{:S(2)}, u32[]{:S(2)}) collective-permute-start(s32[2,4]{1,0:T(2,128)} %bitcast.9), channel_id=1, source_target_pairs={{0,8},{4,12},{8,0},{12,4},{1,9},{5,13},{9,1},{13,5},{2,10},{6,14},... | collective-permute-start | bytes 104 | tf_op jit(solution)/shard_map/ppermute | solution.py:427
  5.7 5.6 %collective-permute-start = (s32[2,4]{1,0:T(2,128)}, s32[2,4]{1,0:T(2,128)S(1)}, u32[]{:S(2)}, u32[]{:S(2)}) collective-permute-start(s32[2,4]{1,0:T(2,128)} %bitcast.10), channel_id=1, source_target_pairs={{0,4},{4,8},{8,12},{12,0},{1,5},{5,9},{9,13},{13,1},{2,6},{6,10},{... | collective-permute-start | bytes 104 | tf_op jit(solution)/shard_map/ppermute | solution.py:427
  6.7 0.7 copy-start
  11.3 23.5 %collective-permute-start.3 = (bf16[4,512,256]{2,1,0:T(8,128)(2,1)S(1)}, bf16[4,512,256]{2,1,0:T(8,128)(2,1)S(1)}, u32[]{:S(2)}, u32[]{:S(2)}) collective-permute-start(bf16[4,512,256]{2,1,0:T(8,128)(2,1)S(1)} %take.1.rows_ref), channel_id=1, source_target_pairs={{0,2},{1,3},{2,0},{3,1},{4,6},{5,7},{6,4},{7,5},{8,10},{9,11},{10,... | collective-permute-start | bytes 3145736 | tf_op jit(solution)/shard_map/ppermute | solution.py:412
  15.0 20.0 %collective-permute-start.4 = (bf16[2,320,256]{2,1,0:T(8,128)(2,1)S(1)}, bf16[2,320,256]{2,1,0:T(8,128)(2,1)S(1)}, u32[]{:S(2)}, u32[]{:S(2)}) collective-permute-start(bf16[2,320,256]{2,1,0:T(8,128)(2,1)S(1)} %get-tuple-element.46), channel_id=1, source_target_pairs={{0,4},{4,8},{8,12},{12,0},{1,5},{5,9},{9,13},{13,1},{2,6},{6,10},{... | collective-permute-start | bytes 983048 | tf_op jit(solution)/shard_map/ppermute | solution.py:427
  15.7 23.1 %collective-permute-start.5 = (bf16[2,320,256]{2,1,0:T(8,128)(2,1)S(1)}, bf16[2,320,256]{2,1,0:T(8,128)(2,1)S(1)}, u32[]{:S(2)}, u32[]{:S(2)}) collective-permute-start(bf16[2,320,256]{2,1,0:T(8,128)(2,1)S(1)} %get-tuple-element.47), channel_id=1, source_target_pairs={{0,8},{4,12},{8,0},{12,4},{1,9},{5,13},{9,1},{13,5},{2,10},{6,14},... | collective-permute-start | bytes 983048 | tf_op jit(solution)/shard_map/ppermute | solution.py:427
  16.4 22.3 %collective-permute-start.6 = (bf16[2,320,256]{2,1,0:T(8,128)(2,1)S(1)}, bf16[2,320,256]{2,1,0:T(8,128)(2,1)S(1)}, u32[]{:S(2)}, u32[]{:S(2)}) collective-permute-start(bf16[2,320,256]{2,1,0:T(8,128)(2,1)S(1)} %get-tuple-element.48), channel_id=1, source_target_pairs={{0,12},{4,0},{8,4},{12,8},{1,13},{5,1},{9,5},{13,9},{2,14},{6,2},{... | collective-permute-start | bytes 983048 | tf_op jit(solution)/shard_map/ppermute | solution.py:427
  34.8 4.0 %copy-start.1 = (s32[4,2]{0,1:T(2,128)S(1)}, s32[4,2]{0,1:T(2,128)}, u32[]{:S(2)}) copy-start(s32[4,2]{0,1:T(2,128)} %param.3) | copy-start | bytes 100
  38.7 23.4 %collective-permute-start.8 = (bf16[2,4,512,256]{3,2,1,0:T(8,128)(2,1)S(1)}, bf16[2,4,512,256]{3,2,1,0:T(8,128)(2,1)S(1)}, u32[]{:S(2)}, u32[]{:S(2)}) collective-permute-start(bf16[2,4,512,256]{3,2,1,0:T(8,128)(2,1)S(1)} %pad_maximum_fusion.refs_0_), channel_id=1, source_target_pairs={{0,1},{1,0},{2,3},{3,2},{4,5},{5,4},{6,7},{7,6},{8,9},{9,8},{10,11... | collective-permute-start | bytes 6291464 | tf_op jit(solution)/shard_map/ppermute | solution.py:412
  40.5 21.6 %collective-permute-start.7 = (bf16[4,320,256]{2,1,0:T(8,128)(2,1)S(1)}, bf16[4,320,256]{2,1,0:T(8,128)(2,1)S(1)}, u32[]{:S(2)}, u32[]{:S(2)}) collective-permute-start(bf16[4,320,256]{2,1,0:T(8,128)(2,1)S(1)} %select.2.refs_2_.refs_0_), channel_id=1, source_target_pairs={{0,2},{1,3},{2,0},{3,1},{4,6},{5,7},{6,4},{7,5},{8,10},{9,11},{10,... | collective-permute-start | bytes 1966088 | tf_op jit(solution)/shard_map/ppermute | solution.py:412
  41.1 13.0 %collective-permute-start.9 = (bf16[2,192,256]{2,1,0:T(8,128)(2,1)S(1)}, bf16[2,192,256]{2,1,0:T(8,128)(2,1)S(1)}, u32[]{:S(2)}, u32[]{:S(2)}) collective-permute-start(bf16[2,192,256]{2,1,0:T(8,128)(2,1)S(1)} %get-tuple-element.53), channel_id=1, source_target_pairs={{0,4},{4,8},{8,12},{12,0},{1,5},{5,9},{9,13},{13,1},{2,6},{6,10},{... | collective-permute-start | bytes 589832 | tf_op jit(solution)/shard_map/ppermute | solution.py:427
  48.4 13.8 %collective-permute-start.10 = (bf16[2,192,256]{2,1,0:T(8,128)(2,1)S(1)}, bf16[2,192,256]{2,1,0:T(8,128)(2,1)S(1)}, u32[]{:S(2)}, u32[]{:S(2)}) collective-permute-start(bf16[2,192,256]{2,1,0:T(8,128)(2,1)S(1)} %get-tuple-element.54), channel_id=1, source_target_pairs={{0,8},{4,12},{8,0},{12,4},{1,9},{5,13},{9,1},{13,5},{2,10},{6,14},... | collective-permute-start | bytes 589832 | tf_op jit(solution)/shard_map/ppermute | solution.py:427
  48.8 13.3 %collective-permute-start.11 = (bf16[2,192,256]{2,1,0:T(8,128)(2,1)S(1)}, bf16[2,192,256]{2,1,0:T(8,128)(2,1)S(1)}, u32[]{:S(2)}, u32[]{:S(2)}) collective-permute-start(bf16[2,192,256]{2,1,0:T(8,128)(2,1)S(1)} %get-tuple-element.55), channel_id=1, source_target_pairs={{0,12},{4,0},{8,4},{12,8},{1,13},{5,1},{9,5},{13,9},{2,14},{6,2},{... | collective-permute-start | bytes 589832 | tf_op jit(solution)/shard_map/ppermute | solution.py:427
  62.1 3.9 %collective-permute-start.13 = (bf16[4,320,256]{2,1,0:T(8,128)(2,1)S(1)}, bf16[4,320,256]{2,1,0:T(8,128)(2,1)S(1)}, u32[]{:S(2)}, u32[]{:S(2)}) collective-permute-start(bf16[4,320,256]{2,1,0:T(8,128)(2,1)S(1)} %collective-permute-done.7.refs_3_), channel_id=1, source_target_pairs={{0,1},{1,0},{2,3},{3,2},{4,5},{5,4},{6,7},{7,6},{8,9},{9,8},{10,11... | collective-permute-start | bytes 1966088 | tf_op jit(solution)/shard_map/ppermute | solution.py:412
  62.2 3.8 %collective-permute-start.12 = (bf16[4,320,256]{2,1,0:T(8,128)(2,1)S(1)}, bf16[4,320,256]{2,1,0:T(8,128)(2,1)S(1)}, u32[]{:S(2)}, u32[]{:S(2)}) collective-permute-start(bf16[4,320,256]{2,1,0:T(8,128)(2,1)S(1)} %select.2.refs_2_.refs_0_), channel_id=1, source_target_pairs={{0,1},{1,0},{2,3},{3,2},{4,5},{5,4},{6,7},{7,6},{8,9},{9,8},{10,11... | collective-permute-start | bytes 1966088 | tf_op jit(solution)/shard_map/ppermute | solution.py:412
  64.4 4.7 %collective-permute-start.15 = (bf16[4,192,256]{2,1,0:T(8,128)(2,1)S(1)}, bf16[4,192,256]{2,1,0:T(8,128)(2,1)S(1)}, u32[]{:S(2)}, u32[]{:S(2)}) collective-permute-start(bf16[4,192,256]{2,1,0:T(8,128)(2,1)S(1)} %select.3.refs_6_.refs_1_), channel_id=1, source_target_pairs={{0,1},{1,0},{2,3},{3,2},{4,5},{5,4},{6,7},{7,6},{8,9},{9,8},{10,11... | collective-permute-start | bytes 1179656 | tf_op jit(solution)/shard_map/ppermute | solution.py:412
  64.5 11.5 %collective-permute-start.14 = (bf16[4,192,256]{2,1,0:T(8,128)(2,1)S(1)}, bf16[4,192,256]{2,1,0:T(8,128)(2,1)S(1)}, u32[]{:S(2)}, u32[]{:S(2)}) collective-permute-start(bf16[4,192,256]{2,1,0:T(8,128)(2,1)S(1)} %select.3.refs_6_.refs_1_), channel_id=1, source_target_pairs={{0,2},{1,3},{2,0},{3,1},{4,6},{5,7},{6,4},{7,5},{8,10},{9,11},{10,... | collective-permute-start | bytes 1179656 | tf_op jit(solution)/shard_map/ppermute | solution.py:412
  76.0 1.7 %collective-permute-start.16 = (bf16[4,192,256]{2,1,0:T(8,128)(2,1)S(1)}, bf16[4,192,256]{2,1,0:T(8,128)(2,1)S(1)}, u32[]{:S(2)}, u32[]{:S(2)}) collective-permute-start(bf16[4,192,256]{2,1,0:T(8,128)(2,1)S(1)} %collective-permute-done.14.refs_7_), channel_id=1, source_target_pairs={{0,1},{1,0},{2,3},{3,2},{4,5},{5,4},{6,7},{7,6},{8,9},{9,8},{10,11... | collective-permute-start | bytes 1179656 | tf_op jit(solution)/shard_map/ppermute | solution.py:412
  80.2 9.4 %collective-permute-start.17 = (f32[8,512]{1,0:T(8,128)S(1)}, f32[8,512]{1,0:T(8,128)S(1)}, u32[]{:S(2)}, u32[]{:S(2)}) collective-permute-start(f32[8,512]{1,0:T(8,128)S(1)} %get-tuple-element.75), channel_id=1, source_target_pairs={{0,4},{4,8},{8,12},{12,0},{1,5},{5,9},{9,13},{13,1},{2,6},{6,10},{... | collective-permute-start | bytes 49160 | tf_op jit(solution)/shard_map/ppermute | solution.py:427
  84.4 5.2 %collective-permute-start.18 = (f32[8,512]{1,0:T(8,128)S(1)}, f32[8,512]{1,0:T(8,128)S(1)}, u32[]{:S(2)}, u32[]{:S(2)}) collective-permute-start(f32[8,512]{1,0:T(8,128)S(1)} %get-tuple-element.76), channel_id=1, source_target_pairs={{0,8},{4,12},{8,0},{12,4},{1,9},{5,13},{9,1},{13,5},{2,10},{6,14},... | collective-permute-start | bytes 49160 | tf_op jit(solution)/shard_map/ppermute | solution.py:427
  87.5 3.7 %collective-permute-start.19 = (f32[8,512]{1,0:T(8,128)S(1)}, f32[8,512]{1,0:T(8,128)S(1)}, u32[]{:S(2)}, u32[]{:S(2)}) collective-permute-start(f32[8,512]{1,0:T(8,128)S(1)} %get-tuple-element.77), channel_id=1, source_target_pairs={{0,12},{4,0},{8,4},{12,8},{1,13},{5,1},{9,5},{13,9},{2,14},{6,2},{... | collective-permute-start | bytes 49160 | tf_op jit(solution)/shard_map/ppermute | solution.py:427

commit v8 on v7

--- a/solution.py
+++ b/solution.py
@@ -11,7 +11,7 @@
 BR = 512
 BLK_DEV = 8
 LANES = 128
-CHUNKS = ((0, 320), (320, 192))
+CHUNKS = ((0, 368), (368, 144))
 WINDOWS = ((0, 256), (256, 512))
 
 
@@ -88,35 +88,38 @@
     return [outs[c * each : (c + 1) * each] for c in range(len(CHUNKS))]
 
 
-def take_kernel(pairs_ref, blocks_ref, out_ref, sems):
+def take_kernel(pairs_ref, blocks_ref, rows_ref, cols_ref, sems):
     copies = []
-    for pair in range(out_ref.shape[0]):
-        source = blocks_ref.at[pairs_ref[0, pair] & 7]
-        copies.append(pltpu.make_async_copy(source, out_ref.at[pair], sems.at[pair]))
-        copies[-1].start()
+    for pair in range(rows_ref.shape[0]):
+        for side, out in enumerate((rows_ref, cols_ref)):
+            source = blocks_ref.at[pairs_ref[side, pair] & 7]
+            copies.append(pltpu.make_async_copy(source, out.at[pair], sems.at[len(copies)]))
+            copies[-1].start()
     for copy in copies:
         copy.wait()
 
 
 def take(pairs, blocks):
     pair_count = pairs.shape[1]
+    taken = pltpu.VMEM((pair_count, *blocks.shape[1:]), blocks.dtype)
     return pl.pallas_call(
         take_kernel,
-        out_shape=pltpu.VMEM((pair_count, *blocks.shape[1:]), blocks.dtype),
+        out_shape=[taken, taken],
         in_specs=[smem(), anywhere()],
-        out_specs=anywhere(),
-        scratch_shapes=[pltpu.SemaphoreType.DMA((pair_count,))],
+        out_specs=[anywhere(), anywhere()],
+        scratch_shapes=[pltpu.SemaphoreType.DMA((2 * pair_count,))],
         compiler_params=params(4),
         name="take",
     )(pairs, in_hbm(blocks))
 
 
-def select_kernel(wide_count, pair_count, start, size, me_ref, list_ref, blocks_ref, *refs):
-    received, out_ref, sems = refs[:-2], refs[-2], refs[-1]
-    me = me_ref[0]
-    owners = [list_ref[1, pair] >> 3 for pair in range(pair_count)]
+def select_kernel(start, me_ref, pairs_ref, own_ref, *refs):
+    received, out_ref = refs[:-1], refs[-1]
+    wide_count = len(received) + 1
+    pair_count, size, _ = out_ref.shape
+    owners = [pairs_ref[1, pair] >> 3 for pair in range(pair_count)]
     for pair in range(pair_count):
-        shift = me - owners[pair]
+        shift = me_ref[0] - owners[pair]
         shift = jnp.where(shift < 0, shift + wide_count, shift)
         rank = jnp.int32(0)
         for before in range(pair):
@@ -124,32 +127,25 @@
 
         @pl.when(shift == 0)
         def _():
-            source = blocks_ref.at[list_ref[1, pair] & 7, pl.ds(start, size)]
-            pltpu.make_async_copy(source, out_ref.at[pair], sems.at[pair]).start()
+            out_ref[pair] = own_ref[pair, start : start + size]
 
         for other in range(1, wide_count):
 
             @pl.when(shift == other)
             def _():
-                source = received[other - 1].at[rank]
-                pltpu.make_async_copy(source, out_ref.at[pair], sems.at[pair]).start()
-
-    for pair in range(pair_count):
-        source = blocks_ref.at[0, pl.ds(start, size)]
-        pltpu.make_async_copy(source, out_ref.at[pair], sems.at[pair]).wait()
-
-
-def select(me, pairs, blocks, received, start, size):
-    pair_count, feat = pairs.shape[1], blocks.shape[-1]
+                out_ref[pair] = received[other - 1][rank]
+
+
+def select(me, pairs, own, received, start, size):
+    pair_count, _, feat = own.shape
     return pl.pallas_call(
-        functools.partial(select_kernel, len(received) + 1, pair_count, start, size),
-        out_shape=pltpu.VMEM((pair_count, size, feat), blocks.dtype),
-        in_specs=[smem(), smem(), anywhere()] + [anywhere()] * len(received),
-        out_specs=anywhere(),
-        scratch_shapes=[pltpu.SemaphoreType.DMA((pair_count,))],
+        functools.partial(select_kernel, start),
+        out_shape=pltpu.VMEM((pair_count, size, feat), own.dtype),
+        in_specs=[smem(), smem()] + [vmem()] * (1 + len(received)),
+        out_specs=vmem(),
         compiler_params=params(4),
         name="select",
-    )(me, pairs, in_hbm(blocks), *[in_vmem(x) for x in received])
+    )(me, pairs, *[in_vmem(x) for x in (own, *received)])
 
 
 def tree(parts):
@@ -439,11 +435,11 @@
     blocks = embeddings.reshape(BLK_DEV, BR, feat)
     lists = to_wide([pairs] * (wide_count - 1))
     fixed = lax.optimization_barrier
-    lists, row_slices = fixed((lists, take(pairs, blocks)))
+    lists, (row_slices, own) = fixed((lists, take(pairs, blocks)))
     outgoing = pack(me, lists, blocks, capacity)
 
     def pick(received, chunk):
-        return select(me, pairs, blocks, received, *CHUNKS[chunk])
+        return select(me, pairs, own, received, *CHUNKS[chunk])
 
     rows = jnp.stack(first_hops(row_slices))
     rows, received, kept = fixed((rows, to_wide(outgoing[0]), keep(blocks)))

time: 92.2 us -> 91 us (0.987)
  starting transfers between devices: 31.4 us -> 36.2 us
  waiting for transfers between devices: 37.5 us -> 32.8 us
  Pallas kernels: 21.2 us -> 20 us
    ppermute x12, starting transfers between devices: 27.1 us -> 31.9 us  [to_wide(): lax.ppermute(piece, 'wide', [(i, (i + shift) % count) for i in range(coun...]
    ppermute x12, waiting for transfers between devices: 18.8 us -> 16.4 us  [to_wide(): lax.ppermute(piece, 'wide', [(i, (i + shift) % count) for i in range(coun...]
    ppermute x8, waiting for transfers between devices: 18.7 us -> 16.4 us  [hop(): lax.ppermute(part, 'narrow', [(i, i ^ step) for i in range(count)])]
    pallas_call x3, Pallas kernels: 5.14 us -> 3.75 us  [the longest x1 2.4 us: take(): pl.pallas_call(take_kernel, out_shape=[taken, taken], in_specs=[smem(), a...]
  transfers between devices with their start and end apart: 20 -> 20, of which waited for: 9 -> 9; matrix products, arithmetic and copies ran while one was open for 0% -> 0% of each run, Pallas kernels for 20% -> 19%
where the time goes in v8:
time: 91 us; the launch traced here: 90.6 us
  starting transfers between devices  36.2 us (40%)
  waiting for transfers between devices  32.8 us (36%)
  Pallas kernels  20 us (22%)
    ppermute x12, starting transfers between devices, to_wide(): lax.ppermute(piece, 'wide', [(i, (i + shift) % count) for i in range(coun...  31.9 us
    ppermute x8, waiting for transfers between devices, hop(): lax.ppermute(part, 'narrow', [(i, i ^ step) for i in range(count)])  16.4 us
    ppermute x12, waiting for transfers between devices, to_wide(): lax.ppermute(piece, 'wide', [(i, (i + shift) % count) for i in range(coun...  16.4 us
    pallas_call x1, Pallas kernels, keep(): pl.pallas_call(keep_kernel, out_shape=pltpu.HBM(blocks.shape, blocks.dtyp...  5.63 us
    ppermute x8, starting transfers between devices, hop(): lax.ppermute(part, 'narrow', [(i, i ^ step) for i in range(count)])  4.3 us
    pallas_call x1, Pallas kernels, first_window(): pl.pallas_call(functools.partial(first_kernel, window), out_shape=[lanes,...  3.1 us
    pallas_call x1, Pallas kernels, last_window(): pl.pallas_call(functools.partial(last_kernel, window, wide_count), out_sh...  2.51 us
    pallas_call x1, Pallas kernels, take(): pl.pallas_call(take_kernel, out_shape=[taken, taken], in_specs=[smem(), a...  2.4 us
  transfers between devices with their start and end apart: 20, of which 9 were waited for; matrix products, arithmetic and copies ran while one was open for 0% of the time, Pallas kernels for 19%

profile of v8, /device:TPU:0, one launch (start us, length us, event | category | flops | bytes accessed | tf_op | source)
XLA Modules:
  0.0 90.6 jit_solution(9655800375988067786)
XLA Ops:
  0.6 5.1 %collective-permute-start.2 = (s32[2,4]{1,0:T(2,128)}, s32[2,4]{1,0:T(2,128)S(1)}, u32[]{:S(2)}, u32[]{:S(2)}) collective-permute-start(s32[2,4]{1,0:T(2,128)} %bitcast.8), channel_id=1, source_target_pairs={{0,12},{4,0},{8,4},{12,8},{1,13},{5,1},{9,5},{13,9},{2,14},{6,2},{... | collective-permute-start | bytes 104 | tf_op jit(solution)/shard_map/ppermute | solution.py:423
  5.7 1.0 %collective-permute-start = (s32[2,4]{1,0:T(2,128)}, s32[2,4]{1,0:T(2,128)S(1)}, u32[]{:S(2)}, u32[]{:S(2)}) collective-permute-start(s32[2,4]{1,0:T(2,128)} %bitcast.10), channel_id=1, source_target_pairs={{0,4},{4,8},{8,12},{12,0},{1,5},{5,9},{9,13},{13,1},{2,6},{6,10},{... | collective-permute-start | bytes 104 | tf_op jit(solution)/shard_map/ppermute | solution.py:423
  6.7 0.7 copy-done
  7.5 2.4 %take.1 = (bf16[4,512,256]{2,1,0:T(8,128)(2,1)S(1)}, bf16[4,512,256]{2,1,0:T(8,128)(2,1)S(1)}) custom-call(s32[2,4]{1,0:T(2,128)S(1)} %bitcast.11, bf16[8,512,256]{2,1,0:T(8,128)(2,1)} %bitcast.16), custom_call_target="tpu_custom_call" | custom-call | tf_op jit(solution)/shard_map/take/pallas_call | solution.py:105
  9.9 0.5 collective-permute-done.1.refs_1_
  10.4 0.9 collective-permute-done.refs_0_
  11.3 1.5 %collective-permute-start.3 = (bf16[4,512,256]{2,1,0:T(8,128)(2,1)S(1)}, bf16[4,512,256]{2,1,0:T(8,128)(2,1)S(1)}, u32[]{:S(2)}, u32[]{:S(2)}) collective-permute-start(bf16[4,512,256]{2,1,0:T(8,128)(2,1)S(1)} %get-tuple-element.48.rows_ref), channel_id=1, source_target_pairs={{0,2},{1,3},{2,0},{3,1},{4,6},{5,7},{6,4},{7,5},{8,10},{9,11},{10,... | collective-permute-start | bytes 3145736 | tf_op jit(solution)/shard_map/ppermute | solution.py:408
  12.8 2.1 %pack.1 = (bf16[2,368,256]{2,1,0:T(8,128)(2,1)S(1)}, bf16[2,368,256]{2,1,0:T(8,128)(2,1)S(1)}, bf16[2,368,256]{2,1,0:T(8,128)(2,1)S(1)}, bf16[2,144,256]{2,1,0:T...) custom-call(s32[1]{0:T(128)} %bitcast.me_ref, ...), custom_call_target="tpu_custom_call" | custom-call | tf_op jit(solution)/shard_map/pack/pallas_call | solution.py:78
  15.0 1.0 %collective-permute-start.4 = (bf16[2,368,256]{2,1,0:T(8,128)(2,1)S(1)}, bf16[2,368,256]{2,1,0:T(8,128)(2,1)S(1)}, u32[]{:S(2)}, u32[]{:S(2)}) collective-permute-start(bf16[2,368,256]{2,1,0:T(8,128)(2,1)S(1)} %get-tuple-element.52), channel_id=1, source_target_pairs={{0,4},{4,8},{8,12},{12,0},{1,5},{5,9},{9,13},{13,1},{2,6},{6,10},{... | collective-permute-start | bytes 1130504 | tf_op jit(solution)/shard_map/ppermute | solution.py:423
  15.9 1.3 %collective-permute-start.5 = (bf16[2,368,256]{2,1,0:T(8,128)(2,1)S(1)}, bf16[2,368,256]{2,1,0:T(8,128)(2,1)S(1)}, u32[]{:S(2)}, u32[]{:S(2)}) collective-permute-start(bf16[2,368,256]{2,1,0:T(8,128)(2,1)S(1)} %get-tuple-element.53), channel_id=1, source_target_pairs={{0,8},{4,12},{8,0},{12,4},{1,9},{5,13},{9,1},{13,5},{2,10},{6,14},... | collective-permute-start | bytes 1130504 | tf_op jit(solution)/shard_map/ppermute | solution.py:423
  17.2 1.9 %collective-permute-start.6 = (bf16[2,368,256]{2,1,0:T(8,128)(2,1)S(1)}, bf16[2,368,256]{2,1,0:T(8,128)(2,1)S(1)}, u32[]{:S(2)}, u32[]{:S(2)}) collective-permute-start(bf16[2,368,256]{2,1,0:T(8,128)(2,1)S(1)} %get-tuple-element.54), channel_id=1, source_target_pairs={{0,12},{4,0},{8,4},{12,8},{1,13},{5,1},{9,5},{13,9},{2,14},{6,2},{... | collective-permute-start | bytes 1130504 | tf_op jit(solution)/shard_map/ppermute | solution.py:423
  19.1 5.6 %keep.1.refs_2_ = bf16[8,512,256]{2,1,0:T(8,128)(2,1)} custom-call(bf16[8,512,256]{2,1,0:T(8,128)(2,1)} %bitcast.18), custom_call_target="tpu_custom_call" | custom-call | tf_op jit(solution)/shard_map/keep/pallas_call | solution.py:300
  24.7 10.1 %collective-permute-done.3 = bf16[4,512,256]{2,1,0:T(8,128)(2,1)S(1)} collective-permute-done((bf16[4,512,256]{2,1,0:T(8,128)(2,1)S(1)}, bf16[4,512,256]{2,1,0:T(8,128)(2,1)S(1)}, u32[]{:S(2)}, u32[]{:S(2)}) %collective-permute-start.3) | collective-permute-done | bytes 1048608 | tf_op jit(solution)/shard_map/ppermute | solution.py:408
  35.0 6.9 %collective-permute-done.5.refs_1_ = bf16[2,368,256]{2,1,0:T(8,128)(2,1)S(1)} collective-permute-done((bf16[2,368,256]{2,1,0:T(8,128)(2,1)S(1)}, bf16[2,368,256]{2,1,0:T(8,128)(2,1)S(1)}, u32[]{:S(2)}, u32[]{:S(2)}) %collective-permute-start.5) | collective-permute-done | bytes 376864 | tf_op jit(solution)/shard_map/ppermute | solution.py:423
  41.9 0.7 select.2.refs_2_.refs_0_
  42.6 0.6 collective-permute-start.7
  43.2 8.5 %collective-permute-start.9 = (bf16[2,144,256]{2,1,0:T(8,128)(2,1)S(1)}, bf16[2,144,256]{2,1,0:T(8,128)(2,1)S(1)}, u32[]{:S(2)}, u32[]{:S(2)}) collective-permute-start(bf16[2,144,256]{2,1,0:T(8,128)(2,1)S(1)} %get-tuple-element.59), channel_id=1, source_target_pairs={{0,4},{4,8},{8,12},{12,0},{1,5},{5,9},{9,13},{13,1},{2,6},{6,10},{... | collective-permute-start | bytes 442376 | tf_op jit(solution)/shard_map/ppermute | solution.py:423
  52.0 2.1 %collective-permute-start.11 = (bf16[2,144,256]{2,1,0:T(8,128)(2,1)S(1)}, bf16[2,144,256]{2,1,0:T(8,128)(2,1)S(1)}, u32[]{:S(2)}, u32[]{:S(2)}) collective-permute-start(bf16[2,144,256]{2,1,0:T(8,128)(2,1)S(1)} %get-tuple-element.61), channel_id=1, source_target_pairs={{0,12},{4,0},{8,4},{12,8},{1,13},{5,1},{9,5},{13,9},{2,14},{6,2},{... | collective-permute-start | bytes 442376 | tf_op jit(solution)/shard_map/ppermute | solution.py:423
  54.1 2.1 %collective-permute-done.9.refs_0_ = bf16[2,144,256]{2,1,0:T(8,128)(2,1)S(1)} collective-permute-done((bf16[2,144,256]{2,1,0:T(8,128)(2,1)S(1)}, bf16[2,144,256]{2,1,0:T(8,128)(2,1)S(1)}, u32[]{:S(2)}, u32[]{:S(2)}) %collective-permute-start.9) | collective-permute-done | bytes 147488 | tf_op jit(solution)/shard_map/ppermute | solution.py:423
  56.2 5.9 %collective-permute-done.10.refs_1_ = bf16[2,144,256]{2,1,0:T(8,128)(2,1)S(1)} collective-permute-done((bf16[2,144,256]{2,1,0:T(8,128)(2,1)S(1)}, bf16[2,144,256]{2,1,0:T(8,128)(2,1)S(1)}, u32[]{:S(2)}, u32[]{:S(2)}) %collective-permute-start.10) | collective-permute-done | bytes 147488 | tf_op jit(solution)/shard_map/ppermute | solution.py:423
  62.2 0.5 collective-permute-start.12
  62.7 0.7 select.3.refs_6_.refs_1_
  63.5 1.5 %collective-permute-start.14 = (bf16[4,144,256]{2,1,0:T(8,128)(2,1)S(1)}, bf16[4,144,256]{2,1,0:T(8,128)(2,1)S(1)}, u32[]{:S(2)}, u32[]{:S(2)}) collective-permute-start(bf16[4,144,256]{2,1,0:T(8,128)(2,1)S(1)} %select.3.refs_6_.refs_1_), channel_id=1, source_target_pairs={{0,2},{1,3},{2,0},{3,1},{4,6},{5,7},{6,4},{7,5},{8,10},{9,11},{10,... | collective-permute-start | bytes 884744 | tf_op jit(solution)/shard_map/ppermute | solution.py:408
  65.0 0.5 collective-permute-done.12.refs_4_
  65.5 3.1 %first_window.1 = (f32[4,512,128]{2,1,0:T(8,128)S(1)}, f32[4,512,128]{2,1,0:T(8,128)S(1)}, f32[4,512,256]{2,1,0:T(8,128)S(1)}, f32[4,256]{1,0:T(4,128)S(1)}) custom-call(bf16[2,4,512,256]{3,2,1,0:T(8,128)(2,1)S(1)} %pad_maximum_fusion.refs_0_, bf16[2,4,512,256]{3,2,1,0:T(8,128)(2,1)S(1)} %collective-permute-done.8.refs_1_, ...), custom_call_target="tpu_custom_call" | custom-call | flops 1073741824 | bytes 8388608 | tf_op jit(solution)/shard_map/first_window/pallas_call | solution.py:258
  68.6 4.3 %collective-permute-done.14.refs_7_ = bf16[4,144,256]{2,1,0:T(8,128)(2,1)S(1)} collective-permute-done((bf16[4,144,256]{2,1,0:T(8,128)(2,1)S(1)}, bf16[4,144,256]{2,1,0:T(8,128)(2,1)S(1)}, u32[]{:S(2)}, u32[]{:S(2)}) %collective-permute-start.14) | collective-permute-done | bytes 294944 | tf_op jit(solution)/shard_map/ppermute | solution.py:408
  72.9 1.6 %collective-permute-done.16.refs_9_ = bf16[4,144,256]{2,1,0:T(8,128)(2,1)S(1)} collective-permute-done((bf16[4,144,256]{2,1,0:T(8,128)(2,1)S(1)}, bf16[4,144,256]{2,1,0:T(8,128)(2,1)S(1)}, u32[]{:S(2)}, u32[]{:S(2)}) %collective-permute-start.16) | collective-permute-done | bytes 294944 | tf_op jit(solution)/shard_map/ppermute | solution.py:408
  74.5 2.5 %last_window.1 = (bf16[4,512,256]{2,1,0:T(8,128)(2,1)S(1)}, f32[4,512,128]{2,1,0:T(8,128)S(1)}, f32[8,512]{1,0:T(8,128)S(1)}, f32[8,512]{1,0:T(8,128)S(1)}, f32[...) custom-call(s32[1]{0:T(128)} %bitcast.me_ref, s32[2,4]{1,0:T(2,128)S(1)} %bitcast.14, ...), custom_call_target="tpu_custom_call" | custom-call | flops 1073741824 | bytes 8388608 | tf_op jit(solution)/shard_map/last_window/pallas_call | solution.py:282
  77.0 8.3 %collective-permute-start.17 = (f32[8,512]{1,0:T(8,128)S(1)}, f32[8,512]{1,0:T(8,128)S(1)}, u32[]{:S(2)}, u32[]{:S(2)}) collective-permute-start(f32[8,512]{1,0:T(8,128)S(1)} %get-tuple-element.81), channel_id=1, source_target_pairs={{0,4},{4,8},{8,12},{12,0},{1,5},{5,9},{9,13},{13,1},{2,6},{6,10},{... | collective-permute-start | bytes 49160 | tf_op jit(solution)/shard_map/ppermute | solution.py:423
  85.6 2.1 %collective-permute-start.19 = (f32[8,512]{1,0:T(8,128)S(1)}, f32[8,512]{1,0:T(8,128)S(1)}, u32[]{:S(2)}, u32[]{:S(2)}) collective-permute-start(f32[8,512]{1,0:T(8,128)S(1)} %get-tuple-element.83), channel_id=1, source_target_pairs={{0,12},{4,0},{8,4},{12,8},{1,13},{5,1},{9,5},{13,9},{2,14},{6,2},{... | collective-permute-start | bytes 49160 | tf_op jit(solution)/shard_map/ppermute | solution.py:423
  87.7 2.2 %means.1 = bf16[8,512,256]{2,1,0:T(8,128)(2,1)} custom-call(s32[2,4]{1,0:T(2,128)S(1)} %bitcast.15, bf16[4,512,256]{2,1,0:T(8,128)(2,1)S(1)} %get-tuple-element.48.rows_ref, bf16[4,512,256]{2,1,0:T(8,128)(2,1)S(1)} %get-tuple-element.84.kernel_ref, f32[4,512,128]{2,1,0:T(8,128)S(1)} %get-tuple-element.85.mass_ref, ...), custom_call_target="tpu_custom_call", output_to_operand_aliasing={{}: (7, {})} | custom-call | flops 536870912 | bytes 8388608 | tf_op jit(solution)/shard_map/means/pallas_call | solution.py:361
  90.0 0.6 weights.1
  (22 shorter events, 1.0 us)
Async XLA Ops:
  0.6 9.2 %collective-permute-start.2 = (s32[2,4]{1,0:T(2,128)}, s32[2,4]{1,0:T(2,128)S(1)}, u32[]{:S(2)}, u32[]{:S(2)}) collective-permute-start(s32[2,4]{1,0:T(2,128)} %bitcast.8), channel_id=1, source_target_pairs={{0,12},{4,0},{8,4},{12,8},{1,13},{5,1},{9,5},{13,9},{2,14},{6,2},{... | collective-permute-start | bytes 104 | tf_op jit(solution)/shard_map/ppermute | solution.py:423
  5.7 4.7 %collective-permute-start.1 = (s32[2,4]{1,0:T(2,128)}, s32[2,4]{1,0:T(2,128)S(1)}, u32[]{:S(2)}, u32[]{:S(2)}) collective-permute-start(s32[2,4]{1,0:T(2,128)} %bitcast.9), channel_id=1, source_target_pairs={{0,8},{4,12},{8,0},{12,4},{1,9},{5,13},{9,1},{13,5},{2,10},{6,14},... | collective-permute-start | bytes 104 | tf_op jit(solution)/shard_map/ppermute | solution.py:423
  5.7 5.6 %collective-permute-start = (s32[2,4]{1,0:T(2,128)}, s32[2,4]{1,0:T(2,128)S(1)}, u32[]{:S(2)}, u32[]{:S(2)}) collective-permute-start(s32[2,4]{1,0:T(2,128)} %bitcast.10), channel_id=1, source_target_pairs={{0,4},{4,8},{8,12},{12,0},{1,5},{5,9},{9,13},{13,1},{2,6},{6,10},{... | collective-permute-start | bytes 104 | tf_op jit(solution)/shard_map/ppermute | solution.py:423
  6.7 0.7 copy-start
  11.3 23.5 %collective-permute-start.3 = (bf16[4,512,256]{2,1,0:T(8,128)(2,1)S(1)}, bf16[4,512,256]{2,1,0:T(8,128)(2,1)S(1)}, u32[]{:S(2)}, u32[]{:S(2)}) collective-permute-start(bf16[4,512,256]{2,1,0:T(8,128)(2,1)S(1)} %get-tuple-element.48.rows_ref), channel_id=1, source_target_pairs={{0,2},{1,3},{2,0},{3,1},{4,6},{5,7},{6,4},{7,5},{8,10},{9,11},{10,... | collective-permute-start | bytes 3145736 | tf_op jit(solution)/shard_map/ppermute | solution.py:408
  15.0 20.0 %collective-permute-start.4 = (bf16[2,368,256]{2,1,0:T(8,128)(2,1)S(1)}, bf16[2,368,256]{2,1,0:T(8,128)(2,1)S(1)}, u32[]{:S(2)}, u32[]{:S(2)}) collective-permute-start(bf16[2,368,256]{2,1,0:T(8,128)(2,1)S(1)} %get-tuple-element.52), channel_id=1, source_target_pairs={{0,4},{4,8},{8,12},{12,0},{1,5},{5,9},{9,13},{13,1},{2,6},{6,10},{... | collective-permute-start | bytes 1130504 | tf_op jit(solution)/shard_map/ppermute | solution.py:423
  15.9 26.0 %collective-permute-start.5 = (bf16[2,368,256]{2,1,0:T(8,128)(2,1)S(1)}, bf16[2,368,256]{2,1,0:T(8,128)(2,1)S(1)}, u32[]{:S(2)}, u32[]{:S(2)}) collective-permute-start(bf16[2,368,256]{2,1,0:T(8,128)(2,1)S(1)} %get-tuple-element.53), channel_id=1, source_target_pairs={{0,8},{4,12},{8,0},{12,4},{1,9},{5,13},{9,1},{13,5},{2,10},{6,14},... | collective-permute-start | bytes 1130504 | tf_op jit(solution)/shard_map/ppermute | solution.py:423
  17.2 24.7 %collective-permute-start.6 = (bf16[2,368,256]{2,1,0:T(8,128)(2,1)S(1)}, bf16[2,368,256]{2,1,0:T(8,128)(2,1)S(1)}, u32[]{:S(2)}, u32[]{:S(2)}) collective-permute-start(bf16[2,368,256]{2,1,0:T(8,128)(2,1)S(1)} %get-tuple-element.54), channel_id=1, source_target_pairs={{0,12},{4,0},{8,4},{12,8},{1,13},{5,1},{9,5},{13,9},{2,14},{6,2},{... | collective-permute-start | bytes 1130504 | tf_op jit(solution)/shard_map/ppermute | solution.py:423
  34.8 7.1 %copy-start.1 = (s32[4,2]{0,1:T(2,128)S(1)}, s32[4,2]{0,1:T(2,128)}, u32[]{:S(2)}) copy-start(s32[4,2]{0,1:T(2,128)} %param.3) | copy-start | bytes 100
  41.9 20.2 %collective-permute-start.8 = (bf16[2,4,512,256]{3,2,1,0:T(8,128)(2,1)S(1)}, bf16[2,4,512,256]{3,2,1,0:T(8,128)(2,1)S(1)}, u32[]{:S(2)}, u32[]{:S(2)}) collective-permute-start(bf16[2,4,512,256]{3,2,1,0:T(8,128)(2,1)S(1)} %pad_maximum_fusion.refs_0_), channel_id=1, source_target_pairs={{0,1},{1,0},{2,3},{3,2},{4,5},{5,4},{6,7},{7,6},{8,9},{9,8},{10,11... | collective-permute-start | bytes 6291464 | tf_op jit(solution)/shard_map/ppermute | solution.py:408
  42.6 19.5 %collective-permute-start.7 = (bf16[4,368,256]{2,1,0:T(8,128)(2,1)S(1)}, bf16[4,368,256]{2,1,0:T(8,128)(2,1)S(1)}, u32[]{:S(2)}, u32[]{:S(2)}) collective-permute-start(bf16[4,368,256]{2,1,0:T(8,128)(2,1)S(1)} %select.2.refs_2_.refs_0_), channel_id=1, source_target_pairs={{0,2},{1,3},{2,0},{3,1},{4,6},{5,7},{6,4},{7,5},{8,10},{9,11},{10,... | collective-permute-start | bytes 2261000 | tf_op jit(solution)/shard_map/ppermute | solution.py:408
  43.2 13.0 %collective-permute-start.9 = (bf16[2,144,256]{2,1,0:T(8,128)(2,1)S(1)}, bf16[2,144,256]{2,1,0:T(8,128)(2,1)S(1)}, u32[]{:S(2)}, u32[]{:S(2)}) collective-permute-start(bf16[2,144,256]{2,1,0:T(8,128)(2,1)S(1)} %get-tuple-element.59), channel_id=1, source_target_pairs={{0,4},{4,8},{8,12},{12,0},{1,5},{5,9},{9,13},{13,1},{2,6},{6,10},{... | collective-permute-start | bytes 442376 | tf_op jit(solution)/shard_map/ppermute | solution.py:423
  51.8 10.4 %collective-permute-start.10 = (bf16[2,144,256]{2,1,0:T(8,128)(2,1)S(1)}, bf16[2,144,256]{2,1,0:T(8,128)(2,1)S(1)}, u32[]{:S(2)}, u32[]{:S(2)}) collective-permute-start(bf16[2,144,256]{2,1,0:T(8,128)(2,1)S(1)} %get-tuple-element.60), channel_id=1, source_target_pairs={{0,8},{4,12},{8,0},{12,4},{1,9},{5,13},{9,1},{13,5},{2,10},{6,14},... | collective-permute-start | bytes 442376 | tf_op jit(solution)/shard_map/ppermute | solution.py:423
  52.0 10.1 %collective-permute-start.11 = (bf16[2,144,256]{2,1,0:T(8,128)(2,1)S(1)}, bf16[2,144,256]{2,1,0:T(8,128)(2,1)S(1)}, u32[]{:S(2)}, u32[]{:S(2)}) collective-permute-start(bf16[2,144,256]{2,1,0:T(8,128)(2,1)S(1)} %get-tuple-element.61), channel_id=1, source_target_pairs={{0,12},{4,0},{8,4},{12,8},{1,13},{5,1},{9,5},{13,9},{2,14},{6,2},{... | collective-permute-start | bytes 442376 | tf_op jit(solution)/shard_map/ppermute | solution.py:423
  62.1 2.9 %collective-permute-start.13 = (bf16[4,368,256]{2,1,0:T(8,128)(2,1)S(1)}, bf16[4,368,256]{2,1,0:T(8,128)(2,1)S(1)}, u32[]{:S(2)}, u32[]{:S(2)}) collective-permute-start(bf16[4,368,256]{2,1,0:T(8,128)(2,1)S(1)} %collective-permute-done.7.refs_3_), channel_id=1, source_target_pairs={{0,1},{1,0},{2,3},{3,2},{4,5},{5,4},{6,7},{7,6},{8,9},{9,8},{10,11... | collective-permute-start | bytes 2261000 | tf_op jit(solution)/shard_map/ppermute | solution.py:408
  62.2 3.3 %collective-permute-start.12 = (bf16[4,368,256]{2,1,0:T(8,128)(2,1)S(1)}, bf16[4,368,256]{2,1,0:T(8,128)(2,1)S(1)}, u32[]{:S(2)}, u32[]{:S(2)}) collective-permute-start(bf16[4,368,256]{2,1,0:T(8,128)(2,1)S(1)} %select.2.refs_2_.refs_0_), channel_id=1, source_target_pairs={{0,1},{1,0},{2,3},{3,2},{4,5},{5,4},{6,7},{7,6},{8,9},{9,8},{10,11... | collective-permute-start | bytes 2261000 | tf_op jit(solution)/shard_map/ppermute | solution.py:408
  63.4 5.2 %collective-permute-start.15 = (bf16[4,144,256]{2,1,0:T(8,128)(2,1)S(1)}, bf16[4,144,256]{2,1,0:T(8,128)(2,1)S(1)}, u32[]{:S(2)}, u32[]{:S(2)}) collective-permute-start(bf16[4,144,256]{2,1,0:T(8,128)(2,1)S(1)} %select.3.refs_6_.refs_1_), channel_id=1, source_target_pairs={{0,1},{1,0},{2,3},{3,2},{4,5},{5,4},{6,7},{7,6},{8,9},{9,8},{10,11... | collective-permute-start | bytes 884744 | tf_op jit(solution)/shard_map/ppermute | solution.py:408
  63.5 9.4 %collective-permute-start.14 = (bf16[4,144,256]{2,1,0:T(8,128)(2,1)S(1)}, bf16[4,144,256]{2,1,0:T(8,128)(2,1)S(1)}, u32[]{:S(2)}, u32[]{:S(2)}) collective-permute-start(bf16[4,144,256]{2,1,0:T(8,128)(2,1)S(1)} %select.3.refs_6_.refs_1_), channel_id=1, source_target_pairs={{0,2},{1,3},{2,0},{3,1},{4,6},{5,7},{6,4},{7,5},{8,10},{9,11},{10,... | collective-permute-start | bytes 884744 | tf_op jit(solution)/shard_map/ppermute | solution.py:408
  72.9 1.6 %collective-permute-start.16 = (bf16[4,144,256]{2,1,0:T(8,128)(2,1)S(1)}, bf16[4,144,256]{2,1,0:T(8,128)(2,1)S(1)}, u32[]{:S(2)}, u32[]{:S(2)}) collective-permute-start(bf16[4,144,256]{2,1,0:T(8,128)(2,1)S(1)} %collective-permute-done.14.refs_7_), channel_id=1, source_target_pairs={{0,1},{1,0},{2,3},{3,2},{4,5},{5,4},{6,7},{7,6},{8,9},{9,8},{10,11... | collective-permute-start | bytes 884744 | tf_op jit(solution)/shard_map/ppermute | solution.py:408
  77.0 13.0 %collective-permute-start.17 = (f32[8,512]{1,0:T(8,128)S(1)}, f32[8,512]{1,0:T(8,128)S(1)}, u32[]{:S(2)}, u32[]{:S(2)}) collective-permute-start(f32[8,512]{1,0:T(8,128)S(1)} %get-tuple-element.81), channel_id=1, source_target_pairs={{0,4},{4,8},{8,12},{12,0},{1,5},{5,9},{9,13},{13,1},{2,6},{6,10},{... | collective-permute-start | bytes 49160 | tf_op jit(solution)/shard_map/ppermute | solution.py:423
  85.3 4.7 %collective-permute-start.18 = (f32[8,512]{1,0:T(8,128)S(1)}, f32[8,512]{1,0:T(8,128)S(1)}, u32[]{:S(2)}, u32[]{:S(2)}) collective-permute-start(f32[8,512]{1,0:T(8,128)S(1)} %get-tuple-element.82), channel_id=1, source_target_pairs={{0,8},{4,12},{8,0},{12,4},{1,9},{5,13},{9,1},{13,5},{2,10},{6,14},... | collective-permute-start | bytes 49160 | tf_op jit(solution)/shard_map/ppermute | solution.py:423
  85.6 4.4 %collective-permute-start.19 = (f32[8,512]{1,0:T(8,128)S(1)}, f32[8,512]{1,0:T(8,128)S(1)}, u32[]{:S(2)}, u32[]{:S(2)}) collective-permute-start(f32[8,512]{1,0:T(8,128)S(1)} %get-tuple-element.83), channel_id=1, source_target_pairs={{0,12},{4,0},{8,4},{12,8},{1,13},{5,1},{9,5},{13,9},{2,14},{6,2},{... | collective-permute-start | bytes 49160 | tf_op jit(solution)/shard_map/ppermute | solution.py:423

commit v9 on v8

--- a/solution.py
+++ b/solution.py
@@ -11,7 +11,8 @@
 BR = 512
 BLK_DEV = 8
 LANES = 128
-CHUNKS = ((0, 368), (368, 144))
+CHUNKS = ((0, 336), (336, 176))
+PIECES = (2, 1)
 WINDOWS = ((0, 256), (256, 512))
 
 
@@ -113,10 +114,11 @@
     )(pairs, in_hbm(blocks))
 
 
-def select_kernel(start, me_ref, pairs_ref, own_ref, *refs):
-    received, out_ref = refs[:-1], refs[-1]
-    wide_count = len(received) + 1
-    pair_count, size, _ = out_ref.shape
+def select_kernel(wide_count, start, me_ref, pairs_ref, own_ref, *refs):
+    pair_count = own_ref.shape[0]
+    outs = refs[wide_count - 1 :]
+    received = refs[: wide_count - 1]
+    each, size, _ = outs[0].shape
     owners = [pairs_ref[1, pair] >> 3 for pair in range(pair_count)]
     for pair in range(pair_count):
         shift = me_ref[0] - owners[pair]
@@ -125,24 +127,26 @@
         for before in range(pair):
             rank = rank + (owners[before] == owners[pair]).astype(jnp.int32)
 
+        out = outs[pair // each].at[pair % each]
+
         @pl.when(shift == 0)
         def _():
-            out_ref[pair] = own_ref[pair, start : start + size]
+            out[...] = own_ref[pair, start : start + size]
 
         for other in range(1, wide_count):
 
             @pl.when(shift == other)
             def _():
-                out_ref[pair] = received[other - 1][rank]
-
-
-def select(me, pairs, own, received, start, size):
+                out[...] = received[other - 1][rank]
+
+
+def select(me, pairs, own, received, start, size, pieces):
     pair_count, _, feat = own.shape
     return pl.pallas_call(
-        functools.partial(select_kernel, start),
-        out_shape=pltpu.VMEM((pair_count, size, feat), own.dtype),
+        functools.partial(select_kernel, len(received) + 1, start),
+        out_shape=[pltpu.VMEM((pair_count // pieces, size, feat), own.dtype)] * pieces,
         in_specs=[smem(), smem()] + [vmem()] * (1 + len(received)),
-        out_specs=vmem(),
+        out_specs=[vmem()] * pieces,
         compiler_params=params(4),
         name="select",
     )(me, pairs, *[in_vmem(x) for x in (own, *received)])
@@ -189,26 +193,41 @@
     return kernel.astype(jnp.bfloat16), jnp.sum(kernel, axis=0, keepdims=True), mass
 
 
-def window_parts(window, refs, pair):
-    held = segments(window)
-    half_count = refs[0].shape[0]
-    narrow_count = 2 * half_count
-    rows = [ref[i, pair] for ref in refs[:2] for i in range(half_count)]
-    chunks = [refs[2 + i * narrow_count :][:narrow_count] for i in range(len(held))]
-    cols = [own_columns(window, [chunk[i] for chunk in chunks], pair) for i in range(narrow_count)]
-    return rows, cols
+def take_parts(refs, narrow_count, pieces):
+    parts = [refs[i * pieces : (i + 1) * pieces] for i in range(narrow_count)]
+    return parts, refs[narrow_count * pieces :]
+
+
+def of_pair(part, pair):
+    each = part[0].shape[0]
+    return part[pair // each].at[pair % each]
+
+
+def window_parts(window, narrow_count, refs):
+    rows, refs = take_parts(refs, narrow_count, 1)
+    chunks = []
+    for chunk, _, _ in segments(window):
+        cols, refs = take_parts(refs, narrow_count, PIECES[chunk])
+        chunks.append(cols)
+    return rows, chunks
 
 
 def own_columns(window, chunks, pair):
     held = segments(window)
-    pieces = [ref[pair, at : at + size] for ref, (_, at, size) in zip(chunks, held)]
+    pieces = [of_pair(part, pair)[at : at + size] for part, (_, at, size) in zip(chunks, held)]
     return jnp.concatenate(pieces, axis=0) if len(pieces) > 1 else pieces[0]
 
 
-def first_kernel(window, *refs):
+def pair_parts(window, rows, chunks, pair):
+    cols = [own_columns(window, [c[i] for c in chunks], pair) for i in range(len(rows))]
+    return [of_pair(part, pair)[...] for part in rows], cols
+
+
+def first_kernel(window, narrow_count, *refs):
     square_ref, mass_ref, total_ref, sums_ref = refs[-4:]
+    all_rows, chunks = window_parts(window, narrow_count, refs)
     for pair in range(square_ref.shape[0]):
-        rows, cols = window_parts(window, refs, pair)
+        rows, cols = pair_parts(window, all_rows, chunks, pair)
         square = jnp.sum(tree([lane_sum(row) for row in rows]), axis=1, keepdims=True)
         square = jnp.broadcast_to(square, (BR, LANES))
         kernel, sums, mass = scores(rows, cols, square)
@@ -218,14 +237,15 @@
         total_ref[pair] = jnp.dot(kernel, cols[0], preferred_element_type=jnp.float32)
 
 
-def last_kernel(window, wide_count, me_ref, pairs_ref, *refs):
+def last_kernel(window, narrow_count, wide_count, me_ref, pairs_ref, *refs):
     square_in, mass_in, sums_in = refs[-6 - wide_count : -3 - wide_count]
     kernel_ref, mass_ref, row_ref = refs[-3 - wide_count : -wide_count]
     shares = refs[-wide_count:]
     for ref in (row_ref, *shares):
         ref[...] = jnp.zeros_like(ref)
+    all_rows, chunks = window_parts(window, narrow_count, refs)
     for pair in range(square_in.shape[0]):
-        rows, cols = window_parts(window, refs, pair)
+        rows, cols = pair_parts(window, all_rows, chunks, pair)
         kernel, sums, mass = scores(rows, cols, square_in[pair])
         kernel_ref[pair] = kernel
         sums = jnp.concatenate([sums_in[pair : pair + 1], sums], axis=1)
@@ -247,27 +267,31 @@
     )
 
 
+def operands(parts):
+    return [piece for part in parts for piece in part]
+
+
 def first_window(rows, cols):
-    _, pair_count, _, feat = rows[0].shape
+    pair_count, _, feat = rows[0][0].shape
     window = WINDOWS[0]
     lanes = pltpu.VMEM((pair_count, BR, LANES), jnp.float32)
     total = pltpu.VMEM((pair_count, BR, feat), jnp.float32)
-    args = list(rows)
+    args = operands(rows)
     for chunk, _, _ in segments(window):
-        args += cols[chunk]
+        args += operands(cols[chunk])
     return pl.pallas_call(
-        functools.partial(first_kernel, window),
+        functools.partial(first_kernel, window, len(rows)),
         out_shape=[lanes, lanes, total, pltpu.VMEM((pair_count, window[1]), jnp.float32)],
         in_specs=[vmem()] * len(args),
         out_specs=[vmem()] * 4,
         compiler_params=params(16),
-        cost_estimate=estimate(pair_count, window[1]),
+        cost_estimate=pl.CostEstimate(flops=0, transcendentals=0, bytes_accessed=0),
         name="first_window",
     )(*[in_vmem(x) for x in args])
 
 
 def last_window(me, pairs, rows, cols, square, mass, sums, wide_count):
-    pair_count = rows[0].shape[1]
+    pair_count = rows[0][0].shape[0]
     window = WINDOWS[1]
     size = window[1] - window[0]
     by_block = pltpu.VMEM((BLK_DEV, BR), jnp.float32)
@@ -275,12 +299,12 @@
         pltpu.VMEM((pair_count, BR, size), jnp.bfloat16),
         pltpu.VMEM((pair_count, BR, LANES), jnp.float32),
     ] + [by_block] * (1 + wide_count)
-    args = list(rows)
+    args = operands(rows)
     for chunk, _, _ in segments(window):
-        args += cols[chunk]
+        args += operands(cols[chunk])
     args += [square, mass, sums]
     kernel, mass, row_sums, *shares = pl.pallas_call(
-        functools.partial(last_kernel, window, wide_count),
+        functools.partial(last_kernel, window, len(rows), wide_count),
         out_shape=shapes,
         in_specs=[smem(), smem()] + [vmem()] * len(args),
         out_specs=[vmem()] * len(shapes),
@@ -309,7 +333,11 @@
 
 
 def mean_kernel(window, local_ref, rows_ref, kernel_ref, mass_ref, total_ref, *refs):
-    *chunks, _, out_ref, part, weight, total, mass, made, sems = refs
+    *refs, _, out_ref, part, weight, total, mass, made, sems = refs
+    chunks = []
+    for chunk, _, _ in segments(window):
+        (own,), refs = take_parts(refs, 1, PIECES[chunk])
+        chunks.append(own)
     pair_count, _, feat = rows_ref.shape
     local = [local_ref[0, pair] & 7 for pair in range(pair_count)]
 
@@ -356,7 +384,7 @@
 def means(pairs, rows, kernel, mass, total, cols, kept):
     pair_count, _, feat = rows.shape
     window = WINDOWS[1]
-    own = [cols[chunk][0] for chunk, _, _ in segments(window)]
+    own = operands(cols[chunk][0] for chunk, _, _ in segments(window))
     args = [in_vmem(x) for x in (rows, kernel, mass, total, *own)]
     return pl.pallas_call(
         functools.partial(mean_kernel, window),
@@ -405,7 +433,8 @@
 
 def hop(parts, step):
     count = lax.axis_size("narrow")
-    return [lax.ppermute(part, "narrow", [(i, i ^ step) for i in range(count)]) for part in parts]
+    perm = [(i, i ^ step) for i in range(count)]
+    return [[lax.ppermute(piece, "narrow", perm) for piece in part] for part in parts]
 
 
 def first_hops(part):
@@ -439,18 +468,19 @@
     outgoing = pack(me, lists, blocks, capacity)
 
     def pick(received, chunk):
-        return select(me, pairs, own, received, *CHUNKS[chunk])
-
-    rows = jnp.stack(first_hops(row_slices))
-    rows, received, kept = fixed((rows, to_wide(outgoing[0]), keep(blocks)))
+        return select(me, pairs, own, received, *CHUNKS[chunk], PIECES[chunk])
+
+    rows = first_hops([row_slices])
+    rows_last = hop(rows[:1], 1)
+    rows, rows_last, received, kept = fixed((rows, rows_last, to_wide(outgoing[0]), keep(blocks)))
     cols_a = first_hops(pick(received, 0))
-    rows = [rows, *hop([rows], 1)]
+    rows = rows + rows_last + hop(rows[1:], 1)
     cols_a, rows, received = fixed((cols_a, rows, to_wide(outgoing[1])))
     cols_b = first_hops(pick(received, 1))
     last_b = hop(cols_b[:1], 1)
     cols_a = cols_a + hop(cols_a, 1)
     carry = first_window(rows, [cols_a])
-    cols_b, last_b, carry = fixed((cols_b, last_b, carry))
+    cols_b, carry = fixed((cols_b, carry))
     cols_b = cols_b + last_b + hop(cols_b[1:], 1)
     square, mass, total, sums = carry
     kernel, mass, row_sums, shares = last_window(

time: 91 us -> 89.8 us (0.987)
  starting transfers between devices: 36.2 us -> 30.1 us
  waiting for transfers between devices: 32.8 us -> 37.2 us
  local copies, waits for them, and re-layouts: 0.72 us -> 1.69 us
    ppermute x12, waiting for transfers between devices: 16.4 us -> 27.7 us  [to_wide(): lax.ppermute(piece, 'wide', [(i, (i + shift) % count) for i in range(coun...]
    ppermute x12, starting transfers between devices: 31.9 us -> 24.7 us  [to_wide(): lax.ppermute(piece, 'wide', [(i, (i + shift) % count) for i in range(coun...]
    ppermute x8 -> x12, waiting for transfers between devices: 16.4 us -> 9.46 us  [hop(): lax.ppermute(piece, 'narrow', perm)]
    ppermute x8 -> x12, starting transfers between devices: 4.3 us -> 5.42 us  [hop(): lax.ppermute(piece, 'narrow', perm)]
    unnamed x4 -> x8, local copies, waits for them, and re-layouts: 0.72 us -> 1.69 us
  transfers between devices with their start and end apart: 20 -> 24, of which waited for: 9 -> 13; matrix products, arithmetic and copies ran while one was open for 0% -> 0% of each run, Pallas kernels for 19% -> 18%
where the time goes in v9:
time: 89.8 us; the launch traced here: 89.5 us
  waiting for transfers between devices  37.2 us (41%)
  starting transfers between devices  30.1 us (34%)
  Pallas kernels  19.7 us (22%)
  local copies, waits for them, and re-layouts  1.69 us (2%)
    ppermute x12, waiting for transfers between devices, to_wide(): lax.ppermute(piece, 'wide', [(i, (i + shift) % count) for i in range(coun...  27.7 us
    ppermute x12, starting transfers between devices, to_wide(): lax.ppermute(piece, 'wide', [(i, (i + shift) % count) for i in range(coun...  24.7 us
    ppermute x12, waiting for transfers between devices, hop(): lax.ppermute(piece, 'narrow', perm)  9.46 us
    pallas_call x1, Pallas kernels, keep(): pl.pallas_call(keep_kernel, out_shape=pltpu.HBM(blocks.shape, blocks.dtyp...  5.63 us
    ppermute x12, starting transfers between devices, hop(): lax.ppermute(piece, 'narrow', perm)  5.42 us
    pallas_call x1, Pallas kernels, first_window(): pl.pallas_call(functools.partial(first_kernel, window, len(rows)), out_sh...  3.11 us
    pallas_call x1, Pallas kernels, last_window(): pl.pallas_call(functools.partial(last_kernel, window, len(rows), wide_cou...  2.5 us
    pallas_call x1, Pallas kernels, means(): pl.pallas_call(functools.partial(mean_kernel, window), out_shape=pltpu.HB...  2.24 us
  transfers between devices with their start and end apart: 24, of which 13 were waited for; matrix products, arithmetic and copies ran while one was open for 0% of the time, Pallas kernels for 18%

profile of v9, /device:TPU:0, one launch (start us, length us, event | category | flops | bytes accessed | tf_op | source)
XLA Modules:
  0.0 89.5 jit_solution(16905284434630651360)
XLA Ops:
  0.6 5.1 %collective-permute-start.2 = (s32[2,4]{1,0:T(2,128)}, s32[2,4]{1,0:T(2,128)S(1)}, u32[]{:S(2)}, u32[]{:S(2)}) collective-permute-start(s32[2,4]{1,0:T(2,128)} %bitcast.5), channel_id=1, source_target_pairs={{0,12},{4,0},{8,4},{12,8},{1,13},{5,1},{9,5},{13,9},{2,14},{6,2},{... | collective-permute-start | bytes 104 | tf_op jit(solution)/shard_map/ppermute | solution.py:452
  5.7 1.0 %collective-permute-start = (s32[2,4]{1,0:T(2,128)}, s32[2,4]{1,0:T(2,128)S(1)}, u32[]{:S(2)}, u32[]{:S(2)}) collective-permute-start(s32[2,4]{1,0:T(2,128)} %bitcast.7), channel_id=1, source_target_pairs={{0,4},{4,8},{8,12},{12,0},{1,5},{5,9},{9,13},{13,1},{2,6},{6,10},{... | collective-permute-start | bytes 104 | tf_op jit(solution)/shard_map/ppermute | solution.py:452
  6.7 0.7 copy-done.2
  7.5 2.1 %take.1 = (bf16[4,512,256]{2,1,0:T(8,128)(2,1)S(1)}, bf16[4,512,256]{2,1,0:T(8,128)(2,1)S(1)}) custom-call(s32[2,4]{1,0:T(2,128)S(1)} %bitcast.8, bf16[8,512,256]{2,1,0:T(8,128)(2,1)} %bitcast.13), custom_call_target="tpu_custom_call" | custom-call | tf_op jit(solution)/shard_map/take/pallas_call | solution.py:106
  9.6 1.0 %copy-done = bf16[4,512,256]{2,1,0:T(8,128)(2,1)} copy-done((bf16[4,512,256]{2,1,0:T(8,128)(2,1)}, bf16[4,512,256]{2,1,0:T(8,128)(2,1)S(1)}, u32[]{:S(2)}) %copy-start) | copy-done | bytes 1048600
  10.6 0.7 collective-permute-done.refs_0_
  11.3 1.5 %collective-permute-start.3 = (bf16[4,512,256]{2,1,0:T(8,128)(2,1)S(1)}, bf16[4,512,256]{2,1,0:T(8,128)(2,1)S(1)}, u32[]{:S(2)}, u32[]{:S(2)}) collective-permute-start(bf16[4,512,256]{2,1,0:T(8,128)(2,1)S(1)} %get-tuple-element.73.refs_0_.rows_ref), channel_id=1, source_target_pairs={{0,2},{1,3},{2,0},{3,1},{4,6},{5,7},{6,4},{7,5},{8,10},{9,11},{10,... | collective-permute-start | bytes 3145736 | tf_op jit(solution)/shard_map/ppermute | solution.py:437
  12.8 2.2 %pack.1 = (bf16[2,336,256]{2,1,0:T(8,128)(2,1)S(1)}, bf16[2,336,256]{2,1,0:T(8,128)(2,1)S(1)}, bf16[2,336,256]{2,1,0:T(8,128)(2,1)S(1)}, bf16[2,176,256]{2,1,0:T...) custom-call(s32[1]{0:T(128)} %bitcast.me_ref, ...), custom_call_target="tpu_custom_call" | custom-call | tf_op jit(solution)/shard_map/pack/pallas_call | solution.py:79
  15.0 1.9 %collective-permute-start.5 = (bf16[2,336,256]{2,1,0:T(8,128)(2,1)S(1)}, bf16[2,336,256]{2,1,0:T(8,128)(2,1)S(1)}, u32[]{:S(2)}, u32[]{:S(2)}) collective-permute-start(bf16[2,336,256]{2,1,0:T(8,128)(2,1)S(1)} %get-tuple-element.59), channel_id=1, source_target_pairs={{0,4},{4,8},{8,12},{12,0},{1,5},{5,9},{9,13},{13,1},{2,6},{6,10},{... | collective-permute-start | bytes 1032200 | tf_op jit(solution)/shard_map/ppermute | solution.py:452
  16.9 1.1 %collective-permute-start.6 = (bf16[2,336,256]{2,1,0:T(8,128)(2,1)S(1)}, bf16[2,336,256]{2,1,0:T(8,128)(2,1)S(1)}, u32[]{:S(2)}, u32[]{:S(2)}) collective-permute-start(bf16[2,336,256]{2,1,0:T(8,128)(2,1)S(1)} %get-tuple-element.60), channel_id=1, source_target_pairs={{0,8},{4,12},{8,0},{12,4},{1,9},{5,13},{9,1},{13,5},{2,10},{6,14},... | collective-permute-start | bytes 1032200 | tf_op jit(solution)/shard_map/ppermute | solution.py:452
  18.1 1.4 %collective-permute-start.7 = (bf16[2,336,256]{2,1,0:T(8,128)(2,1)S(1)}, bf16[2,336,256]{2,1,0:T(8,128)(2,1)S(1)}, u32[]{:S(2)}, u32[]{:S(2)}) collective-permute-start(bf16[2,336,256]{2,1,0:T(8,128)(2,1)S(1)} %get-tuple-element.61), channel_id=1, source_target_pairs={{0,12},{4,0},{8,4},{12,8},{1,13},{5,1},{9,5},{13,9},{2,14},{6,2},{... | collective-permute-start | bytes 1032200 | tf_op jit(solution)/shard_map/ppermute | solution.py:452
  19.4 5.6 %keep.1.refs_3_ = bf16[8,512,256]{2,1,0:T(8,128)(2,1)} custom-call(bf16[8,512,256]{2,1,0:T(8,128)(2,1)} %bitcast.15), custom_call_target="tpu_custom_call" | custom-call | tf_op jit(solution)/shard_map/keep/pallas_call | solution.py:324
  25.1 2.8 %collective-permute-done.5.refs_0_ = bf16[2,336,256]{2,1,0:T(8,128)(2,1)S(1)} collective-permute-done((bf16[2,336,256]{2,1,0:T(8,128)(2,1)S(1)}, bf16[2,336,256]{2,1,0:T(8,128)(2,1)S(1)}, u32[]{:S(2)}, u32[]{:S(2)}) %collective-permute-start.5) | collective-permute-done | bytes 344096 | tf_op jit(solution)/shard_map/ppermute | solution.py:452
  27.9 14.0 %collective-permute-done.6.refs_1_ = bf16[2,336,256]{2,1,0:T(8,128)(2,1)S(1)} collective-permute-done((bf16[2,336,256]{2,1,0:T(8,128)(2,1)S(1)}, bf16[2,336,256]{2,1,0:T(8,128)(2,1)S(1)}, u32[]{:S(2)}, u32[]{:S(2)}) %collective-permute-start.6) | collective-permute-done | bytes 344096 | tf_op jit(solution)/shard_map/ppermute | solution.py:452
  42.0 7.8 %collective-permute-start.11 = (bf16[2,176,256]{2,1,0:T(8,128)(2,1)S(1)}, bf16[2,176,256]{2,1,0:T(8,128)(2,1)S(1)}, u32[]{:S(2)}, u32[]{:S(2)}) collective-permute-start(bf16[2,176,256]{2,1,0:T(8,128)(2,1)S(1)} %get-tuple-element.70), channel_id=1, source_target_pairs={{0,4},{4,8},{8,12},{12,0},{1,5},{5,9},{9,13},{13,1},{2,6},{6,10},{... | collective-permute-start | bytes 540680 | tf_op jit(solution)/shard_map/ppermute | solution.py:452
  49.8 0.7 select.2
  51.1 1.5 %collective-permute-start.9 = (bf16[2,336,256]{2,1,0:T(8,128)(2,1)S(1)}, bf16[2,336,256]{2,1,0:T(8,128)(2,1)S(1)}, u32[]{:S(2)}, u32[]{:S(2)}) collective-permute-start(bf16[2,336,256]{2,1,0:T(8,128)(2,1)S(1)} %get-tuple-element.78.refs_5_.refs_1_), channel_id=1, source_target_pairs={{0,2},{1,3},{2,0},{3,1},{4,6},{5,7},{6,4},{7,5},{8,10},{9,11},{10,... | collective-permute-start | bytes 1032200 | tf_op jit(solution)/shard_map/ppermute | solution.py:437
  52.6 0.7 collective-permute-start.12
  53.3 1.8 %collective-permute-done.11.refs_0_ = bf16[2,176,256]{2,1,0:T(8,128)(2,1)S(1)} collective-permute-done((bf16[2,176,256]{2,1,0:T(8,128)(2,1)S(1)}, bf16[2,176,256]{2,1,0:T(8,128)(2,1)S(1)}, u32[]{:S(2)}, u32[]{:S(2)}) %collective-permute-start.11) | collective-permute-done | bytes 180256 | tf_op jit(solution)/shard_map/ppermute | solution.py:452
  55.1 1.7 %collective-permute-start.13 = (bf16[2,176,256]{2,1,0:T(8,128)(2,1)S(1)}, bf16[2,176,256]{2,1,0:T(8,128)(2,1)S(1)}, u32[]{:S(2)}, u32[]{:S(2)}) collective-permute-start(bf16[2,176,256]{2,1,0:T(8,128)(2,1)S(1)} %get-tuple-element.72), channel_id=1, source_target_pairs={{0,12},{4,0},{8,4},{12,8},{1,13},{5,1},{9,5},{13,9},{2,14},{6,2},{... | collective-permute-start | bytes 540680 | tf_op jit(solution)/shard_map/ppermute | solution.py:452
  56.8 6.5 %collective-permute-done.12.refs_1_ = bf16[2,176,256]{2,1,0:T(8,128)(2,1)S(1)} collective-permute-done((bf16[2,176,256]{2,1,0:T(8,128)(2,1)S(1)}, bf16[2,176,256]{2,1,0:T(8,128)(2,1)S(1)}, u32[]{:S(2)}, u32[]{:S(2)}) %collective-permute-start.12) | collective-permute-done | bytes 180256 | tf_op jit(solution)/shard_map/ppermute | solution.py:452
  63.3 1.9 %collective-permute-done.13.refs_2_ = bf16[2,176,256]{2,1,0:T(8,128)(2,1)S(1)} collective-permute-done((bf16[2,176,256]{2,1,0:T(8,128)(2,1)S(1)}, bf16[2,176,256]{2,1,0:T(8,128)(2,1)S(1)}, u32[]{:S(2)}, u32[]{:S(2)}) %collective-permute-start.13) | collective-permute-done | bytes 180256 | tf_op jit(solution)/shard_map/ppermute | solution.py:452
  65.2 2.9 %collective-permute-done.9.refs_7_ = bf16[2,336,256]{2,1,0:T(8,128)(2,1)S(1)} collective-permute-done((bf16[2,336,256]{2,1,0:T(8,128)(2,1)S(1)}, bf16[2,336,256]{2,1,0:T(8,128)(2,1)S(1)}, u32[]{:S(2)}, u32[]{:S(2)}) %collective-permute-start.9) | collective-permute-done | bytes 344096 | tf_op jit(solution)/shard_map/ppermute | solution.py:437
  68.1 0.7 select.3.refs_12_.refs_2_
  72.5 3.1 %first_window.1 = (f32[4,512,128]{2,1,0:T(8,128)S(1)}, f32[4,512,128]{2,1,0:T(8,128)S(1)}, f32[4,512,256]{2,1,0:T(8,128)S(1)}, f32[4,256]{1,0:T(4,128)S(1)}) custom-call(bf16[4,512,256]{2,1,0:T(8,128)(2,1)S(1)} %get-tuple-element.73.refs_0_.rows_ref, bf16[4,512,256]{2,1,0:T(8,128)(2,1)S(1)} %collective-permute-done.3.refs_1_, ...), custom_call_target="tpu_custom_call" | custom-call | tf_op jit(solution)/shard_map/first_window/pallas_call | solution.py:282
  75.6 2.9 %collective-permute-done.18.refs_13_ = bf16[4,176,256]{2,1,0:T(8,128)(2,1)S(1)} collective-permute-done((bf16[4,176,256]{2,1,0:T(8,128)(2,1)S(1)}, bf16[4,176,256]{2,1,0:T(8,128)(2,1)S(1)}, u32[]{:S(2)}, u32[]{:S(2)}) %collective-permute-start.18) | collective-permute-done | bytes 360480 | tf_op jit(solution)/shard_map/ppermute | solution.py:437
  78.5 1.7 %collective-permute-done.20.refs_15_ = bf16[4,176,256]{2,1,0:T(8,128)(2,1)S(1)} collective-permute-done((bf16[4,176,256]{2,1,0:T(8,128)(2,1)S(1)}, bf16[4,176,256]{2,1,0:T(8,128)(2,1)S(1)}, u32[]{:S(2)}, u32[]{:S(2)}) %collective-permute-start.20) | collective-permute-done | bytes 360480 | tf_op jit(solution)/shard_map/ppermute | solution.py:437
  80.2 2.5 %last_window.1 = (bf16[4,512,256]{2,1,0:T(8,128)(2,1)S(1)}, f32[4,512,128]{2,1,0:T(8,128)S(1)}, f32[8,512]{1,0:T(8,128)S(1)}, f32[8,512]{1,0:T(8,128)S(1)}, f32[...) custom-call(s32[1]{0:T(128)} %bitcast.me_ref, s32[2,4]{1,0:T(2,128)S(1)} %bitcast.11, ...), custom_call_target="tpu_custom_call" | custom-call | flops 1073741824 | bytes 8388608 | tf_op jit(solution)/shard_map/last_window/pallas_call | solution.py:306
  82.7 0.7 collective-permute-start.21
  83.3 1.3 %collective-permute-start.22 = (f32[8,512]{1,0:T(8,128)S(1)}, f32[8,512]{1,0:T(8,128)S(1)}, u32[]{:S(2)}, u32[]{:S(2)}) collective-permute-start(f32[8,512]{1,0:T(8,128)S(1)} %get-tuple-element.96), channel_id=1, source_target_pairs={{0,8},{4,12},{8,0},{12,4},{1,9},{5,13},{9,1},{13,5},{2,10},{6,14},... | collective-permute-start | bytes 49160 | tf_op jit(solution)/shard_map/ppermute | solution.py:452
  84.7 1.9 %collective-permute-start.23 = (f32[8,512]{1,0:T(8,128)S(1)}, f32[8,512]{1,0:T(8,128)S(1)}, u32[]{:S(2)}, u32[]{:S(2)}) collective-permute-start(f32[8,512]{1,0:T(8,128)S(1)} %get-tuple-element.97), channel_id=1, source_target_pairs={{0,12},{4,0},{8,4},{12,8},{1,13},{5,1},{9,5},{13,9},{2,14},{6,2},{... | collective-permute-start | bytes 49160 | tf_op jit(solution)/shard_map/ppermute | solution.py:452
  86.6 2.2 %means.1 = bf16[8,512,256]{2,1,0:T(8,128)(2,1)} custom-call(s32[2,4]{1,0:T(2,128)S(1)} %bitcast.12, bf16[4,512,256]{2,1,0:T(8,128)(2,1)S(1)} %get-tuple-element.73.refs_0_.rows_ref, bf16[4,512,256]{2,1,0:T(8,128)(2,1)S(1)} %get-tuple-element.98.kernel_ref, f32[4,512,128]{2,1,0:T(8,128)S(1)} %get-tuple-element.99.mass_ref, ...), custom_call_target="tpu_custom_call", output_to_operand_aliasing={{}: (8, {})} | custom-call | flops 536870912 | bytes 8388608 | tf_op jit(solution)/shard_map/means/pallas_call | solution.py:389
  (33 shorter events, 5.1 us)
Async XLA Ops:
  0.6 9.9 %collective-permute-start.2 = (s32[2,4]{1,0:T(2,128)}, s32[2,4]{1,0:T(2,128)S(1)}, u32[]{:S(2)}, u32[]{:S(2)}) collective-permute-start(s32[2,4]{1,0:T(2,128)} %bitcast.5), channel_id=1, source_target_pairs={{0,12},{4,0},{8,4},{12,8},{1,13},{5,1},{9,5},{13,9},{2,14},{6,2},{... | collective-permute-start | bytes 104 | tf_op jit(solution)/shard_map/ppermute | solution.py:452
  5.7 4.8 %collective-permute-start.1 = (s32[2,4]{1,0:T(2,128)}, s32[2,4]{1,0:T(2,128)S(1)}, u32[]{:S(2)}, u32[]{:S(2)}) collective-permute-start(s32[2,4]{1,0:T(2,128)} %bitcast.6), channel_id=1, source_target_pairs={{0,8},{4,12},{8,0},{12,4},{1,9},{5,13},{9,1},{13,5},{2,10},{6,14},... | collective-permute-start | bytes 104 | tf_op jit(solution)/shard_map/ppermute | solution.py:452
  5.7 5.6 %collective-permute-start = (s32[2,4]{1,0:T(2,128)}, s32[2,4]{1,0:T(2,128)S(1)}, u32[]{:S(2)}, u32[]{:S(2)}) collective-permute-start(s32[2,4]{1,0:T(2,128)} %bitcast.7), channel_id=1, source_target_pairs={{0,4},{4,8},{8,12},{12,0},{1,5},{5,9},{9,13},{13,1},{2,6},{6,10},{... | collective-permute-start | bytes 104 | tf_op jit(solution)/shard_map/ppermute | solution.py:452
  6.7 0.7 copy-start.2
  9.6 1.0 %copy-start = (bf16[4,512,256]{2,1,0:T(8,128)(2,1)}, bf16[4,512,256]{2,1,0:T(8,128)(2,1)S(1)}, u32[]{:S(2)}) copy-start(bf16[4,512,256]{2,1,0:T(8,128)(2,1)S(1)} %get-tuple-element.54.own_ref) | copy-start | bytes 3145732
  11.3 30.6 %collective-permute-start.4 = (bf16[4,512,256]{2,1,0:T(8,128)(2,1)S(1)}, bf16[4,512,256]{2,1,0:T(8,128)(2,1)S(1)}, u32[]{:S(2)}, u32[]{:S(2)}) collective-permute-start(bf16[4,512,256]{2,1,0:T(8,128)(2,1)S(1)} %get-tuple-element.73.refs_0_.rows_ref), channel_id=1, source_target_pairs={{0,1},{1,0},{2,3},{3,2},{4,5},{5,4},{6,7},{7,6},{8,9},{9,8},{10,11... | collective-permute-start | bytes 3145736 | tf_op jit(solution)/shard_map/ppermute | solution.py:437
  11.3 30.6 %collective-permute-start.3 = (bf16[4,512,256]{2,1,0:T(8,128)(2,1)S(1)}, bf16[4,512,256]{2,1,0:T(8,128)(2,1)S(1)}, u32[]{:S(2)}, u32[]{:S(2)}) collective-permute-start(bf16[4,512,256]{2,1,0:T(8,128)(2,1)S(1)} %get-tuple-element.73.refs_0_.rows_ref), channel_id=1, source_target_pairs={{0,2},{1,3},{2,0},{3,1},{4,6},{5,7},{6,4},{7,5},{8,10},{9,11},{10,... | collective-permute-start | bytes 3145736 | tf_op jit(solution)/shard_map/ppermute | solution.py:437
  15.0 12.9 %collective-permute-start.5 = (bf16[2,336,256]{2,1,0:T(8,128)(2,1)S(1)}, bf16[2,336,256]{2,1,0:T(8,128)(2,1)S(1)}, u32[]{:S(2)}, u32[]{:S(2)}) collective-permute-start(bf16[2,336,256]{2,1,0:T(8,128)(2,1)S(1)} %get-tuple-element.59), channel_id=1, source_target_pairs={{0,4},{4,8},{8,12},{12,0},{1,5},{5,9},{9,13},{13,1},{2,6},{6,10},{... | collective-permute-start | bytes 1032200 | tf_op jit(solution)/shard_map/ppermute | solution.py:452
  16.9 25.0 %collective-permute-start.6 = (bf16[2,336,256]{2,1,0:T(8,128)(2,1)S(1)}, bf16[2,336,256]{2,1,0:T(8,128)(2,1)S(1)}, u32[]{:S(2)}, u32[]{:S(2)}) collective-permute-start(bf16[2,336,256]{2,1,0:T(8,128)(2,1)S(1)} %get-tuple-element.60), channel_id=1, source_target_pairs={{0,8},{4,12},{8,0},{12,4},{1,9},{5,13},{9,1},{13,5},{2,10},{6,14},... | collective-permute-start | bytes 1032200 | tf_op jit(solution)/shard_map/ppermute | solution.py:452
  18.1 31.8 %copy-start.1 = (bf16[4,512,256]{2,1,0:T(8,128)(2,1)S(1)}, bf16[4,512,256]{2,1,0:T(8,128)(2,1)}, u32[]{:S(2)}) copy-start(bf16[4,512,256]{2,1,0:T(8,128)(2,1)} %copy-done) | copy-start | bytes 3145732
  18.1 31.8 %copy-start.3 = (s32[4,2]{0,1:T(2,128)S(1)}, s32[4,2]{0,1:T(2,128)}, u32[]{:S(2)}) copy-start(s32[4,2]{0,1:T(2,128)} %param.3) | copy-start | bytes 100
  18.1 23.8 %collective-permute-start.7 = (bf16[2,336,256]{2,1,0:T(8,128)(2,1)S(1)}, bf16[2,336,256]{2,1,0:T(8,128)(2,1)S(1)}, u32[]{:S(2)}, u32[]{:S(2)}) collective-permute-start(bf16[2,336,256]{2,1,0:T(8,128)(2,1)S(1)} %get-tuple-element.61), channel_id=1, source_target_pairs={{0,12},{4,0},{8,4},{12,8},{1,13},{5,1},{9,5},{13,9},{2,14},{6,2},{... | collective-permute-start | bytes 1032200 | tf_op jit(solution)/shard_map/ppermute | solution.py:452
  41.9 26.2 %collective-permute-start.10 = (bf16[4,512,256]{2,1,0:T(8,128)(2,1)S(1)}, bf16[4,512,256]{2,1,0:T(8,128)(2,1)S(1)}, u32[]{:S(2)}, u32[]{:S(2)}) collective-permute-start(bf16[4,512,256]{2,1,0:T(8,128)(2,1)S(1)} %collective-permute-done.3.refs_1_), channel_id=1, source_target_pairs={{0,1},{1,0},{2,3},{3,2},{4,5},{5,4},{6,7},{7,6},{8,9},{9,8},{10,11... | collective-permute-start | bytes 3145736 | tf_op jit(solution)/shard_map/ppermute | solution.py:437
  42.0 13.1 %collective-permute-start.11 = (bf16[2,176,256]{2,1,0:T(8,128)(2,1)S(1)}, bf16[2,176,256]{2,1,0:T(8,128)(2,1)S(1)}, u32[]{:S(2)}, u32[]{:S(2)}) collective-permute-start(bf16[2,176,256]{2,1,0:T(8,128)(2,1)S(1)} %get-tuple-element.70), channel_id=1, source_target_pairs={{0,4},{4,8},{8,12},{12,0},{1,5},{5,9},{9,13},{13,1},{2,6},{6,10},{... | collective-permute-start | bytes 540680 | tf_op jit(solution)/shard_map/ppermute | solution.py:452
  50.5 14.7 %collective-permute-start.8 = (bf16[2,336,256]{2,1,0:T(8,128)(2,1)S(1)}, bf16[2,336,256]{2,1,0:T(8,128)(2,1)S(1)}, u32[]{:S(2)}, u32[]{:S(2)}) collective-permute-start(bf16[2,336,256]{2,1,0:T(8,128)(2,1)S(1)} %get-tuple-element.77.refs_4_.refs_0_), channel_id=1, source_target_pairs={{0,2},{1,3},{2,0},{3,1},{4,6},{5,7},{6,4},{7,5},{8,10},{9,11},{10,... | collective-permute-start | bytes 1032200 | tf_op jit(solution)/shard_map/ppermute | solution.py:437
  51.1 17.0 %collective-permute-start.9 = (bf16[2,336,256]{2,1,0:T(8,128)(2,1)S(1)}, bf16[2,336,256]{2,1,0:T(8,128)(2,1)S(1)}, u32[]{:S(2)}, u32[]{:S(2)}) collective-permute-start(bf16[2,336,256]{2,1,0:T(8,128)(2,1)S(1)} %get-tuple-element.78.refs_5_.refs_1_), channel_id=1, source_target_pairs={{0,2},{1,3},{2,0},{3,1},{4,6},{5,7},{6,4},{7,5},{8,10},{9,11},{10,... | collective-permute-start | bytes 1032200 | tf_op jit(solution)/shard_map/ppermute | solution.py:437
  52.6 10.7 %collective-permute-start.12 = (bf16[2,176,256]{2,1,0:T(8,128)(2,1)S(1)}, bf16[2,176,256]{2,1,0:T(8,128)(2,1)S(1)}, u32[]{:S(2)}, u32[]{:S(2)}) collective-permute-start(bf16[2,176,256]{2,1,0:T(8,128)(2,1)S(1)} %get-tuple-element.71), channel_id=1, source_target_pairs={{0,8},{4,12},{8,0},{12,4},{1,9},{5,13},{9,1},{13,5},{2,10},{6,14},... | collective-permute-start | bytes 540680 | tf_op jit(solution)/shard_map/ppermute | solution.py:452
  55.1 10.1 %collective-permute-start.13 = (bf16[2,176,256]{2,1,0:T(8,128)(2,1)S(1)}, bf16[2,176,256]{2,1,0:T(8,128)(2,1)S(1)}, u32[]{:S(2)}, u32[]{:S(2)}) collective-permute-start(bf16[2,176,256]{2,1,0:T(8,128)(2,1)S(1)} %get-tuple-element.72), channel_id=1, source_target_pairs={{0,12},{4,0},{8,4},{12,8},{1,13},{5,1},{9,5},{13,9},{2,14},{6,2},{... | collective-permute-start | bytes 540680 | tf_op jit(solution)/shard_map/ppermute | solution.py:452
  68.8 9.7 %collective-permute-start.18 = (bf16[4,176,256]{2,1,0:T(8,128)(2,1)S(1)}, bf16[4,176,256]{2,1,0:T(8,128)(2,1)S(1)}, u32[]{:S(2)}, u32[]{:S(2)}) collective-permute-start(bf16[4,176,256]{2,1,0:T(8,128)(2,1)S(1)} %select.3.refs_12_.refs_2_), channel_id=1, source_target_pairs={{0,2},{1,3},{2,0},{3,1},{4,6},{5,7},{6,4},{7,5},{8,10},{9,11},{10,... | collective-permute-start | bytes 1081352 | tf_op jit(solution)/shard_map/ppermute | solution.py:437
  69.4 1.7 %collective-permute-start.16 = (bf16[2,336,256]{2,1,0:T(8,128)(2,1)S(1)}, bf16[2,336,256]{2,1,0:T(8,128)(2,1)S(1)}, u32[]{:S(2)}, u32[]{:S(2)}) collective-permute-start(bf16[2,336,256]{2,1,0:T(8,128)(2,1)S(1)} %collective-permute-done.8.refs_6_), channel_id=1, source_target_pairs={{0,1},{1,0},{2,3},{3,2},{4,5},{5,4},{6,7},{7,6},{8,9},{9,8},{10,11... | collective-permute-start | bytes 1032200 | tf_op jit(solution)/shard_map/ppermute | solution.py:437
  69.4 2.1 %collective-permute-start.17 = (bf16[2,336,256]{2,1,0:T(8,128)(2,1)S(1)}, bf16[2,336,256]{2,1,0:T(8,128)(2,1)S(1)}, u32[]{:S(2)}, u32[]{:S(2)}) collective-permute-start(bf16[2,336,256]{2,1,0:T(8,128)(2,1)S(1)} %collective-permute-done.9.refs_7_), channel_id=1, source_target_pairs={{0,1},{1,0},{2,3},{3,2},{4,5},{5,4},{6,7},{7,6},{8,9},{9,8},{10,11... | collective-permute-start | bytes 1032200 | tf_op jit(solution)/shard_map/ppermute | solution.py:437
  69.9 2.1 %collective-permute-start.14 = (bf16[2,336,256]{2,1,0:T(8,128)(2,1)S(1)}, bf16[2,336,256]{2,1,0:T(8,128)(2,1)S(1)}, u32[]{:S(2)}, u32[]{:S(2)}) collective-permute-start(bf16[2,336,256]{2,1,0:T(8,128)(2,1)S(1)} %get-tuple-element.77.refs_4_.refs_0_), channel_id=1, source_target_pairs={{0,1},{1,0},{2,3},{3,2},{4,5},{5,4},{6,7},{7,6},{8,9},{9,8},{10,11... | collective-permute-start | bytes 1032200 | tf_op jit(solution)/shard_map/ppermute | solution.py:437
  69.9 2.6 %collective-permute-start.15 = (bf16[2,336,256]{2,1,0:T(8,128)(2,1)S(1)}, bf16[2,336,256]{2,1,0:T(8,128)(2,1)S(1)}, u32[]{:S(2)}, u32[]{:S(2)}) collective-permute-start(bf16[2,336,256]{2,1,0:T(8,128)(2,1)S(1)} %get-tuple-element.78.refs_5_.refs_1_), channel_id=1, source_target_pairs={{0,1},{1,0},{2,3},{3,2},{4,5},{5,4},{6,7},{7,6},{8,9},{9,8},{10,11... | collective-permute-start | bytes 1032200 | tf_op jit(solution)/shard_map/ppermute | solution.py:437
  71.0 7.5 %collective-permute-start.19 = (bf16[4,176,256]{2,1,0:T(8,128)(2,1)S(1)}, bf16[4,176,256]{2,1,0:T(8,128)(2,1)S(1)}, u32[]{:S(2)}, u32[]{:S(2)}) collective-permute-start(bf16[4,176,256]{2,1,0:T(8,128)(2,1)S(1)} %select.3.refs_12_.refs_2_), channel_id=1, source_target_pairs={{0,1},{1,0},{2,3},{3,2},{4,5},{5,4},{6,7},{7,6},{8,9},{9,8},{10,11... | collective-permute-start | bytes 1081352 | tf_op jit(solution)/shard_map/ppermute | solution.py:437
  78.5 1.7 %collective-permute-start.20 = (bf16[4,176,256]{2,1,0:T(8,128)(2,1)S(1)}, bf16[4,176,256]{2,1,0:T(8,128)(2,1)S(1)}, u32[]{:S(2)}, u32[]{:S(2)}) collective-permute-start(bf16[4,176,256]{2,1,0:T(8,128)(2,1)S(1)} %collective-permute-done.18.refs_13_), channel_id=1, source_target_pairs={{0,1},{1,0},{2,3},{3,2},{4,5},{5,4},{6,7},{7,6},{8,9},{9,8},{10,11... | collective-permute-start | bytes 1081352 | tf_op jit(solution)/shard_map/ppermute | solution.py:437
  82.7 6.1 %collective-permute-start.21 = (f32[8,512]{1,0:T(8,128)S(1)}, f32[8,512]{1,0:T(8,128)S(1)}, u32[]{:S(2)}, u32[]{:S(2)}) collective-permute-start(f32[8,512]{1,0:T(8,128)S(1)} %get-tuple-element.95), channel_id=1, source_target_pairs={{0,4},{4,8},{8,12},{12,0},{1,5},{5,9},{9,13},{13,1},{2,6},{6,10},{... | collective-permute-start | bytes 49160 | tf_op jit(solution)/shard_map/ppermute | solution.py:452
  83.3 5.5 %collective-permute-start.22 = (f32[8,512]{1,0:T(8,128)S(1)}, f32[8,512]{1,0:T(8,128)S(1)}, u32[]{:S(2)}, u32[]{:S(2)}) collective-permute-start(f32[8,512]{1,0:T(8,128)S(1)} %get-tuple-element.96), channel_id=1, source_target_pairs={{0,8},{4,12},{8,0},{12,4},{1,9},{5,13},{9,1},{13,5},{2,10},{6,14},... | collective-permute-start | bytes 49160 | tf_op jit(solution)/shard_map/ppermute | solution.py:452
  84.7 4.1 %collective-permute-start.23 = (f32[8,512]{1,0:T(8,128)S(1)}, f32[8,512]{1,0:T(8,128)S(1)}, u32[]{:S(2)}, u32[]{:S(2)}) collective-permute-start(f32[8,512]{1,0:T(8,128)S(1)} %get-tuple-element.97), channel_id=1, source_target_pairs={{0,12},{4,0},{8,4},{12,8},{1,13},{5,1},{9,5},{13,9},{2,14},{6,2},{... | collective-permute-start | bytes 49160 | tf_op jit(solution)/shard_map/ppermute | solution.py:452

commit v10 on v9

--- a/solution.py
+++ b/solution.py
@@ -11,7 +11,7 @@
 BR = 512
 BLK_DEV = 8
 LANES = 128
-CHUNKS = ((0, 336), (336, 176))
+CHUNKS = ((0, 320), (320, 192))
 PIECES = (2, 1)
 WINDOWS = ((0, 256), (256, 512))
 
@@ -40,9 +40,9 @@
     return pltpu.CompilerParams(vmem_limit_bytes=mebibytes * 1024 * 1024)
 
 
-def pack_kernel(wide_count, pair_count, capacity, me_ref, *refs):
+def pack_kernel(wide_count, pair_count, capacity, me_ref, pairs_ref, *refs):
     lists, blocks_ref = refs[: wide_count - 1], refs[wide_count - 1]
-    outs, sems = refs[wide_count:-1], refs[-1]
+    *outs, rows_ref, sems = refs[wide_count:]
     me = me_ref[0]
     copies = []
 
@@ -64,54 +64,32 @@
             out = outs[chunk * (wide_count - 1) + shift - 1]
             for slot in range(capacity):
                 send(blocks_ref.at[picks[slot], pl.ds(start, size)], out.at[slot])
+    for pair in range(pair_count):
+        send(blocks_ref.at[pairs_ref[0, pair] & 7], rows_ref.at[pair])
     for copy in copies:
         copy.wait()
 
 
-def pack(me, lists, blocks, capacity):
-    wide_count, pair_count = len(lists) + 1, lists[0].shape[1]
+def pack(me, pairs, lists, blocks, capacity):
+    wide_count, pair_count = len(lists) + 1, pairs.shape[1]
     feat = blocks.shape[-1]
     shapes = [
         pltpu.VMEM((capacity, size, feat), blocks.dtype)
         for _, size in CHUNKS
         for _ in range(1, wide_count)
-    ]
+    ] + [pltpu.VMEM((pair_count, BR, feat), blocks.dtype)]
+    copies = (len(shapes) - 1) * capacity + pair_count
     outs = pl.pallas_call(
         functools.partial(pack_kernel, wide_count, pair_count, capacity),
         out_shape=shapes,
-        in_specs=[smem()] * wide_count + [anywhere()],
+        in_specs=[smem()] * (1 + wide_count) + [anywhere()],
         out_specs=[anywhere()] * len(shapes),
-        scratch_shapes=[pltpu.SemaphoreType.DMA((len(shapes) * capacity,))],
+        scratch_shapes=[pltpu.SemaphoreType.DMA((copies,))],
         compiler_params=params(4),
         name="pack",
-    )(me, *lists, in_hbm(blocks))
+    )(me, in_hbm(pairs), *lists, in_hbm(blocks))
     each = wide_count - 1
-    return [outs[c * each : (c + 1) * each] for c in range(len(CHUNKS))]
-
-
-def take_kernel(pairs_ref, blocks_ref, rows_ref, cols_ref, sems):
-    copies = []
-    for pair in range(rows_ref.shape[0]):
-        for side, out in enumerate((rows_ref, cols_ref)):
-            source = blocks_ref.at[pairs_ref[side, pair] & 7]
-            copies.append(pltpu.make_async_copy(source, out.at[pair], sems.at[len(copies)]))
-            copies[-1].start()
-    for copy in copies:
-        copy.wait()
-
-
-def take(pairs, blocks):
-    pair_count = pairs.shape[1]
-    taken = pltpu.VMEM((pair_count, *blocks.shape[1:]), blocks.dtype)
-    return pl.pallas_call(
-        take_kernel,
-        out_shape=[taken, taken],
-        in_specs=[smem(), anywhere()],
-        out_specs=[anywhere(), anywhere()],
-        scratch_shapes=[pltpu.SemaphoreType.DMA((2 * pair_count,))],
-        compiler_params=params(4),
-        name="take",
-    )(pairs, in_hbm(blocks))
+    return [outs[c * each : (c + 1) * each] for c in range(len(CHUNKS))], outs[-1]
 
 
 def select_kernel(wide_count, start, me_ref, pairs_ref, own_ref, *refs):
@@ -149,7 +127,7 @@
         out_specs=[vmem()] * pieces,
         compiler_params=params(4),
         name="select",
-    )(me, pairs, *[in_vmem(x) for x in (own, *received)])
+    )(me, in_hbm(pairs), *[in_vmem(x) for x in (own, *received)])
 
 
 def tree(parts):
@@ -204,7 +182,7 @@
 
 
 def window_parts(window, narrow_count, refs):
-    rows, refs = take_parts(refs, narrow_count, 1)
+    rows, refs = [ref.at[i] for ref in refs[:2] for i in range(narrow_count // 2)], refs[2:]
     chunks = []
     for chunk, _, _ in segments(window):
         cols, refs = take_parts(refs, narrow_count, PIECES[chunk])
@@ -220,7 +198,7 @@
 
 def pair_parts(window, rows, chunks, pair):
     cols = [own_columns(window, [c[i] for c in chunks], pair) for i in range(len(rows))]
-    return [of_pair(part, pair)[...] for part in rows], cols
+    return [part[pair] for part in rows], cols
 
 
 def first_kernel(window, narrow_count, *refs):
@@ -272,7 +250,7 @@
 
 
 def first_window(rows, cols):
-    pair_count, _, feat = rows[0][0].shape
+    _, pair_count, _, feat = rows[0][0].shape
     window = WINDOWS[0]
     lanes = pltpu.VMEM((pair_count, BR, LANES), jnp.float32)
     total = pltpu.VMEM((pair_count, BR, feat), jnp.float32)
@@ -280,7 +258,7 @@
     for chunk, _, _ in segments(window):
         args += operands(cols[chunk])
     return pl.pallas_call(
-        functools.partial(first_kernel, window, len(rows)),
+        functools.partial(first_kernel, window, len(cols[0])),
         out_shape=[lanes, lanes, total, pltpu.VMEM((pair_count, window[1]), jnp.float32)],
         in_specs=[vmem()] * len(args),
         out_specs=[vmem()] * 4,
@@ -291,7 +269,7 @@
 
 
 def last_window(me, pairs, rows, cols, square, mass, sums, wide_count):
-    pair_count = rows[0][0].shape[0]
+    pair_count = rows[0][0].shape[1]
     window = WINDOWS[1]
     size = window[1] - window[0]
     by_block = pltpu.VMEM((BLK_DEV, BR), jnp.float32)
@@ -304,32 +282,54 @@
         args += operands(cols[chunk])
     args += [square, mass, sums]
     kernel, mass, row_sums, *shares = pl.pallas_call(
-        functools.partial(last_kernel, window, len(rows), wide_count),
+        functools.partial(last_kernel, window, len(cols[0]), wide_count),
         out_shape=shapes,
         in_specs=[smem(), smem()] + [vmem()] * len(args),
         out_specs=[vmem()] * len(shapes),
         compiler_params=params(16),
         cost_estimate=estimate(pair_count, size),
         name="last_window",
-    )(me, pairs, *[in_vmem(x) for x in args])
+    )(me, in_hbm(pairs), *[in_vmem(x) for x in args])
     return kernel, mass, row_sums, shares
 
 
-def keep_kernel(block_ref, out_ref):
+def keep_kernel(pairs_ref, block_ref, blocks_ref, out_ref, own_ref, sems):
+    here = pl.program_id(0)
+
+    def copies():
+        for pair in range(own_ref.shape[0]):
+            source = blocks_ref.at[pairs_ref[1, pair] & 7]
+            yield pltpu.make_async_copy(source, own_ref.at[pair], sems.at[pair])
+
+    @pl.when(here == 0)
+    def _():
+        for copy in copies():
+            copy.start()
+
     out_ref[...] = block_ref[...]
 
-
-def keep(blocks):
+    @pl.when(here == pl.num_programs(0) - 1)
+    def _():
+        for copy in copies():
+            copy.wait()
+
+
+def keep(pairs, blocks):
+    pair_count = pairs.shape[1]
     block = pl.BlockSpec((1, *blocks.shape[1:]), lambda k: (k, 0, 0))
     return pl.pallas_call(
         keep_kernel,
-        out_shape=pltpu.HBM(blocks.shape, blocks.dtype),
+        out_shape=[
+            pltpu.HBM(blocks.shape, blocks.dtype),
+            pltpu.VMEM((pair_count, *blocks.shape[1:]), blocks.dtype),
+        ],
         grid=(blocks.shape[0],),
-        in_specs=[block],
-        out_specs=block,
+        in_specs=[smem(), block, anywhere()],
+        out_specs=[block, anywhere()],
+        scratch_shapes=[pltpu.SemaphoreType.DMA((pair_count,))],
         compiler_params=params(4),
         name="keep",
-    )(in_hbm(blocks))
+    )(in_hbm(pairs), in_hbm(blocks), in_hbm(blocks))
 
 
 def mean_kernel(window, local_ref, rows_ref, kernel_ref, mass_ref, total_ref, *refs):
@@ -403,7 +403,7 @@
         compiler_params=params(16),
         cost_estimate=estimate(pair_count, 128),
         name="means",
-    )(pairs, *args, in_hbm(kept))
+    )(in_hbm(pairs), *args, in_hbm(kept))
 
 
 def weight_kernel(*refs):
@@ -464,17 +464,15 @@
     blocks = embeddings.reshape(BLK_DEV, BR, feat)
     lists = to_wide([pairs] * (wide_count - 1))
     fixed = lax.optimization_barrier
-    lists, (row_slices, own) = fixed((lists, take(pairs, blocks)))
-    outgoing = pack(me, lists, blocks, capacity)
+    outgoing, row_slices = pack(me, pairs, lists, blocks, capacity)
 
     def pick(received, chunk):
         return select(me, pairs, own, received, *CHUNKS[chunk], PIECES[chunk])
 
-    rows = first_hops([row_slices])
-    rows_last = hop(rows[:1], 1)
-    rows, rows_last, received, kept = fixed((rows, rows_last, to_wide(outgoing[0]), keep(blocks)))
+    rows = jnp.stack([part[0] for part in first_hops([row_slices])])
+    rows, received, (kept, own) = fixed((rows, to_wide(outgoing[0]), keep(pairs, blocks)))
     cols_a = first_hops(pick(received, 0))
-    rows = rows + rows_last + hop(rows[1:], 1)
+    rows = [[rows], *hop([[rows]], 1)]
     cols_a, rows, received = fixed((cols_a, rows, to_wide(outgoing[1])))
     cols_b = first_hops(pick(received, 1))
     last_b = hop(cols_b[:1], 1)

time: 89.8 us -> 88.1 us (0.981)
  waiting for transfers between devices: 37.2 us -> 39.1 us
  local copies, waits for them, and re-layouts: 1.69 us -> 0 us
  starting transfers between devices: 30.1 us -> 28.6 us
    ppermute x12 -> x11, waiting for transfers between devices: 9.46 us -> 20.8 us  [hop(): lax.ppermute(piece, 'narrow', perm)]
    ppermute x12, waiting for transfers between devices: 27.7 us -> 18.3 us  [to_wide(): lax.ppermute(piece, 'wide', [(i, (i + shift) % count) for i in range(coun...]
    unnamed x8 -> x0, local copies, waits for them, and re-layouts: 1.69 us -> none
    pallas_call x4 -> x3, Pallas kernels: 13.4 us -> 11.8 us  [the longest x1 6.02 us: keep(): pl.pallas_call(keep_kernel, out_shape=[pltpu.HBM(blocks.shape, blocks.dty...]
    ppermute x12, starting transfers between devices: 24.7 us -> 23.2 us  [to_wide(): lax.ppermute(piece, 'wide', [(i, (i + shift) % count) for i in range(coun...]
    ppermute x12 -> x11, starting transfers between devices: 5.42 us -> 5.41 us  [hop(): lax.ppermute(piece, 'narrow', perm)]
  transfers between devices with their start and end apart: 24 -> 23, of which waited for: 13 -> 16; matrix products, arithmetic and copies ran while one was open for 0% -> 0% of each run, Pallas kernels for 18% -> 14%
where the time goes in v10:
time: 88.1 us; the launch traced here: 87.9 us
  waiting for transfers between devices  39.1 us (44%)
  starting transfers between devices  28.6 us (32%)
  Pallas kernels  19.2 us (22%)
    ppermute x12, starting transfers between devices, to_wide(): lax.ppermute(piece, 'wide', [(i, (i + shift) % count) for i in range(coun...  23.2 us
    ppermute x11, waiting for transfers between devices, hop(): lax.ppermute(piece, 'narrow', perm)  20.8 us
    ppermute x12, waiting for transfers between devices, to_wide(): lax.ppermute(piece, 'wide', [(i, (i + shift) % count) for i in range(coun...  18.3 us
    pallas_call x1, Pallas kernels, keep(): pl.pallas_call(keep_kernel, out_shape=[pltpu.HBM(blocks.shape, blocks.dty...  6.02 us
    ppermute x11, starting transfers between devices, hop(): lax.ppermute(piece, 'narrow', perm)  5.41 us
    pallas_call x1, Pallas kernels, first_window(): pl.pallas_call(functools.partial(first_kernel, window, len(cols[0])), out...  3.1 us
    pallas_call x1, Pallas kernels, pack(): pl.pallas_call(functools.partial(pack_kernel, wide_count, pair_count, cap...  2.9 us
    pallas_call x1, Pallas kernels, last_window(): pl.pallas_call(functools.partial(last_kernel, window, len(cols[0]), wide_...  2.64 us
  transfers between devices with their start and end apart: 23, of which 16 were waited for; matrix products, arithmetic and copies ran while one was open for 0% of the time, Pallas kernels for 14%

profile of v10, /device:TPU:0, one launch (start us, length us, event | category | flops | bytes accessed | tf_op | source)
XLA Modules:
  0.0 87.9 jit_solution(9865002583830705218)
XLA Ops:
  0.6 5.1 %collective-permute-start.2 = (s32[2,4]{1,0:T(2,128)}, s32[2,4]{1,0:T(2,128)S(1)}, u32[]{:S(2)}, u32[]{:S(2)}) collective-permute-start(s32[2,4]{1,0:T(2,128)} %bitcast.13), channel_id=1, source_target_pairs={{0,12},{4,0},{8,4},{12,8},{1,13},{5,1},{9,5},{13,9},{2,14},{6,2},{... | collective-permute-start | bytes 104 | tf_op jit(solution)/shard_map/ppermute | solution.py:452
  5.7 1.0 %collective-permute-start = (s32[2,4]{1,0:T(2,128)}, s32[2,4]{1,0:T(2,128)S(1)}, u32[]{:S(2)}, u32[]{:S(2)}) collective-permute-start(s32[2,4]{1,0:T(2,128)} %bitcast.15), channel_id=1, source_target_pairs={{0,4},{4,8},{8,12},{12,0},{1,5},{5,9},{9,13},{13,1},{2,6},{6,10},{... | collective-permute-start | bytes 104 | tf_op jit(solution)/shard_map/ppermute | solution.py:452
  7.2 3.2 %collective-permute-done.1.refs_1_ = s32[2,4]{1,0:T(2,128)S(1)} collective-permute-done((s32[2,4]{1,0:T(2,128)}, s32[2,4]{1,0:T(2,128)S(1)}, u32[]{:S(2)}, u32[]{:S(2)}) %collective-permute-start.1) | collective-permute-done | bytes 64 | tf_op jit(solution)/shard_map/ppermute | solution.py:452
  10.4 0.9 %collective-permute-done.refs_0_ = s32[2,4]{1,0:T(2,128)S(1)} collective-permute-done((s32[2,4]{1,0:T(2,128)}, s32[2,4]{1,0:T(2,128)S(1)}, u32[]{:S(2)}, u32[]{:S(2)}) %collective-permute-start) | collective-permute-done | bytes 64 | tf_op jit(solution)/shard_map/ppermute | solution.py:452
  11.3 2.9 %pack.1 = (bf16[2,320,256]{2,1,0:T(8,128)(2,1)S(1)}, bf16[2,320,256]{2,1,0:T(8,128)(2,1)S(1)}, bf16[2,320,256]{2,1,0:T(8,128)(2,1)S(1)}, bf16[2,192,256]{2,1,0:T...) custom-call(s32[1]{0:T(128)} %bitcast.me_ref, ...), custom_call_target="tpu_custom_call" | custom-call | tf_op jit(solution)/shard_map/pack/pallas_call | solution.py:82
  14.2 1.6 %collective-permute-start.3 = (bf16[4,512,256]{2,1,0:T(8,128)(2,1)S(1)}, bf16[4,512,256]{2,1,0:T(8,128)(2,1)S(1)}, u32[]{:S(2)}, u32[]{:S(2)}) collective-permute-start(bf16[4,512,256]{2,1,0:T(8,128)(2,1)S(1)} %get-tuple-element.45.rows_ref), channel_id=1, source_target_pairs={{0,2},{1,3},{2,0},{3,1},{4,6},{5,7},{6,4},{7,5},{8,10},{9,11},{10,... | collective-permute-start | bytes 3145736 | tf_op jit(solution)/shard_map/ppermute | solution.py:437
  15.8 0.9 %collective-permute-start.5 = (bf16[2,320,256]{2,1,0:T(8,128)(2,1)S(1)}, bf16[2,320,256]{2,1,0:T(8,128)(2,1)S(1)}, u32[]{:S(2)}, u32[]{:S(2)}) collective-permute-start(bf16[2,320,256]{2,1,0:T(8,128)(2,1)S(1)} %get-tuple-element.47), channel_id=1, source_target_pairs={{0,8},{4,12},{8,0},{12,4},{1,9},{5,13},{9,1},{13,5},{2,10},{6,14},... | collective-permute-start | bytes 983048 | tf_op jit(solution)/shard_map/ppermute | solution.py:452
  16.7 2.9 %collective-permute-start.6 = (bf16[2,320,256]{2,1,0:T(8,128)(2,1)S(1)}, bf16[2,320,256]{2,1,0:T(8,128)(2,1)S(1)}, u32[]{:S(2)}, u32[]{:S(2)}) collective-permute-start(bf16[2,320,256]{2,1,0:T(8,128)(2,1)S(1)} %get-tuple-element.48), channel_id=1, source_target_pairs={{0,12},{4,0},{8,4},{12,8},{1,13},{5,1},{9,5},{13,9},{2,14},{6,2},{... | collective-permute-start | bytes 983048 | tf_op jit(solution)/shard_map/ppermute | solution.py:452
  19.6 6.0 %keep.1 = (bf16[8,512,256]{2,1,0:T(8,128)(2,1)}, bf16[4,512,256]{2,1,0:T(8,128)(2,1)S(1)}) custom-call(s32[2,4]{1,0:T(2,128)} %bitcast.17, bf16[8,512,256]{2,1,0:T(8,128)(2,1)} %bitcast.9, bf16[8,512,256]{2,1,0:T(8,128)(2,1)} %bitcast.10), custom_call_target="tpu_custom_call" | custom-call | tf_op jit(solution)/shard_map/keep/pallas_call | solution.py:320
  25.6 12.1 %collective-permute-done.3 = bf16[4,512,256]{2,1,0:T(8,128)(2,1)S(1)} collective-permute-done((bf16[4,512,256]{2,1,0:T(8,128)(2,1)S(1)}, bf16[4,512,256]{2,1,0:T(8,128)(2,1)S(1)}, u32[]{:S(2)}, u32[]{:S(2)}) %collective-permute-start.3) | collective-permute-done | bytes 1048608 | tf_op jit(solution)/shard_map/ppermute | solution.py:437
  38.0 1.6 %collective-permute-done.5.refs_1_ = bf16[2,320,256]{2,1,0:T(8,128)(2,1)S(1)} collective-permute-done((bf16[2,320,256]{2,1,0:T(8,128)(2,1)S(1)}, bf16[2,320,256]{2,1,0:T(8,128)(2,1)S(1)}, u32[]{:S(2)}, u32[]{:S(2)}) %collective-permute-start.5) | collective-permute-done | bytes 327712 | tf_op jit(solution)/shard_map/ppermute | solution.py:452
  39.6 6.5 %collective-permute-start.10 = (bf16[2,192,256]{2,1,0:T(8,128)(2,1)S(1)}, bf16[2,192,256]{2,1,0:T(8,128)(2,1)S(1)}, u32[]{:S(2)}, u32[]{:S(2)}) collective-permute-start(bf16[2,192,256]{2,1,0:T(8,128)(2,1)S(1)} %get-tuple-element.58), channel_id=1, source_target_pairs={{0,4},{4,8},{8,12},{12,0},{1,5},{5,9},{9,13},{13,1},{2,6},{6,10},{... | collective-permute-start | bytes 589832 | tf_op jit(solution)/shard_map/ppermute | solution.py:452
  46.1 0.8 select.2
  46.9 0.6 collective-permute-start.7
  47.5 1.5 %collective-permute-start.8 = (bf16[2,320,256]{2,1,0:T(8,128)(2,1)S(1)}, bf16[2,320,256]{2,1,0:T(8,128)(2,1)S(1)}, u32[]{:S(2)}, u32[]{:S(2)}) collective-permute-start(bf16[2,320,256]{2,1,0:T(8,128)(2,1)S(1)} %get-tuple-element.64.refs_3_.refs_1_), channel_id=1, source_target_pairs={{0,2},{1,3},{2,0},{3,1},{4,6},{5,7},{6,4},{7,5},{8,10},{9,11},{10,... | collective-permute-start | bytes 983048 | tf_op jit(solution)/shard_map/ppermute | solution.py:437
  49.6 2.1 %collective-permute-done.10.refs_0_ = bf16[2,192,256]{2,1,0:T(8,128)(2,1)S(1)} collective-permute-done((bf16[2,192,256]{2,1,0:T(8,128)(2,1)S(1)}, bf16[2,192,256]{2,1,0:T(8,128)(2,1)S(1)}, u32[]{:S(2)}, u32[]{:S(2)}) %collective-permute-start.10) | collective-permute-done | bytes 196640 | tf_op jit(solution)/shard_map/ppermute | solution.py:452
  51.7 1.7 %collective-permute-start.12 = (bf16[2,192,256]{2,1,0:T(8,128)(2,1)S(1)}, bf16[2,192,256]{2,1,0:T(8,128)(2,1)S(1)}, u32[]{:S(2)}, u32[]{:S(2)}) collective-permute-start(bf16[2,192,256]{2,1,0:T(8,128)(2,1)S(1)} %get-tuple-element.60), channel_id=1, source_target_pairs={{0,12},{4,0},{8,4},{12,8},{1,13},{5,1},{9,5},{13,9},{2,14},{6,2},{... | collective-permute-start | bytes 589832 | tf_op jit(solution)/shard_map/ppermute | solution.py:452
  53.4 7.0 %collective-permute-done.11.refs_1_ = bf16[2,192,256]{2,1,0:T(8,128)(2,1)S(1)} collective-permute-done((bf16[2,192,256]{2,1,0:T(8,128)(2,1)S(1)}, bf16[2,192,256]{2,1,0:T(8,128)(2,1)S(1)}, u32[]{:S(2)}, u32[]{:S(2)}) %collective-permute-start.11) | collective-permute-done | bytes 196640 | tf_op jit(solution)/shard_map/ppermute | solution.py:452
  60.5 2.1 %collective-permute-done.12.refs_2_ = bf16[2,192,256]{2,1,0:T(8,128)(2,1)S(1)} collective-permute-done((bf16[2,192,256]{2,1,0:T(8,128)(2,1)S(1)}, bf16[2,192,256]{2,1,0:T(8,128)(2,1)S(1)}, u32[]{:S(2)}, u32[]{:S(2)}) %collective-permute-start.12) | collective-permute-done | bytes 196640 | tf_op jit(solution)/shard_map/ppermute | solution.py:452
  62.5 1.3 %collective-permute-done.8.refs_5_ = bf16[2,320,256]{2,1,0:T(8,128)(2,1)S(1)} collective-permute-done((bf16[2,320,256]{2,1,0:T(8,128)(2,1)S(1)}, bf16[2,320,256]{2,1,0:T(8,128)(2,1)S(1)}, u32[]{:S(2)}, u32[]{:S(2)}) %collective-permute-start.8) | collective-permute-done | bytes 327712 | tf_op jit(solution)/shard_map/ppermute | solution.py:437
  63.9 0.8 select.3.refs_10_.refs_2_
  64.7 0.6 collective-permute-start.17
  66.3 0.6 collective-permute-done.15.refs_8_
  68.3 3.1 %first_window.1 = (f32[4,512,128]{2,1,0:T(8,128)S(1)}, f32[4,512,128]{2,1,0:T(8,128)S(1)}, f32[4,512,256]{2,1,0:T(8,128)S(1)}, f32[4,256]{1,0:T(4,128)S(1)}) custom-call(bf16[2,4,512,256]{3,2,1,0:T(8,128)(2,1)S(1)} %pad_maximum_fusion.refs_0_, bf16[2,4,512,256]{3,2,1,0:T(8,128)(2,1)S(1)} %collective-permute-done.9.refs_1_, ...), custom_call_target="tpu_custom_call" | custom-call | tf_op jit(solution)/shard_map/first_window/pallas_call | solution.py:260
  71.4 3.8 %collective-permute-done.17.refs_11_ = bf16[4,192,256]{2,1,0:T(8,128)(2,1)S(1)} collective-permute-done((bf16[4,192,256]{2,1,0:T(8,128)(2,1)S(1)}, bf16[4,192,256]{2,1,0:T(8,128)(2,1)S(1)}, u32[]{:S(2)}, u32[]{:S(2)}) %collective-permute-start.17) | collective-permute-done | bytes 393248 | tf_op jit(solution)/shard_map/ppermute | solution.py:437
  75.2 1.7 %collective-permute-done.19.refs_13_ = bf16[4,192,256]{2,1,0:T(8,128)(2,1)S(1)} collective-permute-done((bf16[4,192,256]{2,1,0:T(8,128)(2,1)S(1)}, bf16[4,192,256]{2,1,0:T(8,128)(2,1)S(1)}, u32[]{:S(2)}, u32[]{:S(2)}) %collective-permute-start.19) | collective-permute-done | bytes 393248 | tf_op jit(solution)/shard_map/ppermute | solution.py:437
  76.9 2.6 %last_window.1 = (bf16[4,512,256]{2,1,0:T(8,128)(2,1)S(1)}, f32[4,512,128]{2,1,0:T(8,128)S(1)}, f32[8,512]{1,0:T(8,128)S(1)}, f32[8,512]{1,0:T(8,128)S(1)}, f32[...) custom-call(s32[1]{0:T(128)} %bitcast.me_ref, s32[2,4]{1,0:T(2,128)} %bitcast.20, ...), custom_call_target="tpu_custom_call" | custom-call | flops 1073741824 | bytes 8388608 | tf_op jit(solution)/shard_map/last_window/pallas_call | solution.py:284
  79.5 2.0 %collective-permute-start.20 = (f32[8,512]{1,0:T(8,128)S(1)}, f32[8,512]{1,0:T(8,128)S(1)}, u32[]{:S(2)}, u32[]{:S(2)}) collective-permute-start(f32[8,512]{1,0:T(8,128)S(1)} %get-tuple-element.81), channel_id=1, source_target_pairs={{0,4},{4,8},{8,12},{12,0},{1,5},{5,9},{9,13},{13,1},{2,6},{6,10},{... | collective-permute-start | bytes 49160 | tf_op jit(solution)/shard_map/ppermute | solution.py:452
  81.5 2.0 %collective-permute-start.21 = (f32[8,512]{1,0:T(8,128)S(1)}, f32[8,512]{1,0:T(8,128)S(1)}, u32[]{:S(2)}, u32[]{:S(2)}) collective-permute-start(f32[8,512]{1,0:T(8,128)S(1)} %get-tuple-element.82), channel_id=1, source_target_pairs={{0,8},{4,12},{8,0},{12,4},{1,9},{5,13},{9,1},{13,5},{2,10},{6,14},... | collective-permute-start | bytes 49160 | tf_op jit(solution)/shard_map/ppermute | solution.py:452
  83.9 2.3 %means.1 = bf16[8,512,256]{2,1,0:T(8,128)(2,1)} custom-call(s32[2,4]{1,0:T(2,128)} %bitcast.21, bf16[4,512,256]{2,1,0:T(8,128)(2,1)S(1)} %get-tuple-element.45.rows_ref, bf16[4,512,256]{2,1,0:T(8,128)(2,1)S(1)} %get-tuple-element.84.kernel_ref, f32[4,512,128]{2,1,0:T(8,128)S(1)} %get-tuple-element.85.mass_ref, ...), custom_call_target="tpu_custom_call", output_to_operand_aliasing={{}: (8, {})} | custom-call | flops 536870912 | bytes 8388608 | tf_op jit(solution)/shard_map/means/pallas_call | solution.py:389
  86.3 0.9 %collective-permute-done.22.refs_4_ = f32[8,512]{1,0:T(8,128)S(1)} collective-permute-done((f32[8,512]{1,0:T(8,128)S(1)}, f32[8,512]{1,0:T(8,128)S(1)}, u32[]{:S(2)}, u32[]{:S(2)}) %collective-permute-start.22) | collective-permute-done | bytes 16416 | tf_op jit(solution)/shard_map/ppermute | solution.py:452
  87.2 0.6 weights.1
  (23 shorter events, 4.1 us)
Async XLA Ops:
  0.6 6.6 %collective-permute-start.2 = (s32[2,4]{1,0:T(2,128)}, s32[2,4]{1,0:T(2,128)S(1)}, u32[]{:S(2)}, u32[]{:S(2)}) collective-permute-start(s32[2,4]{1,0:T(2,128)} %bitcast.13), channel_id=1, source_target_pairs={{0,12},{4,0},{8,4},{12,8},{1,13},{5,1},{9,5},{13,9},{2,14},{6,2},{... | collective-permute-start | bytes 104 | tf_op jit(solution)/shard_map/ppermute | solution.py:452
  5.7 4.7 %collective-permute-start.1 = (s32[2,4]{1,0:T(2,128)}, s32[2,4]{1,0:T(2,128)S(1)}, u32[]{:S(2)}, u32[]{:S(2)}) collective-permute-start(s32[2,4]{1,0:T(2,128)} %bitcast.14), channel_id=1, source_target_pairs={{0,8},{4,12},{8,0},{12,4},{1,9},{5,13},{9,1},{13,5},{2,10},{6,14},... | collective-permute-start | bytes 104 | tf_op jit(solution)/shard_map/ppermute | solution.py:452
  5.7 5.6 %collective-permute-start = (s32[2,4]{1,0:T(2,128)}, s32[2,4]{1,0:T(2,128)S(1)}, u32[]{:S(2)}, u32[]{:S(2)}) collective-permute-start(s32[2,4]{1,0:T(2,128)} %bitcast.15), channel_id=1, source_target_pairs={{0,4},{4,8},{8,12},{12,0},{1,5},{5,9},{9,13},{13,1},{2,6},{6,10},{... | collective-permute-start | bytes 104 | tf_op jit(solution)/shard_map/ppermute | solution.py:452
  14.2 23.5 %collective-permute-start.3 = (bf16[4,512,256]{2,1,0:T(8,128)(2,1)S(1)}, bf16[4,512,256]{2,1,0:T(8,128)(2,1)S(1)}, u32[]{:S(2)}, u32[]{:S(2)}) collective-permute-start(bf16[4,512,256]{2,1,0:T(8,128)(2,1)S(1)} %get-tuple-element.45.rows_ref), channel_id=1, source_target_pairs={{0,2},{1,3},{2,0},{3,1},{4,6},{5,7},{6,4},{7,5},{8,10},{9,11},{10,... | collective-permute-start | bytes 3145736 | tf_op jit(solution)/shard_map/ppermute | solution.py:437
  15.8 22.2 %collective-permute-start.4 = (bf16[2,320,256]{2,1,0:T(8,128)(2,1)S(1)}, bf16[2,320,256]{2,1,0:T(8,128)(2,1)S(1)}, u32[]{:S(2)}, u32[]{:S(2)}) collective-permute-start(bf16[2,320,256]{2,1,0:T(8,128)(2,1)S(1)} %get-tuple-element.46), channel_id=1, source_target_pairs={{0,4},{4,8},{8,12},{12,0},{1,5},{5,9},{9,13},{13,1},{2,6},{6,10},{... | collective-permute-start | bytes 983048 | tf_op jit(solution)/shard_map/ppermute | solution.py:452
  15.8 23.8 %collective-permute-start.5 = (bf16[2,320,256]{2,1,0:T(8,128)(2,1)S(1)}, bf16[2,320,256]{2,1,0:T(8,128)(2,1)S(1)}, u32[]{:S(2)}, u32[]{:S(2)}) collective-permute-start(bf16[2,320,256]{2,1,0:T(8,128)(2,1)S(1)} %get-tuple-element.47), channel_id=1, source_target_pairs={{0,8},{4,12},{8,0},{12,4},{1,9},{5,13},{9,1},{13,5},{2,10},{6,14},... | collective-permute-start | bytes 983048 | tf_op jit(solution)/shard_map/ppermute | solution.py:452
  16.7 22.9 %collective-permute-start.6 = (bf16[2,320,256]{2,1,0:T(8,128)(2,1)S(1)}, bf16[2,320,256]{2,1,0:T(8,128)(2,1)S(1)}, u32[]{:S(2)}, u32[]{:S(2)}) collective-permute-start(bf16[2,320,256]{2,1,0:T(8,128)(2,1)S(1)} %get-tuple-element.48), channel_id=1, source_target_pairs={{0,12},{4,0},{8,4},{12,8},{1,13},{5,1},{9,5},{13,9},{2,14},{6,2},{... | collective-permute-start | bytes 983048 | tf_op jit(solution)/shard_map/ppermute | solution.py:452
  39.6 24.3 %collective-permute-start.9 = (bf16[2,4,512,256]{3,2,1,0:T(8,128)(2,1)S(1)}, bf16[2,4,512,256]{3,2,1,0:T(8,128)(2,1)S(1)}, u32[]{:S(2)}, u32[]{:S(2)}) collective-permute-start(bf16[2,4,512,256]{3,2,1,0:T(8,128)(2,1)S(1)} %pad_maximum_fusion.refs_0_), channel_id=1, source_target_pairs={{0,1},{1,0},{2,3},{3,2},{4,5},{5,4},{6,7},{7,6},{8,9},{9,8},{10,11... | collective-permute-start | bytes 6291464 | tf_op jit(solution)/shard_map/ppermute | solution.py:437
  39.6 12.1 %collective-permute-start.10 = (bf16[2,192,256]{2,1,0:T(8,128)(2,1)S(1)}, bf16[2,192,256]{2,1,0:T(8,128)(2,1)S(1)}, u32[]{:S(2)}, u32[]{:S(2)}) collective-permute-start(bf16[2,192,256]{2,1,0:T(8,128)(2,1)S(1)} %get-tuple-element.58), channel_id=1, source_target_pairs={{0,4},{4,8},{8,12},{12,0},{1,5},{5,9},{9,13},{13,1},{2,6},{6,10},{... | collective-permute-start | bytes 589832 | tf_op jit(solution)/shard_map/ppermute | solution.py:452
  46.9 15.6 %collective-permute-start.7 = (bf16[2,320,256]{2,1,0:T(8,128)(2,1)S(1)}, bf16[2,320,256]{2,1,0:T(8,128)(2,1)S(1)}, u32[]{:S(2)}, u32[]{:S(2)}) collective-permute-start(bf16[2,320,256]{2,1,0:T(8,128)(2,1)S(1)} %get-tuple-element.63.refs_2_.refs_0_), channel_id=1, source_target_pairs={{0,2},{1,3},{2,0},{3,1},{4,6},{5,7},{6,4},{7,5},{8,10},{9,11},{10,... | collective-permute-start | bytes 983048 | tf_op jit(solution)/shard_map/ppermute | solution.py:437
  47.5 16.3 %collective-permute-start.8 = (bf16[2,320,256]{2,1,0:T(8,128)(2,1)S(1)}, bf16[2,320,256]{2,1,0:T(8,128)(2,1)S(1)}, u32[]{:S(2)}, u32[]{:S(2)}) collective-permute-start(bf16[2,320,256]{2,1,0:T(8,128)(2,1)S(1)} %get-tuple-element.64.refs_3_.refs_1_), channel_id=1, source_target_pairs={{0,2},{1,3},{2,0},{3,1},{4,6},{5,7},{6,4},{7,5},{8,10},{9,11},{10,... | collective-permute-start | bytes 983048 | tf_op jit(solution)/shard_map/ppermute | solution.py:437
  49.0 11.4 %collective-permute-start.11 = (bf16[2,192,256]{2,1,0:T(8,128)(2,1)S(1)}, bf16[2,192,256]{2,1,0:T(8,128)(2,1)S(1)}, u32[]{:S(2)}, u32[]{:S(2)}) collective-permute-start(bf16[2,192,256]{2,1,0:T(8,128)(2,1)S(1)} %get-tuple-element.59), channel_id=1, source_target_pairs={{0,8},{4,12},{8,0},{12,4},{1,9},{5,13},{9,1},{13,5},{2,10},{6,14},... | collective-permute-start | bytes 589832 | tf_op jit(solution)/shard_map/ppermute | solution.py:452
  51.7 10.8 %collective-permute-start.12 = (bf16[2,192,256]{2,1,0:T(8,128)(2,1)S(1)}, bf16[2,192,256]{2,1,0:T(8,128)(2,1)S(1)}, u32[]{:S(2)}, u32[]{:S(2)}) collective-permute-start(bf16[2,192,256]{2,1,0:T(8,128)(2,1)S(1)} %get-tuple-element.60), channel_id=1, source_target_pairs={{0,12},{4,0},{8,4},{12,8},{1,13},{5,1},{9,5},{13,9},{2,14},{6,2},{... | collective-permute-start | bytes 589832 | tf_op jit(solution)/shard_map/ppermute | solution.py:452
  64.7 10.5 %collective-permute-start.17 = (bf16[4,192,256]{2,1,0:T(8,128)(2,1)S(1)}, bf16[4,192,256]{2,1,0:T(8,128)(2,1)S(1)}, u32[]{:S(2)}, u32[]{:S(2)}) collective-permute-start(bf16[4,192,256]{2,1,0:T(8,128)(2,1)S(1)} %select.3.refs_10_.refs_2_), channel_id=1, source_target_pairs={{0,2},{1,3},{2,0},{3,1},{4,6},{5,7},{6,4},{7,5},{8,10},{9,11},{10,... | collective-permute-start | bytes 1179656 | tf_op jit(solution)/shard_map/ppermute | solution.py:437
  65.3 1.6 %collective-permute-start.15 = (bf16[2,320,256]{2,1,0:T(8,128)(2,1)S(1)}, bf16[2,320,256]{2,1,0:T(8,128)(2,1)S(1)}, u32[]{:S(2)}, u32[]{:S(2)}) collective-permute-start(bf16[2,320,256]{2,1,0:T(8,128)(2,1)S(1)} %collective-permute-done.7.refs_4_), channel_id=1, source_target_pairs={{0,1},{1,0},{2,3},{3,2},{4,5},{5,4},{6,7},{7,6},{8,9},{9,8},{10,11... | collective-permute-start | bytes 983048 | tf_op jit(solution)/shard_map/ppermute | solution.py:437
  65.3 2.1 %collective-permute-start.16 = (bf16[2,320,256]{2,1,0:T(8,128)(2,1)S(1)}, bf16[2,320,256]{2,1,0:T(8,128)(2,1)S(1)}, u32[]{:S(2)}, u32[]{:S(2)}) collective-permute-start(bf16[2,320,256]{2,1,0:T(8,128)(2,1)S(1)} %collective-permute-done.8.refs_5_), channel_id=1, source_target_pairs={{0,1},{1,0},{2,3},{3,2},{4,5},{5,4},{6,7},{7,6},{8,9},{9,8},{10,11... | collective-permute-start | bytes 983048 | tf_op jit(solution)/shard_map/ppermute | solution.py:437
  65.8 2.1 %collective-permute-start.13 = (bf16[2,320,256]{2,1,0:T(8,128)(2,1)S(1)}, bf16[2,320,256]{2,1,0:T(8,128)(2,1)S(1)}, u32[]{:S(2)}, u32[]{:S(2)}) collective-permute-start(bf16[2,320,256]{2,1,0:T(8,128)(2,1)S(1)} %get-tuple-element.63.refs_2_.refs_0_), channel_id=1, source_target_pairs={{0,1},{1,0},{2,3},{3,2},{4,5},{5,4},{6,7},{7,6},{8,9},{9,8},{10,11... | collective-permute-start | bytes 983048 | tf_op jit(solution)/shard_map/ppermute | solution.py:437
  65.8 2.5 %collective-permute-start.14 = (bf16[2,320,256]{2,1,0:T(8,128)(2,1)S(1)}, bf16[2,320,256]{2,1,0:T(8,128)(2,1)S(1)}, u32[]{:S(2)}, u32[]{:S(2)}) collective-permute-start(bf16[2,320,256]{2,1,0:T(8,128)(2,1)S(1)} %get-tuple-element.64.refs_3_.refs_1_), channel_id=1, source_target_pairs={{0,1},{1,0},{2,3},{3,2},{4,5},{5,4},{6,7},{7,6},{8,9},{9,8},{10,11... | collective-permute-start | bytes 983048 | tf_op jit(solution)/shard_map/ppermute | solution.py:437
  66.9 8.3 %collective-permute-start.18 = (bf16[4,192,256]{2,1,0:T(8,128)(2,1)S(1)}, bf16[4,192,256]{2,1,0:T(8,128)(2,1)S(1)}, u32[]{:S(2)}, u32[]{:S(2)}) collective-permute-start(bf16[4,192,256]{2,1,0:T(8,128)(2,1)S(1)} %select.3.refs_10_.refs_2_), channel_id=1, source_target_pairs={{0,1},{1,0},{2,3},{3,2},{4,5},{5,4},{6,7},{7,6},{8,9},{9,8},{10,11... | collective-permute-start | bytes 1179656 | tf_op jit(solution)/shard_map/ppermute | solution.py:437
  75.2 1.7 %collective-permute-start.19 = (bf16[4,192,256]{2,1,0:T(8,128)(2,1)S(1)}, bf16[4,192,256]{2,1,0:T(8,128)(2,1)S(1)}, u32[]{:S(2)}, u32[]{:S(2)}) collective-permute-start(bf16[4,192,256]{2,1,0:T(8,128)(2,1)S(1)} %collective-permute-done.17.refs_11_), channel_id=1, source_target_pairs={{0,1},{1,0},{2,3},{3,2},{4,5},{5,4},{6,7},{7,6},{8,9},{9,8},{10,11... | collective-permute-start | bytes 1179656 | tf_op jit(solution)/shard_map/ppermute | solution.py:437
  79.5 6.8 %collective-permute-start.20 = (f32[8,512]{1,0:T(8,128)S(1)}, f32[8,512]{1,0:T(8,128)S(1)}, u32[]{:S(2)}, u32[]{:S(2)}) collective-permute-start(f32[8,512]{1,0:T(8,128)S(1)} %get-tuple-element.81), channel_id=1, source_target_pairs={{0,4},{4,8},{8,12},{12,0},{1,5},{5,9},{9,13},{13,1},{2,6},{6,10},{... | collective-permute-start | bytes 49160 | tf_op jit(solution)/shard_map/ppermute | solution.py:452
  81.5 4.8 %collective-permute-start.21 = (f32[8,512]{1,0:T(8,128)S(1)}, f32[8,512]{1,0:T(8,128)S(1)}, u32[]{:S(2)}, u32[]{:S(2)}) collective-permute-start(f32[8,512]{1,0:T(8,128)S(1)} %get-tuple-element.82), channel_id=1, source_target_pairs={{0,8},{4,12},{8,0},{12,4},{1,9},{5,13},{9,1},{13,5},{2,10},{6,14},... | collective-permute-start | bytes 49160 | tf_op jit(solution)/shard_map/ppermute | solution.py:452
  83.5 3.7 %collective-permute-start.22 = (f32[8,512]{1,0:T(8,128)S(1)}, f32[8,512]{1,0:T(8,128)S(1)}, u32[]{:S(2)}, u32[]{:S(2)}) collective-permute-start(f32[8,512]{1,0:T(8,128)S(1)} %get-tuple-element.83), channel_id=1, source_target_pairs={{0,12},{4,0},{8,4},{12,8},{1,13},{5,1},{9,5},{13,9},{2,14},{6,2},{... | collective-permute-start | bytes 49160 | tf_op jit(solution)/shard_map/ppermute | solution.py:452

commit v11 on v10

--- a/solution.py
+++ b/solution.py
@@ -11,8 +11,8 @@
 BR = 512
 BLK_DEV = 8
 LANES = 128
-CHUNKS = ((0, 320), (320, 192))
-PIECES = (2, 1)
+CHUNKS = ((0, 256), (256, 160), (416, 96))
+STACKED = (True, False, False)
 WINDOWS = ((0, 256), (256, 512))
 
 
@@ -94,9 +94,7 @@
 
 def select_kernel(wide_count, start, me_ref, pairs_ref, own_ref, *refs):
     pair_count = own_ref.shape[0]
-    outs = refs[wide_count - 1 :]
-    received = refs[: wide_count - 1]
-    each, size, _ = outs[0].shape
+    *received, out_ref = refs
     owners = [pairs_ref[1, pair] >> 3 for pair in range(pair_count)]
     for pair in range(pair_count):
         shift = me_ref[0] - owners[pair]
@@ -105,26 +103,24 @@
         for before in range(pair):
             rank = rank + (owners[before] == owners[pair]).astype(jnp.int32)
 
-        out = outs[pair // each].at[pair % each]
-
         @pl.when(shift == 0)
         def _():
-            out[...] = own_ref[pair, start : start + size]
+            out_ref[pair] = own_ref[pair, start : start + out_ref.shape[1]]
 
         for other in range(1, wide_count):
 
             @pl.when(shift == other)
             def _():
-                out[...] = received[other - 1][rank]
-
-
-def select(me, pairs, own, received, start, size, pieces):
+                out_ref[pair] = received[other - 1][rank]
+
+
+def select(me, pairs, own, received, start, size):
     pair_count, _, feat = own.shape
     return pl.pallas_call(
         functools.partial(select_kernel, len(received) + 1, start),
-        out_shape=[pltpu.VMEM((pair_count // pieces, size, feat), own.dtype)] * pieces,
+        out_shape=pltpu.VMEM((pair_count, size, feat), own.dtype),
         in_specs=[smem(), smem()] + [vmem()] * (1 + len(received)),
-        out_specs=[vmem()] * pieces,
+        out_specs=vmem(),
         compiler_params=params(4),
         name="select",
     )(me, in_hbm(pairs), *[in_vmem(x) for x in (own, *received)])
@@ -171,28 +167,24 @@
     return kernel.astype(jnp.bfloat16), jnp.sum(kernel, axis=0, keepdims=True), mass
 
 
-def take_parts(refs, narrow_count, pieces):
-    parts = [refs[i * pieces : (i + 1) * pieces] for i in range(narrow_count)]
-    return parts, refs[narrow_count * pieces :]
-
-
-def of_pair(part, pair):
-    each = part[0].shape[0]
-    return part[pair // each].at[pair % each]
+def take_parts(refs, narrow_count, stacked):
+    if stacked:
+        return [ref.at[i] for ref in refs[:2] for i in range(narrow_count // 2)], refs[2:]
+    return refs[:narrow_count], refs[narrow_count:]
 
 
 def window_parts(window, narrow_count, refs):
-    rows, refs = [ref.at[i] for ref in refs[:2] for i in range(narrow_count // 2)], refs[2:]
+    rows, refs = take_parts(refs, narrow_count, True)
     chunks = []
     for chunk, _, _ in segments(window):
-        cols, refs = take_parts(refs, narrow_count, PIECES[chunk])
+        cols, refs = take_parts(refs, narrow_count, STACKED[chunk])
         chunks.append(cols)
     return rows, chunks
 
 
 def own_columns(window, chunks, pair):
     held = segments(window)
-    pieces = [of_pair(part, pair)[at : at + size] for part, (_, at, size) in zip(chunks, held)]
+    pieces = [ref[pair, at : at + size] for ref, (_, at, size) in zip(chunks, held)]
     return jnp.concatenate(pieces, axis=0) if len(pieces) > 1 else pieces[0]
 
 
@@ -245,20 +237,16 @@
     )
 
 
-def operands(parts):
-    return [piece for part in parts for piece in part]
-
-
-def first_window(rows, cols):
-    _, pair_count, _, feat = rows[0][0].shape
+def first_window(rows, cols, narrow_count):
+    _, pair_count, _, feat = rows[0].shape
     window = WINDOWS[0]
     lanes = pltpu.VMEM((pair_count, BR, LANES), jnp.float32)
     total = pltpu.VMEM((pair_count, BR, feat), jnp.float32)
-    args = operands(rows)
+    args = list(rows)
     for chunk, _, _ in segments(window):
-        args += operands(cols[chunk])
+        args += cols[chunk]
     return pl.pallas_call(
-        functools.partial(first_kernel, window, len(cols[0])),
+        functools.partial(first_kernel, window, narrow_count),
         out_shape=[lanes, lanes, total, pltpu.VMEM((pair_count, window[1]), jnp.float32)],
         in_specs=[vmem()] * len(args),
         out_specs=[vmem()] * 4,
@@ -268,8 +256,8 @@
     )(*[in_vmem(x) for x in args])
 
 
-def last_window(me, pairs, rows, cols, square, mass, sums, wide_count):
-    pair_count = rows[0][0].shape[1]
+def last_window(me, pairs, rows, cols, square, mass, sums, narrow_count, wide_count):
+    pair_count = rows[0].shape[1]
     window = WINDOWS[1]
     size = window[1] - window[0]
     by_block = pltpu.VMEM((BLK_DEV, BR), jnp.float32)
@@ -277,12 +265,12 @@
         pltpu.VMEM((pair_count, BR, size), jnp.bfloat16),
         pltpu.VMEM((pair_count, BR, LANES), jnp.float32),
     ] + [by_block] * (1 + wide_count)
-    args = operands(rows)
+    args = list(rows)
     for chunk, _, _ in segments(window):
-        args += operands(cols[chunk])
+        args += cols[chunk]
     args += [square, mass, sums]
     kernel, mass, row_sums, *shares = pl.pallas_call(
-        functools.partial(last_kernel, window, len(cols[0]), wide_count),
+        functools.partial(last_kernel, window, narrow_count, wide_count),
         out_shape=shapes,
         in_specs=[smem(), smem()] + [vmem()] * len(args),
         out_specs=[vmem()] * len(shapes),
@@ -333,11 +321,7 @@
 
 
 def mean_kernel(window, local_ref, rows_ref, kernel_ref, mass_ref, total_ref, *refs):
-    *refs, _, out_ref, part, weight, total, mass, made, sems = refs
-    chunks = []
-    for chunk, _, _ in segments(window):
-        (own,), refs = take_parts(refs, 1, PIECES[chunk])
-        chunks.append(own)
+    *chunks, _, out_ref, part, weight, total, mass, made, sems = refs
     pair_count, _, feat = rows_ref.shape
     local = [local_ref[0, pair] & 7 for pair in range(pair_count)]
 
@@ -384,7 +368,7 @@
 def means(pairs, rows, kernel, mass, total, cols, kept):
     pair_count, _, feat = rows.shape
     window = WINDOWS[1]
-    own = operands(cols[chunk][0] for chunk, _, _ in segments(window))
+    own = [cols[chunk][0] for chunk, _, _ in segments(window)]
     args = [in_vmem(x) for x in (rows, kernel, mass, total, *own)]
     return pl.pallas_call(
         functools.partial(mean_kernel, window),
@@ -434,11 +418,10 @@
 def hop(parts, step):
     count = lax.axis_size("narrow")
     perm = [(i, i ^ step) for i in range(count)]
-    return [[lax.ppermute(piece, "narrow", perm) for piece in part] for part in parts]
-
-
-def first_hops(part):
-    parts = [part]
+    return [lax.ppermute(part, "narrow", perm) for part in parts]
+
+
+def first_hops(parts):
     step = lax.axis_size("narrow") // 2
     while step > 1:
         parts = parts + hop(parts, step)
@@ -467,25 +450,29 @@
     outgoing, row_slices = pack(me, pairs, lists, blocks, capacity)
 
     def pick(received, chunk):
-        return select(me, pairs, own, received, *CHUNKS[chunk], PIECES[chunk])
-
-    rows = jnp.stack([part[0] for part in first_hops([row_slices])])
+        return select(me, pairs, own, received, *CHUNKS[chunk])
+
+    rows = jnp.stack(first_hops([row_slices]))
     rows, received, (kept, own) = fixed((rows, to_wide(outgoing[0]), keep(pairs, blocks)))
-    cols_a = first_hops(pick(received, 0))
-    rows = [[rows], *hop([[rows]], 1)]
+    cols_a = jnp.stack(first_hops([pick(received, 0)]))
+    rows = [rows, *hop([rows], 1)]
     cols_a, rows, received = fixed((cols_a, rows, to_wide(outgoing[1])))
-    cols_b = first_hops(pick(received, 1))
-    last_b = hop(cols_b[:1], 1)
-    cols_a = cols_a + hop(cols_a, 1)
-    carry = first_window(rows, [cols_a])
-    cols_b, carry = fixed((cols_b, carry))
-    cols_b = cols_b + last_b + hop(cols_b[1:], 1)
+    cols_b = first_hops([pick(received, 1)])
+    cols_a = [cols_a, *hop([cols_a], 1)]
+    cols_a, cols_b, received = fixed((cols_a, cols_b, to_wide(outgoing[2])))
+    cols_c = first_hops([pick(received, 2)])
+    last_c = hop(cols_c[:1], 1)
+    cols_b = cols_b + hop(cols_b, 1)
+    narrow_count = len(cols_b)
+    carry = first_window(rows, [cols_a], narrow_count)
+    cols_b, cols_c, carry = fixed((cols_b, cols_c, carry))
+    cols_c = cols_c + last_c + hop(cols_c[1:], 1)
     square, mass, total, sums = carry
     kernel, mass, row_sums, shares = last_window(
-        me, pairs, rows, [cols_a, cols_b], square, mass, sums, wide_count
+        me, pairs, rows, [cols_a, cols_b, cols_c], square, mass, sums, narrow_count, wide_count
     )
     came = to_wide(shares[1:])
-    mean = means(pairs, row_slices, kernel, mass, total, [cols_a, cols_b], kept)
+    mean = means(pairs, row_slices, kernel, mass, total, [cols_a, cols_b, cols_c], kept)
     weights = block_weights([row_sums, shares[0], *came])
     return weights, mean.reshape(BLK_DEV * BR, feat)
 

time: 88.1 us -> 90.6 us (1.028)
  starting transfers between devices: 28.6 us -> 30.6 us
    ppermute x12 -> x15, waiting for transfers between devices: 18.3 us -> 13.5 us  [to_wide(): lax.ppermute(piece, 'wide', [(i, (i + shift) % count) for i in range(coun...]
    ppermute x11 -> x10, waiting for transfers between devices: 20.8 us -> 25.3 us  [hop(): return [lax.ppermute(part, 'narrow', perm) for part in parts]]
    ppermute x12 -> x15, starting transfers between devices: 23.2 us -> 25.3 us  [to_wide(): lax.ppermute(piece, 'wide', [(i, (i + shift) % count) for i in range(coun...]
    pallas_call x2 -> x3, Pallas kernels: 1.62 us -> 2.41 us  [select(): pl.pallas_call(functools.partial(select_kernel, len(received) + 1, start)...]
    ppermute x11 -> x10, starting transfers between devices: 5.41 us -> 5.25 us  [hop(): return [lax.ppermute(part, 'narrow', perm) for part in parts]]
  transfers between devices with their start and end apart: 23 -> 25, of which waited for: 16 -> 11; matrix products, arithmetic and copies ran while one was open for 0% -> 0% of each run, Pallas kernels for 14% -> 15%
where the time goes in v11:
time: 90.6 us; the launch traced here: 90.1 us
  waiting for transfers between devices  38.8 us (43%)
  starting transfers between devices  30.6 us (34%)
  Pallas kernels  19.7 us (22%)
    ppermute x15, starting transfers between devices, to_wide(): lax.ppermute(piece, 'wide', [(i, (i + shift) % count) for i in range(coun...  25.3 us
    ppermute x10, waiting for transfers between devices, hop(): return [lax.ppermute(part, 'narrow', perm) for part in parts]  25.3 us
    ppermute x15, waiting for transfers between devices, to_wide(): lax.ppermute(piece, 'wide', [(i, (i + shift) % count) for i in range(coun...  13.5 us
    pallas_call x1, Pallas kernels, keep(): pl.pallas_call(keep_kernel, out_shape=[pltpu.HBM(blocks.shape, blocks.dty...  6.02 us
    ppermute x10, starting transfers between devices, hop(): return [lax.ppermute(part, 'narrow', perm) for part in parts]  5.25 us
    pallas_call x1, Pallas kernels, first_window(): pl.pallas_call(functools.partial(first_kernel, window, narrow_count), out...  3.09 us
    pallas_call x1, Pallas kernels, pack(): pl.pallas_call(functools.partial(pack_kernel, wide_count, pair_count, cap...  2.7 us
    pallas_call x1, Pallas kernels, last_window(): pl.pallas_call(functools.partial(last_kernel, window, narrow_count, wide_...  2.61 us
  transfers between devices with their start and end apart: 25, of which 11 were waited for; matrix products, arithmetic and copies ran while one was open for 0% of the time, Pallas kernels for 15%

profile of v11, /device:TPU:0, one launch (start us, length us, event | category | flops | bytes accessed | tf_op | source)
XLA Modules:
  0.0 90.1 jit_solution(8500943292390804800)
XLA Ops:
  0.6 5.1 %collective-permute-start.2 = (s32[2,4]{1,0:T(2,128)}, s32[2,4]{1,0:T(2,128)S(1)}, u32[]{:S(2)}, u32[]{:S(2)}) collective-permute-start(s32[2,4]{1,0:T(2,128)} %bitcast.17), channel_id=1, source_target_pairs={{0,12},{4,0},{8,4},{12,8},{1,13},{5,1},{9,5},{13,9},{2,14},{6,2},{... | collective-permute-start | bytes 104 | tf_op jit(solution)/shard_map/ppermute | solution.py:435
  5.7 1.0 %collective-permute-start = (s32[2,4]{1,0:T(2,128)}, s32[2,4]{1,0:T(2,128)S(1)}, u32[]{:S(2)}, u32[]{:S(2)}) collective-permute-start(s32[2,4]{1,0:T(2,128)} %bitcast.19), channel_id=1, source_target_pairs={{0,4},{4,8},{8,12},{12,0},{1,5},{5,9},{9,13},{13,1},{2,6},{6,10},{... | collective-permute-start | bytes 104 | tf_op jit(solution)/shard_map/ppermute | solution.py:435
  7.2 3.2 %collective-permute-done.1.refs_1_ = s32[2,4]{1,0:T(2,128)S(1)} collective-permute-done((s32[2,4]{1,0:T(2,128)}, s32[2,4]{1,0:T(2,128)S(1)}, u32[]{:S(2)}, u32[]{:S(2)}) %collective-permute-start.1) | collective-permute-done | bytes 64 | tf_op jit(solution)/shard_map/ppermute | solution.py:435
  10.4 0.9 %collective-permute-done.refs_0_ = s32[2,4]{1,0:T(2,128)S(1)} collective-permute-done((s32[2,4]{1,0:T(2,128)}, s32[2,4]{1,0:T(2,128)S(1)}, u32[]{:S(2)}, u32[]{:S(2)}) %collective-permute-start) | collective-permute-done | bytes 64 | tf_op jit(solution)/shard_map/ppermute | solution.py:435
  11.3 2.7 %pack.1 = (bf16[2,256,256]{2,1,0:T(8,128)(2,1)S(1)}, bf16[2,256,256]{2,1,0:T(8,128)(2,1)S(1)}, bf16[2,256,256]{2,1,0:T(8,128)(2,1)S(1)}, bf16[2,160,256]{2,1,0:T...) custom-call(s32[1]{0:T(128)} %bitcast.me_ref, ...), custom_call_target="tpu_custom_call" | custom-call | tf_op jit(solution)/shard_map/pack/pallas_call | solution.py:82
  14.0 1.6 %collective-permute-start.3 = (bf16[4,512,256]{2,1,0:T(8,128)(2,1)S(1)}, bf16[4,512,256]{2,1,0:T(8,128)(2,1)S(1)}, u32[]{:S(2)}, u32[]{:S(2)}) collective-permute-start(bf16[4,512,256]{2,1,0:T(8,128)(2,1)S(1)} %get-tuple-element.54.rows_ref), channel_id=1, source_target_pairs={{0,2},{1,3},{2,0},{3,1},{4,6},{5,7},{6,4},{7,5},{8,10},{9,11},{10,... | collective-permute-start | bytes 3145736 | tf_op jit(solution)/shard_map/ppermute | solution.py:421
  15.6 1.2 %collective-permute-start.5 = (bf16[2,256,256]{2,1,0:T(8,128)(2,1)S(1)}, bf16[2,256,256]{2,1,0:T(8,128)(2,1)S(1)}, u32[]{:S(2)}, u32[]{:S(2)}) collective-permute-start(bf16[2,256,256]{2,1,0:T(8,128)(2,1)S(1)} %get-tuple-element.56), channel_id=1, source_target_pairs={{0,8},{4,12},{8,0},{12,4},{1,9},{5,13},{9,1},{13,5},{2,10},{6,14},... | collective-permute-start | bytes 786440 | tf_op jit(solution)/shard_map/ppermute | solution.py:435
  16.7 2.9 %collective-permute-start.6 = (bf16[2,256,256]{2,1,0:T(8,128)(2,1)S(1)}, bf16[2,256,256]{2,1,0:T(8,128)(2,1)S(1)}, u32[]{:S(2)}, u32[]{:S(2)}) collective-permute-start(bf16[2,256,256]{2,1,0:T(8,128)(2,1)S(1)} %get-tuple-element.57), channel_id=1, source_target_pairs={{0,12},{4,0},{8,4},{12,8},{1,13},{5,1},{9,5},{13,9},{2,14},{6,2},{... | collective-permute-start | bytes 786440 | tf_op jit(solution)/shard_map/ppermute | solution.py:435
  19.6 6.0 %keep.1 = (bf16[8,512,256]{2,1,0:T(8,128)(2,1)}, bf16[4,512,256]{2,1,0:T(8,128)(2,1)S(1)}) custom-call(s32[2,4]{1,0:T(2,128)} %bitcast.21, bf16[8,512,256]{2,1,0:T(8,128)(2,1)} %bitcast.12, bf16[8,512,256]{2,1,0:T(8,128)(2,1)} %bitcast.13), custom_call_target="tpu_custom_call" | custom-call | tf_op jit(solution)/shard_map/keep/pallas_call | solution.py:308
  25.7 11.9 %collective-permute-done.3 = bf16[4,512,256]{2,1,0:T(8,128)(2,1)S(1)} collective-permute-done((bf16[4,512,256]{2,1,0:T(8,128)(2,1)S(1)}, bf16[4,512,256]{2,1,0:T(8,128)(2,1)S(1)}, u32[]{:S(2)}, u32[]{:S(2)}) %collective-permute-start.3) | collective-permute-done | bytes 1048608 | tf_op jit(solution)/shard_map/ppermute | solution.py:421
  37.9 0.8 select.3
  38.7 1.6 %collective-permute-start.7 = (bf16[4,256,256]{2,1,0:T(8,128)(2,1)S(1)}, bf16[4,256,256]{2,1,0:T(8,128)(2,1)S(1)}, u32[]{:S(2)}, u32[]{:S(2)}) collective-permute-start(bf16[4,256,256]{2,1,0:T(8,128)(2,1)S(1)} %select.3), channel_id=1, source_target_pairs={{0,2},{1,3},{2,0},{3,1},{4,6},{5,7},{6,4},{7,5},{8,10},{9,11},{10,... | collective-permute-start | bytes 1572872 | tf_op jit(solution)/shard_map/ppermute | solution.py:421
  40.2 1.5 %collective-permute-start.9 = (bf16[2,160,256]{2,1,0:T(8,128)(2,1)S(1)}, bf16[2,160,256]{2,1,0:T(8,128)(2,1)S(1)}, u32[]{:S(2)}, u32[]{:S(2)}) collective-permute-start(bf16[2,160,256]{2,1,0:T(8,128)(2,1)S(1)} %get-tuple-element.65), channel_id=1, source_target_pairs={{0,4},{4,8},{8,12},{12,0},{1,5},{5,9},{9,13},{13,1},{2,6},{6,10},{... | collective-permute-start | bytes 491528 | tf_op jit(solution)/shard_map/ppermute | solution.py:435
  41.7 0.8 collective-permute-start.10
  42.5 1.6 %collective-permute-start.11 = (bf16[2,160,256]{2,1,0:T(8,128)(2,1)S(1)}, bf16[2,160,256]{2,1,0:T(8,128)(2,1)S(1)}, u32[]{:S(2)}, u32[]{:S(2)}) collective-permute-start(bf16[2,160,256]{2,1,0:T(8,128)(2,1)S(1)} %get-tuple-element.67), channel_id=1, source_target_pairs={{0,12},{4,0},{8,4},{12,8},{1,13},{5,1},{9,5},{13,9},{2,14},{6,2},{... | collective-permute-start | bytes 491528 | tf_op jit(solution)/shard_map/ppermute | solution.py:435
  44.1 9.0 %collective-permute-done.7 = bf16[4,256,256]{2,1,0:T(8,128)(2,1)S(1)} collective-permute-done((bf16[4,256,256]{2,1,0:T(8,128)(2,1)S(1)}, bf16[4,256,256]{2,1,0:T(8,128)(2,1)S(1)}, u32[]{:S(2)}, u32[]{:S(2)}) %collective-permute-start.7) | collective-permute-done | bytes 524320 | tf_op jit(solution)/shard_map/ppermute | solution.py:421
  53.2 2.3 %collective-permute-done.10.refs_1_ = bf16[2,160,256]{2,1,0:T(8,128)(2,1)S(1)} collective-permute-done((bf16[2,160,256]{2,1,0:T(8,128)(2,1)S(1)}, bf16[2,160,256]{2,1,0:T(8,128)(2,1)S(1)}, u32[]{:S(2)}, u32[]{:S(2)}) %collective-permute-start.10) | collective-permute-done | bytes 163872 | tf_op jit(solution)/shard_map/ppermute | solution.py:435
  55.5 0.8 select.4.refs_2_.refs_0_
  56.9 4.0 %collective-permute-start.14 = (bf16[2,96,256]{2,1,0:T(8,128)(2,1)S(1)}, bf16[2,96,256]{2,1,0:T(8,128)(2,1)S(1)}, u32[]{:S(2)}, u32[]{:S(2)}) collective-permute-start(bf16[2,96,256]{2,1,0:T(8,128)(2,1)S(1)} %get-tuple-element.74), channel_id=1, source_target_pairs={{0,4},{4,8},{8,12},{12,0},{1,5},{5,9},{9,13},{13,1},{2,6},{6,10},{... | collective-permute-start | bytes 294920 | tf_op jit(solution)/shard_map/ppermute | solution.py:435
  60.9 1.2 %collective-permute-start.15 = (bf16[2,96,256]{2,1,0:T(8,128)(2,1)S(1)}, bf16[2,96,256]{2,1,0:T(8,128)(2,1)S(1)}, u32[]{:S(2)}, u32[]{:S(2)}) collective-permute-start(bf16[2,96,256]{2,1,0:T(8,128)(2,1)S(1)} %get-tuple-element.75), channel_id=1, source_target_pairs={{0,8},{4,12},{8,0},{12,4},{1,9},{5,13},{9,1},{13,5},{2,10},{6,14},... | collective-permute-start | bytes 294920 | tf_op jit(solution)/shard_map/ppermute | solution.py:435
  62.1 1.2 %collective-permute-start.16 = (bf16[2,96,256]{2,1,0:T(8,128)(2,1)S(1)}, bf16[2,96,256]{2,1,0:T(8,128)(2,1)S(1)}, u32[]{:S(2)}, u32[]{:S(2)}) collective-permute-start(bf16[2,96,256]{2,1,0:T(8,128)(2,1)S(1)} %get-tuple-element.76), channel_id=1, source_target_pairs={{0,12},{4,0},{8,4},{12,8},{1,13},{5,1},{9,5},{13,9},{2,14},{6,2},{... | collective-permute-start | bytes 294920 | tf_op jit(solution)/shard_map/ppermute | solution.py:435
  63.3 1.9 %collective-permute-done.14.refs_0_ = bf16[2,96,256]{2,1,0:T(8,128)(2,1)S(1)} collective-permute-done((bf16[2,96,256]{2,1,0:T(8,128)(2,1)S(1)}, bf16[2,96,256]{2,1,0:T(8,128)(2,1)S(1)}, u32[]{:S(2)}, u32[]{:S(2)}) %collective-permute-start.14) | collective-permute-done | bytes 98336 | tf_op jit(solution)/shard_map/ppermute | solution.py:435
  65.2 3.8 %collective-permute-done.15.refs_1_ = bf16[2,96,256]{2,1,0:T(8,128)(2,1)S(1)} collective-permute-done((bf16[2,96,256]{2,1,0:T(8,128)(2,1)S(1)}, bf16[2,96,256]{2,1,0:T(8,128)(2,1)S(1)}, u32[]{:S(2)}, u32[]{:S(2)}) %collective-permute-start.15) | collective-permute-done | bytes 98336 | tf_op jit(solution)/shard_map/ppermute | solution.py:435
  70.4 0.9 collective-permute-start.19
  71.3 3.1 %first_window.1 = (f32[4,512,128]{2,1,0:T(8,128)S(1)}, f32[4,512,128]{2,1,0:T(8,128)S(1)}, f32[4,512,256]{2,1,0:T(8,128)S(1)}, f32[4,256]{1,0:T(4,128)S(1)}) custom-call(bf16[2,4,512,256]{3,2,1,0:T(8,128)(2,1)S(1)} %pad_maximum_fusion.refs_0_, bf16[2,4,512,256]{3,2,1,0:T(8,128)(2,1)S(1)} %collective-permute-done.8.refs_1_, ...), custom_call_target="tpu_custom_call" | custom-call | tf_op jit(solution)/shard_map/first_window/pallas_call | solution.py:248
  74.4 3.0 %collective-permute-done.19.refs_7_ = bf16[4,96,256]{2,1,0:T(8,128)(2,1)S(1)} collective-permute-done((bf16[4,96,256]{2,1,0:T(8,128)(2,1)S(1)}, bf16[4,96,256]{2,1,0:T(8,128)(2,1)S(1)}, u32[]{:S(2)}, u32[]{:S(2)}) %collective-permute-start.19) | collective-permute-done | bytes 196640 | tf_op jit(solution)/shard_map/ppermute | solution.py:421
  77.4 1.4 %collective-permute-done.21.refs_9_ = bf16[4,96,256]{2,1,0:T(8,128)(2,1)S(1)} collective-permute-done((bf16[4,96,256]{2,1,0:T(8,128)(2,1)S(1)}, bf16[4,96,256]{2,1,0:T(8,128)(2,1)S(1)}, u32[]{:S(2)}, u32[]{:S(2)}) %collective-permute-start.21) | collective-permute-done | bytes 196640 | tf_op jit(solution)/shard_map/ppermute | solution.py:421
  78.8 2.6 %last_window.1 = (bf16[4,512,256]{2,1,0:T(8,128)(2,1)S(1)}, f32[4,512,128]{2,1,0:T(8,128)S(1)}, f32[8,512]{1,0:T(8,128)S(1)}, f32[8,512]{1,0:T(8,128)S(1)}, f32[...) custom-call(s32[1]{0:T(128)} %bitcast.me_ref, s32[2,4]{1,0:T(2,128)} %bitcast.25, ...), custom_call_target="tpu_custom_call" | custom-call | flops 1073741824 | bytes 8388608 | tf_op jit(solution)/shard_map/last_window/pallas_call | solution.py:272
  81.4 2.6 %collective-permute-start.22 = (f32[8,512]{1,0:T(8,128)S(1)}, f32[8,512]{1,0:T(8,128)S(1)}, u32[]{:S(2)}, u32[]{:S(2)}) collective-permute-start(f32[8,512]{1,0:T(8,128)S(1)} %get-tuple-element.99), channel_id=1, source_target_pairs={{0,4},{4,8},{8,12},{12,0},{1,5},{5,9},{9,13},{13,1},{2,6},{6,10},{... | collective-permute-start | bytes 49160 | tf_op jit(solution)/shard_map/ppermute | solution.py:435
  84.0 1.8 %collective-permute-start.23 = (f32[8,512]{1,0:T(8,128)S(1)}, f32[8,512]{1,0:T(8,128)S(1)}, u32[]{:S(2)}, u32[]{:S(2)}) collective-permute-start(f32[8,512]{1,0:T(8,128)S(1)} %get-tuple-element.100), channel_id=1, source_target_pairs={{0,8},{4,12},{8,0},{12,4},{1,9},{5,13},{9,1},{13,5},{2,10},{6,14},... | collective-permute-start | bytes 49160 | tf_op jit(solution)/shard_map/ppermute | solution.py:435
  86.4 2.3 %means.1 = bf16[8,512,256]{2,1,0:T(8,128)(2,1)} custom-call(s32[2,4]{1,0:T(2,128)} %bitcast.26, bf16[4,512,256]{2,1,0:T(8,128)(2,1)S(1)} %get-tuple-element.54.rows_ref, bf16[4,512,256]{2,1,0:T(8,128)(2,1)S(1)} %get-tuple-element.102.kernel_ref, f32[4,512,128]{2,1,0:T(8,128)S(1)} %get-tuple-element.103.mass_ref, ...), custom_call_target="tpu_custom_call", output_to_operand_aliasing={{}: (7, {})} | custom-call | flops 536870912 | bytes 8388608 | tf_op jit(solution)/shard_map/means/pallas_call | solution.py:373
  88.7 0.8 collective-permute-done.24.refs_4_
  (29 shorter events, 4.1 us)
Async XLA Ops:
  0.6 6.6 %collective-permute-start.2 = (s32[2,4]{1,0:T(2,128)}, s32[2,4]{1,0:T(2,128)S(1)}, u32[]{:S(2)}, u32[]{:S(2)}) collective-permute-start(s32[2,4]{1,0:T(2,128)} %bitcast.17), channel_id=1, source_target_pairs={{0,12},{4,0},{8,4},{12,8},{1,13},{5,1},{9,5},{13,9},{2,14},{6,2},{... | collective-permute-start | bytes 104 | tf_op jit(solution)/shard_map/ppermute | solution.py:435
  5.7 4.7 %collective-permute-start.1 = (s32[2,4]{1,0:T(2,128)}, s32[2,4]{1,0:T(2,128)S(1)}, u32[]{:S(2)}, u32[]{:S(2)}) collective-permute-start(s32[2,4]{1,0:T(2,128)} %bitcast.18), channel_id=1, source_target_pairs={{0,8},{4,12},{8,0},{12,4},{1,9},{5,13},{9,1},{13,5},{2,10},{6,14},... | collective-permute-start | bytes 104 | tf_op jit(solution)/shard_map/ppermute | solution.py:435
  5.7 5.6 %collective-permute-start = (s32[2,4]{1,0:T(2,128)}, s32[2,4]{1,0:T(2,128)S(1)}, u32[]{:S(2)}, u32[]{:S(2)}) collective-permute-start(s32[2,4]{1,0:T(2,128)} %bitcast.19), channel_id=1, source_target_pairs={{0,4},{4,8},{8,12},{12,0},{1,5},{5,9},{9,13},{13,1},{2,6},{6,10},{... | collective-permute-start | bytes 104 | tf_op jit(solution)/shard_map/ppermute | solution.py:435
  14.0 23.5 %collective-permute-start.3 = (bf16[4,512,256]{2,1,0:T(8,128)(2,1)S(1)}, bf16[4,512,256]{2,1,0:T(8,128)(2,1)S(1)}, u32[]{:S(2)}, u32[]{:S(2)}) collective-permute-start(bf16[4,512,256]{2,1,0:T(8,128)(2,1)S(1)} %get-tuple-element.54.rows_ref), channel_id=1, source_target_pairs={{0,2},{1,3},{2,0},{3,1},{4,6},{5,7},{6,4},{7,5},{8,10},{9,11},{10,... | collective-permute-start | bytes 3145736 | tf_op jit(solution)/shard_map/ppermute | solution.py:421
  15.6 22.2 %collective-permute-start.4 = (bf16[2,256,256]{2,1,0:T(8,128)(2,1)S(1)}, bf16[2,256,256]{2,1,0:T(8,128)(2,1)S(1)}, u32[]{:S(2)}, u32[]{:S(2)}) collective-permute-start(bf16[2,256,256]{2,1,0:T(8,128)(2,1)S(1)} %get-tuple-element.55), channel_id=1, source_target_pairs={{0,4},{4,8},{8,12},{12,0},{1,5},{5,9},{9,13},{13,1},{2,6},{6,10},{... | collective-permute-start | bytes 786440 | tf_op jit(solution)/shard_map/ppermute | solution.py:435
  15.6 22.2 %collective-permute-start.5 = (bf16[2,256,256]{2,1,0:T(8,128)(2,1)S(1)}, bf16[2,256,256]{2,1,0:T(8,128)(2,1)S(1)}, u32[]{:S(2)}, u32[]{:S(2)}) collective-permute-start(bf16[2,256,256]{2,1,0:T(8,128)(2,1)S(1)} %get-tuple-element.56), channel_id=1, source_target_pairs={{0,8},{4,12},{8,0},{12,4},{1,9},{5,13},{9,1},{13,5},{2,10},{6,14},... | collective-permute-start | bytes 786440 | tf_op jit(solution)/shard_map/ppermute | solution.py:435
  16.7 21.0 %collective-permute-start.6 = (bf16[2,256,256]{2,1,0:T(8,128)(2,1)S(1)}, bf16[2,256,256]{2,1,0:T(8,128)(2,1)S(1)}, u32[]{:S(2)}, u32[]{:S(2)}) collective-permute-start(bf16[2,256,256]{2,1,0:T(8,128)(2,1)S(1)} %get-tuple-element.57), channel_id=1, source_target_pairs={{0,12},{4,0},{8,4},{12,8},{1,13},{5,1},{9,5},{13,9},{2,14},{6,2},{... | collective-permute-start | bytes 786440 | tf_op jit(solution)/shard_map/ppermute | solution.py:435
  37.8 17.7 %collective-permute-start.8 = (bf16[2,4,512,256]{3,2,1,0:T(8,128)(2,1)S(1)}, bf16[2,4,512,256]{3,2,1,0:T(8,128)(2,1)S(1)}, u32[]{:S(2)}, u32[]{:S(2)}) collective-permute-start(bf16[2,4,512,256]{3,2,1,0:T(8,128)(2,1)S(1)} %pad_maximum_fusion.refs_0_), channel_id=1, source_target_pairs={{0,1},{1,0},{2,3},{3,2},{4,5},{5,4},{6,7},{7,6},{8,9},{9,8},{10,11... | collective-permute-start | bytes 6291464 | tf_op jit(solution)/shard_map/ppermute | solution.py:421
  38.7 14.4 %collective-permute-start.7 = (bf16[4,256,256]{2,1,0:T(8,128)(2,1)S(1)}, bf16[4,256,256]{2,1,0:T(8,128)(2,1)S(1)}, u32[]{:S(2)}, u32[]{:S(2)}) collective-permute-start(bf16[4,256,256]{2,1,0:T(8,128)(2,1)S(1)} %select.3), channel_id=1, source_target_pairs={{0,2},{1,3},{2,0},{3,1},{4,6},{5,7},{6,4},{7,5},{8,10},{9,11},{10,... | collective-permute-start | bytes 1572872 | tf_op jit(solution)/shard_map/ppermute | solution.py:421
  40.2 12.9 %collective-permute-start.9 = (bf16[2,160,256]{2,1,0:T(8,128)(2,1)S(1)}, bf16[2,160,256]{2,1,0:T(8,128)(2,1)S(1)}, u32[]{:S(2)}, u32[]{:S(2)}) collective-permute-start(bf16[2,160,256]{2,1,0:T(8,128)(2,1)S(1)} %get-tuple-element.65), channel_id=1, source_target_pairs={{0,4},{4,8},{8,12},{12,0},{1,5},{5,9},{9,13},{13,1},{2,6},{6,10},{... | collective-permute-start | bytes 491528 | tf_op jit(solution)/shard_map/ppermute | solution.py:435
  41.7 13.8 %collective-permute-start.10 = (bf16[2,160,256]{2,1,0:T(8,128)(2,1)S(1)}, bf16[2,160,256]{2,1,0:T(8,128)(2,1)S(1)}, u32[]{:S(2)}, u32[]{:S(2)}) collective-permute-start(bf16[2,160,256]{2,1,0:T(8,128)(2,1)S(1)} %get-tuple-element.66), channel_id=1, source_target_pairs={{0,8},{4,12},{8,0},{12,4},{1,9},{5,13},{9,1},{13,5},{2,10},{6,14},... | collective-permute-start | bytes 491528 | tf_op jit(solution)/shard_map/ppermute | solution.py:435
  42.5 13.0 %collective-permute-start.11 = (bf16[2,160,256]{2,1,0:T(8,128)(2,1)S(1)}, bf16[2,160,256]{2,1,0:T(8,128)(2,1)S(1)}, u32[]{:S(2)}, u32[]{:S(2)}) collective-permute-start(bf16[2,160,256]{2,1,0:T(8,128)(2,1)S(1)} %get-tuple-element.67), channel_id=1, source_target_pairs={{0,12},{4,0},{8,4},{12,8},{1,13},{5,1},{9,5},{13,9},{2,14},{6,2},{... | collective-permute-start | bytes 491528 | tf_op jit(solution)/shard_map/ppermute | solution.py:435
  55.5 13.5 %collective-permute-start.12 = (bf16[2,4,256,256]{3,2,1,0:T(8,128)(2,1)S(1)}, bf16[2,4,256,256]{3,2,1,0:T(8,128)(2,1)S(1)}, u32[]{:S(2)}, u32[]{:S(2)}) collective-permute-start(bf16[2,4,256,256]{3,2,1,0:T(8,128)(2,1)S(1)} %pad_maximum_fusion.1.refs_2_), channel_id=1, source_target_pairs={{0,1},{1,0},{2,3},{3,2},{4,5},{5,4},{6,7},{7,6},{8,9},{9,8},{10,11... | collective-permute-start | bytes 3145736 | tf_op jit(solution)/shard_map/ppermute | solution.py:421
  56.3 12.7 %collective-permute-start.13 = (bf16[4,160,256]{2,1,0:T(8,128)(2,1)S(1)}, bf16[4,160,256]{2,1,0:T(8,128)(2,1)S(1)}, u32[]{:S(2)}, u32[]{:S(2)}) collective-permute-start(bf16[4,160,256]{2,1,0:T(8,128)(2,1)S(1)} %select.4.refs_2_.refs_0_), channel_id=1, source_target_pairs={{0,2},{1,3},{2,0},{3,1},{4,6},{5,7},{6,4},{7,5},{8,10},{9,11},{10,... | collective-permute-start | bytes 983048 | tf_op jit(solution)/shard_map/ppermute | solution.py:421
  56.9 8.3 %collective-permute-start.14 = (bf16[2,96,256]{2,1,0:T(8,128)(2,1)S(1)}, bf16[2,96,256]{2,1,0:T(8,128)(2,1)S(1)}, u32[]{:S(2)}, u32[]{:S(2)}) collective-permute-start(bf16[2,96,256]{2,1,0:T(8,128)(2,1)S(1)} %get-tuple-element.74), channel_id=1, source_target_pairs={{0,4},{4,8},{8,12},{12,0},{1,5},{5,9},{9,13},{13,1},{2,6},{6,10},{... | collective-permute-start | bytes 294920 | tf_op jit(solution)/shard_map/ppermute | solution.py:435
  60.9 8.1 %collective-permute-start.15 = (bf16[2,96,256]{2,1,0:T(8,128)(2,1)S(1)}, bf16[2,96,256]{2,1,0:T(8,128)(2,1)S(1)}, u32[]{:S(2)}, u32[]{:S(2)}) collective-permute-start(bf16[2,96,256]{2,1,0:T(8,128)(2,1)S(1)} %get-tuple-element.75), channel_id=1, source_target_pairs={{0,8},{4,12},{8,0},{12,4},{1,9},{5,13},{9,1},{13,5},{2,10},{6,14},... | collective-permute-start | bytes 294920 | tf_op jit(solution)/shard_map/ppermute | solution.py:435
  62.1 6.9 %collective-permute-start.16 = (bf16[2,96,256]{2,1,0:T(8,128)(2,1)S(1)}, bf16[2,96,256]{2,1,0:T(8,128)(2,1)S(1)}, u32[]{:S(2)}, u32[]{:S(2)}) collective-permute-start(bf16[2,96,256]{2,1,0:T(8,128)(2,1)S(1)} %get-tuple-element.76), channel_id=1, source_target_pairs={{0,12},{4,0},{8,4},{12,8},{1,13},{5,1},{9,5},{13,9},{2,14},{6,2},{... | collective-permute-start | bytes 294920 | tf_op jit(solution)/shard_map/ppermute | solution.py:435
  69.1 8.3 %collective-permute-start.17 = (bf16[4,160,256]{2,1,0:T(8,128)(2,1)S(1)}, bf16[4,160,256]{2,1,0:T(8,128)(2,1)S(1)}, u32[]{:S(2)}, u32[]{:S(2)}) collective-permute-start(bf16[4,160,256]{2,1,0:T(8,128)(2,1)S(1)} %select.4.refs_2_.refs_0_), channel_id=1, source_target_pairs={{0,1},{1,0},{2,3},{3,2},{4,5},{5,4},{6,7},{7,6},{8,9},{9,8},{10,11... | collective-permute-start | bytes 983048 | tf_op jit(solution)/shard_map/ppermute | solution.py:421
  69.1 8.3 %collective-permute-start.18 = (bf16[4,160,256]{2,1,0:T(8,128)(2,1)S(1)}, bf16[4,160,256]{2,1,0:T(8,128)(2,1)S(1)}, u32[]{:S(2)}, u32[]{:S(2)}) collective-permute-start(bf16[4,160,256]{2,1,0:T(8,128)(2,1)S(1)} %collective-permute-done.13.refs_3_), channel_id=1, source_target_pairs={{0,1},{1,0},{2,3},{3,2},{4,5},{5,4},{6,7},{7,6},{8,9},{9,8},{10,11... | collective-permute-start | bytes 983048 | tf_op jit(solution)/shard_map/ppermute | solution.py:421
  70.4 7.0 %collective-permute-start.19 = (bf16[4,96,256]{2,1,0:T(8,128)(2,1)S(1)}, bf16[4,96,256]{2,1,0:T(8,128)(2,1)S(1)}, u32[]{:S(2)}, u32[]{:S(2)}) collective-permute-start(bf16[4,96,256]{2,1,0:T(8,128)(2,1)S(1)} %select.5.refs_6_.refs_1_), channel_id=1, source_target_pairs={{0,2},{1,3},{2,0},{3,1},{4,6},{5,7},{6,4},{7,5},{8,10},{9,11},{10,... | collective-permute-start | bytes 589832 | tf_op jit(solution)/shard_map/ppermute | solution.py:421
  71.3 6.1 %collective-permute-start.20 = (bf16[4,96,256]{2,1,0:T(8,128)(2,1)S(1)}, bf16[4,96,256]{2,1,0:T(8,128)(2,1)S(1)}, u32[]{:S(2)}, u32[]{:S(2)}) collective-permute-start(bf16[4,96,256]{2,1,0:T(8,128)(2,1)S(1)} %select.5.refs_6_.refs_1_), channel_id=1, source_target_pairs={{0,1},{1,0},{2,3},{3,2},{4,5},{5,4},{6,7},{7,6},{8,9},{9,8},{10,11... | collective-permute-start | bytes 589832 | tf_op jit(solution)/shard_map/ppermute | solution.py:421
  77.4 1.4 %collective-permute-start.21 = (bf16[4,96,256]{2,1,0:T(8,128)(2,1)S(1)}, bf16[4,96,256]{2,1,0:T(8,128)(2,1)S(1)}, u32[]{:S(2)}, u32[]{:S(2)}) collective-permute-start(bf16[4,96,256]{2,1,0:T(8,128)(2,1)S(1)} %collective-permute-done.19.refs_7_), channel_id=1, source_target_pairs={{0,1},{1,0},{2,3},{3,2},{4,5},{5,4},{6,7},{7,6},{8,9},{9,8},{10,11... | collective-permute-start | bytes 589832 | tf_op jit(solution)/shard_map/ppermute | solution.py:421
  81.4 7.3 %collective-permute-start.22 = (f32[8,512]{1,0:T(8,128)S(1)}, f32[8,512]{1,0:T(8,128)S(1)}, u32[]{:S(2)}, u32[]{:S(2)}) collective-permute-start(f32[8,512]{1,0:T(8,128)S(1)} %get-tuple-element.99), channel_id=1, source_target_pairs={{0,4},{4,8},{8,12},{12,0},{1,5},{5,9},{9,13},{13,1},{2,6},{6,10},{... | collective-permute-start | bytes 49160 | tf_op jit(solution)/shard_map/ppermute | solution.py:435
  84.0 4.7 %collective-permute-start.23 = (f32[8,512]{1,0:T(8,128)S(1)}, f32[8,512]{1,0:T(8,128)S(1)}, u32[]{:S(2)}, u32[]{:S(2)}) collective-permute-start(f32[8,512]{1,0:T(8,128)S(1)} %get-tuple-element.100), channel_id=1, source_target_pairs={{0,8},{4,12},{8,0},{12,4},{1,9},{5,13},{9,1},{13,5},{2,10},{6,14},... | collective-permute-start | bytes 49160 | tf_op jit(solution)/shard_map/ppermute | solution.py:435
  85.8 3.7 %collective-permute-start.24 = (f32[8,512]{1,0:T(8,128)S(1)}, f32[8,512]{1,0:T(8,128)S(1)}, u32[]{:S(2)}, u32[]{:S(2)}) collective-permute-start(f32[8,512]{1,0:T(8,128)S(1)} %get-tuple-element.101), channel_id=1, source_target_pairs={{0,12},{4,0},{8,4},{12,8},{1,13},{5,1},{9,5},{13,9},{2,14},{6,2},{... | collective-permute-start | bytes 49160 | tf_op jit(solution)/shard_map/ppermute | solution.py:435

commit v12 on v10

--- a/solution.py
+++ b/solution.py
@@ -52,7 +52,7 @@
 
     for chunk, (start, size) in enumerate(CHUNKS):
         for shift in range(1, wide_count):
-            asked = lists[wide_count - shift - 1]
+            asked = lists[shift - 1]
             picks = [jnp.int32(0)] * capacity
             count = jnp.int32(0)
             for pair in range(pair_count):
@@ -462,7 +462,7 @@
     capacity = max(2, 2 * pair_count // wide_count)
     feat = embeddings.shape[1]
     blocks = embeddings.reshape(BLK_DEV, BR, feat)
-    lists = to_wide([pairs] * (wide_count - 1))
+    lists = to_wide([pairs] * (wide_count - 1))[::-1]
     fixed = lax.optimization_barrier
     outgoing, row_slices = pack(me, pairs, lists, blocks, capacity)
 

time: 88.1 us -> 87.4 us (level)
  waiting for transfers between devices: 39.1 us -> 37.1 us
  starting transfers between devices: 28.6 us -> 29.5 us
    ppermute x12, waiting for transfers between devices: 18.3 us -> 16.2 us  [to_wide(): lax.ppermute(piece, 'wide', [(i, (i + shift) % count) for i in range(coun...]
    ppermute x12, starting transfers between devices: 23.2 us -> 24.1 us  [to_wide(): lax.ppermute(piece, 'wide', [(i, (i + shift) % count) for i in range(coun...]
  transfers between devices with their start and end apart: 23 -> 23, of which waited for: 16 -> 15; matrix products, arithmetic and copies ran while one was open for 0% -> 0% of each run, Pallas kernels for 14% -> 14%
where the time goes in v12:
time: 87.4 us; the launch traced here: 86.9 us
  waiting for transfers between devices  37.1 us (42%)
  starting transfers between devices  29.5 us (34%)
  Pallas kernels  19.4 us (22%)
    ppermute x12, starting transfers between devices, to_wide(): lax.ppermute(piece, 'wide', [(i, (i + shift) % count) for i in range(coun...  24.1 us
    ppermute x11, waiting for transfers between devices, hop(): lax.ppermute(piece, 'narrow', perm)  20.9 us
    ppermute x12, waiting for transfers between devices, to_wide(): lax.ppermute(piece, 'wide', [(i, (i + shift) % count) for i in range(coun...  16.2 us
    pallas_call x1, Pallas kernels, keep(): pl.pallas_call(keep_kernel, out_shape=[pltpu.HBM(blocks.shape, blocks.dty...  6.02 us
    ppermute x11, starting transfers between devices, hop(): lax.ppermute(piece, 'narrow', perm)  5.41 us
    pallas_call x1, Pallas kernels, first_window(): pl.pallas_call(functools.partial(first_kernel, window, len(cols[0])), out...  3.1 us
    pallas_call x1, Pallas kernels, pack(): pl.pallas_call(functools.partial(pack_kernel, wide_count, pair_count, cap...  3.04 us
    pallas_call x1, Pallas kernels, last_window(): pl.pallas_call(functools.partial(last_kernel, window, len(cols[0]), wide_...  2.65 us
  transfers between devices with their start and end apart: 23, of which 15 were waited for; matrix products, arithmetic and copies ran while one was open for 0% of the time, Pallas kernels for 14%

profile of v12, /device:TPU:0, one launch (start us, length us, event | category | flops | bytes accessed | tf_op | source)
XLA Modules:
  0.0 86.9 jit_solution(11112923831817167550)
XLA Ops:
  0.6 3.1 %collective-permute-start.2 = (s32[2,4]{1,0:T(2,128)}, s32[2,4]{1,0:T(2,128)S(1)}, u32[]{:S(2)}, u32[]{:S(2)}) collective-permute-start(s32[2,4]{1,0:T(2,128)} %bitcast.13), channel_id=1, source_target_pairs={{0,4},{4,8},{8,12},{12,0},{1,5},{5,9},{9,13},{13,1},{2,6},{6,10},{... | collective-permute-start | bytes 104 | tf_op jit(solution)/shard_map/ppermute | solution.py:452
  3.7 2.6 %collective-permute-start.1 = (s32[2,4]{1,0:T(2,128)}, s32[2,4]{1,0:T(2,128)S(1)}, u32[]{:S(2)}, u32[]{:S(2)}) collective-permute-start(s32[2,4]{1,0:T(2,128)} %bitcast.14), channel_id=1, source_target_pairs={{0,8},{4,12},{8,0},{12,4},{1,9},{5,13},{9,1},{13,5},{2,10},{6,14},... | collective-permute-start | bytes 104 | tf_op jit(solution)/shard_map/ppermute | solution.py:452
  6.3 1.3 %collective-permute-start = (s32[2,4]{1,0:T(2,128)}, s32[2,4]{1,0:T(2,128)S(1)}, u32[]{:S(2)}, u32[]{:S(2)}) collective-permute-start(s32[2,4]{1,0:T(2,128)} %bitcast.15), channel_id=1, source_target_pairs={{0,12},{4,0},{8,4},{12,8},{1,13},{5,1},{9,5},{13,9},{2,14},{6,2},{... | collective-permute-start | bytes 104 | tf_op jit(solution)/shard_map/ppermute | solution.py:452
  7.6 0.7 collective-permute-done.1.refs_1_
  8.4 1.7 %collective-permute-done.refs_0_ = s32[2,4]{1,0:T(2,128)S(1)} collective-permute-done((s32[2,4]{1,0:T(2,128)}, s32[2,4]{1,0:T(2,128)S(1)}, u32[]{:S(2)}, u32[]{:S(2)}) %collective-permute-start) | collective-permute-done | bytes 64 | tf_op jit(solution)/shard_map/ppermute | solution.py:452
  10.1 3.0 %pack.1 = (bf16[2,320,256]{2,1,0:T(8,128)(2,1)S(1)}, bf16[2,320,256]{2,1,0:T(8,128)(2,1)S(1)}, bf16[2,320,256]{2,1,0:T(8,128)(2,1)S(1)}, bf16[2,192,256]{2,1,0:T...) custom-call(s32[1]{0:T(128)} %bitcast.me_ref, ...), custom_call_target="tpu_custom_call" | custom-call | tf_op jit(solution)/shard_map/pack/pallas_call | solution.py:82
  13.1 1.6 %collective-permute-start.3 = (bf16[4,512,256]{2,1,0:T(8,128)(2,1)S(1)}, bf16[4,512,256]{2,1,0:T(8,128)(2,1)S(1)}, u32[]{:S(2)}, u32[]{:S(2)}) collective-permute-start(bf16[4,512,256]{2,1,0:T(8,128)(2,1)S(1)} %get-tuple-element.45.rows_ref), channel_id=1, source_target_pairs={{0,2},{1,3},{2,0},{3,1},{4,6},{5,7},{6,4},{7,5},{8,10},{9,11},{10,... | collective-permute-start | bytes 3145736 | tf_op jit(solution)/shard_map/ppermute | solution.py:437
  14.7 3.3 %collective-permute-start.5 = (bf16[2,320,256]{2,1,0:T(8,128)(2,1)S(1)}, bf16[2,320,256]{2,1,0:T(8,128)(2,1)S(1)}, u32[]{:S(2)}, u32[]{:S(2)}) collective-permute-start(bf16[2,320,256]{2,1,0:T(8,128)(2,1)S(1)} %get-tuple-element.47), channel_id=1, source_target_pairs={{0,8},{4,12},{8,0},{12,4},{1,9},{5,13},{9,1},{13,5},{2,10},{6,14},... | collective-permute-start | bytes 983048 | tf_op jit(solution)/shard_map/ppermute | solution.py:452
  18.5 6.0 %keep.1 = (bf16[8,512,256]{2,1,0:T(8,128)(2,1)}, bf16[4,512,256]{2,1,0:T(8,128)(2,1)S(1)}) custom-call(s32[2,4]{1,0:T(2,128)} %bitcast.17, bf16[8,512,256]{2,1,0:T(8,128)(2,1)} %bitcast.9, bf16[8,512,256]{2,1,0:T(8,128)(2,1)} %bitcast.10), custom_call_target="tpu_custom_call" | custom-call | tf_op jit(solution)/shard_map/keep/pallas_call | solution.py:320
  24.5 12.1 %collective-permute-done.3 = bf16[4,512,256]{2,1,0:T(8,128)(2,1)S(1)} collective-permute-done((bf16[4,512,256]{2,1,0:T(8,128)(2,1)S(1)}, bf16[4,512,256]{2,1,0:T(8,128)(2,1)S(1)}, u32[]{:S(2)}, u32[]{:S(2)}) %collective-permute-start.3) | collective-permute-done | bytes 1048608 | tf_op jit(solution)/shard_map/ppermute | solution.py:437
  36.9 1.6 %collective-permute-done.5.refs_1_ = bf16[2,320,256]{2,1,0:T(8,128)(2,1)S(1)} collective-permute-done((bf16[2,320,256]{2,1,0:T(8,128)(2,1)S(1)}, bf16[2,320,256]{2,1,0:T(8,128)(2,1)S(1)}, u32[]{:S(2)}, u32[]{:S(2)}) %collective-permute-start.5) | collective-permute-done | bytes 327712 | tf_op jit(solution)/shard_map/ppermute | solution.py:452
  38.5 6.6 %collective-permute-start.10 = (bf16[2,192,256]{2,1,0:T(8,128)(2,1)S(1)}, bf16[2,192,256]{2,1,0:T(8,128)(2,1)S(1)}, u32[]{:S(2)}, u32[]{:S(2)}) collective-permute-start(bf16[2,192,256]{2,1,0:T(8,128)(2,1)S(1)} %get-tuple-element.58), channel_id=1, source_target_pairs={{0,4},{4,8},{8,12},{12,0},{1,5},{5,9},{9,13},{13,1},{2,6},{6,10},{... | collective-permute-start | bytes 589832 | tf_op jit(solution)/shard_map/ppermute | solution.py:452
  45.1 0.8 select.2
  46.0 0.6 collective-permute-start.7
  46.6 1.5 %collective-permute-start.8 = (bf16[2,320,256]{2,1,0:T(8,128)(2,1)S(1)}, bf16[2,320,256]{2,1,0:T(8,128)(2,1)S(1)}, u32[]{:S(2)}, u32[]{:S(2)}) collective-permute-start(bf16[2,320,256]{2,1,0:T(8,128)(2,1)S(1)} %get-tuple-element.64.refs_3_.refs_1_), channel_id=1, source_target_pairs={{0,2},{1,3},{2,0},{3,1},{4,6},{5,7},{6,4},{7,5},{8,10},{9,11},{10,... | collective-permute-start | bytes 983048 | tf_op jit(solution)/shard_map/ppermute | solution.py:437
  48.5 2.1 %collective-permute-done.10.refs_0_ = bf16[2,192,256]{2,1,0:T(8,128)(2,1)S(1)} collective-permute-done((bf16[2,192,256]{2,1,0:T(8,128)(2,1)S(1)}, bf16[2,192,256]{2,1,0:T(8,128)(2,1)S(1)}, u32[]{:S(2)}, u32[]{:S(2)}) %collective-permute-start.10) | collective-permute-done | bytes 196640 | tf_op jit(solution)/shard_map/ppermute | solution.py:452
  50.6 1.7 %collective-permute-start.12 = (bf16[2,192,256]{2,1,0:T(8,128)(2,1)S(1)}, bf16[2,192,256]{2,1,0:T(8,128)(2,1)S(1)}, u32[]{:S(2)}, u32[]{:S(2)}) collective-permute-start(bf16[2,192,256]{2,1,0:T(8,128)(2,1)S(1)} %get-tuple-element.60), channel_id=1, source_target_pairs={{0,12},{4,0},{8,4},{12,8},{1,13},{5,1},{9,5},{13,9},{2,14},{6,2},{... | collective-permute-start | bytes 589832 | tf_op jit(solution)/shard_map/ppermute | solution.py:452
  52.3 7.1 %collective-permute-done.11.refs_1_ = bf16[2,192,256]{2,1,0:T(8,128)(2,1)S(1)} collective-permute-done((bf16[2,192,256]{2,1,0:T(8,128)(2,1)S(1)}, bf16[2,192,256]{2,1,0:T(8,128)(2,1)S(1)}, u32[]{:S(2)}, u32[]{:S(2)}) %collective-permute-start.11) | collective-permute-done | bytes 196640 | tf_op jit(solution)/shard_map/ppermute | solution.py:452
  59.5 2.0 %collective-permute-done.12.refs_2_ = bf16[2,192,256]{2,1,0:T(8,128)(2,1)S(1)} collective-permute-done((bf16[2,192,256]{2,1,0:T(8,128)(2,1)S(1)}, bf16[2,192,256]{2,1,0:T(8,128)(2,1)S(1)}, u32[]{:S(2)}, u32[]{:S(2)}) %collective-permute-start.12) | collective-permute-done | bytes 196640 | tf_op jit(solution)/shard_map/ppermute | solution.py:452
  61.5 1.4 %collective-permute-done.8.refs_5_ = bf16[2,320,256]{2,1,0:T(8,128)(2,1)S(1)} collective-permute-done((bf16[2,320,256]{2,1,0:T(8,128)(2,1)S(1)}, bf16[2,320,256]{2,1,0:T(8,128)(2,1)S(1)}, u32[]{:S(2)}, u32[]{:S(2)}) %collective-permute-start.8) | collective-permute-done | bytes 327712 | tf_op jit(solution)/shard_map/ppermute | solution.py:437
  62.9 0.8 select.3.refs_10_.refs_2_
  63.7 0.6 collective-permute-start.17
  65.3 0.6 collective-permute-done.15.refs_8_
  67.3 3.1 %first_window.1 = (f32[4,512,128]{2,1,0:T(8,128)S(1)}, f32[4,512,128]{2,1,0:T(8,128)S(1)}, f32[4,512,256]{2,1,0:T(8,128)S(1)}, f32[4,256]{1,0:T(4,128)S(1)}) custom-call(bf16[2,4,512,256]{3,2,1,0:T(8,128)(2,1)S(1)} %pad_maximum_fusion.refs_0_, bf16[2,4,512,256]{3,2,1,0:T(8,128)(2,1)S(1)} %collective-permute-done.9.refs_1_, ...), custom_call_target="tpu_custom_call" | custom-call | tf_op jit(solution)/shard_map/first_window/pallas_call | solution.py:260
  70.4 3.8 %collective-permute-done.17.refs_11_ = bf16[4,192,256]{2,1,0:T(8,128)(2,1)S(1)} collective-permute-done((bf16[4,192,256]{2,1,0:T(8,128)(2,1)S(1)}, bf16[4,192,256]{2,1,0:T(8,128)(2,1)S(1)}, u32[]{:S(2)}, u32[]{:S(2)}) %collective-permute-start.17) | collective-permute-done | bytes 393248 | tf_op jit(solution)/shard_map/ppermute | solution.py:437
  74.2 1.7 %collective-permute-done.19.refs_13_ = bf16[4,192,256]{2,1,0:T(8,128)(2,1)S(1)} collective-permute-done((bf16[4,192,256]{2,1,0:T(8,128)(2,1)S(1)}, bf16[4,192,256]{2,1,0:T(8,128)(2,1)S(1)}, u32[]{:S(2)}, u32[]{:S(2)}) %collective-permute-start.19) | collective-permute-done | bytes 393248 | tf_op jit(solution)/shard_map/ppermute | solution.py:437
  75.9 2.6 %last_window.1 = (bf16[4,512,256]{2,1,0:T(8,128)(2,1)S(1)}, f32[4,512,128]{2,1,0:T(8,128)S(1)}, f32[8,512]{1,0:T(8,128)S(1)}, f32[8,512]{1,0:T(8,128)S(1)}, f32[...) custom-call(s32[1]{0:T(128)} %bitcast.me_ref, s32[2,4]{1,0:T(2,128)} %bitcast.20, ...), custom_call_target="tpu_custom_call" | custom-call | flops 1073741824 | bytes 8388608 | tf_op jit(solution)/shard_map/last_window/pallas_call | solution.py:284
  78.6 2.0 %collective-permute-start.20 = (f32[8,512]{1,0:T(8,128)S(1)}, f32[8,512]{1,0:T(8,128)S(1)}, u32[]{:S(2)}, u32[]{:S(2)}) collective-permute-start(f32[8,512]{1,0:T(8,128)S(1)} %get-tuple-element.81), channel_id=1, source_target_pairs={{0,4},{4,8},{8,12},{12,0},{1,5},{5,9},{9,13},{13,1},{2,6},{6,10},{... | collective-permute-start | bytes 49160 | tf_op jit(solution)/shard_map/ppermute | solution.py:452
  80.5 2.0 %collective-permute-start.21 = (f32[8,512]{1,0:T(8,128)S(1)}, f32[8,512]{1,0:T(8,128)S(1)}, u32[]{:S(2)}, u32[]{:S(2)}) collective-permute-start(f32[8,512]{1,0:T(8,128)S(1)} %get-tuple-element.82), channel_id=1, source_target_pairs={{0,8},{4,12},{8,0},{12,4},{1,9},{5,13},{9,1},{13,5},{2,10},{6,14},... | collective-permute-start | bytes 49160 | tf_op jit(solution)/shard_map/ppermute | solution.py:452
  83.0 2.3 %means.1 = bf16[8,512,256]{2,1,0:T(8,128)(2,1)} custom-call(s32[2,4]{1,0:T(2,128)} %bitcast.21, bf16[4,512,256]{2,1,0:T(8,128)(2,1)S(1)} %get-tuple-element.45.rows_ref, bf16[4,512,256]{2,1,0:T(8,128)(2,1)S(1)} %get-tuple-element.84.kernel_ref, f32[4,512,128]{2,1,0:T(8,128)S(1)} %get-tuple-element.85.mass_ref, ...), custom_call_target="tpu_custom_call", output_to_operand_aliasing={{}: (8, {})} | custom-call | flops 536870912 | bytes 8388608 | tf_op jit(solution)/shard_map/means/pallas_call | solution.py:389
  85.3 1.0 %collective-permute-done.22.refs_4_ = f32[8,512]{1,0:T(8,128)S(1)} collective-permute-done((f32[8,512]{1,0:T(8,128)S(1)}, f32[8,512]{1,0:T(8,128)S(1)}, u32[]{:S(2)}, u32[]{:S(2)}) %collective-permute-start.22) | collective-permute-done | bytes 16416 | tf_op jit(solution)/shard_map/ppermute | solution.py:452
  86.3 0.6 weights.1
  (23 shorter events, 4.0 us)
Async XLA Ops:
  0.6 7.0 %collective-permute-start.2 = (s32[2,4]{1,0:T(2,128)}, s32[2,4]{1,0:T(2,128)S(1)}, u32[]{:S(2)}, u32[]{:S(2)}) collective-permute-start(s32[2,4]{1,0:T(2,128)} %bitcast.13), channel_id=1, source_target_pairs={{0,4},{4,8},{8,12},{12,0},{1,5},{5,9},{9,13},{13,1},{2,6},{6,10},{... | collective-permute-start | bytes 104 | tf_op jit(solution)/shard_map/ppermute | solution.py:452
  3.7 4.7 %collective-permute-start.1 = (s32[2,4]{1,0:T(2,128)}, s32[2,4]{1,0:T(2,128)S(1)}, u32[]{:S(2)}, u32[]{:S(2)}) collective-permute-start(s32[2,4]{1,0:T(2,128)} %bitcast.14), channel_id=1, source_target_pairs={{0,8},{4,12},{8,0},{12,4},{1,9},{5,13},{9,1},{13,5},{2,10},{6,14},... | collective-permute-start | bytes 104 | tf_op jit(solution)/shard_map/ppermute | solution.py:452
  6.3 3.8 %collective-permute-start = (s32[2,4]{1,0:T(2,128)}, s32[2,4]{1,0:T(2,128)S(1)}, u32[]{:S(2)}, u32[]{:S(2)}) collective-permute-start(s32[2,4]{1,0:T(2,128)} %bitcast.15), channel_id=1, source_target_pairs={{0,12},{4,0},{8,4},{12,8},{1,13},{5,1},{9,5},{13,9},{2,14},{6,2},{... | collective-permute-start | bytes 104 | tf_op jit(solution)/shard_map/ppermute | solution.py:452
  13.1 23.6 %collective-permute-start.3 = (bf16[4,512,256]{2,1,0:T(8,128)(2,1)S(1)}, bf16[4,512,256]{2,1,0:T(8,128)(2,1)S(1)}, u32[]{:S(2)}, u32[]{:S(2)}) collective-permute-start(bf16[4,512,256]{2,1,0:T(8,128)(2,1)S(1)} %get-tuple-element.45.rows_ref), channel_id=1, source_target_pairs={{0,2},{1,3},{2,0},{3,1},{4,6},{5,7},{6,4},{7,5},{8,10},{9,11},{10,... | collective-permute-start | bytes 3145736 | tf_op jit(solution)/shard_map/ppermute | solution.py:437
  14.7 22.2 %collective-permute-start.4 = (bf16[2,320,256]{2,1,0:T(8,128)(2,1)S(1)}, bf16[2,320,256]{2,1,0:T(8,128)(2,1)S(1)}, u32[]{:S(2)}, u32[]{:S(2)}) collective-permute-start(bf16[2,320,256]{2,1,0:T(8,128)(2,1)S(1)} %get-tuple-element.46), channel_id=1, source_target_pairs={{0,4},{4,8},{8,12},{12,0},{1,5},{5,9},{9,13},{13,1},{2,6},{6,10},{... | collective-permute-start | bytes 983048 | tf_op jit(solution)/shard_map/ppermute | solution.py:452
  14.7 23.8 %collective-permute-start.5 = (bf16[2,320,256]{2,1,0:T(8,128)(2,1)S(1)}, bf16[2,320,256]{2,1,0:T(8,128)(2,1)S(1)}, u32[]{:S(2)}, u32[]{:S(2)}) collective-permute-start(bf16[2,320,256]{2,1,0:T(8,128)(2,1)S(1)} %get-tuple-element.47), channel_id=1, source_target_pairs={{0,8},{4,12},{8,0},{12,4},{1,9},{5,13},{9,1},{13,5},{2,10},{6,14},... | collective-permute-start | bytes 983048 | tf_op jit(solution)/shard_map/ppermute | solution.py:452
  18.0 20.5 %collective-permute-start.6 = (bf16[2,320,256]{2,1,0:T(8,128)(2,1)S(1)}, bf16[2,320,256]{2,1,0:T(8,128)(2,1)S(1)}, u32[]{:S(2)}, u32[]{:S(2)}) collective-permute-start(bf16[2,320,256]{2,1,0:T(8,128)(2,1)S(1)} %get-tuple-element.48), channel_id=1, source_target_pairs={{0,12},{4,0},{8,4},{12,8},{1,13},{5,1},{9,5},{13,9},{2,14},{6,2},{... | collective-permute-start | bytes 983048 | tf_op jit(solution)/shard_map/ppermute | solution.py:452
  38.5 24.4 %collective-permute-start.9 = (bf16[2,4,512,256]{3,2,1,0:T(8,128)(2,1)S(1)}, bf16[2,4,512,256]{3,2,1,0:T(8,128)(2,1)S(1)}, u32[]{:S(2)}, u32[]{:S(2)}) collective-permute-start(bf16[2,4,512,256]{3,2,1,0:T(8,128)(2,1)S(1)} %pad_maximum_fusion.refs_0_), channel_id=1, source_target_pairs={{0,1},{1,0},{2,3},{3,2},{4,5},{5,4},{6,7},{7,6},{8,9},{9,8},{10,11... | collective-permute-start | bytes 6291464 | tf_op jit(solution)/shard_map/ppermute | solution.py:437
  38.5 12.1 %collective-permute-start.10 = (bf16[2,192,256]{2,1,0:T(8,128)(2,1)S(1)}, bf16[2,192,256]{2,1,0:T(8,128)(2,1)S(1)}, u32[]{:S(2)}, u32[]{:S(2)}) collective-permute-start(bf16[2,192,256]{2,1,0:T(8,128)(2,1)S(1)} %get-tuple-element.58), channel_id=1, source_target_pairs={{0,4},{4,8},{8,12},{12,0},{1,5},{5,9},{9,13},{13,1},{2,6},{6,10},{... | collective-permute-start | bytes 589832 | tf_op jit(solution)/shard_map/ppermute | solution.py:452
  46.0 15.5 %collective-permute-start.7 = (bf16[2,320,256]{2,1,0:T(8,128)(2,1)S(1)}, bf16[2,320,256]{2,1,0:T(8,128)(2,1)S(1)}, u32[]{:S(2)}, u32[]{:S(2)}) collective-permute-start(bf16[2,320,256]{2,1,0:T(8,128)(2,1)S(1)} %get-tuple-element.63.refs_2_.refs_0_), channel_id=1, source_target_pairs={{0,2},{1,3},{2,0},{3,1},{4,6},{5,7},{6,4},{7,5},{8,10},{9,11},{10,... | collective-permute-start | bytes 983048 | tf_op jit(solution)/shard_map/ppermute | solution.py:437
  46.6 16.3 %collective-permute-start.8 = (bf16[2,320,256]{2,1,0:T(8,128)(2,1)S(1)}, bf16[2,320,256]{2,1,0:T(8,128)(2,1)S(1)}, u32[]{:S(2)}, u32[]{:S(2)}) collective-permute-start(bf16[2,320,256]{2,1,0:T(8,128)(2,1)S(1)} %get-tuple-element.64.refs_3_.refs_1_), channel_id=1, source_target_pairs={{0,2},{1,3},{2,0},{3,1},{4,6},{5,7},{6,4},{7,5},{8,10},{9,11},{10,... | collective-permute-start | bytes 983048 | tf_op jit(solution)/shard_map/ppermute | solution.py:437
  48.1 11.4 %collective-permute-start.11 = (bf16[2,192,256]{2,1,0:T(8,128)(2,1)S(1)}, bf16[2,192,256]{2,1,0:T(8,128)(2,1)S(1)}, u32[]{:S(2)}, u32[]{:S(2)}) collective-permute-start(bf16[2,192,256]{2,1,0:T(8,128)(2,1)S(1)} %get-tuple-element.59), channel_id=1, source_target_pairs={{0,8},{4,12},{8,0},{12,4},{1,9},{5,13},{9,1},{13,5},{2,10},{6,14},... | collective-permute-start | bytes 589832 | tf_op jit(solution)/shard_map/ppermute | solution.py:452
  50.6 10.8 %collective-permute-start.12 = (bf16[2,192,256]{2,1,0:T(8,128)(2,1)S(1)}, bf16[2,192,256]{2,1,0:T(8,128)(2,1)S(1)}, u32[]{:S(2)}, u32[]{:S(2)}) collective-permute-start(bf16[2,192,256]{2,1,0:T(8,128)(2,1)S(1)} %get-tuple-element.60), channel_id=1, source_target_pairs={{0,12},{4,0},{8,4},{12,8},{1,13},{5,1},{9,5},{13,9},{2,14},{6,2},{... | collective-permute-start | bytes 589832 | tf_op jit(solution)/shard_map/ppermute | solution.py:452
  63.7 10.5 %collective-permute-start.17 = (bf16[4,192,256]{2,1,0:T(8,128)(2,1)S(1)}, bf16[4,192,256]{2,1,0:T(8,128)(2,1)S(1)}, u32[]{:S(2)}, u32[]{:S(2)}) collective-permute-start(bf16[4,192,256]{2,1,0:T(8,128)(2,1)S(1)} %select.3.refs_10_.refs_2_), channel_id=1, source_target_pairs={{0,2},{1,3},{2,0},{3,1},{4,6},{5,7},{6,4},{7,5},{8,10},{9,11},{10,... | collective-permute-start | bytes 1179656 | tf_op jit(solution)/shard_map/ppermute | solution.py:437
  64.3 1.6 %collective-permute-start.15 = (bf16[2,320,256]{2,1,0:T(8,128)(2,1)S(1)}, bf16[2,320,256]{2,1,0:T(8,128)(2,1)S(1)}, u32[]{:S(2)}, u32[]{:S(2)}) collective-permute-start(bf16[2,320,256]{2,1,0:T(8,128)(2,1)S(1)} %collective-permute-done.7.refs_4_), channel_id=1, source_target_pairs={{0,1},{1,0},{2,3},{3,2},{4,5},{5,4},{6,7},{7,6},{8,9},{9,8},{10,11... | collective-permute-start | bytes 983048 | tf_op jit(solution)/shard_map/ppermute | solution.py:437
  64.3 2.1 %collective-permute-start.16 = (bf16[2,320,256]{2,1,0:T(8,128)(2,1)S(1)}, bf16[2,320,256]{2,1,0:T(8,128)(2,1)S(1)}, u32[]{:S(2)}, u32[]{:S(2)}) collective-permute-start(bf16[2,320,256]{2,1,0:T(8,128)(2,1)S(1)} %collective-permute-done.8.refs_5_), channel_id=1, source_target_pairs={{0,1},{1,0},{2,3},{3,2},{4,5},{5,4},{6,7},{7,6},{8,9},{9,8},{10,11... | collective-permute-start | bytes 983048 | tf_op jit(solution)/shard_map/ppermute | solution.py:437
  64.8 2.1 %collective-permute-start.13 = (bf16[2,320,256]{2,1,0:T(8,128)(2,1)S(1)}, bf16[2,320,256]{2,1,0:T(8,128)(2,1)S(1)}, u32[]{:S(2)}, u32[]{:S(2)}) collective-permute-start(bf16[2,320,256]{2,1,0:T(8,128)(2,1)S(1)} %get-tuple-element.63.refs_2_.refs_0_), channel_id=1, source_target_pairs={{0,1},{1,0},{2,3},{3,2},{4,5},{5,4},{6,7},{7,6},{8,9},{9,8},{10,11... | collective-permute-start | bytes 983048 | tf_op jit(solution)/shard_map/ppermute | solution.py:437
  64.8 2.5 %collective-permute-start.14 = (bf16[2,320,256]{2,1,0:T(8,128)(2,1)S(1)}, bf16[2,320,256]{2,1,0:T(8,128)(2,1)S(1)}, u32[]{:S(2)}, u32[]{:S(2)}) collective-permute-start(bf16[2,320,256]{2,1,0:T(8,128)(2,1)S(1)} %get-tuple-element.64.refs_3_.refs_1_), channel_id=1, source_target_pairs={{0,1},{1,0},{2,3},{3,2},{4,5},{5,4},{6,7},{7,6},{8,9},{9,8},{10,11... | collective-permute-start | bytes 983048 | tf_op jit(solution)/shard_map/ppermute | solution.py:437
  65.9 8.3 %collective-permute-start.18 = (bf16[4,192,256]{2,1,0:T(8,128)(2,1)S(1)}, bf16[4,192,256]{2,1,0:T(8,128)(2,1)S(1)}, u32[]{:S(2)}, u32[]{:S(2)}) collective-permute-start(bf16[4,192,256]{2,1,0:T(8,128)(2,1)S(1)} %select.3.refs_10_.refs_2_), channel_id=1, source_target_pairs={{0,1},{1,0},{2,3},{3,2},{4,5},{5,4},{6,7},{7,6},{8,9},{9,8},{10,11... | collective-permute-start | bytes 1179656 | tf_op jit(solution)/shard_map/ppermute | solution.py:437
  74.2 1.7 %collective-permute-start.19 = (bf16[4,192,256]{2,1,0:T(8,128)(2,1)S(1)}, bf16[4,192,256]{2,1,0:T(8,128)(2,1)S(1)}, u32[]{:S(2)}, u32[]{:S(2)}) collective-permute-start(bf16[4,192,256]{2,1,0:T(8,128)(2,1)S(1)} %collective-permute-done.17.refs_11_), channel_id=1, source_target_pairs={{0,1},{1,0},{2,3},{3,2},{4,5},{5,4},{6,7},{7,6},{8,9},{9,8},{10,11... | collective-permute-start | bytes 1179656 | tf_op jit(solution)/shard_map/ppermute | solution.py:437
  78.6 6.7 %collective-permute-start.20 = (f32[8,512]{1,0:T(8,128)S(1)}, f32[8,512]{1,0:T(8,128)S(1)}, u32[]{:S(2)}, u32[]{:S(2)}) collective-permute-start(f32[8,512]{1,0:T(8,128)S(1)} %get-tuple-element.81), channel_id=1, source_target_pairs={{0,4},{4,8},{8,12},{12,0},{1,5},{5,9},{9,13},{13,1},{2,6},{6,10},{... | collective-permute-start | bytes 49160 | tf_op jit(solution)/shard_map/ppermute | solution.py:452
  80.5 4.8 %collective-permute-start.21 = (f32[8,512]{1,0:T(8,128)S(1)}, f32[8,512]{1,0:T(8,128)S(1)}, u32[]{:S(2)}, u32[]{:S(2)}) collective-permute-start(f32[8,512]{1,0:T(8,128)S(1)} %get-tuple-element.82), channel_id=1, source_target_pairs={{0,8},{4,12},{8,0},{12,4},{1,9},{5,13},{9,1},{13,5},{2,10},{6,14},... | collective-permute-start | bytes 49160 | tf_op jit(solution)/shard_map/ppermute | solution.py:452
  82.5 3.7 %collective-permute-start.22 = (f32[8,512]{1,0:T(8,128)S(1)}, f32[8,512]{1,0:T(8,128)S(1)}, u32[]{:S(2)}, u32[]{:S(2)}) collective-permute-start(f32[8,512]{1,0:T(8,128)S(1)} %get-tuple-element.83), channel_id=1, source_target_pairs={{0,12},{4,0},{8,4},{12,8},{1,13},{5,1},{9,5},{13,9},{2,14},{6,2},{... | collective-permute-start | bytes 49160 | tf_op jit(solution)/shard_map/ppermute | solution.py:452

commit v13 on v12

--- a/solution.py
+++ b/solution.py
@@ -182,7 +182,7 @@
 
 
 def window_parts(window, narrow_count, refs):
-    rows, refs = [ref.at[i] for ref in refs[:2] for i in range(narrow_count // 2)], refs[2:]
+    rows, refs = refs[0], refs[1:]
     chunks = []
     for chunk, _, _ in segments(window):
         cols, refs = take_parts(refs, narrow_count, PIECES[chunk])
@@ -196,16 +196,25 @@
     return jnp.concatenate(pieces, axis=0) if len(pieces) > 1 else pieces[0]
 
 
-def pair_parts(window, rows, chunks, pair):
-    cols = [own_columns(window, [c[i] for c in chunks], pair) for i in range(len(rows))]
-    return [part[pair] for part in rows], cols
-
-
-def first_kernel(window, narrow_count, *refs):
+def hop_order(narrow_count):
+    order, step = [0], narrow_count // 2
+    while step:
+        order = order + [other ^ step for other in order]
+        step //= 2
+    return order
+
+
+def pair_parts(window, lane, rows, chunks, pair):
+    order = hop_order(rows.shape[0])
+    cols = [own_columns(window, [c[i] for c in chunks], pair) for i in range(len(order))]
+    return [rows[lane ^ other, pair] for other in order], cols
+
+
+def first_kernel(window, narrow_count, lane_ref, *refs):
     square_ref, mass_ref, total_ref, sums_ref = refs[-4:]
     all_rows, chunks = window_parts(window, narrow_count, refs)
     for pair in range(square_ref.shape[0]):
-        rows, cols = pair_parts(window, all_rows, chunks, pair)
+        rows, cols = pair_parts(window, lane_ref[0], all_rows, chunks, pair)
         square = jnp.sum(tree([lane_sum(row) for row in rows]), axis=1, keepdims=True)
         square = jnp.broadcast_to(square, (BR, LANES))
         kernel, sums, mass = scores(rows, cols, square)
@@ -215,7 +224,7 @@
         total_ref[pair] = jnp.dot(kernel, cols[0], preferred_element_type=jnp.float32)
 
 
-def last_kernel(window, narrow_count, wide_count, me_ref, pairs_ref, *refs):
+def last_kernel(window, narrow_count, wide_count, me_ref, lane_ref, pairs_ref, *refs):
     square_in, mass_in, sums_in = refs[-6 - wide_count : -3 - wide_count]
     kernel_ref, mass_ref, row_ref = refs[-3 - wide_count : -wide_count]
     shares = refs[-wide_count:]
@@ -223,7 +232,7 @@
         ref[...] = jnp.zeros_like(ref)
     all_rows, chunks = window_parts(window, narrow_count, refs)
     for pair in range(square_in.shape[0]):
-        rows, cols = pair_parts(window, all_rows, chunks, pair)
+        rows, cols = pair_parts(window, lane_ref[0], all_rows, chunks, pair)
         kernel, sums, mass = scores(rows, cols, square_in[pair])
         kernel_ref[pair] = kernel
         sums = jnp.concatenate([sums_in[pair : pair + 1], sums], axis=1)
@@ -249,27 +258,27 @@
     return [piece for part in parts for piece in part]
 
 
-def first_window(rows, cols):
-    _, pair_count, _, feat = rows[0][0].shape
+def first_window(lane, rows, cols):
+    _, pair_count, _, feat = rows.shape
     window = WINDOWS[0]
     lanes = pltpu.VMEM((pair_count, BR, LANES), jnp.float32)
     total = pltpu.VMEM((pair_count, BR, feat), jnp.float32)
-    args = operands(rows)
+    args = [rows]
     for chunk, _, _ in segments(window):
         args += operands(cols[chunk])
     return pl.pallas_call(
         functools.partial(first_kernel, window, len(cols[0])),
         out_shape=[lanes, lanes, total, pltpu.VMEM((pair_count, window[1]), jnp.float32)],
-        in_specs=[vmem()] * len(args),
+        in_specs=[smem()] + [vmem()] * len(args),
         out_specs=[vmem()] * 4,
         compiler_params=params(16),
         cost_estimate=pl.CostEstimate(flops=0, transcendentals=0, bytes_accessed=0),
         name="first_window",
-    )(*[in_vmem(x) for x in args])
-
-
-def last_window(me, pairs, rows, cols, square, mass, sums, wide_count):
-    pair_count = rows[0][0].shape[1]
+    )(lane, *[in_vmem(x) for x in args])
+
+
+def last_window(me, lane, pairs, rows, cols, square, mass, sums, wide_count):
+    pair_count = rows.shape[1]
     window = WINDOWS[1]
     size = window[1] - window[0]
     by_block = pltpu.VMEM((BLK_DEV, BR), jnp.float32)
@@ -277,19 +286,19 @@
         pltpu.VMEM((pair_count, BR, size), jnp.bfloat16),
         pltpu.VMEM((pair_count, BR, LANES), jnp.float32),
     ] + [by_block] * (1 + wide_count)
-    args = operands(rows)
+    args = [rows]
     for chunk, _, _ in segments(window):
         args += operands(cols[chunk])
     args += [square, mass, sums]
     kernel, mass, row_sums, *shares = pl.pallas_call(
         functools.partial(last_kernel, window, len(cols[0]), wide_count),
         out_shape=shapes,
-        in_specs=[smem(), smem()] + [vmem()] * len(args),
+        in_specs=[smem(), smem(), smem()] + [vmem()] * len(args),
         out_specs=[vmem()] * len(shapes),
         compiler_params=params(16),
         cost_estimate=estimate(pair_count, size),
         name="last_window",
-    )(me, in_hbm(pairs), *[in_vmem(x) for x in args])
+    )(me, lane, in_hbm(pairs), *[in_vmem(x) for x in args])
     return kernel, mass, row_sums, shares
 
 
@@ -457,6 +466,7 @@
 def on_device(embeddings, pair_list):
     wide_count = lax.axis_size("wide")
     me = lax.axis_index("wide").astype(jnp.int32).reshape(1)
+    lane = lax.axis_index("narrow").astype(jnp.int32).reshape(1)
     pairs = pair_list.T
     pair_count = pairs.shape[1]
     capacity = max(2, 2 * pair_count // wide_count)
@@ -469,20 +479,19 @@
     def pick(received, chunk):
         return select(me, pairs, own, received, *CHUNKS[chunk], PIECES[chunk])
 
-    rows = jnp.stack([part[0] for part in first_hops([row_slices])])
+    rows = lax.all_gather(row_slices, "narrow", axis=0)
     rows, received, (kept, own) = fixed((rows, to_wide(outgoing[0]), keep(pairs, blocks)))
     cols_a = first_hops(pick(received, 0))
-    rows = [[rows], *hop([[rows]], 1)]
-    cols_a, rows, received = fixed((cols_a, rows, to_wide(outgoing[1])))
+    cols_a, received = fixed((cols_a, to_wide(outgoing[1])))
     cols_b = first_hops(pick(received, 1))
     last_b = hop(cols_b[:1], 1)
     cols_a = cols_a + hop(cols_a, 1)
-    carry = first_window(rows, [cols_a])
+    carry = first_window(lane, rows, [cols_a])
     cols_b, carry = fixed((cols_b, carry))
     cols_b = cols_b + last_b + hop(cols_b[1:], 1)
     square, mass, total, sums = carry
     kernel, mass, row_sums, shares = last_window(
-        me, pairs, rows, [cols_a, cols_b], square, mass, sums, wide_count
+        me, lane, pairs, rows, [cols_a, cols_b], square, mass, sums, wide_count
     )
     came = to_wide(shares[1:])
     mean = means(pairs, row_slices, kernel, mass, total, [cols_a, cols_b], kept)

time: 87.4 us -> 140 us (1.60)
  Pallas kernels: 19.4 us -> 50.8 us
  between operations: 0.72 us -> 14.1 us
  waiting for transfers between devices: 37.1 us -> 45.5 us
  starting transfers between devices: 29.5 us -> 26.7 us
  local copies, waits for them, and re-layouts: 0 us -> 2.71 us
    pallas_call x1, Pallas kernels: 3.04 us -> 33.8 us  [pack(): pl.pallas_call(functools.partial(pack_kernel, wide_count, pair_count, cap...]
    ppermute x11 -> x9, waiting for transfers between devices: 20.9 us -> 5.88 us  [hop(): lax.ppermute(piece, 'narrow', perm)]
    ppermute x12, waiting for transfers between devices: 16.2 us -> 28.3 us  [to_wide(): lax.ppermute(piece, 'wide', [(i, (i + shift) % count) for i in range(coun...]
    all_gather x0 -> x1, waiting for transfers between devices: none -> 11.3 us  [on_device(): rows = lax.all_gather(row_slices, 'narrow', axis=0)]
    unnamed x0 -> x6, local copies, waits for them, and re-layouts: none -> 2.71 us
    ppermute x11 -> x9, starting transfers between devices: 5.41 us -> 3.66 us  [hop(): lax.ppermute(piece, 'narrow', perm)]
  transfers between devices with their start and end apart: 23 -> 22, of which waited for: 15 -> 13; matrix products, arithmetic and copies ran while one was open for 0% -> 0% of each run, Pallas kernels for 14% -> 9%
where the time goes in v13:
time: 140 us
  Pallas kernels  50.8 us (36%)
  waiting for transfers between devices  45.5 us (32%)
  starting transfers between devices  26.7 us (19%)
  between operations  14.1 us (10%)
  local copies, waits for them, and re-layouts  2.71 us (2%)
    pallas_call x1, Pallas kernels, pack(): pl.pallas_call(functools.partial(pack_kernel, wide_count, pair_count, cap...  33.8 us
    ppermute x12, waiting for transfers between devices, to_wide(): lax.ppermute(piece, 'wide', [(i, (i + shift) % count) for i in range(coun...  28.3 us
    ppermute x12, starting transfers between devices, to_wide(): lax.ppermute(piece, 'wide', [(i, (i + shift) % count) for i in range(coun...  23 us
    all_gather x1, waiting for transfers between devices, on_device(): rows = lax.all_gather(row_slices, 'narrow', axis=0)  11.3 us
    pallas_call x1, Pallas kernels, keep(): pl.pallas_call(keep_kernel, out_shape=[pltpu.HBM(blocks.shape, blocks.dty...  6.08 us
    ppermute x9, waiting for transfers between devices, hop(): lax.ppermute(piece, 'narrow', perm)  5.88 us
    ppermute x9, starting transfers between devices, hop(): lax.ppermute(piece, 'narrow', perm)  3.66 us
    pallas_call x1, Pallas kernels, first_window(): pl.pallas_call(functools.partial(first_kernel, window, len(cols[0])), out...  3.09 us
  transfers between devices with their start and end apart: 22, of which 13 were waited for; matrix products, arithmetic and copies ran while one was open for 0% of the time, Pallas kernels for 9%

profile of v13, /device:TPU:0, one launch (start us, length us, event | category | flops | bytes accessed | tf_op | source)
XLA Modules:
  0.0 139.8 jit_solution(3120370479214820684)
XLA Ops:
  7.2 3.1 %collective-permute-start.2 = (s32[2,4]{1,0:T(2,128)}, s32[2,4]{1,0:T(2,128)S(1)}, u32[]{:S(2)}, u32[]{:S(2)}) collective-permute-start(s32[2,4]{1,0:T(2,128)} %bitcast.13), channel_id=1, source_target_pairs={{0,4},{4,8},{8,12},{12,0},{1,5},{5,9},{9,13},{13,1},{2,6},{6,10},{... | collective-permute-start | bytes 104 | tf_op jit(solution)/shard_map/ppermute | solution.py:461
  10.3 2.6 %collective-permute-start.1 = (s32[2,4]{1,0:T(2,128)}, s32[2,4]{1,0:T(2,128)S(1)}, u32[]{:S(2)}, u32[]{:S(2)}) collective-permute-start(s32[2,4]{1,0:T(2,128)} %bitcast.14), channel_id=1, source_target_pairs={{0,8},{4,12},{8,0},{12,4},{1,9},{5,13},{9,1},{13,5},{2,10},{6,14},... | collective-permute-start | bytes 104 | tf_op jit(solution)/shard_map/ppermute | solution.py:461
  12.9 1.3 collective-permute-start
  14.2 0.7 collective-permute-done.1.refs_1_
  15.0 1.7 %collective-permute-done.refs_0_ = s32[2,4]{1,0:T(2,128)S(1)} collective-permute-done((s32[2,4]{1,0:T(2,128)}, s32[2,4]{1,0:T(2,128)S(1)}, u32[]{:S(2)}, u32[]{:S(2)}) %collective-permute-start) | collective-permute-done | bytes 64 | tf_op jit(solution)/shard_map/ppermute | solution.py:461
  16.7 33.8 %pack.1 = (bf16[2,320,256]{2,1,0:T(8,128)(2,1)S(1)}, bf16[2,320,256]{2,1,0:T(8,128)(2,1)S(1)}, bf16[2,320,256]{2,1,0:T(8,128)(2,1)S(1)}, bf16[2,192,256]{2,1,0:T...) custom-call(s32[1]{0:T(128)} %bitcast.me_ref, ...), custom_call_target="tpu_custom_call" | custom-call | tf_op jit(solution)/shard_map/pack/pallas_call | solution.py:82
  50.6 0.5 copy-done.2
  51.1 3.1 %collective-permute-start.4 = (bf16[2,320,256]{2,1,0:T(8,128)(2,1)S(1)}, bf16[2,320,256]{2,1,0:T(8,128)(2,1)S(1)}, u32[]{:S(2)}, u32[]{:S(2)}) collective-permute-start(bf16[2,320,256]{2,1,0:T(8,128)(2,1)S(1)} %get-tuple-element.45), channel_id=1, source_target_pairs={{0,8},{4,12},{8,0},{12,4},{1,9},{5,13},{9,1},{13,5},{2,10},{6,14},... | collective-permute-start | bytes 983048 | tf_op jit(solution)/shard_map/ppermute | solution.py:461
  54.4 6.1 %keep.1 = (bf16[8,512,256]{2,1,0:T(8,128)(2,1)}, bf16[4,512,256]{2,1,0:T(8,128)(2,1)S(1)}) custom-call(s32[2,4]{1,0:T(2,128)} %bitcast.17, bf16[8,512,256]{2,1,0:T(8,128)(2,1)} %bitcast.10, bf16[8,512,256]{2,1,0:T(8,128)(2,1)} %bitcast.11), custom_call_target="tpu_custom_call" | custom-call | tf_op jit(solution)/shard_map/keep/pallas_call | solution.py:329
  60.5 2.6 %collective-permute-done.3.refs_0_ = bf16[2,320,256]{2,1,0:T(8,128)(2,1)S(1)} collective-permute-done((bf16[2,320,256]{2,1,0:T(8,128)(2,1)S(1)}, bf16[2,320,256]{2,1,0:T(8,128)(2,1)S(1)}, u32[]{:S(2)}, u32[]{:S(2)}) %collective-permute-start.3) | collective-permute-done | bytes 327712 | tf_op jit(solution)/shard_map/ppermute | solution.py:461
  63.1 11.5 %collective-permute-done.4.refs_1_ = bf16[2,320,256]{2,1,0:T(8,128)(2,1)S(1)} collective-permute-done((bf16[2,320,256]{2,1,0:T(8,128)(2,1)S(1)}, bf16[2,320,256]{2,1,0:T(8,128)(2,1)S(1)}, u32[]{:S(2)}, u32[]{:S(2)}) %collective-permute-start.4) | collective-permute-done | bytes 327712 | tf_op jit(solution)/shard_map/ppermute | solution.py:461
  74.6 11.3 %all-gather.3.cloned.1.call-done = bf16[16,512,256]{2,1,0:T(8,128)(2,1)} async-done(((bf16[4,512,256]{2,1,0:T(8,128)(2,1)}), bf16[16,512,256]{2,1,0:T(8,128)(2,1)}) %all-gather.3.cloned.1.call-update) | async-done | bytes 4194320 | tf_op jit(solution)/shard_map/all_gather | solution.py:482
  85.9 0.8 select.2
  87.1 1.7 %collective-permute-start.7 = (bf16[2,320,256]{2,1,0:T(8,128)(2,1)S(1)}, bf16[2,320,256]{2,1,0:T(8,128)(2,1)S(1)}, u32[]{:S(2)}, u32[]{:S(2)}) collective-permute-start(bf16[2,320,256]{2,1,0:T(8,128)(2,1)S(1)} %get-tuple-element.60.refs_2_.refs_1_), channel_id=1, source_target_pairs={{0,2},{1,3},{2,0},{3,1},{4,6},{5,7},{6,4},{7,5},{8,10},{9,11},{10,... | collective-permute-start | bytes 983048 | tf_op jit(solution)/shard_map/ppermute | solution.py:446
  88.8 1.5 %collective-permute-start.8 = (bf16[2,192,256]{2,1,0:T(8,128)(2,1)}, bf16[2,192,256]{2,1,0:T(8,128)(2,1)S(1)}, u32[]{:S(2)}, u32[]{:S(2)}) collective-permute-start(bf16[2,192,256]{2,1,0:T(8,128)(2,1)} %copy-done.2), channel_id=1, source_target_pairs={{0,4},{4,8},{8,12},{12,0},{1,5},{5,9},{9,13},{13,1},{2,6},{6,10},{... | collective-permute-start | bytes 589832 | tf_op jit(solution)/shard_map/ppermute | solution.py:461
  90.3 2.4 %collective-permute-start.9 = (bf16[2,192,256]{2,1,0:T(8,128)(2,1)S(1)}, bf16[2,192,256]{2,1,0:T(8,128)(2,1)S(1)}, u32[]{:S(2)}, u32[]{:S(2)}) collective-permute-start(bf16[2,192,256]{2,1,0:T(8,128)(2,1)S(1)} %get-tuple-element.57), channel_id=1, source_target_pairs={{0,8},{4,12},{8,0},{12,4},{1,9},{5,13},{9,1},{13,5},{2,10},{6,14},... | collective-permute-start | bytes 589832 | tf_op jit(solution)/shard_map/ppermute | solution.py:461
  92.7 1.4 %collective-permute-start.10 = (bf16[2,192,256]{2,1,0:T(8,128)(2,1)S(1)}, bf16[2,192,256]{2,1,0:T(8,128)(2,1)S(1)}, u32[]{:S(2)}, u32[]{:S(2)}) collective-permute-start(bf16[2,192,256]{2,1,0:T(8,128)(2,1)S(1)} %get-tuple-element.58), channel_id=1, source_target_pairs={{0,12},{4,0},{8,4},{12,8},{1,13},{5,1},{9,5},{13,9},{2,14},{6,2},{... | collective-permute-start | bytes 589832 | tf_op jit(solution)/shard_map/ppermute | solution.py:461
  94.2 4.6 %collective-permute-done.8.refs_0_ = bf16[2,192,256]{2,1,0:T(8,128)(2,1)S(1)} collective-permute-done((bf16[2,192,256]{2,1,0:T(8,128)(2,1)}, bf16[2,192,256]{2,1,0:T(8,128)(2,1)S(1)}, u32[]{:S(2)}, u32[]{:S(2)}) %collective-permute-start.8) | collective-permute-done | bytes 196640 | tf_op jit(solution)/shard_map/ppermute | solution.py:461
  98.8 7.1 %collective-permute-done.9.refs_1_ = bf16[2,192,256]{2,1,0:T(8,128)(2,1)S(1)} collective-permute-done((bf16[2,192,256]{2,1,0:T(8,128)(2,1)S(1)}, bf16[2,192,256]{2,1,0:T(8,128)(2,1)S(1)}, u32[]{:S(2)}, u32[]{:S(2)}) %collective-permute-start.9) | collective-permute-done | bytes 196640 | tf_op jit(solution)/shard_map/ppermute | solution.py:461
  105.9 0.8 select.3.refs_9_.refs_2_
  107.1 0.5 collective-permute-start.14
  107.6 0.5 collective-permute-start.12
  108.1 0.6 collective-permute-done.13.refs_7_
  110.1 2.2 %copy-done = bf16[16,512,256]{2,1,0:T(8,128)(2,1)S(1)} copy-done((bf16[16,512,256]{2,1,0:T(8,128)(2,1)S(1)}, bf16[16,512,256]{2,1,0:T(8,128)(2,1)}, u32[]{:S(2)}) %copy-start) | copy-done | bytes 4194328
  112.3 3.1 %first_window.1 = (f32[4,512,128]{2,1,0:T(8,128)S(1)}, f32[4,512,128]{2,1,0:T(8,128)S(1)}, f32[4,512,256]{2,1,0:T(8,128)S(1)}, f32[4,256]{1,0:T(4,128)S(1)}) custom-call(s32[1]{0:T(128)} %bitcast.1.lane_ref, bf16[4,4,512,256]{3,2,1,0:T(8,128)(2,1)S(1)} %bitcast.7, bf16[2,320,256]{2,1,0:T(8,128)(2,1)S(1)} %get-tuple-element.59.refs_1_.refs_0_, ...), custom_call_target="tpu_custom_call" | custom-call | tf_op jit(solution)/shard_map/first_window/pallas_call | solution.py:269
  115.4 2.3 %collective-permute-done.15.refs_10_ = bf16[4,192,256]{2,1,0:T(8,128)(2,1)S(1)} collective-permute-done((bf16[4,192,256]{2,1,0:T(8,128)(2,1)S(1)}, bf16[4,192,256]{2,1,0:T(8,128)(2,1)S(1)}, u32[]{:S(2)}, u32[]{:S(2)}) %collective-permute-start.15) | collective-permute-done | bytes 393248 | tf_op jit(solution)/shard_map/ppermute | solution.py:446
  117.7 1.7 %collective-permute-done.17.refs_12_ = bf16[4,192,256]{2,1,0:T(8,128)(2,1)S(1)} collective-permute-done((bf16[4,192,256]{2,1,0:T(8,128)(2,1)S(1)}, bf16[4,192,256]{2,1,0:T(8,128)(2,1)S(1)}, u32[]{:S(2)}, u32[]{:S(2)}) %collective-permute-start.17) | collective-permute-done | bytes 393248 | tf_op jit(solution)/shard_map/ppermute | solution.py:446
  119.4 2.6 %last_window.1 = (bf16[4,512,256]{2,1,0:T(8,128)(2,1)S(1)}, f32[4,512,128]{2,1,0:T(8,128)S(1)}, f32[8,512]{1,0:T(8,128)S(1)}, f32[8,512]{1,0:T(8,128)S(1)}, f32[...) custom-call(s32[1]{0:T(128)} %bitcast.me_ref, s32[1]{0:T(128)} %bitcast.1.lane_ref, s32[2,4]{1,0:T(2,128)} %bitcast.20, ...), custom_call_target="tpu_custom_call" | custom-call | flops 1073741824 | bytes 8388608 | tf_op jit(solution)/shard_map/last_window/pallas_call | solution.py:293
  122.1 4.8 %collective-permute-start.18 = (f32[8,512]{1,0:T(8,128)S(1)}, f32[8,512]{1,0:T(8,128)S(1)}, u32[]{:S(2)}, u32[]{:S(2)}) collective-permute-start(f32[8,512]{1,0:T(8,128)S(1)} %get-tuple-element.77), channel_id=1, source_target_pairs={{0,4},{4,8},{8,12},{12,0},{1,5},{5,9},{9,13},{13,1},{2,6},{6,10},{... | collective-permute-start | bytes 49160 | tf_op jit(solution)/shard_map/ppermute | solution.py:461
  127.2 2.2 %collective-permute-start.20 = (f32[8,512]{1,0:T(8,128)S(1)}, f32[8,512]{1,0:T(8,128)S(1)}, u32[]{:S(2)}, u32[]{:S(2)}) collective-permute-start(f32[8,512]{1,0:T(8,128)S(1)} %get-tuple-element.79), channel_id=1, source_target_pairs={{0,12},{4,0},{8,4},{12,8},{1,13},{5,1},{9,5},{13,9},{2,14},{6,2},{... | collective-permute-start | bytes 49160 | tf_op jit(solution)/shard_map/ppermute | solution.py:461
  129.3 2.9 %means.1 = bf16[8,512,256]{2,1,0:T(8,128)(2,1)} custom-call(s32[2,4]{1,0:T(2,128)} %bitcast.21, bf16[4,512,256]{2,1,0:T(8,128)(2,1)} %get-tuple-element.43.rows_ref, bf16[4,512,256]{2,1,0:T(8,128)(2,1)S(1)} %get-tuple-element.80.kernel_ref, f32[4,512,128]{2,1,0:T(8,128)S(1)} %get-tuple-element.81.mass_ref, ...), custom_call_target="tpu_custom_call", output_to_operand_aliasing={{}: (8, {})} | custom-call | flops 536870912 | bytes 8388608 | tf_op jit(solution)/shard_map/means/pallas_call | solution.py:398
  132.3 0.6 weights.1
  (27 shorter events, 2.8 us)
Async XLA Ops:
  7.2 78.7 %all-gather.3.cloned.1.call-start = ((), (), s32[]{:S(2)}) async-start(), calls=%async_computation | async-start | bytes 5242880 | tf_op jit(solution)/shard_map/all_gather | solution.py:482
  7.2 7.0 %collective-permute-start.2 = (s32[2,4]{1,0:T(2,128)}, s32[2,4]{1,0:T(2,128)S(1)}, u32[]{:S(2)}, u32[]{:S(2)}) collective-permute-start(s32[2,4]{1,0:T(2,128)} %bitcast.13), channel_id=1, source_target_pairs={{0,4},{4,8},{8,12},{12,0},{1,5},{5,9},{9,13},{13,1},{2,6},{6,10},{... | collective-permute-start | bytes 104 | tf_op jit(solution)/shard_map/ppermute | solution.py:461
  10.3 4.7 %collective-permute-start.1 = (s32[2,4]{1,0:T(2,128)}, s32[2,4]{1,0:T(2,128)S(1)}, u32[]{:S(2)}, u32[]{:S(2)}) collective-permute-start(s32[2,4]{1,0:T(2,128)} %bitcast.14), channel_id=1, source_target_pairs={{0,8},{4,12},{8,0},{12,4},{1,9},{5,13},{9,1},{13,5},{2,10},{6,14},... | collective-permute-start | bytes 104 | tf_op jit(solution)/shard_map/ppermute | solution.py:461
  12.9 3.8 %collective-permute-start = (s32[2,4]{1,0:T(2,128)}, s32[2,4]{1,0:T(2,128)S(1)}, u32[]{:S(2)}, u32[]{:S(2)}) collective-permute-start(s32[2,4]{1,0:T(2,128)} %bitcast.15), channel_id=1, source_target_pairs={{0,12},{4,0},{8,4},{12,8},{1,13},{5,1},{9,5},{13,9},{2,14},{6,2},{... | collective-permute-start | bytes 104 | tf_op jit(solution)/shard_map/ppermute | solution.py:461
  50.4 0.7 copy-start.2
  50.5 12.6 %collective-permute-start.3 = (bf16[2,320,256]{2,1,0:T(8,128)(2,1)S(1)}, bf16[2,320,256]{2,1,0:T(8,128)(2,1)S(1)}, u32[]{:S(2)}, u32[]{:S(2)}) collective-permute-start(bf16[2,320,256]{2,1,0:T(8,128)(2,1)S(1)} %get-tuple-element.44), channel_id=1, source_target_pairs={{0,4},{4,8},{8,12},{12,0},{1,5},{5,9},{9,13},{13,1},{2,6},{6,10},{... | collective-permute-start | bytes 983048 | tf_op jit(solution)/shard_map/ppermute | solution.py:461
  51.1 23.5 %collective-permute-start.4 = (bf16[2,320,256]{2,1,0:T(8,128)(2,1)S(1)}, bf16[2,320,256]{2,1,0:T(8,128)(2,1)S(1)}, u32[]{:S(2)}, u32[]{:S(2)}) collective-permute-start(bf16[2,320,256]{2,1,0:T(8,128)(2,1)S(1)} %get-tuple-element.45), channel_id=1, source_target_pairs={{0,8},{4,12},{8,0},{12,4},{1,9},{5,13},{9,1},{13,5},{2,10},{6,14},... | collective-permute-start | bytes 983048 | tf_op jit(solution)/shard_map/ppermute | solution.py:461
  54.2 20.4 %collective-permute-start.5 = (bf16[2,320,256]{2,1,0:T(8,128)(2,1)S(1)}, bf16[2,320,256]{2,1,0:T(8,128)(2,1)S(1)}, u32[]{:S(2)}, u32[]{:S(2)}) collective-permute-start(bf16[2,320,256]{2,1,0:T(8,128)(2,1)S(1)} %get-tuple-element.46), channel_id=1, source_target_pairs={{0,12},{4,0},{8,4},{12,8},{1,13},{5,1},{9,5},{13,9},{2,14},{6,2},{... | collective-permute-start | bytes 983048 | tf_op jit(solution)/shard_map/ppermute | solution.py:461
  86.7 19.1 %collective-permute-start.6 = (bf16[2,320,256]{2,1,0:T(8,128)(2,1)S(1)}, bf16[2,320,256]{2,1,0:T(8,128)(2,1)S(1)}, u32[]{:S(2)}, u32[]{:S(2)}) collective-permute-start(bf16[2,320,256]{2,1,0:T(8,128)(2,1)S(1)} %get-tuple-element.59.refs_1_.refs_0_), channel_id=1, source_target_pairs={{0,2},{1,3},{2,0},{3,1},{4,6},{5,7},{6,4},{7,5},{8,10},{9,11},{10,... | collective-permute-start | bytes 983048 | tf_op jit(solution)/shard_map/ppermute | solution.py:446
  87.1 18.8 %collective-permute-start.7 = (bf16[2,320,256]{2,1,0:T(8,128)(2,1)S(1)}, bf16[2,320,256]{2,1,0:T(8,128)(2,1)S(1)}, u32[]{:S(2)}, u32[]{:S(2)}) collective-permute-start(bf16[2,320,256]{2,1,0:T(8,128)(2,1)S(1)} %get-tuple-element.60.refs_2_.refs_1_), channel_id=1, source_target_pairs={{0,2},{1,3},{2,0},{3,1},{4,6},{5,7},{6,4},{7,5},{8,10},{9,11},{10,... | collective-permute-start | bytes 983048 | tf_op jit(solution)/shard_map/ppermute | solution.py:446
  88.8 9.9 %collective-permute-start.8 = (bf16[2,192,256]{2,1,0:T(8,128)(2,1)}, bf16[2,192,256]{2,1,0:T(8,128)(2,1)S(1)}, u32[]{:S(2)}, u32[]{:S(2)}) collective-permute-start(bf16[2,192,256]{2,1,0:T(8,128)(2,1)} %copy-done.2), channel_id=1, source_target_pairs={{0,4},{4,8},{8,12},{12,0},{1,5},{5,9},{9,13},{13,1},{2,6},{6,10},{... | collective-permute-start | bytes 589832 | tf_op jit(solution)/shard_map/ppermute | solution.py:461
  90.3 15.6 %collective-permute-start.9 = (bf16[2,192,256]{2,1,0:T(8,128)(2,1)S(1)}, bf16[2,192,256]{2,1,0:T(8,128)(2,1)S(1)}, u32[]{:S(2)}, u32[]{:S(2)}) collective-permute-start(bf16[2,192,256]{2,1,0:T(8,128)(2,1)S(1)} %get-tuple-element.57), channel_id=1, source_target_pairs={{0,8},{4,12},{8,0},{12,4},{1,9},{5,13},{9,1},{13,5},{2,10},{6,14},... | collective-permute-start | bytes 589832 | tf_op jit(solution)/shard_map/ppermute | solution.py:461
  92.7 13.2 %collective-permute-start.10 = (bf16[2,192,256]{2,1,0:T(8,128)(2,1)S(1)}, bf16[2,192,256]{2,1,0:T(8,128)(2,1)S(1)}, u32[]{:S(2)}, u32[]{:S(2)}) collective-permute-start(bf16[2,192,256]{2,1,0:T(8,128)(2,1)S(1)} %get-tuple-element.58), channel_id=1, source_target_pairs={{0,12},{4,0},{8,4},{12,8},{1,13},{5,1},{9,5},{13,9},{2,14},{6,2},{... | collective-permute-start | bytes 589832 | tf_op jit(solution)/shard_map/ppermute | solution.py:461
  106.7 11.0 %collective-permute-start.15 = (bf16[4,192,256]{2,1,0:T(8,128)(2,1)S(1)}, bf16[4,192,256]{2,1,0:T(8,128)(2,1)S(1)}, u32[]{:S(2)}, u32[]{:S(2)}) collective-permute-start(bf16[4,192,256]{2,1,0:T(8,128)(2,1)S(1)} %select.3.refs_9_.refs_2_), channel_id=1, source_target_pairs={{0,2},{1,3},{2,0},{3,1},{4,6},{5,7},{6,4},{7,5},{8,10},{9,11},{10,... | collective-permute-start | bytes 1179656 | tf_op jit(solution)/shard_map/ppermute | solution.py:446
  107.1 1.6 %collective-permute-start.13 = (bf16[2,320,256]{2,1,0:T(8,128)(2,1)S(1)}, bf16[2,320,256]{2,1,0:T(8,128)(2,1)S(1)}, u32[]{:S(2)}, u32[]{:S(2)}) collective-permute-start(bf16[2,320,256]{2,1,0:T(8,128)(2,1)S(1)} %collective-permute-done.6.refs_3_), channel_id=1, source_target_pairs={{0,1},{1,0},{2,3},{3,2},{4,5},{5,4},{6,7},{7,6},{8,9},{9,8},{10,11... | collective-permute-start | bytes 983048 | tf_op jit(solution)/shard_map/ppermute | solution.py:446
  107.1 2.1 %collective-permute-start.14 = (bf16[2,320,256]{2,1,0:T(8,128)(2,1)S(1)}, bf16[2,320,256]{2,1,0:T(8,128)(2,1)S(1)}, u32[]{:S(2)}, u32[]{:S(2)}) collective-permute-start(bf16[2,320,256]{2,1,0:T(8,128)(2,1)S(1)} %collective-permute-done.7.refs_4_), channel_id=1, source_target_pairs={{0,1},{1,0},{2,3},{3,2},{4,5},{5,4},{6,7},{7,6},{8,9},{9,8},{10,11... | collective-permute-start | bytes 983048 | tf_op jit(solution)/shard_map/ppermute | solution.py:446
  107.6 2.1 %collective-permute-start.11 = (bf16[2,320,256]{2,1,0:T(8,128)(2,1)S(1)}, bf16[2,320,256]{2,1,0:T(8,128)(2,1)S(1)}, u32[]{:S(2)}, u32[]{:S(2)}) collective-permute-start(bf16[2,320,256]{2,1,0:T(8,128)(2,1)S(1)} %get-tuple-element.59.refs_1_.refs_0_), channel_id=1, source_target_pairs={{0,1},{1,0},{2,3},{3,2},{4,5},{5,4},{6,7},{7,6},{8,9},{9,8},{10,11... | collective-permute-start | bytes 983048 | tf_op jit(solution)/shard_map/ppermute | solution.py:446
  107.6 2.5 %collective-permute-start.12 = (bf16[2,320,256]{2,1,0:T(8,128)(2,1)S(1)}, bf16[2,320,256]{2,1,0:T(8,128)(2,1)S(1)}, u32[]{:S(2)}, u32[]{:S(2)}) collective-permute-start(bf16[2,320,256]{2,1,0:T(8,128)(2,1)S(1)} %get-tuple-element.60.refs_2_.refs_1_), channel_id=1, source_target_pairs={{0,1},{1,0},{2,3},{3,2},{4,5},{5,4},{6,7},{7,6},{8,9},{9,8},{10,11... | collective-permute-start | bytes 983048 | tf_op jit(solution)/shard_map/ppermute | solution.py:446
  108.7 9.0 %collective-permute-start.16 = (bf16[4,192,256]{2,1,0:T(8,128)(2,1)S(1)}, bf16[4,192,256]{2,1,0:T(8,128)(2,1)S(1)}, u32[]{:S(2)}, u32[]{:S(2)}) collective-permute-start(bf16[4,192,256]{2,1,0:T(8,128)(2,1)S(1)} %select.3.refs_9_.refs_2_), channel_id=1, source_target_pairs={{0,1},{1,0},{2,3},{3,2},{4,5},{5,4},{6,7},{7,6},{8,9},{9,8},{10,11... | collective-permute-start | bytes 1179656 | tf_op jit(solution)/shard_map/ppermute | solution.py:446
  110.1 2.2 %copy-start = (bf16[16,512,256]{2,1,0:T(8,128)(2,1)S(1)}, bf16[16,512,256]{2,1,0:T(8,128)(2,1)}, u32[]{:S(2)}) copy-start(bf16[16,512,256]{2,1,0:T(8,128)(2,1)} %all-gather.3.cloned.1.call-done) | copy-start | bytes 12582916
  112.3 7.1 %copy-start.1 = (bf16[16,512,256]{2,1,0:T(8,128)(2,1)S(1)}, bf16[16,512,256]{2,1,0:T(8,128)(2,1)}, u32[]{:S(2)}) copy-start(bf16[16,512,256]{2,1,0:T(8,128)(2,1)} %all-gather.3.cloned.1.call-done) | copy-start | bytes 12582916
  117.7 1.7 %collective-permute-start.17 = (bf16[4,192,256]{2,1,0:T(8,128)(2,1)S(1)}, bf16[4,192,256]{2,1,0:T(8,128)(2,1)S(1)}, u32[]{:S(2)}, u32[]{:S(2)}) collective-permute-start(bf16[4,192,256]{2,1,0:T(8,128)(2,1)S(1)} %collective-permute-done.15.refs_10_), channel_id=1, source_target_pairs={{0,1},{1,0},{2,3},{3,2},{4,5},{5,4},{6,7},{7,6},{8,9},{9,8},{10,11... | collective-permute-start | bytes 1179656 | tf_op jit(solution)/shard_map/ppermute | solution.py:446
  122.1 10.2 %collective-permute-start.18 = (f32[8,512]{1,0:T(8,128)S(1)}, f32[8,512]{1,0:T(8,128)S(1)}, u32[]{:S(2)}, u32[]{:S(2)}) collective-permute-start(f32[8,512]{1,0:T(8,128)S(1)} %get-tuple-element.77), channel_id=1, source_target_pairs={{0,4},{4,8},{8,12},{12,0},{1,5},{5,9},{9,13},{13,1},{2,6},{6,10},{... | collective-permute-start | bytes 49160 | tf_op jit(solution)/shard_map/ppermute | solution.py:461
  126.9 5.4 %collective-permute-start.19 = (f32[8,512]{1,0:T(8,128)S(1)}, f32[8,512]{1,0:T(8,128)S(1)}, u32[]{:S(2)}, u32[]{:S(2)}) collective-permute-start(f32[8,512]{1,0:T(8,128)S(1)} %get-tuple-element.78), channel_id=1, source_target_pairs={{0,8},{4,12},{8,0},{12,4},{1,9},{5,13},{9,1},{13,5},{2,10},{6,14},... | collective-permute-start | bytes 49160 | tf_op jit(solution)/shard_map/ppermute | solution.py:461
  127.2 5.1 %collective-permute-start.20 = (f32[8,512]{1,0:T(8,128)S(1)}, f32[8,512]{1,0:T(8,128)S(1)}, u32[]{:S(2)}, u32[]{:S(2)}) collective-permute-start(f32[8,512]{1,0:T(8,128)S(1)} %get-tuple-element.79), channel_id=1, source_target_pairs={{0,12},{4,0},{8,4},{12,8},{1,13},{5,1},{9,5},{13,9},{2,14},{6,2},{... | collective-permute-start | bytes 49160 | tf_op jit(solution)/shard_map/ppermute | solution.py:461
Sparse Core Ops, SparseCore 0:
  50.6 35.2 all-gather.2

commit v14 on v12

--- a/solution.py
+++ b/solution.py
@@ -40,10 +40,17 @@
     return pltpu.CompilerParams(vmem_limit_bytes=mebibytes * 1024 * 1024)
 
 
-def pack_kernel(wide_count, pair_count, capacity, me_ref, pairs_ref, *refs):
-    lists, blocks_ref = refs[: wide_count - 1], refs[wide_count - 1]
-    *outs, rows_ref, sems = refs[wide_count:]
+def pack_kernel(wide_count, narrow_count, capacity, me_ref, lane_ref, pairs_ref, *refs):
+    lists, blocks_ref = refs[:narrow_count], refs[narrow_count]
+    *outs, rows_ref, sems = refs[narrow_count + 1 :]
+    pair_count = pairs_ref.shape[1]
     me = me_ref[0]
+
+    def asked(shift, pair):
+        back = wide_count - shift
+        other = lane_ref[0] ^ (back % narrow_count)
+        cols = [ref[back // narrow_count, 1, pair] for ref in lists]
+        return sum(jnp.where(other == place, col, 0) for place, col in enumerate(cols))
     copies = []
 
     def send(source, target):
@@ -52,11 +59,10 @@
 
     for chunk, (start, size) in enumerate(CHUNKS):
         for shift in range(1, wide_count):
-            asked = lists[shift - 1]
             picks = [jnp.int32(0)] * capacity
             count = jnp.int32(0)
             for pair in range(pair_count):
-                col = asked[1, pair]
+                col = asked(shift, pair)
                 mine = (col >> 3) == me
                 for slot in range(capacity):
                     picks[slot] = jnp.where(mine & (count == slot), col & 7, picks[slot])
@@ -70,8 +76,8 @@
         copy.wait()
 
 
-def pack(me, pairs, lists, blocks, capacity):
-    wide_count, pair_count = len(lists) + 1, pairs.shape[1]
+def pack(me, lane, pairs, lists, blocks, capacity, wide_count):
+    pair_count = pairs.shape[1]
     feat = blocks.shape[-1]
     shapes = [
         pltpu.VMEM((capacity, size, feat), blocks.dtype)
@@ -80,14 +86,14 @@
     ] + [pltpu.VMEM((pair_count, BR, feat), blocks.dtype)]
     copies = (len(shapes) - 1) * capacity + pair_count
     outs = pl.pallas_call(
-        functools.partial(pack_kernel, wide_count, pair_count, capacity),
+        functools.partial(pack_kernel, wide_count, len(lists), capacity),
         out_shape=shapes,
-        in_specs=[smem()] * (1 + wide_count) + [anywhere()],
+        in_specs=[smem()] * (3 + len(lists)) + [anywhere()],
         out_specs=[anywhere()] * len(shapes),
         scratch_shapes=[pltpu.SemaphoreType.DMA((copies,))],
         compiler_params=params(4),
         name="pack",
-    )(me, in_hbm(pairs), *lists, in_hbm(blocks))
+    )(me, lane, in_hbm(pairs), *lists, in_hbm(blocks))
     each = wide_count - 1
     return [outs[c * each : (c + 1) * each] for c in range(len(CHUNKS))], outs[-1]
 
@@ -215,10 +221,11 @@
         total_ref[pair] = jnp.dot(kernel, cols[0], preferred_element_type=jnp.float32)
 
 
-def last_kernel(window, narrow_count, wide_count, me_ref, pairs_ref, *refs):
-    square_in, mass_in, sums_in = refs[-6 - wide_count : -3 - wide_count]
-    kernel_ref, mass_ref, row_ref = refs[-3 - wide_count : -wide_count]
-    shares = refs[-wide_count:]
+def last_kernel(window, narrow_count, wide_count, me_ref, lane_ref, pairs_ref, *refs):
+    rounds = wide_count // narrow_count
+    square_in, mass_in, sums_in = refs[-6 - rounds : -3 - rounds]
+    kernel_ref, mass_ref, row_ref = refs[-3 - rounds : -rounds]
+    shares = refs[-rounds:]
     for ref in (row_ref, *shares):
         ref[...] = jnp.zeros_like(ref)
     all_rows, chunks = window_parts(window, narrow_count, refs)
@@ -233,8 +240,9 @@
         col = pairs_ref[1, pair]
         shift = (col >> 3) - me_ref[0]
         shift = jnp.where(shift < 0, shift + wide_count, shift)
-        for other, ref in enumerate(shares):
-            ref[pl.ds(col & 7, 1)] += jnp.where(shift == other, sums, 0.0)
+        for number, ref in enumerate(shares):
+            here = shift == number * narrow_count + lane_ref[0]
+            ref[pl.ds(col & 7, 1)] += jnp.where(here, sums, 0.0)
 
 
 def estimate(pair_count, size):
@@ -268,7 +276,7 @@
     )(*[in_vmem(x) for x in args])
 
 
-def last_window(me, pairs, rows, cols, square, mass, sums, wide_count):
+def last_window(me, lane, pairs, rows, cols, square, mass, sums, wide_count):
     pair_count = rows[0][0].shape[1]
     window = WINDOWS[1]
     size = window[1] - window[0]
@@ -276,7 +284,7 @@
     shapes = [
         pltpu.VMEM((pair_count, BR, size), jnp.bfloat16),
         pltpu.VMEM((pair_count, BR, LANES), jnp.float32),
-    ] + [by_block] * (1 + wide_count)
+    ] + [by_block] * (1 + wide_count // len(cols[0]))
     args = operands(rows)
     for chunk, _, _ in segments(window):
         args += operands(cols[chunk])
@@ -284,12 +292,12 @@
     kernel, mass, row_sums, *shares = pl.pallas_call(
         functools.partial(last_kernel, window, len(cols[0]), wide_count),
         out_shape=shapes,
-        in_specs=[smem(), smem()] + [vmem()] * len(args),
+        in_specs=[smem(), smem(), smem()] + [vmem()] * len(args),
         out_specs=[vmem()] * len(shapes),
         compiler_params=params(16),
         cost_estimate=estimate(pair_count, size),
         name="last_window",
-    )(me, in_hbm(pairs), *[in_vmem(x) for x in args])
+    )(me, lane, in_hbm(pairs), *[in_vmem(x) for x in args])
     return kernel, mass, row_sums, shares
 
 
@@ -406,11 +414,9 @@
     )(in_hbm(pairs), *args, in_hbm(kept))
 
 
-def weight_kernel(*refs):
-    out_ref = refs[-1]
-    mass = refs[0][...]
-    for ref in refs[1:-1]:
-        mass = mass + ref[...]
+def weight_kernel(rows_ref, *refs):
+    sums, out_ref = refs[:-1], refs[-1]
+    mass = rows_ref[...] + jnp.sum(tree([ref[...] for ref in sums]), axis=0)
     weight = 1.0 / (1.0 + mass / BR)
     parts = BR // LANES
     for block in range(BLK_DEV):
@@ -419,15 +425,15 @@
             out_ref[block * parts + part : block * parts + part + 1] = weight[block : block + 1, lanes]
 
 
-def block_weights(sums):
+def block_weights(row_sums, sums):
     out = pl.pallas_call(
         weight_kernel,
         out_shape=jax.ShapeDtypeStruct((BLK_DEV * BR // LANES, LANES), jnp.float32),
-        in_specs=[vmem()] * len(sums),
+        in_specs=[vmem()] * (1 + len(sums)),
         out_specs=vmem(),
         compiler_params=params(4),
         name="weights",
-    )(*[in_vmem(x) for x in sums])
+    )(*[in_vmem(x) for x in (row_sums, *sums)])
     return out.reshape(BLK_DEV * BR)
 
 
@@ -444,6 +450,23 @@
         parts = parts + hop(parts, step)
         step //= 2
     return parts
+
+
+def spread(pieces):
+    wide_count, narrow_count = lax.axis_size("wide"), lax.axis_size("narrow")
+    came = []
+    for number, piece in enumerate(pieces):
+        perm = []
+        for wide in range(wide_count):
+            for narrow in range(narrow_count):
+                target = (wide + number * narrow_count + narrow) % wide_count
+                perm.append((wide * narrow_count + narrow, target * narrow_count + narrow))
+        came.append(lax.ppermute(piece, ("wide", "narrow"), perm))
+    came = jnp.stack(came)
+    return [came] + [
+        lax.ppermute(came, "narrow", [(i, i ^ other) for i in range(narrow_count)])
+        for other in range(1, narrow_count)
+    ]
 
 
 def to_wide(pieces):
@@ -462,9 +485,11 @@
     capacity = max(2, 2 * pair_count // wide_count)
     feat = embeddings.shape[1]
     blocks = embeddings.reshape(BLK_DEV, BR, feat)
-    lists = to_wide([pairs] * (wide_count - 1))[::-1]
+    lane = lax.axis_index("narrow").astype(jnp.int32).reshape(1)
+    rounds = wide_count // lax.axis_size("narrow")
+    lists = spread([pairs] * rounds)
     fixed = lax.optimization_barrier
-    outgoing, row_slices = pack(me, pairs, lists, blocks, capacity)
+    outgoing, row_slices = pack(me, lane, pairs, lists, blocks, capacity, wide_count)
 
     def pick(received, chunk):
         return select(me, pairs, own, received, *CHUNKS[chunk], PIECES[chunk])
@@ -482,11 +507,11 @@
     cols_b = cols_b + last_b + hop(cols_b[1:], 1)
     square, mass, total, sums = carry
     kernel, mass, row_sums, shares = last_window(
-        me, pairs, rows, [cols_a, cols_b], square, mass, sums, wide_count
+        me, lane, pairs, rows, [cols_a, cols_b], square, mass, sums, wide_count
     )
-    came = to_wide(shares[1:])
+    col_sums = spread(shares)
     mean = means(pairs, row_slices, kernel, mass, total, [cols_a, cols_b], kept)
-    weights = block_weights([row_sums, shares[0], *came])
+    weights = block_weights(row_sums, col_sums)
     return weights, mean.reshape(BLK_DEV * BR, feat)
 
 

time: 87.4 us -> 94.4 us (1.080)
  starting transfers between devices: 29.5 us -> 39.1 us
  waiting for transfers between devices: 37.1 us -> 34.5 us
    ppermute x0 -> x8, starting transfers between devices: none -> 17.8 us  [the longest x6 15.8 us: spread(): lax.ppermute(came, 'narrow', [(i, i ^ other) for i in range(narrow_count)])]
    ppermute x12 -> x6, starting transfers between devices: 24.1 us -> 15.4 us  [to_wide(): lax.ppermute(piece, 'wide', [(i, (i + shift) % count) for i in range(coun...]
    ppermute x12 -> x6, waiting for transfers between devices: 16.2 us -> 11.7 us  [to_wide(): lax.ppermute(piece, 'wide', [(i, (i + shift) % count) for i in range(coun...]
    ppermute x0 -> x8, waiting for transfers between devices: none -> 2.66 us  [the longest x6 2.65 us: spread(): lax.ppermute(came, 'narrow', [(i, i ^ other) for i in range(narrow_count)])]
  transfers between devices with their start and end apart: 23 -> 25, of which waited for: 15 -> 15; matrix products, arithmetic and copies ran while one was open for 0% -> 0% of each run, Pallas kernels for 14% -> 13%
where the time goes in v14:
time: 94.4 us; the launch traced here: 94.1 us
  starting transfers between devices  39.1 us (41%)
  waiting for transfers between devices  34.5 us (37%)
  Pallas kernels  19.5 us (21%)
    ppermute x11, waiting for transfers between devices, hop(): lax.ppermute(piece, 'narrow', perm)  20.2 us
    ppermute x6, starting transfers between devices, spread(): lax.ppermute(came, 'narrow', [(i, i ^ other) for i in range(narrow_count)])  15.8 us
    ppermute x6, starting transfers between devices, to_wide(): lax.ppermute(piece, 'wide', [(i, (i + shift) % count) for i in range(coun...  15.4 us
    ppermute x6, waiting for transfers between devices, to_wide(): lax.ppermute(piece, 'wide', [(i, (i + shift) % count) for i in range(coun...  11.7 us
    pallas_call x1, Pallas kernels, keep(): pl.pallas_call(keep_kernel, out_shape=[pltpu.HBM(blocks.shape, blocks.dty...  6.02 us
    ppermute x11, starting transfers between devices, hop(): lax.ppermute(piece, 'narrow', perm)  5.85 us
    pallas_call x1, Pallas kernels, pack(): pl.pallas_call(functools.partial(pack_kernel, wide_count, len(lists), cap...  3.15 us
    pallas_call x1, Pallas kernels, first_window(): pl.pallas_call(functools.partial(first_kernel, window, len(cols[0])), out...  3.1 us
  transfers between devices with their start and end apart: 25, of which 15 were waited for; matrix products, arithmetic and copies ran while one was open for 0% of the time, Pallas kernels for 13%

profile of v14, /device:TPU:0, one launch (start us, length us, event | category | flops | bytes accessed | tf_op | source)
XLA Modules:
  0.0 94.1 jit_solution(10481983530260303811)
XLA Ops:
  0.6 1.3 %collective-permute-start = (s32[2,4]{1,0:T(2,128)}, s32[2,4]{1,0:T(2,128)S(1)}, u32[]{:S(2)}, u32[]{:S(2)}) collective-permute-start(s32[2,4]{1,0:T(2,128)} %bitcast.24), channel_id=1, source_target_pairs={{0,0},{1,5},{2,10},{3,15},{4,4},{5,9},{6,14},{7,3},{8,8},{9,13},{1... | collective-permute-start | bytes 104 | tf_op jit(solution)/shard_map/ppermute | solution.py:464
  2.0 7.2 %collective-permute-start.3 = (s32[1,2,4]{2,1,0:T(2,128)S(1)}, s32[1,2,4]{2,1,0:T(2,128)S(1)}, u32[]{:S(2)}, u32[]{:S(2)}) collective-permute-start(s32[1,2,4]{2,1,0:T(2,128)S(1)} %bitcast.15), channel_id=1, source_target_pairs={{0,3},{1,2},{2,1},{3,0},{4,7},{5,6},{6,5},{7,4},{8,11},{9,10},{10,... | collective-permute-start | bytes 104 | tf_op jit(solution)/shard_map/ppermute | solution.py:467
  9.2 1.0 %collective-permute-start.2 = (s32[1,2,4]{2,1,0:T(2,128)S(1)}, s32[1,2,4]{2,1,0:T(2,128)S(1)}, u32[]{:S(2)}, u32[]{:S(2)}) collective-permute-start(s32[1,2,4]{2,1,0:T(2,128)S(1)} %bitcast.16), channel_id=1, source_target_pairs={{0,2},{1,3},{2,0},{3,1},{4,6},{5,7},{6,4},{7,5},{8,10},{9,11},{10,... | collective-permute-start | bytes 104 | tf_op jit(solution)/shard_map/ppermute | solution.py:467
  10.5 2.3 %collective-permute-done.2.refs_2_ = s32[1,2,4]{2,1,0:T(2,128)S(1)} collective-permute-done((s32[1,2,4]{2,1,0:T(2,128)S(1)}, s32[1,2,4]{2,1,0:T(2,128)S(1)}, u32[]{:S(2)}, u32[]{:S(2)}) %collective-permute-start.2) | collective-permute-done | bytes 64 | tf_op jit(solution)/shard_map/ppermute | solution.py:467
  12.7 3.2 %pack.1 = (bf16[2,320,256]{2,1,0:T(8,128)(2,1)S(1)}, bf16[2,320,256]{2,1,0:T(8,128)(2,1)S(1)}, bf16[2,320,256]{2,1,0:T(8,128)(2,1)S(1)}, bf16[2,192,256]{2,1,0:T...) custom-call(s32[1]{0:T(128)} %bitcast.me_ref, ...), custom_call_target="tpu_custom_call" | custom-call | tf_op jit(solution)/shard_map/pack/pallas_call | solution.py:88
  15.9 1.1 %collective-permute-start.4 = (bf16[4,512,256]{2,1,0:T(8,128)(2,1)S(1)}, bf16[4,512,256]{2,1,0:T(8,128)(2,1)S(1)}, u32[]{:S(2)}, u32[]{:S(2)}) collective-permute-start(bf16[4,512,256]{2,1,0:T(8,128)(2,1)S(1)} %get-tuple-element.42.rows_ref), channel_id=1, source_target_pairs={{0,2},{1,3},{2,0},{3,1},{4,6},{5,7},{6,4},{7,5},{8,10},{9,11},{10,... | collective-permute-start | bytes 3145736 | tf_op jit(solution)/shard_map/ppermute | solution.py:443
  17.0 1.1 %collective-permute-start.5 = (bf16[2,320,256]{2,1,0:T(8,128)(2,1)S(1)}, bf16[2,320,256]{2,1,0:T(8,128)(2,1)S(1)}, u32[]{:S(2)}, u32[]{:S(2)}) collective-permute-start(bf16[2,320,256]{2,1,0:T(8,128)(2,1)S(1)} %get-tuple-element.43), channel_id=1, source_target_pairs={{0,4},{4,8},{8,12},{12,0},{1,5},{5,9},{9,13},{13,1},{2,6},{6,10},{... | collective-permute-start | bytes 983048 | tf_op jit(solution)/shard_map/ppermute | solution.py:475
  18.1 2.6 %collective-permute-start.6 = (bf16[2,320,256]{2,1,0:T(8,128)(2,1)S(1)}, bf16[2,320,256]{2,1,0:T(8,128)(2,1)S(1)}, u32[]{:S(2)}, u32[]{:S(2)}) collective-permute-start(bf16[2,320,256]{2,1,0:T(8,128)(2,1)S(1)} %get-tuple-element.44), channel_id=1, source_target_pairs={{0,8},{4,12},{8,0},{12,4},{1,9},{5,13},{9,1},{13,5},{2,10},{6,14},... | collective-permute-start | bytes 983048 | tf_op jit(solution)/shard_map/ppermute | solution.py:475
  20.7 1.3 %collective-permute-start.7 = (bf16[2,320,256]{2,1,0:T(8,128)(2,1)S(1)}, bf16[2,320,256]{2,1,0:T(8,128)(2,1)S(1)}, u32[]{:S(2)}, u32[]{:S(2)}) collective-permute-start(bf16[2,320,256]{2,1,0:T(8,128)(2,1)S(1)} %get-tuple-element.45), channel_id=1, source_target_pairs={{0,12},{4,0},{8,4},{12,8},{1,13},{5,1},{9,5},{13,9},{2,14},{6,2},{... | collective-permute-start | bytes 983048 | tf_op jit(solution)/shard_map/ppermute | solution.py:475
  22.0 6.0 %keep.1 = (bf16[8,512,256]{2,1,0:T(8,128)(2,1)}, bf16[4,512,256]{2,1,0:T(8,128)(2,1)S(1)}) custom-call(s32[2,4]{1,0:T(2,128)} %bitcast.26, bf16[8,512,256]{2,1,0:T(8,128)(2,1)} %bitcast.20, bf16[8,512,256]{2,1,0:T(8,128)(2,1)} %bitcast.21), custom_call_target="tpu_custom_call" | custom-call | tf_op jit(solution)/shard_map/keep/pallas_call | solution.py:328
  28.1 13.1 %collective-permute-done.4 = bf16[4,512,256]{2,1,0:T(8,128)(2,1)S(1)} collective-permute-done((bf16[4,512,256]{2,1,0:T(8,128)(2,1)S(1)}, bf16[4,512,256]{2,1,0:T(8,128)(2,1)S(1)}, u32[]{:S(2)}, u32[]{:S(2)}) %collective-permute-start.4) | collective-permute-done | bytes 1048608 | tf_op jit(solution)/shard_map/ppermute | solution.py:443
  41.8 7.5 %collective-permute-start.11 = (bf16[2,192,256]{2,1,0:T(8,128)(2,1)S(1)}, bf16[2,192,256]{2,1,0:T(8,128)(2,1)S(1)}, u32[]{:S(2)}, u32[]{:S(2)}) collective-permute-start(bf16[2,192,256]{2,1,0:T(8,128)(2,1)S(1)} %get-tuple-element.55), channel_id=1, source_target_pairs={{0,4},{4,8},{8,12},{12,0},{1,5},{5,9},{9,13},{13,1},{2,6},{6,10},{... | collective-permute-start | bytes 589832 | tf_op jit(solution)/shard_map/ppermute | solution.py:475
  49.3 0.8 select.2
  50.1 1.5 %collective-permute-start.8 = (bf16[2,320,256]{2,1,0:T(8,128)(2,1)S(1)}, bf16[2,320,256]{2,1,0:T(8,128)(2,1)S(1)}, u32[]{:S(2)}, u32[]{:S(2)}) collective-permute-start(bf16[2,320,256]{2,1,0:T(8,128)(2,1)S(1)} %get-tuple-element.60.refs_2_.refs_0_), channel_id=1, source_target_pairs={{0,2},{1,3},{2,0},{3,1},{4,6},{5,7},{6,4},{7,5},{8,10},{9,11},{10,... | collective-permute-start | bytes 983048 | tf_op jit(solution)/shard_map/ppermute | solution.py:443
  52.2 1.2 %collective-permute-start.12 = (bf16[2,192,256]{2,1,0:T(8,128)(2,1)S(1)}, bf16[2,192,256]{2,1,0:T(8,128)(2,1)S(1)}, u32[]{:S(2)}, u32[]{:S(2)}) collective-permute-start(bf16[2,192,256]{2,1,0:T(8,128)(2,1)S(1)} %get-tuple-element.56), channel_id=1, source_target_pairs={{0,8},{4,12},{8,0},{12,4},{1,9},{5,13},{9,1},{13,5},{2,10},{6,14},... | collective-permute-start | bytes 589832 | tf_op jit(solution)/shard_map/ppermute | solution.py:475
  53.4 2.3 %collective-permute-done.11.refs_0_ = bf16[2,192,256]{2,1,0:T(8,128)(2,1)S(1)} collective-permute-done((bf16[2,192,256]{2,1,0:T(8,128)(2,1)S(1)}, bf16[2,192,256]{2,1,0:T(8,128)(2,1)S(1)}, u32[]{:S(2)}, u32[]{:S(2)}) %collective-permute-start.11) | collective-permute-done | bytes 196640 | tf_op jit(solution)/shard_map/ppermute | solution.py:475
  55.7 1.7 %collective-permute-start.13 = (bf16[2,192,256]{2,1,0:T(8,128)(2,1)S(1)}, bf16[2,192,256]{2,1,0:T(8,128)(2,1)S(1)}, u32[]{:S(2)}, u32[]{:S(2)}) collective-permute-start(bf16[2,192,256]{2,1,0:T(8,128)(2,1)S(1)} %get-tuple-element.57), channel_id=1, source_target_pairs={{0,12},{4,0},{8,4},{12,8},{1,13},{5,1},{9,5},{13,9},{2,14},{6,2},{... | collective-permute-start | bytes 589832 | tf_op jit(solution)/shard_map/ppermute | solution.py:475
  57.4 6.6 %collective-permute-done.12.refs_1_ = bf16[2,192,256]{2,1,0:T(8,128)(2,1)S(1)} collective-permute-done((bf16[2,192,256]{2,1,0:T(8,128)(2,1)S(1)}, bf16[2,192,256]{2,1,0:T(8,128)(2,1)S(1)}, u32[]{:S(2)}, u32[]{:S(2)}) %collective-permute-start.12) | collective-permute-done | bytes 196640 | tf_op jit(solution)/shard_map/ppermute | solution.py:475
  64.1 2.3 %collective-permute-done.13.refs_2_ = bf16[2,192,256]{2,1,0:T(8,128)(2,1)S(1)} collective-permute-done((bf16[2,192,256]{2,1,0:T(8,128)(2,1)S(1)}, bf16[2,192,256]{2,1,0:T(8,128)(2,1)S(1)}, u32[]{:S(2)}, u32[]{:S(2)}) %collective-permute-start.13) | collective-permute-done | bytes 196640 | tf_op jit(solution)/shard_map/ppermute | solution.py:475
  66.3 0.7 collective-permute-done.9.refs_5_
  67.0 0.8 select.3.refs_10_.refs_2_
  67.8 1.5 %collective-permute-start.18 = (bf16[4,192,256]{2,1,0:T(8,128)(2,1)S(1)}, bf16[4,192,256]{2,1,0:T(8,128)(2,1)S(1)}, u32[]{:S(2)}, u32[]{:S(2)}) collective-permute-start(bf16[4,192,256]{2,1,0:T(8,128)(2,1)S(1)} %select.3.refs_10_.refs_2_), channel_id=1, source_target_pairs={{0,2},{1,3},{2,0},{3,1},{4,6},{5,7},{6,4},{7,5},{8,10},{9,11},{10,... | collective-permute-start | bytes 1179656 | tf_op jit(solution)/shard_map/ppermute | solution.py:443
  70.4 0.6 collective-permute-done.16.refs_8_
  72.4 3.1 %first_window.1 = (f32[4,512,128]{2,1,0:T(8,128)S(1)}, f32[4,512,128]{2,1,0:T(8,128)S(1)}, f32[4,512,256]{2,1,0:T(8,128)S(1)}, f32[4,256]{1,0:T(4,128)S(1)}) custom-call(bf16[2,4,512,256]{3,2,1,0:T(8,128)(2,1)S(1)} %pad_maximum_fusion.refs_0_, bf16[2,4,512,256]{3,2,1,0:T(8,128)(2,1)S(1)} %collective-permute-done.10.refs_1_, ...), custom_call_target="tpu_custom_call" | custom-call | tf_op jit(solution)/shard_map/first_window/pallas_call | solution.py:268
  75.5 2.8 %collective-permute-done.18.refs_11_ = bf16[4,192,256]{2,1,0:T(8,128)(2,1)S(1)} collective-permute-done((bf16[4,192,256]{2,1,0:T(8,128)(2,1)S(1)}, bf16[4,192,256]{2,1,0:T(8,128)(2,1)S(1)}, u32[]{:S(2)}, u32[]{:S(2)}) %collective-permute-start.18) | collective-permute-done | bytes 393248 | tf_op jit(solution)/shard_map/ppermute | solution.py:443
  78.3 1.7 %collective-permute-done.20.refs_13_ = bf16[4,192,256]{2,1,0:T(8,128)(2,1)S(1)} collective-permute-done((bf16[4,192,256]{2,1,0:T(8,128)(2,1)S(1)}, bf16[4,192,256]{2,1,0:T(8,128)(2,1)S(1)}, u32[]{:S(2)}, u32[]{:S(2)}) %collective-permute-start.20) | collective-permute-done | bytes 393248 | tf_op jit(solution)/shard_map/ppermute | solution.py:443
  80.1 2.6 %last_window.1 = (bf16[4,512,256]{2,1,0:T(8,128)(2,1)S(1)}, f32[4,512,128]{2,1,0:T(8,128)S(1)}, f32[8,512]{1,0:T(8,128)S(1)}, f32[8,512]{1,0:T(8,128)S(1)}) custom-call(s32[1]{0:T(128)} %bitcast.me_ref, s32[1]{0:T(128)} %bitcast.1.lane_ref, s32[2,4]{1,0:T(2,128)} %bitcast.29, bf16[2,4,512,256]{3,2,1,0:T(8,128)(2,1)S(1)} %pad_maximum_fusion.refs_0_, ...), custom_call_target="tpu_custom_call" | custom-call | flops 1073741824 | bytes 8388608 | tf_op jit(solution)/shard_map/last_window/pallas_call | solution.py:292
  82.7 0.7 collective-permute-start.21
  83.4 6.4 %collective-permute-start.24 = (f32[1,8,512]{2,1,0:T(8,128)S(1)}, f32[1,8,512]{2,1,0:T(8,128)S(1)}, u32[]{:S(2)}, u32[]{:S(2)}) collective-permute-start(f32[1,8,512]{2,1,0:T(8,128)S(1)} %bitcast.11), channel_id=1, source_target_pairs={{0,3},{1,2},{2,1},{3,0},{4,7},{5,6},{6,5},{7,4},{8,11},{9,10},{10,... | collective-permute-start | bytes 49160 | tf_op jit(solution)/shard_map/ppermute | solution.py:467
  89.7 1.1 %collective-permute-start.23 = (f32[1,8,512]{2,1,0:T(8,128)S(1)}, f32[1,8,512]{2,1,0:T(8,128)S(1)}, u32[]{:S(2)}, u32[]{:S(2)}) collective-permute-start(f32[1,8,512]{2,1,0:T(8,128)S(1)} %bitcast.12), channel_id=1, source_target_pairs={{0,2},{1,3},{2,0},{3,1},{4,6},{5,7},{6,4},{7,5},{8,10},{9,11},{10,... | collective-permute-start | bytes 49160 | tf_op jit(solution)/shard_map/ppermute | solution.py:467
  90.9 2.3 %means.1 = bf16[8,512,256]{2,1,0:T(8,128)(2,1)} custom-call(s32[2,4]{1,0:T(2,128)} %bitcast.30, bf16[4,512,256]{2,1,0:T(8,128)(2,1)S(1)} %get-tuple-element.42.rows_ref, bf16[4,512,256]{2,1,0:T(8,128)(2,1)S(1)} %get-tuple-element.78.kernel_ref, f32[4,512,128]{2,1,0:T(8,128)S(1)} %get-tuple-element.79.mass_ref, ...), custom_call_target="tpu_custom_call", output_to_operand_aliasing={{}: (8, {})} | custom-call | flops 536870912 | bytes 8388608 | tf_op jit(solution)/shard_map/means/pallas_call | solution.py:397
  93.5 0.6 weights.1
  (27 shorter events, 4.2 us)
Async XLA Ops:
  0.6 1.3 %collective-permute-start = (s32[2,4]{1,0:T(2,128)}, s32[2,4]{1,0:T(2,128)S(1)}, u32[]{:S(2)}, u32[]{:S(2)}) collective-permute-start(s32[2,4]{1,0:T(2,128)} %bitcast.24), channel_id=1, source_target_pairs={{0,0},{1,5},{2,10},{3,15},{4,4},{5,9},{6,14},{7,3},{8,8},{9,13},{1... | collective-permute-start | bytes 104 | tf_op jit(solution)/shard_map/ppermute | solution.py:464
  2.0 8.5 %collective-permute-start.3 = (s32[1,2,4]{2,1,0:T(2,128)S(1)}, s32[1,2,4]{2,1,0:T(2,128)S(1)}, u32[]{:S(2)}, u32[]{:S(2)}) collective-permute-start(s32[1,2,4]{2,1,0:T(2,128)S(1)} %bitcast.15), channel_id=1, source_target_pairs={{0,3},{1,2},{2,1},{3,0},{4,7},{5,6},{6,5},{7,4},{8,11},{9,10},{10,... | collective-permute-start | bytes 104 | tf_op jit(solution)/shard_map/ppermute | solution.py:467
  9.2 3.6 %collective-permute-start.2 = (s32[1,2,4]{2,1,0:T(2,128)S(1)}, s32[1,2,4]{2,1,0:T(2,128)S(1)}, u32[]{:S(2)}, u32[]{:S(2)}) collective-permute-start(s32[1,2,4]{2,1,0:T(2,128)S(1)} %bitcast.16), channel_id=1, source_target_pairs={{0,2},{1,3},{2,0},{3,1},{4,6},{5,7},{6,4},{7,5},{8,10},{9,11},{10,... | collective-permute-start | bytes 104 | tf_op jit(solution)/shard_map/ppermute | solution.py:467
  10.2 2.6 %collective-permute-start.1 = (s32[1,2,4]{2,1,0:T(2,128)S(1)}, s32[1,2,4]{2,1,0:T(2,128)S(1)}, u32[]{:S(2)}, u32[]{:S(2)}) collective-permute-start(s32[1,2,4]{2,1,0:T(2,128)S(1)} %bitcast.17), channel_id=1, source_target_pairs={{0,1},{1,0},{2,3},{3,2},{4,5},{5,4},{6,7},{7,6},{8,9},{9,8},{10,11... | collective-permute-start | bytes 104 | tf_op jit(solution)/shard_map/ppermute | solution.py:467
  15.9 25.2 %collective-permute-start.4 = (bf16[4,512,256]{2,1,0:T(8,128)(2,1)S(1)}, bf16[4,512,256]{2,1,0:T(8,128)(2,1)S(1)}, u32[]{:S(2)}, u32[]{:S(2)}) collective-permute-start(bf16[4,512,256]{2,1,0:T(8,128)(2,1)S(1)} %get-tuple-element.42.rows_ref), channel_id=1, source_target_pairs={{0,2},{1,3},{2,0},{3,1},{4,6},{5,7},{6,4},{7,5},{8,10},{9,11},{10,... | collective-permute-start | bytes 3145736 | tf_op jit(solution)/shard_map/ppermute | solution.py:443
  17.0 24.4 %collective-permute-start.5 = (bf16[2,320,256]{2,1,0:T(8,128)(2,1)S(1)}, bf16[2,320,256]{2,1,0:T(8,128)(2,1)S(1)}, u32[]{:S(2)}, u32[]{:S(2)}) collective-permute-start(bf16[2,320,256]{2,1,0:T(8,128)(2,1)S(1)} %get-tuple-element.43), channel_id=1, source_target_pairs={{0,4},{4,8},{8,12},{12,0},{1,5},{5,9},{9,13},{13,1},{2,6},{6,10},{... | collective-permute-start | bytes 983048 | tf_op jit(solution)/shard_map/ppermute | solution.py:475
  18.1 23.7 %collective-permute-start.6 = (bf16[2,320,256]{2,1,0:T(8,128)(2,1)S(1)}, bf16[2,320,256]{2,1,0:T(8,128)(2,1)S(1)}, u32[]{:S(2)}, u32[]{:S(2)}) collective-permute-start(bf16[2,320,256]{2,1,0:T(8,128)(2,1)S(1)} %get-tuple-element.44), channel_id=1, source_target_pairs={{0,8},{4,12},{8,0},{12,4},{1,9},{5,13},{9,1},{13,5},{2,10},{6,14},... | collective-permute-start | bytes 983048 | tf_op jit(solution)/shard_map/ppermute | solution.py:475
  20.7 21.1 %collective-permute-start.7 = (bf16[2,320,256]{2,1,0:T(8,128)(2,1)S(1)}, bf16[2,320,256]{2,1,0:T(8,128)(2,1)S(1)}, u32[]{:S(2)}, u32[]{:S(2)}) collective-permute-start(bf16[2,320,256]{2,1,0:T(8,128)(2,1)S(1)} %get-tuple-element.45), channel_id=1, source_target_pairs={{0,12},{4,0},{8,4},{12,8},{1,13},{5,1},{9,5},{13,9},{2,14},{6,2},{... | collective-permute-start | bytes 983048 | tf_op jit(solution)/shard_map/ppermute | solution.py:475
  41.8 25.2 %collective-permute-start.10 = (bf16[2,4,512,256]{3,2,1,0:T(8,128)(2,1)S(1)}, bf16[2,4,512,256]{3,2,1,0:T(8,128)(2,1)S(1)}, u32[]{:S(2)}, u32[]{:S(2)}) collective-permute-start(bf16[2,4,512,256]{3,2,1,0:T(8,128)(2,1)S(1)} %pad_maximum_fusion.refs_0_), channel_id=1, source_target_pairs={{0,1},{1,0},{2,3},{3,2},{4,5},{5,4},{6,7},{7,6},{8,9},{9,8},{10,11... | collective-permute-start | bytes 6291464 | tf_op jit(solution)/shard_map/ppermute | solution.py:443
  41.8 13.9 %collective-permute-start.11 = (bf16[2,192,256]{2,1,0:T(8,128)(2,1)S(1)}, bf16[2,192,256]{2,1,0:T(8,128)(2,1)S(1)}, u32[]{:S(2)}, u32[]{:S(2)}) collective-permute-start(bf16[2,192,256]{2,1,0:T(8,128)(2,1)S(1)} %get-tuple-element.55), channel_id=1, source_target_pairs={{0,4},{4,8},{8,12},{12,0},{1,5},{5,9},{9,13},{13,1},{2,6},{6,10},{... | collective-permute-start | bytes 589832 | tf_op jit(solution)/shard_map/ppermute | solution.py:475
  50.1 16.3 %collective-permute-start.8 = (bf16[2,320,256]{2,1,0:T(8,128)(2,1)S(1)}, bf16[2,320,256]{2,1,0:T(8,128)(2,1)S(1)}, u32[]{:S(2)}, u32[]{:S(2)}) collective-permute-start(bf16[2,320,256]{2,1,0:T(8,128)(2,1)S(1)} %get-tuple-element.60.refs_2_.refs_0_), channel_id=1, source_target_pairs={{0,2},{1,3},{2,0},{3,1},{4,6},{5,7},{6,4},{7,5},{8,10},{9,11},{10,... | collective-permute-start | bytes 983048 | tf_op jit(solution)/shard_map/ppermute | solution.py:443
  51.6 15.4 %collective-permute-start.9 = (bf16[2,320,256]{2,1,0:T(8,128)(2,1)S(1)}, bf16[2,320,256]{2,1,0:T(8,128)(2,1)S(1)}, u32[]{:S(2)}, u32[]{:S(2)}) collective-permute-start(bf16[2,320,256]{2,1,0:T(8,128)(2,1)S(1)} %get-tuple-element.61.refs_3_.refs_1_), channel_id=1, source_target_pairs={{0,2},{1,3},{2,0},{3,1},{4,6},{5,7},{6,4},{7,5},{8,10},{9,11},{10,... | collective-permute-start | bytes 983048 | tf_op jit(solution)/shard_map/ppermute | solution.py:443
  52.2 11.9 %collective-permute-start.12 = (bf16[2,192,256]{2,1,0:T(8,128)(2,1)S(1)}, bf16[2,192,256]{2,1,0:T(8,128)(2,1)S(1)}, u32[]{:S(2)}, u32[]{:S(2)}) collective-permute-start(bf16[2,192,256]{2,1,0:T(8,128)(2,1)S(1)} %get-tuple-element.56), channel_id=1, source_target_pairs={{0,8},{4,12},{8,0},{12,4},{1,9},{5,13},{9,1},{13,5},{2,10},{6,14},... | collective-permute-start | bytes 589832 | tf_op jit(solution)/shard_map/ppermute | solution.py:475
  55.7 10.6 %collective-permute-start.13 = (bf16[2,192,256]{2,1,0:T(8,128)(2,1)S(1)}, bf16[2,192,256]{2,1,0:T(8,128)(2,1)S(1)}, u32[]{:S(2)}, u32[]{:S(2)}) collective-permute-start(bf16[2,192,256]{2,1,0:T(8,128)(2,1)S(1)} %get-tuple-element.57), channel_id=1, source_target_pairs={{0,12},{4,0},{8,4},{12,8},{1,13},{5,1},{9,5},{13,9},{2,14},{6,2},{... | collective-permute-start | bytes 589832 | tf_op jit(solution)/shard_map/ppermute | solution.py:475
  67.8 10.5 %collective-permute-start.18 = (bf16[4,192,256]{2,1,0:T(8,128)(2,1)S(1)}, bf16[4,192,256]{2,1,0:T(8,128)(2,1)S(1)}, u32[]{:S(2)}, u32[]{:S(2)}) collective-permute-start(bf16[4,192,256]{2,1,0:T(8,128)(2,1)S(1)} %select.3.refs_10_.refs_2_), channel_id=1, source_target_pairs={{0,2},{1,3},{2,0},{3,1},{4,6},{5,7},{6,4},{7,5},{8,10},{9,11},{10,... | collective-permute-start | bytes 1179656 | tf_op jit(solution)/shard_map/ppermute | solution.py:443
  69.4 1.6 %collective-permute-start.16 = (bf16[2,320,256]{2,1,0:T(8,128)(2,1)S(1)}, bf16[2,320,256]{2,1,0:T(8,128)(2,1)S(1)}, u32[]{:S(2)}, u32[]{:S(2)}) collective-permute-start(bf16[2,320,256]{2,1,0:T(8,128)(2,1)S(1)} %collective-permute-done.8.refs_4_), channel_id=1, source_target_pairs={{0,1},{1,0},{2,3},{3,2},{4,5},{5,4},{6,7},{7,6},{8,9},{9,8},{10,11... | collective-permute-start | bytes 983048 | tf_op jit(solution)/shard_map/ppermute | solution.py:443
  69.4 2.1 %collective-permute-start.17 = (bf16[2,320,256]{2,1,0:T(8,128)(2,1)S(1)}, bf16[2,320,256]{2,1,0:T(8,128)(2,1)S(1)}, u32[]{:S(2)}, u32[]{:S(2)}) collective-permute-start(bf16[2,320,256]{2,1,0:T(8,128)(2,1)S(1)} %collective-permute-done.9.refs_5_), channel_id=1, source_target_pairs={{0,1},{1,0},{2,3},{3,2},{4,5},{5,4},{6,7},{7,6},{8,9},{9,8},{10,11... | collective-permute-start | bytes 983048 | tf_op jit(solution)/shard_map/ppermute | solution.py:443
  69.9 2.1 %collective-permute-start.14 = (bf16[2,320,256]{2,1,0:T(8,128)(2,1)S(1)}, bf16[2,320,256]{2,1,0:T(8,128)(2,1)S(1)}, u32[]{:S(2)}, u32[]{:S(2)}) collective-permute-start(bf16[2,320,256]{2,1,0:T(8,128)(2,1)S(1)} %get-tuple-element.60.refs_2_.refs_0_), channel_id=1, source_target_pairs={{0,1},{1,0},{2,3},{3,2},{4,5},{5,4},{6,7},{7,6},{8,9},{9,8},{10,11... | collective-permute-start | bytes 983048 | tf_op jit(solution)/shard_map/ppermute | solution.py:443
  69.9 2.5 %collective-permute-start.15 = (bf16[2,320,256]{2,1,0:T(8,128)(2,1)S(1)}, bf16[2,320,256]{2,1,0:T(8,128)(2,1)S(1)}, u32[]{:S(2)}, u32[]{:S(2)}) collective-permute-start(bf16[2,320,256]{2,1,0:T(8,128)(2,1)S(1)} %get-tuple-element.61.refs_3_.refs_1_), channel_id=1, source_target_pairs={{0,1},{1,0},{2,3},{3,2},{4,5},{5,4},{6,7},{7,6},{8,9},{9,8},{10,11... | collective-permute-start | bytes 983048 | tf_op jit(solution)/shard_map/ppermute | solution.py:443
  71.0 7.4 %collective-permute-start.19 = (bf16[4,192,256]{2,1,0:T(8,128)(2,1)S(1)}, bf16[4,192,256]{2,1,0:T(8,128)(2,1)S(1)}, u32[]{:S(2)}, u32[]{:S(2)}) collective-permute-start(bf16[4,192,256]{2,1,0:T(8,128)(2,1)S(1)} %select.3.refs_10_.refs_2_), channel_id=1, source_target_pairs={{0,1},{1,0},{2,3},{3,2},{4,5},{5,4},{6,7},{7,6},{8,9},{9,8},{10,11... | collective-permute-start | bytes 1179656 | tf_op jit(solution)/shard_map/ppermute | solution.py:443
  78.3 1.7 %collective-permute-start.20 = (bf16[4,192,256]{2,1,0:T(8,128)(2,1)S(1)}, bf16[4,192,256]{2,1,0:T(8,128)(2,1)S(1)}, u32[]{:S(2)}, u32[]{:S(2)}) collective-permute-start(bf16[4,192,256]{2,1,0:T(8,128)(2,1)S(1)} %collective-permute-done.18.refs_11_), channel_id=1, source_target_pairs={{0,1},{1,0},{2,3},{3,2},{4,5},{5,4},{6,7},{7,6},{8,9},{9,8},{10,11... | collective-permute-start | bytes 1179656 | tf_op jit(solution)/shard_map/ppermute | solution.py:443
  82.7 0.7 collective-permute-start.21
  83.4 9.9 %collective-permute-start.24 = (f32[1,8,512]{2,1,0:T(8,128)S(1)}, f32[1,8,512]{2,1,0:T(8,128)S(1)}, u32[]{:S(2)}, u32[]{:S(2)}) collective-permute-start(f32[1,8,512]{2,1,0:T(8,128)S(1)} %bitcast.11), channel_id=1, source_target_pairs={{0,3},{1,2},{2,1},{3,0},{4,7},{5,6},{6,5},{7,4},{8,11},{9,10},{10,... | collective-permute-start | bytes 49160 | tf_op jit(solution)/shard_map/ppermute | solution.py:467
  89.7 3.7 %collective-permute-start.23 = (f32[1,8,512]{2,1,0:T(8,128)S(1)}, f32[1,8,512]{2,1,0:T(8,128)S(1)}, u32[]{:S(2)}, u32[]{:S(2)}) collective-permute-start(f32[1,8,512]{2,1,0:T(8,128)S(1)} %bitcast.12), channel_id=1, source_target_pairs={{0,2},{1,3},{2,0},{3,1},{4,6},{5,7},{6,4},{7,5},{8,10},{9,11},{10,... | collective-permute-start | bytes 49160 | tf_op jit(solution)/shard_map/ppermute | solution.py:467
  90.8 2.6 %collective-permute-start.22 = (f32[1,8,512]{2,1,0:T(8,128)S(1)}, f32[1,8,512]{2,1,0:T(8,128)S(1)}, u32[]{:S(2)}, u32[]{:S(2)}) collective-permute-start(f32[1,8,512]{2,1,0:T(8,128)S(1)} %bitcast.13), channel_id=1, source_target_pairs={{0,1},{1,0},{2,3},{3,2},{4,5},{5,4},{6,7},{7,6},{8,9},{9,8},{10,11... | collective-permute-start | bytes 49160 | tf_op jit(solution)/shard_map/ppermute | solution.py:467

commit v15 on v12

v15 whole, which is shorter than its diff:
```python
import functools

import jax
import jax.numpy as jnp
from jax import lax
from jax.experimental import pallas as pl
from jax.experimental.pallas import tpu as pltpu
from jax.sharding import PartitionSpec as P

F = 1024
BR = 512
BLK_DEV = 8
LANES = 128
CHUNKS = ((0, 320), (320, 192))
WINDOWS = ((0, 256), (256, 512))


def smem():
    return pl.BlockSpec(memory_space=pltpu.SMEM)


def vmem():
    return pl.BlockSpec(memory_space=pltpu.VMEM)


def anywhere():
    return pl.BlockSpec(memory_space=pl.ANY)


def in_vmem(x):
    return pltpu.with_memory_space_constraint(x, pltpu.VMEM)


def in_hbm(x):
    return pltpu.with_memory_space_constraint(x, pltpu.HBM)


def params(mebibytes):
    return pltpu.CompilerParams(vmem_limit_bytes=mebibytes * 1024 * 1024)


def pair_at(lane_ref, pair_count, place):
    half = pair_count // 2
    pair = place + (lane_ref[0] & 1) * half
    return jnp.where(pair >= pair_count, pair - pair_count, pair)


def pack_kernel(wide_count, pair_count, capacity, me_ref, lane_ref, pairs_ref, *refs):
    lists, blocks_ref = refs[: wide_count - 1], refs[wide_count - 1]
    *outs, rows_ref, sems = refs[wide_count:]
    me = me_ref[0]
    copies = []

    def send(source, target):
        copies.append(pltpu.make_async_copy(source, target, sems.at[len(copies)]))
        copies[-1].start()

    for chunk, (start, size) in enumerate(CHUNKS):
        for shift in range(1, wide_count):
            asked = lists[shift - 1]
            picks = [jnp.int32(0)] * capacity
            count = jnp.int32(0)
            for pair in range(pair_count):
                col = asked[1, pair]
                mine = (col >> 3) == me
                for slot in range(capacity):
                    picks[slot] = jnp.where(mine & (count == slot), col & 7, picks[slot])
                count = count + mine.astype(jnp.int32)
            out = outs[chunk * (wide_count - 1) + shift - 1]
            for slot in range(capacity):
                send(blocks_ref.at[picks[slot], pl.ds(start, size)], out.at[slot])
    for place in range(pair_count):
        pair = pair_at(lane_ref, pair_count, place)
        send(blocks_ref.at[pairs_ref[0, pair] & 7], rows_ref.at[place])
    for copy in copies:
        copy.wait()


def pack(me, lane, pairs, lists, blocks, capacity):
    wide_count, pair_count = len(lists) + 1, pairs.shape[1]
    feat = blocks.shape[-1]
    shapes = [
        pltpu.VMEM((capacity, size, feat), blocks.dtype)
        for _, size in CHUNKS
        for _ in range(1, wide_count)
    ] + [pltpu.VMEM((pair_count, BR, feat), blocks.dtype)]
    copies = (len(shapes) - 1) * capacity + pair_count
    outs = pl.pallas_call(
        functools.partial(pack_kernel, wide_count, pair_count, capacity),
        out_shape=shapes,
        in_specs=[smem()] * (2 + wide_count) + [anywhere()],
        out_specs=[anywhere()] * len(shapes),
        scratch_shapes=[pltpu.SemaphoreType.DMA((copies,))],
        compiler_params=params(4),
        name="pack",
    )(me, lane, in_hbm(pairs), *lists, in_hbm(blocks))
    each = wide_count - 1
    return [outs[c * each : (c + 1) * each] for c in range(len(CHUNKS))], outs[-1]


def select_kernel(wide_count, start, me_ref, lane_ref, pairs_ref, own_ref, *refs):
    received, outs = refs[: wide_count - 1], refs[wide_count - 1 :]
    pair_count = own_ref.shape[0]
    each, size, _ = outs[0].shape
    owners = [pairs_ref[1, pair] >> 3 for pair in range(pair_count)]
    for place in range(pair_count):
        pair = pair_at(lane_ref, pair_count, place)
        owner = pairs_ref[1, pair] >> 3
        shift = me_ref[0] - owner
        shift = jnp.where(shift < 0, shift + wide_count, shift)
        rank = jnp.int32(0)
        for before in range(pair_count):
            rank = rank + ((before < pair) & (owners[before] == owner)).astype(jnp.int32)
        out = outs[place // each].at[place % each]

        @pl.when(shift == 0)
        def _():
            out[...] = own_ref[place, start : start + size]

        for other in range(1, wide_count):

            @pl.when(shift == other)
            def _():
                out[...] = received[other - 1][rank]


def select(me, lane, pairs, own, received, start, size):
    pair_count, _, feat = own.shape
    return pl.pallas_call(
        functools.partial(select_kernel, len(received) + 1, start),
        out_shape=[pltpu.VMEM((pair_count // 2, size, feat), own.dtype)] * 2,
        in_specs=[smem(), smem(), smem()] + [vmem()] * (1 + len(received)),
        out_specs=[vmem()] * 2,
        compiler_params=params(4),
        name="select",
    )(me, lane, in_hbm(pairs), *[in_vmem(x) for x in (own, *received)])


def tree(parts):
    while len(parts) > 1:
        half = len(parts) // 2
        parts = [parts[i] + parts[i + half] for i in range(half)]
    return parts[0]


def across(left, right):
    return lax.dot_general(
        left, right, (((1,), (1,)), ((), ())), preferred_element_type=jnp.float32
    )


def lane_sum(block):
    square = jnp.square(block.astype(jnp.float32))
    return sum(square[:, at : at + LANES] for at in range(0, square.shape[1], LANES))


def segments(window):
    low, high = window
    held = []
    for chunk, (start, size) in enumerate(CHUNKS):
        first, end = max(low, start), min(high, start + size)
        if first < end:
            held.append((chunk, first - start, end - first))
    return held


def scores(rows, cols, square):
    gram = tree([across(row, col) for row, col in zip(rows, cols)])
    other = jnp.sum(tree([lane_sum(col) for col in cols]).T, axis=0, keepdims=True)
    pieces, mass = [], None
    for at in range(0, gram.shape[1], LANES):
        here = slice(at, at + LANES)
        piece = jnp.exp((square + other[:, here] - 2.0 * gram[:, here]) * (-1.0 / F))
        mass = piece if mass is None else mass + piece
        pieces.append(piece)
    kernel = jnp.concatenate(pieces, axis=1) if len(pieces) > 1 else pieces[0]
    return kernel.astype(jnp.bfloat16), jnp.sum(kernel, axis=0, keepdims=True), mass


def of_place(part, place):
    each = part[0].shape[0]
    return part[place // each].at[place % each]


def columns(window, refs):
    held = segments(window)
    pieces = [ref[at : at + size] for ref, (_, at, size) in zip(refs, held)]
    return jnp.concatenate(pieces, axis=0) if len(pieces) > 1 else pieces[0]


def window_parts(window, first_count, refs):
    rows, last, refs = refs[:first_count], refs[first_count], refs[first_count + 1 :]
    count = len(segments(window))
    chunks = [refs[i * 2 * first_count :][: 2 * first_count] for i in range(count)]
    half = last.shape[0] // first_count

    def of_pair(pair):
        own = [ref[pair] for ref in rows] + [last[i * half + pair] for i in range(first_count)]
        cols = [
            columns(window, [chunk[i].at[pair] for chunk in chunks]) for i in range(2 * first_count)
        ]
        return own, cols

    return half, of_pair


def first_kernel(window, first_count, *refs):
    square_ref, mass_ref, kernel_ref, sums_ref = refs[-4:]
    half, of_pair = window_parts(window, first_count, refs)
    for pair in range(half):
        rows, cols = of_pair(pair)
        square = jnp.sum(tree([lane_sum(row) for row in rows]), axis=1, keepdims=True)
        square = jnp.broadcast_to(square, (BR, LANES))
        kernel, sums, mass = scores(rows, cols, square)
        square_ref[pair] = square
        mass_ref[pair] = mass
        sums_ref[pair : pair + 1] = sums
        kernel_ref[pair] = kernel


def last_kernel(window, first_count, wide_count, me_ref, lane_ref, pairs_ref, *refs):
    square_in, mass_in, sums_in = refs[-6 - wide_count : -3 - wide_count]
    kernel_ref, line_ref, row_ref = refs[-3 - wide_count : -wide_count]
    shares = refs[-wide_count:]
    for ref in (row_ref, *shares):
        ref[...] = jnp.zeros_like(ref)
    half, of_pair = window_parts(window, first_count, refs)
    for place in range(half):
        rows, cols = of_pair(place)
        kernel, sums, mass = scores(rows, cols, square_in[place])
        kernel_ref[place] = kernel
        sums = jnp.concatenate([sums_in[place : place + 1], sums], axis=1)
        line = jnp.sum((mass_in[place] + mass).T, axis=0, keepdims=True)
        line_ref[place : place + 1] = line
        pair = pair_at(lane_ref, 2 * half, place)
        row_ref[pl.ds(pairs_ref[0, pair] & 7, 1)] += line
        col = pairs_ref[1, pair]
        shift = (col >> 3) - me_ref[0]
        shift = jnp.where(shift < 0, shift + wide_count, shift)
        for other, ref in enumerate(shares):
            ref[pl.ds(col & 7, 1)] += jnp.where(shift == other, sums, 0.0)


def estimate(pair_count, size):
    return pl.CostEstimate(
        flops=2 * pair_count * BR * size * F,
        transcendentals=pair_count * BR * size,
        bytes_accessed=8 * 1024 * 1024,
    )


def nothing():
    return pl.CostEstimate(flops=0, transcendentals=0, bytes_accessed=0)


def window_operands(rows, cols, window):
    first, last = rows
    args = [*first, last]
    for chunk, _, _ in segments(window):
        args += cols[chunk]
    return args


def first_window(rows, cols):
    window = WINDOWS[0]
    first_count = len(rows[0])
    half = rows[0][0].shape[0] // 2
    lanes = pltpu.VMEM((half, BR, LANES), jnp.float32)
    args = window_operands(rows, cols, window)
    return pl.pallas_call(
        functools.partial(first_kernel, window, first_count),
        out_shape=[
            lanes,
            lanes,
            pltpu.VMEM((half, BR, window[1]), jnp.bfloat16),
            pltpu.VMEM((half, window[1]), jnp.float32),
        ],
        in_specs=[vmem()] * len(args),
        out_specs=[vmem()] * 4,
        compiler_params=params(16),
        cost_estimate=nothing(),
        name="first_window",
    )(*[in_vmem(x) for x in args])


def last_window(me, lane, pairs, rows, cols, square, mass, sums, wide_count):
    window = WINDOWS[1]
    first_count = len(rows[0])
    half = rows[0][0].shape[0] // 2
    size = window[1] - window[0]
    by_block = pltpu.VMEM((BLK_DEV, BR), jnp.float32)
    shapes = [
        pltpu.VMEM((half, BR, size), jnp.bfloat16),
        pltpu.VMEM((half, BR), jnp.float32),
    ] + [by_block] * (1 + wide_count)
    args = window_operands(rows, cols, window) + [square, mass, sums]
    kernel, line, row_sums, *shares = pl.pallas_call(
        functools.partial(last_kernel, window, first_count, wide_count),
        out_shape=shapes,
        in_specs=[smem(), smem(), smem()] + [vmem()] * len(args),
        out_specs=[vmem()] * len(shapes),
        compiler_params=params(16),
        cost_estimate=estimate(half, size),
        name="last_window",
    )(me, lane, in_hbm(pairs), *[in_vmem(x) for x in args])
    return kernel, line, row_sums, shares


def keep_kernel(lane_ref, pairs_ref, block_ref, blocks_ref, out_ref, own_ref, sems):
    here = pl.program_id(0)

    def copies():
        for place in range(own_ref.shape[0]):
            pair = pair_at(lane_ref, own_ref.shape[0], place)
            source = blocks_ref.at[pairs_ref[1, pair] & 7]
            yield pltpu.make_async_copy(source, own_ref.at[place], sems.at[place])

    @pl.when(here == 0)
    def _():
        for copy in copies():
            copy.start()

    out_ref[...] = block_ref[...]

    @pl.when(here == pl.num_programs(0) - 1)
    def _():
        for copy in copies():
            copy.wait()


def keep(lane, pairs, blocks):
    pair_count = pairs.shape[1]
    block = pl.BlockSpec((1, *blocks.shape[1:]), lambda k: (k, 0, 0))
    return pl.pallas_call(
        keep_kernel,
        out_shape=[
            pltpu.HBM(blocks.shape, blocks.dtype),
            pltpu.VMEM((pair_count, *blocks.shape[1:]), blocks.dtype),
        ],
        grid=(blocks.shape[0],),
        in_specs=[smem(), smem(), block, anywhere()],
        out_specs=[block, anywhere()],
        scratch_shapes=[pltpu.SemaphoreType.DMA((pair_count,))],
        compiler_params=params(4),
        name="keep",
    )(lane, in_hbm(pairs), in_hbm(blocks), in_hbm(blocks))


def mean_kernel(lane_ref, pairs_ref, rows_ref, *refs):
    kernels = [refs[2 * i : 2 * i + 2] for i in range(len(WINDOWS))]
    lines, refs = refs[2 * len(WINDOWS) :][:2], refs[2 * len(WINDOWS) + 2 :]
    *chunks, _, out_ref, part, weight, total, mass, made, sems = refs
    pair_count, _, feat = rows_ref.shape
    local = [pairs_ref[0, pair_at(lane_ref, pair_count, p)] & 7 for p in range(pair_count)]

    def copy(place):
        return pltpu.make_async_copy(made.at[place], out_ref.at[local[place]], sems.at[place])

    firsts = []
    for place in range(pair_count):
        kernel = jnp.concatenate([of_place(window, place)[...] for window in kernels], axis=1)
        own = [of_place(chunks[2 * i : 2 * i + 2], place)[...] for i in range(len(CHUNKS))]
        sums = jnp.dot(kernel, jnp.concatenate(own, axis=0), preferred_element_type=jnp.float32)
        part[place] = sums.astype(jnp.bfloat16)
        half = pair_count // 2
        line = lines[place // half][place % half : place % half + 1]
        weight[place] = jnp.broadcast_to(line, (LANES, BR)).T
        same = [local[other] == local[place] for other in range(place)]
        firsts.append(jnp.logical_not(functools.reduce(jnp.logical_or, same, jnp.bool_(False))))
    for place in range(pair_count):

        @pl.when(firsts[place])
        def _():
            total[...] = rows_ref[place].astype(jnp.float32) + part[place].astype(jnp.float32)
            mass[...] = 1.0 + weight[place]
            for other in range(place + 1, pair_count):

                @pl.when(local[other] == local[place])
                def _():
                    total[...] += part[other].astype(jnp.float32)
                    mass[...] += weight[other]

            scale = 1.0 / mass[...]
            for at in range(0, feat, LANES):
                lanes = slice(at, at + LANES)
                made[place, :, lanes] = (total[:, lanes] * scale).astype(jnp.bfloat16)
            copy(place).start()

    for place in range(pair_count):

        @pl.when(firsts[place])
        def _():
            copy(place).wait()


def means(lane, pairs, rows, kernels, lines, own, kept):
    pair_count, _, feat = rows.shape
    args = [in_vmem(x) for x in (rows, *kernels, *lines, *own)]
    return pl.pallas_call(
        mean_kernel,
        out_shape=pltpu.HBM(kept.shape, jnp.bfloat16),
        in_specs=[smem(), smem()] + [vmem()] * len(args) + [anywhere()],
        out_specs=anywhere(),
        scratch_shapes=[
            pltpu.VMEM((pair_count, BR, feat), jnp.bfloat16),
            pltpu.VMEM((pair_count, BR, LANES), jnp.float32),
            pltpu.VMEM((BR, feat), jnp.float32),
            pltpu.VMEM((BR, LANES), jnp.float32),
            pltpu.VMEM((pair_count, BR, feat), jnp.bfloat16),
            pltpu.SemaphoreType.DMA((pair_count,)),
        ],
        input_output_aliases={2 + len(args): 0},
        compiler_params=params(16),
        cost_estimate=estimate(pair_count, 128),
        name="means",
    )(lane, in_hbm(pairs), *args, in_hbm(kept))


def mass_kernel(*refs):
    mass = refs[0][...]
    for ref in refs[1:-1]:
        mass = mass + ref[...]
    refs[-1][...] = mass


def masses(sums):
    return pl.pallas_call(
        mass_kernel,
        out_shape=pltpu.VMEM((BLK_DEV, BR), jnp.float32),
        in_specs=[vmem()] * len(sums),
        out_specs=vmem(),
        compiler_params=params(4),
        name="masses",
    )(*[in_vmem(x) for x in sums])


def weight_kernel(*refs):
    out_ref = refs[-1]
    mass = refs[0][...]
    for ref in refs[1:-1]:
        mass = mass + ref[...]
    weight = 1.0 / (1.0 + mass / BR)
    parts = BR // LANES
    for block in range(BLK_DEV):
        for part in range(parts):
            lanes = slice(part * LANES, (part + 1) * LANES)
            out_ref[block * parts + part : block * parts + part + 1] = weight[block : block + 1, lanes]


def block_weights(sums):
    out = pl.pallas_call(
        weight_kernel,
        out_shape=jax.ShapeDtypeStruct((BLK_DEV * BR // LANES, LANES), jnp.float32),
        in_specs=[vmem()] * len(sums),
        out_specs=vmem(),
        compiler_params=params(4),
        name="weights",
    )(*[in_vmem(x) for x in sums])
    return out.reshape(BLK_DEV * BR)


def hop(parts, step):
    count = lax.axis_size("narrow")
    perm = [(i, i ^ step) for i in range(count)]
    return [lax.ppermute(part, "narrow", perm) for part in parts]


def first_hops(part):
    parts = [part]
    step = lax.axis_size("narrow") // 2
    while step > 1:
        parts = parts + hop(parts, step)
        step //= 2
    return parts


def to_wide(pieces):
    count = lax.axis_size("wide")
    return [
        lax.ppermute(piece, "wide", [(i, (i + shift) % count) for i in range(count)])
        for shift, piece in enumerate(pieces, 1)
    ]


def on_device(embeddings, pair_list):
    wide_count = lax.axis_size("wide")
    me = lax.axis_index("wide").astype(jnp.int32).reshape(1)
    lane = lax.axis_index("narrow").astype(jnp.int32).reshape(1)
    pairs = pair_list.T
    pair_count = pairs.shape[1]
    half = pair_count // 2
    capacity = max(2, 2 * pair_count // wide_count)
    feat = embeddings.shape[1]
    blocks = embeddings.reshape(BLK_DEV, BR, feat)
    lists = to_wide([pairs] * (wide_count - 1))[::-1]
    fixed = lax.optimization_barrier
    outgoing, row_slices = pack(me, lane, pairs, lists, blocks, capacity)

    def pick(received, chunk):
        return select(me, lane, pairs, own, received, *CHUNKS[chunk])

    rows = first_hops(row_slices)
    theirs = jnp.concatenate([part[half:] for part in rows], axis=0)
    rows, theirs, received, (kept, own) = fixed(
        (rows, theirs, to_wide(outgoing[0]), keep(lane, pairs, blocks))
    )
    mine_a, theirs_a = pick(received, 0)
    hops_a, hops_theirs_a = first_hops(mine_a), first_hops(theirs_a)
    rows_last = hop([theirs], 1)
    hops_a, hops_theirs_a, rows_last, received = fixed(
        (hops_a, hops_theirs_a, rows_last, to_wide(outgoing[1]))
    )
    rows = (rows, rows_last[0])
    mine_b, theirs_b = pick(received, 1)
    hops_b, hops_theirs_b = first_hops(mine_b), first_hops(theirs_b)
    cols_a = hops_a + hop(hops_theirs_a, 1)
    carry = first_window(rows, [cols_a])
    hops_b, hops_theirs_b, carry = fixed((hops_b, hops_theirs_b, carry))
    square, mass, kernel_a, sums = carry
    last_b, kernel_a = fixed((hop(hops_theirs_b, 1), kernel_a))
    kernels = [kernel_a, *hop([kernel_a], 1)]
    kernel_b, line, row_sums, shares = last_window(
        me, lane, pairs, rows, [cols_a, hops_b + last_b], square, mass, sums, wide_count
    )
    kernels += [kernel_b, *hop([kernel_b], 1)]
    came = to_wide(shares[1:])
    mean = means(
        lane, pairs, row_slices, kernels, [line, *hop([line], 1)], [mine_a, theirs_a, mine_b, theirs_b], kept
    )
    mean, came = fixed((mean, came))
    sums = masses([row_sums, shares[0], *came])
    weights = block_weights([sums, *hop([sums], 1)])
    return weights, mean.reshape(BLK_DEV * BR, feat)


def solution(mesh):
    in_specs = (P(("groups", "wide"), "narrow"), P(("groups", "wide"), None))
    out_specs = (P(("groups", "wide")), P(("groups", "wide"), "narrow"))
    return jax.shard_map(
        on_device, mesh=mesh, in_specs=in_specs, out_specs=out_specs, check_vma=False
    )
```

time: 87.4 us -> 89.4 us (1.023)
  starting transfers between devices: 29.5 us -> 32.3 us
  Pallas kernels: 19.4 us -> 16.9 us
  waiting for transfers between devices: 37.1 us -> 39.1 us
    ppermute x11 -> x14, waiting for transfers between devices: 20.9 us -> 23.8 us  [hop(): return [lax.ppermute(part, 'narrow', perm) for part in parts]]
    pallas_call x3 -> x4, Pallas kernels: 8.05 us -> 5.61 us  [the longest x1 2.63 us: means(): pl.pallas_call(mean_kernel, out_shape=pltpu.HBM(kept.shape, jnp.bfloat16)...]
    ppermute x11 -> x14, starting transfers between devices: 5.41 us -> 7.63 us  [hop(): return [lax.ppermute(part, 'narrow', perm) for part in parts]]
    ppermute x12, waiting for transfers between devices: 16.2 us -> 15.3 us  [to_wide(): lax.ppermute(piece, 'wide', [(i, (i + shift) % count) for i in range(coun...]
  transfers between devices with their start and end apart: 23 -> 26, of which waited for: 15 -> 13; matrix products, arithmetic and copies ran while one was open for 0% -> 0% of each run, Pallas kernels for 14% -> 13%
where the time goes in v15:
time: 89.4 us; the launch traced here: 89.1 us
  waiting for transfers between devices  39.1 us (44%)
  starting transfers between devices  32.3 us (36%)
  Pallas kernels  16.9 us (19%)
    ppermute x12, starting transfers between devices, to_wide(): lax.ppermute(piece, 'wide', [(i, (i + shift) % count) for i in range(coun...  24.7 us
    ppermute x14, waiting for transfers between devices, hop(): return [lax.ppermute(part, 'narrow', perm) for part in parts]  23.8 us
    ppermute x12, waiting for transfers between devices, to_wide(): lax.ppermute(piece, 'wide', [(i, (i + shift) % count) for i in range(coun...  15.3 us
    ppermute x14, starting transfers between devices, hop(): return [lax.ppermute(part, 'narrow', perm) for part in parts]  7.63 us
    pallas_call x1, Pallas kernels, keep(): pl.pallas_call(keep_kernel, out_shape=[pltpu.HBM(blocks.shape, blocks.dty...  6.03 us
    pallas_call x1, Pallas kernels, pack(): pl.pallas_call(functools.partial(pack_kernel, wide_count, pair_count, cap...  2.9 us
    pallas_call x1, Pallas kernels, means(): pl.pallas_call(mean_kernel, out_shape=pltpu.HBM(kept.shape, jnp.bfloat16)...  2.63 us
  transfers between devices with their start and end apart: 26, of which 13 were waited for; matrix products, arithmetic and copies ran while one was open for 0% of the time, Pallas kernels for 13%

profile of v15, /device:TPU:0, one launch (start us, length us, event | category | flops | bytes accessed | tf_op | source)
XLA Modules:
  0.0 89.1 jit_solution(15776426201878064940)
XLA Ops:
  0.6 3.1 %collective-permute-start.2 = (s32[2,4]{1,0:T(2,128)}, s32[2,4]{1,0:T(2,128)S(1)}, u32[]{:S(2)}, u32[]{:S(2)}) collective-permute-start(s32[2,4]{1,0:T(2,128)} %bitcast.10), channel_id=1, source_target_pairs={{0,4},{4,8},{8,12},{12,0},{1,5},{5,9},{9,13},{13,1},{2,6},{6,10},{... | collective-permute-start | bytes 104 | tf_op jit(solution)/shard_map/ppermute | solution.py:480
  3.7 2.6 %collective-permute-start.1 = (s32[2,4]{1,0:T(2,128)}, s32[2,4]{1,0:T(2,128)S(1)}, u32[]{:S(2)}, u32[]{:S(2)}) collective-permute-start(s32[2,4]{1,0:T(2,128)} %bitcast.11), channel_id=1, source_target_pairs={{0,8},{4,12},{8,0},{12,4},{1,9},{5,13},{9,1},{13,5},{2,10},{6,14},... | collective-permute-start | bytes 104 | tf_op jit(solution)/shard_map/ppermute | solution.py:480
  6.3 1.3 %collective-permute-start = (s32[2,4]{1,0:T(2,128)}, s32[2,4]{1,0:T(2,128)S(1)}, u32[]{:S(2)}, u32[]{:S(2)}) collective-permute-start(s32[2,4]{1,0:T(2,128)} %bitcast.12), channel_id=1, source_target_pairs={{0,12},{4,0},{8,4},{12,8},{1,13},{5,1},{9,5},{13,9},{2,14},{6,2},{... | collective-permute-start | bytes 104 | tf_op jit(solution)/shard_map/ppermute | solution.py:480
  7.6 0.7 collective-permute-done.1.refs_1_
  8.4 1.7 %collective-permute-done.refs_0_ = s32[2,4]{1,0:T(2,128)S(1)} collective-permute-done((s32[2,4]{1,0:T(2,128)}, s32[2,4]{1,0:T(2,128)S(1)}, u32[]{:S(2)}, u32[]{:S(2)}) %collective-permute-start) | collective-permute-done | bytes 64 | tf_op jit(solution)/shard_map/ppermute | solution.py:480
  10.1 2.9 %pack.1 = (bf16[2,320,256]{2,1,0:T(8,128)(2,1)S(1)}, bf16[2,320,256]{2,1,0:T(8,128)(2,1)S(1)}, bf16[2,320,256]{2,1,0:T(8,128)(2,1)S(1)}, bf16[2,192,256]{2,1,0:T...) custom-call(s32[1]{0:T(128)} %bitcast.me_ref, ...), custom_call_target="tpu_custom_call" | custom-call | tf_op jit(solution)/shard_map/pack/pallas_call | solution.py:88
  13.0 1.6 %collective-permute-start.3 = (bf16[4,512,256]{2,1,0:T(8,128)(2,1)S(1)}, bf16[4,512,256]{2,1,0:T(8,128)(2,1)S(1)}, u32[]{:S(2)}, u32[]{:S(2)}) collective-permute-start(bf16[4,512,256]{2,1,0:T(8,128)(2,1)S(1)} %get-tuple-element.63.refs_0_.rows_ref), channel_id=1, source_target_pairs={{0,2},{1,3},{2,0},{3,1},{4,6},{5,7},{6,4},{7,5},{8,10},{9,11},{10,... | collective-permute-start | bytes 3145736 | tf_op jit(solution)/shard_map/ppermute | solution.py:465
  14.6 3.5 %collective-permute-start.5 = (bf16[2,320,256]{2,1,0:T(8,128)(2,1)S(1)}, bf16[2,320,256]{2,1,0:T(8,128)(2,1)S(1)}, u32[]{:S(2)}, u32[]{:S(2)}) collective-permute-start(bf16[2,320,256]{2,1,0:T(8,128)(2,1)S(1)} %get-tuple-element.59), channel_id=1, source_target_pairs={{0,8},{4,12},{8,0},{12,4},{1,9},{5,13},{9,1},{13,5},{2,10},{6,14},... | collective-permute-start | bytes 983048 | tf_op jit(solution)/shard_map/ppermute | solution.py:480
  18.4 6.0 %keep.1 = (bf16[8,512,256]{2,1,0:T(8,128)(2,1)}, bf16[4,512,256]{2,1,0:T(8,128)(2,1)S(1)}) custom-call(s32[1]{0:T(128)} %bitcast.1.lane_ref, s32[2,4]{1,0:T(2,128)} %bitcast.14, bf16[8,512,256]{2,1,0:T(8,128)(2,1)} %bitcast.7, bf16[8,512,256]{2,1,0:T(8,128)(2,1)} %bitcast.8), custom_call_target="tpu_custom_call" | custom-call | tf_op jit(solution)/shard_map/keep/pallas_call | solution.py:334
  24.5 12.1 %collective-permute-done.3.refs_1_ = bf16[4,512,256]{2,1,0:T(8,128)(2,1)S(1)} collective-permute-done((bf16[4,512,256]{2,1,0:T(8,128)(2,1)S(1)}, bf16[4,512,256]{2,1,0:T(8,128)(2,1)S(1)}, u32[]{:S(2)}, u32[]{:S(2)}) %collective-permute-start.3) | collective-permute-done | bytes 1048608 | tf_op jit(solution)/shard_map/ppermute | solution.py:465
  36.7 1.7 %collective-permute-done.5.refs_1_ = bf16[2,320,256]{2,1,0:T(8,128)(2,1)S(1)} collective-permute-done((bf16[2,320,256]{2,1,0:T(8,128)(2,1)S(1)}, bf16[2,320,256]{2,1,0:T(8,128)(2,1)S(1)}, u32[]{:S(2)}, u32[]{:S(2)}) %collective-permute-start.5) | collective-permute-done | bytes 327712 | tf_op jit(solution)/shard_map/ppermute | solution.py:480
  38.4 6.8 %collective-permute-start.10 = (bf16[2,192,256]{2,1,0:T(8,128)(2,1)S(1)}, bf16[2,192,256]{2,1,0:T(8,128)(2,1)S(1)}, u32[]{:S(2)}, u32[]{:S(2)}) collective-permute-start(bf16[2,192,256]{2,1,0:T(8,128)(2,1)S(1)} %get-tuple-element.72), channel_id=1, source_target_pairs={{0,4},{4,8},{8,12},{12,0},{1,5},{5,9},{9,13},{13,1},{2,6},{6,10},{... | collective-permute-start | bytes 589832 | tf_op jit(solution)/shard_map/ppermute | solution.py:480
  45.2 0.9 select.2
  46.7 1.5 %collective-permute-start.8 = (bf16[2,320,256]{2,1,0:T(8,128)(2,1)S(1)}, bf16[2,320,256]{2,1,0:T(8,128)(2,1)S(1)}, u32[]{:S(2)}, u32[]{:S(2)}) collective-permute-start(bf16[2,320,256]{2,1,0:T(8,128)(2,1)S(1)} %get-tuple-element.78.refs_7_), channel_id=1, source_target_pairs={{0,2},{1,3},{2,0},{3,1},{4,6},{5,7},{6,4},{7,5},{8,10},{9,11},{10,... | collective-permute-start | bytes 983048 | tf_op jit(solution)/shard_map/ppermute | solution.py:465
  48.5 2.0 %collective-permute-done.10.refs_0_ = bf16[2,192,256]{2,1,0:T(8,128)(2,1)S(1)} collective-permute-done((bf16[2,192,256]{2,1,0:T(8,128)(2,1)S(1)}, bf16[2,192,256]{2,1,0:T(8,128)(2,1)S(1)}, u32[]{:S(2)}, u32[]{:S(2)}) %collective-permute-start.10) | collective-permute-done | bytes 196640 | tf_op jit(solution)/shard_map/ppermute | solution.py:480
  50.6 1.7 %collective-permute-start.12 = (bf16[2,192,256]{2,1,0:T(8,128)(2,1)S(1)}, bf16[2,192,256]{2,1,0:T(8,128)(2,1)S(1)}, u32[]{:S(2)}, u32[]{:S(2)}) collective-permute-start(bf16[2,192,256]{2,1,0:T(8,128)(2,1)S(1)} %get-tuple-element.74), channel_id=1, source_target_pairs={{0,12},{4,0},{8,4},{12,8},{1,13},{5,1},{9,5},{13,9},{2,14},{6,2},{... | collective-permute-start | bytes 589832 | tf_op jit(solution)/shard_map/ppermute | solution.py:480
  52.3 7.3 %collective-permute-done.11.refs_1_ = bf16[2,192,256]{2,1,0:T(8,128)(2,1)S(1)} collective-permute-done((bf16[2,192,256]{2,1,0:T(8,128)(2,1)S(1)}, bf16[2,192,256]{2,1,0:T(8,128)(2,1)S(1)}, u32[]{:S(2)}, u32[]{:S(2)}) %collective-permute-start.11) | collective-permute-done | bytes 196640 | tf_op jit(solution)/shard_map/ppermute | solution.py:480
  59.6 1.8 %collective-permute-done.12.refs_2_ = bf16[2,192,256]{2,1,0:T(8,128)(2,1)S(1)} collective-permute-done((bf16[2,192,256]{2,1,0:T(8,128)(2,1)S(1)}, bf16[2,192,256]{2,1,0:T(8,128)(2,1)S(1)}, u32[]{:S(2)}, u32[]{:S(2)}) %collective-permute-start.12) | collective-permute-done | bytes 196640 | tf_op jit(solution)/shard_map/ppermute | solution.py:480
  61.4 1.6 %collective-permute-done.8 = bf16[2,320,256]{2,1,0:T(8,128)(2,1)S(1)} collective-permute-done((bf16[2,320,256]{2,1,0:T(8,128)(2,1)S(1)}, bf16[2,320,256]{2,1,0:T(8,128)(2,1)S(1)}, u32[]{:S(2)}, u32[]{:S(2)}) %collective-permute-start.8) | collective-permute-done | bytes 327712 | tf_op jit(solution)/shard_map/ppermute | solution.py:465
  63.5 0.8 select.3
  65.0 1.5 %collective-permute-start.16 = (bf16[2,192,256]{2,1,0:T(8,128)(2,1)S(1)}, bf16[2,192,256]{2,1,0:T(8,128)(2,1)S(1)}, u32[]{:S(2)}, u32[]{:S(2)}) collective-permute-start(bf16[2,192,256]{2,1,0:T(8,128)(2,1)S(1)} %get-tuple-element.91.refs_9_), channel_id=1, source_target_pairs={{0,2},{1,3},{2,0},{3,1},{4,6},{5,7},{6,4},{7,5},{8,10},{9,11},{10,... | collective-permute-start | bytes 589832 | tf_op jit(solution)/shard_map/ppermute | solution.py:465
  66.5 1.2 %first_window.1 = (f32[2,512,128]{2,1,0:T(8,128)S(1)}, f32[2,512,128]{2,1,0:T(8,128)S(1)}, bf16[2,512,256]{2,1,0:T(8,128)(2,1)S(1)}, f32[2,256]{1,0:T(2,128)S(1)}) custom-call(bf16[4,512,256]{2,1,0:T(8,128)(2,1)S(1)} %get-tuple-element.63.refs_0_.rows_ref, bf16[4,512,256]{2,1,0:T(8,128)(2,1)S(1)} %collective-permute-done.3.refs_1_, ...), custom_call_target="tpu_custom_call" | custom-call | tf_op jit(solution)/shard_map/first_window/pallas_call | solution.py:270
  67.7 4.5 %collective-permute-done.15.refs_8_ = bf16[2,192,256]{2,1,0:T(8,128)(2,1)S(1)} collective-permute-done((bf16[2,192,256]{2,1,0:T(8,128)(2,1)S(1)}, bf16[2,192,256]{2,1,0:T(8,128)(2,1)S(1)}, u32[]{:S(2)}, u32[]{:S(2)}) %collective-permute-start.15) | collective-permute-done | bytes 196640 | tf_op jit(solution)/shard_map/ppermute | solution.py:465
  72.2 3.3 %collective-permute-done.16 = bf16[2,192,256]{2,1,0:T(8,128)(2,1)S(1)} collective-permute-done((bf16[2,192,256]{2,1,0:T(8,128)(2,1)S(1)}, bf16[2,192,256]{2,1,0:T(8,128)(2,1)S(1)}, u32[]{:S(2)}, u32[]{:S(2)}) %collective-permute-start.16) | collective-permute-done | bytes 196640 | tf_op jit(solution)/shard_map/ppermute | solution.py:465
  76.0 0.9 %collective-permute-done.17.refs_9_ = bf16[2,192,256]{2,1,0:T(8,128)(2,1)S(1)} collective-permute-done((bf16[2,192,256]{2,1,0:T(8,128)(2,1)S(1)}, bf16[2,192,256]{2,1,0:T(8,128)(2,1)S(1)}, u32[]{:S(2)}, u32[]{:S(2)}) %collective-permute-start.17) | collective-permute-done | bytes 196640 | tf_op jit(solution)/shard_map/ppermute | solution.py:465
  77.2 1.7 %last_window.1 = (bf16[2,512,256]{2,1,0:T(8,128)(2,1)S(1)}, f32[2,512]{1,0:T(2,128)S(1)}, f32[8,512]{1,0:T(8,128)S(1)}, f32[8,512]{1,0:T(8,128)S(1)}, f32[8,512]...) custom-call(s32[1]{0:T(128)} %bitcast.me_ref, s32[1]{0:T(128)} %bitcast.1.lane_ref, s32[2,4]{1,0:T(2,128)} %bitcast.17, ...), custom_call_target="tpu_custom_call" | custom-call | flops 536870912 | bytes 8388608 | tf_op jit(solution)/shard_map/last_window/pallas_call | solution.py:297
  79.7 1.4 %collective-permute-start.22 = (f32[8,512]{1,0:T(8,128)S(1)}, f32[8,512]{1,0:T(8,128)S(1)}, u32[]{:S(2)}, u32[]{:S(2)}) collective-permute-start(f32[8,512]{1,0:T(8,128)S(1)} %get-tuple-element.105), channel_id=1, source_target_pairs={{0,4},{4,8},{8,12},{12,0},{1,5},{5,9},{9,13},{13,1},{2,6},{6,10},{... | collective-permute-start | bytes 49160 | tf_op jit(solution)/shard_map/ppermute | solution.py:480
  81.2 2.1 %collective-permute-start.23 = (f32[8,512]{1,0:T(8,128)S(1)}, f32[8,512]{1,0:T(8,128)S(1)}, u32[]{:S(2)}, u32[]{:S(2)}) collective-permute-start(f32[8,512]{1,0:T(8,128)S(1)} %get-tuple-element.106), channel_id=1, source_target_pairs={{0,8},{4,12},{8,0},{12,4},{1,9},{5,13},{9,1},{13,5},{2,10},{6,14},... | collective-permute-start | bytes 49160 | tf_op jit(solution)/shard_map/ppermute | solution.py:480
  83.2 1.4 %collective-permute-start.24 = (f32[8,512]{1,0:T(8,128)S(1)}, f32[8,512]{1,0:T(8,128)S(1)}, u32[]{:S(2)}, u32[]{:S(2)}) collective-permute-start(f32[8,512]{1,0:T(8,128)S(1)} %get-tuple-element.107), channel_id=1, source_target_pairs={{0,12},{4,0},{8,4},{12,8},{1,13},{5,1},{9,5},{13,9},{2,14},{6,2},{... | collective-permute-start | bytes 49160 | tf_op jit(solution)/shard_map/ppermute | solution.py:480
  84.6 2.6 %means.1 = bf16[8,512,256]{2,1,0:T(8,128)(2,1)} custom-call(s32[1]{0:T(128)} %bitcast.1.lane_ref, s32[2,4]{1,0:T(2,128)} %bitcast.18, bf16[4,512,256]{2,1,0:T(8,128)(2,1)S(1)} %get-tuple-element.63.refs_0_.rows_ref, bf16[2,512,256]{2,1,0:T(8,128)(2,1)S(1)} %get-tuple-element.101.refs_0_, ...), custom_call_target="tpu_custom_call", output_to_operand_aliasing={{}: (13, {})} | custom-call | flops 536870912 | bytes 8388608 | tf_op jit(solution)/shard_map/means/pallas_call | solution.py:399
  87.4 1.2 %collective-permute-done.25.refs_1_ = f32[8,512]{1,0:T(8,128)S(1)} collective-permute-done((f32[8,512]{1,0:T(8,128)S(1)}, f32[8,512]{1,0:T(8,128)S(1)}, u32[]{:S(2)}, u32[]{:S(2)}) %collective-permute-start.25) | collective-permute-done | bytes 16416 | tf_op jit(solution)/shard_map/ppermute | solution.py:465
  88.5 0.6 weights.1
  (32 shorter events, 4.3 us)
Async XLA Ops:
  0.6 7.0 %collective-permute-start.2 = (s32[2,4]{1,0:T(2,128)}, s32[2,4]{1,0:T(2,128)S(1)}, u32[]{:S(2)}, u32[]{:S(2)}) collective-permute-start(s32[2,4]{1,0:T(2,128)} %bitcast.10), channel_id=1, source_target_pairs={{0,4},{4,8},{8,12},{12,0},{1,5},{5,9},{9,13},{13,1},{2,6},{6,10},{... | collective-permute-start | bytes 104 | tf_op jit(solution)/shard_map/ppermute | solution.py:480
  3.7 4.7 %collective-permute-start.1 = (s32[2,4]{1,0:T(2,128)}, s32[2,4]{1,0:T(2,128)S(1)}, u32[]{:S(2)}, u32[]{:S(2)}) collective-permute-start(s32[2,4]{1,0:T(2,128)} %bitcast.11), channel_id=1, source_target_pairs={{0,8},{4,12},{8,0},{12,4},{1,9},{5,13},{9,1},{13,5},{2,10},{6,14},... | collective-permute-start | bytes 104 | tf_op jit(solution)/shard_map/ppermute | solution.py:480
  6.3 3.8 %collective-permute-start = (s32[2,4]{1,0:T(2,128)}, s32[2,4]{1,0:T(2,128)S(1)}, u32[]{:S(2)}, u32[]{:S(2)}) collective-permute-start(s32[2,4]{1,0:T(2,128)} %bitcast.12), channel_id=1, source_target_pairs={{0,12},{4,0},{8,4},{12,8},{1,13},{5,1},{9,5},{13,9},{2,14},{6,2},{... | collective-permute-start | bytes 104 | tf_op jit(solution)/shard_map/ppermute | solution.py:480
  13.0 23.6 %collective-permute-start.3 = (bf16[4,512,256]{2,1,0:T(8,128)(2,1)S(1)}, bf16[4,512,256]{2,1,0:T(8,128)(2,1)S(1)}, u32[]{:S(2)}, u32[]{:S(2)}) collective-permute-start(bf16[4,512,256]{2,1,0:T(8,128)(2,1)S(1)} %get-tuple-element.63.refs_0_.rows_ref), channel_id=1, source_target_pairs={{0,2},{1,3},{2,0},{3,1},{4,6},{5,7},{6,4},{7,5},{8,10},{9,11},{10,... | collective-permute-start | bytes 3145736 | tf_op jit(solution)/shard_map/ppermute | solution.py:465
  14.5 22.1 %collective-permute-start.4 = (bf16[2,320,256]{2,1,0:T(8,128)(2,1)S(1)}, bf16[2,320,256]{2,1,0:T(8,128)(2,1)S(1)}, u32[]{:S(2)}, u32[]{:S(2)}) collective-permute-start(bf16[2,320,256]{2,1,0:T(8,128)(2,1)S(1)} %get-tuple-element.58), channel_id=1, source_target_pairs={{0,4},{4,8},{8,12},{12,0},{1,5},{5,9},{9,13},{13,1},{2,6},{6,10},{... | collective-permute-start | bytes 983048 | tf_op jit(solution)/shard_map/ppermute | solution.py:480
  14.6 23.8 %collective-permute-start.5 = (bf16[2,320,256]{2,1,0:T(8,128)(2,1)S(1)}, bf16[2,320,256]{2,1,0:T(8,128)(2,1)S(1)}, u32[]{:S(2)}, u32[]{:S(2)}) collective-permute-start(bf16[2,320,256]{2,1,0:T(8,128)(2,1)S(1)} %get-tuple-element.59), channel_id=1, source_target_pairs={{0,8},{4,12},{8,0},{12,4},{1,9},{5,13},{9,1},{13,5},{2,10},{6,14},... | collective-permute-start | bytes 983048 | tf_op jit(solution)/shard_map/ppermute | solution.py:480
  18.1 20.3 %collective-permute-start.6 = (bf16[2,320,256]{2,1,0:T(8,128)(2,1)S(1)}, bf16[2,320,256]{2,1,0:T(8,128)(2,1)S(1)}, u32[]{:S(2)}, u32[]{:S(2)}) collective-permute-start(bf16[2,320,256]{2,1,0:T(8,128)(2,1)S(1)} %get-tuple-element.60), channel_id=1, source_target_pairs={{0,12},{4,0},{8,4},{12,8},{1,13},{5,1},{9,5},{13,9},{2,14},{6,2},{... | collective-permute-start | bytes 983048 | tf_op jit(solution)/shard_map/ppermute | solution.py:480
  38.4 24.6 %collective-permute-start.9 = (bf16[4,512,256]{2,1,0:T(8,128)(2,1)S(1)}, bf16[4,512,256]{2,1,0:T(8,128)(2,1)S(1)}, u32[]{:S(2)}, u32[]{:S(2)}) collective-permute-start(bf16[4,512,256]{2,1,0:T(8,128)(2,1)S(1)} %pad_maximum_fusion), channel_id=1, source_target_pairs={{0,1},{1,0},{2,3},{3,2},{4,5},{5,4},{6,7},{7,6},{8,9},{9,8},{10,11... | collective-permute-start | bytes 3145736 | tf_op jit(solution)/shard_map/ppermute | solution.py:465
  38.4 12.2 %collective-permute-start.10 = (bf16[2,192,256]{2,1,0:T(8,128)(2,1)S(1)}, bf16[2,192,256]{2,1,0:T(8,128)(2,1)S(1)}, u32[]{:S(2)}, u32[]{:S(2)}) collective-permute-start(bf16[2,192,256]{2,1,0:T(8,128)(2,1)S(1)} %get-tuple-element.72), channel_id=1, source_target_pairs={{0,4},{4,8},{8,12},{12,0},{1,5},{5,9},{9,13},{13,1},{2,6},{6,10},{... | collective-permute-start | bytes 589832 | tf_op jit(solution)/shard_map/ppermute | solution.py:480
  46.1 15.4 %collective-permute-start.7 = (bf16[2,320,256]{2,1,0:T(8,128)(2,1)S(1)}, bf16[2,320,256]{2,1,0:T(8,128)(2,1)S(1)}, u32[]{:S(2)}, u32[]{:S(2)}) collective-permute-start(bf16[2,320,256]{2,1,0:T(8,128)(2,1)S(1)} %get-tuple-element.76.refs_3_.refs_6_), channel_id=1, source_target_pairs={{0,2},{1,3},{2,0},{3,1},{4,6},{5,7},{6,4},{7,5},{8,10},{9,11},{10,... | collective-permute-start | bytes 983048 | tf_op jit(solution)/shard_map/ppermute | solution.py:465
  46.7 16.3 %collective-permute-start.8 = (bf16[2,320,256]{2,1,0:T(8,128)(2,1)S(1)}, bf16[2,320,256]{2,1,0:T(8,128)(2,1)S(1)}, u32[]{:S(2)}, u32[]{:S(2)}) collective-permute-start(bf16[2,320,256]{2,1,0:T(8,128)(2,1)S(1)} %get-tuple-element.78.refs_7_), channel_id=1, source_target_pairs={{0,2},{1,3},{2,0},{3,1},{4,6},{5,7},{6,4},{7,5},{8,10},{9,11},{10,... | collective-permute-start | bytes 983048 | tf_op jit(solution)/shard_map/ppermute | solution.py:465
  48.2 11.4 %collective-permute-start.11 = (bf16[2,192,256]{2,1,0:T(8,128)(2,1)S(1)}, bf16[2,192,256]{2,1,0:T(8,128)(2,1)S(1)}, u32[]{:S(2)}, u32[]{:S(2)}) collective-permute-start(bf16[2,192,256]{2,1,0:T(8,128)(2,1)S(1)} %get-tuple-element.73), channel_id=1, source_target_pairs={{0,8},{4,12},{8,0},{12,4},{1,9},{5,13},{9,1},{13,5},{2,10},{6,14},... | collective-permute-start | bytes 589832 | tf_op jit(solution)/shard_map/ppermute | solution.py:480
  50.6 10.8 %collective-permute-start.12 = (bf16[2,192,256]{2,1,0:T(8,128)(2,1)S(1)}, bf16[2,192,256]{2,1,0:T(8,128)(2,1)S(1)}, u32[]{:S(2)}, u32[]{:S(2)}) collective-permute-start(bf16[2,192,256]{2,1,0:T(8,128)(2,1)S(1)} %get-tuple-element.74), channel_id=1, source_target_pairs={{0,12},{4,0},{8,4},{12,8},{1,13},{5,1},{9,5},{13,9},{2,14},{6,2},{... | collective-permute-start | bytes 589832 | tf_op jit(solution)/shard_map/ppermute | solution.py:480
  63.0 3.5 %collective-permute-start.13 = (bf16[2,320,256]{2,1,0:T(8,128)(2,1)S(1)}, bf16[2,320,256]{2,1,0:T(8,128)(2,1)S(1)}, u32[]{:S(2)}, u32[]{:S(2)}) collective-permute-start(bf16[2,320,256]{2,1,0:T(8,128)(2,1)S(1)} %get-tuple-element.78.refs_7_), channel_id=1, source_target_pairs={{0,1},{1,0},{2,3},{3,2},{4,5},{5,4},{6,7},{7,6},{8,9},{9,8},{10,11... | collective-permute-start | bytes 983048 | tf_op jit(solution)/shard_map/ppermute | solution.py:465
  63.0 3.5 %collective-permute-start.14 = (bf16[2,320,256]{2,1,0:T(8,128)(2,1)S(1)}, bf16[2,320,256]{2,1,0:T(8,128)(2,1)S(1)}, u32[]{:S(2)}, u32[]{:S(2)}) collective-permute-start(bf16[2,320,256]{2,1,0:T(8,128)(2,1)S(1)} %collective-permute-done.8), channel_id=1, source_target_pairs={{0,1},{1,0},{2,3},{3,2},{4,5},{5,4},{6,7},{7,6},{8,9},{9,8},{10,11... | collective-permute-start | bytes 983048 | tf_op jit(solution)/shard_map/ppermute | solution.py:465
  64.4 7.8 %collective-permute-start.15 = (bf16[2,192,256]{2,1,0:T(8,128)(2,1)S(1)}, bf16[2,192,256]{2,1,0:T(8,128)(2,1)S(1)}, u32[]{:S(2)}, u32[]{:S(2)}) collective-permute-start(bf16[2,192,256]{2,1,0:T(8,128)(2,1)S(1)} %get-tuple-element.89.refs_7_.refs_8_), channel_id=1, source_target_pairs={{0,2},{1,3},{2,0},{3,1},{4,6},{5,7},{6,4},{7,5},{8,10},{9,11},{10,... | collective-permute-start | bytes 589832 | tf_op jit(solution)/shard_map/ppermute | solution.py:465
  65.0 10.5 %collective-permute-start.16 = (bf16[2,192,256]{2,1,0:T(8,128)(2,1)S(1)}, bf16[2,192,256]{2,1,0:T(8,128)(2,1)S(1)}, u32[]{:S(2)}, u32[]{:S(2)}) collective-permute-start(bf16[2,192,256]{2,1,0:T(8,128)(2,1)S(1)} %get-tuple-element.91.refs_9_), channel_id=1, source_target_pairs={{0,2},{1,3},{2,0},{3,1},{4,6},{5,7},{6,4},{7,5},{8,10},{9,11},{10,... | collective-permute-start | bytes 589832 | tf_op jit(solution)/shard_map/ppermute | solution.py:465
  75.5 1.4 %collective-permute-start.17 = (bf16[2,192,256]{2,1,0:T(8,128)(2,1)S(1)}, bf16[2,192,256]{2,1,0:T(8,128)(2,1)S(1)}, u32[]{:S(2)}, u32[]{:S(2)}) collective-permute-start(bf16[2,192,256]{2,1,0:T(8,128)(2,1)S(1)} %get-tuple-element.91.refs_9_), channel_id=1, source_target_pairs={{0,1},{1,0},{2,3},{3,2},{4,5},{5,4},{6,7},{7,6},{8,9},{9,8},{10,11... | collective-permute-start | bytes 589832 | tf_op jit(solution)/shard_map/ppermute | solution.py:465
  75.5 1.7 %collective-permute-start.18 = (bf16[2,192,256]{2,1,0:T(8,128)(2,1)S(1)}, bf16[2,192,256]{2,1,0:T(8,128)(2,1)S(1)}, u32[]{:S(2)}, u32[]{:S(2)}) collective-permute-start(bf16[2,192,256]{2,1,0:T(8,128)(2,1)S(1)} %collective-permute-done.16), channel_id=1, source_target_pairs={{0,1},{1,0},{2,3},{3,2},{4,5},{5,4},{6,7},{7,6},{8,9},{9,8},{10,11... | collective-permute-start | bytes 589832 | tf_op jit(solution)/shard_map/ppermute | solution.py:465
  78.9 5.7 %collective-permute-start.20 = (bf16[2,512,256]{2,1,0:T(8,128)(2,1)S(1)}, bf16[2,512,256]{2,1,0:T(8,128)(2,1)S(1)}, u32[]{:S(2)}, u32[]{:S(2)}) collective-permute-start(bf16[2,512,256]{2,1,0:T(8,128)(2,1)S(1)} %get-tuple-element.102.refs_2_), channel_id=1, source_target_pairs={{0,1},{1,0},{2,3},{3,2},{4,5},{5,4},{6,7},{7,6},{8,9},{9,8},{10,11... | collective-permute-start | bytes 1572872 | tf_op jit(solution)/shard_map/ppermute | solution.py:465
  79.2 5.4 %collective-permute-start.19 = (bf16[2,512,256]{2,1,0:T(8,128)(2,1)S(1)}, bf16[2,512,256]{2,1,0:T(8,128)(2,1)S(1)}, u32[]{:S(2)}, u32[]{:S(2)}) collective-permute-start(bf16[2,512,256]{2,1,0:T(8,128)(2,1)S(1)} %get-tuple-element.101.refs_0_), channel_id=1, source_target_pairs={{0,1},{1,0},{2,3},{3,2},{4,5},{5,4},{6,7},{7,6},{8,9},{9,8},{10,11... | collective-permute-start | bytes 1572872 | tf_op jit(solution)/shard_map/ppermute | solution.py:465
  79.5 3.7 %collective-permute-start.21 = (f32[2,512]{1,0:T(2,128)S(1)}, f32[2,512]{1,0:T(2,128)S(1)}, u32[]{:S(2)}, u32[]{:S(2)}) collective-permute-start(f32[2,512]{1,0:T(2,128)S(1)} %get-tuple-element.103.refs_4_), channel_id=1, source_target_pairs={{0,1},{1,0},{2,3},{3,2},{4,5},{5,4},{6,7},{7,6},{8,9},{9,8},{10,11... | collective-permute-start | bytes 12296 | tf_op jit(solution)/shard_map/ppermute | solution.py:465
  79.7 7.5 %collective-permute-start.22 = (f32[8,512]{1,0:T(8,128)S(1)}, f32[8,512]{1,0:T(8,128)S(1)}, u32[]{:S(2)}, u32[]{:S(2)}) collective-permute-start(f32[8,512]{1,0:T(8,128)S(1)} %get-tuple-element.105), channel_id=1, source_target_pairs={{0,4},{4,8},{8,12},{12,0},{1,5},{5,9},{9,13},{13,1},{2,6},{6,10},{... | collective-permute-start | bytes 49160 | tf_op jit(solution)/shard_map/ppermute | solution.py:480
  81.2 6.1 %collective-permute-start.23 = (f32[8,512]{1,0:T(8,128)S(1)}, f32[8,512]{1,0:T(8,128)S(1)}, u32[]{:S(2)}, u32[]{:S(2)}) collective-permute-start(f32[8,512]{1,0:T(8,128)S(1)} %get-tuple-element.106), channel_id=1, source_target_pairs={{0,8},{4,12},{8,0},{12,4},{1,9},{5,13},{9,1},{13,5},{2,10},{6,14},... | collective-permute-start | bytes 49160 | tf_op jit(solution)/shard_map/ppermute | solution.py:480
  83.2 4.0 %collective-permute-start.24 = (f32[8,512]{1,0:T(8,128)S(1)}, f32[8,512]{1,0:T(8,128)S(1)}, u32[]{:S(2)}, u32[]{:S(2)}) collective-permute-start(f32[8,512]{1,0:T(8,128)S(1)} %get-tuple-element.107), channel_id=1, source_target_pairs={{0,12},{4,0},{8,4},{12,8},{1,13},{5,1},{9,5},{13,9},{2,14},{6,2},{... | collective-permute-start | bytes 49160 | tf_op jit(solution)/shard_map/ppermute | solution.py:480
  87.3 1.2 %collective-permute-start.25 = (f32[8,512]{1,0:T(8,128)S(1)}, f32[8,512]{1,0:T(8,128)S(1)}, u32[]{:S(2)}, u32[]{:S(2)}) collective-permute-start(f32[8,512]{1,0:T(8,128)S(1)} %masses.1.refs_0_), channel_id=1, source_target_pairs={{0,1},{1,0},{2,3},{3,2},{4,5},{5,4},{6,7},{7,6},{8,9},{9,8},{10,11... | collective-permute-start | bytes 49160 | tf_op jit(solution)/shard_map/ppermute | solution.py:465

commit v16 on v12

--- a/solution.py
+++ b/solution.py
@@ -12,7 +12,6 @@
 BLK_DEV = 8
 LANES = 128
 CHUNKS = ((0, 320), (320, 192))
-PIECES = (2, 1)
 WINDOWS = ((0, 256), (256, 512))
 
 
@@ -38,6 +37,10 @@
 
 def params(mebibytes):
     return pltpu.CompilerParams(vmem_limit_bytes=mebibytes * 1024 * 1024)
+
+
+def others(wide_count):
+    return range(wide_count - 1, 0, -1)
 
 
 def pack_kernel(wide_count, pair_count, capacity, me_ref, pairs_ref, *refs):
@@ -51,8 +54,8 @@
         copies[-1].start()
 
     for chunk, (start, size) in enumerate(CHUNKS):
-        for shift in range(1, wide_count):
-            asked = lists[shift - 1]
+        for number, other in enumerate(others(wide_count)):
+            asked = lists[other - 1]
             picks = [jnp.int32(0)] * capacity
             count = jnp.int32(0)
             for pair in range(pair_count):
@@ -61,7 +64,7 @@
                 for slot in range(capacity):
                     picks[slot] = jnp.where(mine & (count == slot), col & 7, picks[slot])
                 count = count + mine.astype(jnp.int32)
-            out = outs[chunk * (wide_count - 1) + shift - 1]
+            out = outs[chunk * (wide_count - 1) + number]
             for slot in range(capacity):
                 send(blocks_ref.at[picks[slot], pl.ds(start, size)], out.at[slot])
     for pair in range(pair_count):
@@ -92,42 +95,52 @@
     return [outs[c * each : (c + 1) * each] for c in range(len(CHUNKS))], outs[-1]
 
 
-def select_kernel(wide_count, start, me_ref, pairs_ref, own_ref, *refs):
+def select_kernel(wide_count, groups, start, me_ref, pairs_ref, own_ref, *refs):
     pair_count = own_ref.shape[0]
     outs = refs[wide_count - 1 :]
     received = refs[: wide_count - 1]
-    each, size, _ = outs[0].shape
+    size = outs[0].shape[1]
     owners = [pairs_ref[1, pair] >> 3 for pair in range(pair_count)]
     for pair in range(pair_count):
-        shift = me_ref[0] - owners[pair]
-        shift = jnp.where(shift < 0, shift + wide_count, shift)
+        apart = me_ref[0] ^ owners[pair]
         rank = jnp.int32(0)
         for before in range(pair):
             rank = rank + (owners[before] == owners[pair]).astype(jnp.int32)
 
-        out = outs[pair // each].at[pair % each]
-
-        @pl.when(shift == 0)
+        places, rest = [], outs
+        for pieces in groups:
+            places.append(of_pair(rest[:pieces], pair))
+            rest = rest[pieces:]
+
+        @pl.when(apart == 0)
         def _():
-            out[...] = own_ref[pair, start : start + size]
-
-        for other in range(1, wide_count):
-
-            @pl.when(shift == other)
+            for out in places:
+                out[...] = own_ref[pair, start : start + size]
+
+        for number, other in enumerate(others(wide_count)):
+
+            @pl.when(apart == other)
             def _():
-                out[...] = received[other - 1][rank]
-
-
-def select(me, pairs, own, received, start, size, pieces):
+                for out in places:
+                    out[...] = received[number][rank]
+
+
+def select(me, pairs, own, received, start, size, groups):
     pair_count, _, feat = own.shape
-    return pl.pallas_call(
-        functools.partial(select_kernel, len(received) + 1, start),
-        out_shape=[pltpu.VMEM((pair_count // pieces, size, feat), own.dtype)] * pieces,
+    shapes = [
+        pltpu.VMEM((pair_count // pieces, size, feat), own.dtype)
+        for pieces in groups
+        for _ in range(pieces)
+    ]
+    outs = pl.pallas_call(
+        functools.partial(select_kernel, len(received) + 1, groups, start),
+        out_shape=shapes,
         in_specs=[smem(), smem()] + [vmem()] * (1 + len(received)),
-        out_specs=[vmem()] * pieces,
+        out_specs=[vmem()] * len(shapes),
         compiler_params=params(4),
         name="select",
     )(me, in_hbm(pairs), *[in_vmem(x) for x in (own, *received)])
+    return take_parts(outs, groups)[0]
 
 
 def tree(parts):
@@ -171,9 +184,12 @@
     return kernel.astype(jnp.bfloat16), jnp.sum(kernel, axis=0, keepdims=True), mass
 
 
-def take_parts(refs, narrow_count, pieces):
-    parts = [refs[i * pieces : (i + 1) * pieces] for i in range(narrow_count)]
-    return parts, refs[narrow_count * pieces :]
+def take_parts(refs, counts):
+    parts = []
+    for count in counts:
+        parts.append(refs[:count])
+        refs = refs[count:]
+    return parts, refs
 
 
 def of_pair(part, pair):
@@ -181,11 +197,12 @@
     return part[pair // each].at[pair % each]
 
 
-def window_parts(window, narrow_count, refs):
-    rows, refs = [ref.at[i] for ref in refs[:2] for i in range(narrow_count // 2)], refs[2:]
+def window_parts(counts, refs):
+    half = len(counts[0]) // 2
+    rows, refs = [ref.at[i] for ref in refs[:2] for i in range(half)], refs[2:]
     chunks = []
-    for chunk, _, _ in segments(window):
-        cols, refs = take_parts(refs, narrow_count, PIECES[chunk])
+    for chunk_counts in counts:
+        cols, refs = take_parts(refs, chunk_counts)
         chunks.append(cols)
     return rows, chunks
 
@@ -201,9 +218,9 @@
     return [part[pair] for part in rows], cols
 
 
-def first_kernel(window, narrow_count, *refs):
+def first_kernel(window, counts, *refs):
     square_ref, mass_ref, total_ref, sums_ref = refs[-4:]
-    all_rows, chunks = window_parts(window, narrow_count, refs)
+    all_rows, chunks = window_parts(counts, refs)
     for pair in range(square_ref.shape[0]):
         rows, cols = pair_parts(window, all_rows, chunks, pair)
         square = jnp.sum(tree([lane_sum(row) for row in rows]), axis=1, keepdims=True)
@@ -215,13 +232,13 @@
         total_ref[pair] = jnp.dot(kernel, cols[0], preferred_element_type=jnp.float32)
 
 
-def last_kernel(window, narrow_count, wide_count, me_ref, pairs_ref, *refs):
+def last_kernel(window, counts, wide_count, me_ref, pairs_ref, *refs):
     square_in, mass_in, sums_in = refs[-6 - wide_count : -3 - wide_count]
     kernel_ref, mass_ref, row_ref = refs[-3 - wide_count : -wide_count]
     shares = refs[-wide_count:]
     for ref in (row_ref, *shares):
         ref[...] = jnp.zeros_like(ref)
-    all_rows, chunks = window_parts(window, narrow_count, refs)
+    all_rows, chunks = window_parts(counts, refs)
     for pair in range(square_in.shape[0]):
         rows, cols = pair_parts(window, all_rows, chunks, pair)
         kernel, sums, mass = scores(rows, cols, square_in[pair])
@@ -231,10 +248,9 @@
         mass_ref[pair] = mass
         row_ref[pl.ds(pairs_ref[0, pair] & 7, 1)] += jnp.sum(mass.T, axis=0, keepdims=True)
         col = pairs_ref[1, pair]
-        shift = (col >> 3) - me_ref[0]
-        shift = jnp.where(shift < 0, shift + wide_count, shift)
-        for other, ref in enumerate(shares):
-            ref[pl.ds(col & 7, 1)] += jnp.where(shift == other, sums, 0.0)
+        apart = (col >> 3) ^ me_ref[0]
+        for other, ref in zip([*others(wide_count), 0], shares):
+            ref[pl.ds(col & 7, 1)] += jnp.where(apart == other, sums, 0.0)
 
 
 def estimate(pair_count, size):
@@ -243,6 +259,10 @@
         transcendentals=pair_count * BR * size,
         bytes_accessed=8 * 1024 * 1024,
     )
+
+
+def piece_counts(window, cols):
+    return tuple(tuple(len(part) for part in cols[chunk]) for chunk, _, _ in segments(window))
 
 
 def operands(parts):
@@ -258,7 +278,7 @@
     for chunk, _, _ in segments(window):
         args += operands(cols[chunk])
     return pl.pallas_call(
-        functools.partial(first_kernel, window, len(cols[0])),
+        functools.partial(first_kernel, window, piece_counts(window, cols)),
         out_shape=[lanes, lanes, total, pltpu.VMEM((pair_count, window[1]), jnp.float32)],
         in_specs=[vmem()] * len(args),
         out_specs=[vmem()] * 4,
@@ -282,7 +302,7 @@
         args += operands(cols[chunk])
     args += [square, mass, sums]
     kernel, mass, row_sums, *shares = pl.pallas_call(
-        functools.partial(last_kernel, window, len(cols[0]), wide_count),
+        functools.partial(last_kernel, window, piece_counts(window, cols), wide_count),
         out_shape=shapes,
         in_specs=[smem(), smem()] + [vmem()] * len(args),
         out_specs=[vmem()] * len(shapes),
@@ -332,11 +352,11 @@
     )(in_hbm(pairs), in_hbm(blocks), in_hbm(blocks))
 
 
-def mean_kernel(window, local_ref, rows_ref, kernel_ref, mass_ref, total_ref, *refs):
+def mean_kernel(window, counts, local_ref, rows_ref, kernel_ref, mass_ref, total_ref, *refs):
     *refs, _, out_ref, part, weight, total, mass, made, sems = refs
     chunks = []
     for chunk, _, _ in segments(window):
-        (own,), refs = take_parts(refs, 1, PIECES[chunk])
+        (own,), refs = take_parts(refs, counts[len(chunks)][:1])
         chunks.append(own)
     pair_count, _, feat = rows_ref.shape
     local = [local_ref[0, pair] & 7 for pair in range(pair_count)]
@@ -387,7 +407,7 @@
     own = operands(cols[chunk][0] for chunk, _, _ in segments(window))
     args = [in_vmem(x) for x in (rows, kernel, mass, total, *own)]
     return pl.pallas_call(
-        functools.partial(mean_kernel, window),
+        functools.partial(mean_kernel, window, piece_counts(window, cols)),
         out_shape=pltpu.HBM(kept.shape, jnp.bfloat16),
         in_specs=[smem()] + [vmem()] * len(args) + [anywhere()],
         out_specs=anywhere(),
@@ -446,11 +466,11 @@
     return parts
 
 
-def to_wide(pieces):
+def to_wide(pieces, apart):
     count = lax.axis_size("wide")
     return [
-        lax.ppermute(piece, "wide", [(i, (i + shift) % count) for i in range(count)])
-        for shift, piece in enumerate(pieces, 1)
+        lax.ppermute(piece, "wide", [(i, i ^ other) for i in range(count)])
+        for piece, other in zip(pieces, apart)
     ]
 
 
@@ -462,21 +482,29 @@
     capacity = max(2, 2 * pair_count // wide_count)
     feat = embeddings.shape[1]
     blocks = embeddings.reshape(BLK_DEV, BR, feat)
-    lists = to_wide([pairs] * (wide_count - 1))[::-1]
+    apart = others(wide_count)
+    lists = to_wide([pairs] * (wide_count - 1), apart[::-1])
     fixed = lax.optimization_barrier
     outgoing, row_slices = pack(me, pairs, lists, blocks, capacity)
 
-    def pick(received, chunk):
-        return select(me, pairs, own, received, *CHUNKS[chunk], PIECES[chunk])
+    def pick(received, chunk, *groups):
+        return select(me, pairs, own, received, *CHUNKS[chunk], groups)
+
+    def halves(part):
+        middle = pair_count // 2
+        return [part[0][:middle], part[0][middle:]]
 
     rows = jnp.stack([part[0] for part in first_hops([row_slices])])
-    rows, received, (kept, own) = fixed((rows, to_wide(outgoing[0]), keep(pairs, blocks)))
-    cols_a = first_hops(pick(received, 0))
+    received = to_wide(outgoing[0], apart)
+    near = to_wide(outgoing[1][-1:], apart[-1:])
+    rows, received, near, (kept, own) = fixed((rows, received, near, keep(pairs, blocks)))
+    own_a, whole_a = pick(received, 0, 2, 1)
+    cols_a = [own_a] + first_hops(whole_a)[1:]
     rows = [[rows], *hop([[rows]], 1)]
-    cols_a, rows, received = fixed((cols_a, rows, to_wide(outgoing[1])))
-    cols_b = first_hops(pick(received, 1))
+    cols_a, rows, received = fixed((cols_a, rows, to_wide(outgoing[1][:-1], apart[:-1])))
+    cols_b = first_hops(*pick([*received, *near], 1, 1))
     last_b = hop(cols_b[:1], 1)
-    cols_a = cols_a + hop(cols_a, 1)
+    cols_a = cols_a + hop([own_a] + [halves(part) for part in cols_a[1:]], 1)
     carry = first_window(rows, [cols_a])
     cols_b, carry = fixed((cols_b, carry))
     cols_b = cols_b + last_b + hop(cols_b[1:], 1)
@@ -484,9 +512,9 @@
     kernel, mass, row_sums, shares = last_window(
         me, pairs, rows, [cols_a, cols_b], square, mass, sums, wide_count
     )
-    came = to_wide(shares[1:])
+    came = to_wide(shares[:-1], apart)
     mean = means(pairs, row_slices, kernel, mass, total, [cols_a, cols_b], kept)
-    weights = block_weights([row_sums, shares[0], *came])
+    weights = block_weights([row_sums, shares[-1], *came])
     return weights, mean.reshape(BLK_DEV * BR, feat)
 
 

time: 87.4 us -> 87.4 us (level)
  waiting for transfers between devices: 37.1 us -> 45.3 us
  starting transfers between devices: 29.5 us -> 21.6 us
    ppermute x12, waiting for transfers between devices: 16.2 us -> 26.9 us  [to_wide(): lax.ppermute(piece, 'wide', [(i, i ^ other) for i in range(count)])]
    ppermute x12, starting transfers between devices: 24.1 us -> 17.3 us  [to_wide(): lax.ppermute(piece, 'wide', [(i, i ^ other) for i in range(count)])]
    ppermute x11 -> x10, waiting for transfers between devices: 20.9 us -> 18.4 us  [hop(): lax.ppermute(piece, 'narrow', perm)]
    ppermute x11 -> x10, starting transfers between devices: 5.41 us -> 4.37 us  [hop(): lax.ppermute(piece, 'narrow', perm)]
  transfers between devices with their start and end apart: 23 -> 22, of which waited for: 15 -> 11; matrix products, arithmetic and copies ran while one was open for 0% -> 0% of each run, Pallas kernels for 14% -> 15%
where the time goes in v16:
time: 87.4 us; the launch traced here: 87.1 us
  waiting for transfers between devices  45.3 us (52%)
  starting transfers between devices  21.6 us (25%)
  Pallas kernels  19.1 us (22%)
    ppermute x12, waiting for transfers between devices, to_wide(): lax.ppermute(piece, 'wide', [(i, i ^ other) for i in range(count)])  26.9 us
    ppermute x10, waiting for transfers between devices, hop(): lax.ppermute(piece, 'narrow', perm)  18.4 us
    ppermute x12, starting transfers between devices, to_wide(): lax.ppermute(piece, 'wide', [(i, i ^ other) for i in range(count)])  17.3 us
    pallas_call x1, Pallas kernels, keep(): pl.pallas_call(keep_kernel, out_shape=[pltpu.HBM(blocks.shape, blocks.dty...  6.02 us
    ppermute x10, starting transfers between devices, hop(): lax.ppermute(piece, 'narrow', perm)  4.37 us
    pallas_call x1, Pallas kernels, first_window(): pl.pallas_call(functools.partial(first_kernel, window, piece_counts(windo...  3.1 us
    pallas_call x1, Pallas kernels, pack(): pl.pallas_call(functools.partial(pack_kernel, wide_count, pair_count, cap...  2.75 us
    pallas_call x1, Pallas kernels, last_window(): pl.pallas_call(functools.partial(last_kernel, window, piece_counts(window...  2.64 us
  transfers between devices with their start and end apart: 22, of which 11 were waited for; matrix products, arithmetic and copies ran while one was open for 0% of the time, Pallas kernels for 15%

profile of v16, /device:TPU:0, one launch (start us, length us, event | category | flops | bytes accessed | tf_op | source)
XLA Modules:
  0.0 87.1 jit_solution(9492658099189898170)
XLA Ops:
  0.6 5.1 %collective-permute-start.2 = (s32[2,4]{1,0:T(2,128)}, s32[2,4]{1,0:T(2,128)S(1)}, u32[]{:S(2)}, u32[]{:S(2)}) collective-permute-start(s32[2,4]{1,0:T(2,128)} %bitcast.13), channel_id=1, source_target_pairs={{0,12},{4,8},{8,4},{12,0},{1,13},{5,9},{9,5},{13,1},{2,14},{6,10},... | collective-permute-start | bytes 104 | tf_op jit(solution)/shard_map/ppermute | solution.py:472
  5.7 0.6 collective-permute-start
  6.4 1.1 %collective-permute-done.2.refs_2_ = s32[2,4]{1,0:T(2,128)S(1)} collective-permute-done((s32[2,4]{1,0:T(2,128)}, s32[2,4]{1,0:T(2,128)S(1)}, u32[]{:S(2)}, u32[]{:S(2)}) %collective-permute-start.2) | collective-permute-done | bytes 64 | tf_op jit(solution)/shard_map/ppermute | solution.py:472
  7.5 2.9 %collective-permute-done.1.refs_1_ = s32[2,4]{1,0:T(2,128)S(1)} collective-permute-done((s32[2,4]{1,0:T(2,128)}, s32[2,4]{1,0:T(2,128)S(1)}, u32[]{:S(2)}, u32[]{:S(2)}) %collective-permute-start.1) | collective-permute-done | bytes 64 | tf_op jit(solution)/shard_map/ppermute | solution.py:472
  10.4 2.8 %pack.1 = (bf16[2,320,256]{2,1,0:T(8,128)(2,1)S(1)}, bf16[2,320,256]{2,1,0:T(8,128)(2,1)S(1)}, bf16[2,320,256]{2,1,0:T(8,128)(2,1)S(1)}, bf16[2,192,256]{2,1,0:T...) custom-call(s32[1]{0:T(128)} %bitcast.me_ref, ...), custom_call_target="tpu_custom_call" | custom-call | tf_op jit(solution)/shard_map/pack/pallas_call | solution.py:85
  13.2 1.6 %collective-permute-start.3 = (bf16[4,512,256]{2,1,0:T(8,128)(2,1)S(1)}, bf16[4,512,256]{2,1,0:T(8,128)(2,1)S(1)}, u32[]{:S(2)}, u32[]{:S(2)}) collective-permute-start(bf16[4,512,256]{2,1,0:T(8,128)(2,1)S(1)} %get-tuple-element.45.rows_ref), channel_id=1, source_target_pairs={{0,2},{1,3},{2,0},{3,1},{4,6},{5,7},{6,4},{7,5},{8,10},{9,11},{10,... | collective-permute-start | bytes 3145736 | tf_op jit(solution)/shard_map/ppermute | solution.py:457
  14.7 1.7 %collective-permute-start.4 = (bf16[2,320,256]{2,1,0:T(8,128)(2,1)S(1)}, bf16[2,320,256]{2,1,0:T(8,128)(2,1)S(1)}, u32[]{:S(2)}, u32[]{:S(2)}) collective-permute-start(bf16[2,320,256]{2,1,0:T(8,128)(2,1)S(1)} %get-tuple-element.46), channel_id=1, source_target_pairs={{0,12},{4,8},{8,4},{12,0},{1,13},{5,9},{9,5},{13,1},{2,14},{6,10},... | collective-permute-start | bytes 983048 | tf_op jit(solution)/shard_map/ppermute | solution.py:472
  16.4 0.3 collective-permute-start.5
  16.7 2.4 %collective-permute-start.6 = (bf16[2,320,256]{2,1,0:T(8,128)(2,1)S(1)}, bf16[2,320,256]{2,1,0:T(8,128)(2,1)S(1)}, u32[]{:S(2)}, u32[]{:S(2)}) collective-permute-start(bf16[2,320,256]{2,1,0:T(8,128)(2,1)S(1)} %get-tuple-element.48), channel_id=1, source_target_pairs={{0,4},{4,0},{8,12},{12,8},{1,5},{5,1},{9,13},{13,9},{2,6},{6,2},{1... | collective-permute-start | bytes 983048 | tf_op jit(solution)/shard_map/ppermute | solution.py:472
  19.2 6.0 %keep.1 = (bf16[8,512,256]{2,1,0:T(8,128)(2,1)}, bf16[4,512,256]{2,1,0:T(8,128)(2,1)S(1)}) custom-call(s32[2,4]{1,0:T(2,128)} %bitcast.17, bf16[8,512,256]{2,1,0:T(8,128)(2,1)} %bitcast.9, bf16[8,512,256]{2,1,0:T(8,128)(2,1)} %bitcast.10), custom_call_target="tpu_custom_call" | custom-call | tf_op jit(solution)/shard_map/keep/pallas_call | solution.py:340
  25.2 11.5 %collective-permute-done.3 = bf16[4,512,256]{2,1,0:T(8,128)(2,1)S(1)} collective-permute-done((bf16[4,512,256]{2,1,0:T(8,128)(2,1)S(1)}, bf16[4,512,256]{2,1,0:T(8,128)(2,1)S(1)}, u32[]{:S(2)}, u32[]{:S(2)}) %collective-permute-start.3) | collective-permute-done | bytes 1048608 | tf_op jit(solution)/shard_map/ppermute | solution.py:457
  36.7 0.2 pad_maximum_fusion.refs_0_
  36.9 3.4 %collective-permute-done.7.refs_2_ = bf16[2,192,256]{2,1,0:T(8,128)(2,1)S(1)} collective-permute-done((bf16[2,192,256]{2,1,0:T(8,128)(2,1)S(1)}, bf16[2,192,256]{2,1,0:T(8,128)(2,1)S(1)}, u32[]{:S(2)}, u32[]{:S(2)}) %collective-permute-start.7) | collective-permute-done | bytes 196640 | tf_op jit(solution)/shard_map/ppermute | solution.py:472
  40.4 3.2 %collective-permute-done.5.refs_1_ = bf16[2,320,256]{2,1,0:T(8,128)(2,1)S(1)} collective-permute-done((bf16[2,320,256]{2,1,0:T(8,128)(2,1)S(1)}, bf16[2,320,256]{2,1,0:T(8,128)(2,1)S(1)}, u32[]{:S(2)}, u32[]{:S(2)}) %collective-permute-start.5) | collective-permute-done | bytes 327712 | tf_op jit(solution)/shard_map/ppermute | solution.py:472
  43.5 0.9 select.2
  44.4 0.6 collective-permute-start.8
  45.0 2.6 %collective-permute-start.10 = (bf16[2,192,256]{2,1,0:T(8,128)(2,1)S(1)}, bf16[2,192,256]{2,1,0:T(8,128)(2,1)S(1)}, u32[]{:S(2)}, u32[]{:S(2)}) collective-permute-start(bf16[2,192,256]{2,1,0:T(8,128)(2,1)S(1)} %get-tuple-element.60), channel_id=1, source_target_pairs={{0,12},{4,8},{8,4},{12,0},{1,13},{5,9},{9,5},{13,1},{2,14},{6,10},... | collective-permute-start | bytes 589832 | tf_op jit(solution)/shard_map/ppermute | solution.py:472
  47.6 7.0 %collective-permute-done.10.refs_0_ = bf16[2,192,256]{2,1,0:T(8,128)(2,1)S(1)} collective-permute-done((bf16[2,192,256]{2,1,0:T(8,128)(2,1)S(1)}, bf16[2,192,256]{2,1,0:T(8,128)(2,1)S(1)}, u32[]{:S(2)}, u32[]{:S(2)}) %collective-permute-start.10) | collective-permute-done | bytes 196640 | tf_op jit(solution)/shard_map/ppermute | solution.py:472
  54.6 9.3 %collective-permute-done.11.refs_1_ = bf16[2,192,256]{2,1,0:T(8,128)(2,1)S(1)} collective-permute-done((bf16[2,192,256]{2,1,0:T(8,128)(2,1)S(1)}, bf16[2,192,256]{2,1,0:T(8,128)(2,1)S(1)}, u32[]{:S(2)}, u32[]{:S(2)}) %collective-permute-start.11) | collective-permute-done | bytes 196640 | tf_op jit(solution)/shard_map/ppermute | solution.py:472
  63.9 0.8 select.3.refs_9_.refs_2_
  64.7 1.6 %collective-permute-start.16 = (bf16[4,192,256]{2,1,0:T(8,128)(2,1)S(1)}, bf16[4,192,256]{2,1,0:T(8,128)(2,1)S(1)}, u32[]{:S(2)}, u32[]{:S(2)}) collective-permute-start(bf16[4,192,256]{2,1,0:T(8,128)(2,1)S(1)} %select.3.refs_9_.refs_2_), channel_id=1, source_target_pairs={{0,2},{1,3},{2,0},{3,1},{4,6},{5,7},{6,4},{7,5},{8,10},{9,11},{10,... | collective-permute-start | bytes 1179656 | tf_op jit(solution)/shard_map/ppermute | solution.py:457
  66.4 0.5 collective-permute-start.14
  67.0 1.0 %collective-permute-done.15.refs_8_ = bf16[2,320,256]{2,1,0:T(8,128)(2,1)S(1)} collective-permute-done((bf16[2,320,256]{2,1,0:T(8,128)(2,1)S(1)}, bf16[2,320,256]{2,1,0:T(8,128)(2,1)S(1)}, u32[]{:S(2)}, u32[]{:S(2)}) %collective-permute-start.15) | collective-permute-done | bytes 327712 | tf_op jit(solution)/shard_map/ppermute | solution.py:457
  68.0 0.5 collective-permute-done.14.refs_7_
  68.5 3.1 %first_window.1 = (f32[4,512,128]{2,1,0:T(8,128)S(1)}, f32[4,512,128]{2,1,0:T(8,128)S(1)}, f32[4,512,256]{2,1,0:T(8,128)S(1)}, f32[4,256]{1,0:T(4,128)S(1)}) custom-call(bf16[2,4,512,256]{3,2,1,0:T(8,128)(2,1)S(1)} %pad_maximum_fusion.refs_0_, bf16[2,4,512,256]{3,2,1,0:T(8,128)(2,1)S(1)} %collective-permute-done.9.refs_1_, ...), custom_call_target="tpu_custom_call" | custom-call | tf_op jit(solution)/shard_map/first_window/pallas_call | solution.py:280
  71.6 3.6 %collective-permute-done.16.refs_10_ = bf16[4,192,256]{2,1,0:T(8,128)(2,1)S(1)} collective-permute-done((bf16[4,192,256]{2,1,0:T(8,128)(2,1)S(1)}, bf16[4,192,256]{2,1,0:T(8,128)(2,1)S(1)}, u32[]{:S(2)}, u32[]{:S(2)}) %collective-permute-start.16) | collective-permute-done | bytes 393248 | tf_op jit(solution)/shard_map/ppermute | solution.py:457
  75.2 1.7 %collective-permute-done.18.refs_12_ = bf16[4,192,256]{2,1,0:T(8,128)(2,1)S(1)} collective-permute-done((bf16[4,192,256]{2,1,0:T(8,128)(2,1)S(1)}, bf16[4,192,256]{2,1,0:T(8,128)(2,1)S(1)}, u32[]{:S(2)}, u32[]{:S(2)}) %collective-permute-start.18) | collective-permute-done | bytes 393248 | tf_op jit(solution)/shard_map/ppermute | solution.py:457
  77.0 2.6 %last_window.1 = (bf16[4,512,256]{2,1,0:T(8,128)(2,1)S(1)}, f32[4,512,128]{2,1,0:T(8,128)S(1)}, f32[8,512]{1,0:T(8,128)S(1)}, f32[8,512]{1,0:T(8,128)S(1)}, f32[...) custom-call(s32[1]{0:T(128)} %bitcast.me_ref, s32[2,4]{1,0:T(2,128)} %bitcast.20, ...), custom_call_target="tpu_custom_call" | custom-call | flops 1073741824 | bytes 8388608 | tf_op jit(solution)/shard_map/last_window/pallas_call | solution.py:304
  79.6 1.8 %collective-permute-start.19 = (f32[8,512]{1,0:T(8,128)S(1)}, f32[8,512]{1,0:T(8,128)S(1)}, u32[]{:S(2)}, u32[]{:S(2)}) collective-permute-start(f32[8,512]{1,0:T(8,128)S(1)} %get-tuple-element.81), channel_id=1, source_target_pairs={{0,12},{4,8},{8,4},{12,0},{1,13},{5,9},{9,5},{13,1},{2,14},{6,10},... | collective-permute-start | bytes 49160 | tf_op jit(solution)/shard_map/ppermute | solution.py:472
  81.4 2.6 %collective-permute-start.21 = (f32[8,512]{1,0:T(8,128)S(1)}, f32[8,512]{1,0:T(8,128)S(1)}, u32[]{:S(2)}, u32[]{:S(2)}) collective-permute-start(f32[8,512]{1,0:T(8,128)S(1)} %get-tuple-element.83), channel_id=1, source_target_pairs={{0,4},{4,0},{8,12},{12,8},{1,5},{5,1},{9,13},{13,9},{2,6},{6,2},{1... | collective-permute-start | bytes 49160 | tf_op jit(solution)/shard_map/ppermute | solution.py:472
  84.1 2.3 %means.1 = bf16[8,512,256]{2,1,0:T(8,128)(2,1)} custom-call(s32[2,4]{1,0:T(2,128)} %bitcast.21, bf16[4,512,256]{2,1,0:T(8,128)(2,1)S(1)} %get-tuple-element.45.rows_ref, bf16[4,512,256]{2,1,0:T(8,128)(2,1)S(1)} %get-tuple-element.84.kernel_ref, f32[4,512,128]{2,1,0:T(8,128)S(1)} %get-tuple-element.85.mass_ref, ...), custom_call_target="tpu_custom_call", output_to_operand_aliasing={{}: (8, {})} | custom-call | flops 536870912 | bytes 8388608 | tf_op jit(solution)/shard_map/means/pallas_call | solution.py:409
  86.4 0.6 weights.1
  (22 shorter events, 0.3 us)
Async XLA Ops:
  0.6 6.9 %collective-permute-start.2 = (s32[2,4]{1,0:T(2,128)}, s32[2,4]{1,0:T(2,128)S(1)}, u32[]{:S(2)}, u32[]{:S(2)}) collective-permute-start(s32[2,4]{1,0:T(2,128)} %bitcast.13), channel_id=1, source_target_pairs={{0,12},{4,8},{8,4},{12,0},{1,13},{5,9},{9,5},{13,1},{2,14},{6,10},... | collective-permute-start | bytes 104 | tf_op jit(solution)/shard_map/ppermute | solution.py:472
  5.7 4.7 %collective-permute-start.1 = (s32[2,4]{1,0:T(2,128)}, s32[2,4]{1,0:T(2,128)S(1)}, u32[]{:S(2)}, u32[]{:S(2)}) collective-permute-start(s32[2,4]{1,0:T(2,128)} %bitcast.14), channel_id=1, source_target_pairs={{0,8},{4,12},{8,0},{12,4},{1,9},{5,13},{9,1},{13,5},{2,10},{6,14},... | collective-permute-start | bytes 104 | tf_op jit(solution)/shard_map/ppermute | solution.py:472
  5.7 4.7 %collective-permute-start = (s32[2,4]{1,0:T(2,128)}, s32[2,4]{1,0:T(2,128)S(1)}, u32[]{:S(2)}, u32[]{:S(2)}) collective-permute-start(s32[2,4]{1,0:T(2,128)} %bitcast.15), channel_id=1, source_target_pairs={{0,4},{4,0},{8,12},{12,8},{1,5},{5,1},{9,13},{13,9},{2,6},{6,2},{1... | collective-permute-start | bytes 104 | tf_op jit(solution)/shard_map/ppermute | solution.py:472
  13.2 23.5 %collective-permute-start.3 = (bf16[4,512,256]{2,1,0:T(8,128)(2,1)S(1)}, bf16[4,512,256]{2,1,0:T(8,128)(2,1)S(1)}, u32[]{:S(2)}, u32[]{:S(2)}) collective-permute-start(bf16[4,512,256]{2,1,0:T(8,128)(2,1)S(1)} %get-tuple-element.45.rows_ref), channel_id=1, source_target_pairs={{0,2},{1,3},{2,0},{3,1},{4,6},{5,7},{6,4},{7,5},{8,10},{9,11},{10,... | collective-permute-start | bytes 3145736 | tf_op jit(solution)/shard_map/ppermute | solution.py:457
  14.7 25.6 %collective-permute-start.4 = (bf16[2,320,256]{2,1,0:T(8,128)(2,1)S(1)}, bf16[2,320,256]{2,1,0:T(8,128)(2,1)S(1)}, u32[]{:S(2)}, u32[]{:S(2)}) collective-permute-start(bf16[2,320,256]{2,1,0:T(8,128)(2,1)S(1)} %get-tuple-element.46), channel_id=1, source_target_pairs={{0,12},{4,8},{8,4},{12,0},{1,13},{5,9},{9,5},{13,1},{2,14},{6,10},... | collective-permute-start | bytes 983048 | tf_op jit(solution)/shard_map/ppermute | solution.py:472
  16.4 27.1 %collective-permute-start.5 = (bf16[2,320,256]{2,1,0:T(8,128)(2,1)S(1)}, bf16[2,320,256]{2,1,0:T(8,128)(2,1)S(1)}, u32[]{:S(2)}, u32[]{:S(2)}) collective-permute-start(bf16[2,320,256]{2,1,0:T(8,128)(2,1)S(1)} %get-tuple-element.47), channel_id=1, source_target_pairs={{0,8},{4,12},{8,0},{12,4},{1,9},{5,13},{9,1},{13,5},{2,10},{6,14},... | collective-permute-start | bytes 983048 | tf_op jit(solution)/shard_map/ppermute | solution.py:472
  16.7 26.8 %collective-permute-start.6 = (bf16[2,320,256]{2,1,0:T(8,128)(2,1)S(1)}, bf16[2,320,256]{2,1,0:T(8,128)(2,1)S(1)}, u32[]{:S(2)}, u32[]{:S(2)}) collective-permute-start(bf16[2,320,256]{2,1,0:T(8,128)(2,1)S(1)} %get-tuple-element.48), channel_id=1, source_target_pairs={{0,4},{4,0},{8,12},{12,8},{1,5},{5,1},{9,13},{13,9},{2,6},{6,2},{1... | collective-permute-start | bytes 983048 | tf_op jit(solution)/shard_map/ppermute | solution.py:472
  19.1 21.2 %collective-permute-start.7 = (bf16[2,192,256]{2,1,0:T(8,128)(2,1)S(1)}, bf16[2,192,256]{2,1,0:T(8,128)(2,1)S(1)}, u32[]{:S(2)}, u32[]{:S(2)}) collective-permute-start(bf16[2,192,256]{2,1,0:T(8,128)(2,1)S(1)} %get-tuple-element.49), channel_id=1, source_target_pairs={{0,4},{4,0},{8,12},{12,8},{1,5},{5,1},{9,13},{13,9},{2,6},{6,2},{1... | collective-permute-start | bytes 589832 | tf_op jit(solution)/shard_map/ppermute | solution.py:472
  43.5 20.4 %collective-permute-start.9 = (bf16[2,4,512,256]{3,2,1,0:T(8,128)(2,1)S(1)}, bf16[2,4,512,256]{3,2,1,0:T(8,128)(2,1)S(1)}, u32[]{:S(2)}, u32[]{:S(2)}) collective-permute-start(bf16[2,4,512,256]{3,2,1,0:T(8,128)(2,1)S(1)} %pad_maximum_fusion.refs_0_), channel_id=1, source_target_pairs={{0,1},{1,0},{2,3},{3,2},{4,5},{5,4},{6,7},{7,6},{8,9},{9,8},{10,11... | collective-permute-start | bytes 6291464 | tf_op jit(solution)/shard_map/ppermute | solution.py:457
  44.4 19.5 %collective-permute-start.8 = (bf16[4,320,256]{2,1,0:T(8,128)(2,1)S(1)}, bf16[4,320,256]{2,1,0:T(8,128)(2,1)S(1)}, u32[]{:S(2)}, u32[]{:S(2)}) collective-permute-start(bf16[4,320,256]{2,1,0:T(8,128)(2,1)S(1)} %get-tuple-element.58), channel_id=1, source_target_pairs={{0,2},{1,3},{2,0},{3,1},{4,6},{5,7},{6,4},{7,5},{8,10},{9,11},{10,... | collective-permute-start | bytes 1966088 | tf_op jit(solution)/shard_map/ppermute | solution.py:457
  45.0 9.6 %collective-permute-start.10 = (bf16[2,192,256]{2,1,0:T(8,128)(2,1)S(1)}, bf16[2,192,256]{2,1,0:T(8,128)(2,1)S(1)}, u32[]{:S(2)}, u32[]{:S(2)}) collective-permute-start(bf16[2,192,256]{2,1,0:T(8,128)(2,1)S(1)} %get-tuple-element.60), channel_id=1, source_target_pairs={{0,12},{4,8},{8,4},{12,0},{1,13},{5,9},{9,5},{13,1},{2,14},{6,10},... | collective-permute-start | bytes 589832 | tf_op jit(solution)/shard_map/ppermute | solution.py:472
  47.6 16.3 %collective-permute-start.11 = (bf16[2,192,256]{2,1,0:T(8,128)(2,1)S(1)}, bf16[2,192,256]{2,1,0:T(8,128)(2,1)S(1)}, u32[]{:S(2)}, u32[]{:S(2)}) collective-permute-start(bf16[2,192,256]{2,1,0:T(8,128)(2,1)S(1)} %get-tuple-element.61), channel_id=1, source_target_pairs={{0,8},{4,12},{8,0},{12,4},{1,9},{5,13},{9,1},{13,5},{2,10},{6,14},... | collective-permute-start | bytes 589832 | tf_op jit(solution)/shard_map/ppermute | solution.py:472
  47.6 19.3 %collective-permute-start.12 = (bf16[2,320,256]{2,1,0:T(8,128)(2,1)S(1)}, bf16[2,320,256]{2,1,0:T(8,128)(2,1)S(1)}, u32[]{:S(2)}, u32[]{:S(2)}) collective-permute-start(bf16[2,320,256]{2,1,0:T(8,128)(2,1)S(1)} %get-tuple-element.64.refs_2_.refs_0_), channel_id=1, source_target_pairs={{0,1},{1,0},{2,3},{3,2},{4,5},{5,4},{6,7},{7,6},{8,9},{9,8},{10,11... | collective-permute-start | bytes 983048 | tf_op jit(solution)/shard_map/ppermute | solution.py:457
  54.6 12.4 %collective-permute-start.13 = (bf16[2,320,256]{2,1,0:T(8,128)(2,1)S(1)}, bf16[2,320,256]{2,1,0:T(8,128)(2,1)S(1)}, u32[]{:S(2)}, u32[]{:S(2)}) collective-permute-start(bf16[2,320,256]{2,1,0:T(8,128)(2,1)S(1)} %get-tuple-element.65.refs_3_.refs_1_), channel_id=1, source_target_pairs={{0,1},{1,0},{2,3},{3,2},{4,5},{5,4},{6,7},{7,6},{8,9},{9,8},{10,11... | collective-permute-start | bytes 983048 | tf_op jit(solution)/shard_map/ppermute | solution.py:457
  64.7 10.5 %collective-permute-start.16 = (bf16[4,192,256]{2,1,0:T(8,128)(2,1)S(1)}, bf16[4,192,256]{2,1,0:T(8,128)(2,1)S(1)}, u32[]{:S(2)}, u32[]{:S(2)}) collective-permute-start(bf16[4,192,256]{2,1,0:T(8,128)(2,1)S(1)} %select.3.refs_9_.refs_2_), channel_id=1, source_target_pairs={{0,2},{1,3},{2,0},{3,1},{4,6},{5,7},{6,4},{7,5},{8,10},{9,11},{10,... | collective-permute-start | bytes 1179656 | tf_op jit(solution)/shard_map/ppermute | solution.py:457
  66.3 1.7 %collective-permute-start.15 = (bf16[2,320,256]{2,1,0:T(8,128)(2,1)S(1)}, bf16[2,320,256]{2,1,0:T(8,128)(2,1)S(1)}, u32[]{:S(2)}, u32[]{:S(2)}) collective-permute-start(bf16[2,320,256]{2,1,0:T(8,128)(2,1)S(1)} %get-tuple-element.88), channel_id=1, source_target_pairs={{0,1},{1,0},{2,3},{3,2},{4,5},{5,4},{6,7},{7,6},{8,9},{9,8},{10,11... | collective-permute-start | bytes 983048 | tf_op jit(solution)/shard_map/ppermute | solution.py:457
  66.4 2.1 %collective-permute-start.14 = (bf16[2,320,256]{2,1,0:T(8,128)(2,1)S(1)}, bf16[2,320,256]{2,1,0:T(8,128)(2,1)S(1)}, u32[]{:S(2)}, u32[]{:S(2)}) collective-permute-start(bf16[2,320,256]{2,1,0:T(8,128)(2,1)S(1)} %get-tuple-element.89), channel_id=1, source_target_pairs={{0,1},{1,0},{2,3},{3,2},{4,5},{5,4},{6,7},{7,6},{8,9},{9,8},{10,11... | collective-permute-start | bytes 983048 | tf_op jit(solution)/shard_map/ppermute | solution.py:457
  66.9 8.3 %collective-permute-start.17 = (bf16[4,192,256]{2,1,0:T(8,128)(2,1)S(1)}, bf16[4,192,256]{2,1,0:T(8,128)(2,1)S(1)}, u32[]{:S(2)}, u32[]{:S(2)}) collective-permute-start(bf16[4,192,256]{2,1,0:T(8,128)(2,1)S(1)} %select.3.refs_9_.refs_2_), channel_id=1, source_target_pairs={{0,1},{1,0},{2,3},{3,2},{4,5},{5,4},{6,7},{7,6},{8,9},{9,8},{10,11... | collective-permute-start | bytes 1179656 | tf_op jit(solution)/shard_map/ppermute | solution.py:457
  75.2 1.7 %collective-permute-start.18 = (bf16[4,192,256]{2,1,0:T(8,128)(2,1)S(1)}, bf16[4,192,256]{2,1,0:T(8,128)(2,1)S(1)}, u32[]{:S(2)}, u32[]{:S(2)}) collective-permute-start(bf16[4,192,256]{2,1,0:T(8,128)(2,1)S(1)} %collective-permute-done.16.refs_10_), channel_id=1, source_target_pairs={{0,1},{1,0},{2,3},{3,2},{4,5},{5,4},{6,7},{7,6},{8,9},{9,8},{10,11... | collective-permute-start | bytes 1179656 | tf_op jit(solution)/shard_map/ppermute | solution.py:457
  79.6 6.8 %collective-permute-start.19 = (f32[8,512]{1,0:T(8,128)S(1)}, f32[8,512]{1,0:T(8,128)S(1)}, u32[]{:S(2)}, u32[]{:S(2)}) collective-permute-start(f32[8,512]{1,0:T(8,128)S(1)} %get-tuple-element.81), channel_id=1, source_target_pairs={{0,12},{4,8},{8,4},{12,0},{1,13},{5,9},{9,5},{13,1},{2,14},{6,10},... | collective-permute-start | bytes 49160 | tf_op jit(solution)/shard_map/ppermute | solution.py:472
  81.4 5.0 %collective-permute-start.20 = (f32[8,512]{1,0:T(8,128)S(1)}, f32[8,512]{1,0:T(8,128)S(1)}, u32[]{:S(2)}, u32[]{:S(2)}) collective-permute-start(f32[8,512]{1,0:T(8,128)S(1)} %get-tuple-element.82), channel_id=1, source_target_pairs={{0,8},{4,12},{8,0},{12,4},{1,9},{5,13},{9,1},{13,5},{2,10},{6,14},... | collective-permute-start | bytes 49160 | tf_op jit(solution)/shard_map/ppermute | solution.py:472
  81.4 5.0 %collective-permute-start.21 = (f32[8,512]{1,0:T(8,128)S(1)}, f32[8,512]{1,0:T(8,128)S(1)}, u32[]{:S(2)}, u32[]{:S(2)}) collective-permute-start(f32[8,512]{1,0:T(8,128)S(1)} %get-tuple-element.83), channel_id=1, source_target_pairs={{0,4},{4,0},{8,12},{12,8},{1,5},{5,1},{9,13},{13,9},{2,6},{6,2},{1... | collective-permute-start | bytes 49160 | tf_op jit(solution)/shard_map/ppermute | solution.py:472

commit v17 on v16

--- a/solution.py
+++ b/solution.py
@@ -11,7 +11,7 @@
 BR = 512
 BLK_DEV = 8
 LANES = 128
-CHUNKS = ((0, 320), (320, 192))
+CHUNKS = ((0, 336), (336, 176))
 WINDOWS = ((0, 256), (256, 512))
 
 
@@ -55,7 +55,7 @@
 
     for chunk, (start, size) in enumerate(CHUNKS):
         for number, other in enumerate(others(wide_count)):
-            asked = lists[other - 1]
+            asked = lists[list_order(wide_count).index(other)]
             picks = [jnp.int32(0)] * capacity
             count = jnp.int32(0)
             for pair in range(pair_count):
@@ -71,6 +71,11 @@
         send(blocks_ref.at[pairs_ref[0, pair] & 7], rows_ref.at[pair])
     for copy in copies:
         copy.wait()
+
+
+def list_order(wide_count):
+    middle = wide_count // 2
+    return [other for other in range(1, wide_count) if other != middle] + [middle]
 
 
 def pack(me, pairs, lists, blocks, capacity):
@@ -90,7 +95,7 @@
         scratch_shapes=[pltpu.SemaphoreType.DMA((copies,))],
         compiler_params=params(4),
         name="pack",
-    )(me, in_hbm(pairs), *lists, in_hbm(blocks))
+    )(me, in_hbm(pairs), *[lists[other - 1] for other in list_order(wide_count)], in_hbm(blocks))
     each = wide_count - 1
     return [outs[c * each : (c + 1) * each] for c in range(len(CHUNKS))], outs[-1]
 

time: 87.4 us -> 86.4 us (0.989)
  waiting for transfers between devices: 45.3 us -> 44.2 us
  transfers between devices with their start and end apart: 22 -> 22, of which waited for: 11 -> 12; matrix products, arithmetic and copies ran while one was open for 0% -> 0% of each run, Pallas kernels for 15% -> 15%
where the time goes in v17:
time: 86.4 us; the launch traced here: 86 us
  waiting for transfers between devices  44.2 us (51%)
  starting transfers between devices  21.6 us (25%)
  Pallas kernels  19.3 us (22%)
    ppermute x12, waiting for transfers between devices, to_wide(): lax.ppermute(piece, 'wide', [(i, i ^ other) for i in range(count)])  26.5 us
    ppermute x10, waiting for transfers between devices, hop(): lax.ppermute(piece, 'narrow', perm)  17.7 us
    ppermute x12, starting transfers between devices, to_wide(): lax.ppermute(piece, 'wide', [(i, i ^ other) for i in range(count)])  17.2 us
    pallas_call x1, Pallas kernels, keep(): pl.pallas_call(keep_kernel, out_shape=[pltpu.HBM(blocks.shape, blocks.dty...  6.02 us
    ppermute x10, starting transfers between devices, hop(): lax.ppermute(piece, 'narrow', perm)  4.37 us
    pallas_call x1, Pallas kernels, first_window(): pl.pallas_call(functools.partial(first_kernel, window, piece_counts(windo...  3.1 us
    pallas_call x1, Pallas kernels, pack(): pl.pallas_call(functools.partial(pack_kernel, wide_count, pair_count, cap...  2.93 us
    pallas_call x1, Pallas kernels, last_window(): pl.pallas_call(functools.partial(last_kernel, window, piece_counts(window...  2.64 us
  transfers between devices with their start and end apart: 22, of which 12 were waited for; matrix products, arithmetic and copies ran while one was open for 0% of the time, Pallas kernels for 15%

profile of v17, /device:TPU:0, one launch (start us, length us, event | category | flops | bytes accessed | tf_op | source)
XLA Modules:
  0.0 86.0 jit_solution(10193991364105368990)
XLA Ops:
  0.6 4.1 %collective-permute-start.2 = (s32[2,4]{1,0:T(2,128)}, s32[2,4]{1,0:T(2,128)S(1)}, u32[]{:S(2)}, u32[]{:S(2)}) collective-permute-start(s32[2,4]{1,0:T(2,128)} %bitcast.13), channel_id=1, source_target_pairs={{0,8},{4,12},{8,0},{12,4},{1,9},{5,13},{9,1},{13,5},{2,10},{6,14},... | collective-permute-start | bytes 104 | tf_op jit(solution)/shard_map/ppermute | solution.py:477
  4.7 1.3 %collective-permute-start.1 = (s32[2,4]{1,0:T(2,128)}, s32[2,4]{1,0:T(2,128)S(1)}, u32[]{:S(2)}, u32[]{:S(2)}) collective-permute-start(s32[2,4]{1,0:T(2,128)} %bitcast.14), channel_id=1, source_target_pairs={{0,12},{4,8},{8,4},{12,0},{1,13},{5,9},{9,5},{13,1},{2,14},{6,10},... | collective-permute-start | bytes 104 | tf_op jit(solution)/shard_map/ppermute | solution.py:477
  6.1 0.2 collective-permute-start
  6.5 3.8 %collective-permute-done.1.refs_1_ = s32[2,4]{1,0:T(2,128)S(1)} collective-permute-done((s32[2,4]{1,0:T(2,128)}, s32[2,4]{1,0:T(2,128)S(1)}, u32[]{:S(2)}, u32[]{:S(2)}) %collective-permute-start.1) | collective-permute-done | bytes 64 | tf_op jit(solution)/shard_map/ppermute | solution.py:477
  10.3 2.9 %pack.1 = (bf16[2,336,256]{2,1,0:T(8,128)(2,1)S(1)}, bf16[2,336,256]{2,1,0:T(8,128)(2,1)S(1)}, bf16[2,336,256]{2,1,0:T(8,128)(2,1)S(1)}, bf16[2,176,256]{2,1,0:T...) custom-call(s32[1]{0:T(128)} %bitcast.me_ref, ...), custom_call_target="tpu_custom_call" | custom-call | tf_op jit(solution)/shard_map/pack/pallas_call | solution.py:90
  13.3 1.6 %collective-permute-start.3 = (bf16[4,512,256]{2,1,0:T(8,128)(2,1)S(1)}, bf16[4,512,256]{2,1,0:T(8,128)(2,1)S(1)}, u32[]{:S(2)}, u32[]{:S(2)}) collective-permute-start(bf16[4,512,256]{2,1,0:T(8,128)(2,1)S(1)} %get-tuple-element.45.rows_ref), channel_id=1, source_target_pairs={{0,2},{1,3},{2,0},{3,1},{4,6},{5,7},{6,4},{7,5},{8,10},{9,11},{10,... | collective-permute-start | bytes 3145736 | tf_op jit(solution)/shard_map/ppermute | solution.py:462
  14.8 1.8 %collective-permute-start.4 = (bf16[2,336,256]{2,1,0:T(8,128)(2,1)S(1)}, bf16[2,336,256]{2,1,0:T(8,128)(2,1)S(1)}, u32[]{:S(2)}, u32[]{:S(2)}) collective-permute-start(bf16[2,336,256]{2,1,0:T(8,128)(2,1)S(1)} %get-tuple-element.46), channel_id=1, source_target_pairs={{0,12},{4,8},{8,4},{12,0},{1,13},{5,9},{9,5},{13,1},{2,14},{6,10},... | collective-permute-start | bytes 1032200 | tf_op jit(solution)/shard_map/ppermute | solution.py:477
  16.6 2.6 %collective-permute-start.6 = (bf16[2,336,256]{2,1,0:T(8,128)(2,1)S(1)}, bf16[2,336,256]{2,1,0:T(8,128)(2,1)S(1)}, u32[]{:S(2)}, u32[]{:S(2)}) collective-permute-start(bf16[2,336,256]{2,1,0:T(8,128)(2,1)S(1)} %get-tuple-element.48), channel_id=1, source_target_pairs={{0,4},{4,0},{8,12},{12,8},{1,5},{5,1},{9,13},{13,9},{2,6},{6,2},{1... | collective-permute-start | bytes 1032200 | tf_op jit(solution)/shard_map/ppermute | solution.py:477
  19.2 6.0 %keep.1 = (bf16[8,512,256]{2,1,0:T(8,128)(2,1)}, bf16[4,512,256]{2,1,0:T(8,128)(2,1)S(1)}) custom-call(s32[2,4]{1,0:T(2,128)} %bitcast.17, bf16[8,512,256]{2,1,0:T(8,128)(2,1)} %bitcast.9, bf16[8,512,256]{2,1,0:T(8,128)(2,1)} %bitcast.10), custom_call_target="tpu_custom_call" | custom-call | tf_op jit(solution)/shard_map/keep/pallas_call | solution.py:345
  25.3 11.5 %collective-permute-done.3 = bf16[4,512,256]{2,1,0:T(8,128)(2,1)S(1)} collective-permute-done((bf16[4,512,256]{2,1,0:T(8,128)(2,1)S(1)}, bf16[4,512,256]{2,1,0:T(8,128)(2,1)S(1)}, u32[]{:S(2)}, u32[]{:S(2)}) %collective-permute-start.3) | collective-permute-done | bytes 1048608 | tf_op jit(solution)/shard_map/ppermute | solution.py:462
  36.8 0.2 pad_maximum_fusion.refs_0_
  37.0 3.7 %collective-permute-done.7.refs_2_ = bf16[2,176,256]{2,1,0:T(8,128)(2,1)S(1)} collective-permute-done((bf16[2,176,256]{2,1,0:T(8,128)(2,1)S(1)}, bf16[2,176,256]{2,1,0:T(8,128)(2,1)S(1)}, u32[]{:S(2)}, u32[]{:S(2)}) %collective-permute-start.7) | collective-permute-done | bytes 180256 | tf_op jit(solution)/shard_map/ppermute | solution.py:477
  40.7 3.3 %collective-permute-done.5.refs_1_ = bf16[2,336,256]{2,1,0:T(8,128)(2,1)S(1)} collective-permute-done((bf16[2,336,256]{2,1,0:T(8,128)(2,1)S(1)}, bf16[2,336,256]{2,1,0:T(8,128)(2,1)S(1)}, u32[]{:S(2)}, u32[]{:S(2)}) %collective-permute-start.5) | collective-permute-done | bytes 344096 | tf_op jit(solution)/shard_map/ppermute | solution.py:477
  44.0 0.9 %select.2 = (bf16[2,336,256]{2,1,0:T(8,128)(2,1)S(1)}, bf16[2,336,256]{2,1,0:T(8,128)(2,1)S(1)}, bf16[4,336,256]{2,1,0:T(8,128)(2,1)S(1)}) custom-call(s32[1]{0:T(128)} %bitcast.me_ref, s32[2,4]{1,0:T(2,128)} %bitcast.18, bf16[4,512,256]{2,1,0:T(8,128)(2,1)S(1)} %get-tuple-element.52.own_ref, bf16[2,336,256]{2,1,0:T(8,128)(2,1)S(1)} %collective-permute-done.4.refs_0_, ...), custom_call_target="tpu_custom_call" | custom-call | tf_op jit(solution)/shard_map/select/pallas_call | solution.py:140
  44.9 0.6 collective-permute-start.8
  45.5 2.6 %collective-permute-start.10 = (bf16[2,176,256]{2,1,0:T(8,128)(2,1)S(1)}, bf16[2,176,256]{2,1,0:T(8,128)(2,1)S(1)}, u32[]{:S(2)}, u32[]{:S(2)}) collective-permute-start(bf16[2,176,256]{2,1,0:T(8,128)(2,1)S(1)} %get-tuple-element.60), channel_id=1, source_target_pairs={{0,12},{4,8},{8,4},{12,0},{1,13},{5,9},{9,5},{13,1},{2,14},{6,10},... | collective-permute-start | bytes 540680 | tf_op jit(solution)/shard_map/ppermute | solution.py:477
  48.1 6.6 %collective-permute-done.10.refs_0_ = bf16[2,176,256]{2,1,0:T(8,128)(2,1)S(1)} collective-permute-done((bf16[2,176,256]{2,1,0:T(8,128)(2,1)S(1)}, bf16[2,176,256]{2,1,0:T(8,128)(2,1)S(1)}, u32[]{:S(2)}, u32[]{:S(2)}) %collective-permute-start.10) | collective-permute-done | bytes 180256 | tf_op jit(solution)/shard_map/ppermute | solution.py:477
  54.8 8.2 %collective-permute-done.11.refs_1_ = bf16[2,176,256]{2,1,0:T(8,128)(2,1)S(1)} collective-permute-done((bf16[2,176,256]{2,1,0:T(8,128)(2,1)S(1)}, bf16[2,176,256]{2,1,0:T(8,128)(2,1)S(1)}, u32[]{:S(2)}, u32[]{:S(2)}) %collective-permute-start.11) | collective-permute-done | bytes 180256 | tf_op jit(solution)/shard_map/ppermute | solution.py:477
  63.0 0.8 select.3.refs_9_.refs_2_
  63.8 1.6 %collective-permute-start.16 = (bf16[4,176,256]{2,1,0:T(8,128)(2,1)S(1)}, bf16[4,176,256]{2,1,0:T(8,128)(2,1)S(1)}, u32[]{:S(2)}, u32[]{:S(2)}) collective-permute-start(bf16[4,176,256]{2,1,0:T(8,128)(2,1)S(1)} %select.3.refs_9_.refs_2_), channel_id=1, source_target_pairs={{0,2},{1,3},{2,0},{3,1},{4,6},{5,7},{6,4},{7,5},{8,10},{9,11},{10,... | collective-permute-start | bytes 1081352 | tf_op jit(solution)/shard_map/ppermute | solution.py:462
  65.5 0.5 collective-permute-start.14
  66.1 1.1 %collective-permute-done.15.refs_8_ = bf16[2,336,256]{2,1,0:T(8,128)(2,1)S(1)} collective-permute-done((bf16[2,336,256]{2,1,0:T(8,128)(2,1)S(1)}, bf16[2,336,256]{2,1,0:T(8,128)(2,1)S(1)}, u32[]{:S(2)}, u32[]{:S(2)}) %collective-permute-start.15) | collective-permute-done | bytes 344096 | tf_op jit(solution)/shard_map/ppermute | solution.py:462
  67.2 0.5 collective-permute-done.14.refs_7_
  67.7 3.1 %first_window.1 = (f32[4,512,128]{2,1,0:T(8,128)S(1)}, f32[4,512,128]{2,1,0:T(8,128)S(1)}, f32[4,512,256]{2,1,0:T(8,128)S(1)}, f32[4,256]{1,0:T(4,128)S(1)}) custom-call(bf16[2,4,512,256]{3,2,1,0:T(8,128)(2,1)S(1)} %pad_maximum_fusion.refs_0_, bf16[2,4,512,256]{3,2,1,0:T(8,128)(2,1)S(1)} %collective-permute-done.9.refs_1_, ...), custom_call_target="tpu_custom_call" | custom-call | tf_op jit(solution)/shard_map/first_window/pallas_call | solution.py:285
  70.8 3.0 %collective-permute-done.16.refs_10_ = bf16[4,176,256]{2,1,0:T(8,128)(2,1)S(1)} collective-permute-done((bf16[4,176,256]{2,1,0:T(8,128)(2,1)S(1)}, bf16[4,176,256]{2,1,0:T(8,128)(2,1)S(1)}, u32[]{:S(2)}, u32[]{:S(2)}) %collective-permute-start.16) | collective-permute-done | bytes 360480 | tf_op jit(solution)/shard_map/ppermute | solution.py:462
  73.7 1.7 %collective-permute-done.18.refs_12_ = bf16[4,176,256]{2,1,0:T(8,128)(2,1)S(1)} collective-permute-done((bf16[4,176,256]{2,1,0:T(8,128)(2,1)S(1)}, bf16[4,176,256]{2,1,0:T(8,128)(2,1)S(1)}, u32[]{:S(2)}, u32[]{:S(2)}) %collective-permute-start.18) | collective-permute-done | bytes 360480 | tf_op jit(solution)/shard_map/ppermute | solution.py:462
  75.4 2.6 %last_window.1 = (bf16[4,512,256]{2,1,0:T(8,128)(2,1)S(1)}, f32[4,512,128]{2,1,0:T(8,128)S(1)}, f32[8,512]{1,0:T(8,128)S(1)}, f32[8,512]{1,0:T(8,128)S(1)}, f32[...) custom-call(s32[1]{0:T(128)} %bitcast.me_ref, s32[2,4]{1,0:T(2,128)} %bitcast.20, ...), custom_call_target="tpu_custom_call" | custom-call | flops 1073741824 | bytes 8388608 | tf_op jit(solution)/shard_map/last_window/pallas_call | solution.py:309
  78.0 2.7 %collective-permute-start.19 = (f32[8,512]{1,0:T(8,128)S(1)}, f32[8,512]{1,0:T(8,128)S(1)}, u32[]{:S(2)}, u32[]{:S(2)}) collective-permute-start(f32[8,512]{1,0:T(8,128)S(1)} %get-tuple-element.81), channel_id=1, source_target_pairs={{0,12},{4,8},{8,4},{12,0},{1,13},{5,9},{9,5},{13,1},{2,14},{6,10},... | collective-permute-start | bytes 49160 | tf_op jit(solution)/shard_map/ppermute | solution.py:477
  80.8 1.7 %collective-permute-start.21 = (f32[8,512]{1,0:T(8,128)S(1)}, f32[8,512]{1,0:T(8,128)S(1)}, u32[]{:S(2)}, u32[]{:S(2)}) collective-permute-start(f32[8,512]{1,0:T(8,128)S(1)} %get-tuple-element.83), channel_id=1, source_target_pairs={{0,4},{4,0},{8,12},{12,8},{1,5},{5,1},{9,13},{13,9},{2,6},{6,2},{1... | collective-permute-start | bytes 49160 | tf_op jit(solution)/shard_map/ppermute | solution.py:477
  82.5 2.3 %means.1 = bf16[8,512,256]{2,1,0:T(8,128)(2,1)} custom-call(s32[2,4]{1,0:T(2,128)} %bitcast.21, bf16[4,512,256]{2,1,0:T(8,128)(2,1)S(1)} %get-tuple-element.45.rows_ref, bf16[4,512,256]{2,1,0:T(8,128)(2,1)S(1)} %get-tuple-element.84.kernel_ref, f32[4,512,128]{2,1,0:T(8,128)S(1)} %get-tuple-element.85.mass_ref, ...), custom_call_target="tpu_custom_call", output_to_operand_aliasing={{}: (8, {})} | custom-call | flops 536870912 | bytes 8388608 | tf_op jit(solution)/shard_map/means/pallas_call | solution.py:414
  84.9 0.5 collective-permute-done.20.refs_3_
  85.4 0.6 weights.1
  (22 shorter events, 0.5 us)
Async XLA Ops:
  0.6 5.9 %collective-permute-start.2 = (s32[2,4]{1,0:T(2,128)}, s32[2,4]{1,0:T(2,128)S(1)}, u32[]{:S(2)}, u32[]{:S(2)}) collective-permute-start(s32[2,4]{1,0:T(2,128)} %bitcast.13), channel_id=1, source_target_pairs={{0,8},{4,12},{8,0},{12,4},{1,9},{5,13},{9,1},{13,5},{2,10},{6,14},... | collective-permute-start | bytes 104 | tf_op jit(solution)/shard_map/ppermute | solution.py:477
  4.7 5.6 %collective-permute-start.1 = (s32[2,4]{1,0:T(2,128)}, s32[2,4]{1,0:T(2,128)S(1)}, u32[]{:S(2)}, u32[]{:S(2)}) collective-permute-start(s32[2,4]{1,0:T(2,128)} %bitcast.14), channel_id=1, source_target_pairs={{0,12},{4,8},{8,4},{12,0},{1,13},{5,9},{9,5},{13,1},{2,14},{6,10},... | collective-permute-start | bytes 104 | tf_op jit(solution)/shard_map/ppermute | solution.py:477
  6.1 4.2 %collective-permute-start = (s32[2,4]{1,0:T(2,128)}, s32[2,4]{1,0:T(2,128)S(1)}, u32[]{:S(2)}, u32[]{:S(2)}) collective-permute-start(s32[2,4]{1,0:T(2,128)} %bitcast.15), channel_id=1, source_target_pairs={{0,4},{4,0},{8,12},{12,8},{1,5},{5,1},{9,13},{13,9},{2,6},{6,2},{1... | collective-permute-start | bytes 104 | tf_op jit(solution)/shard_map/ppermute | solution.py:477
  13.3 23.5 %collective-permute-start.3 = (bf16[4,512,256]{2,1,0:T(8,128)(2,1)S(1)}, bf16[4,512,256]{2,1,0:T(8,128)(2,1)S(1)}, u32[]{:S(2)}, u32[]{:S(2)}) collective-permute-start(bf16[4,512,256]{2,1,0:T(8,128)(2,1)S(1)} %get-tuple-element.45.rows_ref), channel_id=1, source_target_pairs={{0,2},{1,3},{2,0},{3,1},{4,6},{5,7},{6,4},{7,5},{8,10},{9,11},{10,... | collective-permute-start | bytes 3145736 | tf_op jit(solution)/shard_map/ppermute | solution.py:462
  14.8 25.9 %collective-permute-start.4 = (bf16[2,336,256]{2,1,0:T(8,128)(2,1)S(1)}, bf16[2,336,256]{2,1,0:T(8,128)(2,1)S(1)}, u32[]{:S(2)}, u32[]{:S(2)}) collective-permute-start(bf16[2,336,256]{2,1,0:T(8,128)(2,1)S(1)} %get-tuple-element.46), channel_id=1, source_target_pairs={{0,12},{4,8},{8,4},{12,0},{1,13},{5,9},{9,5},{13,1},{2,14},{6,10},... | collective-permute-start | bytes 1032200 | tf_op jit(solution)/shard_map/ppermute | solution.py:477
  16.6 27.4 %collective-permute-start.5 = (bf16[2,336,256]{2,1,0:T(8,128)(2,1)S(1)}, bf16[2,336,256]{2,1,0:T(8,128)(2,1)S(1)}, u32[]{:S(2)}, u32[]{:S(2)}) collective-permute-start(bf16[2,336,256]{2,1,0:T(8,128)(2,1)S(1)} %get-tuple-element.47), channel_id=1, source_target_pairs={{0,8},{4,12},{8,0},{12,4},{1,9},{5,13},{9,1},{13,5},{2,10},{6,14},... | collective-permute-start | bytes 1032200 | tf_op jit(solution)/shard_map/ppermute | solution.py:477
  16.6 27.4 %collective-permute-start.6 = (bf16[2,336,256]{2,1,0:T(8,128)(2,1)S(1)}, bf16[2,336,256]{2,1,0:T(8,128)(2,1)S(1)}, u32[]{:S(2)}, u32[]{:S(2)}) collective-permute-start(bf16[2,336,256]{2,1,0:T(8,128)(2,1)S(1)} %get-tuple-element.48), channel_id=1, source_target_pairs={{0,4},{4,0},{8,12},{12,8},{1,5},{5,1},{9,13},{13,9},{2,6},{6,2},{1... | collective-permute-start | bytes 1032200 | tf_op jit(solution)/shard_map/ppermute | solution.py:477
  19.2 21.5 %collective-permute-start.7 = (bf16[2,176,256]{2,1,0:T(8,128)(2,1)S(1)}, bf16[2,176,256]{2,1,0:T(8,128)(2,1)S(1)}, u32[]{:S(2)}, u32[]{:S(2)}) collective-permute-start(bf16[2,176,256]{2,1,0:T(8,128)(2,1)S(1)} %get-tuple-element.49), channel_id=1, source_target_pairs={{0,4},{4,0},{8,12},{12,8},{1,5},{5,1},{9,13},{13,9},{2,6},{6,2},{1... | collective-permute-start | bytes 540680 | tf_op jit(solution)/shard_map/ppermute | solution.py:477
  44.0 19.0 %collective-permute-start.9 = (bf16[2,4,512,256]{3,2,1,0:T(8,128)(2,1)S(1)}, bf16[2,4,512,256]{3,2,1,0:T(8,128)(2,1)S(1)}, u32[]{:S(2)}, u32[]{:S(2)}) collective-permute-start(bf16[2,4,512,256]{3,2,1,0:T(8,128)(2,1)S(1)} %pad_maximum_fusion.refs_0_), channel_id=1, source_target_pairs={{0,1},{1,0},{2,3},{3,2},{4,5},{5,4},{6,7},{7,6},{8,9},{9,8},{10,11... | collective-permute-start | bytes 6291464 | tf_op jit(solution)/shard_map/ppermute | solution.py:462
  44.9 18.1 %collective-permute-start.8 = (bf16[4,336,256]{2,1,0:T(8,128)(2,1)S(1)}, bf16[4,336,256]{2,1,0:T(8,128)(2,1)S(1)}, u32[]{:S(2)}, u32[]{:S(2)}) collective-permute-start(bf16[4,336,256]{2,1,0:T(8,128)(2,1)S(1)} %get-tuple-element.58), channel_id=1, source_target_pairs={{0,2},{1,3},{2,0},{3,1},{4,6},{5,7},{6,4},{7,5},{8,10},{9,11},{10,... | collective-permute-start | bytes 2064392 | tf_op jit(solution)/shard_map/ppermute | solution.py:462
  45.5 9.3 %collective-permute-start.10 = (bf16[2,176,256]{2,1,0:T(8,128)(2,1)S(1)}, bf16[2,176,256]{2,1,0:T(8,128)(2,1)S(1)}, u32[]{:S(2)}, u32[]{:S(2)}) collective-permute-start(bf16[2,176,256]{2,1,0:T(8,128)(2,1)S(1)} %get-tuple-element.60), channel_id=1, source_target_pairs={{0,12},{4,8},{8,4},{12,0},{1,13},{5,9},{9,5},{13,1},{2,14},{6,10},... | collective-permute-start | bytes 540680 | tf_op jit(solution)/shard_map/ppermute | solution.py:477
  48.1 14.9 %collective-permute-start.11 = (bf16[2,176,256]{2,1,0:T(8,128)(2,1)S(1)}, bf16[2,176,256]{2,1,0:T(8,128)(2,1)S(1)}, u32[]{:S(2)}, u32[]{:S(2)}) collective-permute-start(bf16[2,176,256]{2,1,0:T(8,128)(2,1)S(1)} %get-tuple-element.61), channel_id=1, source_target_pairs={{0,8},{4,12},{8,0},{12,4},{1,9},{5,13},{9,1},{13,5},{2,10},{6,14},... | collective-permute-start | bytes 540680 | tf_op jit(solution)/shard_map/ppermute | solution.py:477
  48.1 17.9 %collective-permute-start.12 = (bf16[2,336,256]{2,1,0:T(8,128)(2,1)S(1)}, bf16[2,336,256]{2,1,0:T(8,128)(2,1)S(1)}, u32[]{:S(2)}, u32[]{:S(2)}) collective-permute-start(bf16[2,336,256]{2,1,0:T(8,128)(2,1)S(1)} %get-tuple-element.64.refs_2_.refs_0_), channel_id=1, source_target_pairs={{0,1},{1,0},{2,3},{3,2},{4,5},{5,4},{6,7},{7,6},{8,9},{9,8},{10,11... | collective-permute-start | bytes 1032200 | tf_op jit(solution)/shard_map/ppermute | solution.py:462
  54.8 11.3 %collective-permute-start.13 = (bf16[2,336,256]{2,1,0:T(8,128)(2,1)S(1)}, bf16[2,336,256]{2,1,0:T(8,128)(2,1)S(1)}, u32[]{:S(2)}, u32[]{:S(2)}) collective-permute-start(bf16[2,336,256]{2,1,0:T(8,128)(2,1)S(1)} %get-tuple-element.65.refs_3_.refs_1_), channel_id=1, source_target_pairs={{0,1},{1,0},{2,3},{3,2},{4,5},{5,4},{6,7},{7,6},{8,9},{9,8},{10,11... | collective-permute-start | bytes 1032200 | tf_op jit(solution)/shard_map/ppermute | solution.py:462
  63.8 9.9 %collective-permute-start.16 = (bf16[4,176,256]{2,1,0:T(8,128)(2,1)S(1)}, bf16[4,176,256]{2,1,0:T(8,128)(2,1)S(1)}, u32[]{:S(2)}, u32[]{:S(2)}) collective-permute-start(bf16[4,176,256]{2,1,0:T(8,128)(2,1)S(1)} %select.3.refs_9_.refs_2_), channel_id=1, source_target_pairs={{0,2},{1,3},{2,0},{3,1},{4,6},{5,7},{6,4},{7,5},{8,10},{9,11},{10,... | collective-permute-start | bytes 1081352 | tf_op jit(solution)/shard_map/ppermute | solution.py:462
  65.4 1.7 %collective-permute-start.15 = (bf16[2,336,256]{2,1,0:T(8,128)(2,1)S(1)}, bf16[2,336,256]{2,1,0:T(8,128)(2,1)S(1)}, u32[]{:S(2)}, u32[]{:S(2)}) collective-permute-start(bf16[2,336,256]{2,1,0:T(8,128)(2,1)S(1)} %get-tuple-element.88), channel_id=1, source_target_pairs={{0,1},{1,0},{2,3},{3,2},{4,5},{5,4},{6,7},{7,6},{8,9},{9,8},{10,11... | collective-permute-start | bytes 1032200 | tf_op jit(solution)/shard_map/ppermute | solution.py:462
  65.5 2.1 %collective-permute-start.14 = (bf16[2,336,256]{2,1,0:T(8,128)(2,1)S(1)}, bf16[2,336,256]{2,1,0:T(8,128)(2,1)S(1)}, u32[]{:S(2)}, u32[]{:S(2)}) collective-permute-start(bf16[2,336,256]{2,1,0:T(8,128)(2,1)S(1)} %get-tuple-element.89), channel_id=1, source_target_pairs={{0,1},{1,0},{2,3},{3,2},{4,5},{5,4},{6,7},{7,6},{8,9},{9,8},{10,11... | collective-permute-start | bytes 1032200 | tf_op jit(solution)/shard_map/ppermute | solution.py:462
  66.0 7.7 %collective-permute-start.17 = (bf16[4,176,256]{2,1,0:T(8,128)(2,1)S(1)}, bf16[4,176,256]{2,1,0:T(8,128)(2,1)S(1)}, u32[]{:S(2)}, u32[]{:S(2)}) collective-permute-start(bf16[4,176,256]{2,1,0:T(8,128)(2,1)S(1)} %select.3.refs_9_.refs_2_), channel_id=1, source_target_pairs={{0,1},{1,0},{2,3},{3,2},{4,5},{5,4},{6,7},{7,6},{8,9},{9,8},{10,11... | collective-permute-start | bytes 1081352 | tf_op jit(solution)/shard_map/ppermute | solution.py:462
  73.7 1.7 %collective-permute-start.18 = (bf16[4,176,256]{2,1,0:T(8,128)(2,1)S(1)}, bf16[4,176,256]{2,1,0:T(8,128)(2,1)S(1)}, u32[]{:S(2)}, u32[]{:S(2)}) collective-permute-start(bf16[4,176,256]{2,1,0:T(8,128)(2,1)S(1)} %collective-permute-done.16.refs_10_), channel_id=1, source_target_pairs={{0,1},{1,0},{2,3},{3,2},{4,5},{5,4},{6,7},{7,6},{8,9},{9,8},{10,11... | collective-permute-start | bytes 1081352 | tf_op jit(solution)/shard_map/ppermute | solution.py:462
  78.0 6.8 %collective-permute-start.19 = (f32[8,512]{1,0:T(8,128)S(1)}, f32[8,512]{1,0:T(8,128)S(1)}, u32[]{:S(2)}, u32[]{:S(2)}) collective-permute-start(f32[8,512]{1,0:T(8,128)S(1)} %get-tuple-element.81), channel_id=1, source_target_pairs={{0,12},{4,8},{8,4},{12,0},{1,13},{5,9},{9,5},{13,1},{2,14},{6,10},... | collective-permute-start | bytes 49160 | tf_op jit(solution)/shard_map/ppermute | solution.py:477
  80.8 4.6 %collective-permute-start.20 = (f32[8,512]{1,0:T(8,128)S(1)}, f32[8,512]{1,0:T(8,128)S(1)}, u32[]{:S(2)}, u32[]{:S(2)}) collective-permute-start(f32[8,512]{1,0:T(8,128)S(1)} %get-tuple-element.82), channel_id=1, source_target_pairs={{0,8},{4,12},{8,0},{12,4},{1,9},{5,13},{9,1},{13,5},{2,10},{6,14},... | collective-permute-start | bytes 49160 | tf_op jit(solution)/shard_map/ppermute | solution.py:477
  80.8 4.6 %collective-permute-start.21 = (f32[8,512]{1,0:T(8,128)S(1)}, f32[8,512]{1,0:T(8,128)S(1)}, u32[]{:S(2)}, u32[]{:S(2)}) collective-permute-start(f32[8,512]{1,0:T(8,128)S(1)} %get-tuple-element.83), channel_id=1, source_target_pairs={{0,4},{4,0},{8,12},{12,8},{1,5},{5,1},{9,13},{13,9},{2,6},{6,2},{1... | collective-permute-start | bytes 49160 | tf_op jit(solution)/shard_map/ppermute | solution.py:477

commit v18 on v17

--- a/solution.py
+++ b/solution.py
@@ -76,6 +76,10 @@
 def list_order(wide_count):
     middle = wide_count // 2
     return [other for other in range(1, wide_count) if other != middle] + [middle]
+
+
+def sum_order(wide_count):
+    return list_order(wide_count)[::-1]
 
 
 def pack(me, pairs, lists, blocks, capacity):
@@ -254,7 +258,7 @@
         row_ref[pl.ds(pairs_ref[0, pair] & 7, 1)] += jnp.sum(mass.T, axis=0, keepdims=True)
         col = pairs_ref[1, pair]
         apart = (col >> 3) ^ me_ref[0]
-        for other, ref in zip([*others(wide_count), 0], shares):
+        for other, ref in zip([*sum_order(wide_count), 0], shares):
             ref[pl.ds(col & 7, 1)] += jnp.where(apart == other, sums, 0.0)
 
 
@@ -517,7 +521,7 @@
     kernel, mass, row_sums, shares = last_window(
         me, pairs, rows, [cols_a, cols_b], square, mass, sums, wide_count
     )
-    came = to_wide(shares[:-1], apart)
+    came = to_wide(shares[:-1], sum_order(wide_count))
     mean = means(pairs, row_slices, kernel, mass, total, [cols_a, cols_b], kept)
     weights = block_weights([row_sums, shares[-1], *came])
     return weights, mean.reshape(BLK_DEV * BR, feat)

time: 86.4 us -> 85.5 us (0.990)
  starting transfers between devices: 21.6 us -> 20.6 us
    ppermute x12, starting transfers between devices: 17.2 us -> 16.3 us  [to_wide(): lax.ppermute(piece, 'wide', [(i, i ^ other) for i in range(count)])]
  transfers between devices with their start and end apart: 22 -> 22, of which waited for: 12 -> 13; matrix products, arithmetic and copies ran while one was open for 0% -> 0% of each run, Pallas kernels for 15% -> 15%
where the time goes in v18:
time: 85.5 us; the launch traced here: 85.2 us
  waiting for transfers between devices  44 us (51%)
  starting transfers between devices  20.6 us (24%)
  Pallas kernels  19.6 us (23%)
    ppermute x12, waiting for transfers between devices, to_wide(): lax.ppermute(piece, 'wide', [(i, i ^ other) for i in range(count)])  26.2 us
    ppermute x10, waiting for transfers between devices, hop(): lax.ppermute(piece, 'narrow', perm)  17.7 us
    ppermute x12, starting transfers between devices, to_wide(): lax.ppermute(piece, 'wide', [(i, i ^ other) for i in range(count)])  16.3 us
    pallas_call x1, Pallas kernels, keep(): pl.pallas_call(keep_kernel, out_shape=[pltpu.HBM(blocks.shape, blocks.dty...  6.02 us
    ppermute x10, starting transfers between devices, hop(): lax.ppermute(piece, 'narrow', perm)  4.37 us
    pallas_call x1, Pallas kernels, pack(): pl.pallas_call(functools.partial(pack_kernel, wide_count, pair_count, cap...  3.24 us
    pallas_call x1, Pallas kernels, first_window(): pl.pallas_call(functools.partial(first_kernel, window, piece_counts(windo...  3.1 us
    pallas_call x1, Pallas kernels, last_window(): pl.pallas_call(functools.partial(last_kernel, window, piece_counts(window...  2.64 us
  transfers between devices with their start and end apart: 22, of which 13 were waited for; matrix products, arithmetic and copies ran while one was open for 0% of the time, Pallas kernels for 15%

profile of v18, /device:TPU:0, one launch (start us, length us, event | category | flops | bytes accessed | tf_op | source)
XLA Modules:
  0.0 85.2 jit_solution(10808052448742760708)
XLA Ops:
  0.6 4.1 %collective-permute-start.2 = (s32[2,4]{1,0:T(2,128)}, s32[2,4]{1,0:T(2,128)S(1)}, u32[]{:S(2)}, u32[]{:S(2)}) collective-permute-start(s32[2,4]{1,0:T(2,128)} %bitcast.13), channel_id=1, source_target_pairs={{0,8},{4,12},{8,0},{12,4},{1,9},{5,13},{9,1},{13,5},{2,10},{6,14},... | collective-permute-start | bytes 104 | tf_op jit(solution)/shard_map/ppermute | solution.py:481
  4.7 1.3 %collective-permute-start.1 = (s32[2,4]{1,0:T(2,128)}, s32[2,4]{1,0:T(2,128)S(1)}, u32[]{:S(2)}, u32[]{:S(2)}) collective-permute-start(s32[2,4]{1,0:T(2,128)} %bitcast.14), channel_id=1, source_target_pairs={{0,12},{4,8},{8,4},{12,0},{1,13},{5,9},{9,5},{13,1},{2,14},{6,10},... | collective-permute-start | bytes 104 | tf_op jit(solution)/shard_map/ppermute | solution.py:481
  6.1 0.2 collective-permute-start
  6.5 3.8 %collective-permute-done.1.refs_1_ = s32[2,4]{1,0:T(2,128)S(1)} collective-permute-done((s32[2,4]{1,0:T(2,128)}, s32[2,4]{1,0:T(2,128)S(1)}, u32[]{:S(2)}, u32[]{:S(2)}) %collective-permute-start.1) | collective-permute-done | bytes 64 | tf_op jit(solution)/shard_map/ppermute | solution.py:481
  10.3 3.2 %pack.1 = (bf16[2,336,256]{2,1,0:T(8,128)(2,1)S(1)}, bf16[2,336,256]{2,1,0:T(8,128)(2,1)S(1)}, bf16[2,336,256]{2,1,0:T(8,128)(2,1)S(1)}, bf16[2,176,256]{2,1,0:T...) custom-call(s32[1]{0:T(128)} %bitcast.me_ref, ...), custom_call_target="tpu_custom_call" | custom-call | tf_op jit(solution)/shard_map/pack/pallas_call | solution.py:94
  13.6 1.6 %collective-permute-start.3 = (bf16[4,512,256]{2,1,0:T(8,128)(2,1)S(1)}, bf16[4,512,256]{2,1,0:T(8,128)(2,1)S(1)}, u32[]{:S(2)}, u32[]{:S(2)}) collective-permute-start(bf16[4,512,256]{2,1,0:T(8,128)(2,1)S(1)} %get-tuple-element.45.rows_ref), channel_id=1, source_target_pairs={{0,2},{1,3},{2,0},{3,1},{4,6},{5,7},{6,4},{7,5},{8,10},{9,11},{10,... | collective-permute-start | bytes 3145736 | tf_op jit(solution)/shard_map/ppermute | solution.py:466
  15.1 1.5 %collective-permute-start.4 = (bf16[2,336,256]{2,1,0:T(8,128)(2,1)S(1)}, bf16[2,336,256]{2,1,0:T(8,128)(2,1)S(1)}, u32[]{:S(2)}, u32[]{:S(2)}) collective-permute-start(bf16[2,336,256]{2,1,0:T(8,128)(2,1)S(1)} %get-tuple-element.46), channel_id=1, source_target_pairs={{0,12},{4,8},{8,4},{12,0},{1,13},{5,9},{9,5},{13,1},{2,14},{6,10},... | collective-permute-start | bytes 1032200 | tf_op jit(solution)/shard_map/ppermute | solution.py:481
  16.6 2.9 %collective-permute-start.6 = (bf16[2,336,256]{2,1,0:T(8,128)(2,1)S(1)}, bf16[2,336,256]{2,1,0:T(8,128)(2,1)S(1)}, u32[]{:S(2)}, u32[]{:S(2)}) collective-permute-start(bf16[2,336,256]{2,1,0:T(8,128)(2,1)S(1)} %get-tuple-element.48), channel_id=1, source_target_pairs={{0,4},{4,0},{8,12},{12,8},{1,5},{5,1},{9,13},{13,9},{2,6},{6,2},{1... | collective-permute-start | bytes 1032200 | tf_op jit(solution)/shard_map/ppermute | solution.py:481
  19.5 6.0 %keep.1 = (bf16[8,512,256]{2,1,0:T(8,128)(2,1)}, bf16[4,512,256]{2,1,0:T(8,128)(2,1)S(1)}) custom-call(s32[2,4]{1,0:T(2,128)} %bitcast.17, bf16[8,512,256]{2,1,0:T(8,128)(2,1)} %bitcast.9, bf16[8,512,256]{2,1,0:T(8,128)(2,1)} %bitcast.10), custom_call_target="tpu_custom_call" | custom-call | tf_op jit(solution)/shard_map/keep/pallas_call | solution.py:349
  25.6 11.5 %collective-permute-done.3 = bf16[4,512,256]{2,1,0:T(8,128)(2,1)S(1)} collective-permute-done((bf16[4,512,256]{2,1,0:T(8,128)(2,1)S(1)}, bf16[4,512,256]{2,1,0:T(8,128)(2,1)S(1)}, u32[]{:S(2)}, u32[]{:S(2)}) %collective-permute-start.3) | collective-permute-done | bytes 1048608 | tf_op jit(solution)/shard_map/ppermute | solution.py:466
  37.3 3.4 %collective-permute-done.7.refs_2_ = bf16[2,176,256]{2,1,0:T(8,128)(2,1)S(1)} collective-permute-done((bf16[2,176,256]{2,1,0:T(8,128)(2,1)S(1)}, bf16[2,176,256]{2,1,0:T(8,128)(2,1)S(1)}, u32[]{:S(2)}, u32[]{:S(2)}) %collective-permute-start.7) | collective-permute-done | bytes 180256 | tf_op jit(solution)/shard_map/ppermute | solution.py:481
  40.7 3.3 %collective-permute-done.5.refs_1_ = bf16[2,336,256]{2,1,0:T(8,128)(2,1)S(1)} collective-permute-done((bf16[2,336,256]{2,1,0:T(8,128)(2,1)S(1)}, bf16[2,336,256]{2,1,0:T(8,128)(2,1)S(1)}, u32[]{:S(2)}, u32[]{:S(2)}) %collective-permute-start.5) | collective-permute-done | bytes 344096 | tf_op jit(solution)/shard_map/ppermute | solution.py:481
  44.0 0.9 %select.2 = (bf16[2,336,256]{2,1,0:T(8,128)(2,1)S(1)}, bf16[2,336,256]{2,1,0:T(8,128)(2,1)S(1)}, bf16[4,336,256]{2,1,0:T(8,128)(2,1)S(1)}) custom-call(s32[1]{0:T(128)} %bitcast.me_ref, s32[2,4]{1,0:T(2,128)} %bitcast.18, bf16[4,512,256]{2,1,0:T(8,128)(2,1)S(1)} %get-tuple-element.52.own_ref, bf16[2,336,256]{2,1,0:T(8,128)(2,1)S(1)} %collective-permute-done.4.refs_0_, ...), custom_call_target="tpu_custom_call" | custom-call | tf_op jit(solution)/shard_map/select/pallas_call | solution.py:144
  44.9 0.6 collective-permute-start.8
  45.5 2.6 %collective-permute-start.10 = (bf16[2,176,256]{2,1,0:T(8,128)(2,1)S(1)}, bf16[2,176,256]{2,1,0:T(8,128)(2,1)S(1)}, u32[]{:S(2)}, u32[]{:S(2)}) collective-permute-start(bf16[2,176,256]{2,1,0:T(8,128)(2,1)S(1)} %get-tuple-element.60), channel_id=1, source_target_pairs={{0,12},{4,8},{8,4},{12,0},{1,13},{5,9},{9,5},{13,1},{2,14},{6,10},... | collective-permute-start | bytes 540680 | tf_op jit(solution)/shard_map/ppermute | solution.py:481
  48.1 6.7 %collective-permute-done.10.refs_0_ = bf16[2,176,256]{2,1,0:T(8,128)(2,1)S(1)} collective-permute-done((bf16[2,176,256]{2,1,0:T(8,128)(2,1)S(1)}, bf16[2,176,256]{2,1,0:T(8,128)(2,1)S(1)}, u32[]{:S(2)}, u32[]{:S(2)}) %collective-permute-start.10) | collective-permute-done | bytes 180256 | tf_op jit(solution)/shard_map/ppermute | solution.py:481
  54.8 8.2 %collective-permute-done.11.refs_1_ = bf16[2,176,256]{2,1,0:T(8,128)(2,1)S(1)} collective-permute-done((bf16[2,176,256]{2,1,0:T(8,128)(2,1)S(1)}, bf16[2,176,256]{2,1,0:T(8,128)(2,1)S(1)}, u32[]{:S(2)}, u32[]{:S(2)}) %collective-permute-start.11) | collective-permute-done | bytes 180256 | tf_op jit(solution)/shard_map/ppermute | solution.py:481
  63.0 0.8 select.3.refs_9_.refs_2_
  63.8 1.6 %collective-permute-start.16 = (bf16[4,176,256]{2,1,0:T(8,128)(2,1)S(1)}, bf16[4,176,256]{2,1,0:T(8,128)(2,1)S(1)}, u32[]{:S(2)}, u32[]{:S(2)}) collective-permute-start(bf16[4,176,256]{2,1,0:T(8,128)(2,1)S(1)} %select.3.refs_9_.refs_2_), channel_id=1, source_target_pairs={{0,2},{1,3},{2,0},{3,1},{4,6},{5,7},{6,4},{7,5},{8,10},{9,11},{10,... | collective-permute-start | bytes 1081352 | tf_op jit(solution)/shard_map/ppermute | solution.py:466
  65.5 0.5 collective-permute-start.14
  66.1 1.1 %collective-permute-done.15.refs_8_ = bf16[2,336,256]{2,1,0:T(8,128)(2,1)S(1)} collective-permute-done((bf16[2,336,256]{2,1,0:T(8,128)(2,1)S(1)}, bf16[2,336,256]{2,1,0:T(8,128)(2,1)S(1)}, u32[]{:S(2)}, u32[]{:S(2)}) %collective-permute-start.15) | collective-permute-done | bytes 344096 | tf_op jit(solution)/shard_map/ppermute | solution.py:466
  67.1 0.5 collective-permute-done.14.refs_7_
  67.6 3.1 %first_window.1 = (f32[4,512,128]{2,1,0:T(8,128)S(1)}, f32[4,512,128]{2,1,0:T(8,128)S(1)}, f32[4,512,256]{2,1,0:T(8,128)S(1)}, f32[4,256]{1,0:T(4,128)S(1)}) custom-call(bf16[2,4,512,256]{3,2,1,0:T(8,128)(2,1)S(1)} %pad_maximum_fusion.refs_0_, bf16[2,4,512,256]{3,2,1,0:T(8,128)(2,1)S(1)} %collective-permute-done.9.refs_1_, ...), custom_call_target="tpu_custom_call" | custom-call | tf_op jit(solution)/shard_map/first_window/pallas_call | solution.py:289
  70.7 3.0 %collective-permute-done.16.refs_10_ = bf16[4,176,256]{2,1,0:T(8,128)(2,1)S(1)} collective-permute-done((bf16[4,176,256]{2,1,0:T(8,128)(2,1)S(1)}, bf16[4,176,256]{2,1,0:T(8,128)(2,1)S(1)}, u32[]{:S(2)}, u32[]{:S(2)}) %collective-permute-start.16) | collective-permute-done | bytes 360480 | tf_op jit(solution)/shard_map/ppermute | solution.py:466
  73.7 1.7 %collective-permute-done.18.refs_12_ = bf16[4,176,256]{2,1,0:T(8,128)(2,1)S(1)} collective-permute-done((bf16[4,176,256]{2,1,0:T(8,128)(2,1)S(1)}, bf16[4,176,256]{2,1,0:T(8,128)(2,1)S(1)}, u32[]{:S(2)}, u32[]{:S(2)}) %collective-permute-start.18) | collective-permute-done | bytes 360480 | tf_op jit(solution)/shard_map/ppermute | solution.py:466
  75.4 2.6 %last_window.1 = (bf16[4,512,256]{2,1,0:T(8,128)(2,1)S(1)}, f32[4,512,128]{2,1,0:T(8,128)S(1)}, f32[8,512]{1,0:T(8,128)S(1)}, f32[8,512]{1,0:T(8,128)S(1)}, f32[...) custom-call(s32[1]{0:T(128)} %bitcast.me_ref, s32[2,4]{1,0:T(2,128)} %bitcast.20, ...), custom_call_target="tpu_custom_call" | custom-call | flops 1073741824 | bytes 8388608 | tf_op jit(solution)/shard_map/last_window/pallas_call | solution.py:313
  78.0 0.4 collective-permute-start.19
  78.4 2.4 %collective-permute-start.20 = (f32[8,512]{1,0:T(8,128)S(1)}, f32[8,512]{1,0:T(8,128)S(1)}, u32[]{:S(2)}, u32[]{:S(2)}) collective-permute-start(f32[8,512]{1,0:T(8,128)S(1)} %get-tuple-element.82), channel_id=1, source_target_pairs={{0,12},{4,8},{8,4},{12,0},{1,13},{5,9},{9,5},{13,1},{2,14},{6,10},... | collective-permute-start | bytes 49160 | tf_op jit(solution)/shard_map/ppermute | solution.py:481
  80.8 0.8 collective-permute-start.21
  81.6 2.3 %means.1 = bf16[8,512,256]{2,1,0:T(8,128)(2,1)} custom-call(s32[2,4]{1,0:T(2,128)} %bitcast.21, bf16[4,512,256]{2,1,0:T(8,128)(2,1)S(1)} %get-tuple-element.45.rows_ref, bf16[4,512,256]{2,1,0:T(8,128)(2,1)S(1)} %get-tuple-element.84.kernel_ref, f32[4,512,128]{2,1,0:T(8,128)S(1)} %get-tuple-element.85.mass_ref, ...), custom_call_target="tpu_custom_call", output_to_operand_aliasing={{}: (8, {})} | custom-call | flops 536870912 | bytes 8388608 | tf_op jit(solution)/shard_map/means/pallas_call | solution.py:418
  84.0 0.6 collective-permute-done.21.refs_4_
  84.5 0.6 weights.1
  (22 shorter events, 0.7 us)
Async XLA Ops:
  0.6 5.9 %collective-permute-start.2 = (s32[2,4]{1,0:T(2,128)}, s32[2,4]{1,0:T(2,128)S(1)}, u32[]{:S(2)}, u32[]{:S(2)}) collective-permute-start(s32[2,4]{1,0:T(2,128)} %bitcast.13), channel_id=1, source_target_pairs={{0,8},{4,12},{8,0},{12,4},{1,9},{5,13},{9,1},{13,5},{2,10},{6,14},... | collective-permute-start | bytes 104 | tf_op jit(solution)/shard_map/ppermute | solution.py:481
  4.7 5.6 %collective-permute-start.1 = (s32[2,4]{1,0:T(2,128)}, s32[2,4]{1,0:T(2,128)S(1)}, u32[]{:S(2)}, u32[]{:S(2)}) collective-permute-start(s32[2,4]{1,0:T(2,128)} %bitcast.14), channel_id=1, source_target_pairs={{0,12},{4,8},{8,4},{12,0},{1,13},{5,9},{9,5},{13,1},{2,14},{6,10},... | collective-permute-start | bytes 104 | tf_op jit(solution)/shard_map/ppermute | solution.py:481
  6.1 4.2 %collective-permute-start = (s32[2,4]{1,0:T(2,128)}, s32[2,4]{1,0:T(2,128)S(1)}, u32[]{:S(2)}, u32[]{:S(2)}) collective-permute-start(s32[2,4]{1,0:T(2,128)} %bitcast.15), channel_id=1, source_target_pairs={{0,4},{4,0},{8,12},{12,8},{1,5},{5,1},{9,13},{13,9},{2,6},{6,2},{1... | collective-permute-start | bytes 104 | tf_op jit(solution)/shard_map/ppermute | solution.py:481
  13.6 23.5 %collective-permute-start.3 = (bf16[4,512,256]{2,1,0:T(8,128)(2,1)S(1)}, bf16[4,512,256]{2,1,0:T(8,128)(2,1)S(1)}, u32[]{:S(2)}, u32[]{:S(2)}) collective-permute-start(bf16[4,512,256]{2,1,0:T(8,128)(2,1)S(1)} %get-tuple-element.45.rows_ref), channel_id=1, source_target_pairs={{0,2},{1,3},{2,0},{3,1},{4,6},{5,7},{6,4},{7,5},{8,10},{9,11},{10,... | collective-permute-start | bytes 3145736 | tf_op jit(solution)/shard_map/ppermute | solution.py:466
  15.1 25.6 %collective-permute-start.4 = (bf16[2,336,256]{2,1,0:T(8,128)(2,1)S(1)}, bf16[2,336,256]{2,1,0:T(8,128)(2,1)S(1)}, u32[]{:S(2)}, u32[]{:S(2)}) collective-permute-start(bf16[2,336,256]{2,1,0:T(8,128)(2,1)S(1)} %get-tuple-element.46), channel_id=1, source_target_pairs={{0,12},{4,8},{8,4},{12,0},{1,13},{5,9},{9,5},{13,1},{2,14},{6,10},... | collective-permute-start | bytes 1032200 | tf_op jit(solution)/shard_map/ppermute | solution.py:481
  16.6 27.4 %collective-permute-start.5 = (bf16[2,336,256]{2,1,0:T(8,128)(2,1)S(1)}, bf16[2,336,256]{2,1,0:T(8,128)(2,1)S(1)}, u32[]{:S(2)}, u32[]{:S(2)}) collective-permute-start(bf16[2,336,256]{2,1,0:T(8,128)(2,1)S(1)} %get-tuple-element.47), channel_id=1, source_target_pairs={{0,8},{4,12},{8,0},{12,4},{1,9},{5,13},{9,1},{13,5},{2,10},{6,14},... | collective-permute-start | bytes 1032200 | tf_op jit(solution)/shard_map/ppermute | solution.py:481
  16.6 27.4 %collective-permute-start.6 = (bf16[2,336,256]{2,1,0:T(8,128)(2,1)S(1)}, bf16[2,336,256]{2,1,0:T(8,128)(2,1)S(1)}, u32[]{:S(2)}, u32[]{:S(2)}) collective-permute-start(bf16[2,336,256]{2,1,0:T(8,128)(2,1)S(1)} %get-tuple-element.48), channel_id=1, source_target_pairs={{0,4},{4,0},{8,12},{12,8},{1,5},{5,1},{9,13},{13,9},{2,6},{6,2},{1... | collective-permute-start | bytes 1032200 | tf_op jit(solution)/shard_map/ppermute | solution.py:481
  19.5 21.2 %collective-permute-start.7 = (bf16[2,176,256]{2,1,0:T(8,128)(2,1)S(1)}, bf16[2,176,256]{2,1,0:T(8,128)(2,1)S(1)}, u32[]{:S(2)}, u32[]{:S(2)}) collective-permute-start(bf16[2,176,256]{2,1,0:T(8,128)(2,1)S(1)} %get-tuple-element.49), channel_id=1, source_target_pairs={{0,4},{4,0},{8,12},{12,8},{1,5},{5,1},{9,13},{13,9},{2,6},{6,2},{1... | collective-permute-start | bytes 540680 | tf_op jit(solution)/shard_map/ppermute | solution.py:481
  44.0 19.0 %collective-permute-start.9 = (bf16[2,4,512,256]{3,2,1,0:T(8,128)(2,1)S(1)}, bf16[2,4,512,256]{3,2,1,0:T(8,128)(2,1)S(1)}, u32[]{:S(2)}, u32[]{:S(2)}) collective-permute-start(bf16[2,4,512,256]{3,2,1,0:T(8,128)(2,1)S(1)} %pad_maximum_fusion.refs_0_), channel_id=1, source_target_pairs={{0,1},{1,0},{2,3},{3,2},{4,5},{5,4},{6,7},{7,6},{8,9},{9,8},{10,11... | collective-permute-start | bytes 6291464 | tf_op jit(solution)/shard_map/ppermute | solution.py:466
  44.9 18.1 %collective-permute-start.8 = (bf16[4,336,256]{2,1,0:T(8,128)(2,1)S(1)}, bf16[4,336,256]{2,1,0:T(8,128)(2,1)S(1)}, u32[]{:S(2)}, u32[]{:S(2)}) collective-permute-start(bf16[4,336,256]{2,1,0:T(8,128)(2,1)S(1)} %get-tuple-element.58), channel_id=1, source_target_pairs={{0,2},{1,3},{2,0},{3,1},{4,6},{5,7},{6,4},{7,5},{8,10},{9,11},{10,... | collective-permute-start | bytes 2064392 | tf_op jit(solution)/shard_map/ppermute | solution.py:466
  45.5 9.3 %collective-permute-start.10 = (bf16[2,176,256]{2,1,0:T(8,128)(2,1)S(1)}, bf16[2,176,256]{2,1,0:T(8,128)(2,1)S(1)}, u32[]{:S(2)}, u32[]{:S(2)}) collective-permute-start(bf16[2,176,256]{2,1,0:T(8,128)(2,1)S(1)} %get-tuple-element.60), channel_id=1, source_target_pairs={{0,12},{4,8},{8,4},{12,0},{1,13},{5,9},{9,5},{13,1},{2,14},{6,10},... | collective-permute-start | bytes 540680 | tf_op jit(solution)/shard_map/ppermute | solution.py:481
  48.1 14.9 %collective-permute-start.11 = (bf16[2,176,256]{2,1,0:T(8,128)(2,1)S(1)}, bf16[2,176,256]{2,1,0:T(8,128)(2,1)S(1)}, u32[]{:S(2)}, u32[]{:S(2)}) collective-permute-start(bf16[2,176,256]{2,1,0:T(8,128)(2,1)S(1)} %get-tuple-element.61), channel_id=1, source_target_pairs={{0,8},{4,12},{8,0},{12,4},{1,9},{5,13},{9,1},{13,5},{2,10},{6,14},... | collective-permute-start | bytes 540680 | tf_op jit(solution)/shard_map/ppermute | solution.py:481
  48.1 17.9 %collective-permute-start.12 = (bf16[2,336,256]{2,1,0:T(8,128)(2,1)S(1)}, bf16[2,336,256]{2,1,0:T(8,128)(2,1)S(1)}, u32[]{:S(2)}, u32[]{:S(2)}) collective-permute-start(bf16[2,336,256]{2,1,0:T(8,128)(2,1)S(1)} %get-tuple-element.64.refs_2_.refs_0_), channel_id=1, source_target_pairs={{0,1},{1,0},{2,3},{3,2},{4,5},{5,4},{6,7},{7,6},{8,9},{9,8},{10,11... | collective-permute-start | bytes 1032200 | tf_op jit(solution)/shard_map/ppermute | solution.py:466
  54.8 11.3 %collective-permute-start.13 = (bf16[2,336,256]{2,1,0:T(8,128)(2,1)S(1)}, bf16[2,336,256]{2,1,0:T(8,128)(2,1)S(1)}, u32[]{:S(2)}, u32[]{:S(2)}) collective-permute-start(bf16[2,336,256]{2,1,0:T(8,128)(2,1)S(1)} %get-tuple-element.65.refs_3_.refs_1_), channel_id=1, source_target_pairs={{0,1},{1,0},{2,3},{3,2},{4,5},{5,4},{6,7},{7,6},{8,9},{9,8},{10,11... | collective-permute-start | bytes 1032200 | tf_op jit(solution)/shard_map/ppermute | solution.py:466
  63.8 9.9 %collective-permute-start.16 = (bf16[4,176,256]{2,1,0:T(8,128)(2,1)S(1)}, bf16[4,176,256]{2,1,0:T(8,128)(2,1)S(1)}, u32[]{:S(2)}, u32[]{:S(2)}) collective-permute-start(bf16[4,176,256]{2,1,0:T(8,128)(2,1)S(1)} %select.3.refs_9_.refs_2_), channel_id=1, source_target_pairs={{0,2},{1,3},{2,0},{3,1},{4,6},{5,7},{6,4},{7,5},{8,10},{9,11},{10,... | collective-permute-start | bytes 1081352 | tf_op jit(solution)/shard_map/ppermute | solution.py:466
  65.4 1.7 %collective-permute-start.15 = (bf16[2,336,256]{2,1,0:T(8,128)(2,1)S(1)}, bf16[2,336,256]{2,1,0:T(8,128)(2,1)S(1)}, u32[]{:S(2)}, u32[]{:S(2)}) collective-permute-start(bf16[2,336,256]{2,1,0:T(8,128)(2,1)S(1)} %get-tuple-element.88), channel_id=1, source_target_pairs={{0,1},{1,0},{2,3},{3,2},{4,5},{5,4},{6,7},{7,6},{8,9},{9,8},{10,11... | collective-permute-start | bytes 1032200 | tf_op jit(solution)/shard_map/ppermute | solution.py:466
  65.5 2.1 %collective-permute-start.14 = (bf16[2,336,256]{2,1,0:T(8,128)(2,1)S(1)}, bf16[2,336,256]{2,1,0:T(8,128)(2,1)S(1)}, u32[]{:S(2)}, u32[]{:S(2)}) collective-permute-start(bf16[2,336,256]{2,1,0:T(8,128)(2,1)S(1)} %get-tuple-element.89), channel_id=1, source_target_pairs={{0,1},{1,0},{2,3},{3,2},{4,5},{5,4},{6,7},{7,6},{8,9},{9,8},{10,11... | collective-permute-start | bytes 1032200 | tf_op jit(solution)/shard_map/ppermute | solution.py:466
  66.0 7.7 %collective-permute-start.17 = (bf16[4,176,256]{2,1,0:T(8,128)(2,1)S(1)}, bf16[4,176,256]{2,1,0:T(8,128)(2,1)S(1)}, u32[]{:S(2)}, u32[]{:S(2)}) collective-permute-start(bf16[4,176,256]{2,1,0:T(8,128)(2,1)S(1)} %select.3.refs_9_.refs_2_), channel_id=1, source_target_pairs={{0,1},{1,0},{2,3},{3,2},{4,5},{5,4},{6,7},{7,6},{8,9},{9,8},{10,11... | collective-permute-start | bytes 1081352 | tf_op jit(solution)/shard_map/ppermute | solution.py:466
  73.7 1.7 %collective-permute-start.18 = (bf16[4,176,256]{2,1,0:T(8,128)(2,1)S(1)}, bf16[4,176,256]{2,1,0:T(8,128)(2,1)S(1)}, u32[]{:S(2)}, u32[]{:S(2)}) collective-permute-start(bf16[4,176,256]{2,1,0:T(8,128)(2,1)S(1)} %collective-permute-done.16.refs_10_), channel_id=1, source_target_pairs={{0,1},{1,0},{2,3},{3,2},{4,5},{5,4},{6,7},{7,6},{8,9},{9,8},{10,11... | collective-permute-start | bytes 1081352 | tf_op jit(solution)/shard_map/ppermute | solution.py:466
  78.0 5.9 %collective-permute-start.19 = (f32[8,512]{1,0:T(8,128)S(1)}, f32[8,512]{1,0:T(8,128)S(1)}, u32[]{:S(2)}, u32[]{:S(2)}) collective-permute-start(f32[8,512]{1,0:T(8,128)S(1)} %get-tuple-element.81), channel_id=1, source_target_pairs={{0,8},{4,12},{8,0},{12,4},{1,9},{5,13},{9,1},{13,5},{2,10},{6,14},... | collective-permute-start | bytes 49160 | tf_op jit(solution)/shard_map/ppermute | solution.py:481
  78.4 5.5 %collective-permute-start.20 = (f32[8,512]{1,0:T(8,128)S(1)}, f32[8,512]{1,0:T(8,128)S(1)}, u32[]{:S(2)}, u32[]{:S(2)}) collective-permute-start(f32[8,512]{1,0:T(8,128)S(1)} %get-tuple-element.82), channel_id=1, source_target_pairs={{0,12},{4,8},{8,4},{12,0},{1,13},{5,9},{9,5},{13,1},{2,14},{6,10},... | collective-permute-start | bytes 49160 | tf_op jit(solution)/shard_map/ppermute | solution.py:481
  80.8 3.7 %collective-permute-start.21 = (f32[8,512]{1,0:T(8,128)S(1)}, f32[8,512]{1,0:T(8,128)S(1)}, u32[]{:S(2)}, u32[]{:S(2)}) collective-permute-start(f32[8,512]{1,0:T(8,128)S(1)} %get-tuple-element.83), channel_id=1, source_target_pairs={{0,4},{4,0},{8,12},{12,8},{1,5},{5,1},{9,13},{13,9},{2,6},{6,2},{1... | collective-permute-start | bytes 49160 | tf_op jit(solution)/shard_map/ppermute | solution.py:481

commit v19 on v18

--- a/solution.py
+++ b/solution.py
@@ -67,10 +67,27 @@
             out = outs[chunk * (wide_count - 1) + number]
             for slot in range(capacity):
                 send(blocks_ref.at[picks[slot], pl.ds(start, size)], out.at[slot])
-    for pair in range(pair_count):
-        send(blocks_ref.at[pairs_ref[0, pair] & 7], rows_ref.at[pair])
+    for place, pair in enumerate(in_order(wide_count, me_ref, pairs_ref)):
+        send(blocks_ref.at[pairs_ref[0, pair] & 7], rows_ref.at[place])
     for copy in copies:
         copy.wait()
+
+
+def in_order(wide_count, me_ref, pairs_ref):
+    pair_count = pairs_ref.shape[1]
+    far = [
+        ((pairs_ref[1, pair] >> 3) ^ me_ref[0] == wide_count // 2).astype(jnp.int32)
+        for pair in range(pair_count)
+    ]
+    place_near, place_far = jnp.int32(0), pair_count - sum(far)
+    places = []
+    for is_far in far:
+        places.append(jnp.where(is_far == 1, place_far, place_near))
+        place_near, place_far = place_near + 1 - is_far, place_far + is_far
+    return [
+        sum(jnp.where(at == place, pair, 0) for pair, at in enumerate(places))
+        for place in range(pair_count)
+    ]
 
 
 def list_order(wide_count):
@@ -104,52 +121,60 @@
     return [outs[c * each : (c + 1) * each] for c in range(len(CHUNKS))], outs[-1]
 
 
-def select_kernel(wide_count, groups, start, me_ref, pairs_ref, own_ref, *refs):
+def select_kernel(wide_count, apart, groups, first, start, me_ref, pairs_ref, own_ref, *refs):
+    received, outs = refs[: len(apart)], refs[len(apart) :]
     pair_count = own_ref.shape[0]
-    outs = refs[wide_count - 1 :]
-    received = refs[: wide_count - 1]
     size = outs[0].shape[1]
+    count = sum(ref.shape[0] for ref in outs[: groups[0]])
     owners = [pairs_ref[1, pair] >> 3 for pair in range(pair_count)]
-    for pair in range(pair_count):
-        apart = me_ref[0] ^ owners[pair]
+    order = in_order(wide_count, me_ref, pairs_ref)
+    for place in range(first, first + count):
+        pair = order[place]
+        owner = pairs_ref[1, pair] >> 3
+        away = me_ref[0] ^ owner
         rank = jnp.int32(0)
-        for before in range(pair):
-            rank = rank + (owners[before] == owners[pair]).astype(jnp.int32)
-
-        places, rest = [], outs
+        for before in range(pair_count):
+            rank = rank + ((before < pair) & (owners[before] == owner)).astype(jnp.int32)
+        targets, rest = [], outs
         for pieces in groups:
-            places.append(of_pair(rest[:pieces], pair))
+            targets.append(of_pair(rest[:pieces], place - first))
             rest = rest[pieces:]
 
-        @pl.when(apart == 0)
+        @pl.when(away == 0)
         def _():
-            for out in places:
-                out[...] = own_ref[pair, start : start + size]
-
-        for number, other in enumerate(others(wide_count)):
-
-            @pl.when(apart == other)
+            for out in targets:
+                out[...] = own_ref[place, start : start + size]
+
+        for number, other in enumerate(apart):
+
+            @pl.when(away == other)
             def _():
-                for out in places:
+                for out in targets:
                     out[...] = received[number][rank]
 
 
-def select(me, pairs, own, received, start, size, groups):
-    pair_count, _, feat = own.shape
+def select(me, pairs, own, received, apart, wide_count, places, start, size, groups):
+    _, _, feat = own.shape
+    first, count = places
     shapes = [
-        pltpu.VMEM((pair_count // pieces, size, feat), own.dtype)
+        pltpu.VMEM((count // pieces, size, feat), own.dtype)
         for pieces in groups
         for _ in range(pieces)
     ]
     outs = pl.pallas_call(
-        functools.partial(select_kernel, len(received) + 1, groups, start),
+        functools.partial(select_kernel, wide_count, apart, groups, first, start),
         out_shape=shapes,
         in_specs=[smem(), smem()] + [vmem()] * (1 + len(received)),
         out_specs=[vmem()] * len(shapes),
         compiler_params=params(4),
+        cost_estimate=nothing(),
         name="select",
     )(me, in_hbm(pairs), *[in_vmem(x) for x in (own, *received)])
     return take_parts(outs, groups)[0]
+
+
+def nothing():
+    return pl.CostEstimate(flops=0, transcendentals=0, bytes_accessed=0)
 
 
 def tree(parts):
@@ -248,13 +273,14 @@
     for ref in (row_ref, *shares):
         ref[...] = jnp.zeros_like(ref)
     all_rows, chunks = window_parts(counts, refs)
-    for pair in range(square_in.shape[0]):
-        rows, cols = pair_parts(window, all_rows, chunks, pair)
-        kernel, sums, mass = scores(rows, cols, square_in[pair])
-        kernel_ref[pair] = kernel
-        sums = jnp.concatenate([sums_in[pair : pair + 1], sums], axis=1)
-        mass = mass_in[pair] + mass
-        mass_ref[pair] = mass
+    order = in_order(wide_count, me_ref, pairs_ref)
+    for place, pair in enumerate(order):
+        rows, cols = pair_parts(window, all_rows, chunks, place)
+        kernel, sums, mass = scores(rows, cols, square_in[place])
+        kernel_ref[place] = kernel
+        sums = jnp.concatenate([sums_in[place : place + 1], sums], axis=1)
+        mass = mass_in[place] + mass
+        mass_ref[place] = mass
         row_ref[pl.ds(pairs_ref[0, pair] & 7, 1)] += jnp.sum(mass.T, axis=0, keepdims=True)
         col = pairs_ref[1, pair]
         apart = (col >> 3) ^ me_ref[0]
@@ -322,13 +348,13 @@
     return kernel, mass, row_sums, shares
 
 
-def keep_kernel(pairs_ref, block_ref, blocks_ref, out_ref, own_ref, sems):
+def keep_kernel(wide_count, me_ref, pairs_ref, block_ref, blocks_ref, out_ref, own_ref, sems):
     here = pl.program_id(0)
 
     def copies():
-        for pair in range(own_ref.shape[0]):
+        for place, pair in enumerate(in_order(wide_count, me_ref, pairs_ref)):
             source = blocks_ref.at[pairs_ref[1, pair] & 7]
-            yield pltpu.make_async_copy(source, own_ref.at[pair], sems.at[pair])
+            yield pltpu.make_async_copy(source, own_ref.at[place], sems.at[place])
 
     @pl.when(here == 0)
     def _():
@@ -343,32 +369,32 @@
             copy.wait()
 
 
-def keep(pairs, blocks):
+def keep(me, pairs, blocks, wide_count):
     pair_count = pairs.shape[1]
     block = pl.BlockSpec((1, *blocks.shape[1:]), lambda k: (k, 0, 0))
     return pl.pallas_call(
-        keep_kernel,
+        functools.partial(keep_kernel, wide_count),
         out_shape=[
             pltpu.HBM(blocks.shape, blocks.dtype),
             pltpu.VMEM((pair_count, *blocks.shape[1:]), blocks.dtype),
         ],
         grid=(blocks.shape[0],),
-        in_specs=[smem(), block, anywhere()],
+        in_specs=[smem(), smem(), block, anywhere()],
         out_specs=[block, anywhere()],
         scratch_shapes=[pltpu.SemaphoreType.DMA((pair_count,))],
         compiler_params=params(4),
         name="keep",
-    )(in_hbm(pairs), in_hbm(blocks), in_hbm(blocks))
-
-
-def mean_kernel(window, counts, local_ref, rows_ref, kernel_ref, mass_ref, total_ref, *refs):
+    )(me, in_hbm(pairs), in_hbm(blocks), in_hbm(blocks))
+
+
+def mean_kernel(window, counts, wide_count, me_ref, local_ref, rows_ref, kernel_ref, mass_ref, total_ref, *refs):
     *refs, _, out_ref, part, weight, total, mass, made, sems = refs
     chunks = []
     for chunk, _, _ in segments(window):
         (own,), refs = take_parts(refs, counts[len(chunks)][:1])
         chunks.append(own)
     pair_count, _, feat = rows_ref.shape
-    local = [local_ref[0, pair] & 7 for pair in range(pair_count)]
+    local = [local_ref[0, pair] & 7 for pair in in_order(wide_count, me_ref, local_ref)]
 
     def copy(pair):
         return pltpu.make_async_copy(made.at[pair], out_ref.at[local[pair]], sems.at[pair])
@@ -410,15 +436,15 @@
             copy(pair).wait()
 
 
-def means(pairs, rows, kernel, mass, total, cols, kept):
+def means(me, wide_count, pairs, rows, kernel, mass, total, cols, kept):
     pair_count, _, feat = rows.shape
     window = WINDOWS[1]
     own = operands(cols[chunk][0] for chunk, _, _ in segments(window))
     args = [in_vmem(x) for x in (rows, kernel, mass, total, *own)]
     return pl.pallas_call(
-        functools.partial(mean_kernel, window, piece_counts(window, cols)),
+        functools.partial(mean_kernel, window, piece_counts(window, cols), wide_count),
         out_shape=pltpu.HBM(kept.shape, jnp.bfloat16),
-        in_specs=[smem()] + [vmem()] * len(args) + [anywhere()],
+        in_specs=[smem(), smem()] + [vmem()] * len(args) + [anywhere()],
         out_specs=anywhere(),
         scratch_shapes=[
             pltpu.VMEM((pair_count, BR, feat), jnp.bfloat16),
@@ -428,11 +454,11 @@
             pltpu.VMEM((pair_count, BR, feat), jnp.bfloat16),
             pltpu.SemaphoreType.DMA((pair_count,)),
         ],
-        input_output_aliases={1 + len(args): 0},
+        input_output_aliases={2 + len(args): 0},
         compiler_params=params(16),
         cost_estimate=estimate(pair_count, 128),
         name="means",
-    )(in_hbm(pairs), *args, in_hbm(kept))
+    )(me, in_hbm(pairs), *args, in_hbm(kept))
 
 
 def weight_kernel(*refs):
@@ -496,33 +522,39 @@
     fixed = lax.optimization_barrier
     outgoing, row_slices = pack(me, pairs, lists, blocks, capacity)
 
-    def pick(received, chunk, *groups):
-        return select(me, pairs, own, received, *CHUNKS[chunk], groups)
+    def pick(received, apart, chunk, places, *groups):
+        start, size = CHUNKS[chunk]
+        return select(me, pairs, own, received, tuple(apart), wide_count, places, start, size, groups)
 
     def halves(part):
         middle = pair_count // 2
         return [part[0][:middle], part[0][middle:]]
 
+    half, middle = pair_count // 2, wide_count // 2
     rows = jnp.stack([part[0] for part in first_hops([row_slices])])
     received = to_wide(outgoing[0], apart)
     near = to_wide(outgoing[1][-1:], apart[-1:])
-    rows, received, near, (kept, own) = fixed((rows, received, near, keep(pairs, blocks)))
-    own_a, whole_a = pick(received, 0, 2, 1)
+    rows, received, near, (kept, own) = fixed((rows, received, near, keep(me, pairs, blocks, wide_count)))
+    own_a, whole_a = pick(received, apart, 0, (0, pair_count), 2, 1)
     cols_a = [own_a] + first_hops(whole_a)[1:]
     rows = [[rows], *hop([[rows]], 1)]
-    cols_a, rows, received = fixed((cols_a, rows, to_wide(outgoing[1][:-1], apart[:-1])))
-    cols_b = first_hops(*pick([*received, *near], 1, 1))
-    last_b = hop(cols_b[:1], 1)
+    came = dict(zip(apart, to_wide(outgoing[1][:-1], apart[:-1]) + near))
+    early = {other: piece for other, piece in came.items() if other != middle}
+    cols_b = first_hops(*pick(list(early.values()), early, 1, (0, half), 1))
+    cols_a, rows, cols_b, came = fixed((cols_a, rows, cols_b, came))
+    late_b, cols_a = fixed((pick(list(came.values()), came, 1, (half, half), 1), cols_a))
+    late_b = first_hops(*late_b)
     cols_a = cols_a + hop([own_a] + [halves(part) for part in cols_a[1:]], 1)
     carry = first_window(rows, [cols_a])
-    cols_b, carry = fixed((cols_b, carry))
-    cols_b = cols_b + last_b + hop(cols_b[1:], 1)
+    late_b, carry = fixed((late_b, carry))
+    cols_b = [early + late for early, late in zip(cols_b, late_b)]
+    cols_b = cols_b + hop(cols_b, 1)
     square, mass, total, sums = carry
     kernel, mass, row_sums, shares = last_window(
         me, pairs, rows, [cols_a, cols_b], square, mass, sums, wide_count
     )
     came = to_wide(shares[:-1], sum_order(wide_count))
-    mean = means(pairs, row_slices, kernel, mass, total, [cols_a, cols_b], kept)
+    mean = means(me, wide_count, pairs, row_slices, kernel, mass, total, [cols_a, cols_b], kept)
     weights = block_weights([row_sums, shares[-1], *came])
     return weights, mean.reshape(BLK_DEV * BR, feat)
 

time: 85.5 us -> 86.5 us (1.012)
  starting transfers between devices: 20.6 us -> 22.1 us
  waiting for transfers between devices: 44 us -> 42.9 us
    ppermute x12, waiting for transfers between devices: 26.2 us -> 24.3 us  [to_wide(): lax.ppermute(piece, 'wide', [(i, i ^ other) for i in range(count)])]
    ppermute x10 -> x13, starting transfers between devices: 4.37 us -> 5.84 us  [hop(): lax.ppermute(piece, 'narrow', perm)]
    pallas_call x3 -> x4, Pallas kernels: 7.68 us -> 8.59 us  [the longest x1 6.14 us: keep(): pl.pallas_call(functools.partial(keep_kernel, wide_count), out_shape=[plt...]
    ppermute x10 -> x13, waiting for transfers between devices: 17.7 us -> 18.6 us  [hop(): lax.ppermute(piece, 'narrow', perm)]
  transfers between devices with their start and end apart: 22 -> 25, of which waited for: 13 -> 14; matrix products, arithmetic and copies ran while one was open for 0% -> 0% of each run, Pallas kernels for 15% -> 16%
where the time goes in v19:
time: 86.5 us; the launch traced here: 86.1 us
  waiting for transfers between devices  42.9 us (50%)
  starting transfers between devices  22.1 us (26%)
  Pallas kernels  20.1 us (23%)
    ppermute x12, waiting for transfers between devices, to_wide(): lax.ppermute(piece, 'wide', [(i, i ^ other) for i in range(count)])  24.3 us
    ppermute x13, waiting for transfers between devices, hop(): lax.ppermute(piece, 'narrow', perm)  18.6 us
    ppermute x12, starting transfers between devices, to_wide(): lax.ppermute(piece, 'wide', [(i, i ^ other) for i in range(count)])  16.3 us
    pallas_call x1, Pallas kernels, keep(): pl.pallas_call(functools.partial(keep_kernel, wide_count), out_shape=[plt...  6.14 us
    ppermute x13, starting transfers between devices, hop(): lax.ppermute(piece, 'narrow', perm)  5.84 us
    pallas_call x1, Pallas kernels, first_window(): pl.pallas_call(functools.partial(first_kernel, window, piece_counts(windo...  3.1 us
    pallas_call x1, Pallas kernels, pack(): pl.pallas_call(functools.partial(pack_kernel, wide_count, pair_count, cap...  2.72 us
    pallas_call x1, Pallas kernels, last_window(): pl.pallas_call(functools.partial(last_kernel, window, piece_counts(window...  2.64 us
  transfers between devices with their start and end apart: 25, of which 14 were waited for; matrix products, arithmetic and copies ran while one was open for 0% of the time, Pallas kernels for 16%

profile of v19, /device:TPU:0, one launch (start us, length us, event | category | flops | bytes accessed | tf_op | source)
XLA Modules:
  0.0 86.1 jit_solution(12552069479746835919)
XLA Ops:
  0.6 4.1 %collective-permute-start.2 = (s32[2,4]{1,0:T(2,128)}, s32[2,4]{1,0:T(2,128)S(1)}, u32[]{:S(2)}, u32[]{:S(2)}) collective-permute-start(s32[2,4]{1,0:T(2,128)} %bitcast.13), channel_id=1, source_target_pairs={{0,8},{4,12},{8,0},{12,4},{1,9},{5,13},{9,1},{13,5},{2,10},{6,14},... | collective-permute-start | bytes 104 | tf_op jit(solution)/shard_map/ppermute | solution.py:507
  4.7 1.3 %collective-permute-start.1 = (s32[2,4]{1,0:T(2,128)}, s32[2,4]{1,0:T(2,128)S(1)}, u32[]{:S(2)}, u32[]{:S(2)}) collective-permute-start(s32[2,4]{1,0:T(2,128)} %bitcast.14), channel_id=1, source_target_pairs={{0,12},{4,8},{8,4},{12,0},{1,13},{5,9},{9,5},{13,1},{2,14},{6,10},... | collective-permute-start | bytes 104 | tf_op jit(solution)/shard_map/ppermute | solution.py:507
  6.5 3.8 %collective-permute-done.1.refs_1_ = s32[2,4]{1,0:T(2,128)S(1)} collective-permute-done((s32[2,4]{1,0:T(2,128)}, s32[2,4]{1,0:T(2,128)S(1)}, u32[]{:S(2)}, u32[]{:S(2)}) %collective-permute-start.1) | collective-permute-done | bytes 64 | tf_op jit(solution)/shard_map/ppermute | solution.py:507
  10.3 2.7 %pack.1 = (bf16[2,336,256]{2,1,0:T(8,128)(2,1)S(1)}, bf16[2,336,256]{2,1,0:T(8,128)(2,1)S(1)}, bf16[2,336,256]{2,1,0:T(8,128)(2,1)S(1)}, bf16[2,176,256]{2,1,0:T...) custom-call(s32[1]{0:T(128)} %bitcast.me_ref, ...), custom_call_target="tpu_custom_call" | custom-call | tf_op jit(solution)/shard_map/pack/pallas_call | solution.py:111
  13.0 1.6 %collective-permute-start.3 = (bf16[4,512,256]{2,1,0:T(8,128)(2,1)S(1)}, bf16[4,512,256]{2,1,0:T(8,128)(2,1)S(1)}, u32[]{:S(2)}, u32[]{:S(2)}) collective-permute-start(bf16[4,512,256]{2,1,0:T(8,128)(2,1)S(1)} %get-tuple-element.52.rows_ref), channel_id=1, source_target_pairs={{0,2},{1,3},{2,0},{3,1},{4,6},{5,7},{6,4},{7,5},{8,10},{9,11},{10,... | collective-permute-start | bytes 3145736 | tf_op jit(solution)/shard_map/ppermute | solution.py:492
  14.6 2.3 %collective-permute-start.4 = (bf16[2,336,256]{2,1,0:T(8,128)(2,1)S(1)}, bf16[2,336,256]{2,1,0:T(8,128)(2,1)S(1)}, u32[]{:S(2)}, u32[]{:S(2)}) collective-permute-start(bf16[2,336,256]{2,1,0:T(8,128)(2,1)S(1)} %get-tuple-element.53), channel_id=1, source_target_pairs={{0,12},{4,8},{8,4},{12,0},{1,13},{5,9},{9,5},{13,1},{2,14},{6,10},... | collective-permute-start | bytes 1032200 | tf_op jit(solution)/shard_map/ppermute | solution.py:507
  16.9 2.1 %collective-permute-start.6 = (bf16[2,336,256]{2,1,0:T(8,128)(2,1)S(1)}, bf16[2,336,256]{2,1,0:T(8,128)(2,1)S(1)}, u32[]{:S(2)}, u32[]{:S(2)}) collective-permute-start(bf16[2,336,256]{2,1,0:T(8,128)(2,1)S(1)} %get-tuple-element.55), channel_id=1, source_target_pairs={{0,4},{4,0},{8,12},{12,8},{1,5},{5,1},{9,13},{13,9},{2,6},{6,2},{1... | collective-permute-start | bytes 1032200 | tf_op jit(solution)/shard_map/ppermute | solution.py:507
  19.0 6.1 %keep.1 = (bf16[8,512,256]{2,1,0:T(8,128)(2,1)}, bf16[4,512,256]{2,1,0:T(8,128)(2,1)S(1)}) custom-call(s32[1]{0:T(128)} %bitcast.me_ref, s32[2,4]{1,0:T(2,128)} %bitcast.17, bf16[8,512,256]{2,1,0:T(8,128)(2,1)} %bitcast.9, bf16[8,512,256]{2,1,0:T(8,128)(2,1)} %bitcast.10), custom_call_target="tpu_custom_call" | custom-call | tf_op jit(solution)/shard_map/keep/pallas_call | solution.py:375
  25.2 11.4 %collective-permute-done.3 = bf16[4,512,256]{2,1,0:T(8,128)(2,1)S(1)} collective-permute-done((bf16[4,512,256]{2,1,0:T(8,128)(2,1)S(1)}, bf16[4,512,256]{2,1,0:T(8,128)(2,1)S(1)}, u32[]{:S(2)}, u32[]{:S(2)}) %collective-permute-start.3) | collective-permute-done | bytes 1048608 | tf_op jit(solution)/shard_map/ppermute | solution.py:492
  36.8 4.2 %collective-permute-done.7.refs_1_.refs_0_ = bf16[2,176,256]{2,1,0:T(8,128)(2,1)S(1)} collective-permute-done((bf16[2,176,256]{2,1,0:T(8,128)(2,1)S(1)}, bf16[2,176,256]{2,1,0:T(8,128)(2,1)S(1)}, u32[]{:S(2)}, u32[]{:S(2)}) %collective-permute-start.7) | collective-permute-done | bytes 180256 | tf_op jit(solution)/shard_map/ppermute | solution.py:507
  41.0 3.0 %collective-permute-done.5.refs_1_ = bf16[2,336,256]{2,1,0:T(8,128)(2,1)S(1)} collective-permute-done((bf16[2,336,256]{2,1,0:T(8,128)(2,1)S(1)}, bf16[2,336,256]{2,1,0:T(8,128)(2,1)S(1)}, u32[]{:S(2)}, u32[]{:S(2)}) %collective-permute-start.5) | collective-permute-done | bytes 344096 | tf_op jit(solution)/shard_map/ppermute | solution.py:507
  44.0 0.9 %select.3 = (bf16[2,336,256]{2,1,0:T(8,128)(2,1)S(1)}, bf16[2,336,256]{2,1,0:T(8,128)(2,1)S(1)}, bf16[4,336,256]{2,1,0:T(8,128)(2,1)S(1)}) custom-call(s32[1]{0:T(128)} %bitcast.me_ref, s32[2,4]{1,0:T(2,128)} %bitcast.18, bf16[4,512,256]{2,1,0:T(8,128)(2,1)S(1)} %get-tuple-element.59.own_ref, bf16[2,336,256]{2,1,0:T(8,128)(2,1)S(1)} %collective-permute-done.4.refs_0_, ...), custom_call_target="tpu_custom_call" | custom-call | tf_op jit(solution)/shard_map/select/pallas_call | solution.py:164
  44.9 0.6 collective-permute-start.8
  45.5 2.6 %collective-permute-start.10 = (bf16[2,176,256]{2,1,0:T(8,128)(2,1)S(1)}, bf16[2,176,256]{2,1,0:T(8,128)(2,1)S(1)}, u32[]{:S(2)}, u32[]{:S(2)}) collective-permute-start(bf16[2,176,256]{2,1,0:T(8,128)(2,1)S(1)} %get-tuple-element.67), channel_id=1, source_target_pairs={{0,12},{4,8},{8,4},{12,0},{1,13},{5,9},{9,5},{13,1},{2,14},{6,10},... | collective-permute-start | bytes 540680 | tf_op jit(solution)/shard_map/ppermute | solution.py:507
  48.1 6.7 %collective-permute-done.10.refs_0_.refs_2_ = bf16[2,176,256]{2,1,0:T(8,128)(2,1)S(1)} collective-permute-done((bf16[2,176,256]{2,1,0:T(8,128)(2,1)S(1)}, bf16[2,176,256]{2,1,0:T(8,128)(2,1)S(1)}, u32[]{:S(2)}, u32[]{:S(2)}) %collective-permute-start.10) | collective-permute-done | bytes 180256 | tf_op jit(solution)/shard_map/ppermute | solution.py:507
  54.8 0.8 select.4.refs_9_.refs_2_
  55.6 1.6 %collective-permute-start.11 = (bf16[2,176,256]{2,1,0:T(8,128)(2,1)S(1)}, bf16[2,176,256]{2,1,0:T(8,128)(2,1)S(1)}, u32[]{:S(2)}, u32[]{:S(2)}) collective-permute-start(bf16[2,176,256]{2,1,0:T(8,128)(2,1)S(1)} %select.4.refs_9_.refs_2_), channel_id=1, source_target_pairs={{0,2},{1,3},{2,0},{3,1},{4,6},{5,7},{6,4},{7,5},{8,10},{9,11},{10,... | collective-permute-start | bytes 540680 | tf_op jit(solution)/shard_map/ppermute | solution.py:492
  57.1 5.9 %collective-permute-done.12.refs_1_ = bf16[2,176,256]{2,1,0:T(8,128)(2,1)S(1)} collective-permute-done((bf16[2,176,256]{2,1,0:T(8,128)(2,1)S(1)}, bf16[2,176,256]{2,1,0:T(8,128)(2,1)S(1)}, u32[]{:S(2)}, u32[]{:S(2)}) %collective-permute-start.12) | collective-permute-done | bytes 180256 | tf_op jit(solution)/shard_map/ppermute | solution.py:507
  63.0 3.7 %collective-permute-done.11.refs_11_ = bf16[2,176,256]{2,1,0:T(8,128)(2,1)S(1)} collective-permute-done((bf16[2,176,256]{2,1,0:T(8,128)(2,1)S(1)}, bf16[2,176,256]{2,1,0:T(8,128)(2,1)S(1)}, u32[]{:S(2)}, u32[]{:S(2)}) %collective-permute-start.11) | collective-permute-done | bytes 180256 | tf_op jit(solution)/shard_map/ppermute | solution.py:492
  66.7 0.8 select.5.refs_10_.refs_3_
  68.1 0.5 collective-permute-start.17
  68.7 0.5 collective-permute-start.18
  69.8 3.1 %first_window.1 = (f32[4,512,128]{2,1,0:T(8,128)S(1)}, f32[4,512,128]{2,1,0:T(8,128)S(1)}, f32[4,512,256]{2,1,0:T(8,128)S(1)}, f32[4,256]{1,0:T(4,128)S(1)}) custom-call(bf16[2,4,512,256]{3,2,1,0:T(8,128)(2,1)S(1)} %pad_maximum_fusion.refs_0_, bf16[2,4,512,256]{3,2,1,0:T(8,128)(2,1)S(1)} %collective-permute-done.9.refs_1_, ...), custom_call_target="tpu_custom_call" | custom-call | tf_op jit(solution)/shard_map/first_window/pallas_call | solution.py:315
  72.9 1.8 %collective-permute-done.17.refs_12_ = bf16[2,176,256]{2,1,0:T(8,128)(2,1)S(1)} collective-permute-done((bf16[2,176,256]{2,1,0:T(8,128)(2,1)S(1)}, bf16[2,176,256]{2,1,0:T(8,128)(2,1)S(1)}, u32[]{:S(2)}, u32[]{:S(2)}) %collective-permute-start.17) | collective-permute-done | bytes 180256 | tf_op jit(solution)/shard_map/ppermute | solution.py:492
  74.7 0.5 collective-permute-start.19
  75.2 0.9 %collective-permute-done.21.refs_16_ = bf16[2,176,256]{2,1,0:T(8,128)(2,1)S(1)} collective-permute-done((bf16[2,176,256]{2,1,0:T(8,128)(2,1)S(1)}, bf16[2,176,256]{2,1,0:T(8,128)(2,1)S(1)}, u32[]{:S(2)}, u32[]{:S(2)}) %collective-permute-start.21) | collective-permute-done | bytes 180256 | tf_op jit(solution)/shard_map/ppermute | solution.py:492
  76.3 2.6 %last_window.1 = (bf16[4,512,256]{2,1,0:T(8,128)(2,1)S(1)}, f32[4,512,128]{2,1,0:T(8,128)S(1)}, f32[8,512]{1,0:T(8,128)S(1)}, f32[8,512]{1,0:T(8,128)S(1)}, f32[...) custom-call(s32[1]{0:T(128)} %bitcast.me_ref, s32[2,4]{1,0:T(2,128)} %bitcast.21, ...), custom_call_target="tpu_custom_call" | custom-call | flops 1073741824 | bytes 8388608 | tf_op jit(solution)/shard_map/last_window/pallas_call | solution.py:339
  79.1 2.7 %collective-permute-start.23 = (f32[8,512]{1,0:T(8,128)S(1)}, f32[8,512]{1,0:T(8,128)S(1)}, u32[]{:S(2)}, u32[]{:S(2)}) collective-permute-start(f32[8,512]{1,0:T(8,128)S(1)} %get-tuple-element.96), channel_id=1, source_target_pairs={{0,12},{4,8},{8,4},{12,0},{1,13},{5,9},{9,5},{13,1},{2,14},{6,10},... | collective-permute-start | bytes 49160 | tf_op jit(solution)/shard_map/ppermute | solution.py:507
  81.7 0.8 collective-permute-start.24
  82.5 2.4 %means.1 = bf16[8,512,256]{2,1,0:T(8,128)(2,1)} custom-call(s32[1]{0:T(128)} %bitcast.me_ref, s32[2,4]{1,0:T(2,128)} %bitcast.22, bf16[4,512,256]{2,1,0:T(8,128)(2,1)S(1)} %get-tuple-element.52.rows_ref, bf16[4,512,256]{2,1,0:T(8,128)(2,1)S(1)} %get-tuple-element.98.kernel_ref, ...), custom_call_target="tpu_custom_call", output_to_operand_aliasing={{}: (10, {})} | custom-call | flops 536870912 | bytes 8388608 | tf_op jit(solution)/shard_map/means/pallas_call | solution.py:444
  84.9 0.5 collective-permute-done.24.refs_4_
  85.5 0.6 weights.1
  (29 shorter events, 2.2 us)
Async XLA Ops:
  0.6 5.9 %collective-permute-start.2 = (s32[2,4]{1,0:T(2,128)}, s32[2,4]{1,0:T(2,128)S(1)}, u32[]{:S(2)}, u32[]{:S(2)}) collective-permute-start(s32[2,4]{1,0:T(2,128)} %bitcast.13), channel_id=1, source_target_pairs={{0,8},{4,12},{8,0},{12,4},{1,9},{5,13},{9,1},{13,5},{2,10},{6,14},... | collective-permute-start | bytes 104 | tf_op jit(solution)/shard_map/ppermute | solution.py:507
  4.7 5.6 %collective-permute-start.1 = (s32[2,4]{1,0:T(2,128)}, s32[2,4]{1,0:T(2,128)S(1)}, u32[]{:S(2)}, u32[]{:S(2)}) collective-permute-start(s32[2,4]{1,0:T(2,128)} %bitcast.14), channel_id=1, source_target_pairs={{0,12},{4,8},{8,4},{12,0},{1,13},{5,9},{9,5},{13,1},{2,14},{6,10},... | collective-permute-start | bytes 104 | tf_op jit(solution)/shard_map/ppermute | solution.py:507
  6.1 4.2 %collective-permute-start = (s32[2,4]{1,0:T(2,128)}, s32[2,4]{1,0:T(2,128)S(1)}, u32[]{:S(2)}, u32[]{:S(2)}) collective-permute-start(s32[2,4]{1,0:T(2,128)} %bitcast.15), channel_id=1, source_target_pairs={{0,4},{4,0},{8,12},{12,8},{1,5},{5,1},{9,13},{13,9},{2,6},{6,2},{1... | collective-permute-start | bytes 104 | tf_op jit(solution)/shard_map/ppermute | solution.py:507
  13.0 23.5 %collective-permute-start.3 = (bf16[4,512,256]{2,1,0:T(8,128)(2,1)S(1)}, bf16[4,512,256]{2,1,0:T(8,128)(2,1)S(1)}, u32[]{:S(2)}, u32[]{:S(2)}) collective-permute-start(bf16[4,512,256]{2,1,0:T(8,128)(2,1)S(1)} %get-tuple-element.52.rows_ref), channel_id=1, source_target_pairs={{0,2},{1,3},{2,0},{3,1},{4,6},{5,7},{6,4},{7,5},{8,10},{9,11},{10,... | collective-permute-start | bytes 3145736 | tf_op jit(solution)/shard_map/ppermute | solution.py:492
  14.6 26.4 %collective-permute-start.4 = (bf16[2,336,256]{2,1,0:T(8,128)(2,1)S(1)}, bf16[2,336,256]{2,1,0:T(8,128)(2,1)S(1)}, u32[]{:S(2)}, u32[]{:S(2)}) collective-permute-start(bf16[2,336,256]{2,1,0:T(8,128)(2,1)S(1)} %get-tuple-element.53), channel_id=1, source_target_pairs={{0,12},{4,8},{8,4},{12,0},{1,13},{5,9},{9,5},{13,1},{2,14},{6,10},... | collective-permute-start | bytes 1032200 | tf_op jit(solution)/shard_map/ppermute | solution.py:507
  16.9 27.1 %collective-permute-start.5 = (bf16[2,336,256]{2,1,0:T(8,128)(2,1)S(1)}, bf16[2,336,256]{2,1,0:T(8,128)(2,1)S(1)}, u32[]{:S(2)}, u32[]{:S(2)}) collective-permute-start(bf16[2,336,256]{2,1,0:T(8,128)(2,1)S(1)} %get-tuple-element.54), channel_id=1, source_target_pairs={{0,8},{4,12},{8,0},{12,4},{1,9},{5,13},{9,1},{13,5},{2,10},{6,14},... | collective-permute-start | bytes 1032200 | tf_op jit(solution)/shard_map/ppermute | solution.py:507
  16.9 27.1 %collective-permute-start.6 = (bf16[2,336,256]{2,1,0:T(8,128)(2,1)S(1)}, bf16[2,336,256]{2,1,0:T(8,128)(2,1)S(1)}, u32[]{:S(2)}, u32[]{:S(2)}) collective-permute-start(bf16[2,336,256]{2,1,0:T(8,128)(2,1)S(1)} %get-tuple-element.55), channel_id=1, source_target_pairs={{0,4},{4,0},{8,12},{12,8},{1,5},{5,1},{9,13},{13,9},{2,6},{6,2},{1... | collective-permute-start | bytes 1032200 | tf_op jit(solution)/shard_map/ppermute | solution.py:507
  19.0 22.0 %collective-permute-start.7 = (bf16[2,176,256]{2,1,0:T(8,128)(2,1)S(1)}, bf16[2,176,256]{2,1,0:T(8,128)(2,1)S(1)}, u32[]{:S(2)}, u32[]{:S(2)}) collective-permute-start(bf16[2,176,256]{2,1,0:T(8,128)(2,1)S(1)} %get-tuple-element.56), channel_id=1, source_target_pairs={{0,4},{4,0},{8,12},{12,8},{1,5},{5,1},{9,13},{13,9},{2,6},{6,2},{1... | collective-permute-start | bytes 540680 | tf_op jit(solution)/shard_map/ppermute | solution.py:507
  44.0 22.7 %collective-permute-start.9 = (bf16[2,4,512,256]{3,2,1,0:T(8,128)(2,1)S(1)}, bf16[2,4,512,256]{3,2,1,0:T(8,128)(2,1)S(1)}, u32[]{:S(2)}, u32[]{:S(2)}) collective-permute-start(bf16[2,4,512,256]{3,2,1,0:T(8,128)(2,1)S(1)} %pad_maximum_fusion.refs_0_), channel_id=1, source_target_pairs={{0,1},{1,0},{2,3},{3,2},{4,5},{5,4},{6,7},{7,6},{8,9},{9,8},{10,11... | collective-permute-start | bytes 6291464 | tf_op jit(solution)/shard_map/ppermute | solution.py:492
  44.9 21.8 %collective-permute-start.8 = (bf16[4,336,256]{2,1,0:T(8,128)(2,1)S(1)}, bf16[4,336,256]{2,1,0:T(8,128)(2,1)S(1)}, u32[]{:S(2)}, u32[]{:S(2)}) collective-permute-start(bf16[4,336,256]{2,1,0:T(8,128)(2,1)S(1)} %get-tuple-element.65), channel_id=1, source_target_pairs={{0,2},{1,3},{2,0},{3,1},{4,6},{5,7},{6,4},{7,5},{8,10},{9,11},{10,... | collective-permute-start | bytes 2064392 | tf_op jit(solution)/shard_map/ppermute | solution.py:492
  45.5 9.3 %collective-permute-start.10 = (bf16[2,176,256]{2,1,0:T(8,128)(2,1)S(1)}, bf16[2,176,256]{2,1,0:T(8,128)(2,1)S(1)}, u32[]{:S(2)}, u32[]{:S(2)}) collective-permute-start(bf16[2,176,256]{2,1,0:T(8,128)(2,1)S(1)} %get-tuple-element.67), channel_id=1, source_target_pairs={{0,12},{4,8},{8,4},{12,0},{1,13},{5,9},{9,5},{13,1},{2,14},{6,10},... | collective-permute-start | bytes 540680 | tf_op jit(solution)/shard_map/ppermute | solution.py:507
  48.1 14.9 %collective-permute-start.12 = (bf16[2,176,256]{2,1,0:T(8,128)(2,1)S(1)}, bf16[2,176,256]{2,1,0:T(8,128)(2,1)S(1)}, u32[]{:S(2)}, u32[]{:S(2)}) collective-permute-start(bf16[2,176,256]{2,1,0:T(8,128)(2,1)S(1)} %get-tuple-element.69), channel_id=1, source_target_pairs={{0,8},{4,12},{8,0},{12,4},{1,9},{5,13},{9,1},{13,5},{2,10},{6,14},... | collective-permute-start | bytes 540680 | tf_op jit(solution)/shard_map/ppermute | solution.py:507
  55.6 11.1 %collective-permute-start.11 = (bf16[2,176,256]{2,1,0:T(8,128)(2,1)S(1)}, bf16[2,176,256]{2,1,0:T(8,128)(2,1)S(1)}, u32[]{:S(2)}, u32[]{:S(2)}) collective-permute-start(bf16[2,176,256]{2,1,0:T(8,128)(2,1)S(1)} %select.4.refs_9_.refs_2_), channel_id=1, source_target_pairs={{0,2},{1,3},{2,0},{3,1},{4,6},{5,7},{6,4},{7,5},{8,10},{9,11},{10,... | collective-permute-start | bytes 540680 | tf_op jit(solution)/shard_map/ppermute | solution.py:492
  57.1 11.5 %collective-permute-start.13 = (bf16[2,336,256]{2,1,0:T(8,128)(2,1)S(1)}, bf16[2,336,256]{2,1,0:T(8,128)(2,1)S(1)}, u32[]{:S(2)}, u32[]{:S(2)}) collective-permute-start(bf16[2,336,256]{2,1,0:T(8,128)(2,1)S(1)} %get-tuple-element.78.refs_2_.refs_0_), channel_id=1, source_target_pairs={{0,1},{1,0},{2,3},{3,2},{4,5},{5,4},{6,7},{7,6},{8,9},{9,8},{10,11... | collective-permute-start | bytes 1032200 | tf_op jit(solution)/shard_map/ppermute | solution.py:492
  63.0 5.6 %collective-permute-start.14 = (bf16[2,336,256]{2,1,0:T(8,128)(2,1)S(1)}, bf16[2,336,256]{2,1,0:T(8,128)(2,1)S(1)}, u32[]{:S(2)}, u32[]{:S(2)}) collective-permute-start(bf16[2,336,256]{2,1,0:T(8,128)(2,1)S(1)} %get-tuple-element.79.refs_3_.refs_1_), channel_id=1, source_target_pairs={{0,1},{1,0},{2,3},{3,2},{4,5},{5,4},{6,7},{7,6},{8,9},{9,8},{10,11... | collective-permute-start | bytes 1032200 | tf_op jit(solution)/shard_map/ppermute | solution.py:492
  67.5 1.7 %collective-permute-start.16 = (bf16[2,336,256]{2,1,0:T(8,128)(2,1)S(1)}, bf16[2,336,256]{2,1,0:T(8,128)(2,1)S(1)}, u32[]{:S(2)}, u32[]{:S(2)}) collective-permute-start(bf16[2,336,256]{2,1,0:T(8,128)(2,1)S(1)} %get-tuple-element.102), channel_id=1, source_target_pairs={{0,1},{1,0},{2,3},{3,2},{4,5},{5,4},{6,7},{7,6},{8,9},{9,8},{10,11... | collective-permute-start | bytes 1032200 | tf_op jit(solution)/shard_map/ppermute | solution.py:492
  67.6 2.1 %collective-permute-start.15 = (bf16[2,336,256]{2,1,0:T(8,128)(2,1)S(1)}, bf16[2,336,256]{2,1,0:T(8,128)(2,1)S(1)}, u32[]{:S(2)}, u32[]{:S(2)}) collective-permute-start(bf16[2,336,256]{2,1,0:T(8,128)(2,1)S(1)} %get-tuple-element.103), channel_id=1, source_target_pairs={{0,1},{1,0},{2,3},{3,2},{4,5},{5,4},{6,7},{7,6},{8,9},{9,8},{10,11... | collective-permute-start | bytes 1032200 | tf_op jit(solution)/shard_map/ppermute | solution.py:492
  68.1 6.5 %collective-permute-start.17 = (bf16[2,176,256]{2,1,0:T(8,128)(2,1)S(1)}, bf16[2,176,256]{2,1,0:T(8,128)(2,1)S(1)}, u32[]{:S(2)}, u32[]{:S(2)}) collective-permute-start(bf16[2,176,256]{2,1,0:T(8,128)(2,1)S(1)} %select.5.refs_10_.refs_3_), channel_id=1, source_target_pairs={{0,2},{1,3},{2,0},{3,1},{4,6},{5,7},{6,4},{7,5},{8,10},{9,11},{10,... | collective-permute-start | bytes 540680 | tf_op jit(solution)/shard_map/ppermute | solution.py:492
  68.7 6.5 %collective-permute-start.20 = (bf16[2,176,256]{2,1,0:T(8,128)(2,1)S(1)}, bf16[2,176,256]{2,1,0:T(8,128)(2,1)S(1)}, u32[]{:S(2)}, u32[]{:S(2)}) collective-permute-start(bf16[2,176,256]{2,1,0:T(8,128)(2,1)S(1)} %collective-permute-done.11.refs_11_), channel_id=1, source_target_pairs={{0,1},{1,0},{2,3},{3,2},{4,5},{5,4},{6,7},{7,6},{8,9},{9,8},{10,11... | collective-permute-start | bytes 540680 | tf_op jit(solution)/shard_map/ppermute | solution.py:492
  68.7 6.5 %collective-permute-start.18 = (bf16[2,176,256]{2,1,0:T(8,128)(2,1)S(1)}, bf16[2,176,256]{2,1,0:T(8,128)(2,1)S(1)}, u32[]{:S(2)}, u32[]{:S(2)}) collective-permute-start(bf16[2,176,256]{2,1,0:T(8,128)(2,1)S(1)} %select.4.refs_9_.refs_2_), channel_id=1, source_target_pairs={{0,1},{1,0},{2,3},{3,2},{4,5},{5,4},{6,7},{7,6},{8,9},{9,8},{10,11... | collective-permute-start | bytes 540680 | tf_op jit(solution)/shard_map/ppermute | solution.py:492
  74.7 1.4 %collective-permute-start.21 = (bf16[2,176,256]{2,1,0:T(8,128)(2,1)S(1)}, bf16[2,176,256]{2,1,0:T(8,128)(2,1)S(1)}, u32[]{:S(2)}, u32[]{:S(2)}) collective-permute-start(bf16[2,176,256]{2,1,0:T(8,128)(2,1)S(1)} %collective-permute-done.17.refs_12_), channel_id=1, source_target_pairs={{0,1},{1,0},{2,3},{3,2},{4,5},{5,4},{6,7},{7,6},{8,9},{9,8},{10,11... | collective-permute-start | bytes 540680 | tf_op jit(solution)/shard_map/ppermute | solution.py:492
  74.7 1.7 %collective-permute-start.19 = (bf16[2,176,256]{2,1,0:T(8,128)(2,1)S(1)}, bf16[2,176,256]{2,1,0:T(8,128)(2,1)S(1)}, u32[]{:S(2)}, u32[]{:S(2)}) collective-permute-start(bf16[2,176,256]{2,1,0:T(8,128)(2,1)S(1)} %select.5.refs_10_.refs_3_), channel_id=1, source_target_pairs={{0,1},{1,0},{2,3},{3,2},{4,5},{5,4},{6,7},{7,6},{8,9},{9,8},{10,11... | collective-permute-start | bytes 540680 | tf_op jit(solution)/shard_map/ppermute | solution.py:492
  79.0 6.0 %collective-permute-start.22 = (f32[8,512]{1,0:T(8,128)S(1)}, f32[8,512]{1,0:T(8,128)S(1)}, u32[]{:S(2)}, u32[]{:S(2)}) collective-permute-start(f32[8,512]{1,0:T(8,128)S(1)} %get-tuple-element.95), channel_id=1, source_target_pairs={{0,8},{4,12},{8,0},{12,4},{1,9},{5,13},{9,1},{13,5},{2,10},{6,14},... | collective-permute-start | bytes 49160 | tf_op jit(solution)/shard_map/ppermute | solution.py:507
  79.1 5.9 %collective-permute-start.23 = (f32[8,512]{1,0:T(8,128)S(1)}, f32[8,512]{1,0:T(8,128)S(1)}, u32[]{:S(2)}, u32[]{:S(2)}) collective-permute-start(f32[8,512]{1,0:T(8,128)S(1)} %get-tuple-element.96), channel_id=1, source_target_pairs={{0,12},{4,8},{8,4},{12,0},{1,13},{5,9},{9,5},{13,1},{2,14},{6,10},... | collective-permute-start | bytes 49160 | tf_op jit(solution)/shard_map/ppermute | solution.py:507
  81.7 3.7 %collective-permute-start.24 = (f32[8,512]{1,0:T(8,128)S(1)}, f32[8,512]{1,0:T(8,128)S(1)}, u32[]{:S(2)}, u32[]{:S(2)}) collective-permute-start(f32[8,512]{1,0:T(8,128)S(1)} %get-tuple-element.97), channel_id=1, source_target_pairs={{0,4},{4,0},{8,12},{12,8},{1,5},{5,1},{9,13},{13,9},{2,6},{6,2},{1... | collective-permute-start | bytes 49160 | tf_op jit(solution)/shard_map/ppermute | solution.py:507

commit v20 on v19

--- a/solution.py
+++ b/solution.py
@@ -11,7 +11,7 @@
 BR = 512
 BLK_DEV = 8
 LANES = 128
-CHUNKS = ((0, 336), (336, 176))
+CHUNKS = ((0, 304), (304, 208))
 WINDOWS = ((0, 256), (256, 512))
 
 

time: 86.5 us -> 87.7 us (1.014)
  starting transfers between devices: 22.1 us -> 24.4 us
  waiting for transfers between devices: 42.9 us -> 42 us
    ppermute x13, waiting for transfers between devices: 18.6 us -> 15.2 us  [hop(): lax.ppermute(piece, 'narrow', perm)]
    ppermute x12, waiting for transfers between devices: 24.3 us -> 26.9 us  [to_wide(): lax.ppermute(piece, 'wide', [(i, i ^ other) for i in range(count)])]
    ppermute x12, starting transfers between devices: 16.3 us -> 17.5 us  [to_wide(): lax.ppermute(piece, 'wide', [(i, i ^ other) for i in range(count)])]
    ppermute x13, starting transfers between devices: 5.84 us -> 6.95 us  [hop(): lax.ppermute(piece, 'narrow', perm)]
  transfers between devices with their start and end apart: 25 -> 25, of which waited for: 14 -> 11; matrix products, arithmetic and copies ran while one was open for 0% -> 0% of each run, Pallas kernels for 16% -> 16%
where the time goes in v20:
time: 87.7 us; the launch traced here: 87.3 us
  waiting for transfers between devices  42 us (48%)
  starting transfers between devices  24.4 us (28%)
  Pallas kernels  19.9 us (23%)
    ppermute x12, waiting for transfers between devices, to_wide(): lax.ppermute(piece, 'wide', [(i, i ^ other) for i in range(count)])  26.9 us
    ppermute x12, starting transfers between devices, to_wide(): lax.ppermute(piece, 'wide', [(i, i ^ other) for i in range(count)])  17.5 us
    ppermute x13, waiting for transfers between devices, hop(): lax.ppermute(piece, 'narrow', perm)  15.2 us
    ppermute x13, starting transfers between devices, hop(): lax.ppermute(piece, 'narrow', perm)  6.95 us
    pallas_call x1, Pallas kernels, keep(): pl.pallas_call(functools.partial(keep_kernel, wide_count), out_shape=[plt...  6.14 us
    pallas_call x1, Pallas kernels, first_window(): pl.pallas_call(functools.partial(first_kernel, window, piece_counts(windo...  3.1 us
    pallas_call x1, Pallas kernels, pack(): pl.pallas_call(functools.partial(pack_kernel, wide_count, pair_count, cap...  2.73 us
    pallas_call x1, Pallas kernels, last_window(): pl.pallas_call(functools.partial(last_kernel, window, piece_counts(window...  2.63 us
  transfers between devices with their start and end apart: 25, of which 11 were waited for; matrix products, arithmetic and copies ran while one was open for 0% of the time, Pallas kernels for 16%

profile of v20, /device:TPU:0, one launch (start us, length us, event | category | flops | bytes accessed | tf_op | source)
XLA Modules:
  0.0 87.3 jit_solution(1944119889444085838)
XLA Ops:
  0.6 4.1 %collective-permute-start.2 = (s32[2,4]{1,0:T(2,128)}, s32[2,4]{1,0:T(2,128)S(1)}, u32[]{:S(2)}, u32[]{:S(2)}) collective-permute-start(s32[2,4]{1,0:T(2,128)} %bitcast.13), channel_id=1, source_target_pairs={{0,8},{4,12},{8,0},{12,4},{1,9},{5,13},{9,1},{13,5},{2,10},{6,14},... | collective-permute-start | bytes 104 | tf_op jit(solution)/shard_map/ppermute | solution.py:507
  4.7 1.3 %collective-permute-start.1 = (s32[2,4]{1,0:T(2,128)}, s32[2,4]{1,0:T(2,128)S(1)}, u32[]{:S(2)}, u32[]{:S(2)}) collective-permute-start(s32[2,4]{1,0:T(2,128)} %bitcast.14), channel_id=1, source_target_pairs={{0,12},{4,8},{8,4},{12,0},{1,13},{5,9},{9,5},{13,1},{2,14},{6,10},... | collective-permute-start | bytes 104 | tf_op jit(solution)/shard_map/ppermute | solution.py:507
  6.5 3.8 %collective-permute-done.1.refs_1_ = s32[2,4]{1,0:T(2,128)S(1)} collective-permute-done((s32[2,4]{1,0:T(2,128)}, s32[2,4]{1,0:T(2,128)S(1)}, u32[]{:S(2)}, u32[]{:S(2)}) %collective-permute-start.1) | collective-permute-done | bytes 64 | tf_op jit(solution)/shard_map/ppermute | solution.py:507
  10.3 2.7 %pack.1 = (bf16[2,304,256]{2,1,0:T(8,128)(2,1)S(1)}, bf16[2,304,256]{2,1,0:T(8,128)(2,1)S(1)}, bf16[2,304,256]{2,1,0:T(8,128)(2,1)S(1)}, bf16[2,208,256]{2,1,0:T...) custom-call(s32[1]{0:T(128)} %bitcast.me_ref, ...), custom_call_target="tpu_custom_call" | custom-call | tf_op jit(solution)/shard_map/pack/pallas_call | solution.py:111
  13.0 1.6 %collective-permute-start.3 = (bf16[4,512,256]{2,1,0:T(8,128)(2,1)S(1)}, bf16[4,512,256]{2,1,0:T(8,128)(2,1)S(1)}, u32[]{:S(2)}, u32[]{:S(2)}) collective-permute-start(bf16[4,512,256]{2,1,0:T(8,128)(2,1)S(1)} %get-tuple-element.52.rows_ref), channel_id=1, source_target_pairs={{0,2},{1,3},{2,0},{3,1},{4,6},{5,7},{6,4},{7,5},{8,10},{9,11},{10,... | collective-permute-start | bytes 3145736 | tf_op jit(solution)/shard_map/ppermute | solution.py:492
  14.6 2.0 %collective-permute-start.4 = (bf16[2,304,256]{2,1,0:T(8,128)(2,1)S(1)}, bf16[2,304,256]{2,1,0:T(8,128)(2,1)S(1)}, u32[]{:S(2)}, u32[]{:S(2)}) collective-permute-start(bf16[2,304,256]{2,1,0:T(8,128)(2,1)S(1)} %get-tuple-element.53), channel_id=1, source_target_pairs={{0,12},{4,8},{8,4},{12,0},{1,13},{5,9},{9,5},{13,1},{2,14},{6,10},... | collective-permute-start | bytes 933896 | tf_op jit(solution)/shard_map/ppermute | solution.py:507
  16.6 2.4 %collective-permute-start.6 = (bf16[2,304,256]{2,1,0:T(8,128)(2,1)S(1)}, bf16[2,304,256]{2,1,0:T(8,128)(2,1)S(1)}, u32[]{:S(2)}, u32[]{:S(2)}) collective-permute-start(bf16[2,304,256]{2,1,0:T(8,128)(2,1)S(1)} %get-tuple-element.55), channel_id=1, source_target_pairs={{0,4},{4,0},{8,12},{12,8},{1,5},{5,1},{9,13},{13,9},{2,6},{6,2},{1... | collective-permute-start | bytes 933896 | tf_op jit(solution)/shard_map/ppermute | solution.py:507
  19.0 6.1 %keep.1 = (bf16[8,512,256]{2,1,0:T(8,128)(2,1)}, bf16[4,512,256]{2,1,0:T(8,128)(2,1)S(1)}) custom-call(s32[1]{0:T(128)} %bitcast.me_ref, s32[2,4]{1,0:T(2,128)} %bitcast.17, bf16[8,512,256]{2,1,0:T(8,128)(2,1)} %bitcast.9, bf16[8,512,256]{2,1,0:T(8,128)(2,1)} %bitcast.10), custom_call_target="tpu_custom_call" | custom-call | tf_op jit(solution)/shard_map/keep/pallas_call | solution.py:375
  25.2 11.4 %collective-permute-done.3 = bf16[4,512,256]{2,1,0:T(8,128)(2,1)S(1)} collective-permute-done((bf16[4,512,256]{2,1,0:T(8,128)(2,1)S(1)}, bf16[4,512,256]{2,1,0:T(8,128)(2,1)S(1)}, u32[]{:S(2)}, u32[]{:S(2)}) %collective-permute-start.3) | collective-permute-done | bytes 1048608 | tf_op jit(solution)/shard_map/ppermute | solution.py:492
  36.8 5.0 %collective-permute-done.7.refs_1_.refs_0_ = bf16[2,208,256]{2,1,0:T(8,128)(2,1)S(1)} collective-permute-done((bf16[2,208,256]{2,1,0:T(8,128)(2,1)S(1)}, bf16[2,208,256]{2,1,0:T(8,128)(2,1)S(1)}, u32[]{:S(2)}, u32[]{:S(2)}) %collective-permute-start.7) | collective-permute-done | bytes 213024 | tf_op jit(solution)/shard_map/ppermute | solution.py:507
  41.9 0.9 %select.3 = (bf16[2,304,256]{2,1,0:T(8,128)(2,1)S(1)}, bf16[2,304,256]{2,1,0:T(8,128)(2,1)S(1)}, bf16[4,304,256]{2,1,0:T(8,128)(2,1)S(1)}) custom-call(s32[1]{0:T(128)} %bitcast.me_ref, s32[2,4]{1,0:T(2,128)} %bitcast.18, bf16[4,512,256]{2,1,0:T(8,128)(2,1)S(1)} %get-tuple-element.59.own_ref, bf16[2,304,256]{2,1,0:T(8,128)(2,1)S(1)} %collective-permute-done.4.refs_0_, ...), custom_call_target="tpu_custom_call" | custom-call | tf_op jit(solution)/shard_map/select/pallas_call | solution.py:164
  42.8 0.6 collective-permute-start.8
  43.4 2.0 %collective-permute-start.10 = (bf16[2,208,256]{2,1,0:T(8,128)(2,1)S(1)}, bf16[2,208,256]{2,1,0:T(8,128)(2,1)S(1)}, u32[]{:S(2)}, u32[]{:S(2)}) collective-permute-start(bf16[2,208,256]{2,1,0:T(8,128)(2,1)S(1)} %get-tuple-element.67), channel_id=1, source_target_pairs={{0,12},{4,8},{8,4},{12,0},{1,13},{5,9},{9,5},{13,1},{2,14},{6,10},... | collective-permute-start | bytes 638984 | tf_op jit(solution)/shard_map/ppermute | solution.py:507
  45.4 8.0 %collective-permute-done.10.refs_0_.refs_2_ = bf16[2,208,256]{2,1,0:T(8,128)(2,1)S(1)} collective-permute-done((bf16[2,208,256]{2,1,0:T(8,128)(2,1)S(1)}, bf16[2,208,256]{2,1,0:T(8,128)(2,1)S(1)}, u32[]{:S(2)}, u32[]{:S(2)}) %collective-permute-start.10) | collective-permute-done | bytes 213024 | tf_op jit(solution)/shard_map/ppermute | solution.py:507
  53.4 0.8 select.4.refs_9_.refs_2_
  54.2 1.6 %collective-permute-start.11 = (bf16[2,208,256]{2,1,0:T(8,128)(2,1)S(1)}, bf16[2,208,256]{2,1,0:T(8,128)(2,1)S(1)}, u32[]{:S(2)}, u32[]{:S(2)}) collective-permute-start(bf16[2,208,256]{2,1,0:T(8,128)(2,1)S(1)} %select.4.refs_9_.refs_2_), channel_id=1, source_target_pairs={{0,2},{1,3},{2,0},{3,1},{4,6},{5,7},{6,4},{7,5},{8,10},{9,11},{10,... | collective-permute-start | bytes 638984 | tf_op jit(solution)/shard_map/ppermute | solution.py:492
  55.7 8.2 %collective-permute-done.12.refs_1_ = bf16[2,208,256]{2,1,0:T(8,128)(2,1)S(1)} collective-permute-done((bf16[2,208,256]{2,1,0:T(8,128)(2,1)S(1)}, bf16[2,208,256]{2,1,0:T(8,128)(2,1)S(1)}, u32[]{:S(2)}, u32[]{:S(2)}) %collective-permute-start.12) | collective-permute-done | bytes 213024 | tf_op jit(solution)/shard_map/ppermute | solution.py:507
  63.9 0.8 select.5.refs_10_.refs_3_
  64.8 0.6 collective-permute-start.16
  65.4 1.5 %collective-permute-start.17 = (bf16[2,208,256]{2,1,0:T(8,128)(2,1)S(1)}, bf16[2,208,256]{2,1,0:T(8,128)(2,1)S(1)}, u32[]{:S(2)}, u32[]{:S(2)}) collective-permute-start(bf16[2,208,256]{2,1,0:T(8,128)(2,1)S(1)} %select.5.refs_10_.refs_3_), channel_id=1, source_target_pairs={{0,2},{1,3},{2,0},{3,1},{4,6},{5,7},{6,4},{7,5},{8,10},{9,11},{10,... | collective-permute-start | bytes 638984 | tf_op jit(solution)/shard_map/ppermute | solution.py:492
  67.1 0.3 collective-permute-start.18
  67.4 3.1 %first_window.1 = (f32[4,512,128]{2,1,0:T(8,128)S(1)}, f32[4,512,128]{2,1,0:T(8,128)S(1)}, f32[4,512,256]{2,1,0:T(8,128)S(1)}, f32[4,256]{1,0:T(4,128)S(1)}) custom-call(bf16[2,4,512,256]{3,2,1,0:T(8,128)(2,1)S(1)} %pad_maximum_fusion.refs_0_, bf16[2,4,512,256]{3,2,1,0:T(8,128)(2,1)S(1)} %collective-permute-done.9.refs_1_, ...), custom_call_target="tpu_custom_call" | custom-call | tf_op jit(solution)/shard_map/first_window/pallas_call | solution.py:315
  70.5 2.5 %collective-permute-done.17.refs_12_ = bf16[2,208,256]{2,1,0:T(8,128)(2,1)S(1)} collective-permute-done((bf16[2,208,256]{2,1,0:T(8,128)(2,1)S(1)}, bf16[2,208,256]{2,1,0:T(8,128)(2,1)S(1)}, u32[]{:S(2)}, u32[]{:S(2)}) %collective-permute-start.17) | collective-permute-done | bytes 213024 | tf_op jit(solution)/shard_map/ppermute | solution.py:492
  73.0 0.5 collective-permute-start.19
  73.5 0.9 %collective-permute-done.21.refs_16_ = bf16[2,208,256]{2,1,0:T(8,128)(2,1)S(1)} collective-permute-done((bf16[2,208,256]{2,1,0:T(8,128)(2,1)S(1)}, bf16[2,208,256]{2,1,0:T(8,128)(2,1)S(1)}, u32[]{:S(2)}, u32[]{:S(2)}) %collective-permute-start.21) | collective-permute-done | bytes 213024 | tf_op jit(solution)/shard_map/ppermute | solution.py:492
  74.5 0.3 collective-permute-done.19.refs_14_
  74.8 2.6 %last_window.1 = (bf16[4,512,256]{2,1,0:T(8,128)(2,1)S(1)}, f32[4,512,128]{2,1,0:T(8,128)S(1)}, f32[8,512]{1,0:T(8,128)S(1)}, f32[8,512]{1,0:T(8,128)S(1)}, f32[...) custom-call(s32[1]{0:T(128)} %bitcast.me_ref, s32[2,4]{1,0:T(2,128)} %bitcast.21, ...), custom_call_target="tpu_custom_call" | custom-call | flops 1073741824 | bytes 8388608 | tf_op jit(solution)/shard_map/last_window/pallas_call | solution.py:339
  77.4 3.6 %collective-permute-start.22 = (f32[8,512]{1,0:T(8,128)S(1)}, f32[8,512]{1,0:T(8,128)S(1)}, u32[]{:S(2)}, u32[]{:S(2)}) collective-permute-start(f32[8,512]{1,0:T(8,128)S(1)} %get-tuple-element.95), channel_id=1, source_target_pairs={{0,8},{4,12},{8,0},{12,4},{1,9},{5,13},{9,1},{13,5},{2,10},{6,14},... | collective-permute-start | bytes 49160 | tf_op jit(solution)/shard_map/ppermute | solution.py:507
  81.0 1.8 %collective-permute-start.23 = (f32[8,512]{1,0:T(8,128)S(1)}, f32[8,512]{1,0:T(8,128)S(1)}, u32[]{:S(2)}, u32[]{:S(2)}) collective-permute-start(f32[8,512]{1,0:T(8,128)S(1)} %get-tuple-element.96), channel_id=1, source_target_pairs={{0,12},{4,8},{8,4},{12,0},{1,13},{5,9},{9,5},{13,1},{2,14},{6,10},... | collective-permute-start | bytes 49160 | tf_op jit(solution)/shard_map/ppermute | solution.py:507
  82.8 2.2 %means.1 = bf16[8,512,256]{2,1,0:T(8,128)(2,1)} custom-call(s32[1]{0:T(128)} %bitcast.me_ref, s32[2,4]{1,0:T(2,128)} %bitcast.22, bf16[4,512,256]{2,1,0:T(8,128)(2,1)S(1)} %get-tuple-element.52.rows_ref, bf16[4,512,256]{2,1,0:T(8,128)(2,1)S(1)} %get-tuple-element.98.kernel_ref, ...), custom_call_target="tpu_custom_call", output_to_operand_aliasing={{}: (10, {})} | custom-call | flops 536870912 | bytes 8388608 | tf_op jit(solution)/shard_map/means/pallas_call | solution.py:444
  85.1 1.5 %collective-permute-done.23.refs_3_ = f32[8,512]{1,0:T(8,128)S(1)} collective-permute-done((f32[8,512]{1,0:T(8,128)S(1)}, f32[8,512]{1,0:T(8,128)S(1)}, u32[]{:S(2)}, u32[]{:S(2)}) %collective-permute-start.23) | collective-permute-done | bytes 16416 | tf_op jit(solution)/shard_map/ppermute | solution.py:507
  86.7 0.6 weights.1
  (29 shorter events, 1.2 us)
Async XLA Ops:
  0.6 5.9 %collective-permute-start.2 = (s32[2,4]{1,0:T(2,128)}, s32[2,4]{1,0:T(2,128)S(1)}, u32[]{:S(2)}, u32[]{:S(2)}) collective-permute-start(s32[2,4]{1,0:T(2,128)} %bitcast.13), channel_id=1, source_target_pairs={{0,8},{4,12},{8,0},{12,4},{1,9},{5,13},{9,1},{13,5},{2,10},{6,14},... | collective-permute-start | bytes 104 | tf_op jit(solution)/shard_map/ppermute | solution.py:507
  4.7 5.6 %collective-permute-start.1 = (s32[2,4]{1,0:T(2,128)}, s32[2,4]{1,0:T(2,128)S(1)}, u32[]{:S(2)}, u32[]{:S(2)}) collective-permute-start(s32[2,4]{1,0:T(2,128)} %bitcast.14), channel_id=1, source_target_pairs={{0,12},{4,8},{8,4},{12,0},{1,13},{5,9},{9,5},{13,1},{2,14},{6,10},... | collective-permute-start | bytes 104 | tf_op jit(solution)/shard_map/ppermute | solution.py:507
  6.1 4.2 %collective-permute-start = (s32[2,4]{1,0:T(2,128)}, s32[2,4]{1,0:T(2,128)S(1)}, u32[]{:S(2)}, u32[]{:S(2)}) collective-permute-start(s32[2,4]{1,0:T(2,128)} %bitcast.15), channel_id=1, source_target_pairs={{0,4},{4,0},{8,12},{12,8},{1,5},{5,1},{9,13},{13,9},{2,6},{6,2},{1... | collective-permute-start | bytes 104 | tf_op jit(solution)/shard_map/ppermute | solution.py:507
  13.0 23.5 %collective-permute-start.3 = (bf16[4,512,256]{2,1,0:T(8,128)(2,1)S(1)}, bf16[4,512,256]{2,1,0:T(8,128)(2,1)S(1)}, u32[]{:S(2)}, u32[]{:S(2)}) collective-permute-start(bf16[4,512,256]{2,1,0:T(8,128)(2,1)S(1)} %get-tuple-element.52.rows_ref), channel_id=1, source_target_pairs={{0,2},{1,3},{2,0},{3,1},{4,6},{5,7},{6,4},{7,5},{8,10},{9,11},{10,... | collective-permute-start | bytes 3145736 | tf_op jit(solution)/shard_map/ppermute | solution.py:492
  14.6 27.2 %collective-permute-start.4 = (bf16[2,304,256]{2,1,0:T(8,128)(2,1)S(1)}, bf16[2,304,256]{2,1,0:T(8,128)(2,1)S(1)}, u32[]{:S(2)}, u32[]{:S(2)}) collective-permute-start(bf16[2,304,256]{2,1,0:T(8,128)(2,1)S(1)} %get-tuple-element.53), channel_id=1, source_target_pairs={{0,12},{4,8},{8,4},{12,0},{1,13},{5,9},{9,5},{13,1},{2,14},{6,10},... | collective-permute-start | bytes 933896 | tf_op jit(solution)/shard_map/ppermute | solution.py:507
  16.6 25.2 %collective-permute-start.5 = (bf16[2,304,256]{2,1,0:T(8,128)(2,1)S(1)}, bf16[2,304,256]{2,1,0:T(8,128)(2,1)S(1)}, u32[]{:S(2)}, u32[]{:S(2)}) collective-permute-start(bf16[2,304,256]{2,1,0:T(8,128)(2,1)S(1)} %get-tuple-element.54), channel_id=1, source_target_pairs={{0,8},{4,12},{8,0},{12,4},{1,9},{5,13},{9,1},{13,5},{2,10},{6,14},... | collective-permute-start | bytes 933896 | tf_op jit(solution)/shard_map/ppermute | solution.py:507
  16.6 25.2 %collective-permute-start.6 = (bf16[2,304,256]{2,1,0:T(8,128)(2,1)S(1)}, bf16[2,304,256]{2,1,0:T(8,128)(2,1)S(1)}, u32[]{:S(2)}, u32[]{:S(2)}) collective-permute-start(bf16[2,304,256]{2,1,0:T(8,128)(2,1)S(1)} %get-tuple-element.55), channel_id=1, source_target_pairs={{0,4},{4,0},{8,12},{12,8},{1,5},{5,1},{9,13},{13,9},{2,6},{6,2},{1... | collective-permute-start | bytes 933896 | tf_op jit(solution)/shard_map/ppermute | solution.py:507
  19.0 22.8 %collective-permute-start.7 = (bf16[2,208,256]{2,1,0:T(8,128)(2,1)S(1)}, bf16[2,208,256]{2,1,0:T(8,128)(2,1)S(1)}, u32[]{:S(2)}, u32[]{:S(2)}) collective-permute-start(bf16[2,208,256]{2,1,0:T(8,128)(2,1)S(1)} %get-tuple-element.56), channel_id=1, source_target_pairs={{0,4},{4,0},{8,12},{12,8},{1,5},{5,1},{9,13},{13,9},{2,6},{6,2},{1... | collective-permute-start | bytes 638984 | tf_op jit(solution)/shard_map/ppermute | solution.py:507
  41.8 22.1 %collective-permute-start.9 = (bf16[2,4,512,256]{3,2,1,0:T(8,128)(2,1)S(1)}, bf16[2,4,512,256]{3,2,1,0:T(8,128)(2,1)S(1)}, u32[]{:S(2)}, u32[]{:S(2)}) collective-permute-start(bf16[2,4,512,256]{3,2,1,0:T(8,128)(2,1)S(1)} %pad_maximum_fusion.refs_0_), channel_id=1, source_target_pairs={{0,1},{1,0},{2,3},{3,2},{4,5},{5,4},{6,7},{7,6},{8,9},{9,8},{10,11... | collective-permute-start | bytes 6291464 | tf_op jit(solution)/shard_map/ppermute | solution.py:492
  42.8 21.1 %collective-permute-start.8 = (bf16[4,304,256]{2,1,0:T(8,128)(2,1)S(1)}, bf16[4,304,256]{2,1,0:T(8,128)(2,1)S(1)}, u32[]{:S(2)}, u32[]{:S(2)}) collective-permute-start(bf16[4,304,256]{2,1,0:T(8,128)(2,1)S(1)} %get-tuple-element.65), channel_id=1, source_target_pairs={{0,2},{1,3},{2,0},{3,1},{4,6},{5,7},{6,4},{7,5},{8,10},{9,11},{10,... | collective-permute-start | bytes 1867784 | tf_op jit(solution)/shard_map/ppermute | solution.py:492
  43.4 10.0 %collective-permute-start.10 = (bf16[2,208,256]{2,1,0:T(8,128)(2,1)S(1)}, bf16[2,208,256]{2,1,0:T(8,128)(2,1)S(1)}, u32[]{:S(2)}, u32[]{:S(2)}) collective-permute-start(bf16[2,208,256]{2,1,0:T(8,128)(2,1)S(1)} %get-tuple-element.67), channel_id=1, source_target_pairs={{0,12},{4,8},{8,4},{12,0},{1,13},{5,9},{9,5},{13,1},{2,14},{6,10},... | collective-permute-start | bytes 638984 | tf_op jit(solution)/shard_map/ppermute | solution.py:507
  45.4 18.5 %collective-permute-start.12 = (bf16[2,208,256]{2,1,0:T(8,128)(2,1)S(1)}, bf16[2,208,256]{2,1,0:T(8,128)(2,1)S(1)}, u32[]{:S(2)}, u32[]{:S(2)}) collective-permute-start(bf16[2,208,256]{2,1,0:T(8,128)(2,1)S(1)} %get-tuple-element.69), channel_id=1, source_target_pairs={{0,8},{4,12},{8,0},{12,4},{1,9},{5,13},{9,1},{13,5},{2,10},{6,14},... | collective-permute-start | bytes 638984 | tf_op jit(solution)/shard_map/ppermute | solution.py:507
  54.2 9.7 %collective-permute-start.11 = (bf16[2,208,256]{2,1,0:T(8,128)(2,1)S(1)}, bf16[2,208,256]{2,1,0:T(8,128)(2,1)S(1)}, u32[]{:S(2)}, u32[]{:S(2)}) collective-permute-start(bf16[2,208,256]{2,1,0:T(8,128)(2,1)S(1)} %select.4.refs_9_.refs_2_), channel_id=1, source_target_pairs={{0,2},{1,3},{2,0},{3,1},{4,6},{5,7},{6,4},{7,5},{8,10},{9,11},{10,... | collective-permute-start | bytes 638984 | tf_op jit(solution)/shard_map/ppermute | solution.py:492
  55.7 11.2 %collective-permute-start.13 = (bf16[2,304,256]{2,1,0:T(8,128)(2,1)S(1)}, bf16[2,304,256]{2,1,0:T(8,128)(2,1)S(1)}, u32[]{:S(2)}, u32[]{:S(2)}) collective-permute-start(bf16[2,304,256]{2,1,0:T(8,128)(2,1)S(1)} %get-tuple-element.78.refs_2_.refs_0_), channel_id=1, source_target_pairs={{0,1},{1,0},{2,3},{3,2},{4,5},{5,4},{6,7},{7,6},{8,9},{9,8},{10,11... | collective-permute-start | bytes 933896 | tf_op jit(solution)/shard_map/ppermute | solution.py:492
  63.9 3.2 %collective-permute-start.14 = (bf16[2,304,256]{2,1,0:T(8,128)(2,1)S(1)}, bf16[2,304,256]{2,1,0:T(8,128)(2,1)S(1)}, u32[]{:S(2)}, u32[]{:S(2)}) collective-permute-start(bf16[2,304,256]{2,1,0:T(8,128)(2,1)S(1)} %get-tuple-element.79.refs_3_.refs_1_), channel_id=1, source_target_pairs={{0,1},{1,0},{2,3},{3,2},{4,5},{5,4},{6,7},{7,6},{8,9},{9,8},{10,11... | collective-permute-start | bytes 933896 | tf_op jit(solution)/shard_map/ppermute | solution.py:492
  64.8 2.7 %collective-permute-start.16 = (bf16[2,304,256]{2,1,0:T(8,128)(2,1)S(1)}, bf16[2,304,256]{2,1,0:T(8,128)(2,1)S(1)}, u32[]{:S(2)}, u32[]{:S(2)}) collective-permute-start(bf16[2,304,256]{2,1,0:T(8,128)(2,1)S(1)} %get-tuple-element.102), channel_id=1, source_target_pairs={{0,1},{1,0},{2,3},{3,2},{4,5},{5,4},{6,7},{7,6},{8,9},{9,8},{10,11... | collective-permute-start | bytes 933896 | tf_op jit(solution)/shard_map/ppermute | solution.py:492
  65.3 2.1 %collective-permute-start.15 = (bf16[2,304,256]{2,1,0:T(8,128)(2,1)S(1)}, bf16[2,304,256]{2,1,0:T(8,128)(2,1)S(1)}, u32[]{:S(2)}, u32[]{:S(2)}) collective-permute-start(bf16[2,304,256]{2,1,0:T(8,128)(2,1)S(1)} %get-tuple-element.103), channel_id=1, source_target_pairs={{0,1},{1,0},{2,3},{3,2},{4,5},{5,4},{6,7},{7,6},{8,9},{9,8},{10,11... | collective-permute-start | bytes 933896 | tf_op jit(solution)/shard_map/ppermute | solution.py:492
  65.4 7.6 %collective-permute-start.17 = (bf16[2,208,256]{2,1,0:T(8,128)(2,1)S(1)}, bf16[2,208,256]{2,1,0:T(8,128)(2,1)S(1)}, u32[]{:S(2)}, u32[]{:S(2)}) collective-permute-start(bf16[2,208,256]{2,1,0:T(8,128)(2,1)S(1)} %select.5.refs_10_.refs_3_), channel_id=1, source_target_pairs={{0,2},{1,3},{2,0},{3,1},{4,6},{5,7},{6,4},{7,5},{8,10},{9,11},{10,... | collective-permute-start | bytes 638984 | tf_op jit(solution)/shard_map/ppermute | solution.py:492
  66.9 6.6 %collective-permute-start.20 = (bf16[2,208,256]{2,1,0:T(8,128)(2,1)S(1)}, bf16[2,208,256]{2,1,0:T(8,128)(2,1)S(1)}, u32[]{:S(2)}, u32[]{:S(2)}) collective-permute-start(bf16[2,208,256]{2,1,0:T(8,128)(2,1)S(1)} %collective-permute-done.11.refs_11_), channel_id=1, source_target_pairs={{0,1},{1,0},{2,3},{3,2},{4,5},{5,4},{6,7},{7,6},{8,9},{9,8},{10,11... | collective-permute-start | bytes 638984 | tf_op jit(solution)/shard_map/ppermute | solution.py:492
  67.1 6.5 %collective-permute-start.18 = (bf16[2,208,256]{2,1,0:T(8,128)(2,1)S(1)}, bf16[2,208,256]{2,1,0:T(8,128)(2,1)S(1)}, u32[]{:S(2)}, u32[]{:S(2)}) collective-permute-start(bf16[2,208,256]{2,1,0:T(8,128)(2,1)S(1)} %select.4.refs_9_.refs_2_), channel_id=1, source_target_pairs={{0,1},{1,0},{2,3},{3,2},{4,5},{5,4},{6,7},{7,6},{8,9},{9,8},{10,11... | collective-permute-start | bytes 638984 | tf_op jit(solution)/shard_map/ppermute | solution.py:492
  73.0 1.5 %collective-permute-start.21 = (bf16[2,208,256]{2,1,0:T(8,128)(2,1)S(1)}, bf16[2,208,256]{2,1,0:T(8,128)(2,1)S(1)}, u32[]{:S(2)}, u32[]{:S(2)}) collective-permute-start(bf16[2,208,256]{2,1,0:T(8,128)(2,1)S(1)} %collective-permute-done.17.refs_12_), channel_id=1, source_target_pairs={{0,1},{1,0},{2,3},{3,2},{4,5},{5,4},{6,7},{7,6},{8,9},{9,8},{10,11... | collective-permute-start | bytes 638984 | tf_op jit(solution)/shard_map/ppermute | solution.py:492
  73.0 1.8 %collective-permute-start.19 = (bf16[2,208,256]{2,1,0:T(8,128)(2,1)S(1)}, bf16[2,208,256]{2,1,0:T(8,128)(2,1)S(1)}, u32[]{:S(2)}, u32[]{:S(2)}) collective-permute-start(bf16[2,208,256]{2,1,0:T(8,128)(2,1)S(1)} %select.5.refs_10_.refs_3_), channel_id=1, source_target_pairs={{0,1},{1,0},{2,3},{3,2},{4,5},{5,4},{6,7},{7,6},{8,9},{9,8},{10,11... | collective-permute-start | bytes 638984 | tf_op jit(solution)/shard_map/ppermute | solution.py:492
  77.4 7.6 %collective-permute-start.22 = (f32[8,512]{1,0:T(8,128)S(1)}, f32[8,512]{1,0:T(8,128)S(1)}, u32[]{:S(2)}, u32[]{:S(2)}) collective-permute-start(f32[8,512]{1,0:T(8,128)S(1)} %get-tuple-element.95), channel_id=1, source_target_pairs={{0,8},{4,12},{8,0},{12,4},{1,9},{5,13},{9,1},{13,5},{2,10},{6,14},... | collective-permute-start | bytes 49160 | tf_op jit(solution)/shard_map/ppermute | solution.py:507
  81.0 5.6 %collective-permute-start.23 = (f32[8,512]{1,0:T(8,128)S(1)}, f32[8,512]{1,0:T(8,128)S(1)}, u32[]{:S(2)}, u32[]{:S(2)}) collective-permute-start(f32[8,512]{1,0:T(8,128)S(1)} %get-tuple-element.96), channel_id=1, source_target_pairs={{0,12},{4,8},{8,4},{12,0},{1,13},{5,9},{9,5},{13,1},{2,14},{6,10},... | collective-permute-start | bytes 49160 | tf_op jit(solution)/shard_map/ppermute | solution.py:507
  82.8 3.9 %collective-permute-start.24 = (f32[8,512]{1,0:T(8,128)S(1)}, f32[8,512]{1,0:T(8,128)S(1)}, u32[]{:S(2)}, u32[]{:S(2)}) collective-permute-start(f32[8,512]{1,0:T(8,128)S(1)} %get-tuple-element.97), channel_id=1, source_target_pairs={{0,4},{4,0},{8,12},{12,8},{1,5},{5,1},{9,13},{13,9},{2,6},{6,2},{1... | collective-permute-start | bytes 49160 | tf_op jit(solution)/shard_map/ppermute | solution.py:507

commit v21 on v20

--- a/solution.py
+++ b/solution.py
@@ -11,7 +11,7 @@
 BR = 512
 BLK_DEV = 8
 LANES = 128
-CHUNKS = ((0, 304), (304, 208))
+CHUNKS = ((0, 320), (320, 192))
 WINDOWS = ((0, 256), (256, 512))
 
 
@@ -76,7 +76,7 @@
 def in_order(wide_count, me_ref, pairs_ref):
     pair_count = pairs_ref.shape[1]
     far = [
-        ((pairs_ref[1, pair] >> 3) ^ me_ref[0] == wide_count // 2).astype(jnp.int32)
+        ((pairs_ref[1, pair] >> 3) ^ me_ref[0] == wide_count - 1).astype(jnp.int32)
         for pair in range(pair_count)
     ]
     place_near, place_far = jnp.int32(0), pair_count - sum(far)
@@ -530,7 +530,7 @@
         middle = pair_count // 2
         return [part[0][:middle], part[0][middle:]]
 
-    half, middle = pair_count // 2, wide_count // 2
+    half, far = pair_count // 2, apart[0]
     rows = jnp.stack([part[0] for part in first_hops([row_slices])])
     received = to_wide(outgoing[0], apart)
     near = to_wide(outgoing[1][-1:], apart[-1:])
@@ -538,8 +538,10 @@
     own_a, whole_a = pick(received, apart, 0, (0, pair_count), 2, 1)
     cols_a = [own_a] + first_hops(whole_a)[1:]
     rows = [[rows], *hop([[rows]], 1)]
-    came = dict(zip(apart, to_wide(outgoing[1][:-1], apart[:-1]) + near))
-    early = {other: piece for other, piece in came.items() if other != middle}
+    later = [*apart[1:-1], far]
+    pieces = [*outgoing[1][1:-1], outgoing[1][0]]
+    came = dict(zip([*later, apart[-1]], to_wide(pieces, later) + near))
+    early = {other: piece for other, piece in came.items() if other != far}
     cols_b = first_hops(*pick(list(early.values()), early, 1, (0, half), 1))
     cols_a, rows, cols_b, came = fixed((cols_a, rows, cols_b, came))
     late_b, cols_a = fixed((pick(list(came.values()), came, 1, (half, half), 1), cols_a))

time: 87.7 us -> 87.8 us (level)
  waiting for transfers between devices: 42 us -> 43 us
  starting transfers between devices: 24.4 us -> 23.5 us
    ppermute x13, waiting for transfers between devices: 15.2 us -> 19.2 us  [hop(): lax.ppermute(piece, 'narrow', perm)]
    ppermute x12, waiting for transfers between devices: 26.9 us -> 23.8 us  [to_wide(): lax.ppermute(piece, 'wide', [(i, i ^ other) for i in range(count)])]
    ppermute x12, starting transfers between devices: 17.5 us -> 16.2 us  [to_wide(): lax.ppermute(piece, 'wide', [(i, i ^ other) for i in range(count)])]
  transfers between devices with their start and end apart: 25 -> 25, of which waited for: 11 -> 10; matrix products, arithmetic and copies ran while one was open for 0% -> 0% of each run, Pallas kernels for 16% -> 16%
where the time goes in v21:
time: 87.8 us; the launch traced here: 87.4 us
  waiting for transfers between devices  43 us (49%)
  starting transfers between devices  23.5 us (27%)
  Pallas kernels  19.9 us (23%)
    ppermute x12, waiting for transfers between devices, to_wide(): lax.ppermute(piece, 'wide', [(i, i ^ other) for i in range(count)])  23.8 us
    ppermute x13, waiting for transfers between devices, hop(): lax.ppermute(piece, 'narrow', perm)  19.2 us
    ppermute x12, starting transfers between devices, to_wide(): lax.ppermute(piece, 'wide', [(i, i ^ other) for i in range(count)])  16.2 us
    ppermute x13, starting transfers between devices, hop(): lax.ppermute(piece, 'narrow', perm)  7.3 us
    pallas_call x1, Pallas kernels, keep(): pl.pallas_call(functools.partial(keep_kernel, wide_count), out_shape=[plt...  6.14 us
    pallas_call x1, Pallas kernels, first_window(): pl.pallas_call(functools.partial(first_kernel, window, piece_counts(windo...  3.1 us
    pallas_call x1, Pallas kernels, pack(): pl.pallas_call(functools.partial(pack_kernel, wide_count, pair_count, cap...  2.67 us
    pallas_call x1, Pallas kernels, last_window(): pl.pallas_call(functools.partial(last_kernel, window, piece_counts(window...  2.63 us
  transfers between devices with their start and end apart: 25, of which 10 were waited for; matrix products, arithmetic and copies ran while one was open for 0% of the time, Pallas kernels for 16%

profile of v21, /device:TPU:0, one launch (start us, length us, event | category | flops | bytes accessed | tf_op | source)
XLA Modules:
  0.0 87.4 jit_solution(6893161525349460890)
XLA Ops:
  0.6 4.1 %collective-permute-start.2 = (s32[2,4]{1,0:T(2,128)}, s32[2,4]{1,0:T(2,128)S(1)}, u32[]{:S(2)}, u32[]{:S(2)}) collective-permute-start(s32[2,4]{1,0:T(2,128)} %bitcast.13), channel_id=1, source_target_pairs={{0,8},{4,12},{8,0},{12,4},{1,9},{5,13},{9,1},{13,5},{2,10},{6,14},... | collective-permute-start | bytes 104 | tf_op jit(solution)/shard_map/ppermute | solution.py:507
  4.7 1.3 %collective-permute-start.1 = (s32[2,4]{1,0:T(2,128)}, s32[2,4]{1,0:T(2,128)S(1)}, u32[]{:S(2)}, u32[]{:S(2)}) collective-permute-start(s32[2,4]{1,0:T(2,128)} %bitcast.14), channel_id=1, source_target_pairs={{0,12},{4,8},{8,4},{12,0},{1,13},{5,9},{9,5},{13,1},{2,14},{6,10},... | collective-permute-start | bytes 104 | tf_op jit(solution)/shard_map/ppermute | solution.py:507
  6.5 3.8 %collective-permute-done.1.refs_1_ = s32[2,4]{1,0:T(2,128)S(1)} collective-permute-done((s32[2,4]{1,0:T(2,128)}, s32[2,4]{1,0:T(2,128)S(1)}, u32[]{:S(2)}, u32[]{:S(2)}) %collective-permute-start.1) | collective-permute-done | bytes 64 | tf_op jit(solution)/shard_map/ppermute | solution.py:507
  10.3 2.7 %pack.1 = (bf16[2,320,256]{2,1,0:T(8,128)(2,1)S(1)}, bf16[2,320,256]{2,1,0:T(8,128)(2,1)S(1)}, bf16[2,320,256]{2,1,0:T(8,128)(2,1)S(1)}, bf16[2,192,256]{2,1,0:T...) custom-call(s32[1]{0:T(128)} %bitcast.me_ref, ...), custom_call_target="tpu_custom_call" | custom-call | tf_op jit(solution)/shard_map/pack/pallas_call | solution.py:111
  13.0 1.6 %collective-permute-start.3 = (bf16[4,512,256]{2,1,0:T(8,128)(2,1)S(1)}, bf16[4,512,256]{2,1,0:T(8,128)(2,1)S(1)}, u32[]{:S(2)}, u32[]{:S(2)}) collective-permute-start(bf16[4,512,256]{2,1,0:T(8,128)(2,1)S(1)} %get-tuple-element.52.rows_ref), channel_id=1, source_target_pairs={{0,2},{1,3},{2,0},{3,1},{4,6},{5,7},{6,4},{7,5},{8,10},{9,11},{10,... | collective-permute-start | bytes 3145736 | tf_op jit(solution)/shard_map/ppermute | solution.py:492
  14.5 2.1 %collective-permute-start.4 = (bf16[2,320,256]{2,1,0:T(8,128)(2,1)S(1)}, bf16[2,320,256]{2,1,0:T(8,128)(2,1)S(1)}, u32[]{:S(2)}, u32[]{:S(2)}) collective-permute-start(bf16[2,320,256]{2,1,0:T(8,128)(2,1)S(1)} %get-tuple-element.53), channel_id=1, source_target_pairs={{0,12},{4,8},{8,4},{12,0},{1,13},{5,9},{9,5},{13,1},{2,14},{6,10},... | collective-permute-start | bytes 983048 | tf_op jit(solution)/shard_map/ppermute | solution.py:507
  16.7 2.3 %collective-permute-start.6 = (bf16[2,320,256]{2,1,0:T(8,128)(2,1)S(1)}, bf16[2,320,256]{2,1,0:T(8,128)(2,1)S(1)}, u32[]{:S(2)}, u32[]{:S(2)}) collective-permute-start(bf16[2,320,256]{2,1,0:T(8,128)(2,1)S(1)} %get-tuple-element.55), channel_id=1, source_target_pairs={{0,4},{4,0},{8,12},{12,8},{1,5},{5,1},{9,13},{13,9},{2,6},{6,2},{1... | collective-permute-start | bytes 983048 | tf_op jit(solution)/shard_map/ppermute | solution.py:507
  19.0 6.1 %keep.1 = (bf16[8,512,256]{2,1,0:T(8,128)(2,1)}, bf16[4,512,256]{2,1,0:T(8,128)(2,1)S(1)}) custom-call(s32[1]{0:T(128)} %bitcast.me_ref, s32[2,4]{1,0:T(2,128)} %bitcast.17, bf16[8,512,256]{2,1,0:T(8,128)(2,1)} %bitcast.9, bf16[8,512,256]{2,1,0:T(8,128)(2,1)} %bitcast.10), custom_call_target="tpu_custom_call" | custom-call | tf_op jit(solution)/shard_map/keep/pallas_call | solution.py:375
  25.1 11.4 %collective-permute-done.3 = bf16[4,512,256]{2,1,0:T(8,128)(2,1)S(1)} collective-permute-done((bf16[4,512,256]{2,1,0:T(8,128)(2,1)S(1)}, bf16[4,512,256]{2,1,0:T(8,128)(2,1)S(1)}, u32[]{:S(2)}, u32[]{:S(2)}) %collective-permute-start.3) | collective-permute-done | bytes 1048608 | tf_op jit(solution)/shard_map/ppermute | solution.py:492
  36.7 3.3 %collective-permute-done.7.refs_1_.refs_0_ = bf16[2,192,256]{2,1,0:T(8,128)(2,1)S(1)} collective-permute-done((bf16[2,192,256]{2,1,0:T(8,128)(2,1)S(1)}, bf16[2,192,256]{2,1,0:T(8,128)(2,1)S(1)}, u32[]{:S(2)}, u32[]{:S(2)}) %collective-permute-start.7) | collective-permute-done | bytes 196640 | tf_op jit(solution)/shard_map/ppermute | solution.py:507
  40.1 2.7 %collective-permute-done.5.refs_1_ = bf16[2,320,256]{2,1,0:T(8,128)(2,1)S(1)} collective-permute-done((bf16[2,320,256]{2,1,0:T(8,128)(2,1)S(1)}, bf16[2,320,256]{2,1,0:T(8,128)(2,1)S(1)}, u32[]{:S(2)}, u32[]{:S(2)}) %collective-permute-start.5) | collective-permute-done | bytes 327712 | tf_op jit(solution)/shard_map/ppermute | solution.py:507
  42.8 0.9 %select.3 = (bf16[2,320,256]{2,1,0:T(8,128)(2,1)S(1)}, bf16[2,320,256]{2,1,0:T(8,128)(2,1)S(1)}, bf16[4,320,256]{2,1,0:T(8,128)(2,1)S(1)}) custom-call(s32[1]{0:T(128)} %bitcast.me_ref, s32[2,4]{1,0:T(2,128)} %bitcast.18, bf16[4,512,256]{2,1,0:T(8,128)(2,1)S(1)} %get-tuple-element.59.own_ref, bf16[2,320,256]{2,1,0:T(8,128)(2,1)S(1)} %collective-permute-done.4.refs_0_, ...), custom_call_target="tpu_custom_call" | custom-call | tf_op jit(solution)/shard_map/select/pallas_call | solution.py:164
  43.7 0.6 collective-permute-start.8
  44.6 2.2 %collective-permute-start.12 = (bf16[2,192,256]{2,1,0:T(8,128)(2,1)S(1)}, bf16[2,192,256]{2,1,0:T(8,128)(2,1)S(1)}, u32[]{:S(2)}, u32[]{:S(2)}) collective-permute-start(bf16[2,192,256]{2,1,0:T(8,128)(2,1)S(1)} %get-tuple-element.69), channel_id=1, source_target_pairs={{0,12},{4,8},{8,4},{12,0},{1,13},{5,9},{9,5},{13,1},{2,14},{6,10},... | collective-permute-start | bytes 589832 | tf_op jit(solution)/shard_map/ppermute | solution.py:507
  46.8 13.8 %collective-permute-done.10.refs_0_.refs_1_ = bf16[2,192,256]{2,1,0:T(8,128)(2,1)S(1)} collective-permute-done((bf16[2,192,256]{2,1,0:T(8,128)(2,1)S(1)}, bf16[2,192,256]{2,1,0:T(8,128)(2,1)S(1)}, u32[]{:S(2)}, u32[]{:S(2)}) %collective-permute-start.10) | collective-permute-done | bytes 196640 | tf_op jit(solution)/shard_map/ppermute | solution.py:507
  60.6 0.8 select.4.refs_9_.refs_2_
  61.4 1.6 %collective-permute-start.11 = (bf16[2,192,256]{2,1,0:T(8,128)(2,1)S(1)}, bf16[2,192,256]{2,1,0:T(8,128)(2,1)S(1)}, u32[]{:S(2)}, u32[]{:S(2)}) collective-permute-start(bf16[2,192,256]{2,1,0:T(8,128)(2,1)S(1)} %select.4.refs_9_.refs_2_), channel_id=1, source_target_pairs={{0,2},{1,3},{2,0},{3,1},{4,6},{5,7},{6,4},{7,5},{8,10},{9,11},{10,... | collective-permute-start | bytes 589832 | tf_op jit(solution)/shard_map/ppermute | solution.py:492
  63.0 0.5 collective-permute-start.14
  63.5 4.8 %collective-permute-done.11.refs_11_ = bf16[2,192,256]{2,1,0:T(8,128)(2,1)S(1)} collective-permute-done((bf16[2,192,256]{2,1,0:T(8,128)(2,1)S(1)}, bf16[2,192,256]{2,1,0:T(8,128)(2,1)S(1)}, u32[]{:S(2)}, u32[]{:S(2)}) %collective-permute-start.11) | collective-permute-done | bytes 196640 | tf_op jit(solution)/shard_map/ppermute | solution.py:492
  68.2 0.8 select.5.refs_10_.refs_3_
  69.2 0.5 collective-permute-start.15
  69.7 1.5 %collective-permute-start.17 = (bf16[2,192,256]{2,1,0:T(8,128)(2,1)S(1)}, bf16[2,192,256]{2,1,0:T(8,128)(2,1)S(1)}, u32[]{:S(2)}, u32[]{:S(2)}) collective-permute-start(bf16[2,192,256]{2,1,0:T(8,128)(2,1)S(1)} %select.5.refs_10_.refs_3_), channel_id=1, source_target_pairs={{0,2},{1,3},{2,0},{3,1},{4,6},{5,7},{6,4},{7,5},{8,10},{9,11},{10,... | collective-permute-start | bytes 589832 | tf_op jit(solution)/shard_map/ppermute | solution.py:492
  71.2 0.5 collective-permute-start.18
  71.7 3.1 %first_window.1 = (f32[4,512,128]{2,1,0:T(8,128)S(1)}, f32[4,512,128]{2,1,0:T(8,128)S(1)}, f32[4,512,256]{2,1,0:T(8,128)S(1)}, f32[4,256]{1,0:T(4,128)S(1)}) custom-call(bf16[2,4,512,256]{3,2,1,0:T(8,128)(2,1)S(1)} %pad_maximum_fusion.refs_0_, bf16[2,4,512,256]{3,2,1,0:T(8,128)(2,1)S(1)} %collective-permute-done.9.refs_1_, ...), custom_call_target="tpu_custom_call" | custom-call | tf_op jit(solution)/shard_map/first_window/pallas_call | solution.py:315
  74.8 1.8 %collective-permute-done.17.refs_12_ = bf16[2,192,256]{2,1,0:T(8,128)(2,1)S(1)} collective-permute-done((bf16[2,192,256]{2,1,0:T(8,128)(2,1)S(1)}, bf16[2,192,256]{2,1,0:T(8,128)(2,1)S(1)}, u32[]{:S(2)}, u32[]{:S(2)}) %collective-permute-start.17) | collective-permute-done | bytes 196640 | tf_op jit(solution)/shard_map/ppermute | solution.py:492
  76.5 0.5 collective-permute-start.19
  77.1 0.9 %collective-permute-done.21.refs_16_ = bf16[2,192,256]{2,1,0:T(8,128)(2,1)S(1)} collective-permute-done((bf16[2,192,256]{2,1,0:T(8,128)(2,1)S(1)}, bf16[2,192,256]{2,1,0:T(8,128)(2,1)S(1)}, u32[]{:S(2)}, u32[]{:S(2)}) %collective-permute-start.21) | collective-permute-done | bytes 196640 | tf_op jit(solution)/shard_map/ppermute | solution.py:492
  78.3 2.6 %last_window.1 = (bf16[4,512,256]{2,1,0:T(8,128)(2,1)S(1)}, f32[4,512,128]{2,1,0:T(8,128)S(1)}, f32[8,512]{1,0:T(8,128)S(1)}, f32[8,512]{1,0:T(8,128)S(1)}, f32[...) custom-call(s32[1]{0:T(128)} %bitcast.me_ref, s32[2,4]{1,0:T(2,128)} %bitcast.21, ...), custom_call_target="tpu_custom_call" | custom-call | flops 1073741824 | bytes 8388608 | tf_op jit(solution)/shard_map/last_window/pallas_call | solution.py:339
  81.0 1.4 %collective-permute-start.23 = (f32[8,512]{1,0:T(8,128)S(1)}, f32[8,512]{1,0:T(8,128)S(1)}, u32[]{:S(2)}, u32[]{:S(2)}) collective-permute-start(f32[8,512]{1,0:T(8,128)S(1)} %get-tuple-element.96), channel_id=1, source_target_pairs={{0,12},{4,8},{8,4},{12,0},{1,13},{5,9},{9,5},{13,1},{2,14},{6,10},... | collective-permute-start | bytes 49160 | tf_op jit(solution)/shard_map/ppermute | solution.py:507
  82.3 2.1 %collective-permute-start.24 = (f32[8,512]{1,0:T(8,128)S(1)}, f32[8,512]{1,0:T(8,128)S(1)}, u32[]{:S(2)}, u32[]{:S(2)}) collective-permute-start(f32[8,512]{1,0:T(8,128)S(1)} %get-tuple-element.97), channel_id=1, source_target_pairs={{0,4},{4,0},{8,12},{12,8},{1,5},{5,1},{9,13},{13,9},{2,6},{6,2},{1... | collective-permute-start | bytes 49160 | tf_op jit(solution)/shard_map/ppermute | solution.py:507
  84.5 2.3 %means.1 = bf16[8,512,256]{2,1,0:T(8,128)(2,1)} custom-call(s32[1]{0:T(128)} %bitcast.me_ref, s32[2,4]{1,0:T(2,128)} %bitcast.22, bf16[4,512,256]{2,1,0:T(8,128)(2,1)S(1)} %get-tuple-element.52.rows_ref, bf16[4,512,256]{2,1,0:T(8,128)(2,1)S(1)} %get-tuple-element.98.kernel_ref, ...), custom_call_target="tpu_custom_call", output_to_operand_aliasing={{}: (10, {})} | custom-call | flops 536870912 | bytes 8388608 | tf_op jit(solution)/shard_map/means/pallas_call | solution.py:444
  86.8 0.6 weights.1
  (29 shorter events, 1.5 us)
Async XLA Ops:
  0.6 5.9 %collective-permute-start.2 = (s32[2,4]{1,0:T(2,128)}, s32[2,4]{1,0:T(2,128)S(1)}, u32[]{:S(2)}, u32[]{:S(2)}) collective-permute-start(s32[2,4]{1,0:T(2,128)} %bitcast.13), channel_id=1, source_target_pairs={{0,8},{4,12},{8,0},{12,4},{1,9},{5,13},{9,1},{13,5},{2,10},{6,14},... | collective-permute-start | bytes 104 | tf_op jit(solution)/shard_map/ppermute | solution.py:507
  4.7 5.6 %collective-permute-start.1 = (s32[2,4]{1,0:T(2,128)}, s32[2,4]{1,0:T(2,128)S(1)}, u32[]{:S(2)}, u32[]{:S(2)}) collective-permute-start(s32[2,4]{1,0:T(2,128)} %bitcast.14), channel_id=1, source_target_pairs={{0,12},{4,8},{8,4},{12,0},{1,13},{5,9},{9,5},{13,1},{2,14},{6,10},... | collective-permute-start | bytes 104 | tf_op jit(solution)/shard_map/ppermute | solution.py:507
  6.1 4.2 %collective-permute-start = (s32[2,4]{1,0:T(2,128)}, s32[2,4]{1,0:T(2,128)S(1)}, u32[]{:S(2)}, u32[]{:S(2)}) collective-permute-start(s32[2,4]{1,0:T(2,128)} %bitcast.15), channel_id=1, source_target_pairs={{0,4},{4,0},{8,12},{12,8},{1,5},{5,1},{9,13},{13,9},{2,6},{6,2},{1... | collective-permute-start | bytes 104 | tf_op jit(solution)/shard_map/ppermute | solution.py:507
  13.0 23.5 %collective-permute-start.3 = (bf16[4,512,256]{2,1,0:T(8,128)(2,1)S(1)}, bf16[4,512,256]{2,1,0:T(8,128)(2,1)S(1)}, u32[]{:S(2)}, u32[]{:S(2)}) collective-permute-start(bf16[4,512,256]{2,1,0:T(8,128)(2,1)S(1)} %get-tuple-element.52.rows_ref), channel_id=1, source_target_pairs={{0,2},{1,3},{2,0},{3,1},{4,6},{5,7},{6,4},{7,5},{8,10},{9,11},{10,... | collective-permute-start | bytes 3145736 | tf_op jit(solution)/shard_map/ppermute | solution.py:492
  14.5 25.5 %collective-permute-start.4 = (bf16[2,320,256]{2,1,0:T(8,128)(2,1)S(1)}, bf16[2,320,256]{2,1,0:T(8,128)(2,1)S(1)}, u32[]{:S(2)}, u32[]{:S(2)}) collective-permute-start(bf16[2,320,256]{2,1,0:T(8,128)(2,1)S(1)} %get-tuple-element.53), channel_id=1, source_target_pairs={{0,12},{4,8},{8,4},{12,0},{1,13},{5,9},{9,5},{13,1},{2,14},{6,10},... | collective-permute-start | bytes 983048 | tf_op jit(solution)/shard_map/ppermute | solution.py:507
  16.7 26.1 %collective-permute-start.5 = (bf16[2,320,256]{2,1,0:T(8,128)(2,1)S(1)}, bf16[2,320,256]{2,1,0:T(8,128)(2,1)S(1)}, u32[]{:S(2)}, u32[]{:S(2)}) collective-permute-start(bf16[2,320,256]{2,1,0:T(8,128)(2,1)S(1)} %get-tuple-element.54), channel_id=1, source_target_pairs={{0,8},{4,12},{8,0},{12,4},{1,9},{5,13},{9,1},{13,5},{2,10},{6,14},... | collective-permute-start | bytes 983048 | tf_op jit(solution)/shard_map/ppermute | solution.py:507
  16.7 26.1 %collective-permute-start.6 = (bf16[2,320,256]{2,1,0:T(8,128)(2,1)S(1)}, bf16[2,320,256]{2,1,0:T(8,128)(2,1)S(1)}, u32[]{:S(2)}, u32[]{:S(2)}) collective-permute-start(bf16[2,320,256]{2,1,0:T(8,128)(2,1)S(1)} %get-tuple-element.55), channel_id=1, source_target_pairs={{0,4},{4,0},{8,12},{12,8},{1,5},{5,1},{9,13},{13,9},{2,6},{6,2},{1... | collective-permute-start | bytes 983048 | tf_op jit(solution)/shard_map/ppermute | solution.py:507
  18.9 21.1 %collective-permute-start.7 = (bf16[2,192,256]{2,1,0:T(8,128)(2,1)S(1)}, bf16[2,192,256]{2,1,0:T(8,128)(2,1)S(1)}, u32[]{:S(2)}, u32[]{:S(2)}) collective-permute-start(bf16[2,192,256]{2,1,0:T(8,128)(2,1)S(1)} %get-tuple-element.56), channel_id=1, source_target_pairs={{0,4},{4,0},{8,12},{12,8},{1,5},{5,1},{9,13},{13,9},{2,6},{6,2},{1... | collective-permute-start | bytes 589832 | tf_op jit(solution)/shard_map/ppermute | solution.py:507
  42.8 25.5 %collective-permute-start.9 = (bf16[2,4,512,256]{3,2,1,0:T(8,128)(2,1)S(1)}, bf16[2,4,512,256]{3,2,1,0:T(8,128)(2,1)S(1)}, u32[]{:S(2)}, u32[]{:S(2)}) collective-permute-start(bf16[2,4,512,256]{3,2,1,0:T(8,128)(2,1)S(1)} %pad_maximum_fusion.refs_0_), channel_id=1, source_target_pairs={{0,1},{1,0},{2,3},{3,2},{4,5},{5,4},{6,7},{7,6},{8,9},{9,8},{10,11... | collective-permute-start | bytes 6291464 | tf_op jit(solution)/shard_map/ppermute | solution.py:492
  43.7 24.6 %collective-permute-start.8 = (bf16[4,320,256]{2,1,0:T(8,128)(2,1)S(1)}, bf16[4,320,256]{2,1,0:T(8,128)(2,1)S(1)}, u32[]{:S(2)}, u32[]{:S(2)}) collective-permute-start(bf16[4,320,256]{2,1,0:T(8,128)(2,1)S(1)} %get-tuple-element.65), channel_id=1, source_target_pairs={{0,2},{1,3},{2,0},{3,1},{4,6},{5,7},{6,4},{7,5},{8,10},{9,11},{10,... | collective-permute-start | bytes 1966088 | tf_op jit(solution)/shard_map/ppermute | solution.py:492
  44.3 16.3 %collective-permute-start.10 = (bf16[2,192,256]{2,1,0:T(8,128)(2,1)S(1)}, bf16[2,192,256]{2,1,0:T(8,128)(2,1)S(1)}, u32[]{:S(2)}, u32[]{:S(2)}) collective-permute-start(bf16[2,192,256]{2,1,0:T(8,128)(2,1)S(1)} %get-tuple-element.67), channel_id=1, source_target_pairs={{0,8},{4,12},{8,0},{12,4},{1,9},{5,13},{9,1},{13,5},{2,10},{6,14},... | collective-permute-start | bytes 589832 | tf_op jit(solution)/shard_map/ppermute | solution.py:507
  44.6 18.3 %collective-permute-start.12 = (bf16[2,192,256]{2,1,0:T(8,128)(2,1)S(1)}, bf16[2,192,256]{2,1,0:T(8,128)(2,1)S(1)}, u32[]{:S(2)}, u32[]{:S(2)}) collective-permute-start(bf16[2,192,256]{2,1,0:T(8,128)(2,1)S(1)} %get-tuple-element.69), channel_id=1, source_target_pairs={{0,12},{4,8},{8,4},{12,0},{1,13},{5,9},{9,5},{13,1},{2,14},{6,10},... | collective-permute-start | bytes 589832 | tf_op jit(solution)/shard_map/ppermute | solution.py:507
  61.4 6.9 %collective-permute-start.11 = (bf16[2,192,256]{2,1,0:T(8,128)(2,1)S(1)}, bf16[2,192,256]{2,1,0:T(8,128)(2,1)S(1)}, u32[]{:S(2)}, u32[]{:S(2)}) collective-permute-start(bf16[2,192,256]{2,1,0:T(8,128)(2,1)S(1)} %select.4.refs_9_.refs_2_), channel_id=1, source_target_pairs={{0,2},{1,3},{2,0},{3,1},{4,6},{5,7},{6,4},{7,5},{8,10},{9,11},{10,... | collective-permute-start | bytes 589832 | tf_op jit(solution)/shard_map/ppermute | solution.py:492
  62.9 8.2 %collective-permute-start.13 = (bf16[2,320,256]{2,1,0:T(8,128)(2,1)S(1)}, bf16[2,320,256]{2,1,0:T(8,128)(2,1)S(1)}, u32[]{:S(2)}, u32[]{:S(2)}) collective-permute-start(bf16[2,320,256]{2,1,0:T(8,128)(2,1)S(1)} %get-tuple-element.78.refs_2_.refs_0_), channel_id=1, source_target_pairs={{0,1},{1,0},{2,3},{3,2},{4,5},{5,4},{6,7},{7,6},{8,9},{9,8},{10,11... | collective-permute-start | bytes 983048 | tf_op jit(solution)/shard_map/ppermute | solution.py:492
  63.0 8.2 %collective-permute-start.14 = (bf16[2,320,256]{2,1,0:T(8,128)(2,1)S(1)}, bf16[2,320,256]{2,1,0:T(8,128)(2,1)S(1)}, u32[]{:S(2)}, u32[]{:S(2)}) collective-permute-start(bf16[2,320,256]{2,1,0:T(8,128)(2,1)S(1)} %get-tuple-element.79.refs_3_.refs_1_), channel_id=1, source_target_pairs={{0,1},{1,0},{2,3},{3,2},{4,5},{5,4},{6,7},{7,6},{8,9},{9,8},{10,11... | collective-permute-start | bytes 983048 | tf_op jit(solution)/shard_map/ppermute | solution.py:492
  69.1 2.6 %collective-permute-start.16 = (bf16[2,320,256]{2,1,0:T(8,128)(2,1)S(1)}, bf16[2,320,256]{2,1,0:T(8,128)(2,1)S(1)}, u32[]{:S(2)}, u32[]{:S(2)}) collective-permute-start(bf16[2,320,256]{2,1,0:T(8,128)(2,1)S(1)} %get-tuple-element.102), channel_id=1, source_target_pairs={{0,1},{1,0},{2,3},{3,2},{4,5},{5,4},{6,7},{7,6},{8,9},{9,8},{10,11... | collective-permute-start | bytes 983048 | tf_op jit(solution)/shard_map/ppermute | solution.py:492
  69.2 2.5 %collective-permute-start.15 = (bf16[2,320,256]{2,1,0:T(8,128)(2,1)S(1)}, bf16[2,320,256]{2,1,0:T(8,128)(2,1)S(1)}, u32[]{:S(2)}, u32[]{:S(2)}) collective-permute-start(bf16[2,320,256]{2,1,0:T(8,128)(2,1)S(1)} %get-tuple-element.103), channel_id=1, source_target_pairs={{0,1},{1,0},{2,3},{3,2},{4,5},{5,4},{6,7},{7,6},{8,9},{9,8},{10,11... | collective-permute-start | bytes 983048 | tf_op jit(solution)/shard_map/ppermute | solution.py:492
  69.7 6.9 %collective-permute-start.17 = (bf16[2,192,256]{2,1,0:T(8,128)(2,1)S(1)}, bf16[2,192,256]{2,1,0:T(8,128)(2,1)S(1)}, u32[]{:S(2)}, u32[]{:S(2)}) collective-permute-start(bf16[2,192,256]{2,1,0:T(8,128)(2,1)S(1)} %select.5.refs_10_.refs_3_), channel_id=1, source_target_pairs={{0,2},{1,3},{2,0},{3,1},{4,6},{5,7},{6,4},{7,5},{8,10},{9,11},{10,... | collective-permute-start | bytes 589832 | tf_op jit(solution)/shard_map/ppermute | solution.py:492
  71.2 5.9 %collective-permute-start.20 = (bf16[2,192,256]{2,1,0:T(8,128)(2,1)S(1)}, bf16[2,192,256]{2,1,0:T(8,128)(2,1)S(1)}, u32[]{:S(2)}, u32[]{:S(2)}) collective-permute-start(bf16[2,192,256]{2,1,0:T(8,128)(2,1)S(1)} %collective-permute-done.11.refs_11_), channel_id=1, source_target_pairs={{0,1},{1,0},{2,3},{3,2},{4,5},{5,4},{6,7},{7,6},{8,9},{9,8},{10,11... | collective-permute-start | bytes 589832 | tf_op jit(solution)/shard_map/ppermute | solution.py:492
  71.2 5.9 %collective-permute-start.18 = (bf16[2,192,256]{2,1,0:T(8,128)(2,1)S(1)}, bf16[2,192,256]{2,1,0:T(8,128)(2,1)S(1)}, u32[]{:S(2)}, u32[]{:S(2)}) collective-permute-start(bf16[2,192,256]{2,1,0:T(8,128)(2,1)S(1)} %select.4.refs_9_.refs_2_), channel_id=1, source_target_pairs={{0,1},{1,0},{2,3},{3,2},{4,5},{5,4},{6,7},{7,6},{8,9},{9,8},{10,11... | collective-permute-start | bytes 589832 | tf_op jit(solution)/shard_map/ppermute | solution.py:492
  76.5 1.4 %collective-permute-start.21 = (bf16[2,192,256]{2,1,0:T(8,128)(2,1)S(1)}, bf16[2,192,256]{2,1,0:T(8,128)(2,1)S(1)}, u32[]{:S(2)}, u32[]{:S(2)}) collective-permute-start(bf16[2,192,256]{2,1,0:T(8,128)(2,1)S(1)} %collective-permute-done.17.refs_12_), channel_id=1, source_target_pairs={{0,1},{1,0},{2,3},{3,2},{4,5},{5,4},{6,7},{7,6},{8,9},{9,8},{10,11... | collective-permute-start | bytes 589832 | tf_op jit(solution)/shard_map/ppermute | solution.py:492
  76.5 1.7 %collective-permute-start.19 = (bf16[2,192,256]{2,1,0:T(8,128)(2,1)S(1)}, bf16[2,192,256]{2,1,0:T(8,128)(2,1)S(1)}, u32[]{:S(2)}, u32[]{:S(2)}) collective-permute-start(bf16[2,192,256]{2,1,0:T(8,128)(2,1)S(1)} %select.5.refs_10_.refs_3_), channel_id=1, source_target_pairs={{0,1},{1,0},{2,3},{3,2},{4,5},{5,4},{6,7},{7,6},{8,9},{9,8},{10,11... | collective-permute-start | bytes 589832 | tf_op jit(solution)/shard_map/ppermute | solution.py:492
  80.9 5.9 %collective-permute-start.22 = (f32[8,512]{1,0:T(8,128)S(1)}, f32[8,512]{1,0:T(8,128)S(1)}, u32[]{:S(2)}, u32[]{:S(2)}) collective-permute-start(f32[8,512]{1,0:T(8,128)S(1)} %get-tuple-element.95), channel_id=1, source_target_pairs={{0,8},{4,12},{8,0},{12,4},{1,9},{5,13},{9,1},{13,5},{2,10},{6,14},... | collective-permute-start | bytes 49160 | tf_op jit(solution)/shard_map/ppermute | solution.py:507
  81.0 5.8 %collective-permute-start.23 = (f32[8,512]{1,0:T(8,128)S(1)}, f32[8,512]{1,0:T(8,128)S(1)}, u32[]{:S(2)}, u32[]{:S(2)}) collective-permute-start(f32[8,512]{1,0:T(8,128)S(1)} %get-tuple-element.96), channel_id=1, source_target_pairs={{0,12},{4,8},{8,4},{12,0},{1,13},{5,9},{9,5},{13,1},{2,14},{6,10},... | collective-permute-start | bytes 49160 | tf_op jit(solution)/shard_map/ppermute | solution.py:507
  82.3 4.5 %collective-permute-start.24 = (f32[8,512]{1,0:T(8,128)S(1)}, f32[8,512]{1,0:T(8,128)S(1)}, u32[]{:S(2)}, u32[]{:S(2)}) collective-permute-start(f32[8,512]{1,0:T(8,128)S(1)} %get-tuple-element.97), channel_id=1, source_target_pairs={{0,4},{4,0},{8,12},{12,8},{1,5},{5,1},{9,13},{13,9},{2,6},{6,2},{1... | collective-permute-start | bytes 49160 | tf_op jit(solution)/shard_map/ppermute | solution.py:507

commit v22 on v17

--- a/solution.py
+++ b/solution.py
@@ -238,10 +238,9 @@
 
 
 def last_kernel(window, counts, wide_count, me_ref, pairs_ref, *refs):
-    square_in, mass_in, sums_in = refs[-6 - wide_count : -3 - wide_count]
-    kernel_ref, mass_ref, row_ref = refs[-3 - wide_count : -wide_count]
-    shares = refs[-wide_count:]
-    for ref in (row_ref, *shares):
+    square_in, mass_in, sums_in, kernel_ref, mass_ref, row_ref, near_ref, far_ref = refs[-8:]
+    half = wide_count // 2
+    for ref in (row_ref, near_ref, far_ref):
         ref[...] = jnp.zeros_like(ref)
     all_rows, chunks = window_parts(counts, refs)
     for pair in range(square_in.shape[0]):
@@ -254,8 +253,9 @@
         row_ref[pl.ds(pairs_ref[0, pair] & 7, 1)] += jnp.sum(mass.T, axis=0, keepdims=True)
         col = pairs_ref[1, pair]
         apart = (col >> 3) ^ me_ref[0]
-        for other, ref in zip([*others(wide_count), 0], shares):
-            ref[pl.ds(col & 7, 1)] += jnp.where(apart == other, sums, 0.0)
+        for share, ref in enumerate((near_ref, far_ref)):
+            here = jnp.where((apart >= half) == (share == 1), sums, 0.0)
+            ref[apart & (half - 1), pl.ds(col & 7, 1)] += here
 
 
 def estimate(pair_count, size):
@@ -301,12 +301,12 @@
     shapes = [
         pltpu.VMEM((pair_count, BR, size), jnp.bfloat16),
         pltpu.VMEM((pair_count, BR, LANES), jnp.float32),
-    ] + [by_block] * (1 + wide_count)
+    ] + [by_block] + [pltpu.VMEM((wide_count // 2, BLK_DEV, BR), jnp.float32)] * 2
     args = operands(rows)
     for chunk, _, _ in segments(window):
         args += operands(cols[chunk])
     args += [square, mass, sums]
-    kernel, mass, row_sums, *shares = pl.pallas_call(
+    kernel, mass, row_sums, near, far = pl.pallas_call(
         functools.partial(last_kernel, window, piece_counts(window, cols), wide_count),
         out_shape=shapes,
         in_specs=[smem(), smem()] + [vmem()] * len(args),
@@ -315,7 +315,7 @@
         cost_estimate=estimate(pair_count, size),
         name="last_window",
     )(me, in_hbm(pairs), *[in_vmem(x) for x in args])
-    return kernel, mass, row_sums, shares
+    return kernel, mass, row_sums, near, far
 
 
 def keep_kernel(pairs_ref, block_ref, blocks_ref, out_ref, own_ref, sems):
@@ -431,12 +431,26 @@
     )(in_hbm(pairs), *args, in_hbm(kept))
 
 
-def weight_kernel(*refs):
-    out_ref = refs[-1]
-    mass = refs[0][...]
-    for ref in refs[1:-1]:
-        mass = mass + ref[...]
-    weight = 1.0 / (1.0 + mass / BR)
+def fold_kernel(near_ref, came_ref, low_ref, high_ref):
+    half = low_ref.shape[0]
+    low_ref[...] = near_ref[:half] + came_ref[:half]
+    high_ref[...] = near_ref[half:] + came_ref[half:]
+
+
+def fold(near, came):
+    half = pltpu.VMEM((near.shape[0] // 2, *near.shape[1:]), jnp.float32)
+    return pl.pallas_call(
+        fold_kernel,
+        out_shape=[half, half],
+        in_specs=[vmem(), vmem()],
+        out_specs=[vmem(), vmem()],
+        compiler_params=params(4),
+        name="fold",
+    )(in_vmem(near), in_vmem(came))
+
+
+def weight_kernel(rows_ref, near_ref, came_ref, out_ref):
+    weight = 1.0 / (1.0 + (rows_ref[...] + near_ref[0] + came_ref[0]) / BR)
     parts = BR // LANES
     for block in range(BLK_DEV):
         for part in range(parts):
@@ -444,16 +458,23 @@
             out_ref[block * parts + part : block * parts + part + 1] = weight[block : block + 1, lanes]
 
 
-def block_weights(sums):
+def block_weights(row_sums, near, far, beside):
+    step = lax.axis_size("wide") // 2
+    while step > 1:
+        (came,) = to_wide([far], [step])
+        came, beside = lax.optimization_barrier((came, beside))
+        near, far = fold(near, came)
+        step //= 2
+    (came,) = to_wide([far], [1])
     out = pl.pallas_call(
         weight_kernel,
         out_shape=jax.ShapeDtypeStruct((BLK_DEV * BR // LANES, LANES), jnp.float32),
-        in_specs=[vmem()] * len(sums),
+        in_specs=[vmem()] * 3,
         out_specs=vmem(),
         compiler_params=params(4),
         name="weights",
-    )(*[in_vmem(x) for x in sums])
-    return out.reshape(BLK_DEV * BR)
+    )(*[in_vmem(x) for x in (row_sums, near, came)])
+    return out.reshape(BLK_DEV * BR), beside
 
 
 def hop(parts, step):
@@ -514,12 +535,11 @@
     cols_b, carry = fixed((cols_b, carry))
     cols_b = cols_b + last_b + hop(cols_b[1:], 1)
     square, mass, total, sums = carry
-    kernel, mass, row_sums, shares = last_window(
+    kernel, mass, row_sums, near_sums, far_sums = last_window(
         me, pairs, rows, [cols_a, cols_b], square, mass, sums, wide_count
     )
-    came = to_wide(shares[:-1], apart)
     mean = means(pairs, row_slices, kernel, mass, total, [cols_a, cols_b], kept)
-    weights = block_weights([row_sums, shares[-1], *came])
+    weights, mean = block_weights(row_sums, near_sums, far_sums, mean)
     return weights, mean.reshape(BLK_DEV * BR, feat)
 
 

time: 86.4 us -> 87.9 us (1.017)
  waiting for transfers between devices: 44.2 us -> 49.7 us
  starting transfers between devices: 21.6 us -> 17.6 us
    ppermute x12 -> x11, waiting for transfers between devices: 26.5 us -> 31.8 us  [to_wide(): lax.ppermute(piece, 'wide', [(i, i ^ other) for i in range(count)])]
    ppermute x12 -> x11, starting transfers between devices: 17.2 us -> 13.3 us  [to_wide(): lax.ppermute(piece, 'wide', [(i, i ^ other) for i in range(count)])]
  transfers between devices with their start and end apart: 22 -> 21, of which waited for: 12 -> 13; matrix products, arithmetic and copies ran while one was open for 0% -> 0% of each run, Pallas kernels for 15% -> 15%
where the time goes in v22:
time: 87.9 us; the launch traced here: 87.5 us
  waiting for transfers between devices  49.7 us (57%)
  Pallas kernels  19.2 us (22%)
  starting transfers between devices  17.6 us (20%)
    ppermute x11, waiting for transfers between devices, to_wide(): lax.ppermute(piece, 'wide', [(i, i ^ other) for i in range(count)])  31.8 us
    ppermute x10, waiting for transfers between devices, hop(): lax.ppermute(piece, 'narrow', perm)  17.9 us
    ppermute x11, starting transfers between devices, to_wide(): lax.ppermute(piece, 'wide', [(i, i ^ other) for i in range(count)])  13.3 us
    pallas_call x1, Pallas kernels, keep(): pl.pallas_call(keep_kernel, out_shape=[pltpu.HBM(blocks.shape, blocks.dty...  6.02 us
    ppermute x10, starting transfers between devices, hop(): lax.ppermute(piece, 'narrow', perm)  4.37 us
    pallas_call x1, Pallas kernels, first_window(): pl.pallas_call(functools.partial(first_kernel, window, piece_counts(windo...  3.1 us
    pallas_call x1, Pallas kernels, pack(): pl.pallas_call(functools.partial(pack_kernel, wide_count, pair_count, cap...  2.8 us
    pallas_call x1, Pallas kernels, last_window(): pl.pallas_call(functools.partial(last_kernel, window, piece_counts(window...  2.63 us
  transfers between devices with their start and end apart: 21, of which 13 were waited for; matrix products, arithmetic and copies ran while one was open for 0% of the time, Pallas kernels for 15%

profile of v22, /device:TPU:0, one launch (start us, length us, event | category | flops | bytes accessed | tf_op | source)
XLA Modules:
  0.0 87.5 jit_solution(14806748380284211420)
XLA Ops:
  0.6 4.1 %collective-permute-start.2 = (s32[2,4]{1,0:T(2,128)}, s32[2,4]{1,0:T(2,128)S(1)}, u32[]{:S(2)}, u32[]{:S(2)}) collective-permute-start(s32[2,4]{1,0:T(2,128)} %bitcast.13), channel_id=1, source_target_pairs={{0,8},{4,12},{8,0},{12,4},{1,9},{5,13},{9,1},{13,5},{2,10},{6,14},... | collective-permute-start | bytes 104 | tf_op jit(solution)/shard_map/ppermute | solution.py:498
  4.7 1.3 %collective-permute-start.1 = (s32[2,4]{1,0:T(2,128)}, s32[2,4]{1,0:T(2,128)S(1)}, u32[]{:S(2)}, u32[]{:S(2)}) collective-permute-start(s32[2,4]{1,0:T(2,128)} %bitcast.14), channel_id=1, source_target_pairs={{0,12},{4,8},{8,4},{12,0},{1,13},{5,9},{9,5},{13,1},{2,14},{6,10},... | collective-permute-start | bytes 104 | tf_op jit(solution)/shard_map/ppermute | solution.py:498
  6.1 0.2 collective-permute-start
  6.5 3.8 %collective-permute-done.1.refs_1_ = s32[2,4]{1,0:T(2,128)S(1)} collective-permute-done((s32[2,4]{1,0:T(2,128)}, s32[2,4]{1,0:T(2,128)S(1)}, u32[]{:S(2)}, u32[]{:S(2)}) %collective-permute-start.1) | collective-permute-done | bytes 64 | tf_op jit(solution)/shard_map/ppermute | solution.py:498
  10.3 2.8 %pack.1 = (bf16[2,336,256]{2,1,0:T(8,128)(2,1)S(1)}, bf16[2,336,256]{2,1,0:T(8,128)(2,1)S(1)}, bf16[2,336,256]{2,1,0:T(8,128)(2,1)S(1)}, bf16[2,176,256]{2,1,0:T...) custom-call(s32[1]{0:T(128)} %bitcast.me_ref, ...), custom_call_target="tpu_custom_call" | custom-call | tf_op jit(solution)/shard_map/pack/pallas_call | solution.py:90
  13.1 1.6 %collective-permute-start.3 = (bf16[4,512,256]{2,1,0:T(8,128)(2,1)S(1)}, bf16[4,512,256]{2,1,0:T(8,128)(2,1)S(1)}, u32[]{:S(2)}, u32[]{:S(2)}) collective-permute-start(bf16[4,512,256]{2,1,0:T(8,128)(2,1)S(1)} %get-tuple-element.47.rows_ref), channel_id=1, source_target_pairs={{0,2},{1,3},{2,0},{3,1},{4,6},{5,7},{6,4},{7,5},{8,10},{9,11},{10,... | collective-permute-start | bytes 3145736 | tf_op jit(solution)/shard_map/ppermute | solution.py:483
  14.7 1.9 %collective-permute-start.4 = (bf16[2,336,256]{2,1,0:T(8,128)(2,1)S(1)}, bf16[2,336,256]{2,1,0:T(8,128)(2,1)S(1)}, u32[]{:S(2)}, u32[]{:S(2)}) collective-permute-start(bf16[2,336,256]{2,1,0:T(8,128)(2,1)S(1)} %get-tuple-element.48), channel_id=1, source_target_pairs={{0,12},{4,8},{8,4},{12,0},{1,13},{5,9},{9,5},{13,1},{2,14},{6,10},... | collective-permute-start | bytes 1032200 | tf_op jit(solution)/shard_map/ppermute | solution.py:498
  16.6 2.5 %collective-permute-start.6 = (bf16[2,336,256]{2,1,0:T(8,128)(2,1)S(1)}, bf16[2,336,256]{2,1,0:T(8,128)(2,1)S(1)}, u32[]{:S(2)}, u32[]{:S(2)}) collective-permute-start(bf16[2,336,256]{2,1,0:T(8,128)(2,1)S(1)} %get-tuple-element.50), channel_id=1, source_target_pairs={{0,4},{4,0},{8,12},{12,8},{1,5},{5,1},{9,13},{13,9},{2,6},{6,2},{1... | collective-permute-start | bytes 1032200 | tf_op jit(solution)/shard_map/ppermute | solution.py:498
  19.1 6.0 %keep.1 = (bf16[8,512,256]{2,1,0:T(8,128)(2,1)}, bf16[4,512,256]{2,1,0:T(8,128)(2,1)S(1)}) custom-call(s32[2,4]{1,0:T(2,128)} %bitcast.17, bf16[8,512,256]{2,1,0:T(8,128)(2,1)} %bitcast.9, bf16[8,512,256]{2,1,0:T(8,128)(2,1)} %bitcast.10), custom_call_target="tpu_custom_call" | custom-call | tf_op jit(solution)/shard_map/keep/pallas_call | solution.py:345
  25.1 11.5 %collective-permute-done.3 = bf16[4,512,256]{2,1,0:T(8,128)(2,1)S(1)} collective-permute-done((bf16[4,512,256]{2,1,0:T(8,128)(2,1)S(1)}, bf16[4,512,256]{2,1,0:T(8,128)(2,1)S(1)}, u32[]{:S(2)}, u32[]{:S(2)}) %collective-permute-start.3) | collective-permute-done | bytes 1048608 | tf_op jit(solution)/shard_map/ppermute | solution.py:483
  36.7 0.2 pad_maximum_fusion.refs_0_
  36.8 3.8 %collective-permute-done.7.refs_2_ = bf16[2,176,256]{2,1,0:T(8,128)(2,1)S(1)} collective-permute-done((bf16[2,176,256]{2,1,0:T(8,128)(2,1)S(1)}, bf16[2,176,256]{2,1,0:T(8,128)(2,1)S(1)}, u32[]{:S(2)}, u32[]{:S(2)}) %collective-permute-start.7) | collective-permute-done | bytes 180256 | tf_op jit(solution)/shard_map/ppermute | solution.py:498
  40.7 3.5 %collective-permute-done.5.refs_1_ = bf16[2,336,256]{2,1,0:T(8,128)(2,1)S(1)} collective-permute-done((bf16[2,336,256]{2,1,0:T(8,128)(2,1)S(1)}, bf16[2,336,256]{2,1,0:T(8,128)(2,1)S(1)}, u32[]{:S(2)}, u32[]{:S(2)}) %collective-permute-start.5) | collective-permute-done | bytes 344096 | tf_op jit(solution)/shard_map/ppermute | solution.py:498
  44.2 0.9 select.2
  45.1 0.6 collective-permute-start.8
  45.7 2.4 %collective-permute-start.10 = (bf16[2,176,256]{2,1,0:T(8,128)(2,1)S(1)}, bf16[2,176,256]{2,1,0:T(8,128)(2,1)S(1)}, u32[]{:S(2)}, u32[]{:S(2)}) collective-permute-start(bf16[2,176,256]{2,1,0:T(8,128)(2,1)S(1)} %get-tuple-element.62), channel_id=1, source_target_pairs={{0,12},{4,8},{8,4},{12,0},{1,13},{5,9},{9,5},{13,1},{2,14},{6,10},... | collective-permute-start | bytes 540680 | tf_op jit(solution)/shard_map/ppermute | solution.py:498
  48.1 6.8 %collective-permute-done.10.refs_0_ = bf16[2,176,256]{2,1,0:T(8,128)(2,1)S(1)} collective-permute-done((bf16[2,176,256]{2,1,0:T(8,128)(2,1)S(1)}, bf16[2,176,256]{2,1,0:T(8,128)(2,1)S(1)}, u32[]{:S(2)}, u32[]{:S(2)}) %collective-permute-start.10) | collective-permute-done | bytes 180256 | tf_op jit(solution)/shard_map/ppermute | solution.py:498
  55.0 8.0 %collective-permute-done.11.refs_1_ = bf16[2,176,256]{2,1,0:T(8,128)(2,1)S(1)} collective-permute-done((bf16[2,176,256]{2,1,0:T(8,128)(2,1)S(1)}, bf16[2,176,256]{2,1,0:T(8,128)(2,1)S(1)}, u32[]{:S(2)}, u32[]{:S(2)}) %collective-permute-start.11) | collective-permute-done | bytes 180256 | tf_op jit(solution)/shard_map/ppermute | solution.py:498
  63.0 0.8 select.3.refs_9_.refs_2_
  63.8 1.6 %collective-permute-start.16 = (bf16[4,176,256]{2,1,0:T(8,128)(2,1)S(1)}, bf16[4,176,256]{2,1,0:T(8,128)(2,1)S(1)}, u32[]{:S(2)}, u32[]{:S(2)}) collective-permute-start(bf16[4,176,256]{2,1,0:T(8,128)(2,1)S(1)} %select.3.refs_9_.refs_2_), channel_id=1, source_target_pairs={{0,2},{1,3},{2,0},{3,1},{4,6},{5,7},{6,4},{7,5},{8,10},{9,11},{10,... | collective-permute-start | bytes 1081352 | tf_op jit(solution)/shard_map/ppermute | solution.py:483
  65.5 0.5 collective-permute-start.14
  66.1 1.1 %collective-permute-done.15.refs_8_ = bf16[2,336,256]{2,1,0:T(8,128)(2,1)S(1)} collective-permute-done((bf16[2,336,256]{2,1,0:T(8,128)(2,1)S(1)}, bf16[2,336,256]{2,1,0:T(8,128)(2,1)S(1)}, u32[]{:S(2)}, u32[]{:S(2)}) %collective-permute-start.15) | collective-permute-done | bytes 344096 | tf_op jit(solution)/shard_map/ppermute | solution.py:483
  67.1 0.5 collective-permute-done.14.refs_7_
  67.6 3.1 %first_window.1 = (f32[4,512,128]{2,1,0:T(8,128)S(1)}, f32[4,512,128]{2,1,0:T(8,128)S(1)}, f32[4,512,256]{2,1,0:T(8,128)S(1)}, f32[4,256]{1,0:T(4,128)S(1)}) custom-call(bf16[2,4,512,256]{3,2,1,0:T(8,128)(2,1)S(1)} %pad_maximum_fusion.refs_0_, bf16[2,4,512,256]{3,2,1,0:T(8,128)(2,1)S(1)} %collective-permute-done.9.refs_1_, ...), custom_call_target="tpu_custom_call" | custom-call | tf_op jit(solution)/shard_map/first_window/pallas_call | solution.py:285
  70.7 3.2 %collective-permute-done.16.refs_10_ = bf16[4,176,256]{2,1,0:T(8,128)(2,1)S(1)} collective-permute-done((bf16[4,176,256]{2,1,0:T(8,128)(2,1)S(1)}, bf16[4,176,256]{2,1,0:T(8,128)(2,1)S(1)}, u32[]{:S(2)}, u32[]{:S(2)}) %collective-permute-start.16) | collective-permute-done | bytes 360480 | tf_op jit(solution)/shard_map/ppermute | solution.py:483
  73.9 1.7 %collective-permute-done.18.refs_12_ = bf16[4,176,256]{2,1,0:T(8,128)(2,1)S(1)} collective-permute-done((bf16[4,176,256]{2,1,0:T(8,128)(2,1)S(1)}, bf16[4,176,256]{2,1,0:T(8,128)(2,1)S(1)}, u32[]{:S(2)}, u32[]{:S(2)}) %collective-permute-start.18) | collective-permute-done | bytes 360480 | tf_op jit(solution)/shard_map/ppermute | solution.py:483
  75.6 2.6 %last_window.1 = (bf16[4,512,256]{2,1,0:T(8,128)(2,1)S(1)}, f32[4,512,128]{2,1,0:T(8,128)S(1)}, f32[8,512]{1,0:T(8,128)S(1)}, f32[2,8,512]{2,1,0:T(8,128)S(1)}, f32[2,8,512]{2,1,0:T(8,128)S(1)}) custom-call(s32[1]{0:T(128)} %bitcast.me_ref, s32[2,4]{1,0:T(2,128)} %bitcast.20, bf16[2,4,512,256]{3,2,1,0:T(8,128)(2,1)S(1)} %pad_maximum_fusion.refs_0_, ...), custom_call_target="tpu_custom_call" | custom-call | flops 1073741824 | bytes 8388608 | tf_op jit(solution)/shard_map/last_window/pallas_call | solution.py:309
  78.3 2.3 %means.1 = bf16[8,512,256]{2,1,0:T(8,128)(2,1)} custom-call(s32[2,4]{1,0:T(2,128)} %bitcast.21, bf16[4,512,256]{2,1,0:T(8,128)(2,1)S(1)} %get-tuple-element.47.rows_ref, bf16[4,512,256]{2,1,0:T(8,128)(2,1)S(1)} %get-tuple-element.84.kernel_ref, f32[4,512,128]{2,1,0:T(8,128)S(1)} %get-tuple-element.85.mass_ref, ...), custom_call_target="tpu_custom_call", output_to_operand_aliasing={{}: (8, {})} | custom-call | flops 536870912 | bytes 8388608 | tf_op jit(solution)/shard_map/means/pallas_call | solution.py:414
  80.6 2.5 %collective-permute-done.19.came_ref = f32[2,8,512]{2,1,0:T(8,128)S(1)} collective-permute-done((f32[2,8,512]{2,1,0:T(8,128)S(1)}, f32[2,8,512]{2,1,0:T(8,128)S(1)}, u32[]{:S(2)}, u32[]{:S(2)}) %collective-permute-start.19) | collective-permute-done | bytes 32800 | tf_op jit(solution)/shard_map/ppermute | solution.py:498
  83.1 0.7 collective-permute-start.20
  83.8 3.1 %collective-permute-done.20.came_ref = f32[1,8,512]{2,1,0:T(8,128)S(1)} collective-permute-done((f32[1,8,512]{2,1,0:T(8,128)S(1)}, f32[1,8,512]{2,1,0:T(8,128)S(1)}, u32[]{:S(2)}, u32[]{:S(2)}) %collective-permute-start.20) | collective-permute-done | bytes 16416 | tf_op jit(solution)/shard_map/ppermute | solution.py:498
  86.8 0.6 weights.1
  (21 shorter events, 0.5 us)
Async XLA Ops:
  0.6 5.9 %collective-permute-start.2 = (s32[2,4]{1,0:T(2,128)}, s32[2,4]{1,0:T(2,128)S(1)}, u32[]{:S(2)}, u32[]{:S(2)}) collective-permute-start(s32[2,4]{1,0:T(2,128)} %bitcast.13), channel_id=1, source_target_pairs={{0,8},{4,12},{8,0},{12,4},{1,9},{5,13},{9,1},{13,5},{2,10},{6,14},... | collective-permute-start | bytes 104 | tf_op jit(solution)/shard_map/ppermute | solution.py:498
  4.7 5.6 %collective-permute-start.1 = (s32[2,4]{1,0:T(2,128)}, s32[2,4]{1,0:T(2,128)S(1)}, u32[]{:S(2)}, u32[]{:S(2)}) collective-permute-start(s32[2,4]{1,0:T(2,128)} %bitcast.14), channel_id=1, source_target_pairs={{0,12},{4,8},{8,4},{12,0},{1,13},{5,9},{9,5},{13,1},{2,14},{6,10},... | collective-permute-start | bytes 104 | tf_op jit(solution)/shard_map/ppermute | solution.py:498
  6.1 4.2 %collective-permute-start = (s32[2,4]{1,0:T(2,128)}, s32[2,4]{1,0:T(2,128)S(1)}, u32[]{:S(2)}, u32[]{:S(2)}) collective-permute-start(s32[2,4]{1,0:T(2,128)} %bitcast.15), channel_id=1, source_target_pairs={{0,4},{4,0},{8,12},{12,8},{1,5},{5,1},{9,13},{13,9},{2,6},{6,2},{1... | collective-permute-start | bytes 104 | tf_op jit(solution)/shard_map/ppermute | solution.py:498
  13.1 23.5 %collective-permute-start.3 = (bf16[4,512,256]{2,1,0:T(8,128)(2,1)S(1)}, bf16[4,512,256]{2,1,0:T(8,128)(2,1)S(1)}, u32[]{:S(2)}, u32[]{:S(2)}) collective-permute-start(bf16[4,512,256]{2,1,0:T(8,128)(2,1)S(1)} %get-tuple-element.47.rows_ref), channel_id=1, source_target_pairs={{0,2},{1,3},{2,0},{3,1},{4,6},{5,7},{6,4},{7,5},{8,10},{9,11},{10,... | collective-permute-start | bytes 3145736 | tf_op jit(solution)/shard_map/ppermute | solution.py:483
  14.7 26.0 %collective-permute-start.4 = (bf16[2,336,256]{2,1,0:T(8,128)(2,1)S(1)}, bf16[2,336,256]{2,1,0:T(8,128)(2,1)S(1)}, u32[]{:S(2)}, u32[]{:S(2)}) collective-permute-start(bf16[2,336,256]{2,1,0:T(8,128)(2,1)S(1)} %get-tuple-element.48), channel_id=1, source_target_pairs={{0,12},{4,8},{8,4},{12,0},{1,13},{5,9},{9,5},{13,1},{2,14},{6,10},... | collective-permute-start | bytes 1032200 | tf_op jit(solution)/shard_map/ppermute | solution.py:498
  16.6 27.6 %collective-permute-start.5 = (bf16[2,336,256]{2,1,0:T(8,128)(2,1)S(1)}, bf16[2,336,256]{2,1,0:T(8,128)(2,1)S(1)}, u32[]{:S(2)}, u32[]{:S(2)}) collective-permute-start(bf16[2,336,256]{2,1,0:T(8,128)(2,1)S(1)} %get-tuple-element.49), channel_id=1, source_target_pairs={{0,8},{4,12},{8,0},{12,4},{1,9},{5,13},{9,1},{13,5},{2,10},{6,14},... | collective-permute-start | bytes 1032200 | tf_op jit(solution)/shard_map/ppermute | solution.py:498
  16.6 27.6 %collective-permute-start.6 = (bf16[2,336,256]{2,1,0:T(8,128)(2,1)S(1)}, bf16[2,336,256]{2,1,0:T(8,128)(2,1)S(1)}, u32[]{:S(2)}, u32[]{:S(2)}) collective-permute-start(bf16[2,336,256]{2,1,0:T(8,128)(2,1)S(1)} %get-tuple-element.50), channel_id=1, source_target_pairs={{0,4},{4,0},{8,12},{12,8},{1,5},{5,1},{9,13},{13,9},{2,6},{6,2},{1... | collective-permute-start | bytes 1032200 | tf_op jit(solution)/shard_map/ppermute | solution.py:498
  19.1 21.6 %collective-permute-start.7 = (bf16[2,176,256]{2,1,0:T(8,128)(2,1)S(1)}, bf16[2,176,256]{2,1,0:T(8,128)(2,1)S(1)}, u32[]{:S(2)}, u32[]{:S(2)}) collective-permute-start(bf16[2,176,256]{2,1,0:T(8,128)(2,1)S(1)} %get-tuple-element.51), channel_id=1, source_target_pairs={{0,4},{4,0},{8,12},{12,8},{1,5},{5,1},{9,13},{13,9},{2,6},{6,2},{1... | collective-permute-start | bytes 540680 | tf_op jit(solution)/shard_map/ppermute | solution.py:498
  44.2 18.8 %collective-permute-start.9 = (bf16[2,4,512,256]{3,2,1,0:T(8,128)(2,1)S(1)}, bf16[2,4,512,256]{3,2,1,0:T(8,128)(2,1)S(1)}, u32[]{:S(2)}, u32[]{:S(2)}) collective-permute-start(bf16[2,4,512,256]{3,2,1,0:T(8,128)(2,1)S(1)} %pad_maximum_fusion.refs_0_), channel_id=1, source_target_pairs={{0,1},{1,0},{2,3},{3,2},{4,5},{5,4},{6,7},{7,6},{8,9},{9,8},{10,11... | collective-permute-start | bytes 6291464 | tf_op jit(solution)/shard_map/ppermute | solution.py:483
  45.1 17.9 %collective-permute-start.8 = (bf16[4,336,256]{2,1,0:T(8,128)(2,1)S(1)}, bf16[4,336,256]{2,1,0:T(8,128)(2,1)S(1)}, u32[]{:S(2)}, u32[]{:S(2)}) collective-permute-start(bf16[4,336,256]{2,1,0:T(8,128)(2,1)S(1)} %get-tuple-element.60), channel_id=1, source_target_pairs={{0,2},{1,3},{2,0},{3,1},{4,6},{5,7},{6,4},{7,5},{8,10},{9,11},{10,... | collective-permute-start | bytes 2064392 | tf_op jit(solution)/shard_map/ppermute | solution.py:483
  45.7 9.3 %collective-permute-start.10 = (bf16[2,176,256]{2,1,0:T(8,128)(2,1)S(1)}, bf16[2,176,256]{2,1,0:T(8,128)(2,1)S(1)}, u32[]{:S(2)}, u32[]{:S(2)}) collective-permute-start(bf16[2,176,256]{2,1,0:T(8,128)(2,1)S(1)} %get-tuple-element.62), channel_id=1, source_target_pairs={{0,12},{4,8},{8,4},{12,0},{1,13},{5,9},{9,5},{13,1},{2,14},{6,10},... | collective-permute-start | bytes 540680 | tf_op jit(solution)/shard_map/ppermute | solution.py:498
  48.1 14.9 %collective-permute-start.11 = (bf16[2,176,256]{2,1,0:T(8,128)(2,1)S(1)}, bf16[2,176,256]{2,1,0:T(8,128)(2,1)S(1)}, u32[]{:S(2)}, u32[]{:S(2)}) collective-permute-start(bf16[2,176,256]{2,1,0:T(8,128)(2,1)S(1)} %get-tuple-element.63), channel_id=1, source_target_pairs={{0,8},{4,12},{8,0},{12,4},{1,9},{5,13},{9,1},{13,5},{2,10},{6,14},... | collective-permute-start | bytes 540680 | tf_op jit(solution)/shard_map/ppermute | solution.py:498
  48.1 17.9 %collective-permute-start.12 = (bf16[2,336,256]{2,1,0:T(8,128)(2,1)S(1)}, bf16[2,336,256]{2,1,0:T(8,128)(2,1)S(1)}, u32[]{:S(2)}, u32[]{:S(2)}) collective-permute-start(bf16[2,336,256]{2,1,0:T(8,128)(2,1)S(1)} %get-tuple-element.66.refs_2_.refs_0_), channel_id=1, source_target_pairs={{0,1},{1,0},{2,3},{3,2},{4,5},{5,4},{6,7},{7,6},{8,9},{9,8},{10,11... | collective-permute-start | bytes 1032200 | tf_op jit(solution)/shard_map/ppermute | solution.py:483
  55.0 11.1 %collective-permute-start.13 = (bf16[2,336,256]{2,1,0:T(8,128)(2,1)S(1)}, bf16[2,336,256]{2,1,0:T(8,128)(2,1)S(1)}, u32[]{:S(2)}, u32[]{:S(2)}) collective-permute-start(bf16[2,336,256]{2,1,0:T(8,128)(2,1)S(1)} %get-tuple-element.67.refs_3_.refs_1_), channel_id=1, source_target_pairs={{0,1},{1,0},{2,3},{3,2},{4,5},{5,4},{6,7},{7,6},{8,9},{9,8},{10,11... | collective-permute-start | bytes 1032200 | tf_op jit(solution)/shard_map/ppermute | solution.py:483
  63.8 10.1 %collective-permute-start.16 = (bf16[4,176,256]{2,1,0:T(8,128)(2,1)S(1)}, bf16[4,176,256]{2,1,0:T(8,128)(2,1)S(1)}, u32[]{:S(2)}, u32[]{:S(2)}) collective-permute-start(bf16[4,176,256]{2,1,0:T(8,128)(2,1)S(1)} %select.3.refs_9_.refs_2_), channel_id=1, source_target_pairs={{0,2},{1,3},{2,0},{3,1},{4,6},{5,7},{6,4},{7,5},{8,10},{9,11},{10,... | collective-permute-start | bytes 1081352 | tf_op jit(solution)/shard_map/ppermute | solution.py:483
  65.4 1.7 %collective-permute-start.15 = (bf16[2,336,256]{2,1,0:T(8,128)(2,1)S(1)}, bf16[2,336,256]{2,1,0:T(8,128)(2,1)S(1)}, u32[]{:S(2)}, u32[]{:S(2)}) collective-permute-start(bf16[2,336,256]{2,1,0:T(8,128)(2,1)S(1)} %get-tuple-element.92), channel_id=1, source_target_pairs={{0,1},{1,0},{2,3},{3,2},{4,5},{5,4},{6,7},{7,6},{8,9},{9,8},{10,11... | collective-permute-start | bytes 1032200 | tf_op jit(solution)/shard_map/ppermute | solution.py:483
  65.5 2.1 %collective-permute-start.14 = (bf16[2,336,256]{2,1,0:T(8,128)(2,1)S(1)}, bf16[2,336,256]{2,1,0:T(8,128)(2,1)S(1)}, u32[]{:S(2)}, u32[]{:S(2)}) collective-permute-start(bf16[2,336,256]{2,1,0:T(8,128)(2,1)S(1)} %get-tuple-element.93), channel_id=1, source_target_pairs={{0,1},{1,0},{2,3},{3,2},{4,5},{5,4},{6,7},{7,6},{8,9},{9,8},{10,11... | collective-permute-start | bytes 1032200 | tf_op jit(solution)/shard_map/ppermute | solution.py:483
  66.0 7.9 %collective-permute-start.17 = (bf16[4,176,256]{2,1,0:T(8,128)(2,1)S(1)}, bf16[4,176,256]{2,1,0:T(8,128)(2,1)S(1)}, u32[]{:S(2)}, u32[]{:S(2)}) collective-permute-start(bf16[4,176,256]{2,1,0:T(8,128)(2,1)S(1)} %select.3.refs_9_.refs_2_), channel_id=1, source_target_pairs={{0,1},{1,0},{2,3},{3,2},{4,5},{5,4},{6,7},{7,6},{8,9},{9,8},{10,11... | collective-permute-start | bytes 1081352 | tf_op jit(solution)/shard_map/ppermute | solution.py:483
  73.9 1.7 %collective-permute-start.18 = (bf16[4,176,256]{2,1,0:T(8,128)(2,1)S(1)}, bf16[4,176,256]{2,1,0:T(8,128)(2,1)S(1)}, u32[]{:S(2)}, u32[]{:S(2)}) collective-permute-start(bf16[4,176,256]{2,1,0:T(8,128)(2,1)S(1)} %collective-permute-done.16.refs_10_), channel_id=1, source_target_pairs={{0,1},{1,0},{2,3},{3,2},{4,5},{5,4},{6,7},{7,6},{8,9},{9,8},{10,11... | collective-permute-start | bytes 1081352 | tf_op jit(solution)/shard_map/ppermute | solution.py:483
  78.2 4.9 %collective-permute-start.19 = (f32[2,8,512]{2,1,0:T(8,128)S(1)}, f32[2,8,512]{2,1,0:T(8,128)S(1)}, u32[]{:S(2)}, u32[]{:S(2)}) collective-permute-start(f32[2,8,512]{2,1,0:T(8,128)S(1)} %get-tuple-element.83), channel_id=1, source_target_pairs={{0,8},{4,12},{8,0},{12,4},{1,9},{5,13},{9,1},{13,5},{2,10},{6,14},... | collective-permute-start | bytes 98312 | tf_op jit(solution)/shard_map/ppermute | solution.py:498
  83.1 3.7 %collective-permute-start.20 = (f32[1,8,512]{2,1,0:T(8,128)S(1)}, f32[1,8,512]{2,1,0:T(8,128)S(1)}, u32[]{:S(2)}, u32[]{:S(2)}) collective-permute-start(f32[1,8,512]{2,1,0:T(8,128)S(1)} %get-tuple-element.90), channel_id=1, source_target_pairs={{0,4},{4,0},{8,12},{12,8},{1,5},{5,1},{9,13},{13,9},{2,6},{6,2},{1... | collective-permute-start | bytes 49160 | tf_op jit(solution)/shard_map/ppermute | solution.py:498

commit v23 on v18

--- a/solution.py
+++ b/solution.py
@@ -43,32 +43,32 @@
     return range(wide_count - 1, 0, -1)
 
 
-def pack_kernel(wide_count, pair_count, capacity, me_ref, pairs_ref, *refs):
+def pack_kernel(chunk, with_rows, wide_count, pair_count, capacity, me_ref, pairs_ref, *refs):
     lists, blocks_ref = refs[: wide_count - 1], refs[wide_count - 1]
-    *outs, rows_ref, sems = refs[wide_count:]
+    *outs, sems = refs[wide_count:]
     me = me_ref[0]
+    start, size = CHUNKS[chunk]
     copies = []
 
     def send(source, target):
         copies.append(pltpu.make_async_copy(source, target, sems.at[len(copies)]))
         copies[-1].start()
 
-    for chunk, (start, size) in enumerate(CHUNKS):
-        for number, other in enumerate(others(wide_count)):
-            asked = lists[list_order(wide_count).index(other)]
-            picks = [jnp.int32(0)] * capacity
-            count = jnp.int32(0)
-            for pair in range(pair_count):
-                col = asked[1, pair]
-                mine = (col >> 3) == me
-                for slot in range(capacity):
-                    picks[slot] = jnp.where(mine & (count == slot), col & 7, picks[slot])
-                count = count + mine.astype(jnp.int32)
-            out = outs[chunk * (wide_count - 1) + number]
+    for number, other in enumerate(others(wide_count)):
+        asked = lists[list_order(wide_count).index(other)]
+        picks = [jnp.int32(0)] * capacity
+        count = jnp.int32(0)
+        for pair in range(pair_count):
+            col = asked[1, pair]
+            mine = (col >> 3) == me
             for slot in range(capacity):
-                send(blocks_ref.at[picks[slot], pl.ds(start, size)], out.at[slot])
-    for pair in range(pair_count):
-        send(blocks_ref.at[pairs_ref[0, pair] & 7], rows_ref.at[pair])
+                picks[slot] = jnp.where(mine & (count == slot), col & 7, picks[slot])
+            count = count + mine.astype(jnp.int32)
+        for slot in range(capacity):
+            send(blocks_ref.at[picks[slot], pl.ds(start, size)], outs[number].at[slot])
+    if with_rows:
+        for pair in range(pair_count):
+            send(blocks_ref.at[pairs_ref[0, pair] & 7], outs[-1].at[pair])
     for copy in copies:
         copy.wait()
 
@@ -82,17 +82,16 @@
     return list_order(wide_count)[::-1]
 
 
-def pack(me, pairs, lists, blocks, capacity):
+def pack(me, pairs, lists, blocks, capacity, chunk, with_rows):
     wide_count, pair_count = len(lists) + 1, pairs.shape[1]
     feat = blocks.shape[-1]
-    shapes = [
-        pltpu.VMEM((capacity, size, feat), blocks.dtype)
-        for _, size in CHUNKS
-        for _ in range(1, wide_count)
-    ] + [pltpu.VMEM((pair_count, BR, feat), blocks.dtype)]
-    copies = (len(shapes) - 1) * capacity + pair_count
-    outs = pl.pallas_call(
-        functools.partial(pack_kernel, wide_count, pair_count, capacity),
+    shapes = [pltpu.VMEM((capacity, CHUNKS[chunk][1], feat), blocks.dtype)] * (wide_count - 1)
+    copies = len(shapes) * capacity
+    if with_rows:
+        shapes.append(pltpu.VMEM((pair_count, BR, feat), blocks.dtype))
+        copies += pair_count
+    return pl.pallas_call(
+        functools.partial(pack_kernel, chunk, with_rows, wide_count, pair_count, capacity),
         out_shape=shapes,
         in_specs=[smem()] * (1 + wide_count) + [anywhere()],
         out_specs=[anywhere()] * len(shapes),
@@ -100,8 +99,6 @@
         compiler_params=params(4),
         name="pack",
     )(me, in_hbm(pairs), *[lists[other - 1] for other in list_order(wide_count)], in_hbm(blocks))
-    each = wide_count - 1
-    return [outs[c * each : (c + 1) * each] for c in range(len(CHUNKS))], outs[-1]
 
 
 def select_kernel(wide_count, groups, start, me_ref, pairs_ref, own_ref, *refs):
@@ -373,20 +370,37 @@
     def copy(pair):
         return pltpu.make_async_copy(made.at[pair], out_ref.at[local[pair]], sems.at[pair])
 
-    firsts = []
+    def either(found):
+        return functools.reduce(jnp.logical_or, found, jnp.bool_(False))
+
+    def finish(pair, total, scale):
+        for at in range(0, feat, LANES):
+            lanes = slice(at, at + LANES)
+            made[pair, :, lanes] = (total[:, lanes] * scale).astype(jnp.bfloat16)
+        copy(pair).start()
+
+    firsts, alone = [], []
     for pair in range(pair_count):
+        before = either([local[other] == local[pair] for other in range(pair)])
+        after = either([local[other] == local[pair] for other in range(pair + 1, pair_count)])
+        firsts.append(jnp.logical_not(before))
+        alone.append(jnp.logical_not(before | after))
         sums = total_ref[pair] + jnp.dot(
             kernel_ref[pair], own_columns(window, chunks, pair), preferred_element_type=jnp.float32
         )
-        part[pair] = sums.astype(jnp.bfloat16)
-        weight[pair] = jnp.broadcast_to(
-            jnp.sum(mass_ref[pair], axis=1, keepdims=True), (BR, LANES)
-        )
-        same = [local[other] == local[pair] for other in range(pair)]
-        firsts.append(jnp.logical_not(functools.reduce(jnp.logical_or, same, jnp.bool_(False))))
+        sums = sums.astype(jnp.bfloat16)
+        lines = jnp.broadcast_to(jnp.sum(mass_ref[pair], axis=1, keepdims=True), (BR, LANES))
+        part[pair] = sums
+        weight[pair] = lines
+
+        @pl.when(alone[pair])
+        def _():
+            mean = rows_ref[pair].astype(jnp.float32) + sums.astype(jnp.float32)
+            finish(pair, mean, 1.0 / (1.0 + lines))
+
     for pair in range(pair_count):
 
-        @pl.when(firsts[pair])
+        @pl.when(firsts[pair] & jnp.logical_not(alone[pair]))
         def _():
             total[...] = rows_ref[pair].astype(jnp.float32) + part[pair].astype(jnp.float32)
             mass[...] = 1.0 + weight[pair]
@@ -397,11 +411,7 @@
                     total[...] += part[other].astype(jnp.float32)
                     mass[...] += weight[other]
 
-            scale = 1.0 / mass[...]
-            for at in range(0, feat, LANES):
-                lanes = slice(at, at + LANES)
-                made[pair, :, lanes] = (total[:, lanes] * scale).astype(jnp.bfloat16)
-            copy(pair).start()
+            finish(pair, total, 1.0 / mass[...])
 
     for pair in range(pair_count):
 
@@ -494,7 +504,8 @@
     apart = others(wide_count)
     lists = to_wide([pairs] * (wide_count - 1), apart[::-1])
     fixed = lax.optimization_barrier
-    outgoing, row_slices = pack(me, pairs, lists, blocks, capacity)
+    *outgoing, row_slices = pack(me, pairs, lists, blocks, capacity, 0, True)
+    later = pack(me, pairs, lists, blocks, capacity, 1, False)
 
     def pick(received, chunk, *groups):
         return select(me, pairs, own, received, *CHUNKS[chunk], groups)
@@ -504,13 +515,13 @@
         return [part[0][:middle], part[0][middle:]]
 
     rows = jnp.stack([part[0] for part in first_hops([row_slices])])
-    received = to_wide(outgoing[0], apart)
-    near = to_wide(outgoing[1][-1:], apart[-1:])
+    received = to_wide(outgoing, apart)
+    near = to_wide(later[-1:], apart[-1:])
     rows, received, near, (kept, own) = fixed((rows, received, near, keep(pairs, blocks)))
     own_a, whole_a = pick(received, 0, 2, 1)
     cols_a = [own_a] + first_hops(whole_a)[1:]
     rows = [[rows], *hop([[rows]], 1)]
-    cols_a, rows, received = fixed((cols_a, rows, to_wide(outgoing[1][:-1], apart[:-1])))
+    cols_a, rows, received = fixed((cols_a, rows, to_wide(later[:-1], apart[:-1])))
     cols_b = first_hops(*pick([*received, *near], 1, 1))
     last_b = hop(cols_b[:1], 1)
     cols_a = cols_a + hop([own_a] + [halves(part) for part in cols_a[1:]], 1)

time: 85.5 us -> 85.5 us (level)
  waiting for transfers between devices: 44 us -> 42 us
  Pallas kernels: 19.6 us -> 21.4 us
    ppermute x10, waiting for transfers between devices: 17.7 us -> 15.7 us  [hop(): lax.ppermute(piece, 'narrow', perm)]
    pallas_call x1 -> x2, Pallas kernels: 3.24 us -> 4.35 us  [pack(): pl.pallas_call(functools.partial(pack_kernel, chunk, with_rows, wide_coun...]
  transfers between devices with their start and end apart: 22 -> 22, of which waited for: 13 -> 11; matrix products, arithmetic and copies ran while one was open for 0% -> 0% of each run, Pallas kernels for 15% -> 18%
where the time goes in v23:
time: 85.5 us; the launch traced here: 85.1 us
  waiting for transfers between devices  42 us (49%)
  Pallas kernels  21.4 us (25%)
  starting transfers between devices  20.7 us (24%)
    ppermute x12, waiting for transfers between devices, to_wide(): lax.ppermute(piece, 'wide', [(i, i ^ other) for i in range(count)])  26.3 us
    ppermute x12, starting transfers between devices, to_wide(): lax.ppermute(piece, 'wide', [(i, i ^ other) for i in range(count)])  16.3 us
    ppermute x10, waiting for transfers between devices, hop(): lax.ppermute(piece, 'narrow', perm)  15.7 us
    pallas_call x1, Pallas kernels, keep(): pl.pallas_call(keep_kernel, out_shape=[pltpu.HBM(blocks.shape, blocks.dty...  6.05 us
    ppermute x10, starting transfers between devices, hop(): lax.ppermute(piece, 'narrow', perm)  4.37 us
    pallas_call x2, Pallas kernels, pack(): pl.pallas_call(functools.partial(pack_kernel, chunk, with_rows, wide_coun...  4.35 us
    pallas_call x1, Pallas kernels, first_window(): pl.pallas_call(functools.partial(first_kernel, window, piece_counts(windo...  3.1 us
    pallas_call x1, Pallas kernels, means(): pl.pallas_call(functools.partial(mean_kernel, window, piece_counts(window...  3 us
  transfers between devices with their start and end apart: 22, of which 11 were waited for; matrix products, arithmetic and copies ran while one was open for 0% of the time, Pallas kernels for 18%

profile of v23, /device:TPU:0, one launch (start us, length us, event | category | flops | bytes accessed | tf_op | source)
XLA Modules:
  0.0 85.1 jit_solution(8560566593067912356)
XLA Ops:
  0.6 4.1 %collective-permute-start.2 = (s32[2,4]{1,0:T(2,128)}, s32[2,4]{1,0:T(2,128)S(1)}, u32[]{:S(2)}, u32[]{:S(2)}) collective-permute-start(s32[2,4]{1,0:T(2,128)} %bitcast.14), channel_id=1, source_target_pairs={{0,8},{4,12},{8,0},{12,4},{1,9},{5,13},{9,1},{13,5},{2,10},{6,14},... | collective-permute-start | bytes 104 | tf_op jit(solution)/shard_map/ppermute | solution.py:491
  4.7 1.3 %collective-permute-start.1 = (s32[2,4]{1,0:T(2,128)}, s32[2,4]{1,0:T(2,128)S(1)}, u32[]{:S(2)}, u32[]{:S(2)}) collective-permute-start(s32[2,4]{1,0:T(2,128)} %bitcast.15), channel_id=1, source_target_pairs={{0,12},{4,8},{8,4},{12,0},{1,13},{5,9},{9,5},{13,1},{2,14},{6,10},... | collective-permute-start | bytes 104 | tf_op jit(solution)/shard_map/ppermute | solution.py:491
  6.1 0.2 collective-permute-start
  6.5 3.8 %collective-permute-done.1.refs_1_ = s32[2,4]{1,0:T(2,128)S(1)} collective-permute-done((s32[2,4]{1,0:T(2,128)}, s32[2,4]{1,0:T(2,128)S(1)}, u32[]{:S(2)}, u32[]{:S(2)}) %collective-permute-start.1) | collective-permute-done | bytes 64 | tf_op jit(solution)/shard_map/ppermute | solution.py:491
  10.3 2.5 %pack.2 = (bf16[2,336,256]{2,1,0:T(8,128)(2,1)S(1)}, bf16[2,336,256]{2,1,0:T(8,128)(2,1)S(1)}, bf16[2,336,256]{2,1,0:T(8,128)(2,1)S(1)}, bf16[4,512,256]{2,1,0:T(8,128)(2,1)S(1)}) custom-call(s32[1]{0:T(128)} %bitcast.me_ref, s32[2,4]{1,0:T(2,128)} %bitcast.17, s32[2,4]{1,0:T(2,128)S(1)} %collective-permute-done.refs_0_, ...), custom_call_target="tpu_custom_call" | custom-call | tf_op jit(solution)/shard_map/pack/pallas_call | solution.py:93
  12.8 1.6 %collective-permute-start.3 = (bf16[4,512,256]{2,1,0:T(8,128)(2,1)S(1)}, bf16[4,512,256]{2,1,0:T(8,128)(2,1)S(1)}, u32[]{:S(2)}, u32[]{:S(2)}) collective-permute-start(bf16[4,512,256]{2,1,0:T(8,128)(2,1)S(1)} %get-tuple-element.45.rows_ref), channel_id=1, source_target_pairs={{0,2},{1,3},{2,0},{3,1},{4,6},{5,7},{6,4},{7,5},{8,10},{9,11},{10,... | collective-permute-start | bytes 3145736 | tf_op jit(solution)/shard_map/ppermute | solution.py:476
  14.3 2.0 %collective-permute-start.4 = (bf16[2,336,256]{2,1,0:T(8,128)(2,1)S(1)}, bf16[2,336,256]{2,1,0:T(8,128)(2,1)S(1)}, u32[]{:S(2)}, u32[]{:S(2)}) collective-permute-start(bf16[2,336,256]{2,1,0:T(8,128)(2,1)S(1)} %get-tuple-element.46), channel_id=1, source_target_pairs={{0,12},{4,8},{8,4},{12,0},{1,13},{5,9},{9,5},{13,1},{2,14},{6,10},... | collective-permute-start | bytes 1032200 | tf_op jit(solution)/shard_map/ppermute | solution.py:491
  16.4 2.4 %collective-permute-start.6 = (bf16[2,336,256]{2,1,0:T(8,128)(2,1)S(1)}, bf16[2,336,256]{2,1,0:T(8,128)(2,1)S(1)}, u32[]{:S(2)}, u32[]{:S(2)}) collective-permute-start(bf16[2,336,256]{2,1,0:T(8,128)(2,1)S(1)} %get-tuple-element.48), channel_id=1, source_target_pairs={{0,4},{4,0},{8,12},{12,8},{1,5},{5,1},{9,13},{13,9},{2,6},{6,2},{1... | collective-permute-start | bytes 1032200 | tf_op jit(solution)/shard_map/ppermute | solution.py:491
  18.7 1.9 %pack.3 = (bf16[2,176,256]{2,1,0:T(8,128)(2,1)S(1)}, bf16[2,176,256]{2,1,0:T(8,128)(2,1)S(1)}, bf16[2,176,256]{2,1,0:T(8,128)(2,1)S(1)}) custom-call(s32[1]{0:T(128)} %bitcast.me_ref, s32[2,4]{1,0:T(2,128)} %bitcast.18, s32[2,4]{1,0:T(2,128)S(1)} %collective-permute-done.refs_0_, s32[2,4]{1,0:T(2,128)S(1)} %collective-permute-done.1.refs_1_, ...), custom_call_target="tpu_custom_call" | custom-call | tf_op jit(solution)/shard_map/pack/pallas_call | solution.py:93
  20.7 6.0 %keep.1 = (bf16[8,512,256]{2,1,0:T(8,128)(2,1)}, bf16[4,512,256]{2,1,0:T(8,128)(2,1)S(1)}) custom-call(s32[2,4]{1,0:T(2,128)} %bitcast.19, bf16[8,512,256]{2,1,0:T(8,128)(2,1)} %bitcast.10, bf16[8,512,256]{2,1,0:T(8,128)(2,1)} %bitcast.11), custom_call_target="tpu_custom_call" | custom-call | tf_op jit(solution)/shard_map/keep/pallas_call | solution.py:346
  26.8 9.6 %collective-permute-done.3 = bf16[4,512,256]{2,1,0:T(8,128)(2,1)S(1)} collective-permute-done((bf16[4,512,256]{2,1,0:T(8,128)(2,1)S(1)}, bf16[4,512,256]{2,1,0:T(8,128)(2,1)S(1)}, u32[]{:S(2)}, u32[]{:S(2)}) %collective-permute-start.3) | collective-permute-done | bytes 1048608 | tf_op jit(solution)/shard_map/ppermute | solution.py:476
  36.3 0.2 pad_maximum_fusion.refs_0_
  36.5 4.0 %collective-permute-done.7.refs_2_ = bf16[2,176,256]{2,1,0:T(8,128)(2,1)S(1)} collective-permute-done((bf16[2,176,256]{2,1,0:T(8,128)(2,1)S(1)}, bf16[2,176,256]{2,1,0:T(8,128)(2,1)S(1)}, u32[]{:S(2)}, u32[]{:S(2)}) %collective-permute-start.7) | collective-permute-done | bytes 180256 | tf_op jit(solution)/shard_map/ppermute | solution.py:491
  40.5 3.4 %collective-permute-done.5.refs_1_ = bf16[2,336,256]{2,1,0:T(8,128)(2,1)S(1)} collective-permute-done((bf16[2,336,256]{2,1,0:T(8,128)(2,1)S(1)}, bf16[2,336,256]{2,1,0:T(8,128)(2,1)S(1)}, u32[]{:S(2)}, u32[]{:S(2)}) %collective-permute-start.5) | collective-permute-done | bytes 344096 | tf_op jit(solution)/shard_map/ppermute | solution.py:491
  43.9 0.9 %select.2 = (bf16[2,336,256]{2,1,0:T(8,128)(2,1)S(1)}, bf16[2,336,256]{2,1,0:T(8,128)(2,1)S(1)}, bf16[4,336,256]{2,1,0:T(8,128)(2,1)S(1)}) custom-call(s32[1]{0:T(128)} %bitcast.me_ref, s32[2,4]{1,0:T(2,128)} %bitcast.20, bf16[4,512,256]{2,1,0:T(8,128)(2,1)S(1)} %get-tuple-element.52.own_ref, bf16[2,336,256]{2,1,0:T(8,128)(2,1)S(1)} %collective-permute-done.4.refs_0_, ...), custom_call_target="tpu_custom_call" | custom-call | tf_op jit(solution)/shard_map/select/pallas_call | solution.py:141
  44.8 0.6 collective-permute-start.8
  45.4 2.6 %collective-permute-start.10 = (bf16[2,176,256]{2,1,0:T(8,128)(2,1)S(1)}, bf16[2,176,256]{2,1,0:T(8,128)(2,1)S(1)}, u32[]{:S(2)}, u32[]{:S(2)}) collective-permute-start(bf16[2,176,256]{2,1,0:T(8,128)(2,1)S(1)} %get-tuple-element.60), channel_id=1, source_target_pairs={{0,12},{4,8},{8,4},{12,0},{1,13},{5,9},{9,5},{13,1},{2,14},{6,10},... | collective-permute-start | bytes 540680 | tf_op jit(solution)/shard_map/ppermute | solution.py:491
  48.0 6.6 %collective-permute-done.10.refs_0_ = bf16[2,176,256]{2,1,0:T(8,128)(2,1)S(1)} collective-permute-done((bf16[2,176,256]{2,1,0:T(8,128)(2,1)S(1)}, bf16[2,176,256]{2,1,0:T(8,128)(2,1)S(1)}, u32[]{:S(2)}, u32[]{:S(2)}) %collective-permute-start.10) | collective-permute-done | bytes 180256 | tf_op jit(solution)/shard_map/ppermute | solution.py:491
  54.6 8.2 %collective-permute-done.11.refs_1_ = bf16[2,176,256]{2,1,0:T(8,128)(2,1)S(1)} collective-permute-done((bf16[2,176,256]{2,1,0:T(8,128)(2,1)S(1)}, bf16[2,176,256]{2,1,0:T(8,128)(2,1)S(1)}, u32[]{:S(2)}, u32[]{:S(2)}) %collective-permute-start.11) | collective-permute-done | bytes 180256 | tf_op jit(solution)/shard_map/ppermute | solution.py:491
  62.9 0.8 select.3.refs_9_.refs_2_
  63.7 1.6 %collective-permute-start.16 = (bf16[4,176,256]{2,1,0:T(8,128)(2,1)S(1)}, bf16[4,176,256]{2,1,0:T(8,128)(2,1)S(1)}, u32[]{:S(2)}, u32[]{:S(2)}) collective-permute-start(bf16[4,176,256]{2,1,0:T(8,128)(2,1)S(1)} %select.3.refs_9_.refs_2_), channel_id=1, source_target_pairs={{0,2},{1,3},{2,0},{3,1},{4,6},{5,7},{6,4},{7,5},{8,10},{9,11},{10,... | collective-permute-start | bytes 1081352 | tf_op jit(solution)/shard_map/ppermute | solution.py:476
  65.4 0.5 collective-permute-start.14
  66.0 1.1 %collective-permute-done.15.refs_8_ = bf16[2,336,256]{2,1,0:T(8,128)(2,1)S(1)} collective-permute-done((bf16[2,336,256]{2,1,0:T(8,128)(2,1)S(1)}, bf16[2,336,256]{2,1,0:T(8,128)(2,1)S(1)}, u32[]{:S(2)}, u32[]{:S(2)}) %collective-permute-start.15) | collective-permute-done | bytes 344096 | tf_op jit(solution)/shard_map/ppermute | solution.py:476
  67.0 0.5 collective-permute-done.14.refs_7_
  67.5 3.1 %first_window.1 = (f32[4,512,128]{2,1,0:T(8,128)S(1)}, f32[4,512,128]{2,1,0:T(8,128)S(1)}, f32[4,512,256]{2,1,0:T(8,128)S(1)}, f32[4,256]{1,0:T(4,128)S(1)}) custom-call(bf16[2,4,512,256]{3,2,1,0:T(8,128)(2,1)S(1)} %pad_maximum_fusion.refs_0_, bf16[2,4,512,256]{3,2,1,0:T(8,128)(2,1)S(1)} %collective-permute-done.9.refs_1_, ...), custom_call_target="tpu_custom_call" | custom-call | tf_op jit(solution)/shard_map/first_window/pallas_call | solution.py:286
  70.6 3.0 %collective-permute-done.16.refs_10_ = bf16[4,176,256]{2,1,0:T(8,128)(2,1)S(1)} collective-permute-done((bf16[4,176,256]{2,1,0:T(8,128)(2,1)S(1)}, bf16[4,176,256]{2,1,0:T(8,128)(2,1)S(1)}, u32[]{:S(2)}, u32[]{:S(2)}) %collective-permute-start.16) | collective-permute-done | bytes 360480 | tf_op jit(solution)/shard_map/ppermute | solution.py:476
  73.6 1.7 %collective-permute-done.18.refs_12_ = bf16[4,176,256]{2,1,0:T(8,128)(2,1)S(1)} collective-permute-done((bf16[4,176,256]{2,1,0:T(8,128)(2,1)S(1)}, bf16[4,176,256]{2,1,0:T(8,128)(2,1)S(1)}, u32[]{:S(2)}, u32[]{:S(2)}) %collective-permute-start.18) | collective-permute-done | bytes 360480 | tf_op jit(solution)/shard_map/ppermute | solution.py:476
  75.3 2.6 %last_window.1 = (bf16[4,512,256]{2,1,0:T(8,128)(2,1)S(1)}, f32[4,512,128]{2,1,0:T(8,128)S(1)}, f32[8,512]{1,0:T(8,128)S(1)}, f32[8,512]{1,0:T(8,128)S(1)}, f32[...) custom-call(s32[1]{0:T(128)} %bitcast.me_ref, s32[2,4]{1,0:T(2,128)} %bitcast.22, ...), custom_call_target="tpu_custom_call" | custom-call | flops 1073741824 | bytes 8388608 | tf_op jit(solution)/shard_map/last_window/pallas_call | solution.py:310
  78.0 2.7 %collective-permute-start.20 = (f32[8,512]{1,0:T(8,128)S(1)}, f32[8,512]{1,0:T(8,128)S(1)}, u32[]{:S(2)}, u32[]{:S(2)}) collective-permute-start(f32[8,512]{1,0:T(8,128)S(1)} %get-tuple-element.82), channel_id=1, source_target_pairs={{0,12},{4,8},{8,4},{12,0},{1,13},{5,9},{9,5},{13,1},{2,14},{6,10},... | collective-permute-start | bytes 49160 | tf_op jit(solution)/shard_map/ppermute | solution.py:491
  80.7 0.8 collective-permute-start.21
  81.5 3.0 %means.1 = bf16[8,512,256]{2,1,0:T(8,128)(2,1)} custom-call(s32[2,4]{1,0:T(2,128)} %bitcast.23, bf16[4,512,256]{2,1,0:T(8,128)(2,1)S(1)} %get-tuple-element.45.rows_ref, bf16[4,512,256]{2,1,0:T(8,128)(2,1)S(1)} %get-tuple-element.84.kernel_ref, f32[4,512,128]{2,1,0:T(8,128)S(1)} %get-tuple-element.85.mass_ref, ...), custom_call_target="tpu_custom_call", output_to_operand_aliasing={{}: (8, {})} | custom-call | flops 536870912 | bytes 8388608 | tf_op jit(solution)/shard_map/means/pallas_call | solution.py:428
  84.5 0.6 weights.1
  (23 shorter events, 0.6 us)
Async XLA Ops:
  0.6 5.9 %collective-permute-start.2 = (s32[2,4]{1,0:T(2,128)}, s32[2,4]{1,0:T(2,128)S(1)}, u32[]{:S(2)}, u32[]{:S(2)}) collective-permute-start(s32[2,4]{1,0:T(2,128)} %bitcast.14), channel_id=1, source_target_pairs={{0,8},{4,12},{8,0},{12,4},{1,9},{5,13},{9,1},{13,5},{2,10},{6,14},... | collective-permute-start | bytes 104 | tf_op jit(solution)/shard_map/ppermute | solution.py:491
  4.7 5.6 %collective-permute-start.1 = (s32[2,4]{1,0:T(2,128)}, s32[2,4]{1,0:T(2,128)S(1)}, u32[]{:S(2)}, u32[]{:S(2)}) collective-permute-start(s32[2,4]{1,0:T(2,128)} %bitcast.15), channel_id=1, source_target_pairs={{0,12},{4,8},{8,4},{12,0},{1,13},{5,9},{9,5},{13,1},{2,14},{6,10},... | collective-permute-start | bytes 104 | tf_op jit(solution)/shard_map/ppermute | solution.py:491
  6.1 4.2 %collective-permute-start = (s32[2,4]{1,0:T(2,128)}, s32[2,4]{1,0:T(2,128)S(1)}, u32[]{:S(2)}, u32[]{:S(2)}) collective-permute-start(s32[2,4]{1,0:T(2,128)} %bitcast.16), channel_id=1, source_target_pairs={{0,4},{4,0},{8,12},{12,8},{1,5},{5,1},{9,13},{13,9},{2,6},{6,2},{1... | collective-permute-start | bytes 104 | tf_op jit(solution)/shard_map/ppermute | solution.py:491
  12.8 23.5 %collective-permute-start.3 = (bf16[4,512,256]{2,1,0:T(8,128)(2,1)S(1)}, bf16[4,512,256]{2,1,0:T(8,128)(2,1)S(1)}, u32[]{:S(2)}, u32[]{:S(2)}) collective-permute-start(bf16[4,512,256]{2,1,0:T(8,128)(2,1)S(1)} %get-tuple-element.45.rows_ref), channel_id=1, source_target_pairs={{0,2},{1,3},{2,0},{3,1},{4,6},{5,7},{6,4},{7,5},{8,10},{9,11},{10,... | collective-permute-start | bytes 3145736 | tf_op jit(solution)/shard_map/ppermute | solution.py:476
  14.3 26.1 %collective-permute-start.4 = (bf16[2,336,256]{2,1,0:T(8,128)(2,1)S(1)}, bf16[2,336,256]{2,1,0:T(8,128)(2,1)S(1)}, u32[]{:S(2)}, u32[]{:S(2)}) collective-permute-start(bf16[2,336,256]{2,1,0:T(8,128)(2,1)S(1)} %get-tuple-element.46), channel_id=1, source_target_pairs={{0,12},{4,8},{8,4},{12,0},{1,13},{5,9},{9,5},{13,1},{2,14},{6,10},... | collective-permute-start | bytes 1032200 | tf_op jit(solution)/shard_map/ppermute | solution.py:491
  16.4 27.5 %collective-permute-start.5 = (bf16[2,336,256]{2,1,0:T(8,128)(2,1)S(1)}, bf16[2,336,256]{2,1,0:T(8,128)(2,1)S(1)}, u32[]{:S(2)}, u32[]{:S(2)}) collective-permute-start(bf16[2,336,256]{2,1,0:T(8,128)(2,1)S(1)} %get-tuple-element.47), channel_id=1, source_target_pairs={{0,8},{4,12},{8,0},{12,4},{1,9},{5,13},{9,1},{13,5},{2,10},{6,14},... | collective-permute-start | bytes 1032200 | tf_op jit(solution)/shard_map/ppermute | solution.py:491
  16.4 27.5 %collective-permute-start.6 = (bf16[2,336,256]{2,1,0:T(8,128)(2,1)S(1)}, bf16[2,336,256]{2,1,0:T(8,128)(2,1)S(1)}, u32[]{:S(2)}, u32[]{:S(2)}) collective-permute-start(bf16[2,336,256]{2,1,0:T(8,128)(2,1)S(1)} %get-tuple-element.48), channel_id=1, source_target_pairs={{0,4},{4,0},{8,12},{12,8},{1,5},{5,1},{9,13},{13,9},{2,6},{6,2},{1... | collective-permute-start | bytes 1032200 | tf_op jit(solution)/shard_map/ppermute | solution.py:491
  20.6 19.8 %collective-permute-start.7 = (bf16[2,176,256]{2,1,0:T(8,128)(2,1)S(1)}, bf16[2,176,256]{2,1,0:T(8,128)(2,1)S(1)}, u32[]{:S(2)}, u32[]{:S(2)}) collective-permute-start(bf16[2,176,256]{2,1,0:T(8,128)(2,1)S(1)} %get-tuple-element.49), channel_id=1, source_target_pairs={{0,4},{4,0},{8,12},{12,8},{1,5},{5,1},{9,13},{13,9},{2,6},{6,2},{1... | collective-permute-start | bytes 540680 | tf_op jit(solution)/shard_map/ppermute | solution.py:491
  43.9 19.0 %collective-permute-start.9 = (bf16[2,4,512,256]{3,2,1,0:T(8,128)(2,1)S(1)}, bf16[2,4,512,256]{3,2,1,0:T(8,128)(2,1)S(1)}, u32[]{:S(2)}, u32[]{:S(2)}) collective-permute-start(bf16[2,4,512,256]{3,2,1,0:T(8,128)(2,1)S(1)} %pad_maximum_fusion.refs_0_), channel_id=1, source_target_pairs={{0,1},{1,0},{2,3},{3,2},{4,5},{5,4},{6,7},{7,6},{8,9},{9,8},{10,11... | collective-permute-start | bytes 6291464 | tf_op jit(solution)/shard_map/ppermute | solution.py:476
  44.8 18.1 %collective-permute-start.8 = (bf16[4,336,256]{2,1,0:T(8,128)(2,1)S(1)}, bf16[4,336,256]{2,1,0:T(8,128)(2,1)S(1)}, u32[]{:S(2)}, u32[]{:S(2)}) collective-permute-start(bf16[4,336,256]{2,1,0:T(8,128)(2,1)S(1)} %get-tuple-element.58), channel_id=1, source_target_pairs={{0,2},{1,3},{2,0},{3,1},{4,6},{5,7},{6,4},{7,5},{8,10},{9,11},{10,... | collective-permute-start | bytes 2064392 | tf_op jit(solution)/shard_map/ppermute | solution.py:476
  45.4 9.3 %collective-permute-start.10 = (bf16[2,176,256]{2,1,0:T(8,128)(2,1)S(1)}, bf16[2,176,256]{2,1,0:T(8,128)(2,1)S(1)}, u32[]{:S(2)}, u32[]{:S(2)}) collective-permute-start(bf16[2,176,256]{2,1,0:T(8,128)(2,1)S(1)} %get-tuple-element.60), channel_id=1, source_target_pairs={{0,12},{4,8},{8,4},{12,0},{1,13},{5,9},{9,5},{13,1},{2,14},{6,10},... | collective-permute-start | bytes 540680 | tf_op jit(solution)/shard_map/ppermute | solution.py:491
  48.0 14.9 %collective-permute-start.11 = (bf16[2,176,256]{2,1,0:T(8,128)(2,1)S(1)}, bf16[2,176,256]{2,1,0:T(8,128)(2,1)S(1)}, u32[]{:S(2)}, u32[]{:S(2)}) collective-permute-start(bf16[2,176,256]{2,1,0:T(8,128)(2,1)S(1)} %get-tuple-element.61), channel_id=1, source_target_pairs={{0,8},{4,12},{8,0},{12,4},{1,9},{5,13},{9,1},{13,5},{2,10},{6,14},... | collective-permute-start | bytes 540680 | tf_op jit(solution)/shard_map/ppermute | solution.py:491
  48.0 17.9 %collective-permute-start.12 = (bf16[2,336,256]{2,1,0:T(8,128)(2,1)S(1)}, bf16[2,336,256]{2,1,0:T(8,128)(2,1)S(1)}, u32[]{:S(2)}, u32[]{:S(2)}) collective-permute-start(bf16[2,336,256]{2,1,0:T(8,128)(2,1)S(1)} %get-tuple-element.64.refs_2_.refs_0_), channel_id=1, source_target_pairs={{0,1},{1,0},{2,3},{3,2},{4,5},{5,4},{6,7},{7,6},{8,9},{9,8},{10,11... | collective-permute-start | bytes 1032200 | tf_op jit(solution)/shard_map/ppermute | solution.py:476
  54.6 11.3 %collective-permute-start.13 = (bf16[2,336,256]{2,1,0:T(8,128)(2,1)S(1)}, bf16[2,336,256]{2,1,0:T(8,128)(2,1)S(1)}, u32[]{:S(2)}, u32[]{:S(2)}) collective-permute-start(bf16[2,336,256]{2,1,0:T(8,128)(2,1)S(1)} %get-tuple-element.65.refs_3_.refs_1_), channel_id=1, source_target_pairs={{0,1},{1,0},{2,3},{3,2},{4,5},{5,4},{6,7},{7,6},{8,9},{9,8},{10,11... | collective-permute-start | bytes 1032200 | tf_op jit(solution)/shard_map/ppermute | solution.py:476
  63.7 9.9 %collective-permute-start.16 = (bf16[4,176,256]{2,1,0:T(8,128)(2,1)S(1)}, bf16[4,176,256]{2,1,0:T(8,128)(2,1)S(1)}, u32[]{:S(2)}, u32[]{:S(2)}) collective-permute-start(bf16[4,176,256]{2,1,0:T(8,128)(2,1)S(1)} %select.3.refs_9_.refs_2_), channel_id=1, source_target_pairs={{0,2},{1,3},{2,0},{3,1},{4,6},{5,7},{6,4},{7,5},{8,10},{9,11},{10,... | collective-permute-start | bytes 1081352 | tf_op jit(solution)/shard_map/ppermute | solution.py:476
  65.3 1.7 %collective-permute-start.15 = (bf16[2,336,256]{2,1,0:T(8,128)(2,1)S(1)}, bf16[2,336,256]{2,1,0:T(8,128)(2,1)S(1)}, u32[]{:S(2)}, u32[]{:S(2)}) collective-permute-start(bf16[2,336,256]{2,1,0:T(8,128)(2,1)S(1)} %get-tuple-element.88), channel_id=1, source_target_pairs={{0,1},{1,0},{2,3},{3,2},{4,5},{5,4},{6,7},{7,6},{8,9},{9,8},{10,11... | collective-permute-start | bytes 1032200 | tf_op jit(solution)/shard_map/ppermute | solution.py:476
  65.4 2.1 %collective-permute-start.14 = (bf16[2,336,256]{2,1,0:T(8,128)(2,1)S(1)}, bf16[2,336,256]{2,1,0:T(8,128)(2,1)S(1)}, u32[]{:S(2)}, u32[]{:S(2)}) collective-permute-start(bf16[2,336,256]{2,1,0:T(8,128)(2,1)S(1)} %get-tuple-element.89), channel_id=1, source_target_pairs={{0,1},{1,0},{2,3},{3,2},{4,5},{5,4},{6,7},{7,6},{8,9},{9,8},{10,11... | collective-permute-start | bytes 1032200 | tf_op jit(solution)/shard_map/ppermute | solution.py:476
  65.9 7.7 %collective-permute-start.17 = (bf16[4,176,256]{2,1,0:T(8,128)(2,1)S(1)}, bf16[4,176,256]{2,1,0:T(8,128)(2,1)S(1)}, u32[]{:S(2)}, u32[]{:S(2)}) collective-permute-start(bf16[4,176,256]{2,1,0:T(8,128)(2,1)S(1)} %select.3.refs_9_.refs_2_), channel_id=1, source_target_pairs={{0,1},{1,0},{2,3},{3,2},{4,5},{5,4},{6,7},{7,6},{8,9},{9,8},{10,11... | collective-permute-start | bytes 1081352 | tf_op jit(solution)/shard_map/ppermute | solution.py:476
  73.6 1.7 %collective-permute-start.18 = (bf16[4,176,256]{2,1,0:T(8,128)(2,1)S(1)}, bf16[4,176,256]{2,1,0:T(8,128)(2,1)S(1)}, u32[]{:S(2)}, u32[]{:S(2)}) collective-permute-start(bf16[4,176,256]{2,1,0:T(8,128)(2,1)S(1)} %collective-permute-done.16.refs_10_), channel_id=1, source_target_pairs={{0,1},{1,0},{2,3},{3,2},{4,5},{5,4},{6,7},{7,6},{8,9},{9,8},{10,11... | collective-permute-start | bytes 1081352 | tf_op jit(solution)/shard_map/ppermute | solution.py:476
  77.9 6.6 %collective-permute-start.19 = (f32[8,512]{1,0:T(8,128)S(1)}, f32[8,512]{1,0:T(8,128)S(1)}, u32[]{:S(2)}, u32[]{:S(2)}) collective-permute-start(f32[8,512]{1,0:T(8,128)S(1)} %get-tuple-element.81), channel_id=1, source_target_pairs={{0,8},{4,12},{8,0},{12,4},{1,9},{5,13},{9,1},{13,5},{2,10},{6,14},... | collective-permute-start | bytes 49160 | tf_op jit(solution)/shard_map/ppermute | solution.py:491
  78.0 6.5 %collective-permute-start.20 = (f32[8,512]{1,0:T(8,128)S(1)}, f32[8,512]{1,0:T(8,128)S(1)}, u32[]{:S(2)}, u32[]{:S(2)}) collective-permute-start(f32[8,512]{1,0:T(8,128)S(1)} %get-tuple-element.82), channel_id=1, source_target_pairs={{0,12},{4,8},{8,4},{12,0},{1,13},{5,9},{9,5},{13,1},{2,14},{6,10},... | collective-permute-start | bytes 49160 | tf_op jit(solution)/shard_map/ppermute | solution.py:491
  80.7 3.8 %collective-permute-start.21 = (f32[8,512]{1,0:T(8,128)S(1)}, f32[8,512]{1,0:T(8,128)S(1)}, u32[]{:S(2)}, u32[]{:S(2)}) collective-permute-start(f32[8,512]{1,0:T(8,128)S(1)} %get-tuple-element.83), channel_id=1, source_target_pairs={{0,4},{4,0},{8,12},{12,8},{1,5},{5,1},{9,13},{13,9},{2,6},{6,2},{1... | collective-permute-start | bytes 49160 | tf_op jit(solution)/shard_map/ppermute | solution.py:491

commit v24 on v23

--- a/solution.py
+++ b/solution.py
@@ -11,7 +11,7 @@
 BR = 512
 BLK_DEV = 8
 LANES = 128
-CHUNKS = ((0, 336), (336, 176))
+CHUNKS = ((0, 352), (352, 160))
 WINDOWS = ((0, 256), (256, 512))
 
 
@@ -370,37 +370,20 @@
     def copy(pair):
         return pltpu.make_async_copy(made.at[pair], out_ref.at[local[pair]], sems.at[pair])
 
-    def either(found):
-        return functools.reduce(jnp.logical_or, found, jnp.bool_(False))
-
-    def finish(pair, total, scale):
-        for at in range(0, feat, LANES):
-            lanes = slice(at, at + LANES)
-            made[pair, :, lanes] = (total[:, lanes] * scale).astype(jnp.bfloat16)
-        copy(pair).start()
-
-    firsts, alone = [], []
+    firsts = []
     for pair in range(pair_count):
-        before = either([local[other] == local[pair] for other in range(pair)])
-        after = either([local[other] == local[pair] for other in range(pair + 1, pair_count)])
-        firsts.append(jnp.logical_not(before))
-        alone.append(jnp.logical_not(before | after))
         sums = total_ref[pair] + jnp.dot(
             kernel_ref[pair], own_columns(window, chunks, pair), preferred_element_type=jnp.float32
         )
-        sums = sums.astype(jnp.bfloat16)
-        lines = jnp.broadcast_to(jnp.sum(mass_ref[pair], axis=1, keepdims=True), (BR, LANES))
-        part[pair] = sums
-        weight[pair] = lines
-
-        @pl.when(alone[pair])
-        def _():
-            mean = rows_ref[pair].astype(jnp.float32) + sums.astype(jnp.float32)
-            finish(pair, mean, 1.0 / (1.0 + lines))
-
+        part[pair] = sums.astype(jnp.bfloat16)
+        weight[pair] = jnp.broadcast_to(
+            jnp.sum(mass_ref[pair], axis=1, keepdims=True), (BR, LANES)
+        )
+        same = [local[other] == local[pair] for other in range(pair)]
+        firsts.append(jnp.logical_not(functools.reduce(jnp.logical_or, same, jnp.bool_(False))))
     for pair in range(pair_count):
 
-        @pl.when(firsts[pair] & jnp.logical_not(alone[pair]))
+        @pl.when(firsts[pair])
         def _():
             total[...] = rows_ref[pair].astype(jnp.float32) + part[pair].astype(jnp.float32)
             mass[...] = 1.0 + weight[pair]
@@ -411,7 +394,11 @@
                     total[...] += part[other].astype(jnp.float32)
                     mass[...] += weight[other]
 
-            finish(pair, total, 1.0 / mass[...])
+            scale = 1.0 / mass[...]
+            for at in range(0, feat, LANES):
+                lanes = slice(at, at + LANES)
+                made[pair, :, lanes] = (total[:, lanes] * scale).astype(jnp.bfloat16)
+            copy(pair).start()
 
     for pair in range(pair_count):
 

time: 85.5 us -> 87.7 us (1.026)
  waiting for transfers between devices: 42 us -> 46 us
  starting transfers between devices: 20.7 us -> 19.6 us
    ppermute x10, waiting for transfers between devices: 15.7 us -> 19.2 us  [hop(): lax.ppermute(piece, 'narrow', perm)]
    ppermute x10, starting transfers between devices: 4.37 us -> 3.34 us  [hop(): lax.ppermute(piece, 'narrow', perm)]
  transfers between devices with their start and end apart: 22 -> 22, of which waited for: 11 -> 12; matrix products, arithmetic and copies ran while one was open for 0% -> 0% of each run, Pallas kernels for 18% -> 17%
where the time goes in v24:
time: 87.7 us; the launch traced here: 87.3 us
  waiting for transfers between devices  46 us (52%)
  Pallas kernels  20.7 us (24%)
  starting transfers between devices  19.6 us (22%)
    ppermute x12, waiting for transfers between devices, to_wide(): lax.ppermute(piece, 'wide', [(i, i ^ other) for i in range(count)])  26.8 us
    ppermute x10, waiting for transfers between devices, hop(): lax.ppermute(piece, 'narrow', perm)  19.2 us
    ppermute x12, starting transfers between devices, to_wide(): lax.ppermute(piece, 'wide', [(i, i ^ other) for i in range(count)])  16.3 us
    pallas_call x1, Pallas kernels, keep(): pl.pallas_call(keep_kernel, out_shape=[pltpu.HBM(blocks.shape, blocks.dty...  6.02 us
    pallas_call x2, Pallas kernels, pack(): pl.pallas_call(functools.partial(pack_kernel, chunk, with_rows, wide_coun...  4.32 us
    ppermute x10, starting transfers between devices, hop(): lax.ppermute(piece, 'narrow', perm)  3.34 us
    pallas_call x1, Pallas kernels, first_window(): pl.pallas_call(functools.partial(first_kernel, window, piece_counts(windo...  3.1 us
    pallas_call x1, Pallas kernels, last_window(): pl.pallas_call(functools.partial(last_kernel, window, piece_counts(window...  2.64 us
  transfers between devices with their start and end apart: 22, of which 12 were waited for; matrix products, arithmetic and copies ran while one was open for 0% of the time, Pallas kernels for 17%

profile of v24, /device:TPU:0, one launch (start us, length us, event | category | flops | bytes accessed | tf_op | source)
XLA Modules:
  0.0 87.3 jit_solution(13032813087800166199)
XLA Ops:
  0.6 4.1 %collective-permute-start.2 = (s32[2,4]{1,0:T(2,128)}, s32[2,4]{1,0:T(2,128)S(1)}, u32[]{:S(2)}, u32[]{:S(2)}) collective-permute-start(s32[2,4]{1,0:T(2,128)} %bitcast.14), channel_id=1, source_target_pairs={{0,8},{4,12},{8,0},{12,4},{1,9},{5,13},{9,1},{13,5},{2,10},{6,14},... | collective-permute-start | bytes 104 | tf_op jit(solution)/shard_map/ppermute | solution.py:478
  4.7 1.3 %collective-permute-start.1 = (s32[2,4]{1,0:T(2,128)}, s32[2,4]{1,0:T(2,128)S(1)}, u32[]{:S(2)}, u32[]{:S(2)}) collective-permute-start(s32[2,4]{1,0:T(2,128)} %bitcast.15), channel_id=1, source_target_pairs={{0,12},{4,8},{8,4},{12,0},{1,13},{5,9},{9,5},{13,1},{2,14},{6,10},... | collective-permute-start | bytes 104 | tf_op jit(solution)/shard_map/ppermute | solution.py:478
  6.1 0.2 collective-permute-start
  6.5 3.8 %collective-permute-done.1.refs_1_ = s32[2,4]{1,0:T(2,128)S(1)} collective-permute-done((s32[2,4]{1,0:T(2,128)}, s32[2,4]{1,0:T(2,128)S(1)}, u32[]{:S(2)}, u32[]{:S(2)}) %collective-permute-start.1) | collective-permute-done | bytes 64 | tf_op jit(solution)/shard_map/ppermute | solution.py:478
  10.3 2.4 %pack.2 = (bf16[2,352,256]{2,1,0:T(8,128)(2,1)S(1)}, bf16[2,352,256]{2,1,0:T(8,128)(2,1)S(1)}, bf16[2,352,256]{2,1,0:T(8,128)(2,1)S(1)}, bf16[4,512,256]{2,1,0:T(8,128)(2,1)S(1)}) custom-call(s32[1]{0:T(128)} %bitcast.me_ref, s32[2,4]{1,0:T(2,128)} %bitcast.17, s32[2,4]{1,0:T(2,128)S(1)} %collective-permute-done.refs_0_, ...), custom_call_target="tpu_custom_call" | custom-call | tf_op jit(solution)/shard_map/pack/pallas_call | solution.py:93
  12.8 1.6 %collective-permute-start.3 = (bf16[4,512,256]{2,1,0:T(8,128)(2,1)S(1)}, bf16[4,512,256]{2,1,0:T(8,128)(2,1)S(1)}, u32[]{:S(2)}, u32[]{:S(2)}) collective-permute-start(bf16[4,512,256]{2,1,0:T(8,128)(2,1)S(1)} %get-tuple-element.45.rows_ref), channel_id=1, source_target_pairs={{0,2},{1,3},{2,0},{3,1},{4,6},{5,7},{6,4},{7,5},{8,10},{9,11},{10,... | collective-permute-start | bytes 3145736 | tf_op jit(solution)/shard_map/ppermute | solution.py:463
  14.3 2.0 %collective-permute-start.4 = (bf16[2,352,256]{2,1,0:T(8,128)(2,1)S(1)}, bf16[2,352,256]{2,1,0:T(8,128)(2,1)S(1)}, u32[]{:S(2)}, u32[]{:S(2)}) collective-permute-start(bf16[2,352,256]{2,1,0:T(8,128)(2,1)S(1)} %get-tuple-element.46), channel_id=1, source_target_pairs={{0,12},{4,8},{8,4},{12,0},{1,13},{5,9},{9,5},{13,1},{2,14},{6,10},... | collective-permute-start | bytes 1081352 | tf_op jit(solution)/shard_map/ppermute | solution.py:478
  16.3 2.4 %collective-permute-start.6 = (bf16[2,352,256]{2,1,0:T(8,128)(2,1)S(1)}, bf16[2,352,256]{2,1,0:T(8,128)(2,1)S(1)}, u32[]{:S(2)}, u32[]{:S(2)}) collective-permute-start(bf16[2,352,256]{2,1,0:T(8,128)(2,1)S(1)} %get-tuple-element.48), channel_id=1, source_target_pairs={{0,4},{4,0},{8,12},{12,8},{1,5},{5,1},{9,13},{13,9},{2,6},{6,2},{1... | collective-permute-start | bytes 1081352 | tf_op jit(solution)/shard_map/ppermute | solution.py:478
  18.7 6.0 %keep.1 = (bf16[8,512,256]{2,1,0:T(8,128)(2,1)}, bf16[4,512,256]{2,1,0:T(8,128)(2,1)S(1)}) custom-call(s32[2,4]{1,0:T(2,128)} %bitcast.18, bf16[8,512,256]{2,1,0:T(8,128)(2,1)} %bitcast.9, bf16[8,512,256]{2,1,0:T(8,128)(2,1)} %bitcast.10), custom_call_target="tpu_custom_call" | custom-call | tf_op jit(solution)/shard_map/keep/pallas_call | solution.py:346
  24.7 1.9 %pack.3 = (bf16[2,160,256]{2,1,0:T(8,128)(2,1)S(1)}, bf16[2,160,256]{2,1,0:T(8,128)(2,1)S(1)}, bf16[2,160,256]{2,1,0:T(8,128)(2,1)S(1)}) custom-call(s32[1]{0:T(128)} %bitcast.me_ref, s32[2,4]{1,0:T(2,128)} %bitcast.19, s32[2,4]{1,0:T(2,128)S(1)} %collective-permute-done.refs_0_, s32[2,4]{1,0:T(2,128)S(1)} %collective-permute-done.1.refs_1_, ...), custom_call_target="tpu_custom_call" | custom-call | tf_op jit(solution)/shard_map/pack/pallas_call | solution.py:93
  26.8 9.5 %collective-permute-done.3 = bf16[4,512,256]{2,1,0:T(8,128)(2,1)S(1)} collective-permute-done((bf16[4,512,256]{2,1,0:T(8,128)(2,1)S(1)}, bf16[4,512,256]{2,1,0:T(8,128)(2,1)S(1)}, u32[]{:S(2)}, u32[]{:S(2)}) %collective-permute-start.3) | collective-permute-done | bytes 1048608 | tf_op jit(solution)/shard_map/ppermute | solution.py:463
  36.5 4.7 %collective-permute-done.7.refs_2_ = bf16[2,160,256]{2,1,0:T(8,128)(2,1)S(1)} collective-permute-done((bf16[2,160,256]{2,1,0:T(8,128)(2,1)S(1)}, bf16[2,160,256]{2,1,0:T(8,128)(2,1)S(1)}, u32[]{:S(2)}, u32[]{:S(2)}) %collective-permute-start.7) | collective-permute-done | bytes 163872 | tf_op jit(solution)/shard_map/ppermute | solution.py:478
  41.2 4.1 %collective-permute-done.5.refs_1_ = bf16[2,352,256]{2,1,0:T(8,128)(2,1)S(1)} collective-permute-done((bf16[2,352,256]{2,1,0:T(8,128)(2,1)S(1)}, bf16[2,352,256]{2,1,0:T(8,128)(2,1)S(1)}, u32[]{:S(2)}, u32[]{:S(2)}) %collective-permute-start.5) | collective-permute-done | bytes 360480 | tf_op jit(solution)/shard_map/ppermute | solution.py:478
  45.3 0.9 select.2
  46.2 0.6 collective-permute-start.8
  46.8 2.5 %collective-permute-start.10 = (bf16[2,160,256]{2,1,0:T(8,128)(2,1)S(1)}, bf16[2,160,256]{2,1,0:T(8,128)(2,1)S(1)}, u32[]{:S(2)}, u32[]{:S(2)}) collective-permute-start(bf16[2,160,256]{2,1,0:T(8,128)(2,1)S(1)} %get-tuple-element.60), channel_id=1, source_target_pairs={{0,12},{4,8},{8,4},{12,0},{1,13},{5,9},{9,5},{13,1},{2,14},{6,10},... | collective-permute-start | bytes 491528 | tf_op jit(solution)/shard_map/ppermute | solution.py:478
  49.3 6.4 %collective-permute-done.10.refs_0_ = bf16[2,160,256]{2,1,0:T(8,128)(2,1)S(1)} collective-permute-done((bf16[2,160,256]{2,1,0:T(8,128)(2,1)S(1)}, bf16[2,160,256]{2,1,0:T(8,128)(2,1)S(1)}, u32[]{:S(2)}, u32[]{:S(2)}) %collective-permute-start.10) | collective-permute-done | bytes 163872 | tf_op jit(solution)/shard_map/ppermute | solution.py:478
  55.7 7.1 %collective-permute-done.11.refs_1_ = bf16[2,160,256]{2,1,0:T(8,128)(2,1)S(1)} collective-permute-done((bf16[2,160,256]{2,1,0:T(8,128)(2,1)S(1)}, bf16[2,160,256]{2,1,0:T(8,128)(2,1)S(1)}, u32[]{:S(2)}, u32[]{:S(2)}) %collective-permute-start.11) | collective-permute-done | bytes 163872 | tf_op jit(solution)/shard_map/ppermute | solution.py:478
  62.8 2.0 %collective-permute-done.8.refs_4_ = bf16[4,352,256]{2,1,0:T(8,128)(2,1)S(1)} collective-permute-done((bf16[4,352,256]{2,1,0:T(8,128)(2,1)S(1)}, bf16[4,352,256]{2,1,0:T(8,128)(2,1)S(1)}, u32[]{:S(2)}, u32[]{:S(2)}) %collective-permute-start.8) | collective-permute-done | bytes 720928 | tf_op jit(solution)/shard_map/ppermute | solution.py:463
  64.9 0.5 collective-permute-start.14
  65.4 0.8 select.3.refs_9_.refs_2_
  66.2 0.6 collective-permute-start.16
  66.8 0.3 collective-permute-done.14.refs_7_
  67.1 3.1 %first_window.1 = (f32[4,512,128]{2,1,0:T(8,128)S(1)}, f32[4,512,128]{2,1,0:T(8,128)S(1)}, f32[4,512,256]{2,1,0:T(8,128)S(1)}, f32[4,256]{1,0:T(4,128)S(1)}) custom-call(bf16[2,4,512,256]{3,2,1,0:T(8,128)(2,1)S(1)} %pad_maximum_fusion.refs_0_, bf16[2,4,512,256]{3,2,1,0:T(8,128)(2,1)S(1)} %collective-permute-done.9.refs_1_, ...), custom_call_target="tpu_custom_call" | custom-call | tf_op jit(solution)/shard_map/first_window/pallas_call | solution.py:286
  70.2 5.8 %collective-permute-done.16.refs_10_ = bf16[4,160,256]{2,1,0:T(8,128)(2,1)S(1)} collective-permute-done((bf16[4,160,256]{2,1,0:T(8,128)(2,1)S(1)}, bf16[4,160,256]{2,1,0:T(8,128)(2,1)S(1)}, u32[]{:S(2)}, u32[]{:S(2)}) %collective-permute-start.16) | collective-permute-done | bytes 327712 | tf_op jit(solution)/shard_map/ppermute | solution.py:463
  76.0 1.6 %collective-permute-done.18.refs_12_ = bf16[4,160,256]{2,1,0:T(8,128)(2,1)S(1)} collective-permute-done((bf16[4,160,256]{2,1,0:T(8,128)(2,1)S(1)}, bf16[4,160,256]{2,1,0:T(8,128)(2,1)S(1)}, u32[]{:S(2)}, u32[]{:S(2)}) %collective-permute-start.18) | collective-permute-done | bytes 327712 | tf_op jit(solution)/shard_map/ppermute | solution.py:463
  77.6 2.6 %last_window.1 = (bf16[4,512,256]{2,1,0:T(8,128)(2,1)S(1)}, f32[4,512,128]{2,1,0:T(8,128)S(1)}, f32[8,512]{1,0:T(8,128)S(1)}, f32[8,512]{1,0:T(8,128)S(1)}, f32[...) custom-call(s32[1]{0:T(128)} %bitcast.me_ref, s32[2,4]{1,0:T(2,128)} %bitcast.22, ...), custom_call_target="tpu_custom_call" | custom-call | flops 1073741824 | bytes 8388608 | tf_op jit(solution)/shard_map/last_window/pallas_call | solution.py:310
  80.3 2.6 %collective-permute-start.20 = (f32[8,512]{1,0:T(8,128)S(1)}, f32[8,512]{1,0:T(8,128)S(1)}, u32[]{:S(2)}, u32[]{:S(2)}) collective-permute-start(f32[8,512]{1,0:T(8,128)S(1)} %get-tuple-element.82), channel_id=1, source_target_pairs={{0,12},{4,8},{8,4},{12,0},{1,13},{5,9},{9,5},{13,1},{2,14},{6,10},... | collective-permute-start | bytes 49160 | tf_op jit(solution)/shard_map/ppermute | solution.py:478
  82.9 0.9 %collective-permute-start.21 = (f32[8,512]{1,0:T(8,128)S(1)}, f32[8,512]{1,0:T(8,128)S(1)}, u32[]{:S(2)}, u32[]{:S(2)}) collective-permute-start(f32[8,512]{1,0:T(8,128)S(1)} %get-tuple-element.83), channel_id=1, source_target_pairs={{0,4},{4,0},{8,12},{12,8},{1,5},{5,1},{9,13},{13,9},{2,6},{6,2},{1... | collective-permute-start | bytes 49160 | tf_op jit(solution)/shard_map/ppermute | solution.py:478
  83.8 2.3 %means.1 = bf16[8,512,256]{2,1,0:T(8,128)(2,1)} custom-call(s32[2,4]{1,0:T(2,128)} %bitcast.23, bf16[4,512,256]{2,1,0:T(8,128)(2,1)S(1)} %get-tuple-element.45.rows_ref, bf16[4,512,256]{2,1,0:T(8,128)(2,1)S(1)} %get-tuple-element.84.kernel_ref, f32[4,512,128]{2,1,0:T(8,128)S(1)} %get-tuple-element.85.mass_ref, ...), custom_call_target="tpu_custom_call", output_to_operand_aliasing={{}: (8, {})} | custom-call | flops 536870912 | bytes 8388608 | tf_op jit(solution)/shard_map/means/pallas_call | solution.py:415
  86.1 0.5 collective-permute-done.21.refs_4_
  86.6 0.6 weights.1
  (23 shorter events, 0.8 us)
Async XLA Ops:
  0.6 5.9 %collective-permute-start.2 = (s32[2,4]{1,0:T(2,128)}, s32[2,4]{1,0:T(2,128)S(1)}, u32[]{:S(2)}, u32[]{:S(2)}) collective-permute-start(s32[2,4]{1,0:T(2,128)} %bitcast.14), channel_id=1, source_target_pairs={{0,8},{4,12},{8,0},{12,4},{1,9},{5,13},{9,1},{13,5},{2,10},{6,14},... | collective-permute-start | bytes 104 | tf_op jit(solution)/shard_map/ppermute | solution.py:478
  4.7 5.6 %collective-permute-start.1 = (s32[2,4]{1,0:T(2,128)}, s32[2,4]{1,0:T(2,128)S(1)}, u32[]{:S(2)}, u32[]{:S(2)}) collective-permute-start(s32[2,4]{1,0:T(2,128)} %bitcast.15), channel_id=1, source_target_pairs={{0,12},{4,8},{8,4},{12,0},{1,13},{5,9},{9,5},{13,1},{2,14},{6,10},... | collective-permute-start | bytes 104 | tf_op jit(solution)/shard_map/ppermute | solution.py:478
  6.1 4.2 %collective-permute-start = (s32[2,4]{1,0:T(2,128)}, s32[2,4]{1,0:T(2,128)S(1)}, u32[]{:S(2)}, u32[]{:S(2)}) collective-permute-start(s32[2,4]{1,0:T(2,128)} %bitcast.16), channel_id=1, source_target_pairs={{0,4},{4,0},{8,12},{12,8},{1,5},{5,1},{9,13},{13,9},{2,6},{6,2},{1... | collective-permute-start | bytes 104 | tf_op jit(solution)/shard_map/ppermute | solution.py:478
  12.8 23.5 %collective-permute-start.3 = (bf16[4,512,256]{2,1,0:T(8,128)(2,1)S(1)}, bf16[4,512,256]{2,1,0:T(8,128)(2,1)S(1)}, u32[]{:S(2)}, u32[]{:S(2)}) collective-permute-start(bf16[4,512,256]{2,1,0:T(8,128)(2,1)S(1)} %get-tuple-element.45.rows_ref), channel_id=1, source_target_pairs={{0,2},{1,3},{2,0},{3,1},{4,6},{5,7},{6,4},{7,5},{8,10},{9,11},{10,... | collective-permute-start | bytes 3145736 | tf_op jit(solution)/shard_map/ppermute | solution.py:463
  14.3 26.8 %collective-permute-start.4 = (bf16[2,352,256]{2,1,0:T(8,128)(2,1)S(1)}, bf16[2,352,256]{2,1,0:T(8,128)(2,1)S(1)}, u32[]{:S(2)}, u32[]{:S(2)}) collective-permute-start(bf16[2,352,256]{2,1,0:T(8,128)(2,1)S(1)} %get-tuple-element.46), channel_id=1, source_target_pairs={{0,12},{4,8},{8,4},{12,0},{1,13},{5,9},{9,5},{13,1},{2,14},{6,10},... | collective-permute-start | bytes 1081352 | tf_op jit(solution)/shard_map/ppermute | solution.py:478
  16.3 28.9 %collective-permute-start.5 = (bf16[2,352,256]{2,1,0:T(8,128)(2,1)S(1)}, bf16[2,352,256]{2,1,0:T(8,128)(2,1)S(1)}, u32[]{:S(2)}, u32[]{:S(2)}) collective-permute-start(bf16[2,352,256]{2,1,0:T(8,128)(2,1)S(1)} %get-tuple-element.47), channel_id=1, source_target_pairs={{0,8},{4,12},{8,0},{12,4},{1,9},{5,13},{9,1},{13,5},{2,10},{6,14},... | collective-permute-start | bytes 1081352 | tf_op jit(solution)/shard_map/ppermute | solution.py:478
  16.3 28.9 %collective-permute-start.6 = (bf16[2,352,256]{2,1,0:T(8,128)(2,1)S(1)}, bf16[2,352,256]{2,1,0:T(8,128)(2,1)S(1)}, u32[]{:S(2)}, u32[]{:S(2)}) collective-permute-start(bf16[2,352,256]{2,1,0:T(8,128)(2,1)S(1)} %get-tuple-element.48), channel_id=1, source_target_pairs={{0,4},{4,0},{8,12},{12,8},{1,5},{5,1},{9,13},{13,9},{2,6},{6,2},{1... | collective-permute-start | bytes 1081352 | tf_op jit(solution)/shard_map/ppermute | solution.py:478
  26.6 14.5 %collective-permute-start.7 = (bf16[2,160,256]{2,1,0:T(8,128)(2,1)S(1)}, bf16[2,160,256]{2,1,0:T(8,128)(2,1)S(1)}, u32[]{:S(2)}, u32[]{:S(2)}) collective-permute-start(bf16[2,160,256]{2,1,0:T(8,128)(2,1)S(1)} %get-tuple-element.49), channel_id=1, source_target_pairs={{0,4},{4,0},{8,12},{12,8},{1,5},{5,1},{9,13},{13,9},{2,6},{6,2},{1... | collective-permute-start | bytes 491528 | tf_op jit(solution)/shard_map/ppermute | solution.py:478
  45.3 19.5 %collective-permute-start.9 = (bf16[2,4,512,256]{3,2,1,0:T(8,128)(2,1)S(1)}, bf16[2,4,512,256]{3,2,1,0:T(8,128)(2,1)S(1)}, u32[]{:S(2)}, u32[]{:S(2)}) collective-permute-start(bf16[2,4,512,256]{3,2,1,0:T(8,128)(2,1)S(1)} %pad_maximum_fusion.refs_0_), channel_id=1, source_target_pairs={{0,1},{1,0},{2,3},{3,2},{4,5},{5,4},{6,7},{7,6},{8,9},{9,8},{10,11... | collective-permute-start | bytes 6291464 | tf_op jit(solution)/shard_map/ppermute | solution.py:463
  46.2 18.6 %collective-permute-start.8 = (bf16[4,352,256]{2,1,0:T(8,128)(2,1)S(1)}, bf16[4,352,256]{2,1,0:T(8,128)(2,1)S(1)}, u32[]{:S(2)}, u32[]{:S(2)}) collective-permute-start(bf16[4,352,256]{2,1,0:T(8,128)(2,1)S(1)} %get-tuple-element.58), channel_id=1, source_target_pairs={{0,2},{1,3},{2,0},{3,1},{4,6},{5,7},{6,4},{7,5},{8,10},{9,11},{10,... | collective-permute-start | bytes 2162696 | tf_op jit(solution)/shard_map/ppermute | solution.py:463
  46.8 8.9 %collective-permute-start.10 = (bf16[2,160,256]{2,1,0:T(8,128)(2,1)S(1)}, bf16[2,160,256]{2,1,0:T(8,128)(2,1)S(1)}, u32[]{:S(2)}, u32[]{:S(2)}) collective-permute-start(bf16[2,160,256]{2,1,0:T(8,128)(2,1)S(1)} %get-tuple-element.60), channel_id=1, source_target_pairs={{0,12},{4,8},{8,4},{12,0},{1,13},{5,9},{9,5},{13,1},{2,14},{6,10},... | collective-permute-start | bytes 491528 | tf_op jit(solution)/shard_map/ppermute | solution.py:478
  49.3 13.5 %collective-permute-start.11 = (bf16[2,160,256]{2,1,0:T(8,128)(2,1)S(1)}, bf16[2,160,256]{2,1,0:T(8,128)(2,1)S(1)}, u32[]{:S(2)}, u32[]{:S(2)}) collective-permute-start(bf16[2,160,256]{2,1,0:T(8,128)(2,1)S(1)} %get-tuple-element.61), channel_id=1, source_target_pairs={{0,8},{4,12},{8,0},{12,4},{1,9},{5,13},{9,1},{13,5},{2,10},{6,14},... | collective-permute-start | bytes 491528 | tf_op jit(solution)/shard_map/ppermute | solution.py:478
  49.3 17.5 %collective-permute-start.12 = (bf16[2,352,256]{2,1,0:T(8,128)(2,1)S(1)}, bf16[2,352,256]{2,1,0:T(8,128)(2,1)S(1)}, u32[]{:S(2)}, u32[]{:S(2)}) collective-permute-start(bf16[2,352,256]{2,1,0:T(8,128)(2,1)S(1)} %get-tuple-element.64.refs_2_.refs_0_), channel_id=1, source_target_pairs={{0,1},{1,0},{2,3},{3,2},{4,5},{5,4},{6,7},{7,6},{8,9},{9,8},{10,11... | collective-permute-start | bytes 1081352 | tf_op jit(solution)/shard_map/ppermute | solution.py:463
  55.7 11.1 %collective-permute-start.13 = (bf16[2,352,256]{2,1,0:T(8,128)(2,1)S(1)}, bf16[2,352,256]{2,1,0:T(8,128)(2,1)S(1)}, u32[]{:S(2)}, u32[]{:S(2)}) collective-permute-start(bf16[2,352,256]{2,1,0:T(8,128)(2,1)S(1)} %get-tuple-element.65.refs_3_.refs_1_), channel_id=1, source_target_pairs={{0,1},{1,0},{2,3},{3,2},{4,5},{5,4},{6,7},{7,6},{8,9},{9,8},{10,11... | collective-permute-start | bytes 1081352 | tf_op jit(solution)/shard_map/ppermute | solution.py:463
  64.8 2.0 %collective-permute-start.15 = (bf16[2,352,256]{2,1,0:T(8,128)(2,1)S(1)}, bf16[2,352,256]{2,1,0:T(8,128)(2,1)S(1)}, u32[]{:S(2)}, u32[]{:S(2)}) collective-permute-start(bf16[2,352,256]{2,1,0:T(8,128)(2,1)S(1)} %get-tuple-element.88), channel_id=1, source_target_pairs={{0,1},{1,0},{2,3},{3,2},{4,5},{5,4},{6,7},{7,6},{8,9},{9,8},{10,11... | collective-permute-start | bytes 1081352 | tf_op jit(solution)/shard_map/ppermute | solution.py:463
  64.9 2.2 %collective-permute-start.14 = (bf16[2,352,256]{2,1,0:T(8,128)(2,1)S(1)}, bf16[2,352,256]{2,1,0:T(8,128)(2,1)S(1)}, u32[]{:S(2)}, u32[]{:S(2)}) collective-permute-start(bf16[2,352,256]{2,1,0:T(8,128)(2,1)S(1)} %get-tuple-element.89), channel_id=1, source_target_pairs={{0,1},{1,0},{2,3},{3,2},{4,5},{5,4},{6,7},{7,6},{8,9},{9,8},{10,11... | collective-permute-start | bytes 1081352 | tf_op jit(solution)/shard_map/ppermute | solution.py:463
  66.2 9.8 %collective-permute-start.16 = (bf16[4,160,256]{2,1,0:T(8,128)(2,1)S(1)}, bf16[4,160,256]{2,1,0:T(8,128)(2,1)S(1)}, u32[]{:S(2)}, u32[]{:S(2)}) collective-permute-start(bf16[4,160,256]{2,1,0:T(8,128)(2,1)S(1)} %select.3.refs_9_.refs_2_), channel_id=1, source_target_pairs={{0,2},{1,3},{2,0},{3,1},{4,6},{5,7},{6,4},{7,5},{8,10},{9,11},{10,... | collective-permute-start | bytes 983048 | tf_op jit(solution)/shard_map/ppermute | solution.py:463
  66.8 9.2 %collective-permute-start.17 = (bf16[4,160,256]{2,1,0:T(8,128)(2,1)S(1)}, bf16[4,160,256]{2,1,0:T(8,128)(2,1)S(1)}, u32[]{:S(2)}, u32[]{:S(2)}) collective-permute-start(bf16[4,160,256]{2,1,0:T(8,128)(2,1)S(1)} %select.3.refs_9_.refs_2_), channel_id=1, source_target_pairs={{0,1},{1,0},{2,3},{3,2},{4,5},{5,4},{6,7},{7,6},{8,9},{9,8},{10,11... | collective-permute-start | bytes 983048 | tf_op jit(solution)/shard_map/ppermute | solution.py:463
  76.0 1.6 %collective-permute-start.18 = (bf16[4,160,256]{2,1,0:T(8,128)(2,1)S(1)}, bf16[4,160,256]{2,1,0:T(8,128)(2,1)S(1)}, u32[]{:S(2)}, u32[]{:S(2)}) collective-permute-start(bf16[4,160,256]{2,1,0:T(8,128)(2,1)S(1)} %collective-permute-done.16.refs_10_), channel_id=1, source_target_pairs={{0,1},{1,0},{2,3},{3,2},{4,5},{5,4},{6,7},{7,6},{8,9},{9,8},{10,11... | collective-permute-start | bytes 983048 | tf_op jit(solution)/shard_map/ppermute | solution.py:463
  80.2 5.9 %collective-permute-start.19 = (f32[8,512]{1,0:T(8,128)S(1)}, f32[8,512]{1,0:T(8,128)S(1)}, u32[]{:S(2)}, u32[]{:S(2)}) collective-permute-start(f32[8,512]{1,0:T(8,128)S(1)} %get-tuple-element.81), channel_id=1, source_target_pairs={{0,8},{4,12},{8,0},{12,4},{1,9},{5,13},{9,1},{13,5},{2,10},{6,14},... | collective-permute-start | bytes 49160 | tf_op jit(solution)/shard_map/ppermute | solution.py:478
  80.3 5.8 %collective-permute-start.20 = (f32[8,512]{1,0:T(8,128)S(1)}, f32[8,512]{1,0:T(8,128)S(1)}, u32[]{:S(2)}, u32[]{:S(2)}) collective-permute-start(f32[8,512]{1,0:T(8,128)S(1)} %get-tuple-element.82), channel_id=1, source_target_pairs={{0,12},{4,8},{8,4},{12,0},{1,13},{5,9},{9,5},{13,1},{2,14},{6,10},... | collective-permute-start | bytes 49160 | tf_op jit(solution)/shard_map/ppermute | solution.py:478
  82.9 3.7 %collective-permute-start.21 = (f32[8,512]{1,0:T(8,128)S(1)}, f32[8,512]{1,0:T(8,128)S(1)}, u32[]{:S(2)}, u32[]{:S(2)}) collective-permute-start(f32[8,512]{1,0:T(8,128)S(1)} %get-tuple-element.83), channel_id=1, source_target_pairs={{0,4},{4,0},{8,12},{12,8},{1,5},{5,1},{9,13},{13,9},{2,6},{6,2},{1... | collective-permute-start | bytes 49160 | tf_op jit(solution)/shard_map/ppermute | solution.py:478

commit v25 on v24

--- a/solution.py
+++ b/solution.py
@@ -11,7 +11,7 @@
 BR = 512
 BLK_DEV = 8
 LANES = 128
-CHUNKS = ((0, 352), (352, 160))
+CHUNKS = ((0, 336), (336, 176))
 WINDOWS = ((0, 256), (256, 512))
 
 

time: 87.7 us -> 85.4 us (0.974)
  waiting for transfers between devices: 46 us -> 42.6 us
  starting transfers between devices: 19.6 us -> 20.7 us
    ppermute x10, waiting for transfers between devices: 19.2 us -> 15.7 us  [hop(): lax.ppermute(piece, 'narrow', perm)]
    ppermute x10, starting transfers between devices: 3.34 us -> 4.37 us  [hop(): lax.ppermute(piece, 'narrow', perm)]
  transfers between devices with their start and end apart: 22 -> 22, of which waited for: 12 -> 12; matrix products, arithmetic and copies ran while one was open for 0% -> 0% of each run, Pallas kernels for 17% -> 18%
where the time goes in v25:
time: 85.4 us; the launch traced here: 85 us
  waiting for transfers between devices  42.6 us (50%)
  Pallas kernels  20.8 us (24%)
  starting transfers between devices  20.7 us (24%)
    ppermute x12, waiting for transfers between devices, to_wide(): lax.ppermute(piece, 'wide', [(i, i ^ other) for i in range(count)])  26.8 us
    ppermute x12, starting transfers between devices, to_wide(): lax.ppermute(piece, 'wide', [(i, i ^ other) for i in range(count)])  16.3 us
    ppermute x10, waiting for transfers between devices, hop(): lax.ppermute(piece, 'narrow', perm)  15.7 us
    pallas_call x1, Pallas kernels, keep(): pl.pallas_call(keep_kernel, out_shape=[pltpu.HBM(blocks.shape, blocks.dty...  6.05 us
    ppermute x10, starting transfers between devices, hop(): lax.ppermute(piece, 'narrow', perm)  4.37 us
    pallas_call x2, Pallas kernels, pack(): pl.pallas_call(functools.partial(pack_kernel, chunk, with_rows, wide_coun...  4.35 us
    pallas_call x1, Pallas kernels, first_window(): pl.pallas_call(functools.partial(first_kernel, window, piece_counts(windo...  3.1 us
    pallas_call x1, Pallas kernels, last_window(): pl.pallas_call(functools.partial(last_kernel, window, piece_counts(window...  2.65 us
  transfers between devices with their start and end apart: 22, of which 12 were waited for; matrix products, arithmetic and copies ran while one was open for 0% of the time, Pallas kernels for 18%

profile of v25, /device:TPU:0, one launch (start us, length us, event | category | flops | bytes accessed | tf_op | source)
XLA Modules:
  0.0 85.0 jit_solution(15355109007465176126)
XLA Ops:
  0.6 4.1 %collective-permute-start.2 = (s32[2,4]{1,0:T(2,128)}, s32[2,4]{1,0:T(2,128)S(1)}, u32[]{:S(2)}, u32[]{:S(2)}) collective-permute-start(s32[2,4]{1,0:T(2,128)} %bitcast.14), channel_id=1, source_target_pairs={{0,8},{4,12},{8,0},{12,4},{1,9},{5,13},{9,1},{13,5},{2,10},{6,14},... | collective-permute-start | bytes 104 | tf_op jit(solution)/shard_map/ppermute | solution.py:478
  4.7 1.3 %collective-permute-start.1 = (s32[2,4]{1,0:T(2,128)}, s32[2,4]{1,0:T(2,128)S(1)}, u32[]{:S(2)}, u32[]{:S(2)}) collective-permute-start(s32[2,4]{1,0:T(2,128)} %bitcast.15), channel_id=1, source_target_pairs={{0,12},{4,8},{8,4},{12,0},{1,13},{5,9},{9,5},{13,1},{2,14},{6,10},... | collective-permute-start | bytes 104 | tf_op jit(solution)/shard_map/ppermute | solution.py:478
  6.1 0.2 collective-permute-start
  6.5 3.8 %collective-permute-done.1.refs_1_ = s32[2,4]{1,0:T(2,128)S(1)} collective-permute-done((s32[2,4]{1,0:T(2,128)}, s32[2,4]{1,0:T(2,128)S(1)}, u32[]{:S(2)}, u32[]{:S(2)}) %collective-permute-start.1) | collective-permute-done | bytes 64 | tf_op jit(solution)/shard_map/ppermute | solution.py:478
  10.3 2.5 %pack.2 = (bf16[2,336,256]{2,1,0:T(8,128)(2,1)S(1)}, bf16[2,336,256]{2,1,0:T(8,128)(2,1)S(1)}, bf16[2,336,256]{2,1,0:T(8,128)(2,1)S(1)}, bf16[4,512,256]{2,1,0:T(8,128)(2,1)S(1)}) custom-call(s32[1]{0:T(128)} %bitcast.me_ref, s32[2,4]{1,0:T(2,128)} %bitcast.17, s32[2,4]{1,0:T(2,128)S(1)} %collective-permute-done.refs_0_, ...), custom_call_target="tpu_custom_call" | custom-call | tf_op jit(solution)/shard_map/pack/pallas_call | solution.py:93
  12.8 1.6 %collective-permute-start.3 = (bf16[4,512,256]{2,1,0:T(8,128)(2,1)S(1)}, bf16[4,512,256]{2,1,0:T(8,128)(2,1)S(1)}, u32[]{:S(2)}, u32[]{:S(2)}) collective-permute-start(bf16[4,512,256]{2,1,0:T(8,128)(2,1)S(1)} %get-tuple-element.45.rows_ref), channel_id=1, source_target_pairs={{0,2},{1,3},{2,0},{3,1},{4,6},{5,7},{6,4},{7,5},{8,10},{9,11},{10,... | collective-permute-start | bytes 3145736 | tf_op jit(solution)/shard_map/ppermute | solution.py:463
  14.3 2.0 %collective-permute-start.4 = (bf16[2,336,256]{2,1,0:T(8,128)(2,1)S(1)}, bf16[2,336,256]{2,1,0:T(8,128)(2,1)S(1)}, u32[]{:S(2)}, u32[]{:S(2)}) collective-permute-start(bf16[2,336,256]{2,1,0:T(8,128)(2,1)S(1)} %get-tuple-element.46), channel_id=1, source_target_pairs={{0,12},{4,8},{8,4},{12,0},{1,13},{5,9},{9,5},{13,1},{2,14},{6,10},... | collective-permute-start | bytes 1032200 | tf_op jit(solution)/shard_map/ppermute | solution.py:478
  16.4 2.4 %collective-permute-start.6 = (bf16[2,336,256]{2,1,0:T(8,128)(2,1)S(1)}, bf16[2,336,256]{2,1,0:T(8,128)(2,1)S(1)}, u32[]{:S(2)}, u32[]{:S(2)}) collective-permute-start(bf16[2,336,256]{2,1,0:T(8,128)(2,1)S(1)} %get-tuple-element.48), channel_id=1, source_target_pairs={{0,4},{4,0},{8,12},{12,8},{1,5},{5,1},{9,13},{13,9},{2,6},{6,2},{1... | collective-permute-start | bytes 1032200 | tf_op jit(solution)/shard_map/ppermute | solution.py:478
  18.7 1.9 %pack.3 = (bf16[2,176,256]{2,1,0:T(8,128)(2,1)S(1)}, bf16[2,176,256]{2,1,0:T(8,128)(2,1)S(1)}, bf16[2,176,256]{2,1,0:T(8,128)(2,1)S(1)}) custom-call(s32[1]{0:T(128)} %bitcast.me_ref, s32[2,4]{1,0:T(2,128)} %bitcast.18, s32[2,4]{1,0:T(2,128)S(1)} %collective-permute-done.refs_0_, s32[2,4]{1,0:T(2,128)S(1)} %collective-permute-done.1.refs_1_, ...), custom_call_target="tpu_custom_call" | custom-call | tf_op jit(solution)/shard_map/pack/pallas_call | solution.py:93
  20.7 6.0 %keep.1 = (bf16[8,512,256]{2,1,0:T(8,128)(2,1)}, bf16[4,512,256]{2,1,0:T(8,128)(2,1)S(1)}) custom-call(s32[2,4]{1,0:T(2,128)} %bitcast.19, bf16[8,512,256]{2,1,0:T(8,128)(2,1)} %bitcast.10, bf16[8,512,256]{2,1,0:T(8,128)(2,1)} %bitcast.11), custom_call_target="tpu_custom_call" | custom-call | tf_op jit(solution)/shard_map/keep/pallas_call | solution.py:346
  26.8 9.6 %collective-permute-done.3 = bf16[4,512,256]{2,1,0:T(8,128)(2,1)S(1)} collective-permute-done((bf16[4,512,256]{2,1,0:T(8,128)(2,1)S(1)}, bf16[4,512,256]{2,1,0:T(8,128)(2,1)S(1)}, u32[]{:S(2)}, u32[]{:S(2)}) %collective-permute-start.3) | collective-permute-done | bytes 1048608 | tf_op jit(solution)/shard_map/ppermute | solution.py:463
  36.5 4.0 %collective-permute-done.7.refs_2_ = bf16[2,176,256]{2,1,0:T(8,128)(2,1)S(1)} collective-permute-done((bf16[2,176,256]{2,1,0:T(8,128)(2,1)S(1)}, bf16[2,176,256]{2,1,0:T(8,128)(2,1)S(1)}, u32[]{:S(2)}, u32[]{:S(2)}) %collective-permute-start.7) | collective-permute-done | bytes 180256 | tf_op jit(solution)/shard_map/ppermute | solution.py:478
  40.5 3.4 %collective-permute-done.5.refs_1_ = bf16[2,336,256]{2,1,0:T(8,128)(2,1)S(1)} collective-permute-done((bf16[2,336,256]{2,1,0:T(8,128)(2,1)S(1)}, bf16[2,336,256]{2,1,0:T(8,128)(2,1)S(1)}, u32[]{:S(2)}, u32[]{:S(2)}) %collective-permute-start.5) | collective-permute-done | bytes 344096 | tf_op jit(solution)/shard_map/ppermute | solution.py:478
  43.9 0.9 %select.2 = (bf16[2,336,256]{2,1,0:T(8,128)(2,1)S(1)}, bf16[2,336,256]{2,1,0:T(8,128)(2,1)S(1)}, bf16[4,336,256]{2,1,0:T(8,128)(2,1)S(1)}) custom-call(s32[1]{0:T(128)} %bitcast.me_ref, s32[2,4]{1,0:T(2,128)} %bitcast.20, bf16[4,512,256]{2,1,0:T(8,128)(2,1)S(1)} %get-tuple-element.52.own_ref, bf16[2,336,256]{2,1,0:T(8,128)(2,1)S(1)} %collective-permute-done.4.refs_0_, ...), custom_call_target="tpu_custom_call" | custom-call | tf_op jit(solution)/shard_map/select/pallas_call | solution.py:141
  44.8 0.6 collective-permute-start.8
  45.4 2.6 %collective-permute-start.10 = (bf16[2,176,256]{2,1,0:T(8,128)(2,1)S(1)}, bf16[2,176,256]{2,1,0:T(8,128)(2,1)S(1)}, u32[]{:S(2)}, u32[]{:S(2)}) collective-permute-start(bf16[2,176,256]{2,1,0:T(8,128)(2,1)S(1)} %get-tuple-element.60), channel_id=1, source_target_pairs={{0,12},{4,8},{8,4},{12,0},{1,13},{5,9},{9,5},{13,1},{2,14},{6,10},... | collective-permute-start | bytes 540680 | tf_op jit(solution)/shard_map/ppermute | solution.py:478
  48.0 6.6 %collective-permute-done.10.refs_0_ = bf16[2,176,256]{2,1,0:T(8,128)(2,1)S(1)} collective-permute-done((bf16[2,176,256]{2,1,0:T(8,128)(2,1)S(1)}, bf16[2,176,256]{2,1,0:T(8,128)(2,1)S(1)}, u32[]{:S(2)}, u32[]{:S(2)}) %collective-permute-start.10) | collective-permute-done | bytes 180256 | tf_op jit(solution)/shard_map/ppermute | solution.py:478
  54.6 8.2 %collective-permute-done.11.refs_1_ = bf16[2,176,256]{2,1,0:T(8,128)(2,1)S(1)} collective-permute-done((bf16[2,176,256]{2,1,0:T(8,128)(2,1)S(1)}, bf16[2,176,256]{2,1,0:T(8,128)(2,1)S(1)}, u32[]{:S(2)}, u32[]{:S(2)}) %collective-permute-start.11) | collective-permute-done | bytes 180256 | tf_op jit(solution)/shard_map/ppermute | solution.py:478
  62.9 0.8 select.3.refs_9_.refs_2_
  63.7 1.6 %collective-permute-start.16 = (bf16[4,176,256]{2,1,0:T(8,128)(2,1)S(1)}, bf16[4,176,256]{2,1,0:T(8,128)(2,1)S(1)}, u32[]{:S(2)}, u32[]{:S(2)}) collective-permute-start(bf16[4,176,256]{2,1,0:T(8,128)(2,1)S(1)} %select.3.refs_9_.refs_2_), channel_id=1, source_target_pairs={{0,2},{1,3},{2,0},{3,1},{4,6},{5,7},{6,4},{7,5},{8,10},{9,11},{10,... | collective-permute-start | bytes 1081352 | tf_op jit(solution)/shard_map/ppermute | solution.py:463
  65.4 0.5 collective-permute-start.14
  66.0 1.1 %collective-permute-done.15.refs_8_ = bf16[2,336,256]{2,1,0:T(8,128)(2,1)S(1)} collective-permute-done((bf16[2,336,256]{2,1,0:T(8,128)(2,1)S(1)}, bf16[2,336,256]{2,1,0:T(8,128)(2,1)S(1)}, u32[]{:S(2)}, u32[]{:S(2)}) %collective-permute-start.15) | collective-permute-done | bytes 344096 | tf_op jit(solution)/shard_map/ppermute | solution.py:463
  67.0 0.5 collective-permute-done.14.refs_7_
  67.5 3.1 %first_window.1 = (f32[4,512,128]{2,1,0:T(8,128)S(1)}, f32[4,512,128]{2,1,0:T(8,128)S(1)}, f32[4,512,256]{2,1,0:T(8,128)S(1)}, f32[4,256]{1,0:T(4,128)S(1)}) custom-call(bf16[2,4,512,256]{3,2,1,0:T(8,128)(2,1)S(1)} %pad_maximum_fusion.refs_0_, bf16[2,4,512,256]{3,2,1,0:T(8,128)(2,1)S(1)} %collective-permute-done.9.refs_1_, ...), custom_call_target="tpu_custom_call" | custom-call | tf_op jit(solution)/shard_map/first_window/pallas_call | solution.py:286
  70.6 3.0 %collective-permute-done.16.refs_10_ = bf16[4,176,256]{2,1,0:T(8,128)(2,1)S(1)} collective-permute-done((bf16[4,176,256]{2,1,0:T(8,128)(2,1)S(1)}, bf16[4,176,256]{2,1,0:T(8,128)(2,1)S(1)}, u32[]{:S(2)}, u32[]{:S(2)}) %collective-permute-start.16) | collective-permute-done | bytes 360480 | tf_op jit(solution)/shard_map/ppermute | solution.py:463
  73.6 1.7 %collective-permute-done.18.refs_12_ = bf16[4,176,256]{2,1,0:T(8,128)(2,1)S(1)} collective-permute-done((bf16[4,176,256]{2,1,0:T(8,128)(2,1)S(1)}, bf16[4,176,256]{2,1,0:T(8,128)(2,1)S(1)}, u32[]{:S(2)}, u32[]{:S(2)}) %collective-permute-start.18) | collective-permute-done | bytes 360480 | tf_op jit(solution)/shard_map/ppermute | solution.py:463
  75.3 2.7 %last_window.1 = (bf16[4,512,256]{2,1,0:T(8,128)(2,1)S(1)}, f32[4,512,128]{2,1,0:T(8,128)S(1)}, f32[8,512]{1,0:T(8,128)S(1)}, f32[8,512]{1,0:T(8,128)S(1)}, f32[...) custom-call(s32[1]{0:T(128)} %bitcast.me_ref, s32[2,4]{1,0:T(2,128)} %bitcast.22, ...), custom_call_target="tpu_custom_call" | custom-call | flops 1073741824 | bytes 8388608 | tf_op jit(solution)/shard_map/last_window/pallas_call | solution.py:310
  78.0 2.7 %collective-permute-start.20 = (f32[8,512]{1,0:T(8,128)S(1)}, f32[8,512]{1,0:T(8,128)S(1)}, u32[]{:S(2)}, u32[]{:S(2)}) collective-permute-start(f32[8,512]{1,0:T(8,128)S(1)} %get-tuple-element.82), channel_id=1, source_target_pairs={{0,12},{4,8},{8,4},{12,0},{1,13},{5,9},{9,5},{13,1},{2,14},{6,10},... | collective-permute-start | bytes 49160 | tf_op jit(solution)/shard_map/ppermute | solution.py:478
  80.7 0.8 collective-permute-start.21
  81.5 2.3 %means.1 = bf16[8,512,256]{2,1,0:T(8,128)(2,1)} custom-call(s32[2,4]{1,0:T(2,128)} %bitcast.23, bf16[4,512,256]{2,1,0:T(8,128)(2,1)S(1)} %get-tuple-element.45.rows_ref, bf16[4,512,256]{2,1,0:T(8,128)(2,1)S(1)} %get-tuple-element.84.kernel_ref, f32[4,512,128]{2,1,0:T(8,128)S(1)} %get-tuple-element.85.mass_ref, ...), custom_call_target="tpu_custom_call", output_to_operand_aliasing={{}: (8, {})} | custom-call | flops 536870912 | bytes 8388608 | tf_op jit(solution)/shard_map/means/pallas_call | solution.py:415
  83.8 0.6 collective-permute-done.21.refs_4_
  84.4 0.6 weights.1
  (23 shorter events, 0.8 us)
Async XLA Ops:
  0.6 5.9 %collective-permute-start.2 = (s32[2,4]{1,0:T(2,128)}, s32[2,4]{1,0:T(2,128)S(1)}, u32[]{:S(2)}, u32[]{:S(2)}) collective-permute-start(s32[2,4]{1,0:T(2,128)} %bitcast.14), channel_id=1, source_target_pairs={{0,8},{4,12},{8,0},{12,4},{1,9},{5,13},{9,1},{13,5},{2,10},{6,14},... | collective-permute-start | bytes 104 | tf_op jit(solution)/shard_map/ppermute | solution.py:478
  4.7 5.6 %collective-permute-start.1 = (s32[2,4]{1,0:T(2,128)}, s32[2,4]{1,0:T(2,128)S(1)}, u32[]{:S(2)}, u32[]{:S(2)}) collective-permute-start(s32[2,4]{1,0:T(2,128)} %bitcast.15), channel_id=1, source_target_pairs={{0,12},{4,8},{8,4},{12,0},{1,13},{5,9},{9,5},{13,1},{2,14},{6,10},... | collective-permute-start | bytes 104 | tf_op jit(solution)/shard_map/ppermute | solution.py:478
  6.1 4.2 %collective-permute-start = (s32[2,4]{1,0:T(2,128)}, s32[2,4]{1,0:T(2,128)S(1)}, u32[]{:S(2)}, u32[]{:S(2)}) collective-permute-start(s32[2,4]{1,0:T(2,128)} %bitcast.16), channel_id=1, source_target_pairs={{0,4},{4,0},{8,12},{12,8},{1,5},{5,1},{9,13},{13,9},{2,6},{6,2},{1... | collective-permute-start | bytes 104 | tf_op jit(solution)/shard_map/ppermute | solution.py:478
  12.8 23.5 %collective-permute-start.3 = (bf16[4,512,256]{2,1,0:T(8,128)(2,1)S(1)}, bf16[4,512,256]{2,1,0:T(8,128)(2,1)S(1)}, u32[]{:S(2)}, u32[]{:S(2)}) collective-permute-start(bf16[4,512,256]{2,1,0:T(8,128)(2,1)S(1)} %get-tuple-element.45.rows_ref), channel_id=1, source_target_pairs={{0,2},{1,3},{2,0},{3,1},{4,6},{5,7},{6,4},{7,5},{8,10},{9,11},{10,... | collective-permute-start | bytes 3145736 | tf_op jit(solution)/shard_map/ppermute | solution.py:463
  14.3 26.1 %collective-permute-start.4 = (bf16[2,336,256]{2,1,0:T(8,128)(2,1)S(1)}, bf16[2,336,256]{2,1,0:T(8,128)(2,1)S(1)}, u32[]{:S(2)}, u32[]{:S(2)}) collective-permute-start(bf16[2,336,256]{2,1,0:T(8,128)(2,1)S(1)} %get-tuple-element.46), channel_id=1, source_target_pairs={{0,12},{4,8},{8,4},{12,0},{1,13},{5,9},{9,5},{13,1},{2,14},{6,10},... | collective-permute-start | bytes 1032200 | tf_op jit(solution)/shard_map/ppermute | solution.py:478
  16.4 27.5 %collective-permute-start.5 = (bf16[2,336,256]{2,1,0:T(8,128)(2,1)S(1)}, bf16[2,336,256]{2,1,0:T(8,128)(2,1)S(1)}, u32[]{:S(2)}, u32[]{:S(2)}) collective-permute-start(bf16[2,336,256]{2,1,0:T(8,128)(2,1)S(1)} %get-tuple-element.47), channel_id=1, source_target_pairs={{0,8},{4,12},{8,0},{12,4},{1,9},{5,13},{9,1},{13,5},{2,10},{6,14},... | collective-permute-start | bytes 1032200 | tf_op jit(solution)/shard_map/ppermute | solution.py:478
  16.4 27.5 %collective-permute-start.6 = (bf16[2,336,256]{2,1,0:T(8,128)(2,1)S(1)}, bf16[2,336,256]{2,1,0:T(8,128)(2,1)S(1)}, u32[]{:S(2)}, u32[]{:S(2)}) collective-permute-start(bf16[2,336,256]{2,1,0:T(8,128)(2,1)S(1)} %get-tuple-element.48), channel_id=1, source_target_pairs={{0,4},{4,0},{8,12},{12,8},{1,5},{5,1},{9,13},{13,9},{2,6},{6,2},{1... | collective-permute-start | bytes 1032200 | tf_op jit(solution)/shard_map/ppermute | solution.py:478
  20.6 19.8 %collective-permute-start.7 = (bf16[2,176,256]{2,1,0:T(8,128)(2,1)S(1)}, bf16[2,176,256]{2,1,0:T(8,128)(2,1)S(1)}, u32[]{:S(2)}, u32[]{:S(2)}) collective-permute-start(bf16[2,176,256]{2,1,0:T(8,128)(2,1)S(1)} %get-tuple-element.49), channel_id=1, source_target_pairs={{0,4},{4,0},{8,12},{12,8},{1,5},{5,1},{9,13},{13,9},{2,6},{6,2},{1... | collective-permute-start | bytes 540680 | tf_op jit(solution)/shard_map/ppermute | solution.py:478
  43.9 19.0 %collective-permute-start.9 = (bf16[2,4,512,256]{3,2,1,0:T(8,128)(2,1)S(1)}, bf16[2,4,512,256]{3,2,1,0:T(8,128)(2,1)S(1)}, u32[]{:S(2)}, u32[]{:S(2)}) collective-permute-start(bf16[2,4,512,256]{3,2,1,0:T(8,128)(2,1)S(1)} %pad_maximum_fusion.refs_0_), channel_id=1, source_target_pairs={{0,1},{1,0},{2,3},{3,2},{4,5},{5,4},{6,7},{7,6},{8,9},{9,8},{10,11... | collective-permute-start | bytes 6291464 | tf_op jit(solution)/shard_map/ppermute | solution.py:463
  44.8 18.1 %collective-permute-start.8 = (bf16[4,336,256]{2,1,0:T(8,128)(2,1)S(1)}, bf16[4,336,256]{2,1,0:T(8,128)(2,1)S(1)}, u32[]{:S(2)}, u32[]{:S(2)}) collective-permute-start(bf16[4,336,256]{2,1,0:T(8,128)(2,1)S(1)} %get-tuple-element.58), channel_id=1, source_target_pairs={{0,2},{1,3},{2,0},{3,1},{4,6},{5,7},{6,4},{7,5},{8,10},{9,11},{10,... | collective-permute-start | bytes 2064392 | tf_op jit(solution)/shard_map/ppermute | solution.py:463
  45.4 9.3 %collective-permute-start.10 = (bf16[2,176,256]{2,1,0:T(8,128)(2,1)S(1)}, bf16[2,176,256]{2,1,0:T(8,128)(2,1)S(1)}, u32[]{:S(2)}, u32[]{:S(2)}) collective-permute-start(bf16[2,176,256]{2,1,0:T(8,128)(2,1)S(1)} %get-tuple-element.60), channel_id=1, source_target_pairs={{0,12},{4,8},{8,4},{12,0},{1,13},{5,9},{9,5},{13,1},{2,14},{6,10},... | collective-permute-start | bytes 540680 | tf_op jit(solution)/shard_map/ppermute | solution.py:478
  48.0 14.9 %collective-permute-start.11 = (bf16[2,176,256]{2,1,0:T(8,128)(2,1)S(1)}, bf16[2,176,256]{2,1,0:T(8,128)(2,1)S(1)}, u32[]{:S(2)}, u32[]{:S(2)}) collective-permute-start(bf16[2,176,256]{2,1,0:T(8,128)(2,1)S(1)} %get-tuple-element.61), channel_id=1, source_target_pairs={{0,8},{4,12},{8,0},{12,4},{1,9},{5,13},{9,1},{13,5},{2,10},{6,14},... | collective-permute-start | bytes 540680 | tf_op jit(solution)/shard_map/ppermute | solution.py:478
  48.0 17.9 %collective-permute-start.12 = (bf16[2,336,256]{2,1,0:T(8,128)(2,1)S(1)}, bf16[2,336,256]{2,1,0:T(8,128)(2,1)S(1)}, u32[]{:S(2)}, u32[]{:S(2)}) collective-permute-start(bf16[2,336,256]{2,1,0:T(8,128)(2,1)S(1)} %get-tuple-element.64.refs_2_.refs_0_), channel_id=1, source_target_pairs={{0,1},{1,0},{2,3},{3,2},{4,5},{5,4},{6,7},{7,6},{8,9},{9,8},{10,11... | collective-permute-start | bytes 1032200 | tf_op jit(solution)/shard_map/ppermute | solution.py:463
  54.6 11.3 %collective-permute-start.13 = (bf16[2,336,256]{2,1,0:T(8,128)(2,1)S(1)}, bf16[2,336,256]{2,1,0:T(8,128)(2,1)S(1)}, u32[]{:S(2)}, u32[]{:S(2)}) collective-permute-start(bf16[2,336,256]{2,1,0:T(8,128)(2,1)S(1)} %get-tuple-element.65.refs_3_.refs_1_), channel_id=1, source_target_pairs={{0,1},{1,0},{2,3},{3,2},{4,5},{5,4},{6,7},{7,6},{8,9},{9,8},{10,11... | collective-permute-start | bytes 1032200 | tf_op jit(solution)/shard_map/ppermute | solution.py:463
  63.7 9.9 %collective-permute-start.16 = (bf16[4,176,256]{2,1,0:T(8,128)(2,1)S(1)}, bf16[4,176,256]{2,1,0:T(8,128)(2,1)S(1)}, u32[]{:S(2)}, u32[]{:S(2)}) collective-permute-start(bf16[4,176,256]{2,1,0:T(8,128)(2,1)S(1)} %select.3.refs_9_.refs_2_), channel_id=1, source_target_pairs={{0,2},{1,3},{2,0},{3,1},{4,6},{5,7},{6,4},{7,5},{8,10},{9,11},{10,... | collective-permute-start | bytes 1081352 | tf_op jit(solution)/shard_map/ppermute | solution.py:463
  65.3 1.7 %collective-permute-start.15 = (bf16[2,336,256]{2,1,0:T(8,128)(2,1)S(1)}, bf16[2,336,256]{2,1,0:T(8,128)(2,1)S(1)}, u32[]{:S(2)}, u32[]{:S(2)}) collective-permute-start(bf16[2,336,256]{2,1,0:T(8,128)(2,1)S(1)} %get-tuple-element.88), channel_id=1, source_target_pairs={{0,1},{1,0},{2,3},{3,2},{4,5},{5,4},{6,7},{7,6},{8,9},{9,8},{10,11... | collective-permute-start | bytes 1032200 | tf_op jit(solution)/shard_map/ppermute | solution.py:463
  65.4 2.1 %collective-permute-start.14 = (bf16[2,336,256]{2,1,0:T(8,128)(2,1)S(1)}, bf16[2,336,256]{2,1,0:T(8,128)(2,1)S(1)}, u32[]{:S(2)}, u32[]{:S(2)}) collective-permute-start(bf16[2,336,256]{2,1,0:T(8,128)(2,1)S(1)} %get-tuple-element.89), channel_id=1, source_target_pairs={{0,1},{1,0},{2,3},{3,2},{4,5},{5,4},{6,7},{7,6},{8,9},{9,8},{10,11... | collective-permute-start | bytes 1032200 | tf_op jit(solution)/shard_map/ppermute | solution.py:463
  65.9 7.7 %collective-permute-start.17 = (bf16[4,176,256]{2,1,0:T(8,128)(2,1)S(1)}, bf16[4,176,256]{2,1,0:T(8,128)(2,1)S(1)}, u32[]{:S(2)}, u32[]{:S(2)}) collective-permute-start(bf16[4,176,256]{2,1,0:T(8,128)(2,1)S(1)} %select.3.refs_9_.refs_2_), channel_id=1, source_target_pairs={{0,1},{1,0},{2,3},{3,2},{4,5},{5,4},{6,7},{7,6},{8,9},{9,8},{10,11... | collective-permute-start | bytes 1081352 | tf_op jit(solution)/shard_map/ppermute | solution.py:463
  73.6 1.7 %collective-permute-start.18 = (bf16[4,176,256]{2,1,0:T(8,128)(2,1)S(1)}, bf16[4,176,256]{2,1,0:T(8,128)(2,1)S(1)}, u32[]{:S(2)}, u32[]{:S(2)}) collective-permute-start(bf16[4,176,256]{2,1,0:T(8,128)(2,1)S(1)} %collective-permute-done.16.refs_10_), channel_id=1, source_target_pairs={{0,1},{1,0},{2,3},{3,2},{4,5},{5,4},{6,7},{7,6},{8,9},{9,8},{10,11... | collective-permute-start | bytes 1081352 | tf_op jit(solution)/shard_map/ppermute | solution.py:463
  77.9 5.9 %collective-permute-start.19 = (f32[8,512]{1,0:T(8,128)S(1)}, f32[8,512]{1,0:T(8,128)S(1)}, u32[]{:S(2)}, u32[]{:S(2)}) collective-permute-start(f32[8,512]{1,0:T(8,128)S(1)} %get-tuple-element.81), channel_id=1, source_target_pairs={{0,8},{4,12},{8,0},{12,4},{1,9},{5,13},{9,1},{13,5},{2,10},{6,14},... | collective-permute-start | bytes 49160 | tf_op jit(solution)/shard_map/ppermute | solution.py:478
  78.0 5.8 %collective-permute-start.20 = (f32[8,512]{1,0:T(8,128)S(1)}, f32[8,512]{1,0:T(8,128)S(1)}, u32[]{:S(2)}, u32[]{:S(2)}) collective-permute-start(f32[8,512]{1,0:T(8,128)S(1)} %get-tuple-element.82), channel_id=1, source_target_pairs={{0,12},{4,8},{8,4},{12,0},{1,13},{5,9},{9,5},{13,1},{2,14},{6,10},... | collective-permute-start | bytes 49160 | tf_op jit(solution)/shard_map/ppermute | solution.py:478
  80.7 3.7 %collective-permute-start.21 = (f32[8,512]{1,0:T(8,128)S(1)}, f32[8,512]{1,0:T(8,128)S(1)}, u32[]{:S(2)}, u32[]{:S(2)}) collective-permute-start(f32[8,512]{1,0:T(8,128)S(1)} %get-tuple-element.83), channel_id=1, source_target_pairs={{0,4},{4,0},{8,12},{12,8},{1,5},{5,1},{9,13},{13,9},{2,6},{6,2},{1... | collective-permute-start | bytes 49160 | tf_op jit(solution)/shard_map/ppermute | solution.py:478

commit v26 on v25

--- a/solution.py
+++ b/solution.py
@@ -40,7 +40,8 @@
 
 
 def others(wide_count):
-    return range(wide_count - 1, 0, -1)
+    middle = wide_count // 2
+    return [middle] + [other for other in range(wide_count - 1, 0, -1) if other != middle]
 
 
 def pack_kernel(chunk, with_rows, wide_count, pair_count, capacity, me_ref, pairs_ref, *refs):
@@ -489,7 +490,7 @@
     feat = embeddings.shape[1]
     blocks = embeddings.reshape(BLK_DEV, BR, feat)
     apart = others(wide_count)
-    lists = to_wide([pairs] * (wide_count - 1), apart[::-1])
+    lists = to_wide([pairs] * (wide_count - 1), range(1, wide_count))
     fixed = lax.optimization_barrier
     *outgoing, row_slices = pack(me, pairs, lists, blocks, capacity, 0, True)
     later = pack(me, pairs, lists, blocks, capacity, 1, False)

time: 85.4 us -> 87.5 us (1.025)
  starting transfers between devices: 20.7 us -> 24.7 us
  waiting for transfers between devices: 42.6 us -> 40.6 us
    ppermute x12, starting transfers between devices: 16.3 us -> 20.5 us  [to_wide(): lax.ppermute(piece, 'wide', [(i, i ^ other) for i in range(count)])]
    ppermute x12, waiting for transfers between devices: 26.8 us -> 23.3 us  [to_wide(): lax.ppermute(piece, 'wide', [(i, i ^ other) for i in range(count)])]
    ppermute x10, waiting for transfers between devices: 15.7 us -> 17.4 us  [hop(): lax.ppermute(piece, 'narrow', perm)]
  transfers between devices with their start and end apart: 22 -> 22, of which waited for: 12 -> 12; matrix products, arithmetic and copies ran while one was open for 0% -> 0% of each run, Pallas kernels for 18% -> 17%
where the time goes in v26:
time: 87.5 us; the launch traced here: 87 us
  waiting for transfers between devices  40.6 us (46%)
  starting transfers between devices  24.7 us (28%)
  Pallas kernels  20.8 us (24%)
    ppermute x12, waiting for transfers between devices, to_wide(): lax.ppermute(piece, 'wide', [(i, i ^ other) for i in range(count)])  23.3 us
    ppermute x12, starting transfers between devices, to_wide(): lax.ppermute(piece, 'wide', [(i, i ^ other) for i in range(count)])  20.5 us
    ppermute x10, waiting for transfers between devices, hop(): lax.ppermute(piece, 'narrow', perm)  17.4 us
    pallas_call x1, Pallas kernels, keep(): pl.pallas_call(keep_kernel, out_shape=[pltpu.HBM(blocks.shape, blocks.dty...  6.02 us
    pallas_call x2, Pallas kernels, pack(): pl.pallas_call(functools.partial(pack_kernel, chunk, with_rows, wide_coun...  4.42 us
    ppermute x10, starting transfers between devices, hop(): lax.ppermute(piece, 'narrow', perm)  4.16 us
    pallas_call x1, Pallas kernels, first_window(): pl.pallas_call(functools.partial(first_kernel, window, piece_counts(windo...  3.1 us
    pallas_call x1, Pallas kernels, last_window(): pl.pallas_call(functools.partial(last_kernel, window, piece_counts(window...  2.65 us
  transfers between devices with their start and end apart: 22, of which 12 were waited for; matrix products, arithmetic and copies ran while one was open for 0% of the time, Pallas kernels for 17%

profile of v26, /device:TPU:0, one launch (start us, length us, event | category | flops | bytes accessed | tf_op | source)
XLA Modules:
  0.0 87.0 jit_solution(17064244405072279384)
XLA Ops:
  0.6 4.1 %collective-permute-start.2 = (s32[2,4]{1,0:T(2,128)}, s32[2,4]{1,0:T(2,128)S(1)}, u32[]{:S(2)}, u32[]{:S(2)}) collective-permute-start(s32[2,4]{1,0:T(2,128)} %bitcast.14), channel_id=1, source_target_pairs={{0,8},{4,12},{8,0},{12,4},{1,9},{5,13},{9,1},{13,5},{2,10},{6,14},... | collective-permute-start | bytes 104 | tf_op jit(solution)/shard_map/ppermute | solution.py:479
  4.7 1.3 %collective-permute-start.1 = (s32[2,4]{1,0:T(2,128)}, s32[2,4]{1,0:T(2,128)S(1)}, u32[]{:S(2)}, u32[]{:S(2)}) collective-permute-start(s32[2,4]{1,0:T(2,128)} %bitcast.15), channel_id=1, source_target_pairs={{0,12},{4,8},{8,4},{12,0},{1,13},{5,9},{9,5},{13,1},{2,14},{6,10},... | collective-permute-start | bytes 104 | tf_op jit(solution)/shard_map/ppermute | solution.py:479
  6.5 3.8 %collective-permute-done.1.refs_1_ = s32[2,4]{1,0:T(2,128)S(1)} collective-permute-done((s32[2,4]{1,0:T(2,128)}, s32[2,4]{1,0:T(2,128)S(1)}, u32[]{:S(2)}, u32[]{:S(2)}) %collective-permute-start.1) | collective-permute-done | bytes 64 | tf_op jit(solution)/shard_map/ppermute | solution.py:479
  10.3 2.5 %pack.2 = (bf16[2,336,256]{2,1,0:T(8,128)(2,1)S(1)}, bf16[2,336,256]{2,1,0:T(8,128)(2,1)S(1)}, bf16[2,336,256]{2,1,0:T(8,128)(2,1)S(1)}, bf16[4,512,256]{2,1,0:T(8,128)(2,1)S(1)}) custom-call(s32[1]{0:T(128)} %bitcast.me_ref, s32[2,4]{1,0:T(2,128)} %bitcast.17, s32[2,4]{1,0:T(2,128)S(1)} %collective-permute-done.refs_0_, ...), custom_call_target="tpu_custom_call" | custom-call | tf_op jit(solution)/shard_map/pack/pallas_call | solution.py:94
  12.8 1.6 %collective-permute-start.3 = (bf16[4,512,256]{2,1,0:T(8,128)(2,1)S(1)}, bf16[4,512,256]{2,1,0:T(8,128)(2,1)S(1)}, u32[]{:S(2)}, u32[]{:S(2)}) collective-permute-start(bf16[4,512,256]{2,1,0:T(8,128)(2,1)S(1)} %get-tuple-element.45.rows_ref), channel_id=1, source_target_pairs={{0,2},{1,3},{2,0},{3,1},{4,6},{5,7},{6,4},{7,5},{8,10},{9,11},{10,... | collective-permute-start | bytes 3145736 | tf_op jit(solution)/shard_map/ppermute | solution.py:464
  14.4 1.2 %collective-permute-start.4 = (bf16[2,336,256]{2,1,0:T(8,128)(2,1)S(1)}, bf16[2,336,256]{2,1,0:T(8,128)(2,1)S(1)}, u32[]{:S(2)}, u32[]{:S(2)}) collective-permute-start(bf16[2,336,256]{2,1,0:T(8,128)(2,1)S(1)} %get-tuple-element.46), channel_id=1, source_target_pairs={{0,8},{4,12},{8,0},{12,4},{1,9},{5,13},{9,1},{13,5},{2,10},{6,14},... | collective-permute-start | bytes 1032200 | tf_op jit(solution)/shard_map/ppermute | solution.py:479
  15.6 0.9 %collective-permute-start.5 = (bf16[2,336,256]{2,1,0:T(8,128)(2,1)S(1)}, bf16[2,336,256]{2,1,0:T(8,128)(2,1)S(1)}, u32[]{:S(2)}, u32[]{:S(2)}) collective-permute-start(bf16[2,336,256]{2,1,0:T(8,128)(2,1)S(1)} %get-tuple-element.47), channel_id=1, source_target_pairs={{0,12},{4,8},{8,4},{12,0},{1,13},{5,9},{9,5},{13,1},{2,14},{6,10},... | collective-permute-start | bytes 1032200 | tf_op jit(solution)/shard_map/ppermute | solution.py:479
  16.5 1.4 %collective-permute-start.6 = (bf16[2,336,256]{2,1,0:T(8,128)(2,1)S(1)}, bf16[2,336,256]{2,1,0:T(8,128)(2,1)S(1)}, u32[]{:S(2)}, u32[]{:S(2)}) collective-permute-start(bf16[2,336,256]{2,1,0:T(8,128)(2,1)S(1)} %get-tuple-element.48), channel_id=1, source_target_pairs={{0,4},{4,0},{8,12},{12,8},{1,5},{5,1},{9,13},{13,9},{2,6},{6,2},{1... | collective-permute-start | bytes 1032200 | tf_op jit(solution)/shard_map/ppermute | solution.py:479
  17.9 1.9 %pack.3 = (bf16[2,176,256]{2,1,0:T(8,128)(2,1)S(1)}, bf16[2,176,256]{2,1,0:T(8,128)(2,1)S(1)}, bf16[2,176,256]{2,1,0:T(8,128)(2,1)S(1)}) custom-call(s32[1]{0:T(128)} %bitcast.me_ref, s32[2,4]{1,0:T(2,128)} %bitcast.18, s32[2,4]{1,0:T(2,128)S(1)} %collective-permute-done.refs_0_, s32[2,4]{1,0:T(2,128)S(1)} %collective-permute-done.1.refs_1_, ...), custom_call_target="tpu_custom_call" | custom-call | tf_op jit(solution)/shard_map/pack/pallas_call | solution.py:94
  19.8 0.7 collective-permute-start.7
  20.5 6.0 %keep.1 = (bf16[8,512,256]{2,1,0:T(8,128)(2,1)}, bf16[4,512,256]{2,1,0:T(8,128)(2,1)S(1)}) custom-call(s32[2,4]{1,0:T(2,128)} %bitcast.19, bf16[8,512,256]{2,1,0:T(8,128)(2,1)} %bitcast.10, bf16[8,512,256]{2,1,0:T(8,128)(2,1)} %bitcast.11), custom_call_target="tpu_custom_call" | custom-call | tf_op jit(solution)/shard_map/keep/pallas_call | solution.py:347
  26.5 9.9 %collective-permute-done.3 = bf16[4,512,256]{2,1,0:T(8,128)(2,1)S(1)} collective-permute-done((bf16[4,512,256]{2,1,0:T(8,128)(2,1)S(1)}, bf16[4,512,256]{2,1,0:T(8,128)(2,1)S(1)}, u32[]{:S(2)}, u32[]{:S(2)}) %collective-permute-start.3) | collective-permute-done | bytes 1048608 | tf_op jit(solution)/shard_map/ppermute | solution.py:464
  36.6 6.0 %collective-permute-done.7.refs_2_ = bf16[2,176,256]{2,1,0:T(8,128)(2,1)S(1)} collective-permute-done((bf16[2,176,256]{2,1,0:T(8,128)(2,1)S(1)}, bf16[2,176,256]{2,1,0:T(8,128)(2,1)S(1)}, u32[]{:S(2)}, u32[]{:S(2)}) %collective-permute-start.7) | collective-permute-done | bytes 180256 | tf_op jit(solution)/shard_map/ppermute | solution.py:479
  42.7 0.9 select.2
  43.5 0.6 collective-permute-start.8
  44.1 3.8 %collective-permute-start.10 = (bf16[2,176,256]{2,1,0:T(8,128)(2,1)S(1)}, bf16[2,176,256]{2,1,0:T(8,128)(2,1)S(1)}, u32[]{:S(2)}, u32[]{:S(2)}) collective-permute-start(bf16[2,176,256]{2,1,0:T(8,128)(2,1)S(1)} %get-tuple-element.60), channel_id=1, source_target_pairs={{0,8},{4,12},{8,0},{12,4},{1,9},{5,13},{9,1},{13,5},{2,10},{6,14},... | collective-permute-start | bytes 540680 | tf_op jit(solution)/shard_map/ppermute | solution.py:479
  47.9 1.2 %collective-permute-start.11 = (bf16[2,176,256]{2,1,0:T(8,128)(2,1)S(1)}, bf16[2,176,256]{2,1,0:T(8,128)(2,1)S(1)}, u32[]{:S(2)}, u32[]{:S(2)}) collective-permute-start(bf16[2,176,256]{2,1,0:T(8,128)(2,1)S(1)} %get-tuple-element.61), channel_id=1, source_target_pairs={{0,12},{4,8},{8,4},{12,0},{1,13},{5,9},{9,5},{13,1},{2,14},{6,10},... | collective-permute-start | bytes 540680 | tf_op jit(solution)/shard_map/ppermute | solution.py:479
  49.1 11.8 %collective-permute-done.10.refs_0_ = bf16[2,176,256]{2,1,0:T(8,128)(2,1)S(1)} collective-permute-done((bf16[2,176,256]{2,1,0:T(8,128)(2,1)S(1)}, bf16[2,176,256]{2,1,0:T(8,128)(2,1)S(1)}, u32[]{:S(2)}, u32[]{:S(2)}) %collective-permute-start.10) | collective-permute-done | bytes 180256 | tf_op jit(solution)/shard_map/ppermute | solution.py:479
  61.0 0.4 collective-permute-done.8.refs_4_
  61.4 0.8 select.3.refs_9_.refs_2_
  62.2 1.1 %collective-permute-start.16 = (bf16[4,176,256]{2,1,0:T(8,128)(2,1)S(1)}, bf16[4,176,256]{2,1,0:T(8,128)(2,1)S(1)}, u32[]{:S(2)}, u32[]{:S(2)}) collective-permute-start(bf16[4,176,256]{2,1,0:T(8,128)(2,1)S(1)} %select.3.refs_9_.refs_2_), channel_id=1, source_target_pairs={{0,2},{1,3},{2,0},{3,1},{4,6},{5,7},{6,4},{7,5},{8,10},{9,11},{10,... | collective-permute-start | bytes 1081352 | tf_op jit(solution)/shard_map/ppermute | solution.py:464
  64.2 0.9 %collective-permute-done.15.refs_8_ = bf16[2,336,256]{2,1,0:T(8,128)(2,1)S(1)} collective-permute-done((bf16[2,336,256]{2,1,0:T(8,128)(2,1)S(1)}, bf16[2,336,256]{2,1,0:T(8,128)(2,1)S(1)}, u32[]{:S(2)}, u32[]{:S(2)}) %collective-permute-start.15) | collective-permute-done | bytes 344096 | tf_op jit(solution)/shard_map/ppermute | solution.py:464
  65.1 0.5 collective-permute-done.14.refs_7_
  65.6 3.1 %first_window.1 = (f32[4,512,128]{2,1,0:T(8,128)S(1)}, f32[4,512,128]{2,1,0:T(8,128)S(1)}, f32[4,512,256]{2,1,0:T(8,128)S(1)}, f32[4,256]{1,0:T(4,128)S(1)}) custom-call(bf16[2,4,512,256]{3,2,1,0:T(8,128)(2,1)S(1)} %pad_maximum_fusion.refs_0_, bf16[2,4,512,256]{3,2,1,0:T(8,128)(2,1)S(1)} %collective-permute-done.9.refs_1_, ...), custom_call_target="tpu_custom_call" | custom-call | tf_op jit(solution)/shard_map/first_window/pallas_call | solution.py:287
  68.7 4.0 %collective-permute-done.16.refs_10_ = bf16[4,176,256]{2,1,0:T(8,128)(2,1)S(1)} collective-permute-done((bf16[4,176,256]{2,1,0:T(8,128)(2,1)S(1)}, bf16[4,176,256]{2,1,0:T(8,128)(2,1)S(1)}, u32[]{:S(2)}, u32[]{:S(2)}) %collective-permute-start.16) | collective-permute-done | bytes 360480 | tf_op jit(solution)/shard_map/ppermute | solution.py:464
  72.7 1.7 %collective-permute-done.18.refs_12_ = bf16[4,176,256]{2,1,0:T(8,128)(2,1)S(1)} collective-permute-done((bf16[4,176,256]{2,1,0:T(8,128)(2,1)S(1)}, bf16[4,176,256]{2,1,0:T(8,128)(2,1)S(1)}, u32[]{:S(2)}, u32[]{:S(2)}) %collective-permute-start.18) | collective-permute-done | bytes 360480 | tf_op jit(solution)/shard_map/ppermute | solution.py:464
  74.4 2.7 %last_window.1 = (bf16[4,512,256]{2,1,0:T(8,128)(2,1)S(1)}, f32[4,512,128]{2,1,0:T(8,128)S(1)}, f32[8,512]{1,0:T(8,128)S(1)}, f32[8,512]{1,0:T(8,128)S(1)}, f32[...) custom-call(s32[1]{0:T(128)} %bitcast.me_ref, s32[2,4]{1,0:T(2,128)} %bitcast.22, ...), custom_call_target="tpu_custom_call" | custom-call | flops 1073741824 | bytes 8388608 | tf_op jit(solution)/shard_map/last_window/pallas_call | solution.py:311
  77.0 3.5 %collective-permute-start.19 = (f32[8,512]{1,0:T(8,128)S(1)}, f32[8,512]{1,0:T(8,128)S(1)}, u32[]{:S(2)}, u32[]{:S(2)}) collective-permute-start(f32[8,512]{1,0:T(8,128)S(1)} %get-tuple-element.81), channel_id=1, source_target_pairs={{0,8},{4,12},{8,0},{12,4},{1,9},{5,13},{9,1},{13,5},{2,10},{6,14},... | collective-permute-start | bytes 49160 | tf_op jit(solution)/shard_map/ppermute | solution.py:479
  80.5 2.2 %collective-permute-start.20 = (f32[8,512]{1,0:T(8,128)S(1)}, f32[8,512]{1,0:T(8,128)S(1)}, u32[]{:S(2)}, u32[]{:S(2)}) collective-permute-start(f32[8,512]{1,0:T(8,128)S(1)} %get-tuple-element.82), channel_id=1, source_target_pairs={{0,12},{4,8},{8,4},{12,0},{1,13},{5,9},{9,5},{13,1},{2,14},{6,10},... | collective-permute-start | bytes 49160 | tf_op jit(solution)/shard_map/ppermute | solution.py:479
  82.7 2.3 %means.1 = bf16[8,512,256]{2,1,0:T(8,128)(2,1)} custom-call(s32[2,4]{1,0:T(2,128)} %bitcast.23, bf16[4,512,256]{2,1,0:T(8,128)(2,1)S(1)} %get-tuple-element.45.rows_ref, bf16[4,512,256]{2,1,0:T(8,128)(2,1)S(1)} %get-tuple-element.84.kernel_ref, f32[4,512,128]{2,1,0:T(8,128)S(1)} %get-tuple-element.85.mass_ref, ...), custom_call_target="tpu_custom_call", output_to_operand_aliasing={{}: (8, {})} | custom-call | flops 536870912 | bytes 8388608 | tf_op jit(solution)/shard_map/means/pallas_call | solution.py:416
  85.0 1.1 %collective-permute-done.20.refs_3_ = f32[8,512]{1,0:T(8,128)S(1)} collective-permute-done((f32[8,512]{1,0:T(8,128)S(1)}, f32[8,512]{1,0:T(8,128)S(1)}, u32[]{:S(2)}, u32[]{:S(2)}) %collective-permute-start.20) | collective-permute-done | bytes 16416 | tf_op jit(solution)/shard_map/ppermute | solution.py:479
  86.4 0.6 weights.1
  (23 shorter events, 1.9 us)
Async XLA Ops:
  0.6 5.9 %collective-permute-start.2 = (s32[2,4]{1,0:T(2,128)}, s32[2,4]{1,0:T(2,128)S(1)}, u32[]{:S(2)}, u32[]{:S(2)}) collective-permute-start(s32[2,4]{1,0:T(2,128)} %bitcast.14), channel_id=1, source_target_pairs={{0,8},{4,12},{8,0},{12,4},{1,9},{5,13},{9,1},{13,5},{2,10},{6,14},... | collective-permute-start | bytes 104 | tf_op jit(solution)/shard_map/ppermute | solution.py:479
  4.7 5.6 %collective-permute-start.1 = (s32[2,4]{1,0:T(2,128)}, s32[2,4]{1,0:T(2,128)S(1)}, u32[]{:S(2)}, u32[]{:S(2)}) collective-permute-start(s32[2,4]{1,0:T(2,128)} %bitcast.15), channel_id=1, source_target_pairs={{0,12},{4,8},{8,4},{12,0},{1,13},{5,9},{9,5},{13,1},{2,14},{6,10},... | collective-permute-start | bytes 104 | tf_op jit(solution)/shard_map/ppermute | solution.py:479
  6.1 4.2 %collective-permute-start = (s32[2,4]{1,0:T(2,128)}, s32[2,4]{1,0:T(2,128)S(1)}, u32[]{:S(2)}, u32[]{:S(2)}) collective-permute-start(s32[2,4]{1,0:T(2,128)} %bitcast.16), channel_id=1, source_target_pairs={{0,4},{4,0},{8,12},{12,8},{1,5},{5,1},{9,13},{13,9},{2,6},{6,2},{1... | collective-permute-start | bytes 104 | tf_op jit(solution)/shard_map/ppermute | solution.py:479
  12.8 23.5 %collective-permute-start.3 = (bf16[4,512,256]{2,1,0:T(8,128)(2,1)S(1)}, bf16[4,512,256]{2,1,0:T(8,128)(2,1)S(1)}, u32[]{:S(2)}, u32[]{:S(2)}) collective-permute-start(bf16[4,512,256]{2,1,0:T(8,128)(2,1)S(1)} %get-tuple-element.45.rows_ref), channel_id=1, source_target_pairs={{0,2},{1,3},{2,0},{3,1},{4,6},{5,7},{6,4},{7,5},{8,10},{9,11},{10,... | collective-permute-start | bytes 3145736 | tf_op jit(solution)/shard_map/ppermute | solution.py:464
  14.4 28.2 %collective-permute-start.4 = (bf16[2,336,256]{2,1,0:T(8,128)(2,1)S(1)}, bf16[2,336,256]{2,1,0:T(8,128)(2,1)S(1)}, u32[]{:S(2)}, u32[]{:S(2)}) collective-permute-start(bf16[2,336,256]{2,1,0:T(8,128)(2,1)S(1)} %get-tuple-element.46), channel_id=1, source_target_pairs={{0,8},{4,12},{8,0},{12,4},{1,9},{5,13},{9,1},{13,5},{2,10},{6,14},... | collective-permute-start | bytes 1032200 | tf_op jit(solution)/shard_map/ppermute | solution.py:479
  15.6 27.0 %collective-permute-start.5 = (bf16[2,336,256]{2,1,0:T(8,128)(2,1)S(1)}, bf16[2,336,256]{2,1,0:T(8,128)(2,1)S(1)}, u32[]{:S(2)}, u32[]{:S(2)}) collective-permute-start(bf16[2,336,256]{2,1,0:T(8,128)(2,1)S(1)} %get-tuple-element.47), channel_id=1, source_target_pairs={{0,12},{4,8},{8,4},{12,0},{1,13},{5,9},{9,5},{13,1},{2,14},{6,10},... | collective-permute-start | bytes 1032200 | tf_op jit(solution)/shard_map/ppermute | solution.py:479
  16.5 26.1 %collective-permute-start.6 = (bf16[2,336,256]{2,1,0:T(8,128)(2,1)S(1)}, bf16[2,336,256]{2,1,0:T(8,128)(2,1)S(1)}, u32[]{:S(2)}, u32[]{:S(2)}) collective-permute-start(bf16[2,336,256]{2,1,0:T(8,128)(2,1)S(1)} %get-tuple-element.48), channel_id=1, source_target_pairs={{0,4},{4,0},{8,12},{12,8},{1,5},{5,1},{9,13},{13,9},{2,6},{6,2},{1... | collective-permute-start | bytes 1032200 | tf_op jit(solution)/shard_map/ppermute | solution.py:479
  19.8 22.8 %collective-permute-start.7 = (bf16[2,176,256]{2,1,0:T(8,128)(2,1)S(1)}, bf16[2,176,256]{2,1,0:T(8,128)(2,1)S(1)}, u32[]{:S(2)}, u32[]{:S(2)}) collective-permute-start(bf16[2,176,256]{2,1,0:T(8,128)(2,1)S(1)} %get-tuple-element.49), channel_id=1, source_target_pairs={{0,4},{4,0},{8,12},{12,8},{1,5},{5,1},{9,13},{13,9},{2,6},{6,2},{1... | collective-permute-start | bytes 540680 | tf_op jit(solution)/shard_map/ppermute | solution.py:479
  42.6 18.9 %collective-permute-start.9 = (bf16[2,4,512,256]{3,2,1,0:T(8,128)(2,1)S(1)}, bf16[2,4,512,256]{3,2,1,0:T(8,128)(2,1)S(1)}, u32[]{:S(2)}, u32[]{:S(2)}) collective-permute-start(bf16[2,4,512,256]{3,2,1,0:T(8,128)(2,1)S(1)} %pad_maximum_fusion.refs_0_), channel_id=1, source_target_pairs={{0,1},{1,0},{2,3},{3,2},{4,5},{5,4},{6,7},{7,6},{8,9},{9,8},{10,11... | collective-permute-start | bytes 6291464 | tf_op jit(solution)/shard_map/ppermute | solution.py:464
  43.5 17.9 %collective-permute-start.8 = (bf16[4,336,256]{2,1,0:T(8,128)(2,1)S(1)}, bf16[4,336,256]{2,1,0:T(8,128)(2,1)S(1)}, u32[]{:S(2)}, u32[]{:S(2)}) collective-permute-start(bf16[4,336,256]{2,1,0:T(8,128)(2,1)S(1)} %get-tuple-element.58), channel_id=1, source_target_pairs={{0,2},{1,3},{2,0},{3,1},{4,6},{5,7},{6,4},{7,5},{8,10},{9,11},{10,... | collective-permute-start | bytes 2064392 | tf_op jit(solution)/shard_map/ppermute | solution.py:464
  44.1 16.8 %collective-permute-start.10 = (bf16[2,176,256]{2,1,0:T(8,128)(2,1)S(1)}, bf16[2,176,256]{2,1,0:T(8,128)(2,1)S(1)}, u32[]{:S(2)}, u32[]{:S(2)}) collective-permute-start(bf16[2,176,256]{2,1,0:T(8,128)(2,1)S(1)} %get-tuple-element.60), channel_id=1, source_target_pairs={{0,8},{4,12},{8,0},{12,4},{1,9},{5,13},{9,1},{13,5},{2,10},{6,14},... | collective-permute-start | bytes 540680 | tf_op jit(solution)/shard_map/ppermute | solution.py:479
  47.9 13.1 %collective-permute-start.11 = (bf16[2,176,256]{2,1,0:T(8,128)(2,1)S(1)}, bf16[2,176,256]{2,1,0:T(8,128)(2,1)S(1)}, u32[]{:S(2)}, u32[]{:S(2)}) collective-permute-start(bf16[2,176,256]{2,1,0:T(8,128)(2,1)S(1)} %get-tuple-element.61), channel_id=1, source_target_pairs={{0,12},{4,8},{8,4},{12,0},{1,13},{5,9},{9,5},{13,1},{2,14},{6,10},... | collective-permute-start | bytes 540680 | tf_op jit(solution)/shard_map/ppermute | solution.py:479
  49.1 14.9 %collective-permute-start.12 = (bf16[2,336,256]{2,1,0:T(8,128)(2,1)S(1)}, bf16[2,336,256]{2,1,0:T(8,128)(2,1)S(1)}, u32[]{:S(2)}, u32[]{:S(2)}) collective-permute-start(bf16[2,336,256]{2,1,0:T(8,128)(2,1)S(1)} %get-tuple-element.64.refs_2_.refs_0_), channel_id=1, source_target_pairs={{0,1},{1,0},{2,3},{3,2},{4,5},{5,4},{6,7},{7,6},{8,9},{9,8},{10,11... | collective-permute-start | bytes 1032200 | tf_op jit(solution)/shard_map/ppermute | solution.py:464
  61.0 3.2 %collective-permute-start.13 = (bf16[2,336,256]{2,1,0:T(8,128)(2,1)S(1)}, bf16[2,336,256]{2,1,0:T(8,128)(2,1)S(1)}, u32[]{:S(2)}, u32[]{:S(2)}) collective-permute-start(bf16[2,336,256]{2,1,0:T(8,128)(2,1)S(1)} %get-tuple-element.65.refs_3_.refs_1_), channel_id=1, source_target_pairs={{0,1},{1,0},{2,3},{3,2},{4,5},{5,4},{6,7},{7,6},{8,9},{9,8},{10,11... | collective-permute-start | bytes 1032200 | tf_op jit(solution)/shard_map/ppermute | solution.py:464
  62.2 10.5 %collective-permute-start.16 = (bf16[4,176,256]{2,1,0:T(8,128)(2,1)S(1)}, bf16[4,176,256]{2,1,0:T(8,128)(2,1)S(1)}, u32[]{:S(2)}, u32[]{:S(2)}) collective-permute-start(bf16[4,176,256]{2,1,0:T(8,128)(2,1)S(1)} %select.3.refs_9_.refs_2_), channel_id=1, source_target_pairs={{0,2},{1,3},{2,0},{3,1},{4,6},{5,7},{6,4},{7,5},{8,10},{9,11},{10,... | collective-permute-start | bytes 1081352 | tf_op jit(solution)/shard_map/ppermute | solution.py:464
  63.4 1.7 %collective-permute-start.15 = (bf16[2,336,256]{2,1,0:T(8,128)(2,1)S(1)}, bf16[2,336,256]{2,1,0:T(8,128)(2,1)S(1)}, u32[]{:S(2)}, u32[]{:S(2)}) collective-permute-start(bf16[2,336,256]{2,1,0:T(8,128)(2,1)S(1)} %get-tuple-element.88), channel_id=1, source_target_pairs={{0,1},{1,0},{2,3},{3,2},{4,5},{5,4},{6,7},{7,6},{8,9},{9,8},{10,11... | collective-permute-start | bytes 1032200 | tf_op jit(solution)/shard_map/ppermute | solution.py:464
  63.7 1.9 %collective-permute-start.14 = (bf16[2,336,256]{2,1,0:T(8,128)(2,1)S(1)}, bf16[2,336,256]{2,1,0:T(8,128)(2,1)S(1)}, u32[]{:S(2)}, u32[]{:S(2)}) collective-permute-start(bf16[2,336,256]{2,1,0:T(8,128)(2,1)S(1)} %get-tuple-element.89), channel_id=1, source_target_pairs={{0,1},{1,0},{2,3},{3,2},{4,5},{5,4},{6,7},{7,6},{8,9},{9,8},{10,11... | collective-permute-start | bytes 1032200 | tf_op jit(solution)/shard_map/ppermute | solution.py:464
  64.0 8.7 %collective-permute-start.17 = (bf16[4,176,256]{2,1,0:T(8,128)(2,1)S(1)}, bf16[4,176,256]{2,1,0:T(8,128)(2,1)S(1)}, u32[]{:S(2)}, u32[]{:S(2)}) collective-permute-start(bf16[4,176,256]{2,1,0:T(8,128)(2,1)S(1)} %select.3.refs_9_.refs_2_), channel_id=1, source_target_pairs={{0,1},{1,0},{2,3},{3,2},{4,5},{5,4},{6,7},{7,6},{8,9},{9,8},{10,11... | collective-permute-start | bytes 1081352 | tf_op jit(solution)/shard_map/ppermute | solution.py:464
  72.7 1.7 %collective-permute-start.18 = (bf16[4,176,256]{2,1,0:T(8,128)(2,1)S(1)}, bf16[4,176,256]{2,1,0:T(8,128)(2,1)S(1)}, u32[]{:S(2)}, u32[]{:S(2)}) collective-permute-start(bf16[4,176,256]{2,1,0:T(8,128)(2,1)S(1)} %collective-permute-done.16.refs_10_), channel_id=1, source_target_pairs={{0,1},{1,0},{2,3},{3,2},{4,5},{5,4},{6,7},{7,6},{8,9},{9,8},{10,11... | collective-permute-start | bytes 1081352 | tf_op jit(solution)/shard_map/ppermute | solution.py:464
  77.0 8.0 %collective-permute-start.19 = (f32[8,512]{1,0:T(8,128)S(1)}, f32[8,512]{1,0:T(8,128)S(1)}, u32[]{:S(2)}, u32[]{:S(2)}) collective-permute-start(f32[8,512]{1,0:T(8,128)S(1)} %get-tuple-element.81), channel_id=1, source_target_pairs={{0,8},{4,12},{8,0},{12,4},{1,9},{5,13},{9,1},{13,5},{2,10},{6,14},... | collective-permute-start | bytes 49160 | tf_op jit(solution)/shard_map/ppermute | solution.py:479
  80.5 5.5 %collective-permute-start.20 = (f32[8,512]{1,0:T(8,128)S(1)}, f32[8,512]{1,0:T(8,128)S(1)}, u32[]{:S(2)}, u32[]{:S(2)}) collective-permute-start(f32[8,512]{1,0:T(8,128)S(1)} %get-tuple-element.82), channel_id=1, source_target_pairs={{0,12},{4,8},{8,4},{12,0},{1,13},{5,9},{9,5},{13,1},{2,14},{6,10},... | collective-permute-start | bytes 49160 | tf_op jit(solution)/shard_map/ppermute | solution.py:479
  82.7 3.7 %collective-permute-start.21 = (f32[8,512]{1,0:T(8,128)S(1)}, f32[8,512]{1,0:T(8,128)S(1)}, u32[]{:S(2)}, u32[]{:S(2)}) collective-permute-start(f32[8,512]{1,0:T(8,128)S(1)} %get-tuple-element.83), channel_id=1, source_target_pairs={{0,4},{4,0},{8,12},{12,8},{1,5},{5,1},{9,13},{13,9},{2,6},{6,2},{1... | collective-permute-start | bytes 49160 | tf_op jit(solution)/shard_map/ppermute | solution.py:479

commit v27 on v25

--- a/solution.py
+++ b/solution.py
@@ -101,10 +101,10 @@
     )(me, in_hbm(pairs), *[lists[other - 1] for other in list_order(wide_count)], in_hbm(blocks))
 
 
-def select_kernel(wide_count, groups, start, me_ref, pairs_ref, own_ref, *refs):
+def select_kernel(apart_of, groups, start, me_ref, pairs_ref, own_ref, *refs):
     pair_count = own_ref.shape[0]
-    outs = refs[wide_count - 1 :]
-    received = refs[: wide_count - 1]
+    outs = refs[len(apart_of) :]
+    received = refs[: len(apart_of)]
     size = outs[0].shape[1]
     owners = [pairs_ref[1, pair] >> 3 for pair in range(pair_count)]
     for pair in range(pair_count):
@@ -123,7 +123,7 @@
             for out in places:
                 out[...] = own_ref[pair, start : start + size]
 
-        for number, other in enumerate(others(wide_count)):
+        for number, other in enumerate(apart_of):
 
             @pl.when(apart == other)
             def _():
@@ -131,7 +131,7 @@
                     out[...] = received[number][rank]
 
 
-def select(me, pairs, own, received, start, size, groups):
+def select(me, pairs, own, received, apart, start, size, groups):
     pair_count, _, feat = own.shape
     shapes = [
         pltpu.VMEM((pair_count // pieces, size, feat), own.dtype)
@@ -139,7 +139,7 @@
         for _ in range(pieces)
     ]
     outs = pl.pallas_call(
-        functools.partial(select_kernel, len(received) + 1, groups, start),
+        functools.partial(select_kernel, tuple(apart), groups, start),
         out_shape=shapes,
         in_specs=[smem(), smem()] + [vmem()] * (1 + len(received)),
         out_specs=[vmem()] * len(shapes),
@@ -494,8 +494,8 @@
     *outgoing, row_slices = pack(me, pairs, lists, blocks, capacity, 0, True)
     later = pack(me, pairs, lists, blocks, capacity, 1, False)
 
-    def pick(received, chunk, *groups):
-        return select(me, pairs, own, received, *CHUNKS[chunk], groups)
+    def pick(received, apart, chunk, *groups):
+        return select(me, pairs, own, received, apart, *CHUNKS[chunk], groups)
 
     def halves(part):
         middle = pair_count // 2
@@ -505,11 +505,12 @@
     received = to_wide(outgoing, apart)
     near = to_wide(later[-1:], apart[-1:])
     rows, received, near, (kept, own) = fixed((rows, received, near, keep(pairs, blocks)))
-    own_a, whole_a = pick(received, 0, 2, 1)
+    own_a, whole_a = pick(received, apart, 0, 2, 1)
     cols_a = [own_a] + first_hops(whole_a)[1:]
     rows = [[rows], *hop([[rows]], 1)]
-    cols_a, rows, received = fixed((cols_a, rows, to_wide(later[:-1], apart[:-1])))
-    cols_b = first_hops(*pick([*received, *near], 1, 1))
+    back = apart[:-1][::-1]
+    cols_a, rows, received = fixed((cols_a, rows, to_wide(later[:-1][::-1], back)))
+    cols_b = first_hops(*pick([*received, *near], [*back, apart[-1]], 1, 1))
     last_b = hop(cols_b[:1], 1)
     cols_a = cols_a + hop([own_a] + [halves(part) for part in cols_a[1:]], 1)
     carry = first_window(rows, [cols_a])

time: 85.4 us -> 87.8 us (1.028)
  waiting for transfers between devices: 42.6 us -> 44.4 us
    ppermute x10, waiting for transfers between devices: 15.7 us -> 18.9 us  [hop(): lax.ppermute(piece, 'narrow', perm)]
    ppermute x12, starting transfers between devices: 16.3 us -> 18 us  [to_wide(): lax.ppermute(piece, 'wide', [(i, i ^ other) for i in range(count)])]
    ppermute x12, waiting for transfers between devices: 26.8 us -> 25.5 us  [to_wide(): lax.ppermute(piece, 'wide', [(i, i ^ other) for i in range(count)])]
    ppermute x10, starting transfers between devices: 4.37 us -> 3.41 us  [hop(): lax.ppermute(piece, 'narrow', perm)]
  transfers between devices with their start and end apart: 22 -> 22, of which waited for: 12 -> 13; matrix products, arithmetic and copies ran while one was open for 0% -> 0% of each run, Pallas kernels for 18% -> 17%
where the time goes in v27:
time: 87.8 us; the launch traced here: 87.4 us
  waiting for transfers between devices  44.4 us (51%)
  starting transfers between devices  21.4 us (24%)
  Pallas kernels  20.7 us (24%)
    ppermute x12, waiting for transfers between devices, to_wide(): lax.ppermute(piece, 'wide', [(i, i ^ other) for i in range(count)])  25.5 us
    ppermute x10, waiting for transfers between devices, hop(): lax.ppermute(piece, 'narrow', perm)  18.9 us
    ppermute x12, starting transfers between devices, to_wide(): lax.ppermute(piece, 'wide', [(i, i ^ other) for i in range(count)])  18 us
    pallas_call x1, Pallas kernels, keep(): pl.pallas_call(keep_kernel, out_shape=[pltpu.HBM(blocks.shape, blocks.dty...  6.03 us
    pallas_call x2, Pallas kernels, pack(): pl.pallas_call(functools.partial(pack_kernel, chunk, with_rows, wide_coun...  4.36 us
    ppermute x10, starting transfers between devices, hop(): lax.ppermute(piece, 'narrow', perm)  3.41 us
    pallas_call x1, Pallas kernels, first_window(): pl.pallas_call(functools.partial(first_kernel, window, piece_counts(windo...  3.1 us
    pallas_call x1, Pallas kernels, last_window(): pl.pallas_call(functools.partial(last_kernel, window, piece_counts(window...  2.64 us
  transfers between devices with their start and end apart: 22, of which 13 were waited for; matrix products, arithmetic and copies ran while one was open for 0% of the time, Pallas kernels for 17%

profile of v27, /device:TPU:0, one launch (start us, length us, event | category | flops | bytes accessed | tf_op | source)
XLA Modules:
  0.0 87.4 jit_solution(2641011537829280397)
XLA Ops:
  0.6 4.1 %collective-permute-start.2 = (s32[2,4]{1,0:T(2,128)}, s32[2,4]{1,0:T(2,128)S(1)}, u32[]{:S(2)}, u32[]{:S(2)}) collective-permute-start(s32[2,4]{1,0:T(2,128)} %bitcast.14), channel_id=1, source_target_pairs={{0,8},{4,12},{8,0},{12,4},{1,9},{5,13},{9,1},{13,5},{2,10},{6,14},... | collective-permute-start | bytes 104 | tf_op jit(solution)/shard_map/ppermute | solution.py:478
  4.7 1.3 %collective-permute-start.1 = (s32[2,4]{1,0:T(2,128)}, s32[2,4]{1,0:T(2,128)S(1)}, u32[]{:S(2)}, u32[]{:S(2)}) collective-permute-start(s32[2,4]{1,0:T(2,128)} %bitcast.15), channel_id=1, source_target_pairs={{0,12},{4,8},{8,4},{12,0},{1,13},{5,9},{9,5},{13,1},{2,14},{6,10},... | collective-permute-start | bytes 104 | tf_op jit(solution)/shard_map/ppermute | solution.py:478
  6.5 3.8 %collective-permute-done.1.refs_1_ = s32[2,4]{1,0:T(2,128)S(1)} collective-permute-done((s32[2,4]{1,0:T(2,128)}, s32[2,4]{1,0:T(2,128)S(1)}, u32[]{:S(2)}, u32[]{:S(2)}) %collective-permute-start.1) | collective-permute-done | bytes 64 | tf_op jit(solution)/shard_map/ppermute | solution.py:478
  10.3 2.5 %pack.2 = (bf16[2,336,256]{2,1,0:T(8,128)(2,1)S(1)}, bf16[2,336,256]{2,1,0:T(8,128)(2,1)S(1)}, bf16[2,336,256]{2,1,0:T(8,128)(2,1)S(1)}, bf16[4,512,256]{2,1,0:T(8,128)(2,1)S(1)}) custom-call(s32[1]{0:T(128)} %bitcast.me_ref, s32[2,4]{1,0:T(2,128)} %bitcast.17, s32[2,4]{1,0:T(2,128)S(1)} %collective-permute-done.refs_0_, ...), custom_call_target="tpu_custom_call" | custom-call | tf_op jit(solution)/shard_map/pack/pallas_call | solution.py:93
  12.8 1.6 %collective-permute-start.3 = (bf16[4,512,256]{2,1,0:T(8,128)(2,1)S(1)}, bf16[4,512,256]{2,1,0:T(8,128)(2,1)S(1)}, u32[]{:S(2)}, u32[]{:S(2)}) collective-permute-start(bf16[4,512,256]{2,1,0:T(8,128)(2,1)S(1)} %get-tuple-element.45.rows_ref), channel_id=1, source_target_pairs={{0,2},{1,3},{2,0},{3,1},{4,6},{5,7},{6,4},{7,5},{8,10},{9,11},{10,... | collective-permute-start | bytes 3145736 | tf_op jit(solution)/shard_map/ppermute | solution.py:463
  14.3 2.1 %collective-permute-start.4 = (bf16[2,336,256]{2,1,0:T(8,128)(2,1)S(1)}, bf16[2,336,256]{2,1,0:T(8,128)(2,1)S(1)}, u32[]{:S(2)}, u32[]{:S(2)}) collective-permute-start(bf16[2,336,256]{2,1,0:T(8,128)(2,1)S(1)} %get-tuple-element.46), channel_id=1, source_target_pairs={{0,12},{4,8},{8,4},{12,0},{1,13},{5,9},{9,5},{13,1},{2,14},{6,10},... | collective-permute-start | bytes 1032200 | tf_op jit(solution)/shard_map/ppermute | solution.py:478
  16.4 2.3 %collective-permute-start.6 = (bf16[2,336,256]{2,1,0:T(8,128)(2,1)S(1)}, bf16[2,336,256]{2,1,0:T(8,128)(2,1)S(1)}, u32[]{:S(2)}, u32[]{:S(2)}) collective-permute-start(bf16[2,336,256]{2,1,0:T(8,128)(2,1)S(1)} %get-tuple-element.48), channel_id=1, source_target_pairs={{0,4},{4,0},{8,12},{12,8},{1,5},{5,1},{9,13},{13,9},{2,6},{6,2},{1... | collective-permute-start | bytes 1032200 | tf_op jit(solution)/shard_map/ppermute | solution.py:478
  18.7 1.9 %pack.3 = (bf16[2,176,256]{2,1,0:T(8,128)(2,1)S(1)}, bf16[2,176,256]{2,1,0:T(8,128)(2,1)S(1)}, bf16[2,176,256]{2,1,0:T(8,128)(2,1)S(1)}) custom-call(s32[1]{0:T(128)} %bitcast.me_ref, s32[2,4]{1,0:T(2,128)} %bitcast.18, s32[2,4]{1,0:T(2,128)S(1)} %collective-permute-done.refs_0_, s32[2,4]{1,0:T(2,128)S(1)} %collective-permute-done.1.refs_1_, ...), custom_call_target="tpu_custom_call" | custom-call | tf_op jit(solution)/shard_map/pack/pallas_call | solution.py:93
  20.7 6.0 %keep.1 = (bf16[8,512,256]{2,1,0:T(8,128)(2,1)}, bf16[4,512,256]{2,1,0:T(8,128)(2,1)S(1)}) custom-call(s32[2,4]{1,0:T(2,128)} %bitcast.19, bf16[8,512,256]{2,1,0:T(8,128)(2,1)} %bitcast.10, bf16[8,512,256]{2,1,0:T(8,128)(2,1)} %bitcast.11), custom_call_target="tpu_custom_call" | custom-call | tf_op jit(solution)/shard_map/keep/pallas_call | solution.py:346
  26.8 9.6 %collective-permute-done.3 = bf16[4,512,256]{2,1,0:T(8,128)(2,1)S(1)} collective-permute-done((bf16[4,512,256]{2,1,0:T(8,128)(2,1)S(1)}, bf16[4,512,256]{2,1,0:T(8,128)(2,1)S(1)}, u32[]{:S(2)}, u32[]{:S(2)}) %collective-permute-start.3) | collective-permute-done | bytes 1048608 | tf_op jit(solution)/shard_map/ppermute | solution.py:463
  36.5 4.0 %collective-permute-done.7.refs_2_ = bf16[2,176,256]{2,1,0:T(8,128)(2,1)S(1)} collective-permute-done((bf16[2,176,256]{2,1,0:T(8,128)(2,1)S(1)}, bf16[2,176,256]{2,1,0:T(8,128)(2,1)S(1)}, u32[]{:S(2)}, u32[]{:S(2)}) %collective-permute-start.7) | collective-permute-done | bytes 180256 | tf_op jit(solution)/shard_map/ppermute | solution.py:478
  40.5 3.4 %collective-permute-done.5.refs_1_ = bf16[2,336,256]{2,1,0:T(8,128)(2,1)S(1)} collective-permute-done((bf16[2,336,256]{2,1,0:T(8,128)(2,1)S(1)}, bf16[2,336,256]{2,1,0:T(8,128)(2,1)S(1)}, u32[]{:S(2)}, u32[]{:S(2)}) %collective-permute-start.5) | collective-permute-done | bytes 344096 | tf_op jit(solution)/shard_map/ppermute | solution.py:478
  43.9 0.9 select.2
  44.7 0.6 collective-permute-start.8
  45.4 2.6 %collective-permute-start.11 = (bf16[2,176,256]{2,1,0:T(8,128)(2,1)S(1)}, bf16[2,176,256]{2,1,0:T(8,128)(2,1)S(1)}, u32[]{:S(2)}, u32[]{:S(2)}) collective-permute-start(bf16[2,176,256]{2,1,0:T(8,128)(2,1)S(1)} %get-tuple-element.61), channel_id=1, source_target_pairs={{0,12},{4,8},{8,4},{12,0},{1,13},{5,9},{9,5},{13,1},{2,14},{6,10},... | collective-permute-start | bytes 540680 | tf_op jit(solution)/shard_map/ppermute | solution.py:478
  48.0 12.7 %collective-permute-done.10.refs_0_ = bf16[2,176,256]{2,1,0:T(8,128)(2,1)S(1)} collective-permute-done((bf16[2,176,256]{2,1,0:T(8,128)(2,1)S(1)}, bf16[2,176,256]{2,1,0:T(8,128)(2,1)S(1)}, u32[]{:S(2)}, u32[]{:S(2)}) %collective-permute-start.10) | collective-permute-done | bytes 180256 | tf_op jit(solution)/shard_map/ppermute | solution.py:478
  60.7 1.9 %collective-permute-done.8.refs_4_ = bf16[4,336,256]{2,1,0:T(8,128)(2,1)S(1)} collective-permute-done((bf16[4,336,256]{2,1,0:T(8,128)(2,1)S(1)}, bf16[4,336,256]{2,1,0:T(8,128)(2,1)S(1)}, u32[]{:S(2)}, u32[]{:S(2)}) %collective-permute-start.8) | collective-permute-done | bytes 688160 | tf_op jit(solution)/shard_map/ppermute | solution.py:463
  62.7 0.8 select.3.refs_9_.refs_2_
  63.5 0.6 collective-permute-start.16
  64.2 0.5 collective-permute-start.14
  64.8 1.1 %collective-permute-done.15.refs_8_ = bf16[2,336,256]{2,1,0:T(8,128)(2,1)S(1)} collective-permute-done((bf16[2,336,256]{2,1,0:T(8,128)(2,1)S(1)}, bf16[2,336,256]{2,1,0:T(8,128)(2,1)S(1)}, u32[]{:S(2)}, u32[]{:S(2)}) %collective-permute-start.15) | collective-permute-done | bytes 344096 | tf_op jit(solution)/shard_map/ppermute | solution.py:463
  65.8 0.5 collective-permute-done.14.refs_7_
  66.3 3.1 %first_window.1 = (f32[4,512,128]{2,1,0:T(8,128)S(1)}, f32[4,512,128]{2,1,0:T(8,128)S(1)}, f32[4,512,256]{2,1,0:T(8,128)S(1)}, f32[4,256]{1,0:T(4,128)S(1)}) custom-call(bf16[2,4,512,256]{3,2,1,0:T(8,128)(2,1)S(1)} %pad_maximum_fusion.refs_0_, bf16[2,4,512,256]{3,2,1,0:T(8,128)(2,1)S(1)} %collective-permute-done.9.refs_1_, ...), custom_call_target="tpu_custom_call" | custom-call | tf_op jit(solution)/shard_map/first_window/pallas_call | solution.py:286
  69.4 4.1 %collective-permute-done.16.refs_10_ = bf16[4,176,256]{2,1,0:T(8,128)(2,1)S(1)} collective-permute-done((bf16[4,176,256]{2,1,0:T(8,128)(2,1)S(1)}, bf16[4,176,256]{2,1,0:T(8,128)(2,1)S(1)}, u32[]{:S(2)}, u32[]{:S(2)}) %collective-permute-start.16) | collective-permute-done | bytes 360480 | tf_op jit(solution)/shard_map/ppermute | solution.py:463
  73.6 1.7 %collective-permute-done.18.refs_12_ = bf16[4,176,256]{2,1,0:T(8,128)(2,1)S(1)} collective-permute-done((bf16[4,176,256]{2,1,0:T(8,128)(2,1)S(1)}, bf16[4,176,256]{2,1,0:T(8,128)(2,1)S(1)}, u32[]{:S(2)}, u32[]{:S(2)}) %collective-permute-start.18) | collective-permute-done | bytes 360480 | tf_op jit(solution)/shard_map/ppermute | solution.py:463
  75.3 2.6 %last_window.1 = (bf16[4,512,256]{2,1,0:T(8,128)(2,1)S(1)}, f32[4,512,128]{2,1,0:T(8,128)S(1)}, f32[8,512]{1,0:T(8,128)S(1)}, f32[8,512]{1,0:T(8,128)S(1)}, f32[...) custom-call(s32[1]{0:T(128)} %bitcast.me_ref, s32[2,4]{1,0:T(2,128)} %bitcast.22, ...), custom_call_target="tpu_custom_call" | custom-call | flops 1073741824 | bytes 8388608 | tf_op jit(solution)/shard_map/last_window/pallas_call | solution.py:310
  77.9 2.5 %collective-permute-start.19 = (f32[8,512]{1,0:T(8,128)S(1)}, f32[8,512]{1,0:T(8,128)S(1)}, u32[]{:S(2)}, u32[]{:S(2)}) collective-permute-start(f32[8,512]{1,0:T(8,128)S(1)} %get-tuple-element.81), channel_id=1, source_target_pairs={{0,8},{4,12},{8,0},{12,4},{1,9},{5,13},{9,1},{13,5},{2,10},{6,14},... | collective-permute-start | bytes 49160 | tf_op jit(solution)/shard_map/ppermute | solution.py:478
  80.4 2.6 %collective-permute-start.20 = (f32[8,512]{1,0:T(8,128)S(1)}, f32[8,512]{1,0:T(8,128)S(1)}, u32[]{:S(2)}, u32[]{:S(2)}) collective-permute-start(f32[8,512]{1,0:T(8,128)S(1)} %get-tuple-element.82), channel_id=1, source_target_pairs={{0,12},{4,8},{8,4},{12,0},{1,13},{5,9},{9,5},{13,1},{2,14},{6,10},... | collective-permute-start | bytes 49160 | tf_op jit(solution)/shard_map/ppermute | solution.py:478
  83.1 2.3 %means.1 = bf16[8,512,256]{2,1,0:T(8,128)(2,1)} custom-call(s32[2,4]{1,0:T(2,128)} %bitcast.23, bf16[4,512,256]{2,1,0:T(8,128)(2,1)S(1)} %get-tuple-element.45.rows_ref, bf16[4,512,256]{2,1,0:T(8,128)(2,1)S(1)} %get-tuple-element.84.kernel_ref, f32[4,512,128]{2,1,0:T(8,128)S(1)} %get-tuple-element.85.mass_ref, ...), custom_call_target="tpu_custom_call", output_to_operand_aliasing={{}: (8, {})} | custom-call | flops 536870912 | bytes 8388608 | tf_op jit(solution)/shard_map/means/pallas_call | solution.py:415
  85.4 0.6 collective-permute-done.20.refs_3_
  86.0 0.8 collective-permute-done.21.refs_4_
  86.8 0.6 weights.1
  (23 shorter events, 0.9 us)
Async XLA Ops:
  0.6 5.9 %collective-permute-start.2 = (s32[2,4]{1,0:T(2,128)}, s32[2,4]{1,0:T(2,128)S(1)}, u32[]{:S(2)}, u32[]{:S(2)}) collective-permute-start(s32[2,4]{1,0:T(2,128)} %bitcast.14), channel_id=1, source_target_pairs={{0,8},{4,12},{8,0},{12,4},{1,9},{5,13},{9,1},{13,5},{2,10},{6,14},... | collective-permute-start | bytes 104 | tf_op jit(solution)/shard_map/ppermute | solution.py:478
  4.7 5.6 %collective-permute-start.1 = (s32[2,4]{1,0:T(2,128)}, s32[2,4]{1,0:T(2,128)S(1)}, u32[]{:S(2)}, u32[]{:S(2)}) collective-permute-start(s32[2,4]{1,0:T(2,128)} %bitcast.15), channel_id=1, source_target_pairs={{0,12},{4,8},{8,4},{12,0},{1,13},{5,9},{9,5},{13,1},{2,14},{6,10},... | collective-permute-start | bytes 104 | tf_op jit(solution)/shard_map/ppermute | solution.py:478
  6.1 4.2 %collective-permute-start = (s32[2,4]{1,0:T(2,128)}, s32[2,4]{1,0:T(2,128)S(1)}, u32[]{:S(2)}, u32[]{:S(2)}) collective-permute-start(s32[2,4]{1,0:T(2,128)} %bitcast.16), channel_id=1, source_target_pairs={{0,4},{4,0},{8,12},{12,8},{1,5},{5,1},{9,13},{13,9},{2,6},{6,2},{1... | collective-permute-start | bytes 104 | tf_op jit(solution)/shard_map/ppermute | solution.py:478
  12.8 23.5 %collective-permute-start.3 = (bf16[4,512,256]{2,1,0:T(8,128)(2,1)S(1)}, bf16[4,512,256]{2,1,0:T(8,128)(2,1)S(1)}, u32[]{:S(2)}, u32[]{:S(2)}) collective-permute-start(bf16[4,512,256]{2,1,0:T(8,128)(2,1)S(1)} %get-tuple-element.45.rows_ref), channel_id=1, source_target_pairs={{0,2},{1,3},{2,0},{3,1},{4,6},{5,7},{6,4},{7,5},{8,10},{9,11},{10,... | collective-permute-start | bytes 3145736 | tf_op jit(solution)/shard_map/ppermute | solution.py:463
  14.3 26.2 %collective-permute-start.4 = (bf16[2,336,256]{2,1,0:T(8,128)(2,1)S(1)}, bf16[2,336,256]{2,1,0:T(8,128)(2,1)S(1)}, u32[]{:S(2)}, u32[]{:S(2)}) collective-permute-start(bf16[2,336,256]{2,1,0:T(8,128)(2,1)S(1)} %get-tuple-element.46), channel_id=1, source_target_pairs={{0,12},{4,8},{8,4},{12,0},{1,13},{5,9},{9,5},{13,1},{2,14},{6,10},... | collective-permute-start | bytes 1032200 | tf_op jit(solution)/shard_map/ppermute | solution.py:478
  16.4 27.5 %collective-permute-start.5 = (bf16[2,336,256]{2,1,0:T(8,128)(2,1)S(1)}, bf16[2,336,256]{2,1,0:T(8,128)(2,1)S(1)}, u32[]{:S(2)}, u32[]{:S(2)}) collective-permute-start(bf16[2,336,256]{2,1,0:T(8,128)(2,1)S(1)} %get-tuple-element.47), channel_id=1, source_target_pairs={{0,8},{4,12},{8,0},{12,4},{1,9},{5,13},{9,1},{13,5},{2,10},{6,14},... | collective-permute-start | bytes 1032200 | tf_op jit(solution)/shard_map/ppermute | solution.py:478
  16.4 27.5 %collective-permute-start.6 = (bf16[2,336,256]{2,1,0:T(8,128)(2,1)S(1)}, bf16[2,336,256]{2,1,0:T(8,128)(2,1)S(1)}, u32[]{:S(2)}, u32[]{:S(2)}) collective-permute-start(bf16[2,336,256]{2,1,0:T(8,128)(2,1)S(1)} %get-tuple-element.48), channel_id=1, source_target_pairs={{0,4},{4,0},{8,12},{12,8},{1,5},{5,1},{9,13},{13,9},{2,6},{6,2},{1... | collective-permute-start | bytes 1032200 | tf_op jit(solution)/shard_map/ppermute | solution.py:478
  20.6 19.9 %collective-permute-start.7 = (bf16[2,176,256]{2,1,0:T(8,128)(2,1)S(1)}, bf16[2,176,256]{2,1,0:T(8,128)(2,1)S(1)}, u32[]{:S(2)}, u32[]{:S(2)}) collective-permute-start(bf16[2,176,256]{2,1,0:T(8,128)(2,1)S(1)} %get-tuple-element.49), channel_id=1, source_target_pairs={{0,4},{4,0},{8,12},{12,8},{1,5},{5,1},{9,13},{13,9},{2,6},{6,2},{1... | collective-permute-start | bytes 540680 | tf_op jit(solution)/shard_map/ppermute | solution.py:478
  43.9 18.8 %collective-permute-start.9 = (bf16[2,4,512,256]{3,2,1,0:T(8,128)(2,1)S(1)}, bf16[2,4,512,256]{3,2,1,0:T(8,128)(2,1)S(1)}, u32[]{:S(2)}, u32[]{:S(2)}) collective-permute-start(bf16[2,4,512,256]{3,2,1,0:T(8,128)(2,1)S(1)} %pad_maximum_fusion.refs_0_), channel_id=1, source_target_pairs={{0,1},{1,0},{2,3},{3,2},{4,5},{5,4},{6,7},{7,6},{8,9},{9,8},{10,11... | collective-permute-start | bytes 6291464 | tf_op jit(solution)/shard_map/ppermute | solution.py:463
  44.7 17.9 %collective-permute-start.8 = (bf16[4,336,256]{2,1,0:T(8,128)(2,1)S(1)}, bf16[4,336,256]{2,1,0:T(8,128)(2,1)S(1)}, u32[]{:S(2)}, u32[]{:S(2)}) collective-permute-start(bf16[4,336,256]{2,1,0:T(8,128)(2,1)S(1)} %get-tuple-element.58), channel_id=1, source_target_pairs={{0,2},{1,3},{2,0},{3,1},{4,6},{5,7},{6,4},{7,5},{8,10},{9,11},{10,... | collective-permute-start | bytes 2064392 | tf_op jit(solution)/shard_map/ppermute | solution.py:463
  45.3 15.4 %collective-permute-start.10 = (bf16[2,176,256]{2,1,0:T(8,128)(2,1)S(1)}, bf16[2,176,256]{2,1,0:T(8,128)(2,1)S(1)}, u32[]{:S(2)}, u32[]{:S(2)}) collective-permute-start(bf16[2,176,256]{2,1,0:T(8,128)(2,1)S(1)} %get-tuple-element.60), channel_id=1, source_target_pairs={{0,8},{4,12},{8,0},{12,4},{1,9},{5,13},{9,1},{13,5},{2,10},{6,14},... | collective-permute-start | bytes 540680 | tf_op jit(solution)/shard_map/ppermute | solution.py:478
  45.4 15.4 %collective-permute-start.11 = (bf16[2,176,256]{2,1,0:T(8,128)(2,1)S(1)}, bf16[2,176,256]{2,1,0:T(8,128)(2,1)S(1)}, u32[]{:S(2)}, u32[]{:S(2)}) collective-permute-start(bf16[2,176,256]{2,1,0:T(8,128)(2,1)S(1)} %get-tuple-element.61), channel_id=1, source_target_pairs={{0,12},{4,8},{8,4},{12,0},{1,13},{5,9},{9,5},{13,1},{2,14},{6,10},... | collective-permute-start | bytes 540680 | tf_op jit(solution)/shard_map/ppermute | solution.py:478
  48.0 16.7 %collective-permute-start.12 = (bf16[2,336,256]{2,1,0:T(8,128)(2,1)S(1)}, bf16[2,336,256]{2,1,0:T(8,128)(2,1)S(1)}, u32[]{:S(2)}, u32[]{:S(2)}) collective-permute-start(bf16[2,336,256]{2,1,0:T(8,128)(2,1)S(1)} %get-tuple-element.64.refs_2_.refs_0_), channel_id=1, source_target_pairs={{0,1},{1,0},{2,3},{3,2},{4,5},{5,4},{6,7},{7,6},{8,9},{9,8},{10,11... | collective-permute-start | bytes 1032200 | tf_op jit(solution)/shard_map/ppermute | solution.py:463
  60.7 4.1 %collective-permute-start.13 = (bf16[2,336,256]{2,1,0:T(8,128)(2,1)S(1)}, bf16[2,336,256]{2,1,0:T(8,128)(2,1)S(1)}, u32[]{:S(2)}, u32[]{:S(2)}) collective-permute-start(bf16[2,336,256]{2,1,0:T(8,128)(2,1)S(1)} %get-tuple-element.65.refs_3_.refs_1_), channel_id=1, source_target_pairs={{0,1},{1,0},{2,3},{3,2},{4,5},{5,4},{6,7},{7,6},{8,9},{9,8},{10,11... | collective-permute-start | bytes 1032200 | tf_op jit(solution)/shard_map/ppermute | solution.py:463
  63.5 10.1 %collective-permute-start.16 = (bf16[4,176,256]{2,1,0:T(8,128)(2,1)S(1)}, bf16[4,176,256]{2,1,0:T(8,128)(2,1)S(1)}, u32[]{:S(2)}, u32[]{:S(2)}) collective-permute-start(bf16[4,176,256]{2,1,0:T(8,128)(2,1)S(1)} %select.3.refs_9_.refs_2_), channel_id=1, source_target_pairs={{0,2},{1,3},{2,0},{3,1},{4,6},{5,7},{6,4},{7,5},{8,10},{9,11},{10,... | collective-permute-start | bytes 1081352 | tf_op jit(solution)/shard_map/ppermute | solution.py:463
  64.1 1.7 %collective-permute-start.15 = (bf16[2,336,256]{2,1,0:T(8,128)(2,1)S(1)}, bf16[2,336,256]{2,1,0:T(8,128)(2,1)S(1)}, u32[]{:S(2)}, u32[]{:S(2)}) collective-permute-start(bf16[2,336,256]{2,1,0:T(8,128)(2,1)S(1)} %get-tuple-element.88), channel_id=1, source_target_pairs={{0,1},{1,0},{2,3},{3,2},{4,5},{5,4},{6,7},{7,6},{8,9},{9,8},{10,11... | collective-permute-start | bytes 1032200 | tf_op jit(solution)/shard_map/ppermute | solution.py:463
  64.2 2.1 %collective-permute-start.14 = (bf16[2,336,256]{2,1,0:T(8,128)(2,1)S(1)}, bf16[2,336,256]{2,1,0:T(8,128)(2,1)S(1)}, u32[]{:S(2)}, u32[]{:S(2)}) collective-permute-start(bf16[2,336,256]{2,1,0:T(8,128)(2,1)S(1)} %get-tuple-element.89), channel_id=1, source_target_pairs={{0,1},{1,0},{2,3},{3,2},{4,5},{5,4},{6,7},{7,6},{8,9},{9,8},{10,11... | collective-permute-start | bytes 1032200 | tf_op jit(solution)/shard_map/ppermute | solution.py:463
  64.7 8.9 %collective-permute-start.17 = (bf16[4,176,256]{2,1,0:T(8,128)(2,1)S(1)}, bf16[4,176,256]{2,1,0:T(8,128)(2,1)S(1)}, u32[]{:S(2)}, u32[]{:S(2)}) collective-permute-start(bf16[4,176,256]{2,1,0:T(8,128)(2,1)S(1)} %select.3.refs_9_.refs_2_), channel_id=1, source_target_pairs={{0,1},{1,0},{2,3},{3,2},{4,5},{5,4},{6,7},{7,6},{8,9},{9,8},{10,11... | collective-permute-start | bytes 1081352 | tf_op jit(solution)/shard_map/ppermute | solution.py:463
  73.6 1.7 %collective-permute-start.18 = (bf16[4,176,256]{2,1,0:T(8,128)(2,1)S(1)}, bf16[4,176,256]{2,1,0:T(8,128)(2,1)S(1)}, u32[]{:S(2)}, u32[]{:S(2)}) collective-permute-start(bf16[4,176,256]{2,1,0:T(8,128)(2,1)S(1)} %collective-permute-done.16.refs_10_), channel_id=1, source_target_pairs={{0,1},{1,0},{2,3},{3,2},{4,5},{5,4},{6,7},{7,6},{8,9},{9,8},{10,11... | collective-permute-start | bytes 1081352 | tf_op jit(solution)/shard_map/ppermute | solution.py:463
  77.9 7.5 %collective-permute-start.19 = (f32[8,512]{1,0:T(8,128)S(1)}, f32[8,512]{1,0:T(8,128)S(1)}, u32[]{:S(2)}, u32[]{:S(2)}) collective-permute-start(f32[8,512]{1,0:T(8,128)S(1)} %get-tuple-element.81), channel_id=1, source_target_pairs={{0,8},{4,12},{8,0},{12,4},{1,9},{5,13},{9,1},{13,5},{2,10},{6,14},... | collective-permute-start | bytes 49160 | tf_op jit(solution)/shard_map/ppermute | solution.py:478
  80.4 5.5 %collective-permute-start.20 = (f32[8,512]{1,0:T(8,128)S(1)}, f32[8,512]{1,0:T(8,128)S(1)}, u32[]{:S(2)}, u32[]{:S(2)}) collective-permute-start(f32[8,512]{1,0:T(8,128)S(1)} %get-tuple-element.82), channel_id=1, source_target_pairs={{0,12},{4,8},{8,4},{12,0},{1,13},{5,9},{9,5},{13,1},{2,14},{6,10},... | collective-permute-start | bytes 49160 | tf_op jit(solution)/shard_map/ppermute | solution.py:478
  83.1 3.7 %collective-permute-start.21 = (f32[8,512]{1,0:T(8,128)S(1)}, f32[8,512]{1,0:T(8,128)S(1)}, u32[]{:S(2)}, u32[]{:S(2)}) collective-permute-start(f32[8,512]{1,0:T(8,128)S(1)} %get-tuple-element.83), channel_id=1, source_target_pairs={{0,4},{4,0},{8,12},{12,8},{1,5},{5,1},{9,13},{13,9},{2,6},{6,2},{1... | collective-permute-start | bytes 49160 | tf_op jit(solution)/shard_map/ppermute | solution.py:478

commit v28 on v25

--- a/solution.py
+++ b/solution.py
@@ -245,18 +245,24 @@
     for ref in (row_ref, *shares):
         ref[...] = jnp.zeros_like(ref)
     all_rows, chunks = window_parts(counts, refs)
+    each = LANES // square_in.shape[0]
+    lane = lax.broadcasted_iota(jnp.int32, (BR, LANES), 1)
     for pair in range(square_in.shape[0]):
         rows, cols = pair_parts(window, all_rows, chunks, pair)
         kernel, sums, mass = scores(rows, cols, square_in[pair])
         kernel_ref[pair] = kernel
         sums = jnp.concatenate([sums_in[pair : pair + 1], sums], axis=1)
         mass = mass_in[pair] + mass
+        mass = jnp.broadcast_to(jnp.sum(mass, axis=1, keepdims=True), (BR, LANES))
         mass_ref[pair] = mass
-        row_ref[pl.ds(pairs_ref[0, pair] & 7, 1)] += jnp.sum(mass.T, axis=0, keepdims=True)
+        packed = mass if pair == 0 else jnp.where(lane >= pair * each, mass, packed)
         col = pairs_ref[1, pair]
         apart = (col >> 3) ^ me_ref[0]
         for other, ref in zip([*sum_order(wide_count), 0], shares):
             ref[pl.ds(col & 7, 1)] += jnp.where(apart == other, sums, 0.0)
+    lines = packed.T
+    for pair in range(square_in.shape[0]):
+        row_ref[pl.ds(pairs_ref[0, pair] & 7, 1)] += lines[pair * each : pair * each + 1]
 
 
 def estimate(pair_count, size):
@@ -376,9 +382,7 @@
             kernel_ref[pair], own_columns(window, chunks, pair), preferred_element_type=jnp.float32
         )
         part[pair] = sums.astype(jnp.bfloat16)
-        weight[pair] = jnp.broadcast_to(
-            jnp.sum(mass_ref[pair], axis=1, keepdims=True), (BR, LANES)
-        )
+        weight[pair] = mass_ref[pair]
         same = [local[other] == local[pair] for other in range(pair)]
         firsts.append(jnp.logical_not(functools.reduce(jnp.logical_or, same, jnp.bool_(False))))
     for pair in range(pair_count):

time: 85.4 us -> 85.4 us (level)
  no operation moved by 1% of the time
where the time goes in v28:
time: 85.4 us; the launch traced here: 85 us
  waiting for transfers between devices  42.6 us (50%)
  starting transfers between devices  20.7 us (24%)
  Pallas kernels  20.7 us (24%)
    ppermute x12, waiting for transfers between devices, to_wide(): lax.ppermute(piece, 'wide', [(i, i ^ other) for i in range(count)])  26.8 us
    ppermute x12, starting transfers between devices, to_wide(): lax.ppermute(piece, 'wide', [(i, i ^ other) for i in range(count)])  16.3 us
    ppermute x10, waiting for transfers between devices, hop(): lax.ppermute(piece, 'narrow', perm)  15.8 us
    pallas_call x1, Pallas kernels, keep(): pl.pallas_call(keep_kernel, out_shape=[pltpu.HBM(blocks.shape, blocks.dty...  6.02 us
    ppermute x10, starting transfers between devices, hop(): lax.ppermute(piece, 'narrow', perm)  4.37 us
    pallas_call x2, Pallas kernels, pack(): pl.pallas_call(functools.partial(pack_kernel, chunk, with_rows, wide_coun...  4.35 us
    pallas_call x1, Pallas kernels, first_window(): pl.pallas_call(functools.partial(first_kernel, window, piece_counts(windo...  3.1 us
    pallas_call x1, Pallas kernels, last_window(): pl.pallas_call(functools.partial(last_kernel, window, piece_counts(window...  2.71 us
  transfers between devices with their start and end apart: 22, of which 12 were waited for; matrix products, arithmetic and copies ran while one was open for 0% of the time, Pallas kernels for 18%

profile of v28, /device:TPU:0, one launch (start us, length us, event | category | flops | bytes accessed | tf_op | source)
XLA Modules:
  0.0 85.0 jit_solution(9807764282825107179)
XLA Ops:
  0.6 4.1 %collective-permute-start.2 = (s32[2,4]{1,0:T(2,128)}, s32[2,4]{1,0:T(2,128)S(1)}, u32[]{:S(2)}, u32[]{:S(2)}) collective-permute-start(s32[2,4]{1,0:T(2,128)} %bitcast.14), channel_id=1, source_target_pairs={{0,8},{4,12},{8,0},{12,4},{1,9},{5,13},{9,1},{13,5},{2,10},{6,14},... | collective-permute-start | bytes 104 | tf_op jit(solution)/shard_map/ppermute | solution.py:482
  4.7 1.3 %collective-permute-start.1 = (s32[2,4]{1,0:T(2,128)}, s32[2,4]{1,0:T(2,128)S(1)}, u32[]{:S(2)}, u32[]{:S(2)}) collective-permute-start(s32[2,4]{1,0:T(2,128)} %bitcast.15), channel_id=1, source_target_pairs={{0,12},{4,8},{8,4},{12,0},{1,13},{5,9},{9,5},{13,1},{2,14},{6,10},... | collective-permute-start | bytes 104 | tf_op jit(solution)/shard_map/ppermute | solution.py:482
  6.5 3.8 %collective-permute-done.1.refs_1_ = s32[2,4]{1,0:T(2,128)S(1)} collective-permute-done((s32[2,4]{1,0:T(2,128)}, s32[2,4]{1,0:T(2,128)S(1)}, u32[]{:S(2)}, u32[]{:S(2)}) %collective-permute-start.1) | collective-permute-done | bytes 64 | tf_op jit(solution)/shard_map/ppermute | solution.py:482
  10.3 2.5 %pack.2 = (bf16[2,336,256]{2,1,0:T(8,128)(2,1)S(1)}, bf16[2,336,256]{2,1,0:T(8,128)(2,1)S(1)}, bf16[2,336,256]{2,1,0:T(8,128)(2,1)S(1)}, bf16[4,512,256]{2,1,0:T(8,128)(2,1)S(1)}) custom-call(s32[1]{0:T(128)} %bitcast.me_ref, s32[2,4]{1,0:T(2,128)} %bitcast.17, s32[2,4]{1,0:T(2,128)S(1)} %collective-permute-done.refs_0_, ...), custom_call_target="tpu_custom_call" | custom-call | tf_op jit(solution)/shard_map/pack/pallas_call | solution.py:93
  12.8 1.6 %collective-permute-start.3 = (bf16[4,512,256]{2,1,0:T(8,128)(2,1)S(1)}, bf16[4,512,256]{2,1,0:T(8,128)(2,1)S(1)}, u32[]{:S(2)}, u32[]{:S(2)}) collective-permute-start(bf16[4,512,256]{2,1,0:T(8,128)(2,1)S(1)} %get-tuple-element.45.rows_ref), channel_id=1, source_target_pairs={{0,2},{1,3},{2,0},{3,1},{4,6},{5,7},{6,4},{7,5},{8,10},{9,11},{10,... | collective-permute-start | bytes 3145736 | tf_op jit(solution)/shard_map/ppermute | solution.py:467
  14.3 2.0 %collective-permute-start.4 = (bf16[2,336,256]{2,1,0:T(8,128)(2,1)S(1)}, bf16[2,336,256]{2,1,0:T(8,128)(2,1)S(1)}, u32[]{:S(2)}, u32[]{:S(2)}) collective-permute-start(bf16[2,336,256]{2,1,0:T(8,128)(2,1)S(1)} %get-tuple-element.46), channel_id=1, source_target_pairs={{0,12},{4,8},{8,4},{12,0},{1,13},{5,9},{9,5},{13,1},{2,14},{6,10},... | collective-permute-start | bytes 1032200 | tf_op jit(solution)/shard_map/ppermute | solution.py:482
  16.4 2.4 %collective-permute-start.6 = (bf16[2,336,256]{2,1,0:T(8,128)(2,1)S(1)}, bf16[2,336,256]{2,1,0:T(8,128)(2,1)S(1)}, u32[]{:S(2)}, u32[]{:S(2)}) collective-permute-start(bf16[2,336,256]{2,1,0:T(8,128)(2,1)S(1)} %get-tuple-element.48), channel_id=1, source_target_pairs={{0,4},{4,0},{8,12},{12,8},{1,5},{5,1},{9,13},{13,9},{2,6},{6,2},{1... | collective-permute-start | bytes 1032200 | tf_op jit(solution)/shard_map/ppermute | solution.py:482
  18.7 1.9 %pack.3 = (bf16[2,176,256]{2,1,0:T(8,128)(2,1)S(1)}, bf16[2,176,256]{2,1,0:T(8,128)(2,1)S(1)}, bf16[2,176,256]{2,1,0:T(8,128)(2,1)S(1)}) custom-call(s32[1]{0:T(128)} %bitcast.me_ref, s32[2,4]{1,0:T(2,128)} %bitcast.18, s32[2,4]{1,0:T(2,128)S(1)} %collective-permute-done.refs_0_, s32[2,4]{1,0:T(2,128)S(1)} %collective-permute-done.1.refs_1_, ...), custom_call_target="tpu_custom_call" | custom-call | tf_op jit(solution)/shard_map/pack/pallas_call | solution.py:93
  20.6 0.2 collective-permute-start.7
  20.9 6.0 %keep.1 = (bf16[8,512,256]{2,1,0:T(8,128)(2,1)}, bf16[4,512,256]{2,1,0:T(8,128)(2,1)S(1)}) custom-call(s32[2,4]{1,0:T(2,128)} %bitcast.19, bf16[8,512,256]{2,1,0:T(8,128)(2,1)} %bitcast.10, bf16[8,512,256]{2,1,0:T(8,128)(2,1)} %bitcast.11), custom_call_target="tpu_custom_call" | custom-call | tf_op jit(solution)/shard_map/keep/pallas_call | solution.py:352
  26.9 9.4 %collective-permute-done.3 = bf16[4,512,256]{2,1,0:T(8,128)(2,1)S(1)} collective-permute-done((bf16[4,512,256]{2,1,0:T(8,128)(2,1)S(1)}, bf16[4,512,256]{2,1,0:T(8,128)(2,1)S(1)}, u32[]{:S(2)}, u32[]{:S(2)}) %collective-permute-start.3) | collective-permute-done | bytes 1048608 | tf_op jit(solution)/shard_map/ppermute | solution.py:467
  36.5 4.0 %collective-permute-done.7.refs_2_ = bf16[2,176,256]{2,1,0:T(8,128)(2,1)S(1)} collective-permute-done((bf16[2,176,256]{2,1,0:T(8,128)(2,1)S(1)}, bf16[2,176,256]{2,1,0:T(8,128)(2,1)S(1)}, u32[]{:S(2)}, u32[]{:S(2)}) %collective-permute-start.7) | collective-permute-done | bytes 180256 | tf_op jit(solution)/shard_map/ppermute | solution.py:482
  40.5 3.5 %collective-permute-done.5.refs_1_ = bf16[2,336,256]{2,1,0:T(8,128)(2,1)S(1)} collective-permute-done((bf16[2,336,256]{2,1,0:T(8,128)(2,1)S(1)}, bf16[2,336,256]{2,1,0:T(8,128)(2,1)S(1)}, u32[]{:S(2)}, u32[]{:S(2)}) %collective-permute-start.5) | collective-permute-done | bytes 344096 | tf_op jit(solution)/shard_map/ppermute | solution.py:482
  44.0 0.9 %select.2 = (bf16[2,336,256]{2,1,0:T(8,128)(2,1)S(1)}, bf16[2,336,256]{2,1,0:T(8,128)(2,1)S(1)}, bf16[4,336,256]{2,1,0:T(8,128)(2,1)S(1)}) custom-call(s32[1]{0:T(128)} %bitcast.me_ref, s32[2,4]{1,0:T(2,128)} %bitcast.20, bf16[4,512,256]{2,1,0:T(8,128)(2,1)S(1)} %get-tuple-element.52.own_ref, bf16[2,336,256]{2,1,0:T(8,128)(2,1)S(1)} %collective-permute-done.4.refs_0_, ...), custom_call_target="tpu_custom_call" | custom-call | tf_op jit(solution)/shard_map/select/pallas_call | solution.py:141
  44.8 0.6 collective-permute-start.8
  45.4 2.4 %collective-permute-start.10 = (bf16[2,176,256]{2,1,0:T(8,128)(2,1)S(1)}, bf16[2,176,256]{2,1,0:T(8,128)(2,1)S(1)}, u32[]{:S(2)}, u32[]{:S(2)}) collective-permute-start(bf16[2,176,256]{2,1,0:T(8,128)(2,1)S(1)} %get-tuple-element.60), channel_id=1, source_target_pairs={{0,12},{4,8},{8,4},{12,0},{1,13},{5,9},{9,5},{13,1},{2,14},{6,10},... | collective-permute-start | bytes 540680 | tf_op jit(solution)/shard_map/ppermute | solution.py:482
  47.9 6.8 %collective-permute-done.10.refs_0_ = bf16[2,176,256]{2,1,0:T(8,128)(2,1)S(1)} collective-permute-done((bf16[2,176,256]{2,1,0:T(8,128)(2,1)S(1)}, bf16[2,176,256]{2,1,0:T(8,128)(2,1)S(1)}, u32[]{:S(2)}, u32[]{:S(2)}) %collective-permute-start.10) | collective-permute-done | bytes 180256 | tf_op jit(solution)/shard_map/ppermute | solution.py:482
  54.7 8.1 %collective-permute-done.11.refs_1_ = bf16[2,176,256]{2,1,0:T(8,128)(2,1)S(1)} collective-permute-done((bf16[2,176,256]{2,1,0:T(8,128)(2,1)S(1)}, bf16[2,176,256]{2,1,0:T(8,128)(2,1)S(1)}, u32[]{:S(2)}, u32[]{:S(2)}) %collective-permute-start.11) | collective-permute-done | bytes 180256 | tf_op jit(solution)/shard_map/ppermute | solution.py:482
  62.8 0.8 select.3.refs_9_.refs_2_
  63.6 1.6 %collective-permute-start.16 = (bf16[4,176,256]{2,1,0:T(8,128)(2,1)S(1)}, bf16[4,176,256]{2,1,0:T(8,128)(2,1)S(1)}, u32[]{:S(2)}, u32[]{:S(2)}) collective-permute-start(bf16[4,176,256]{2,1,0:T(8,128)(2,1)S(1)} %select.3.refs_9_.refs_2_), channel_id=1, source_target_pairs={{0,2},{1,3},{2,0},{3,1},{4,6},{5,7},{6,4},{7,5},{8,10},{9,11},{10,... | collective-permute-start | bytes 1081352 | tf_op jit(solution)/shard_map/ppermute | solution.py:467
  65.3 0.5 collective-permute-start.14
  65.8 1.1 %collective-permute-done.15.refs_8_ = bf16[2,336,256]{2,1,0:T(8,128)(2,1)S(1)} collective-permute-done((bf16[2,336,256]{2,1,0:T(8,128)(2,1)S(1)}, bf16[2,336,256]{2,1,0:T(8,128)(2,1)S(1)}, u32[]{:S(2)}, u32[]{:S(2)}) %collective-permute-start.15) | collective-permute-done | bytes 344096 | tf_op jit(solution)/shard_map/ppermute | solution.py:467
  66.9 0.5 collective-permute-done.14.refs_7_
  67.4 3.1 %first_window.1 = (f32[4,512,128]{2,1,0:T(8,128)S(1)}, f32[4,512,128]{2,1,0:T(8,128)S(1)}, f32[4,512,256]{2,1,0:T(8,128)S(1)}, f32[4,256]{1,0:T(4,128)S(1)}) custom-call(bf16[2,4,512,256]{3,2,1,0:T(8,128)(2,1)S(1)} %pad_maximum_fusion.refs_0_, bf16[2,4,512,256]{3,2,1,0:T(8,128)(2,1)S(1)} %collective-permute-done.9.refs_1_, ...), custom_call_target="tpu_custom_call" | custom-call | tf_op jit(solution)/shard_map/first_window/pallas_call | solution.py:292
  70.5 3.2 %collective-permute-done.16.refs_10_ = bf16[4,176,256]{2,1,0:T(8,128)(2,1)S(1)} collective-permute-done((bf16[4,176,256]{2,1,0:T(8,128)(2,1)S(1)}, bf16[4,176,256]{2,1,0:T(8,128)(2,1)S(1)}, u32[]{:S(2)}, u32[]{:S(2)}) %collective-permute-start.16) | collective-permute-done | bytes 360480 | tf_op jit(solution)/shard_map/ppermute | solution.py:467
  73.7 1.7 %collective-permute-done.18.refs_12_ = bf16[4,176,256]{2,1,0:T(8,128)(2,1)S(1)} collective-permute-done((bf16[4,176,256]{2,1,0:T(8,128)(2,1)S(1)}, bf16[4,176,256]{2,1,0:T(8,128)(2,1)S(1)}, u32[]{:S(2)}, u32[]{:S(2)}) %collective-permute-start.18) | collective-permute-done | bytes 360480 | tf_op jit(solution)/shard_map/ppermute | solution.py:467
  75.3 2.7 %last_window.1 = (bf16[4,512,256]{2,1,0:T(8,128)(2,1)S(1)}, f32[4,512,128]{2,1,0:T(8,128)S(1)}, f32[8,512]{1,0:T(8,128)S(1)}, f32[8,512]{1,0:T(8,128)S(1)}, f32[...) custom-call(s32[1]{0:T(128)} %bitcast.me_ref, s32[2,4]{1,0:T(2,128)} %bitcast.22, ...), custom_call_target="tpu_custom_call" | custom-call | flops 1073741824 | bytes 8388608 | tf_op jit(solution)/shard_map/last_window/pallas_call | solution.py:316
  78.1 2.5 %collective-permute-start.20 = (f32[8,512]{1,0:T(8,128)S(1)}, f32[8,512]{1,0:T(8,128)S(1)}, u32[]{:S(2)}, u32[]{:S(2)}) collective-permute-start(f32[8,512]{1,0:T(8,128)S(1)} %get-tuple-element.82), channel_id=1, source_target_pairs={{0,12},{4,8},{8,4},{12,0},{1,13},{5,9},{9,5},{13,1},{2,14},{6,10},... | collective-permute-start | bytes 49160 | tf_op jit(solution)/shard_map/ppermute | solution.py:482
  80.6 1.0 %collective-permute-start.21 = (f32[8,512]{1,0:T(8,128)S(1)}, f32[8,512]{1,0:T(8,128)S(1)}, u32[]{:S(2)}, u32[]{:S(2)}) collective-permute-start(f32[8,512]{1,0:T(8,128)S(1)} %get-tuple-element.83), channel_id=1, source_target_pairs={{0,4},{4,0},{8,12},{12,8},{1,5},{5,1},{9,13},{13,9},{2,6},{6,2},{1... | collective-permute-start | bytes 49160 | tf_op jit(solution)/shard_map/ppermute | solution.py:482
  81.6 2.3 %means.1 = bf16[8,512,256]{2,1,0:T(8,128)(2,1)} custom-call(s32[2,4]{1,0:T(2,128)} %bitcast.23, bf16[4,512,256]{2,1,0:T(8,128)(2,1)S(1)} %get-tuple-element.45.rows_ref, bf16[4,512,256]{2,1,0:T(8,128)(2,1)S(1)} %get-tuple-element.84.kernel_ref, f32[4,512,128]{2,1,0:T(8,128)S(1)} %get-tuple-element.85.mass_ref, ...), custom_call_target="tpu_custom_call", output_to_operand_aliasing={{}: (8, {})} | custom-call | flops 536870912 | bytes 8388608 | tf_op jit(solution)/shard_map/means/pallas_call | solution.py:419
  83.9 0.5 collective-permute-done.21.refs_4_
  84.4 0.6 weights.1
  (23 shorter events, 0.9 us)
Async XLA Ops:
  0.6 5.9 %collective-permute-start.2 = (s32[2,4]{1,0:T(2,128)}, s32[2,4]{1,0:T(2,128)S(1)}, u32[]{:S(2)}, u32[]{:S(2)}) collective-permute-start(s32[2,4]{1,0:T(2,128)} %bitcast.14), channel_id=1, source_target_pairs={{0,8},{4,12},{8,0},{12,4},{1,9},{5,13},{9,1},{13,5},{2,10},{6,14},... | collective-permute-start | bytes 104 | tf_op jit(solution)/shard_map/ppermute | solution.py:482
  4.7 5.6 %collective-permute-start.1 = (s32[2,4]{1,0:T(2,128)}, s32[2,4]{1,0:T(2,128)S(1)}, u32[]{:S(2)}, u32[]{:S(2)}) collective-permute-start(s32[2,4]{1,0:T(2,128)} %bitcast.15), channel_id=1, source_target_pairs={{0,12},{4,8},{8,4},{12,0},{1,13},{5,9},{9,5},{13,1},{2,14},{6,10},... | collective-permute-start | bytes 104 | tf_op jit(solution)/shard_map/ppermute | solution.py:482
  6.1 4.2 %collective-permute-start = (s32[2,4]{1,0:T(2,128)}, s32[2,4]{1,0:T(2,128)S(1)}, u32[]{:S(2)}, u32[]{:S(2)}) collective-permute-start(s32[2,4]{1,0:T(2,128)} %bitcast.16), channel_id=1, source_target_pairs={{0,4},{4,0},{8,12},{12,8},{1,5},{5,1},{9,13},{13,9},{2,6},{6,2},{1... | collective-permute-start | bytes 104 | tf_op jit(solution)/shard_map/ppermute | solution.py:482
  12.8 23.5 %collective-permute-start.3 = (bf16[4,512,256]{2,1,0:T(8,128)(2,1)S(1)}, bf16[4,512,256]{2,1,0:T(8,128)(2,1)S(1)}, u32[]{:S(2)}, u32[]{:S(2)}) collective-permute-start(bf16[4,512,256]{2,1,0:T(8,128)(2,1)S(1)} %get-tuple-element.45.rows_ref), channel_id=1, source_target_pairs={{0,2},{1,3},{2,0},{3,1},{4,6},{5,7},{6,4},{7,5},{8,10},{9,11},{10,... | collective-permute-start | bytes 3145736 | tf_op jit(solution)/shard_map/ppermute | solution.py:467
  14.3 26.1 %collective-permute-start.4 = (bf16[2,336,256]{2,1,0:T(8,128)(2,1)S(1)}, bf16[2,336,256]{2,1,0:T(8,128)(2,1)S(1)}, u32[]{:S(2)}, u32[]{:S(2)}) collective-permute-start(bf16[2,336,256]{2,1,0:T(8,128)(2,1)S(1)} %get-tuple-element.46), channel_id=1, source_target_pairs={{0,12},{4,8},{8,4},{12,0},{1,13},{5,9},{9,5},{13,1},{2,14},{6,10},... | collective-permute-start | bytes 1032200 | tf_op jit(solution)/shard_map/ppermute | solution.py:482
  16.4 27.6 %collective-permute-start.5 = (bf16[2,336,256]{2,1,0:T(8,128)(2,1)S(1)}, bf16[2,336,256]{2,1,0:T(8,128)(2,1)S(1)}, u32[]{:S(2)}, u32[]{:S(2)}) collective-permute-start(bf16[2,336,256]{2,1,0:T(8,128)(2,1)S(1)} %get-tuple-element.47), channel_id=1, source_target_pairs={{0,8},{4,12},{8,0},{12,4},{1,9},{5,13},{9,1},{13,5},{2,10},{6,14},... | collective-permute-start | bytes 1032200 | tf_op jit(solution)/shard_map/ppermute | solution.py:482
  16.4 27.6 %collective-permute-start.6 = (bf16[2,336,256]{2,1,0:T(8,128)(2,1)S(1)}, bf16[2,336,256]{2,1,0:T(8,128)(2,1)S(1)}, u32[]{:S(2)}, u32[]{:S(2)}) collective-permute-start(bf16[2,336,256]{2,1,0:T(8,128)(2,1)S(1)} %get-tuple-element.48), channel_id=1, source_target_pairs={{0,4},{4,0},{8,12},{12,8},{1,5},{5,1},{9,13},{13,9},{2,6},{6,2},{1... | collective-permute-start | bytes 1032200 | tf_op jit(solution)/shard_map/ppermute | solution.py:482
  20.6 19.8 %collective-permute-start.7 = (bf16[2,176,256]{2,1,0:T(8,128)(2,1)S(1)}, bf16[2,176,256]{2,1,0:T(8,128)(2,1)S(1)}, u32[]{:S(2)}, u32[]{:S(2)}) collective-permute-start(bf16[2,176,256]{2,1,0:T(8,128)(2,1)S(1)} %get-tuple-element.49), channel_id=1, source_target_pairs={{0,4},{4,0},{8,12},{12,8},{1,5},{5,1},{9,13},{13,9},{2,6},{6,2},{1... | collective-permute-start | bytes 540680 | tf_op jit(solution)/shard_map/ppermute | solution.py:482
  44.0 18.8 %collective-permute-start.9 = (bf16[2,4,512,256]{3,2,1,0:T(8,128)(2,1)S(1)}, bf16[2,4,512,256]{3,2,1,0:T(8,128)(2,1)S(1)}, u32[]{:S(2)}, u32[]{:S(2)}) collective-permute-start(bf16[2,4,512,256]{3,2,1,0:T(8,128)(2,1)S(1)} %pad_maximum_fusion.refs_0_), channel_id=1, source_target_pairs={{0,1},{1,0},{2,3},{3,2},{4,5},{5,4},{6,7},{7,6},{8,9},{9,8},{10,11... | collective-permute-start | bytes 6291464 | tf_op jit(solution)/shard_map/ppermute | solution.py:467
  44.8 17.9 %collective-permute-start.8 = (bf16[4,336,256]{2,1,0:T(8,128)(2,1)S(1)}, bf16[4,336,256]{2,1,0:T(8,128)(2,1)S(1)}, u32[]{:S(2)}, u32[]{:S(2)}) collective-permute-start(bf16[4,336,256]{2,1,0:T(8,128)(2,1)S(1)} %get-tuple-element.58), channel_id=1, source_target_pairs={{0,2},{1,3},{2,0},{3,1},{4,6},{5,7},{6,4},{7,5},{8,10},{9,11},{10,... | collective-permute-start | bytes 2064392 | tf_op jit(solution)/shard_map/ppermute | solution.py:467
  45.4 9.3 %collective-permute-start.10 = (bf16[2,176,256]{2,1,0:T(8,128)(2,1)S(1)}, bf16[2,176,256]{2,1,0:T(8,128)(2,1)S(1)}, u32[]{:S(2)}, u32[]{:S(2)}) collective-permute-start(bf16[2,176,256]{2,1,0:T(8,128)(2,1)S(1)} %get-tuple-element.60), channel_id=1, source_target_pairs={{0,12},{4,8},{8,4},{12,0},{1,13},{5,9},{9,5},{13,1},{2,14},{6,10},... | collective-permute-start | bytes 540680 | tf_op jit(solution)/shard_map/ppermute | solution.py:482
  47.9 14.9 %collective-permute-start.11 = (bf16[2,176,256]{2,1,0:T(8,128)(2,1)S(1)}, bf16[2,176,256]{2,1,0:T(8,128)(2,1)S(1)}, u32[]{:S(2)}, u32[]{:S(2)}) collective-permute-start(bf16[2,176,256]{2,1,0:T(8,128)(2,1)S(1)} %get-tuple-element.61), channel_id=1, source_target_pairs={{0,8},{4,12},{8,0},{12,4},{1,9},{5,13},{9,1},{13,5},{2,10},{6,14},... | collective-permute-start | bytes 540680 | tf_op jit(solution)/shard_map/ppermute | solution.py:482
  47.9 17.9 %collective-permute-start.12 = (bf16[2,336,256]{2,1,0:T(8,128)(2,1)S(1)}, bf16[2,336,256]{2,1,0:T(8,128)(2,1)S(1)}, u32[]{:S(2)}, u32[]{:S(2)}) collective-permute-start(bf16[2,336,256]{2,1,0:T(8,128)(2,1)S(1)} %get-tuple-element.64.refs_2_.refs_0_), channel_id=1, source_target_pairs={{0,1},{1,0},{2,3},{3,2},{4,5},{5,4},{6,7},{7,6},{8,9},{9,8},{10,11... | collective-permute-start | bytes 1032200 | tf_op jit(solution)/shard_map/ppermute | solution.py:467
  54.7 11.1 %collective-permute-start.13 = (bf16[2,336,256]{2,1,0:T(8,128)(2,1)S(1)}, bf16[2,336,256]{2,1,0:T(8,128)(2,1)S(1)}, u32[]{:S(2)}, u32[]{:S(2)}) collective-permute-start(bf16[2,336,256]{2,1,0:T(8,128)(2,1)S(1)} %get-tuple-element.65.refs_3_.refs_1_), channel_id=1, source_target_pairs={{0,1},{1,0},{2,3},{3,2},{4,5},{5,4},{6,7},{7,6},{8,9},{9,8},{10,11... | collective-permute-start | bytes 1032200 | tf_op jit(solution)/shard_map/ppermute | solution.py:467
  63.6 10.1 %collective-permute-start.16 = (bf16[4,176,256]{2,1,0:T(8,128)(2,1)S(1)}, bf16[4,176,256]{2,1,0:T(8,128)(2,1)S(1)}, u32[]{:S(2)}, u32[]{:S(2)}) collective-permute-start(bf16[4,176,256]{2,1,0:T(8,128)(2,1)S(1)} %select.3.refs_9_.refs_2_), channel_id=1, source_target_pairs={{0,2},{1,3},{2,0},{3,1},{4,6},{5,7},{6,4},{7,5},{8,10},{9,11},{10,... | collective-permute-start | bytes 1081352 | tf_op jit(solution)/shard_map/ppermute | solution.py:467
  65.2 1.7 %collective-permute-start.15 = (bf16[2,336,256]{2,1,0:T(8,128)(2,1)S(1)}, bf16[2,336,256]{2,1,0:T(8,128)(2,1)S(1)}, u32[]{:S(2)}, u32[]{:S(2)}) collective-permute-start(bf16[2,336,256]{2,1,0:T(8,128)(2,1)S(1)} %get-tuple-element.88), channel_id=1, source_target_pairs={{0,1},{1,0},{2,3},{3,2},{4,5},{5,4},{6,7},{7,6},{8,9},{9,8},{10,11... | collective-permute-start | bytes 1032200 | tf_op jit(solution)/shard_map/ppermute | solution.py:467
  65.3 2.1 %collective-permute-start.14 = (bf16[2,336,256]{2,1,0:T(8,128)(2,1)S(1)}, bf16[2,336,256]{2,1,0:T(8,128)(2,1)S(1)}, u32[]{:S(2)}, u32[]{:S(2)}) collective-permute-start(bf16[2,336,256]{2,1,0:T(8,128)(2,1)S(1)} %get-tuple-element.89), channel_id=1, source_target_pairs={{0,1},{1,0},{2,3},{3,2},{4,5},{5,4},{6,7},{7,6},{8,9},{9,8},{10,11... | collective-permute-start | bytes 1032200 | tf_op jit(solution)/shard_map/ppermute | solution.py:467
  65.8 7.9 %collective-permute-start.17 = (bf16[4,176,256]{2,1,0:T(8,128)(2,1)S(1)}, bf16[4,176,256]{2,1,0:T(8,128)(2,1)S(1)}, u32[]{:S(2)}, u32[]{:S(2)}) collective-permute-start(bf16[4,176,256]{2,1,0:T(8,128)(2,1)S(1)} %select.3.refs_9_.refs_2_), channel_id=1, source_target_pairs={{0,1},{1,0},{2,3},{3,2},{4,5},{5,4},{6,7},{7,6},{8,9},{9,8},{10,11... | collective-permute-start | bytes 1081352 | tf_op jit(solution)/shard_map/ppermute | solution.py:467
  73.7 1.7 %collective-permute-start.18 = (bf16[4,176,256]{2,1,0:T(8,128)(2,1)S(1)}, bf16[4,176,256]{2,1,0:T(8,128)(2,1)S(1)}, u32[]{:S(2)}, u32[]{:S(2)}) collective-permute-start(bf16[4,176,256]{2,1,0:T(8,128)(2,1)S(1)} %collective-permute-done.16.refs_10_), channel_id=1, source_target_pairs={{0,1},{1,0},{2,3},{3,2},{4,5},{5,4},{6,7},{7,6},{8,9},{9,8},{10,11... | collective-permute-start | bytes 1081352 | tf_op jit(solution)/shard_map/ppermute | solution.py:467
  78.0 5.9 %collective-permute-start.19 = (f32[8,512]{1,0:T(8,128)S(1)}, f32[8,512]{1,0:T(8,128)S(1)}, u32[]{:S(2)}, u32[]{:S(2)}) collective-permute-start(f32[8,512]{1,0:T(8,128)S(1)} %get-tuple-element.81), channel_id=1, source_target_pairs={{0,8},{4,12},{8,0},{12,4},{1,9},{5,13},{9,1},{13,5},{2,10},{6,14},... | collective-permute-start | bytes 49160 | tf_op jit(solution)/shard_map/ppermute | solution.py:482
  78.1 5.8 %collective-permute-start.20 = (f32[8,512]{1,0:T(8,128)S(1)}, f32[8,512]{1,0:T(8,128)S(1)}, u32[]{:S(2)}, u32[]{:S(2)}) collective-permute-start(f32[8,512]{1,0:T(8,128)S(1)} %get-tuple-element.82), channel_id=1, source_target_pairs={{0,12},{4,8},{8,4},{12,0},{1,13},{5,9},{9,5},{13,1},{2,14},{6,10},... | collective-permute-start | bytes 49160 | tf_op jit(solution)/shard_map/ppermute | solution.py:482
  80.6 3.7 %collective-permute-start.21 = (f32[8,512]{1,0:T(8,128)S(1)}, f32[8,512]{1,0:T(8,128)S(1)}, u32[]{:S(2)}, u32[]{:S(2)}) collective-permute-start(f32[8,512]{1,0:T(8,128)S(1)} %get-tuple-element.83), channel_id=1, source_target_pairs={{0,4},{4,0},{8,12},{12,8},{1,5},{5,1},{9,13},{13,9},{2,6},{6,2},{1... | collective-permute-start | bytes 49160 | tf_op jit(solution)/shard_map/ppermute | solution.py:482
